TPU v7x, 32 devices: a whole 2x2x4 slice. The times are simulated.
32 devices in a mesh: mem: 16 (over z, y, core), band: 2 (over x).
Axes of the slice: x: 2, y: 2, z: 4, core: 2. Of those that a mesh axis runs over, the one named last changes fastest.
Arguments:
- coeffs: float32 [16, 2, 2, 2, 640, 640], P('mem', None, None, None, 'band'), may hold values from -0.0390625 to 0.0390625
Outputs:
- ftle: float32 [2, 640, 1280], P(None, 'band')
All inputs are finite; a program needn't handle non-finite values.
Results may differ from a plain program's by a relative error of at most 0.0001.
Values sent between devices are 32-bit elements; how exact they have to be, the bound alone decides.
No kernel may reach another device: no remote copies, remote signals or barrier semaphores. Data moves between devices by JAX's collectives and lax.ppermute only.
A program may use at most 64 MiB of HBM per device.

v0:
```python
import math

import jax
import jax.numpy as jnp
from jax import lax
from jax.sharding import PartitionSpec as P

NLON = 1280
STEPS = 1


def padded(cells, sides, width):
    for axis, dim in sides:
        count = lax.axis_size(axis)
        ends = count - 1
        head = lax.slice_in_dim(cells, 0, width, axis=dim)
        tail = lax.slice_in_dim(cells, cells.shape[dim] - width, cells.shape[dim], axis=dim)
        cells = jnp.concatenate(
            [
                lax.ppermute(tail, axis, [(i, (i + 1) % count) for i in range(ends)]),
                cells,
                lax.ppermute(head, axis, [((i + 1) % count, i) for i in range(ends)]),
            ],
            axis=dim,
        )
    return cells


def slope(extended, winds):
    center = extended[:, 1:-1]
    north = (extended[:, 2:] - extended[:, :-2]) * 0.5
    east = (jnp.roll(center, -1, 2) - jnp.roll(center, 1, 2)) * 0.5
    return -winds - (winds[0] * east + winds[1] * north)


def rimmed(field):
    return padded(field, (("band", 1),), 1)


def tensor(extended):
    center = extended[:, 1:-1]
    north = (extended[:, 2:] - extended[:, :-2]) * 0.5
    east = (jnp.roll(center, -1, 2) - jnp.roll(center, 1, 2)) * 0.5
    g_xx = 1.0 + east[0]
    g_xy = north[0]
    g_yx = east[1]
    g_yy = 1.0 + north[1]
    return jnp.stack(
        [g_xx * g_xx + g_yx * g_yx, g_xx * g_xy + g_yx * g_yy, g_xy * g_xy + g_yy * g_yy]
    )


def integrate(shift, flow, extend):
    first = slope(extend(shift), flow)
    second = slope(extend(0.5 * first), flow)
    third = slope(extend(0.5 * second), flow)
    fourth = slope(extend(third), flow)
    shift = (first + 2.0 * second + 2.0 * third + fourth) / 6.0
    return shift


def finish(partial_sum):
    members = lax.axis_size("mem")
    summed = lax.psum_scatter(partial_sum, "mem", scatter_dimension=3, tiled=True) / members
    first, cross, second = (summed[:, 0], summed[:, 1], summed[:, 2])
    half = (first + second) * 0.5
    differ = (first - second) * 0.5
    largest = half + jnp.sqrt(differ * differ + cross * cross)
    exponent = jnp.log(largest + 1e-06) / (2.0 * STEPS)
    return lax.all_gather(exponent, "mem", axis=2, tiled=True)


def per_device(coeffs):
    spec = coeffs[0]
    levels = spec.shape[0]
    nlat = spec.shape[4]
    waves = spec.shape[3] * lax.axis_size("band")
    stacked = spec.reshape(levels * 2, 2, spec.shape[3], nlat)
    wave_index = lax.iota(jnp.int32, waves)
    column = lax.iota(jnp.int32, NLON)
    phase = wave_index[:, None] * column[None, :] % NLON
    angle = phase.astype(jnp.float32) * (2.0 * math.pi / NLON)
    weight = jnp.where(wave_index == 0, 1.0, 2.0).astype(jnp.float32)[:, None]
    table = jnp.stack([weight * jnp.cos(angle), -weight * jnp.sin(angle)], axis=0)
    winds = jnp.einsum(
        "crwh,rwn->chn",
        lax.all_to_all(stacked, "band", split_axis=3, concat_axis=2, tiled=True),
        table,
        precision=lax.Precision.HIGHEST,
        preferred_element_type=jnp.float32,
    )
    height = winds.shape[1]
    winds = winds.reshape(levels, 2, height, NLON)
    partials = []
    for level in range(levels):
        flow = winds[level]
        shift = integrate(jnp.zeros_like(flow), flow, rimmed)
        local = tensor(rimmed(shift))
        partials.append(local)
    return finish(jnp.stack(partials))


def solution(mesh):
    placed = (P("mem", None, None, None, "band", None),)
    return jax.shard_map(
        per_device, mesh=mesh, in_specs=placed, out_specs=P(None, "band", None), check_vma=False
    )
```

profile of v0, /device:TPU:0, one launch (start us, length us, event | category | flops | bytes accessed | tf_op | source)
XLA Modules:
  0.0 610.6 jit_solution(16892104321472885233)
XLA Ops:
  6.5 12.2 %copy.8 = f32[1,2,2,2,320,640]{4,3,2,1,5,0:T(2,128)} copy(f32[1,2,2,2,320,640]{5,4,3,2,1,0:T(8,128)} %param.1) | data formatting | bytes 13107200 | tf_op args[0]
  18.7 6.8 %all-to-all-start = ((f32[4,2,320,640]{2,1,0,3:T(2,128)}), f32[4,2,320,640]{2,1,0,3:T(2,128)}, u32[]{:S(2)}, u32[]{:S(2)}) async-start(f32[4,2,320,640]{2,1,0,3:T(2,128)} %bitcast.32), calls=%async_computation | async-start | bytes 15728640 | tf_op jit(solution)/shard_map/all_to_all | solution.py:87
  25.6 1.3 collective-permute-start
  26.9 4.9 collective-permute-start.1
  31.8 14.4 %sine_multiply_fusion = (f32[1,640,1280]{2,1,0:T(8,128)S(1)}, f32[1,640,1280]{2,1,0:T(8,128)}) fusion(f32[640]{0:T(1024)S(1)} %fusion.63, f32[640]{0:T(1024)S(1)} %fusion.62), kind=kLoop, calls=%fused_computation.82 | loop fusion | flops 9011200 | bytes 6558720 | tf_op jit(solution)/shard_map/mul | solution.py:84
  46.2 67.6 %all-to-all-done = f32[4,2,320,640]{2,1,0,3:T(2,128)} async-done(((f32[4,2,320,640]{2,1,0,3:T(2,128)}), f32[4,2,320,640]{2,1,0,3:T(2,128)}, u32[]{:S(2)}, u32[]{:S(2)}) %all-to-all-start) | async-done | bytes 6553632 | tf_op jit(solution)/shard_map/all_to_all | solution.py:87
  113.9 12.4 %copy.10 = f32[4,2,2,320,320]{3,2,4,1,0:T(2,128)} copy(f32[4,2,2,320,320]{3,1,0,4,2:T(2,128)} %bitcast.4) | data formatting | bytes 13107200 | tf_op jit(solution)/shard_map/all_to_all | solution.py:87
  126.2 10.0 %all_to_all.16 = f32[4,2,640,320]{2,3,1,0:T(8,128)} reshape(f32[4,2,2,320,320]{3,2,4,1,0:T(2,128)} %copy.10) | data formatting | bytes 13107200 | tf_op jit(solution)/shard_map/all_to_all | solution.py:87
  136.3 31.1 %fusion.3 = f32[4,320,1280]{2,1,0:T(8,128)S(1)} fusion(f32[4,2,640,320]{2,3,1,0:T(8,128)} %all_to_all.16, f32[1,640,1280]{2,1,0:T(8,128)S(1)} %get-tuple-element.71, f32[1,640,1280]{2,1,0:T(8,128)} %get-tuple-element.72), kind=kOutput, calls=%fused_computation.8 | convolution fusion | flops 25167462400 | bytes 19660800 | tf_op jit(solution)/shard_map/crwh,rwn->chn/dot_general | solution.py:85
  167.4 2.2 fusion.53
  169.6 2.4 fusion.50
  173.1 1.3 collective-permute-start.2
  174.4 4.5 collective-permute-start.3
  180.3 4.0 broadcast_multiply_fusion.1
  185.4 1.3 collective-permute-start.4
  186.7 4.8 collective-permute-start.5
  192.6 2.7 fusion.34
  195.3 3.9 fusion.72
  199.2 1.3 collective-permute-start.6
  200.5 4.5 collective-permute-start.7
  206.4 10.7 %fusion.30 = (f32[2,320,1280]{2,1,0:T(8,128)}, f32[2,320,1280]{2,1,0:T(8,128)}) fusion(f32[2,320,1280]{2,1,0:T(8,128)S(1)} %fusion.34, f32[2,1,1280]{2,1,0:T(1,128)S(1)} %collective-permute-done.7, f32[2,1,1280]{2,1,0:T(1,128)S(1)} %collective-permute-done.6, f32[2,320,1]{2,1,0:T(8,128)} %get-tuple-element.27, f32[2,320,1279]{2,1,0:T(8,128)} %get-tuple-element.29, ...), kind=kLoop, calls=%fused_computation.49 | loop fusion | flops 22118400 | bytes 36070400 | tf_op jit(solution)/shard_map/div | solution.py:58
  218.1 5.7 fusion.69
  224.0 3.7 fusion.89
  227.7 1.3 collective-permute-start.8
  229.0 4.5 collective-permute-start.9
  233.6 1.3 collective-permute-start.10
  234.9 4.5 collective-permute-start.11
  239.4 3.1 fusion.42
  242.7 6.0 broadcast_multiply_fusion
  248.7 2.7 fusion.87
  251.4 1.3 collective-permute-start.12
  252.7 4.8 collective-permute-start.13
  258.2 1.9 multiply_add_fusion.5
  260.2 4.1 maximum_bitcast_fusion.2
  264.5 2.8 fusion.18
  267.3 3.7 fusion.84
  271.0 1.3 collective-permute-start.14
  272.3 4.5 collective-permute-start.15
  278.3 6.3 %fusion.14 = f32[2,320,1280]{2,1,0:T(8,128)S(1)} fusion(f32[2,320,1280]{2,1,0:T(8,128)S(1)} %fusion.18, f32[2,1,1280]{2,1,0:T(1,128)S(1)} %collective-permute-done.15, f32[2,1,1280]{2,1,0:T(1,128)S(1)} %collective-permute-done.14, f32[2,320,1]{2,1,0:T(8,128)S(1)} %get-tuple-element.54, f32[2,320,1279]{2,1,0:T(8,128)} %get-tuple-element.56, ...), kind=kLoop, calls=%fused_computation.24 | loop fusion | flops 17203200 | bytes 26240000 | tf_op jit(solution)/shard_map/div | solution.py:58
  285.8 1.3 collective-permute-start.16
  287.1 4.5 collective-permute-start.17
  294.6 1.8 slice-done
  296.6 4.3 pad_maximum_fusion
  300.9 20.1 %copy.11 = f32[2,3,320,1280]{2,0,1,3:T(2,128)} copy(f32[2,3,320,1280]{3,2,1,0:T(8,128)} %pad_maximum_fusion) | data formatting | bytes 19660800 | tf_op jit(solution)/shard_map/stack | solution.py:100
  322.9 221.5 %all-reduce.6.cloned.1.call-done = f32[2,3,320,1280]{2,0,1,3:T(2,128)} async-done(((f32[2,3,320,1280]{2,0,1,3:T(2,128)}), f32[2,3,320,1280]{2,0,1,3:T(2,128)}) %all-reduce.6.cloned.1.call-update) | async-done | bytes 9830416
  544.4 1.4 constant_dynamic-slice_fusion
  546.8 49.0 %all-gather.3.cloned.1.call-done = f32[2,1,320,1280]{2,0,1,3:T(2,128)} async-done(((f32[2,1,320,80]{2,0,1,3:T(2,128)}), f32[2,1,320,1280]{2,0,1,3:T(2,128)}) %all-gather.3.cloned.1.call-update) | async-done | bytes 3276816 | tf_op jit(solution)/shard_map/all_gather | solution.py:70
  595.9 7.4 %copy.14 = f32[2,320,1280]{2,1,0:T(8,128)} copy(f32[2,320,1280]{1,0,2:T(2,128)} %bitcast.35) | data formatting | bytes 6553600 | tf_op jit(solution)/shard_map/all_gather | solution.py:70
  (77 shorter events, 16.2 us)
Async XLA Ops:
  18.7 95.2 %all-to-all-start = ((f32[4,2,320,640]{2,1,0,3:T(2,128)}), f32[4,2,320,640]{2,1,0,3:T(2,128)}, u32[]{:S(2)}, u32[]{:S(2)}) async-start(f32[4,2,320,640]{2,1,0,3:T(2,128)} %bitcast.32), calls=%async_computation | async-start | bytes 15728640 | tf_op jit(solution)/shard_map/all_to_all | solution.py:87
  25.5 518.9 %all-reduce.6.cloned.1.call-start = ((), (), s32[]{:S(2)}) async-start(), calls=%async_computation.2 | async-start | bytes 23592960
  25.6 144.0 %collective-permute-start = (f32[2,1,1280]{2,1,0:T(1,128)S(1)}, f32[2,1,1280]{2,1,0:T(1,128)S(1)}, u32[]{:S(2)}, u32[]{:S(2)}) collective-permute-start(f32[2,1,1280]{2,1,0:T(1,128)S(1)} %broadcast.206), channel_id=1, source_target_pairs={{1,0},{3,2},{5,4},{7,6},{9,8},{11,10},{13,12},{15,14},{17,16},{19,... | collective-permute-start | bytes 30728 | tf_op jit(solution)/shard_map/ppermute | solution.py:22
  26.9 142.7 %collective-permute-start.1 = (f32[2,1,1280]{2,1,0:T(1,128)S(1)}, f32[2,1,1280]{2,1,0:T(1,128)S(1)}, u32[]{:S(2)}, u32[]{:S(2)}) collective-permute-start(f32[2,1,1280]{2,1,0:T(1,128)S(1)} %broadcast.206), channel_id=1, source_target_pairs={{0,1},{2,3},{4,5},{6,7},{8,9},{10,11},{12,13},{14,15},{16,17},{18,... | collective-permute-start | bytes 30728 | tf_op jit(solution)/shard_map/ppermute | solution.py:20
  169.6 23.0 %copy-start.4 = (f32[320,1280]{1,0:T(8,128)}, f32[320,1280]{1,0:T(8,128)S(1)}, u32[]{:S(2)}) copy-start(f32[320,1280]{1,0:T(8,128)S(1)} %get-tuple-element.15) | copy-start | bytes 4915204
  169.6 23.0 %copy-start.5 = (f32[320,1280]{1,0:T(8,128)}, f32[320,1280]{1,0:T(8,128)S(1)}, u32[]{:S(2)}) copy-start(f32[320,1280]{1,0:T(8,128)S(1)} %get-tuple-element.16) | copy-start | bytes 4915204
  173.1 6.0 collective-permute-start.2
  174.4 5.9 collective-permute-start.3
  185.4 6.2 %collective-permute-start.4 = (f32[2,1,1280]{2,1,0:T(1,128)S(1)}, f32[2,1,1280]{2,1,0:T(1,128)S(1)}, u32[]{:S(2)}, u32[]{:S(2)}) collective-permute-start(f32[2,1,1280]{2,1,0:T(1,128)S(1)} %get-tuple-element.36), channel_id=1, source_target_pairs={{1,0},{3,2},{5,4},{7,6},{9,8},{11,10},{13,12},{15,14},{17,16},{19,... | collective-permute-start | bytes 30728 | tf_op jit(solution)/shard_map/ppermute | solution.py:22
  186.7 5.9 collective-permute-start.5
  199.2 6.8 %collective-permute-start.6 = (f32[2,1,1280]{2,1,0:T(1,128)S(1)}, f32[2,1,1280]{2,1,0:T(1,128)S(1)}, u32[]{:S(2)}, u32[]{:S(2)}) collective-permute-start(f32[2,1,1280]{2,1,0:T(1,128)S(1)} %get-tuple-element.30), channel_id=1, source_target_pairs={{1,0},{3,2},{5,4},{7,6},{9,8},{11,10},{13,12},{15,14},{17,16},{19,... | collective-permute-start | bytes 30728 | tf_op jit(solution)/shard_map/ppermute | solution.py:22
  200.5 5.9 collective-permute-start.7
  218.1 5.7 copy-start
  218.1 5.9 copy-start.1
  227.7 29.8 %collective-permute-start.8 = (f32[2,1,1280]{2,1,0:T(1,128)S(1)}, f32[2,1,1280]{2,1,0:T(1,128)S(1)}, u32[]{:S(2)}, u32[]{:S(2)}) collective-permute-start(f32[2,1,1280]{2,1,0:T(1,128)S(1)} %get-tuple-element.24), channel_id=1, source_target_pairs={{1,0},{3,2},{5,4},{7,6},{9,8},{11,10},{13,12},{15,14},{17,16},{19,... | collective-permute-start | bytes 30728 | tf_op jit(solution)/shard_map/ppermute | solution.py:22
  229.0 28.5 %collective-permute-start.9 = (f32[2,1,1280]{2,1,0:T(1,128)S(1)}, f32[2,1,1280]{2,1,0:T(1,128)S(1)}, u32[]{:S(2)}, u32[]{:S(2)}) collective-permute-start(f32[2,1,1280]{2,1,0:T(1,128)S(1)} %get-tuple-element.25), channel_id=1, source_target_pairs={{0,1},{2,3},{4,5},{6,7},{8,9},{10,11},{12,13},{14,15},{16,17},{18,... | collective-permute-start | bytes 30728 | tf_op jit(solution)/shard_map/ppermute | solution.py:20
  233.6 9.1 %collective-permute-start.10 = (f32[2,1,1280]{2,1,0:T(1,128)S(1)}, f32[2,1,1280]{2,1,0:T(1,128)S(1)}, u32[]{:S(2)}, u32[]{:S(2)}) collective-permute-start(f32[2,1,1280]{2,1,0:T(1,128)S(1)} %get-tuple-element.69), channel_id=1, source_target_pairs={{1,0},{3,2},{5,4},{7,6},{9,8},{11,10},{13,12},{15,14},{17,16},{19,... | collective-permute-start | bytes 30728 | tf_op jit(solution)/shard_map/ppermute | solution.py:22
  234.9 7.8 %collective-permute-start.11 = (f32[2,1,1280]{2,1,0:T(1,128)S(1)}, f32[2,1,1280]{2,1,0:T(1,128)S(1)}, u32[]{:S(2)}, u32[]{:S(2)}) collective-permute-start(f32[2,1,1280]{2,1,0:T(1,128)S(1)} %get-tuple-element.70), channel_id=1, source_target_pairs={{0,1},{2,3},{4,5},{6,7},{8,9},{10,11},{12,13},{14,15},{16,17},{18,... | collective-permute-start | bytes 30728 | tf_op jit(solution)/shard_map/ppermute | solution.py:20
  239.4 3.3 copy-start.2
  239.4 3.3 copy-start.3
  251.4 13.0 %collective-permute-start.12 = (f32[2,1,1280]{2,1,0:T(1,128)S(1)}, f32[2,1,1280]{2,1,0:T(1,128)S(1)}, u32[]{:S(2)}, u32[]{:S(2)}) collective-permute-start(f32[2,1,1280]{2,1,0:T(1,128)S(1)} %get-tuple-element.63), channel_id=1, source_target_pairs={{1,0},{3,2},{5,4},{7,6},{9,8},{11,10},{13,12},{15,14},{17,16},{19,... | collective-permute-start | bytes 30728 | tf_op jit(solution)/shard_map/ppermute | solution.py:22
  252.7 11.7 %collective-permute-start.13 = (f32[2,1,1280]{2,1,0:T(1,128)S(1)}, f32[2,1,1280]{2,1,0:T(1,128)S(1)}, u32[]{:S(2)}, u32[]{:S(2)}) collective-permute-start(f32[2,1,1280]{2,1,0:T(1,128)S(1)} %get-tuple-element.64), channel_id=1, source_target_pairs={{0,1},{2,3},{4,5},{6,7},{8,9},{10,11},{12,13},{14,15},{16,17},{18,... | collective-permute-start | bytes 30728 | tf_op jit(solution)/shard_map/ppermute | solution.py:20
  260.2 4.3 copy-start.7
  267.3 10.9 %copy-start.6 = (f32[2,320,1280]{2,1,0:T(8,128)S(1)}, f32[2,320,1280]{2,1,0:T(8,128)}, u32[]{:S(2)}) copy-start(f32[2,320,1280]{2,1,0:T(8,128)} %get-tuple-element.8) | copy-start | bytes 9830404
  271.0 6.0 collective-permute-start.14
  272.3 5.9 collective-permute-start.15
  285.8 6.9 %collective-permute-start.16 = (f32[2,1,1280]{2,1,0:T(1,128)S(1)}, f32[2,1,1280]{2,1,0:T(1,128)S(1)}, u32[]{:S(2)}, u32[]{:S(2)}) collective-permute-start(f32[2,1,1280]{2,1,0:T(1,128)S(1)} %get-tuple-element.51), channel_id=1, source_target_pairs={{1,0},{3,2},{5,4},{7,6},{9,8},{11,10},{13,12},{15,14},{17,16},{19,... | collective-permute-start | bytes 30728 | tf_op jit(solution)/shard_map/ppermute | solution.py:22
  287.1 5.9 collective-permute-start.17
  294.3 2.2 slice-start
  294.3 2.4 slice-start.1
  321.0 0.7 copy-start.8
  321.0 274.9 %all-gather.3.cloned.1.call-start = ((), (), s32[]{:S(2)}) async-start(), calls=%async_computation.1 | async-start | bytes 4177920 | tf_op jit(solution)/shard_map/all_gather | solution.py:70
Sparse Core Ops, SparseCore 0:
  321.1 223.1 all-reduce.5
  547.0 48.8 all-gather.2
where the time goes:
time: 620 us; the launch traced here: 611 us
  waiting for transfers between devices  342 us (55%)
  local copies, waits for them, and re-layouts  93.4 us (15%)
  other arithmetic  68.5 us (11%)
  starting transfers between devices  60.2 us (10%)
  matrix products  31.1 us (5%)
  between operations  15 us (2%)
    unnamed x3, waiting for transfers between devices  222 us
    all_to_all x1, waiting for transfers between devices, per_device(): lax.all_to_all(stacked, 'band', split_axis=3, concat_axis=2, tiled=True)  67.6 us
    all_gather x1, waiting for transfers between devices, finish(): return lax.all_gather(exponent, 'mem', axis=2, tiled=True)  49 us
    ppermute x9, starting transfers between devices, padded(): lax.ppermute(tail, axis, [(i, (i + 1) % count) for i in range(ends)])  41.7 us
    dot_general x1, matrix products, per_device(): jnp.einsum('crwh,rwn->chn', lax.all_to_all(stacked, 'band', split_axis=3,...  31.1 us
    all_to_all x2, local copies, waits for them, and re-layouts, per_device(): lax.all_to_all(stacked, 'band', split_axis=3, concat_axis=2, tiled=True)  22.4 us
    another operation x1, local copies, waits for them, and re-layouts, per_device(): return finish(jnp.stack(partials))  20.1 us
    slice x13, local copies, waits for them, and re-layouts, slope(): east = (jnp.roll(center, -1, 2) - jnp.roll(center, 1, 2)) * 0.5  17.8 us
  transfers between devices with their start and end apart: 21, of which 8 were waited for; matrix products, arithmetic and copies ran while one was open for 13% of the time, Pallas kernels for 0%

commit v1 on v0

--- a/solution.py
+++ b/solution.py
@@ -1,12 +1,20 @@
+import functools
 import math
 
 import jax
 import jax.numpy as jnp
+import ml_dtypes
+import numpy as np
 from jax import lax
+from jax.experimental import pallas as pl
+from jax.experimental.pallas import tpu as pltpu
 from jax.sharding import PartitionSpec as P
 
 NLON = 1280
 STEPS = 1
+SUB = 8
+LANE = 128
+VMEM_LIMIT = 48 * 1024 * 1024
 
 
 def padded(cells, sides, width):
@@ -55,26 +63,24 @@
     second = slope(extend(0.5 * first), flow)
     third = slope(extend(0.5 * second), flow)
     fourth = slope(extend(third), flow)
-    shift = (first + 2.0 * second + 2.0 * third + fourth) / 6.0
-    return shift
-
-
-def finish(partial_sum):
-    members = lax.axis_size("mem")
-    summed = lax.psum_scatter(partial_sum, "mem", scatter_dimension=3, tiled=True) / members
-    first, cross, second = (summed[:, 0], summed[:, 1], summed[:, 2])
+    return (first + 2.0 * second + 2.0 * third + fourth) / 6.0
+
+
+def exponent_of(summed, members):
+    mean = summed / members
+    first, cross, second = (mean[..., 0, :, :], mean[..., 1, :, :], mean[..., 2, :, :])
     half = (first + second) * 0.5
     differ = (first - second) * 0.5
     largest = half + jnp.sqrt(differ * differ + cross * cross)
-    exponent = jnp.log(largest + 1e-06) / (2.0 * STEPS)
-    return lax.all_gather(exponent, "mem", axis=2, tiled=True)
-
-
-def per_device(coeffs):
+    return jnp.log(largest + 1e-06) / (2.0 * STEPS)
+
+
+def by_rows(coeffs):
     spec = coeffs[0]
     levels = spec.shape[0]
     nlat = spec.shape[4]
     waves = spec.shape[3] * lax.axis_size("band")
+    members = lax.axis_size("mem")
     stacked = spec.reshape(levels * 2, 2, spec.shape[3], nlat)
     wave_index = lax.iota(jnp.int32, waves)
     column = lax.iota(jnp.int32, NLON)
@@ -95,9 +101,286 @@
     for level in range(levels):
         flow = winds[level]
         shift = integrate(jnp.zeros_like(flow), flow, rimmed)
-        local = tensor(rimmed(shift))
-        partials.append(local)
-    return finish(jnp.stack(partials))
+        partials.append(tensor(rimmed(shift)))
+    summed = lax.psum_scatter(jnp.stack(partials), "mem", scatter_dimension=3, tiled=True)
+    return lax.all_gather(exponent_of(summed, members), "mem", axis=2, tiled=True)
+
+
+@functools.lru_cache(maxsize=None)
+def wave_table(bands, waves_local):
+    wave = np.arange(bands * waves_local, dtype=np.int64)
+    phase = (wave[:, None] * np.arange(NLON, dtype=np.int64)[None, :]) % NLON
+    angle = phase.astype(np.float64) * (2.0 * np.pi / NLON)
+    weight = np.where(wave == 0, 1.0, 2.0)[:, None]
+    table = np.stack([weight * np.cos(angle), -weight * np.sin(angle)])
+    table = table.reshape(2, bands, waves_local, NLON).transpose(1, 0, 2, 3).reshape(-1, NLON)
+    high = table.astype(ml_dtypes.bfloat16)
+    low = (table - high.astype(np.float64)).astype(ml_dtypes.bfloat16)
+    return high, low
+
+
+class Window:
+    def __init__(self, index, count, start, width, nlat):
+        self.first = index == 0
+        self.last = index == count - 1
+        self.width = width
+        self.extended = width + 2 * SUB
+        low = 0 if self.first else start + SUB
+        high = nlat if self.last else start + width + SUB
+        self.rows = high - low
+        self.row_at = (low, nlat - high)
+        base_up, base_down = start - SUB, nlat - start - width - SUB
+        self.place = (low - base_up, nlat - high - base_down)
+        self.side = "own" if 2 * (start + width) <= nlat else "other" if 2 * start >= nlat else "both"
+
+
+def plan(nlat, widths):
+    starts = np.cumsum([0] + widths[:-1])
+    return [Window(k, len(widths), int(starts[k]), widths[k], nlat) for k in range(len(widths))]
+
+
+def choose(band, pair):
+    return jnp.where(band == 0, pair[0], pair[1])
+
+
+def transpose_kernel(which, spec_ref, out_ref):
+    out_ref[0] = spec_ref[0, 0].T
+
+
+def rows_first(spec, level):
+    depth, nlat = spec.shape[2:]
+    return pl.pallas_call(
+        transpose_kernel,
+        grid_spec=pltpu.PrefetchScalarGridSpec(
+            num_scalar_prefetch=1,
+            grid=(2, nlat // LANE),
+            in_specs=[pl.BlockSpec((1, 1, depth, LANE), lambda c, t, which: (which[0], c, 0, t))],
+            out_specs=pl.BlockSpec((1, LANE, depth), lambda c, t, which: (c, t, 0)),
+        ),
+        out_shape=jax.ShapeDtypeStruct((2, nlat, depth), jnp.float32),
+        compiler_params=pltpu.CompilerParams(vmem_limit_bytes=VMEM_LIMIT),
+        cost_estimate=pl.CostEstimate(
+            flops=0, transcendentals=0, bytes_accessed=2 * 2 * nlat * depth * 4
+        ),
+        name="rows_first",
+    )(level.reshape(1), spec)
+
+
+def east_of(x):
+    return pltpu.roll(x, NLON - 1, axis=1) - pltpu.roll(x, 1, axis=1)
+
+
+def north_of(before, here, after):
+    row = lax.broadcasted_iota(jnp.int32, here.shape, 0)
+    above = jnp.where(row == SUB - 1, pltpu.roll(after, SUB - 1, axis=0), pltpu.roll(here, SUB - 1, axis=0))
+    below = jnp.where(row == 0, pltpu.roll(before, 1, axis=0), pltpu.roll(here, 1, axis=0))
+    return above - below
+
+
+def window_kernel(window, depth, *refs):
+    refs = list(refs)
+    band_ref, local_ref, remote_ref, high_ref, low_ref = refs[:5]
+    refs = refs[5:]
+    carry_ref = None if window.first else refs.pop(0)
+    tensor_ref = refs.pop(0)
+    carried_ref = None if window.last else refs.pop(0)
+    local_buf, lhs, lhs_high, lhs_low, wind, second, third, shift, sem = refs
+    band = band_ref[0]
+    rows, extended = window.rows, window.extended
+
+    def at(pair):
+        return pl.multiple_of(choose(band, pair).astype(jnp.int32), SUB)
+
+    fetch = pltpu.make_async_copy(local_ref.at[:, pl.ds(at(window.row_at), rows)], local_buf, sem)
+    fetch.start()
+    for c in range(2):
+        lhs[c * rows : (c + 1) * rows, pl.ds(pl.multiple_of((1 - band) * depth, LANE), depth)] = remote_ref[c]
+    fetch.wait()
+    for c in range(2):
+        lhs[c * rows : (c + 1) * rows, pl.ds(pl.multiple_of(band * depth, LANE), depth)] = local_buf[c]
+    lhs_high[...] = lhs[...].astype(jnp.bfloat16)
+    lhs_low[...] = (lhs[...] - lhs_high[...].astype(jnp.float32)).astype(jnp.bfloat16)
+
+    place = at(window.place)
+    if window.first or window.last:
+        for c in range(2):
+            if window.first:
+                wind[c, pl.ds(at((0, extended - SUB)), SUB), :] = jnp.zeros((SUB, NLON), jnp.float32)
+            if window.last:
+                wind[c, pl.ds(at((extended - SUB, 0)), SUB), :] = jnp.zeros((SUB, NLON), jnp.float32)
+    if not window.first:
+        for c in range(2):
+            wind[c, pl.ds(at((0, extended - 2 * SUB)), 2 * SUB), :] = carry_ref[c]
+
+    @pl.loop(0, NLON // 256)
+    def _(tile):
+        columns = pl.ds(pl.multiple_of(tile * 256, 256), 256)
+        dot = functools.partial(jnp.dot, preferred_element_type=jnp.float32)
+        total = dot(lhs_high[...], high_ref[:, columns])
+        total += dot(lhs_low[...], high_ref[:, columns])
+        total += dot(lhs_high[...], low_ref[:, columns])
+        for c in range(2):
+            wind[c, pl.ds(place, rows), columns] = total[c * rows : (c + 1) * rows]
+
+    if not window.last:
+        for c in range(2):
+            carried_ref[c] = wind[c, pl.ds(at((extended - 2 * SUB, 0)), 2 * SUB), :]
+
+    blocks = extended // SUB
+
+    def rows_of(block):
+        return pl.ds(pl.multiple_of(block * SUB, SUB), SUB)
+
+    def derivatives(field, block):
+        before, after = jnp.maximum(block - 1, 0), jnp.minimum(block + 1, blocks - 1)
+        result = []
+        for c in range(2):
+            here = field[c, rows_of(block), :]
+            result.append((east_of(here), north_of(field[c, rows_of(before), :], here, field[c, rows_of(after), :])))
+        return result
+
+    @pl.loop(0, blocks)
+    def _(block):
+        flow = [wind[c, rows_of(block), :] for c in range(2)]
+        for c, (east, north) in enumerate(derivatives(wind, block)):
+            second[c, rows_of(block), :] = 0.25 * (flow[0] * east + flow[1] * north) - flow[c]
+
+    @pl.loop(0, blocks)
+    def _(block):
+        flow = [wind[c, rows_of(block), :] for c in range(2)]
+        for c, (east, north) in enumerate(derivatives(second, block)):
+            third[c, rows_of(block), :] = -flow[c] - 0.25 * (flow[0] * east + flow[1] * north)
+
+    @pl.loop(0, blocks)
+    def _(block):
+        flow = [wind[c, rows_of(block), :] for c in range(2)]
+        for c, (east, north) in enumerate(derivatives(third, block)):
+            fourth = -flow[c] - 0.5 * (flow[0] * east + flow[1] * north)
+            both = second[c, rows_of(block), :] + third[c, rows_of(block), :]
+            shift[c, rows_of(block), :] = (2.0 * both + (fourth - flow[c])) * (1.0 / 6.0)
+
+    @pl.loop(0, blocks - 2)
+    def _(block):
+        (e0, n0), (e1, n1) = derivatives(shift, block + 1)
+        g_xx, g_xy, g_yx, g_yy = 1.0 + 0.5 * e0, 0.5 * n0, 0.5 * e1, 1.0 + 0.5 * n1
+        tensor_ref[0, rows_of(block), :] = g_xx * g_xx + g_yx * g_yx
+        tensor_ref[1, rows_of(block), :] = g_xx * g_xy + g_yx * g_yy
+        tensor_ref[2, rows_of(block), :] = g_xy * g_xy + g_yy * g_yy
+
+
+def window_tensor(window, band, local, remote, table, carry):
+    depth = local.shape[2]
+    vmem = pl.BlockSpec(memory_space=pltpu.VMEM)
+    in_specs = [
+        pl.BlockSpec(memory_space=pltpu.SMEM),
+        pl.BlockSpec(memory_space=pl.ANY),
+        vmem,
+        vmem,
+        vmem,
+    ]
+    operands = [band.reshape(1), local, remote, *table]
+    if not window.first:
+        in_specs.append(vmem)
+        operands.append(carry)
+    out_shape = [jax.ShapeDtypeStruct((3, window.width, NLON), jnp.float32)]
+    if not window.last:
+        out_shape.append(jax.ShapeDtypeStruct((2, 2 * SUB, NLON), jnp.float32))
+    field = pltpu.VMEM((2, window.extended, NLON), jnp.float32)
+    lhs_shape = (2 * window.rows, 2 * depth)
+    out = pl.pallas_call(
+        functools.partial(window_kernel, window, depth),
+        out_shape=out_shape,
+        in_specs=in_specs,
+        out_specs=[vmem] * len(out_shape),
+        scratch_shapes=[
+            pltpu.VMEM((2, window.rows, depth), jnp.float32),
+            pltpu.VMEM(lhs_shape, jnp.float32),
+            pltpu.VMEM(lhs_shape, jnp.bfloat16),
+            pltpu.VMEM(lhs_shape, jnp.bfloat16),
+            field,
+            field,
+            field,
+            field,
+            pltpu.SemaphoreType.DMA,
+        ],
+        compiler_params=pltpu.CompilerParams(vmem_limit_bytes=VMEM_LIMIT),
+        cost_estimate=pl.CostEstimate(
+            flops=3 * 2 * lhs_shape[0] * lhs_shape[1] * NLON,
+            transcendentals=0,
+            bytes_accessed=4 * NLON * lhs_shape[1] + 8 * lhs_shape[0] * depth + 12 * window.width * NLON,
+        ),
+        name="window_tensor",
+    )(*operands)
+    return out[0], (None if window.last else out[1])
+
+
+def by_levels(coeffs):
+    spec = coeffs[0]
+    levels, _, parts, waves_local, nlat = spec.shape
+    members = lax.axis_size("mem")
+    band = lax.axis_index("band").astype(jnp.int32)
+    spec = spec.reshape(levels, 2, parts * waves_local, nlat)
+    windows = plan(nlat, [LANE] * (nlat // LANE))
+    table = [jnp.asarray(part) for part in wave_table(levels, waves_local)]
+    swap = [(0, 1), (1, 0)]
+
+    outgoing = rows_first(spec, 1 - band)
+    remotes = []
+    for window in windows:
+        piece = lax.dynamic_slice_in_dim(outgoing, choose(1 - band, window.row_at), window.rows, axis=1)
+        remotes.append(lax.ppermute(piece, "band", swap))
+    local = rows_first(spec, band)
+
+    carry = None
+    pieces = {"own": [], "both": [], "other": []}
+    for window, remote in zip(windows, remotes):
+        partial_sum, carry = window_tensor(window, band, local, remote, table, carry)
+        summed = lax.psum_scatter(partial_sum, "mem", scatter_dimension=1, tiled=True)
+        pieces[window.side].append(exponent_of(summed, members))
+
+    other = lax.ppermute(jnp.stack(pieces["other"]), "band", swap)
+    half = members // 2
+    trades = []
+    for member in range(members):
+        for side in range(2):
+            keeps = (member < half) == (side == 0)
+            mate = (member, side) if keeps else ((member + half) % members, 1 - side)
+            trades.append((member * 2 + side, mate[0] * 2 + mate[1]))
+    both = lax.ppermute(pieces["both"][0], ("mem", "band"), trades)
+
+    def gathered(stack):
+        count, height, _ = stack.shape
+        whole = lax.all_gather(stack, "mem", axis=1, tiled=True)
+        return whole.reshape(count, members * height, NLON)
+
+    own = gathered(jnp.stack(pieces["own"]))
+    late = gathered(jnp.concatenate([other, both[None]]))
+    other, both = late[:-1], late[-1]
+    middle = both.shape[0] // 2
+    low, high = both[:middle], both[middle:]
+
+    up = jnp.stack(
+        [
+            jnp.concatenate([*own, low]),
+            jnp.concatenate([*other[::-1], high]),
+        ]
+    )
+    down = jnp.stack(
+        [
+            jnp.concatenate([low, *other]),
+            jnp.concatenate([high, *own[::-1]]),
+        ]
+    )
+    return jnp.where(band == 0, up, down)
+
+
+def per_device(coeffs):
+    _, levels, _, _, _, nlat = coeffs.shape
+    members = lax.axis_size("mem")
+    rows = nlat // lax.axis_size("band")
+    if levels == lax.axis_size("band") == 2 and LANE % (members * SUB) == 0 and nlat % (2 * LANE) == LANE and rows > LANE:
+        return by_levels(coeffs)
+    return by_rows(coeffs)
 
 
 def solution(mesh):

time: 620 us -> 461 us (0.74); the launches traced: 611 us -> 460 us
  Pallas kernels: 0 us -> 93.9 us
  local copies, waits for them, and re-layouts: 93.4 us -> 11.1 us
  other arithmetic: 68.5 us -> 8.69 us
  starting transfers between devices: 60.2 us -> 10.7 us
  matrix products: 31.1 us -> 0 us
  waiting for transfers between devices: 342 us -> 322 us
    unnamed x3 -> x7, waiting for transfers between devices: 222 us -> 0.63 us
    reduce_scatter x0 -> x5, waiting for transfers between devices: none -> 195 us  [by_levels(): lax.psum_scatter(partial_sum, 'mem', scatter_dimension=1, tiled=True)]
    pallas_call x0 -> x7, Pallas kernels: none -> 93.9 us  [the longest x5 81.9 us: window_tensor(): pl.pallas_call(functools.partial(window_kernel, window, depth), out_shape...]
    all_to_all x1 -> x0, waiting for transfers between devices: 67.6 us -> none  [per_device(): lax.all_to_all(stacked, 'band', split_axis=3, concat_axis=2, tiled=True)]
    ppermute x18 -> x7, waiting for transfers between devices: 4.21 us -> 48.5 us  [the longest x5 48.5 us: by_levels(): remotes.append(lax.ppermute(piece, 'band', swap))]
    ppermute x18 -> x7, starting transfers between devices: 53.3 us -> 10.4 us  [the longest x5 8.23 us: by_levels(): remotes.append(lax.ppermute(piece, 'band', swap))]
    mul x9 -> x0, other arithmetic: 34.4 us -> none  [the longest x1 14.4 us: per_device(): -weight * jnp.sin(angle)]
    dot_general x1 -> x0, matrix products: 31.1 us -> none  [per_device(): jnp.einsum('crwh,rwn->chn', lax.all_to_all(stacked, 'band', split_axis=3,...]
  transfers between devices with their start and end apart: 21 -> 14, of which waited for: 8 -> 10; matrix products, arithmetic and copies ran while one was open for 13% -> 2% of each run, Pallas kernels for 0% -> 16%
where the time goes in v1:
time: 461 us; the launch traced here: 460 us
  waiting for transfers between devices  322 us (70%)
  Pallas kernels  93.9 us (20%)
  between operations  13.8 us (3%)
  local copies, waits for them, and re-layouts  11.1 us (2%)
  starting transfers between devices  10.7 us (2%)
  other arithmetic  8.69 us (2%)
    reduce_scatter x5, waiting for transfers between devices, by_levels(): lax.psum_scatter(partial_sum, 'mem', scatter_dimension=1, tiled=True)  195 us
    pallas_call x5, Pallas kernels, window_tensor(): pl.pallas_call(functools.partial(window_kernel, window, depth), out_shape...  81.9 us
    all_gather x2, waiting for transfers between devices, gathered(): whole = lax.all_gather(stack, 'mem', axis=1, tiled=True)  78.4 us
    ppermute x5, waiting for transfers between devices, by_levels(): remotes.append(lax.ppermute(piece, 'band', swap))  48.5 us
    pallas_call x2, Pallas kernels, rows_first(): pl.pallas_call(transpose_kernel, grid_spec=pltpu.PrefetchScalarGridSpec(n...  12 us
  transfers between devices with their start and end apart: 14, of which 10 were waited for; matrix products, arithmetic and copies ran while one was open for 2% of the time, Pallas kernels for 16%

profile of v1, /device:TPU:0, one launch (start us, length us, event | category | flops | bytes accessed | tf_op | source)
XLA Modules:
  0.0 460.1 jit_solution(17223544541622219682)
XLA Ops:
  6.5 6.0 %rows_first.3 = f32[2,640,640]{2,1,0:T(8,128)S(1)} custom-call(s32[1]{0:T(128)} %bitcast.2.which, f32[2,2,640,640]{3,2,1,0:T(8,128)} %bitcast.26), custom_call_target="tpu_custom_call" | custom-call | bytes 6553600 | tf_op jit(solution)/shard_map/rows_first/pallas_call | solution.py:152
  12.6 0.1 constant_dynamic-slice_fusion.4
  12.6 3.0 collective-permute-start
  15.6 6.0 %rows_first.2.refs_1_ = f32[2,640,640]{2,1,0:T(8,128)S(1)} custom-call(s32[1]{0:T(128)} %bitcast.which.refs_0_, f32[2,2,640,640]{3,2,1,0:T(8,128)} %bitcast.27), custom_call_target="tpu_custom_call" | custom-call | bytes 6553600 | tf_op jit(solution)/shard_map/rows_first/pallas_call | solution.py:152
  21.6 9.6 %collective-permute-done.refs_2_ = f32[2,136,640]{2,1,0:T(8,128)S(1)} collective-permute-done((f32[2,136,640]{2,1,0:T(8,128)S(1)}, f32[2,136,640]{2,1,0:T(8,128)S(1)}, u32[]{:S(2)}, u32[]{:S(2)}) %collective-permute-start) | collective-permute-done | bytes 696352 | tf_op jit(solution)/shard_map/ppermute | solution.py:331
  31.2 15.4 %window_tensor.5 = (f32[3,128,1280]{2,1,0:T(8,128)S(1)}, f32[2,16,1280]{2,1,0:T(8,128)S(1)}) custom-call(s32[1]{0:T(128)} %bitcast.which.refs_0_, f32[2,640,640]{2,1,0:T(8,128)S(1)} %rows_first.2.refs_1_, f32[2,136,640]{2,1,0:T(8,128)S(1)} %collective-permute-done.refs_2_, bf16[1280,1280]{1,0:T(8,128)(2,1)} %constant.51.clone.refs_3_, ...), custom_call_target="tpu_custom_call" | custom-call | flops 2673868800 | bytes 9912320 | tf_op jit(solution)/shard_map/window_tensor/pallas_call | solution.py:290
  46.7 1.3 copy-done.4
  48.0 0.0 reduce-scatter.8.cloned.1.call-start
  48.1 1.2 constant_dynamic-slice_fusion.2
  49.3 1.7 collective-permute-start.1
  51.0 14.2 %collective-permute-done.1.refs_2_ = f32[2,128,640]{2,1,0:T(8,128)S(1)} collective-permute-done((f32[2,128,640]{2,1,0:T(8,128)S(1)}, f32[2,128,640]{2,1,0:T(8,128)S(1)}, u32[]{:S(2)}, u32[]{:S(2)}) %collective-permute-start.1) | collective-permute-done | bytes 655392 | tf_op jit(solution)/shard_map/ppermute | solution.py:331
  65.2 17.6 %window_tensor.6 = (f32[3,128,1280]{2,1,0:T(8,128)}, f32[2,16,1280]{2,1,0:T(8,128)S(1)}) custom-call(s32[1]{0:T(128)} %bitcast.which.refs_0_, f32[2,640,640]{2,1,0:T(8,128)} %copy-done, f32[2,128,640]{2,1,0:T(8,128)S(1)} %collective-permute-done.1.refs_2_, bf16[1280,1280]{1,0:T(8,128)(2,1)} %constant.51.clone.refs_3_, ...), custom_call_target="tpu_custom_call" | custom-call | flops 2516582400 | bytes 9830400 | tf_op jit(solution)/shard_map/window_tensor/pallas_call | solution.py:290
  82.9 0.0 reduce-scatter.10.cloned.1.call-start
  82.9 1.0 copy-done.7
  83.9 1.4 collective-permute-start.3
  85.3 0.6 collective-permute-start.2
  85.9 15.6 %collective-permute-done.3.refs_2_ = f32[2,128,640]{2,1,0:T(8,128)S(1)} collective-permute-done((f32[2,128,640]{2,1,0:T(8,128)S(1)}, f32[2,128,640]{2,1,0:T(8,128)S(1)}, u32[]{:S(2)}, u32[]{:S(2)}) %collective-permute-start.3) | collective-permute-done | bytes 655392 | tf_op jit(solution)/shard_map/ppermute | solution.py:331
  101.6 17.4 %window_tensor.7 = (f32[3,128,1280]{2,1,0:T(8,128)}, f32[2,16,1280]{2,1,0:T(8,128)S(1)}) custom-call(s32[1]{0:T(128)} %bitcast.which.refs_0_, f32[2,640,640]{2,1,0:T(8,128)} %copy-done, f32[2,128,640]{2,1,0:T(8,128)S(1)} %collective-permute-done.3.refs_2_, bf16[1280,1280]{1,0:T(8,128)(2,1)} %constant.51.clone.refs_3_, ...), custom_call_target="tpu_custom_call" | custom-call | flops 2516582400 | bytes 9830400 | tf_op jit(solution)/shard_map/window_tensor/pallas_call | solution.py:290
  119.0 16.4 %window_tensor.8 = (f32[3,128,1280]{2,1,0:T(8,128)S(1)}, f32[2,16,1280]{2,1,0:T(8,128)S(1)}) custom-call(s32[1]{0:T(128)} %bitcast.which.refs_0_, f32[2,640,640]{2,1,0:T(8,128)} %copy-done, f32[2,128,640]{2,1,0:T(8,128)S(1)} %collective-permute-done.2.refs_2_, bf16[1280,1280]{1,0:T(8,128)(2,1)} %constant.51.clone.refs_3_, ...), custom_call_target="tpu_custom_call" | custom-call | flops 2516582400 | bytes 9830400 | tf_op jit(solution)/shard_map/window_tensor/pallas_call | solution.py:290
  135.4 1.3 copy-done.5
  136.7 0.0 reduce-scatter.12.cloned.1.call-start
  136.8 1.1 constant_dynamic-slice_fusion
  137.9 1.5 collective-permute-start.4
  139.4 9.1 %collective-permute-done.4.refs_2_ = f32[2,120,640]{2,1,0:T(8,128)S(1)} collective-permute-done((f32[2,120,640]{2,1,0:T(8,128)S(1)}, f32[2,120,640]{2,1,0:T(8,128)S(1)}, u32[]{:S(2)}, u32[]{:S(2)}) %collective-permute-start.4) | collective-permute-done | bytes 614432 | tf_op jit(solution)/shard_map/ppermute | solution.py:331
  148.4 15.0 %window_tensor.9 = f32[3,128,1280]{2,1,0:T(8,128)S(1)} custom-call(s32[1]{0:T(128)} %bitcast.which.refs_0_, f32[2,640,640]{2,1,0:T(8,128)S(1)} %copy-done.1, f32[2,120,640]{2,1,0:T(8,128)S(1)} %collective-permute-done.4.refs_2_, bf16[1280,1280]{1,0:T(8,128)(2,1)} %constant.51.clone.refs_3_, bf16[1280,1280]{1,0:T(8,128)(2,1)} %constant.52.clone.refs_4_, ...), custom_call_target="tpu_custom_call" | custom-call | flops 2359296000 | bytes 9748480 | tf_op jit(solution)/shard_map/window_tensor/pallas_call | solution.py:290
  163.5 1.3 copy-done.3
  164.8 0.5 reduce-scatter.14.cloned.1.call-update
  165.4 0.9 broadcast_multiply_fusion.4
  166.4 8.2 %reduce-scatter.8.cloned.1.call-done = f32[3,8,1280]{2,1,0:T(8,128)} async-done(((f32[3,128,1280]{2,1,0:T(8,128)}), f32[3,8,1280]{2,1,0:T(8,128)}) %reduce-scatter.8.cloned.1.call-update) | async-done | bytes 122896 | tf_op jit(solution)/shard_map/reduce_scatter | solution.py:338
  174.6 0.9 broadcast_multiply_fusion.3
  175.6 0.6 pad_maximum_fusion.1
  176.2 0.0 all-gather.5.cloned.1.call-start
  176.3 62.3 %reduce-scatter.10.cloned.1.call-done = f32[3,8,1280]{2,1,0:T(8,128)} async-done(((f32[3,128,1280]{2,1,0:T(8,128)}), f32[3,8,1280]{2,1,0:T(8,128)}) %reduce-scatter.10.cloned.1.call-update) | async-done | bytes 122896 | tf_op jit(solution)/shard_map/reduce_scatter | solution.py:338
  238.6 0.9 broadcast_multiply_fusion.2
  239.6 62.8 %reduce-scatter.12.cloned.1.call-done = f32[3,8,1280]{2,1,0:T(8,128)} async-done(((f32[3,128,1280]{2,1,0:T(8,128)}), f32[3,8,1280]{2,1,0:T(8,128)}) %reduce-scatter.12.cloned.1.call-update) | async-done | bytes 122896 | tf_op jit(solution)/shard_map/reduce_scatter | solution.py:338
  302.3 0.9 broadcast_multiply_fusion.1
  303.3 1.5 collective-permute-start.5
  304.8 61.2 %reduce-scatter.14.cloned.1.call-done = f32[3,8,1280]{2,1,0:T(8,128)} async-done(((f32[3,128,1280]{2,1,0:T(8,128)}), f32[3,8,1280]{2,1,0:T(8,128)}) %reduce-scatter.14.cloned.1.call-update) | async-done | bytes 122896 | tf_op jit(solution)/shard_map/reduce_scatter | solution.py:338
  366.0 0.9 broadcast_multiply_fusion
  367.0 0.7 collective-permute-start.6
  367.7 0.7 pad_maximum_fusion
  368.4 37.7 %all-gather.3.cloned.1.call-done = f32[2,128,1280]{2,1,0:T(8,128)} async-done(((f32[2,8,1280]{2,1,0:T(8,128)}), f32[2,128,1280]{2,1,0:T(8,128)}) %all-gather.3.cloned.1.call-update) | async-done | bytes 1310736 | tf_op jit(solution)/shard_map/all_gather | solution.py:353
  406.1 1.4 slice_bitcast_fusion.3
  407.5 40.6 %all-gather.5.cloned.1.call-done = f32[3,128,1280]{2,1,0:T(8,128)} async-done(((f32[3,8,1280]{2,1,0:T(8,128)}), f32[3,128,1280]{2,1,0:T(8,128)}) %all-gather.5.cloned.1.call-update) | async-done | bytes 1966096 | tf_op jit(solution)/shard_map/all_gather | solution.py:353
  448.1 1.1 slice_bitcast_fusion.5
  449.2 1.4 slice_bitcast_fusion.1
  450.6 0.5 maximum_bitcast_fusion.3
  451.1 2.1 maximum_select_fusion
  (31 shorter events, 0.4 us)
Async XLA Ops:
  6.5 158.9 %reduce-scatter.6.cloned.1.call-start = ((), (), s32[]{:S(2)}) async-start(), calls=%async_computation.5 | async-start | bytes 2088960 | tf_op jit(solution)/shard_map/reduce_scatter | solution.py:338
  12.5 35.5 %copy-start.2 = (f32[2,640,640]{2,1,0:T(8,128)}, f32[2,640,640]{2,1,0:T(8,128)S(1)}, u32[]{:S(2)}) copy-start(f32[2,640,640]{2,1,0:T(8,128)S(1)} %rows_first.3) | copy-start | bytes 9830404
  12.6 18.6 %collective-permute-start = (f32[2,136,640]{2,1,0:T(8,128)S(1)}, f32[2,136,640]{2,1,0:T(8,128)S(1)}, u32[]{:S(2)}, u32[]{:S(2)}) collective-permute-start(f32[2,136,640]{2,1,0:T(8,128)S(1)} %constant_dynamic-slice_fusion.4), channel_id=1, source_target_pairs={{0,1},{1,0},{2,3},{3,2},{4,5},{5,4},{6,7},{7,6},{8,9},{9,8},{10,11... | collective-permute-start | bytes 2088968 | tf_op jit(solution)/shard_map/ppermute | solution.py:331
  21.6 25.0 %copy-start = (f32[2,640,640]{2,1,0:T(8,128)}, f32[2,640,640]{2,1,0:T(8,128)S(1)}, u32[]{:S(2)}) copy-start(f32[2,640,640]{2,1,0:T(8,128)S(1)} %rows_first.2.refs_1_) | copy-start | bytes 9830404
  46.7 1.3 copy-start.4
  48.0 126.6 %reduce-scatter.8.cloned.1.call-start = ((), (), s32[]{:S(2)}) async-start(), calls=%async_computation.6 | async-start | bytes 2088960 | tf_op jit(solution)/shard_map/reduce_scatter | solution.py:338
  49.3 15.9 %collective-permute-start.1 = (f32[2,128,640]{2,1,0:T(8,128)S(1)}, f32[2,128,640]{2,1,0:T(8,128)S(1)}, u32[]{:S(2)}, u32[]{:S(2)}) collective-permute-start(f32[2,128,640]{2,1,0:T(8,128)S(1)} %get-tuple-element.23), channel_id=1, source_target_pairs={{0,1},{1,0},{2,3},{3,2},{4,5},{5,4},{6,7},{7,6},{8,9},{9,8},{10,11... | collective-permute-start | bytes 1966088 | tf_op jit(solution)/shard_map/ppermute | solution.py:331
  82.8 1.1 copy-start.7
  82.8 2.5 copy-start.6
  82.9 155.7 %reduce-scatter.10.cloned.1.call-start = ((), (), s32[]{:S(2)}) async-start(), calls=%async_computation.8 | async-start | bytes 2088960 | tf_op jit(solution)/shard_map/reduce_scatter | solution.py:338
  83.9 17.7 %collective-permute-start.3 = (f32[2,128,640]{2,1,0:T(8,128)S(1)}, f32[2,128,640]{2,1,0:T(8,128)S(1)}, u32[]{:S(2)}, u32[]{:S(2)}) collective-permute-start(f32[2,128,640]{2,1,0:T(8,128)S(1)} %copy-done.7), channel_id=1, source_target_pairs={{0,1},{1,0},{2,3},{3,2},{4,5},{5,4},{6,7},{7,6},{8,9},{9,8},{10,11... | collective-permute-start | bytes 1966088 | tf_op jit(solution)/shard_map/ppermute | solution.py:331
  85.3 33.7 %collective-permute-start.2 = (f32[2,128,640]{2,1,0:T(8,128)S(1)}, f32[2,128,640]{2,1,0:T(8,128)S(1)}, u32[]{:S(2)}, u32[]{:S(2)}) collective-permute-start(f32[2,128,640]{2,1,0:T(8,128)S(1)} %copy-done.6), channel_id=1, source_target_pairs={{0,1},{1,0},{2,3},{3,2},{4,5},{5,4},{6,7},{7,6},{8,9},{9,8},{10,11... | collective-permute-start | bytes 1966088 | tf_op jit(solution)/shard_map/ppermute | solution.py:331
  119.0 29.4 %copy-start.1 = (f32[2,640,640]{2,1,0:T(8,128)S(1)}, f32[2,640,640]{2,1,0:T(8,128)}, u32[]{:S(2)}) copy-start(f32[2,640,640]{2,1,0:T(8,128)} %copy-done) | copy-start | bytes 9830404
  135.4 1.3 copy-start.5
  136.7 165.6 %reduce-scatter.12.cloned.1.call-start = ((), (), s32[]{:S(2)}) async-start(), calls=%async_computation.9 | async-start | bytes 2088960 | tf_op jit(solution)/shard_map/reduce_scatter | solution.py:338
  137.9 10.5 %collective-permute-start.4 = (f32[2,120,640]{2,1,0:T(8,128)S(1)}, f32[2,120,640]{2,1,0:T(8,128)S(1)}, u32[]{:S(2)}, u32[]{:S(2)}) collective-permute-start(f32[2,120,640]{2,1,0:T(8,128)S(1)} %constant_dynamic-slice_fusion), channel_id=1, source_target_pairs={{0,1},{1,0},{2,3},{3,2},{4,5},{5,4},{6,7},{7,6},{8,9},{9,8},{10,11... | collective-permute-start | bytes 1843208 | tf_op jit(solution)/shard_map/ppermute | solution.py:331
  163.5 1.3 copy-start.3
  164.8 201.3 %reduce-scatter.14.cloned.1.call-start = ((), (), s32[]{:S(2)}) async-start(), calls=%async_computation.10 | async-start | bytes 2088960 | tf_op jit(solution)/shard_map/reduce_scatter | solution.py:338
  165.4 240.7 %all-gather.3.cloned.1.call-start = ((), (), s32[]{:S(2)}) async-start(), calls=%async_computation.7 | async-start | bytes 1392640 | tf_op jit(solution)/shard_map/all_gather | solution.py:353
  176.2 271.9 %all-gather.5.cloned.1.call-start = ((), (), s32[]{:S(2)}) async-start(), calls=%async_computation.11 | async-start | bytes 2088960 | tf_op jit(solution)/shard_map/all_gather | solution.py:353
  303.3 64.4 %collective-permute-start.5 = (f32[2,8,1280]{2,1,0:T(8,128)S(1)}, f32[2,8,1280]{2,1,0:T(8,128)S(1)}, u32[]{:S(2)}, u32[]{:S(2)}) collective-permute-start(f32[2,8,1280]{2,1,0:T(8,128)S(1)} %pad_maximum_fusion.2), channel_id=1, source_target_pairs={{0,1},{1,0},{2,3},{3,2},{4,5},{5,4},{6,7},{7,6},{8,9},{9,8},{10,11... | collective-permute-start | bytes 245768 | tf_op jit(solution)/shard_map/ppermute | solution.py:341
  367.0 0.7 collective-permute-start.6
Sparse Core Ops, SparseCore 0:
  48.1 62.5 reduce-scatter.5
  114.5 60.1 reduce-scatter.7
  178.4 60.1 reduce-scatter.9
  242.2 60.0 reduce-scatter.11
  305.9 60.0 reduce-scatter.13
  368.2 37.8 all-gather.2
  408.4 39.6 all-gather.4

commit v2 on v1

--- a/solution.py
+++ b/solution.py
@@ -14,7 +14,7 @@
 STEPS = 1
 SUB = 8
 LANE = 128
-VMEM_LIMIT = 48 * 1024 * 1024
+VMEM_LIMIT = 24 * 1024 * 1024
 
 
 def padded(cells, sides, width):
@@ -143,27 +143,27 @@
     return jnp.where(band == 0, pair[0], pair[1])
 
 
-def transpose_kernel(which, spec_ref, out_ref):
+def transpose_kernel(place, spec_ref, out_ref):
     out_ref[0] = spec_ref[0, 0].T
 
 
-def rows_first(spec, level):
-    depth, nlat = spec.shape[2:]
+def rows_first(spec, level, block, width):
+    depth = spec.shape[2]
     return pl.pallas_call(
         transpose_kernel,
         grid_spec=pltpu.PrefetchScalarGridSpec(
             num_scalar_prefetch=1,
-            grid=(2, nlat // LANE),
-            in_specs=[pl.BlockSpec((1, 1, depth, LANE), lambda c, t, which: (which[0], c, 0, t))],
-            out_specs=pl.BlockSpec((1, LANE, depth), lambda c, t, which: (c, t, 0)),
+            grid=(2, width // LANE),
+            in_specs=[pl.BlockSpec((1, 1, depth, LANE), lambda c, t, place: (place[0], c, 0, place[1] + t))],
+            out_specs=pl.BlockSpec((1, LANE, depth), lambda c, t, place: (c, t, 0)),
         ),
-        out_shape=jax.ShapeDtypeStruct((2, nlat, depth), jnp.float32),
+        out_shape=jax.ShapeDtypeStruct((2, width, depth), jnp.float32),
         compiler_params=pltpu.CompilerParams(vmem_limit_bytes=VMEM_LIMIT),
         cost_estimate=pl.CostEstimate(
-            flops=0, transcendentals=0, bytes_accessed=2 * 2 * nlat * depth * 4
+            flops=0, transcendentals=0, bytes_accessed=8 * 2 * width * depth * 4
         ),
         name="rows_first",
-    )(level.reshape(1), spec)
+    )(jnp.stack([level, jnp.asarray(block, jnp.int32)]), spec)
 
 
 def east_of(x):
@@ -179,13 +179,13 @@
 
 def window_kernel(window, depth, *refs):
     refs = list(refs)
-    band_ref, local_ref, remote_ref, high_ref, low_ref = refs[:5]
+    place_ref, local_ref, remote_ref, high_ref, low_ref = refs[:5]
     refs = refs[5:]
     carry_ref = None if window.first else refs.pop(0)
-    tensor_ref = refs.pop(0)
+    keep_ref, send_ref = refs.pop(0), refs.pop(0)
     carried_ref = None if window.last else refs.pop(0)
     local_buf, lhs, lhs_high, lhs_low, wind, second, third, shift, sem = refs
-    band = band_ref[0]
+    band, core = place_ref[0], place_ref[1]
     rows, extended = window.rows, window.extended
 
     def at(pair):
@@ -239,19 +239,19 @@
             result.append((east_of(here), north_of(field[c, rows_of(before), :], here, field[c, rows_of(after), :])))
         return result
 
-    @pl.loop(0, blocks)
+    @pl.loop(0, blocks, unroll=3)
     def _(block):
         flow = [wind[c, rows_of(block), :] for c in range(2)]
         for c, (east, north) in enumerate(derivatives(wind, block)):
             second[c, rows_of(block), :] = 0.25 * (flow[0] * east + flow[1] * north) - flow[c]
 
-    @pl.loop(0, blocks)
+    @pl.loop(0, blocks, unroll=3)
     def _(block):
         flow = [wind[c, rows_of(block), :] for c in range(2)]
         for c, (east, north) in enumerate(derivatives(second, block)):
             third[c, rows_of(block), :] = -flow[c] - 0.25 * (flow[0] * east + flow[1] * north)
 
-    @pl.loop(0, blocks)
+    @pl.loop(0, blocks, unroll=3)
     def _(block):
         flow = [wind[c, rows_of(block), :] for c in range(2)]
         for c, (east, north) in enumerate(derivatives(third, block)):
@@ -259,16 +259,22 @@
             both = second[c, rows_of(block), :] + third[c, rows_of(block), :]
             shift[c, rows_of(block), :] = (2.0 * both + (fourth - flow[c])) * (1.0 / 6.0)
 
-    @pl.loop(0, blocks - 2)
-    def _(block):
-        (e0, n0), (e1, n1) = derivatives(shift, block + 1)
-        g_xx, g_xy, g_yx, g_yy = 1.0 + 0.5 * e0, 0.5 * n0, 0.5 * e1, 1.0 + 0.5 * n1
-        tensor_ref[0, rows_of(block), :] = g_xx * g_xx + g_yx * g_yx
-        tensor_ref[1, rows_of(block), :] = g_xx * g_xy + g_yx * g_yy
-        tensor_ref[2, rows_of(block), :] = g_xy * g_xy + g_yy * g_yy
-
-
-def window_tensor(window, band, local, remote, table, carry):
+    half = window.width // 2 // SUB
+
+    def entries(out_ref, base):
+        @pl.loop(0, half, unroll=2)
+        def _(block):
+            (e0, n0), (e1, n1) = derivatives(shift, base + block + 1)
+            g_xx, g_xy, g_yx, g_yy = 1.0 + 0.5 * e0, 0.5 * n0, 0.5 * e1, 1.0 + 0.5 * n1
+            out_ref[0, rows_of(block), :] = g_xx * g_xx + g_yx * g_yx
+            out_ref[1, rows_of(block), :] = g_xx * g_xy + g_yx * g_yy
+            out_ref[2, rows_of(block), :] = g_xy * g_xy + g_yy * g_yy
+
+    entries(keep_ref, core * half)
+    entries(send_ref, (1 - core) * half)
+
+
+def window_tensor(window, place, local, remote, table, carry):
     depth = local.shape[2]
     vmem = pl.BlockSpec(memory_space=pltpu.VMEM)
     in_specs = [
@@ -278,11 +284,11 @@
         vmem,
         vmem,
     ]
-    operands = [band.reshape(1), local, remote, *table]
+    operands = [place, local, remote, *table]
     if not window.first:
         in_specs.append(vmem)
         operands.append(carry)
-    out_shape = [jax.ShapeDtypeStruct((3, window.width, NLON), jnp.float32)]
+    out_shape = [jax.ShapeDtypeStruct((3, window.width // 2, NLON), jnp.float32)] * 2
     if not window.last:
         out_shape.append(jax.ShapeDtypeStruct((2, 2 * SUB, NLON), jnp.float32))
     field = pltpu.VMEM((2, window.extended, NLON), jnp.float32)
@@ -305,13 +311,17 @@
         ],
         compiler_params=pltpu.CompilerParams(vmem_limit_bytes=VMEM_LIMIT),
         cost_estimate=pl.CostEstimate(
-            flops=3 * 2 * lhs_shape[0] * lhs_shape[1] * NLON,
+            flops=5 * 3 * 2 * lhs_shape[0] * lhs_shape[1] * NLON,
             transcendentals=0,
             bytes_accessed=4 * NLON * lhs_shape[1] + 8 * lhs_shape[0] * depth + 12 * window.width * NLON,
         ),
         name="window_tensor",
     )(*operands)
-    return out[0], (None if window.last else out[1])
+    return out[0], out[1], (None if window.last else out[2])
+
+
+def pairs(members, bit):
+    return [(member, member ^ bit) for member in range(members)]
 
 
 def by_levels(coeffs):
@@ -319,39 +329,56 @@
     levels, _, parts, waves_local, nlat = spec.shape
     members = lax.axis_size("mem")
     band = lax.axis_index("band").astype(jnp.int32)
+    member = lax.axis_index("mem").astype(jnp.int32)
+    core, side = member % 2, member // 2 % 2
+    columns_of = [[m for m in range(members) if m % 4 == k] for k in range(4)]
+    place = jnp.stack([band, core])
     spec = spec.reshape(levels, 2, parts * waves_local, nlat)
     windows = plan(nlat, [LANE] * (nlat // LANE))
     table = [jnp.asarray(part) for part in wave_table(levels, waves_local)]
     swap = [(0, 1), (1, 0)]
 
-    outgoing = rows_first(spec, 1 - band)
-    remotes = []
-    for window in windows:
+    lead = windows[0].rows
+    outgoing = rows_first(spec, 1 - band, choose(1 - band, (0, nlat // LANE - 2)), 2 * LANE)
+    piece = lax.dynamic_slice_in_dim(outgoing, choose(1 - band, (0, 2 * LANE - lead)), lead, axis=1)
+    remotes = [lax.ppermute(piece, "band", swap)]
+    outgoing = rows_first(spec, 1 - band, 0, nlat)
+    for window in windows[1:]:
         piece = lax.dynamic_slice_in_dim(outgoing, choose(1 - band, window.row_at), window.rows, axis=1)
         remotes.append(lax.ppermute(piece, "band", swap))
-    local = rows_first(spec, band)
+    local = rows_first(spec, band, 0, nlat)
 
     carry = None
     pieces = {"own": [], "both": [], "other": []}
     for window, remote in zip(windows, remotes):
-        partial_sum, carry = window_tensor(window, band, local, remote, table, carry)
-        summed = lax.psum_scatter(partial_sum, "mem", scatter_dimension=1, tiled=True)
+        keep, send, carry = window_tensor(window, place, local, remote, table, carry)
+        received = lax.ppermute(send, "mem", pairs(members, 1))
+        quarter = window.width // 4
+
+        def of_side(which):
+            first = which * quarter
+            return lax.dynamic_slice_in_dim(keep, first, quarter, axis=1) + lax.dynamic_slice_in_dim(
+                received, first, quarter, axis=1
+            )
+
+        total = of_side(side) + lax.ppermute(of_side(1 - side), "mem", pairs(members, 2))
+        summed = lax.psum_scatter(total, "mem", scatter_dimension=1, axis_index_groups=columns_of, tiled=True)
         pieces[window.side].append(exponent_of(summed, members))
 
     other = lax.ppermute(jnp.stack(pieces["other"]), "band", swap)
-    half = members // 2
     trades = []
-    for member in range(members):
-        for side in range(2):
-            keeps = (member < half) == (side == 0)
-            mate = (member, side) if keeps else ((member + half) % members, 1 - side)
-            trades.append((member * 2 + side, mate[0] * 2 + mate[1]))
+    for m in range(members):
+        for b in range(2):
+            mate = (m, b) if m % 2 == b else (m ^ 1, 1 - b)
+            trades.append((m * 2 + b, mate[0] * 2 + mate[1]))
     both = lax.ppermute(pieces["both"][0], ("mem", "band"), trades)
 
     def gathered(stack):
-        count, height, _ = stack.shape
-        whole = lax.all_gather(stack, "mem", axis=1, tiled=True)
-        return whole.reshape(count, members * height, NLON)
+        whole = lax.all_gather(stack, "mem", axis_index_groups=columns_of, axis=1, tiled=True)
+        beside = lax.ppermute(whole, "mem", pairs(members, 2))
+        whole = jnp.where(side == 0, jnp.concatenate([whole, beside], axis=1), jnp.concatenate([beside, whole], axis=1))
+        beside = lax.ppermute(whole, "mem", pairs(members, 1))
+        return jnp.where(core == 0, jnp.concatenate([whole, beside], axis=1), jnp.concatenate([beside, whole], axis=1))
 
     own = gathered(jnp.stack(pieces["own"]))
     late = gathered(jnp.concatenate([other, both[None]]))
@@ -378,7 +405,7 @@
     _, levels, _, _, _, nlat = coeffs.shape
     members = lax.axis_size("mem")
     rows = nlat // lax.axis_size("band")
-    if levels == lax.axis_size("band") == 2 and LANE % (members * SUB) == 0 and nlat % (2 * LANE) == LANE and rows > LANE:
+    if levels == lax.axis_size("band") == 2 and members == 16 and nlat % (2 * LANE) == LANE and rows > LANE:
         return by_levels(coeffs)
     return by_rows(coeffs)
 

time: 461 us -> 290 us (0.63)
  waiting for transfers between devices: 322 us -> 124 us
  Pallas kernels: 93.9 us -> 60.1 us
  blocking collectives: 0 us -> 30 us
  other arithmetic: 8.69 us -> 21.1 us
  local copies, waits for them, and re-layouts: 11.1 us -> 21.8 us
  starting transfers between devices: 10.7 us -> 19.1 us
    reduce_scatter x5, waiting for transfers between devices: 195 us -> 39.9 us  [by_levels(): lax.psum_scatter(total, 'mem', scatter_dimension=1, axis_index_groups=col...]
    all_gather x2 -> x0, waiting for transfers between devices: 78.4 us -> none  [gathered(): whole = lax.all_gather(stack, 'mem', axis=1, tiled=True)]
    ppermute x0 -> x15, waiting for transfers between devices: none -> 44.3 us  [the longest x5 33.7 us: by_levels(): lax.ppermute(of_side(1 - side), 'mem', pairs(members, 2))]
    all_gather x0 -> x2, blocking collectives: none -> 30 us  [gathered(): lax.all_gather(stack, 'mem', axis_index_groups=columns_of, axis=1, tiled=...]
    pallas_call x5, Pallas kernels: 81.9 us -> 53.5 us  [window_tensor(): pl.pallas_call(functools.partial(window_kernel, window, depth), out_shape...]
    unnamed x16 -> x40, local copies, waits for them, and re-layouts: 4.85 us -> 18.5 us
    add x0 -> x10, other arithmetic: none -> 13 us  [the longest x5 8.55 us: by_levels(): of_side(side) + lax.ppermute(of_side(1 - side), 'mem', pairs(members, 2))]
    ppermute x0 -> x15, starting transfers between devices: none -> 12.5 us  [the longest x5 6.95 us: by_levels(): lax.ppermute(of_side(1 - side), 'mem', pairs(members, 2))]
  transfers between devices with their start and end apart: 14 -> 26, of which waited for: 10 -> 8; matrix products, arithmetic and copies ran while one was open for 2% -> 7% of each run, Pallas kernels for 16% -> 20%
where the time goes in v2:
time: 290 us; the launch traced here: 289 us
  waiting for transfers between devices  124 us (43%)
  Pallas kernels  60.1 us (21%)
  blocking collectives  30 us (10%)
  local copies, waits for them, and re-layouts  21.8 us (8%)
  other arithmetic  21.1 us (7%)
  starting transfers between devices  19.1 us (7%)
  between operations  13.6 us (5%)
    pallas_call x5, Pallas kernels, window_tensor(): pl.pallas_call(functools.partial(window_kernel, window, depth), out_shape...  53.5 us
    reduce_scatter x5, waiting for transfers between devices, by_levels(): lax.psum_scatter(total, 'mem', scatter_dimension=1, axis_index_groups=col...  39.9 us
    ppermute x4, waiting for transfers between devices, by_levels(): remotes.append(lax.ppermute(piece, 'band', swap))  39.3 us
    ppermute x5, waiting for transfers between devices, by_levels(): lax.ppermute(of_side(1 - side), 'mem', pairs(members, 2))  33.7 us
    all_gather x2, blocking collectives, gathered(): lax.all_gather(stack, 'mem', axis_index_groups=columns_of, axis=1, tiled=...  30 us
    unnamed x40, local copies, waits for them, and re-layouts  18.5 us
    add x5, other arithmetic, by_levels(): of_side(side) + lax.ppermute(of_side(1 - side), 'mem', pairs(members, 2))  8.55 us
    ppermute x2, waiting for transfers between devices, gathered(): beside = lax.ppermute(whole, 'mem', pairs(members, 2))  8.25 us
  transfers between devices with their start and end apart: 26, of which 8 were waited for; matrix products, arithmetic and copies ran while one was open for 7% of the time, Pallas kernels for 20%

profile of v2, /device:TPU:0, one launch (start us, length us, event | category | flops | bytes accessed | tf_op | source)
XLA Modules:
  0.0 289.3 jit_solution(5091965084427705871)
XLA Ops:
  6.6 2.9 copy-done
  9.5 1.4 rows_first.4
  11.8 2.9 %collective-permute-start = (f32[2,136,640]{2,1,0:T(8,128)}, f32[2,136,640]{2,1,0:T(8,128)}, u32[]{:S(2)}, u32[]{:S(2)}) collective-permute-start(f32[2,136,640]{2,1,0:T(8,128)} %constant_dynamic-slice_fusion.4), channel_id=1, source_target_pairs={{0,1},{1,0},{2,3},{3,2},{4,5},{5,4},{6,7},{7,6},{8,9},{9,8},{10,11... | collective-permute-start | bytes 2088968 | tf_op jit(solution)/shard_map/ppermute | solution.py:344
  14.8 2.9 copy-done.1
  17.6 2.6 rows_first.5
  21.1 1.3 constant_dynamic-slice_fusion.2
  22.5 2.0 collective-permute-start.8
  24.5 2.0 collective-permute-start.3
  26.6 2.9 copy-done.2
  29.4 2.6 rows_first.3.refs_1_
  32.1 1.9 copy-done.13
  34.0 1.9 copy-done.16
  35.9 10.6 %window_tensor.5 = (f32[3,64,1280]{2,1,0:T(8,128)S(1)}, f32[3,64,1280]{2,1,0:T(8,128)S(1)}, f32[2,16,1280]{2,1,0:T(8,128)S(1)}) custom-call(s32[2]{0:T(128)S(1)} %get-tuple-element.49.refs_0_, f32[2,640,640]{2,1,0:T(8,128)S(1)} %rows_first.3.refs_1_, f32[2,136,640]{2,1,0:T(8,128)} %collective-permute-done.refs_2_, bf16[1280,1280]{1,0:T(8,128)(2,1)S(1)} %copy-done.16, ...), custom_call_target="tpu_custom_call" | custom-call | flops 13369344000 | bytes 9912320 | tf_op jit(solution)/shard_map/window_tensor/pallas_call | solution.py:296
  46.6 39.3 %collective-permute-done.3.refs_2_ = f32[2,128,640]{2,1,0:T(8,128)} collective-permute-done((f32[2,128,640]{2,1,0:T(8,128)}, f32[2,128,640]{2,1,0:T(8,128)}, u32[]{:S(2)}, u32[]{:S(2)}) %collective-permute-start.3) | collective-permute-done | bytes 655392 | tf_op jit(solution)/shard_map/ppermute | solution.py:348
  85.9 10.2 %window_tensor.6 = (f32[3,64,1280]{2,1,0:T(8,128)S(1)}, f32[3,64,1280]{2,1,0:T(8,128)S(1)}, f32[2,16,1280]{2,1,0:T(8,128)S(1)}) custom-call(s32[2]{0:T(128)S(1)} %get-tuple-element.49.refs_0_, f32[2,640,640]{2,1,0:T(8,128)S(1)} %rows_first.3.refs_1_, f32[2,128,640]{2,1,0:T(8,128)} %collective-permute-done.3.refs_2_, bf16[1280,1280]{1,0:T(8,128)(2,1)S(1)} %copy-done.16, ...), custom_call_target="tpu_custom_call" | custom-call | flops 12582912000 | bytes 9830400 | tf_op jit(solution)/shard_map/window_tensor/pallas_call | solution.py:296
  96.2 11.4 %window_tensor.7 = (f32[3,64,1280]{2,1,0:T(8,128)S(1)}, f32[3,64,1280]{2,1,0:T(8,128)}, f32[2,16,1280]{2,1,0:T(8,128)S(1)}) custom-call(s32[2]{0:T(128)S(1)} %get-tuple-element.49.refs_0_, f32[2,640,640]{2,1,0:T(8,128)S(1)} %rows_first.3.refs_1_, f32[2,128,640]{2,1,0:T(8,128)} %collective-permute-done.9.refs_2_, bf16[1280,1280]{1,0:T(8,128)(2,1)S(1)} %copy-done.16, ...), custom_call_target="tpu_custom_call" | custom-call | flops 12582912000 | bytes 9830400 | tf_op jit(solution)/shard_map/window_tensor/pallas_call | solution.py:296
  108.0 1.8 collective-permute-start.2
  109.9 10.2 %window_tensor.8 = (f32[3,64,1280]{2,1,0:T(8,128)S(1)}, f32[3,64,1280]{2,1,0:T(8,128)S(1)}, f32[2,16,1280]{2,1,0:T(8,128)S(1)}) custom-call(s32[2]{0:T(128)S(1)} %get-tuple-element.49.refs_0_, f32[2,640,640]{2,1,0:T(8,128)S(1)} %rows_first.3.refs_1_, f32[2,128,640]{2,1,0:T(8,128)} %collective-permute-done.8.refs_2_, bf16[1280,1280]{1,0:T(8,128)(2,1)S(1)} %copy-done.16, ...), custom_call_target="tpu_custom_call" | custom-call | flops 12582912000 | bytes 9830400 | tf_op jit(solution)/shard_map/window_tensor/pallas_call | solution.py:296
  120.1 1.0 copy-done.3
  121.1 1.0 dynamic-slice_add_fusion.3
  123.8 1.9 copy-done.15
  125.7 1.9 copy-done.17
  127.6 11.1 %window_tensor.9 = (f32[3,64,1280]{2,1,0:T(8,128)S(1)}, f32[3,64,1280]{2,1,0:T(8,128)}) custom-call(s32[2]{0:T(128)S(1)} %get-tuple-element.49.refs_0_, f32[2,640,640]{2,1,0:T(8,128)S(1)} %rows_first.3.refs_1_, f32[2,120,640]{2,1,0:T(8,128)} %collective-permute-done.12.refs_2_, bf16[1280,1280]{1,0:T(8,128)(2,1)S(1)} %copy-done.17, ...), custom_call_target="tpu_custom_call" | custom-call | flops 11796480000 | bytes 9748480 | tf_op jit(solution)/shard_map/window_tensor/pallas_call | solution.py:296
  138.7 1.0 copy-done.9
  139.8 2.0 add_add_fusion.3
  141.9 1.2 dynamic-slice_add_fusion
  143.1 1.5 collective-permute-start.17
  144.7 12.0 %collective-permute-done.17 = f32[3,32,1280]{2,1,0:T(8,128)S(1)} collective-permute-done((f32[3,32,1280]{2,1,0:T(8,128)S(1)}, f32[3,32,1280]{2,1,0:T(8,128)S(1)}, u32[]{:S(2)}, u32[]{:S(2)}) %collective-permute-start.17) | collective-permute-done | bytes 491552 | tf_op jit(solution)/shard_map/ppermute | solution.py:364
  156.6 1.9 add_add_fusion
  158.8 1.2 dynamic-slice_add_fusion.1
  160.0 1.5 collective-permute-start.14
  161.5 11.3 %collective-permute-done.14 = f32[3,32,1280]{2,1,0:T(8,128)S(1)} collective-permute-done((f32[3,32,1280]{2,1,0:T(8,128)S(1)}, f32[3,32,1280]{2,1,0:T(8,128)S(1)}, u32[]{:S(2)}, u32[]{:S(2)}) %collective-permute-start.14) | collective-permute-done | bytes 491552 | tf_op jit(solution)/shard_map/ppermute | solution.py:364
  172.8 1.9 add_add_fusion.1
  174.8 1.1 dynamic-slice_add_fusion.2
  175.9 1.5 collective-permute-start.11
  177.4 10.4 %collective-permute-done.11 = f32[3,32,1280]{2,1,0:T(8,128)S(1)} collective-permute-done((f32[3,32,1280]{2,1,0:T(8,128)S(1)}, f32[3,32,1280]{2,1,0:T(8,128)S(1)}, u32[]{:S(2)}, u32[]{:S(2)}) %collective-permute-start.11) | collective-permute-done | bytes 491552 | tf_op jit(solution)/shard_map/ppermute | solution.py:364
  187.8 1.9 add_add_fusion.2
  189.8 0.9 broadcast_multiply_fusion.4
  190.8 0.9 broadcast_multiply_fusion.3
  193.4 19.0 %reduce-scatter.12.cloned.1.call-done = f32[3,8,1280]{2,1,0:T(8,128)} async-done(((f32[3,32,1280]{2,1,0:T(8,128)}), f32[3,8,1280]{2,1,0:T(8,128)}) %reduce-scatter.12.cloned.1.call-update) | async-done | bytes 122896 | tf_op jit(solution)/shard_map/reduce_scatter | solution.py:365
  213.4 20.9 %reduce-scatter.10.cloned.1.call-done = f32[3,8,1280]{2,1,0:T(8,128)} async-done(((f32[3,32,1280]{2,1,0:T(8,128)}), f32[3,8,1280]{2,1,0:T(8,128)}) %reduce-scatter.10.cloned.1.call-update) | async-done | bytes 122896 | tf_op jit(solution)/shard_map/reduce_scatter | solution.py:365
  235.2 1.6 collective-permute-start.15
  236.8 14.1 %all_gather.6 = f32[2,32,1280]{2,1,0:T(8,128)S(1)} all-gather(f32[2,8,1280]{2,1,0:T(8,128)S(1)} %pad_maximum_fusion.1), channel_id=1, replica_groups={{0,8,16,24},{2,10,18,26},{4,12,20,28},{6,14,22,30},{1,9,17,25},{3,11,19..., dimensions={1}, use_global_device_ids=true | all-gather | bytes 409600 | tf_op jit(solution)/shard_map/all_gather | solution.py:377
  250.9 1.5 collective-permute-start.6
  252.4 15.8 %all_gather.7 = f32[3,32,1280]{2,1,0:T(8,128)S(1)} all-gather(f32[3,8,1280]{2,1,0:T(8,128)S(1)} %pad_maximum_fusion), channel_id=1, replica_groups={{0,8,16,24},{2,10,18,26},{4,12,20,28},{6,14,22,30},{1,9,17,25},{3,11,19..., dimensions={1}, use_global_device_ids=true | all-gather | bytes 614400 | tf_op jit(solution)/shard_map/all_gather | solution.py:377
  268.9 8.2 %collective-permute-done.19 = f32[3,32,1280]{2,1,0:T(8,128)S(1)} collective-permute-done((f32[3,32,1280]{2,1,0:T(8,128)S(1)}, f32[3,32,1280]{2,1,0:T(8,128)S(1)}, u32[]{:S(2)}, u32[]{:S(2)}) %collective-permute-start.19) | collective-permute-done | bytes 491552 | tf_op jit(solution)/shard_map/ppermute | solution.py:378
  277.5 2.3 collective-permute-done.20
  280.7 2.1 maximum_select_fusion
  (97 shorter events, 10.1 us)
Async XLA Ops:
  6.5 183.3 %reduce-scatter.6.cloned.1.call-start = ((), (), s32[]{:S(2)}) async-start(), calls=%async_computation.5 | async-start | bytes 614400 | tf_op jit(solution)/shard_map/reduce_scatter | solution.py:365
  6.6 2.9 copy-start
  11.8 20.3 %collective-permute-start = (f32[2,136,640]{2,1,0:T(8,128)}, f32[2,136,640]{2,1,0:T(8,128)}, u32[]{:S(2)}, u32[]{:S(2)}) collective-permute-start(f32[2,136,640]{2,1,0:T(8,128)} %constant_dynamic-slice_fusion.4), channel_id=1, source_target_pairs={{0,1},{1,0},{2,3},{3,2},{4,5},{5,4},{6,7},{7,6},{8,9},{9,8},{10,11... | collective-permute-start | bytes 2088968 | tf_op jit(solution)/shard_map/ppermute | solution.py:344
  14.8 2.9 copy-start.1
  21.1 102.6 %collective-permute-start.12 = (f32[2,120,640]{2,1,0:T(8,128)}, f32[2,120,640]{2,1,0:T(8,128)}, u32[]{:S(2)}, u32[]{:S(2)}) collective-permute-start(f32[2,120,640]{2,1,0:T(8,128)} %constant_dynamic-slice_fusion), channel_id=1, source_target_pairs={{0,1},{1,0},{2,3},{3,2},{4,5},{5,4},{6,7},{7,6},{8,9},{9,8},{10,11... | collective-permute-start | bytes 1843208 | tf_op jit(solution)/shard_map/ppermute | solution.py:348
  22.5 87.4 %collective-permute-start.8 = (f32[2,128,640]{2,1,0:T(8,128)}, f32[2,128,640]{2,1,0:T(8,128)}, u32[]{:S(2)}, u32[]{:S(2)}) collective-permute-start(f32[2,128,640]{2,1,0:T(8,128)} %get-tuple-element.33), channel_id=1, source_target_pairs={{0,1},{1,0},{2,3},{3,2},{4,5},{5,4},{6,7},{7,6},{8,9},{9,8},{10,11... | collective-permute-start | bytes 1966088 | tf_op jit(solution)/shard_map/ppermute | solution.py:348
  24.5 71.8 %collective-permute-start.9 = (f32[2,128,640]{2,1,0:T(8,128)}, f32[2,128,640]{2,1,0:T(8,128)}, u32[]{:S(2)}, u32[]{:S(2)}) collective-permute-start(f32[2,128,640]{2,1,0:T(8,128)} %get-tuple-element.34), channel_id=1, source_target_pairs={{0,1},{1,0},{2,3},{3,2},{4,5},{5,4},{6,7},{7,6},{8,9},{9,8},{10,11... | collective-permute-start | bytes 1966088 | tf_op jit(solution)/shard_map/ppermute | solution.py:348
  24.5 61.4 %collective-permute-start.3 = (f32[2,128,640]{2,1,0:T(8,128)}, f32[2,128,640]{2,1,0:T(8,128)}, u32[]{:S(2)}, u32[]{:S(2)}) collective-permute-start(f32[2,128,640]{2,1,0:T(8,128)} %get-tuple-element.35), channel_id=1, source_target_pairs={{0,1},{1,0},{2,3},{3,2},{4,5},{5,4},{6,7},{7,6},{8,9},{9,8},{10,11... | collective-permute-start | bytes 1966088 | tf_op jit(solution)/shard_map/ppermute | solution.py:348
  26.6 2.9 copy-start.2
  32.1 1.9 copy-start.13
  34.0 1.9 copy-start.16
  35.9 50.0 %copy-start.14 = (bf16[1280,1280]{1,0:T(8,128)(2,1)S(1)}, bf16[1280,1280]{1,0:T(8,128)(2,1)}, u32[]{:S(2)}) copy-start(bf16[1280,1280]{1,0:T(8,128)(2,1)} %constant.89.clone.refs_4_) | copy-start | bytes 9830404
  46.5 61.4 %collective-permute-start.1 = (f32[3,64,1280]{2,1,0:T(8,128)S(1)}, f32[3,64,1280]{2,1,0:T(8,128)S(1)}, u32[]{:S(2)}, u32[]{:S(2)}) collective-permute-start(f32[3,64,1280]{2,1,0:T(8,128)S(1)} %get-tuple-element.20), channel_id=1, source_target_pairs={{0,2},{2,0},{4,6},{6,4},{8,10},{10,8},{12,14},{14,12},{16,18},{18,... | collective-permute-start | bytes 2949128 | tf_op jit(solution)/shard_map/ppermute | solution.py:355
  96.1 24.9 %copy-start.7 = (f32[3,64,1280]{2,1,0:T(8,128)}, f32[3,64,1280]{2,1,0:T(8,128)S(1)}, u32[]{:S(2)}) copy-start(f32[3,64,1280]{2,1,0:T(8,128)S(1)} %get-tuple-element.22) | copy-start | bytes 2949124
  96.2 24.9 %collective-permute-start.4 = (f32[3,64,1280]{2,1,0:T(8,128)S(1)}, f32[3,64,1280]{2,1,0:T(8,128)S(1)}, u32[]{:S(2)}, u32[]{:S(2)}) collective-permute-start(f32[3,64,1280]{2,1,0:T(8,128)S(1)} %get-tuple-element.23), channel_id=1, source_target_pairs={{0,2},{2,0},{4,6},{6,4},{8,10},{10,8},{12,14},{14,12},{16,18},{18,... | collective-permute-start | bytes 2949128 | tf_op jit(solution)/shard_map/ppermute | solution.py:355
  107.7 2.2 copy-start.5
  107.7 34.2 %collective-permute-start.16 = (f32[3,64,1280]{2,1,0:T(8,128)}, f32[3,64,1280]{2,1,0:T(8,128)}, u32[]{:S(2)}, u32[]{:S(2)}) collective-permute-start(f32[3,64,1280]{2,1,0:T(8,128)} %get-tuple-element.32), channel_id=1, source_target_pairs={{0,2},{2,0},{4,6},{6,4},{8,10},{10,8},{12,14},{14,12},{16,18},{18,... | collective-permute-start | bytes 2949128 | tf_op jit(solution)/shard_map/ppermute | solution.py:355
  108.0 14.8 %collective-permute-start.2 = (f32[3,32,1280]{2,1,0:T(8,128)S(1)}, f32[3,32,1280]{2,1,0:T(8,128)S(1)}, u32[]{:S(2)}, u32[]{:S(2)}) collective-permute-start(f32[3,32,1280]{2,1,0:T(8,128)S(1)} %dynamic-slice_add_fusion.4), channel_id=1, source_target_pairs={{0,4},{2,6},{4,0},{6,2},{8,12},{10,14},{12,8},{14,10},{16,20},{18,... | collective-permute-start | bytes 1474568 | tf_op jit(solution)/shard_map/ppermute | solution.py:364
  120.1 1.0 copy-start.3
  121.1 1.2 copy-start.11
  121.1 1.7 copy-start.18
  122.2 17.5 %collective-permute-start.5 = (f32[3,32,1280]{2,1,0:T(8,128)}, f32[3,32,1280]{2,1,0:T(8,128)}, u32[]{:S(2)}, u32[]{:S(2)}) collective-permute-start(f32[3,32,1280]{2,1,0:T(8,128)} %dynamic-slice_add_fusion.3), channel_id=1, source_target_pairs={{0,4},{2,6},{4,0},{6,2},{8,12},{10,14},{12,8},{14,10},{16,20},{18,... | collective-permute-start | bytes 1474568 | tf_op jit(solution)/shard_map/ppermute | solution.py:364
  123.7 67.1 %reduce-scatter.8.cloned.1.call-start = ((), (), s32[]{:S(2)}) async-start(), calls=%async_computation.6 | async-start | bytes 614400 | tf_op jit(solution)/shard_map/reduce_scatter | solution.py:365
  123.8 1.9 copy-start.15
  125.7 1.9 copy-start.17
  127.6 12.1 %copy-start.8 = (f32[3,64,1280]{2,1,0:T(8,128)S(1)}, f32[3,64,1280]{2,1,0:T(8,128)}, u32[]{:S(2)}) copy-start(f32[3,64,1280]{2,1,0:T(8,128)} %copy-done.7) | copy-start | bytes 2949124
  127.6 12.2 %copy-start.19 = (f32[3,64,1280]{2,1,0:T(8,128)S(1)}, f32[3,64,1280]{2,1,0:T(8,128)}, u32[]{:S(2)}) copy-start(f32[3,64,1280]{2,1,0:T(8,128)} %copy-done.18) | copy-start | bytes 2949124
  138.7 1.0 copy-start.9
  139.8 2.1 copy-start.6
  139.8 4.9 %copy-start.12 = (f32[3,64,1280]{2,1,0:T(8,128)S(1)}, f32[3,64,1280]{2,1,0:T(8,128)}, u32[]{:S(2)}) copy-start(f32[3,64,1280]{2,1,0:T(8,128)} %copy-done.11) | copy-start | bytes 2949124
  139.8 19.0 %collective-permute-start.13 = (f32[3,64,1280]{2,1,0:T(8,128)}, f32[3,64,1280]{2,1,0:T(8,128)}, u32[]{:S(2)}, u32[]{:S(2)}) collective-permute-start(f32[3,64,1280]{2,1,0:T(8,128)} %get-tuple-element.30), channel_id=1, source_target_pairs={{0,2},{2,0},{4,6},{6,4},{8,10},{10,8},{12,14},{14,12},{16,18},{18,... | collective-permute-start | bytes 2949128 | tf_op jit(solution)/shard_map/ppermute | solution.py:355
  141.8 49.9 %reduce-scatter.14.cloned.1.call-start = ((), (), s32[]{:S(2)}) async-start(), calls=%async_computation.9 | async-start | bytes 614400 | tf_op jit(solution)/shard_map/reduce_scatter | solution.py:365
  141.9 16.9 %copy-start.10 = (f32[3,64,1280]{2,1,0:T(8,128)S(1)}, f32[3,64,1280]{2,1,0:T(8,128)}, u32[]{:S(2)}) copy-start(f32[3,64,1280]{2,1,0:T(8,128)} %copy-done.9) | copy-start | bytes 2949124
  143.1 13.6 %collective-permute-start.17 = (f32[3,32,1280]{2,1,0:T(8,128)S(1)}, f32[3,32,1280]{2,1,0:T(8,128)S(1)}, u32[]{:S(2)}, u32[]{:S(2)}) collective-permute-start(f32[3,32,1280]{2,1,0:T(8,128)S(1)} %dynamic-slice_add_fusion), channel_id=1, source_target_pairs={{0,4},{2,6},{4,0},{6,2},{8,12},{10,14},{12,8},{14,10},{16,20},{18,... | collective-permute-start | bytes 1474568 | tf_op jit(solution)/shard_map/ppermute | solution.py:364
  144.6 30.2 %collective-permute-start.10 = (f32[3,64,1280]{2,1,0:T(8,128)S(1)}, f32[3,64,1280]{2,1,0:T(8,128)}, u32[]{:S(2)}, u32[]{:S(2)}) collective-permute-start(f32[3,64,1280]{2,1,0:T(8,128)S(1)} %copy-done.12), channel_id=1, source_target_pairs={{0,2},{2,0},{4,6},{6,4},{8,10},{10,8},{12,14},{14,12},{16,18},{18,... | collective-permute-start | bytes 2949128 | tf_op jit(solution)/shard_map/ppermute | solution.py:355
  158.6 53.9 %reduce-scatter.12.cloned.1.call-start = ((), (), s32[]{:S(2)}) async-start(), calls=%async_computation.8 | async-start | bytes 614400 | tf_op jit(solution)/shard_map/reduce_scatter | solution.py:365
  158.8 16.0 %copy-start.4 = (f32[3,64,1280]{2,1,0:T(8,128)S(1)}, f32[3,64,1280]{2,1,0:T(8,128)}, u32[]{:S(2)}) copy-start(f32[3,64,1280]{2,1,0:T(8,128)} %copy-done.3) | copy-start | bytes 2949124
  160.0 12.8 %collective-permute-start.14 = (f32[3,32,1280]{2,1,0:T(8,128)S(1)}, f32[3,32,1280]{2,1,0:T(8,128)S(1)}, u32[]{:S(2)}, u32[]{:S(2)}) collective-permute-start(f32[3,32,1280]{2,1,0:T(8,128)S(1)} %dynamic-slice_add_fusion.1), channel_id=1, source_target_pairs={{0,4},{2,6},{4,0},{6,2},{8,12},{10,14},{12,8},{14,10},{16,20},{18,... | collective-permute-start | bytes 1474568 | tf_op jit(solution)/shard_map/ppermute | solution.py:364
  174.7 59.5 %reduce-scatter.10.cloned.1.call-start = ((), (), s32[]{:S(2)}) async-start(), calls=%async_computation.7 | async-start | bytes 614400 | tf_op jit(solution)/shard_map/reduce_scatter | solution.py:365
  175.9 11.9 %collective-permute-start.11 = (f32[3,32,1280]{2,1,0:T(8,128)S(1)}, f32[3,32,1280]{2,1,0:T(8,128)S(1)}, u32[]{:S(2)}, u32[]{:S(2)}) collective-permute-start(f32[3,32,1280]{2,1,0:T(8,128)S(1)} %dynamic-slice_add_fusion.2), channel_id=1, source_target_pairs={{0,4},{2,6},{4,0},{6,2},{8,12},{10,14},{12,8},{14,10},{16,20},{18,... | collective-permute-start | bytes 1474568 | tf_op jit(solution)/shard_map/ppermute | solution.py:364
  192.7 59.7 %collective-permute-start.18 = (f32[8,1280]{1,0:T(8,128)S(1)}, f32[8,1280]{1,0:T(8,128)S(1)}, u32[]{:S(2)}, u32[]{:S(2)}) collective-permute-start(f32[8,1280]{1,0:T(8,128)S(1)} %fusion.6), channel_id=1, source_target_pairs={{0,0},{1,2},{2,1},{3,3},{4,4},{5,6},{6,5},{7,7},{8,8},{9,10},{10,9... | collective-permute-start | bytes 122888 | tf_op jit(solution)/shard_map/ppermute | solution.py:374
  235.2 17.2 %collective-permute-start.15 = (f32[2,8,1280]{2,1,0:T(8,128)S(1)}, f32[2,8,1280]{2,1,0:T(8,128)S(1)}, u32[]{:S(2)}, u32[]{:S(2)}) collective-permute-start(f32[2,8,1280]{2,1,0:T(8,128)S(1)} %pad_maximum_fusion.2), channel_id=1, source_target_pairs={{0,1},{1,0},{2,3},{3,2},{4,5},{5,4},{6,7},{7,6},{8,9},{9,8},{10,11... | collective-permute-start | bytes 245768 | tf_op jit(solution)/shard_map/ppermute | solution.py:368
  250.9 17.8 %collective-permute-start.6 = (f32[2,32,1280]{2,1,0:T(8,128)S(1)}, f32[2,32,1280]{2,1,0:T(8,128)S(1)}, u32[]{:S(2)}, u32[]{:S(2)}) collective-permute-start(f32[2,32,1280]{2,1,0:T(8,128)S(1)} %all_gather.6), channel_id=1, source_target_pairs={{0,4},{2,6},{4,0},{6,2},{8,12},{10,14},{12,8},{14,10},{16,20},{18,... | collective-permute-start | bytes 983048 | tf_op jit(solution)/shard_map/ppermute | solution.py:378
  268.3 8.8 %collective-permute-start.19 = (f32[3,32,1280]{2,1,0:T(8,128)S(1)}, f32[3,32,1280]{2,1,0:T(8,128)S(1)}, u32[]{:S(2)}, u32[]{:S(2)}) collective-permute-start(f32[3,32,1280]{2,1,0:T(8,128)S(1)} %all_gather.7), channel_id=1, source_target_pairs={{0,4},{2,6},{4,0},{6,2},{8,12},{10,14},{12,8},{14,10},{16,20},{18,... | collective-permute-start | bytes 1474568 | tf_op jit(solution)/shard_map/ppermute | solution.py:378
  268.8 8.5 %collective-permute-start.7 = (f32[2,64,1280]{2,1,0:T(8,128)S(1)}, f32[2,64,1280]{2,1,0:T(8,128)S(1)}, u32[]{:S(2)}, u32[]{:S(2)}) collective-permute-start(f32[2,64,1280]{2,1,0:T(8,128)S(1)} %maximum_select_fusion.4), channel_id=1, source_target_pairs={{0,2},{2,0},{4,6},{6,4},{8,10},{10,8},{12,14},{14,12},{16,18},{18,... | collective-permute-start | bytes 1966088 | tf_op jit(solution)/shard_map/ppermute | solution.py:380
  277.2 2.6 collective-permute-start.20
Sparse Core Ops, SparseCore 0:
  123.8 22.4 reduce-scatter.5
  148.7 19.6 reduce-scatter.7
  170.7 19.6 reduce-scatter.13
  192.6 19.7 reduce-scatter.11
  214.6 19.6 reduce-scatter.9

commit v3 on v2

--- a/solution.py
+++ b/solution.py
@@ -128,10 +128,10 @@
         low = 0 if self.first else start + SUB
         high = nlat if self.last else start + width + SUB
         self.rows = high - low
-        self.row_at = (low, nlat - high)
+        self.row_at = (nlat - high, low)
         base_up, base_down = start - SUB, nlat - start - width - SUB
-        self.place = (low - base_up, nlat - high - base_down)
-        self.side = "own" if 2 * (start + width) <= nlat else "other" if 2 * start >= nlat else "both"
+        self.place = (nlat - high - base_down, low - base_up)
+        self.side = "other" if 2 * (start + width) <= nlat else "own" if 2 * start >= nlat else "both"
 
 
 def plan(nlat, widths):
@@ -158,7 +158,7 @@
             out_specs=pl.BlockSpec((1, LANE, depth), lambda c, t, place: (c, t, 0)),
         ),
         out_shape=jax.ShapeDtypeStruct((2, width, depth), jnp.float32),
-        compiler_params=pltpu.CompilerParams(vmem_limit_bytes=VMEM_LIMIT),
+        compiler_params=pltpu.CompilerParams(vmem_limit_bytes=2 * VMEM_LIMIT),
         cost_estimate=pl.CostEstimate(
             flops=0, transcendentals=0, bytes_accessed=8 * 2 * width * depth * 4
         ),
@@ -166,6 +166,26 @@
     )(jnp.stack([level, jnp.asarray(block, jnp.int32)]), spec)
 
 
+def piece_kernel(start_ref, from_ref, *refs):
+    out_ref, sem = refs[-2:]
+    start = pl.multiple_of(start_ref[0], SUB)
+    copy = pltpu.make_async_copy(from_ref.at[:, pl.ds(start, out_ref.shape[1])], out_ref, sem)
+    copy.start()
+    copy.wait()
+
+
+def piece_of(outgoing, start, rows, waits):
+    return pl.pallas_call(
+        piece_kernel,
+        in_specs=[pl.BlockSpec(memory_space=pltpu.SMEM)] + [pl.BlockSpec(memory_space=pl.ANY)] * (1 + len(waits)),
+        out_specs=pl.BlockSpec(memory_space=pl.ANY),
+        out_shape=jax.ShapeDtypeStruct((2, rows, outgoing.shape[2]), jnp.float32),
+        scratch_shapes=[pltpu.SemaphoreType.DMA],
+        cost_estimate=pl.CostEstimate(flops=0, transcendentals=0, bytes_accessed=16 * rows * outgoing.shape[2]),
+        name="piece_of",
+    )(start.astype(jnp.int32).reshape(1), outgoing, *waits)
+
+
 def east_of(x):
     return pltpu.roll(x, NLON - 1, axis=1) - pltpu.roll(x, 1, axis=1)
 
@@ -177,10 +197,10 @@
     return above - below
 
 
-def window_kernel(window, depth, *refs):
+def window_kernel(window, depth, waits, *refs):
     refs = list(refs)
     place_ref, local_ref, remote_ref, high_ref, low_ref = refs[:5]
-    refs = refs[5:]
+    refs = refs[5 + waits :]
     carry_ref = None if window.first else refs.pop(0)
     keep_ref, send_ref = refs.pop(0), refs.pop(0)
     carried_ref = None if window.last else refs.pop(0)
@@ -205,12 +225,12 @@
     if window.first or window.last:
         for c in range(2):
             if window.first:
+                wind[c, pl.ds(at((extended - SUB, 0)), SUB), :] = jnp.zeros((SUB, NLON), jnp.float32)
+            if window.last:
                 wind[c, pl.ds(at((0, extended - SUB)), SUB), :] = jnp.zeros((SUB, NLON), jnp.float32)
-            if window.last:
-                wind[c, pl.ds(at((extended - SUB, 0)), SUB), :] = jnp.zeros((SUB, NLON), jnp.float32)
     if not window.first:
         for c in range(2):
-            wind[c, pl.ds(at((0, extended - 2 * SUB)), 2 * SUB), :] = carry_ref[c]
+            wind[c, pl.ds(at((extended - 2 * SUB, 0)), 2 * SUB), :] = carry_ref[c]
 
     @pl.loop(0, NLON // 256)
     def _(tile):
@@ -224,7 +244,7 @@
 
     if not window.last:
         for c in range(2):
-            carried_ref[c] = wind[c, pl.ds(at((extended - 2 * SUB, 0)), 2 * SUB), :]
+            carried_ref[c] = wind[c, pl.ds(at((0, extended - 2 * SUB)), 2 * SUB), :]
 
     blocks = extended // SUB
 
@@ -239,19 +259,19 @@
             result.append((east_of(here), north_of(field[c, rows_of(before), :], here, field[c, rows_of(after), :])))
         return result
 
-    @pl.loop(0, blocks, unroll=3)
+    @pl.loop(0, blocks, unroll=6)
     def _(block):
         flow = [wind[c, rows_of(block), :] for c in range(2)]
         for c, (east, north) in enumerate(derivatives(wind, block)):
             second[c, rows_of(block), :] = 0.25 * (flow[0] * east + flow[1] * north) - flow[c]
 
-    @pl.loop(0, blocks, unroll=3)
+    @pl.loop(0, blocks, unroll=6)
     def _(block):
         flow = [wind[c, rows_of(block), :] for c in range(2)]
         for c, (east, north) in enumerate(derivatives(second, block)):
             third[c, rows_of(block), :] = -flow[c] - 0.25 * (flow[0] * east + flow[1] * north)
 
-    @pl.loop(0, blocks, unroll=3)
+    @pl.loop(0, blocks, unroll=6)
     def _(block):
         flow = [wind[c, rows_of(block), :] for c in range(2)]
         for c, (east, north) in enumerate(derivatives(third, block)):
@@ -262,7 +282,7 @@
     half = window.width // 2 // SUB
 
     def entries(out_ref, base):
-        @pl.loop(0, half, unroll=2)
+        @pl.loop(0, half, unroll=4)
         def _(block):
             (e0, n0), (e1, n1) = derivatives(shift, base + block + 1)
             g_xx, g_xy, g_yx, g_yy = 1.0 + 0.5 * e0, 0.5 * n0, 0.5 * e1, 1.0 + 0.5 * n1
@@ -274,7 +294,7 @@
     entries(send_ref, (1 - core) * half)
 
 
-def window_tensor(window, place, local, remote, table, carry):
+def window_tensor(window, place, local, remote, table, waits, carry):
     depth = local.shape[2]
     vmem = pl.BlockSpec(memory_space=pltpu.VMEM)
     in_specs = [
@@ -284,7 +304,8 @@
         vmem,
         vmem,
     ]
-    operands = [place, local, remote, *table]
+    in_specs += [pl.BlockSpec(memory_space=pl.ANY)] * len(waits)
+    operands = [place, local, remote, *table, *waits]
     if not window.first:
         in_specs.append(vmem)
         operands.append(carry)
@@ -294,7 +315,7 @@
     field = pltpu.VMEM((2, window.extended, NLON), jnp.float32)
     lhs_shape = (2 * window.rows, 2 * depth)
     out = pl.pallas_call(
-        functools.partial(window_kernel, window, depth),
+        functools.partial(window_kernel, window, depth, len(waits)),
         out_shape=out_shape,
         in_specs=in_specs,
         out_specs=[vmem] * len(out_shape),
@@ -330,40 +351,65 @@
     members = lax.axis_size("mem")
     band = lax.axis_index("band").astype(jnp.int32)
     member = lax.axis_index("mem").astype(jnp.int32)
-    core, side = member % 2, member // 2 % 2
-    columns_of = [[m for m in range(members) if m % 4 == k] for k in range(4)]
-    place = jnp.stack([band, core])
+    place = jnp.stack([band, member % 2])
     spec = spec.reshape(levels, 2, parts * waves_local, nlat)
     windows = plan(nlat, [LANE] * (nlat // LANE))
     table = [jnp.asarray(part) for part in wave_table(levels, waves_local)]
     swap = [(0, 1), (1, 0)]
 
     lead = windows[0].rows
-    outgoing = rows_first(spec, 1 - band, choose(1 - band, (0, nlat // LANE - 2)), 2 * LANE)
-    piece = lax.dynamic_slice_in_dim(outgoing, choose(1 - band, (0, 2 * LANE - lead)), lead, axis=1)
+    outgoing = rows_first(spec, 1 - band, choose(1 - band, (nlat // LANE - 2, 0)), 2 * LANE)
+    piece = piece_of(outgoing, choose(1 - band, (2 * LANE - lead, 0)), lead, [])
     remotes = [lax.ppermute(piece, "band", swap)]
     outgoing = rows_first(spec, 1 - band, 0, nlat)
-    for window in windows[1:]:
-        piece = lax.dynamic_slice_in_dim(outgoing, choose(1 - band, window.row_at), window.rows, axis=1)
+
+    def fetch_rows(k, waits):
+        window = windows[k]
+        piece = piece_of(outgoing, choose(1 - band, window.row_at), window.rows, waits)
         remotes.append(lax.ppermute(piece, "band", swap))
+        return piece
+
+    fetch_rows(1, [])
     local = rows_first(spec, band, 0, nlat)
 
+    bits = [1 << n for n in range(members.bit_length() - 1)]
+
+    def halved(parts_of, bit):
+        half = parts_of[0].shape[1] // 2
+        mine = (member // bit) % 2
+
+        def total(which):
+            return sum(lax.dynamic_slice_in_dim(part, which * half, half, axis=1) for part in parts_of[:2])
+
+        leaves = total(1 - mine)
+        return [total(mine), lax.ppermute(leaves, "mem", pairs(members, bit)), leaves]
+
+    def doubled(part, bit):
+        beside = lax.ppermute(part, "mem", pairs(members, bit))
+        mine = (member // bit) % 2
+        return jnp.where(mine == 0, jnp.concatenate([part, beside], axis=1), jnp.concatenate([beside, part], axis=1))
+
+    def gathered(part):
+        for bit in reversed(bits):
+            part = doubled(part, bit)
+        return part
+
     carry = None
+    sums = []
+    for k, window in enumerate(windows):
+        waits = []
+        if k + 2 < len(windows):
+            waits.append(fetch_rows(k + 2, [remotes[k]] if carry is None else [remotes[k], carry]))
+        for j in range(k - 1):
+            sums[j] = halved(sums[j], bits[k - 1 - j])
+            waits.append(sums[j][2])
+        keep, send, carry = window_tensor(window, place, local, remotes[k], table, waits, carry)
+        sums.append([keep, lax.ppermute(send, "mem", pairs(members, bits[0]))])
     pieces = {"own": [], "both": [], "other": []}
-    for window, remote in zip(windows, remotes):
-        keep, send, carry = window_tensor(window, place, local, remote, table, carry)
-        received = lax.ppermute(send, "mem", pairs(members, 1))
-        quarter = window.width // 4
-
-        def of_side(which):
-            first = which * quarter
-            return lax.dynamic_slice_in_dim(keep, first, quarter, axis=1) + lax.dynamic_slice_in_dim(
-                received, first, quarter, axis=1
-            )
-
-        total = of_side(side) + lax.ppermute(of_side(1 - side), "mem", pairs(members, 2))
-        summed = lax.psum_scatter(total, "mem", scatter_dimension=1, axis_index_groups=columns_of, tiled=True)
-        pieces[window.side].append(exponent_of(summed, members))
+    for k, window in enumerate(windows):
+        for bit in bits[max(len(windows) - 1 - k, 1) :]:
+            sums[k] = halved(sums[k], bit)
+        pieces[window.side].append(exponent_of(sums[k][0] + sums[k][1], members))
 
     other = lax.ppermute(jnp.stack(pieces["other"]), "band", swap)
     trades = []
@@ -373,32 +419,21 @@
             trades.append((m * 2 + b, mate[0] * 2 + mate[1]))
     both = lax.ppermute(pieces["both"][0], ("mem", "band"), trades)
 
-    def gathered(stack):
-        whole = lax.all_gather(stack, "mem", axis_index_groups=columns_of, axis=1, tiled=True)
-        beside = lax.ppermute(whole, "mem", pairs(members, 2))
-        whole = jnp.where(side == 0, jnp.concatenate([whole, beside], axis=1), jnp.concatenate([beside, whole], axis=1))
-        beside = lax.ppermute(whole, "mem", pairs(members, 1))
-        return jnp.where(core == 0, jnp.concatenate([whole, beside], axis=1), jnp.concatenate([beside, whole], axis=1))
-
-    own = gathered(jnp.stack(pieces["own"]))
-    late = gathered(jnp.concatenate([other, both[None]]))
-    other, both = late[:-1], late[-1]
+    early = gathered(jnp.concatenate([other, both[None]]))
+    other, both = early[:-1], early[-1]
     middle = both.shape[0] // 2
     low, high = both[:middle], both[middle:]
-
-    up = jnp.stack(
-        [
-            jnp.concatenate([*own, low]),
-            jnp.concatenate([*other[::-1], high]),
-        ]
-    )
-    down = jnp.stack(
-        [
-            jnp.concatenate([low, *other]),
-            jnp.concatenate([high, *own[::-1]]),
-        ]
-    )
-    return jnp.where(band == 0, up, down)
+    rest = jnp.zeros((nlat // 2 - middle, NLON), jnp.float32)
+    down = jnp.stack([jnp.concatenate([rest, low]), jnp.concatenate([*other, high])])
+    up = jnp.stack([jnp.concatenate([low, *other[::-1]]), jnp.concatenate([high, rest])])
+    out = jnp.where(band == 0, down, up)
+
+    own = gathered(jnp.stack(pieces["own"]))
+    for k, block in enumerate(own):
+        width = block.shape[0]
+        row = choose(band, (nlat // 2 - middle - (k + 1) * width, middle + k * width))
+        out = lax.dynamic_update_slice(out, block[None], (band, row.astype(jnp.int32), jnp.int32(0)))
+    return out
 
 
 def per_device(coeffs):

time: 290 us -> 327 us (1.13)
  Pallas kernels: 60.1 us -> 171 us
  blocking collectives: 30 us -> 0 us
  waiting for transfers between devices: 124 us -> 94.4 us
  between operations: 13.6 us -> 0.64 us
  starting transfers between devices: 19.1 us -> 30.5 us
  other arithmetic: 21.1 us -> 10.5 us
    pallas_call x5 -> x10, Pallas kernels: 53.5 us -> 154 us  [the longest x5 105 us: piece_of(): pl.pallas_call(piece_kernel, in_specs=[pl.BlockSpec(memory_space=pltpu.SM...]
    reduce_scatter x5 -> x0, waiting for transfers between devices: 39.9 us -> none  [by_levels(): lax.psum_scatter(total, 'mem', scatter_dimension=1, axis_index_groups=col...]
    all_gather x2 -> x0, blocking collectives: 30 us -> none  [gathered(): lax.all_gather(stack, 'mem', axis_index_groups=columns_of, axis=1, tiled=...]
    ppermute x18 -> x32, starting transfers between devices: 13.6 us -> 26.2 us  [the longest x15 17.1 us: halved(): lax.ppermute(leaves, 'mem', pairs(members, bit))]
    ppermute x18 -> x32, waiting for transfers between devices: 83.6 us -> 94.4 us  [the longest x15 55.5 us: halved(): lax.ppermute(leaves, 'mem', pairs(members, bit))]
    pallas_call x3, Pallas kernels: 6.56 us -> 16.2 us  [rows_first(): pl.pallas_call(transpose_kernel, grid_spec=pltpu.PrefetchScalarGridSpec(n...]
    add x10 -> x15, other arithmetic: 13 us -> 6.05 us  [total(): sum((lax.dynamic_slice_in_dim(part, which * half, half, axis=1) for part...]
    div x5, other arithmetic: 4.56 us -> 1.02 us  [exponent_of(): mean = summed / members]
  transfers between devices with their start and end apart: 26 -> 35, of which waited for: 8 -> 15; matrix products, arithmetic and copies ran while one was open for 7% -> 3% of each run, Pallas kernels for 20% -> 45%
where the time goes in v3:
time: 327 us; the launch traced here: 326 us
  Pallas kernels  171 us (52%)
  waiting for transfers between devices  94.4 us (29%)
  starting transfers between devices  30.5 us (9%)
  local copies, waits for them, and re-layouts  19.5 us (6%)
  other arithmetic  10.5 us (3%)
    pallas_call x5, Pallas kernels, piece_of(): pl.pallas_call(piece_kernel, in_specs=[pl.BlockSpec(memory_space=pltpu.SM...  105 us
    ppermute x15, waiting for transfers between devices, halved(): lax.ppermute(leaves, 'mem', pairs(members, bit))  55.5 us
    pallas_call x5, Pallas kernels, window_tensor(): pl.pallas_call(functools.partial(window_kernel, window, depth, len(waits)...  49.7 us
    ppermute x8, waiting for transfers between devices, doubled(): beside = lax.ppermute(part, 'mem', pairs(members, bit))  23 us
    unnamed x42, local copies, waits for them, and re-layouts  18.5 us
    ppermute x15, starting transfers between devices, halved(): lax.ppermute(leaves, 'mem', pairs(members, bit))  17.1 us
    pallas_call x3, Pallas kernels, rows_first(): pl.pallas_call(transpose_kernel, grid_spec=pltpu.PrefetchScalarGridSpec(n...  16.2 us
    ppermute x4, waiting for transfers between devices, fetch_rows(): remotes.append(lax.ppermute(piece, 'band', swap))  15.9 us
  transfers between devices with their start and end apart: 35, of which 15 were waited for; matrix products, arithmetic and copies ran while one was open for 3% of the time, Pallas kernels for 45%

profile of v3, /device:TPU:0, one launch (start us, length us, event | category | flops | bytes accessed | tf_op | source)
XLA Modules:
  0.0 326.2 jit_solution(3579401774260917205)
XLA Ops:
  0.1 3.1 rows_first.4.from_ref
  4.2 22.2 %piece_of.5 = f32[2,136,640]{2,1,0:T(8,128)} custom-call(s32[1]{0:T(128)} %bitcast.3.start_ref, f32[2,256,640]{2,1,0:T(8,128)} %copy-done.1), custom_call_target="tpu_custom_call" | custom-call | bytes 1392640 | tf_op jit(solution)/shard_map/piece_of/pallas_call | solution.py:178
  26.4 3.0 collective-permute-start
  29.5 6.6 %rows_first.5.from_ref = f32[2,640,640]{2,1,0:T(8,128)S(1)} custom-call(s32[2]{0:T(128)S(1)} %pad_add_fusion.place, f32[2,2,640,640]{3,2,1,0:T(8,128)} %bitcast.30), custom_call_target="tpu_custom_call" | custom-call | bytes 26214400 | tf_op jit(solution)/shard_map/rows_first/pallas_call | solution.py:152
  36.1 1.7 copy-done
  37.8 21.0 %piece_of.7 = f32[2,128,640]{2,1,0:T(8,128)} custom-call(s32[1]{0:T(128)} %bitcast.7.start_ref, f32[2,640,640]{2,1,0:T(8,128)} %copy-done), custom_call_target="tpu_custom_call" | custom-call | bytes 1310720 | tf_op jit(solution)/shard_map/piece_of/pallas_call | solution.py:178
  58.9 6.6 %rows_first.3.refs_1_ = f32[2,640,640]{2,1,0:T(8,128)S(1)} custom-call(s32[2]{0:T(128)S(1)} %get-tuple-element.61.place, f32[2,2,640,640]{3,2,1,0:T(8,128)} %bitcast.31), custom_call_target="tpu_custom_call" | custom-call | bytes 26214400 | tf_op jit(solution)/shard_map/rows_first/pallas_call | solution.py:152
  65.5 21.0 %piece_of.6.refs_5_ = f32[2,128,640]{2,1,0:T(8,128)} custom-call(s32[1]{0:T(128)} %bitcast.6.start_ref, f32[2,640,640]{2,1,0:T(8,128)} %copy-done, f32[2,136,640]{2,1,0:T(8,128)} %collective-permute-done.refs_0_.refs_2_), custom_call_target="tpu_custom_call" | custom-call | bytes 1310720 | tf_op jit(solution)/shard_map/piece_of/pallas_call | solution.py:178
  86.5 1.9 copy-done.13
  88.4 1.9 copy-done.16
  90.3 10.7 %window_tensor.5 = (f32[3,64,1280]{2,1,0:T(8,128)S(1)}, f32[3,64,1280]{2,1,0:T(8,128)}, f32[2,16,1280]{2,1,0:T(8,128)S(1)}) custom-call(s32[2]{0:T(128)S(1)} %get-tuple-element.62.refs_0_, f32[2,640,640]{2,1,0:T(8,128)S(1)} %rows_first.3.refs_1_, f32[2,136,640]{2,1,0:T(8,128)} %collective-permute-done.refs_0_.refs_2_, bf16[1280,1280]{1,0:T(8,128)(2,1)S(1)} %copy-done.13, ...), custom_call_target="tpu_custom_call" | custom-call | flops 13369344000 | bytes 9912320 | tf_op jit(solution)/shard_map/window_tensor/pallas_call | solution.py:317
  102.7 21.0 %piece_of.8.refs_5_ = f32[2,128,640]{2,1,0:T(8,128)} custom-call(s32[1]{0:T(128)} %bitcast.8.start_ref, f32[2,640,640]{2,1,0:T(8,128)} %copy-done, f32[2,128,640]{2,1,0:T(8,128)} %collective-permute-done.5.refs_0_.refs_2_, f32[2,16,1280]{2,1,0:T(8,128)} %copy-done.11), custom_call_target="tpu_custom_call" | custom-call | bytes 1310720 | tf_op jit(solution)/shard_map/piece_of/pallas_call | solution.py:178
  124.8 1.9 copy-done.14
  126.7 1.9 copy-done.17
  128.6 10.4 %window_tensor.6 = (f32[3,64,1280]{2,1,0:T(8,128)S(1)}, f32[3,64,1280]{2,1,0:T(8,128)}, f32[2,16,1280]{2,1,0:T(8,128)S(1)}) custom-call(s32[2]{0:T(128)S(1)} %get-tuple-element.62.refs_0_, f32[2,640,640]{2,1,0:T(8,128)S(1)} %rows_first.3.refs_1_, f32[2,128,640]{2,1,0:T(8,128)} %collective-permute-done.5.refs_0_.refs_2_, bf16[1280,1280]{1,0:T(8,128)(2,1)S(1)} %copy-done.14, ...), custom_call_target="tpu_custom_call" | custom-call | flops 12582912000 | bytes 9830400 | tf_op jit(solution)/shard_map/window_tensor/pallas_call | solution.py:317
  141.1 2.0 collective-permute-start.11
  143.2 15.8 %collective-permute-done.11.refs_0_.refs_2_ = f32[2,128,640]{2,1,0:T(8,128)} collective-permute-done((f32[2,128,640]{2,1,0:T(8,128)}, f32[2,128,640]{2,1,0:T(8,128)}, u32[]{:S(2)}, u32[]{:S(2)}) %collective-permute-start.11) | collective-permute-done | bytes 655392 | tf_op jit(solution)/shard_map/ppermute | solution.py:369
  159.0 19.7 %piece_of.9.refs_5_ = f32[2,120,640]{2,1,0:T(8,128)} custom-call(s32[1]{0:T(128)} %bitcast.9.start_ref, f32[2,640,640]{2,1,0:T(8,128)} %copy-done, f32[2,128,640]{2,1,0:T(8,128)} %collective-permute-done.11.refs_0_.refs_2_, f32[2,16,1280]{2,1,0:T(8,128)} %copy-done.9), custom_call_target="tpu_custom_call" | custom-call | bytes 1228800 | tf_op jit(solution)/shard_map/piece_of/pallas_call | solution.py:178
  178.7 2.1 collective-permute-start.26
  180.8 1.7 dynamic-slice_add_fusion.9
  182.6 1.6 collective-permute-start.2
  186.1 1.9 copy-done.18
  188.0 9.4 %window_tensor.7 = (f32[3,64,1280]{2,1,0:T(8,128)S(1)}, f32[3,64,1280]{2,1,0:T(8,128)S(1)}, f32[2,16,1280]{2,1,0:T(8,128)S(1)}) custom-call(s32[2]{0:T(128)S(1)} %get-tuple-element.62.refs_0_, f32[2,640,640]{2,1,0:T(8,128)S(1)} %rows_first.3.refs_1_, f32[2,128,640]{2,1,0:T(8,128)} %collective-permute-done.11.refs_0_.refs_2_, ...), custom_call_target="tpu_custom_call" | custom-call | flops 12582912000 | bytes 9830400 | tf_op jit(solution)/shard_map/window_tensor/pallas_call | solution.py:317
  197.6 1.7 collective-permute-start.3
  199.3 5.0 %collective-permute-done.7 = f32[3,32,1280]{2,1,0:T(8,128)S(1)} collective-permute-done((f32[3,32,1280]{2,1,0:T(8,128)S(1)}, f32[3,32,1280]{2,1,0:T(8,128)S(1)}, u32[]{:S(2)}, u32[]{:S(2)}) %collective-permute-start.7) | collective-permute-done | bytes 491552 | tf_op jit(solution)/shard_map/ppermute | solution.py:385
  204.3 1.6 collective-permute-start.8
  206.0 9.6 %window_tensor.8 = (f32[3,64,1280]{2,1,0:T(8,128)S(1)}, f32[3,64,1280]{2,1,0:T(8,128)S(1)}, f32[2,16,1280]{2,1,0:T(8,128)S(1)}) custom-call(s32[2]{0:T(128)S(1)} %get-tuple-element.62.refs_0_, f32[2,640,640]{2,1,0:T(8,128)S(1)} %rows_first.3.refs_1_, f32[2,128,640]{2,1,0:T(8,128)} %collective-permute-done.21.refs_2_, bf16[1280,1280]{1,0:T(8,128)(2,1)S(1)} %copy-done.15, ...), custom_call_target="tpu_custom_call" | custom-call | flops 12582912000 | bytes 9830400 | tf_op jit(solution)/shard_map/window_tensor/pallas_call | solution.py:317
  215.7 2.7 collective-permute-start.4
  218.8 8.8 %collective-permute-done.4 = f32[3,8,1280]{2,1,0:T(8,128)S(1)} collective-permute-done((f32[3,8,1280]{2,1,0:T(8,128)S(1)}, f32[3,8,1280]{2,1,0:T(8,128)S(1)}, u32[]{:S(2)}, u32[]{:S(2)}) %collective-permute-start.4) | collective-permute-done | bytes 122912 | tf_op jit(solution)/shard_map/ppermute | solution.py:385
  227.6 2.5 collective-permute-done.9
  230.3 1.6 collective-permute-start.13
  232.5 11.0 %collective-permute-done.13 = f32[3,32,1280]{2,1,0:T(8,128)S(1)} collective-permute-done((f32[3,32,1280]{2,1,0:T(8,128)S(1)}, f32[3,32,1280]{2,1,0:T(8,128)S(1)}, u32[]{:S(2)}, u32[]{:S(2)}) %collective-permute-start.13) | collective-permute-done | bytes 491552 | tf_op jit(solution)/shard_map/ppermute | solution.py:385
  243.7 9.6 %window_tensor.9 = (f32[3,64,1280]{2,1,0:T(8,128)S(1)}, f32[3,64,1280]{2,1,0:T(8,128)}) custom-call(s32[2]{0:T(128)S(1)} %get-tuple-element.62.refs_0_, f32[2,640,640]{2,1,0:T(8,128)S(1)} %rows_first.3.refs_1_, f32[2,120,640]{2,1,0:T(8,128)S(1)} %collective-permute-done.26.refs_2_, bf16[1280,1280]{1,0:T(8,128)(2,1)S(1)} %copy-done.15, ...), custom_call_target="tpu_custom_call" | custom-call | flops 11796480000 | bytes 9748480 | tf_op jit(solution)/shard_map/window_tensor/pallas_call | solution.py:317
  253.4 2.8 collective-permute-start.15
  258.7 4.2 %collective-permute-done.15 = f32[3,8,1280]{2,1,0:T(8,128)S(1)} collective-permute-done((f32[3,8,1280]{2,1,0:T(8,128)S(1)}, f32[3,8,1280]{2,1,0:T(8,128)S(1)}, u32[]{:S(2)}, u32[]{:S(2)}) %collective-permute-start.15) | collective-permute-done | bytes 122912 | tf_op jit(solution)/shard_map/ppermute | solution.py:385
  263.8 6.9 %collective-permute-done.23 = f32[3,32,1280]{2,1,0:T(8,128)S(1)} collective-permute-done((f32[3,32,1280]{2,1,0:T(8,128)}, f32[3,32,1280]{2,1,0:T(8,128)S(1)}, u32[]{:S(2)}, u32[]{:S(2)}) %collective-permute-start.23) | collective-permute-done | bytes 491552 | tf_op jit(solution)/shard_map/ppermute | solution.py:385
  272.3 1.5 collective-permute-start.28
  273.9 2.1 collective-permute-start.18
  275.9 4.6 %collective-permute-done.24 = f32[3,16,1280]{2,1,0:T(8,128)S(1)} collective-permute-done((f32[3,16,1280]{2,1,0:T(8,128)}, f32[3,16,1280]{2,1,0:T(8,128)S(1)}, u32[]{:S(2)}, u32[]{:S(2)}) %collective-permute-start.24) | collective-permute-done | bytes 245792 | tf_op jit(solution)/shard_map/ppermute | solution.py:385
  280.9 5.2 %collective-permute-done.18 = f32[3,16,1280]{2,1,0:T(8,128)S(1)} collective-permute-done((f32[3,16,1280]{2,1,0:T(8,128)S(1)}, f32[3,16,1280]{2,1,0:T(8,128)S(1)}, u32[]{:S(2)}, u32[]{:S(2)}) %collective-permute-start.18) | collective-permute-done | bytes 245792 | tf_op jit(solution)/shard_map/ppermute | solution.py:388
  286.1 1.6 collective-permute-start.19
  289.3 4.7 %collective-permute-done.29 = f32[3,16,1280]{2,1,0:T(8,128)S(1)} collective-permute-done((f32[3,16,1280]{2,1,0:T(8,128)S(1)}, f32[3,16,1280]{2,1,0:T(8,128)S(1)}, u32[]{:S(2)}, u32[]{:S(2)}) %collective-permute-start.29) | collective-permute-done | bytes 245792 | tf_op jit(solution)/shard_map/ppermute | solution.py:385
  294.8 7.3 %collective-permute-done.30 = f32[3,8,1280]{2,1,0:T(8,128)S(1)} collective-permute-done((f32[3,8,1280]{2,1,0:T(8,128)S(1)}, f32[3,8,1280]{2,1,0:T(8,128)S(1)}, u32[]{:S(2)}, u32[]{:S(2)}) %collective-permute-start.30) | collective-permute-done | bytes 122912 | tf_op jit(solution)/shard_map/ppermute | solution.py:385
  302.4 5.5 %collective-permute-done.31 = f32[2,8,1280]{2,1,0:T(8,128)S(1)} collective-permute-done((f32[2,8,1280]{2,1,0:T(8,128)S(1)}, f32[2,8,1280]{2,1,0:T(8,128)S(1)}, u32[]{:S(2)}, u32[]{:S(2)}) %collective-permute-start.31) | collective-permute-done | bytes 81952 | tf_op jit(solution)/shard_map/ppermute | solution.py:388
  308.0 5.3 %collective-permute-done.32 = f32[2,16,1280]{2,1,0:T(8,128)S(1)} collective-permute-done((f32[2,16,1280]{2,1,0:T(8,128)S(1)}, f32[2,16,1280]{2,1,0:T(8,128)S(1)}, u32[]{:S(2)}, u32[]{:S(2)}) %collective-permute-start.32) | collective-permute-done | bytes 163872 | tf_op jit(solution)/shard_map/ppermute | solution.py:388
  313.4 7.0 %collective-permute-done.33 = f32[2,32,1280]{2,1,0:T(8,128)S(1)} collective-permute-done((f32[2,32,1280]{2,1,0:T(8,128)S(1)}, f32[2,32,1280]{2,1,0:T(8,128)S(1)}, u32[]{:S(2)}, u32[]{:S(2)}) %collective-permute-start.33) | collective-permute-done | bytes 327712 | tf_op jit(solution)/shard_map/ppermute | solution.py:388
  320.6 1.7 maximum_select_fusion.1
  323.6 1.7 copy-done.19
  (122 shorter events, 20.4 us)
Async XLA Ops:
  26.4 39.1 %collective-permute-start = (f32[2,136,640]{2,1,0:T(8,128)}, f32[2,136,640]{2,1,0:T(8,128)}, u32[]{:S(2)}, u32[]{:S(2)}) collective-permute-start(f32[2,136,640]{2,1,0:T(8,128)} %piece_of.5), channel_id=1, source_target_pairs={{0,1},{1,0},{2,3},{3,2},{4,5},{5,4},{6,7},{7,6},{8,9},{9,8},{10,11... | collective-permute-start | bytes 2088968 | tf_op jit(solution)/shard_map/ppermute | solution.py:363
  58.7 44.0 %collective-permute-start.5 = (f32[2,128,640]{2,1,0:T(8,128)}, f32[2,128,640]{2,1,0:T(8,128)}, u32[]{:S(2)}, u32[]{:S(2)}) collective-permute-start(f32[2,128,640]{2,1,0:T(8,128)} %piece_of.7), channel_id=1, source_target_pairs={{0,1},{1,0},{2,3},{3,2},{4,5},{5,4},{6,7},{7,6},{8,9},{9,8},{10,11... | collective-permute-start | bytes 1966088 | tf_op jit(solution)/shard_map/ppermute | solution.py:369
  86.5 1.9 copy-start.13
  88.4 1.9 copy-start.16
  102.7 78.2 %collective-permute-start.1 = (f32[3,64,1280]{2,1,0:T(8,128)}, f32[3,64,1280]{2,1,0:T(8,128)}, u32[]{:S(2)}, u32[]{:S(2)}) collective-permute-start(f32[3,64,1280]{2,1,0:T(8,128)} %get-tuple-element.20), channel_id=1, source_target_pairs={{0,2},{2,0},{4,6},{6,4},{8,10},{10,8},{12,14},{14,12},{16,18},{18,... | collective-permute-start | bytes 2949128 | tf_op jit(solution)/shard_map/ppermute | solution.py:407
  102.7 21.0 %copy-start.12 = (f32[2,16,1280]{2,1,0:T(8,128)S(1)}, f32[2,16,1280]{2,1,0:T(8,128)}, u32[]{:S(2)}) copy-start(f32[2,16,1280]{2,1,0:T(8,128)} %copy-done.11) | copy-start | bytes 491524
  124.8 1.9 copy-start.14
  126.7 1.9 copy-start.17
  140.6 43.6 %collective-permute-start.6 = (f32[3,64,1280]{2,1,0:T(8,128)}, f32[3,64,1280]{2,1,0:T(8,128)}, u32[]{:S(2)}, u32[]{:S(2)}) collective-permute-start(f32[3,64,1280]{2,1,0:T(8,128)} %get-tuple-element.23), channel_id=1, source_target_pairs={{0,2},{2,0},{4,6},{6,4},{8,10},{10,8},{12,14},{14,12},{16,18},{18,... | collective-permute-start | bytes 2949128 | tf_op jit(solution)/shard_map/ppermute | solution.py:407
  141.1 17.9 %collective-permute-start.11 = (f32[2,128,640]{2,1,0:T(8,128)}, f32[2,128,640]{2,1,0:T(8,128)}, u32[]{:S(2)}, u32[]{:S(2)}) collective-permute-start(f32[2,128,640]{2,1,0:T(8,128)} %piece_of.6.refs_5_), channel_id=1, source_target_pairs={{0,1},{1,0},{2,3},{3,2},{4,5},{5,4},{6,7},{7,6},{8,9},{9,8},{10,11... | collective-permute-start | bytes 1966088 | tf_op jit(solution)/shard_map/ppermute | solution.py:369
  143.1 62.8 %collective-permute-start.21 = (f32[2,128,640]{2,1,0:T(8,128)}, f32[2,128,640]{2,1,0:T(8,128)}, u32[]{:S(2)}, u32[]{:S(2)}) collective-permute-start(f32[2,128,640]{2,1,0:T(8,128)} %piece_of.8.refs_5_), channel_id=1, source_target_pairs={{0,1},{1,0},{2,3},{3,2},{4,5},{5,4},{6,7},{7,6},{8,9},{9,8},{10,11... | collective-permute-start | bytes 1966088 | tf_op jit(solution)/shard_map/ppermute | solution.py:369
  178.7 5.4 %copy-start.4 = (f32[3,64,1280]{2,1,0:T(8,128)S(1)}, f32[3,64,1280]{2,1,0:T(8,128)}, u32[]{:S(2)}) copy-start(f32[3,64,1280]{2,1,0:T(8,128)} %copy-done.3) | copy-start | bytes 2949124
  178.7 65.0 %collective-permute-start.26 = (f32[2,120,640]{2,1,0:T(8,128)}, f32[2,120,640]{2,1,0:T(8,128)S(1)}, u32[]{:S(2)}, u32[]{:S(2)}) collective-permute-start(f32[2,120,640]{2,1,0:T(8,128)} %piece_of.9.refs_5_), channel_id=1, source_target_pairs={{0,1},{1,0},{2,3},{3,2},{4,5},{5,4},{6,7},{7,6},{8,9},{9,8},{10,11... | collective-permute-start | bytes 1843208 | tf_op jit(solution)/shard_map/ppermute | solution.py:369
  180.8 5.3 %copy-start.15 = (bf16[1280,1280]{1,0:T(8,128)(2,1)S(1)}, bf16[1280,1280]{1,0:T(8,128)(2,1)}, u32[]{:S(2)}) copy-start(bf16[1280,1280]{1,0:T(8,128)(2,1)} %constant.208.clone.refs_3_) | copy-start | bytes 9830404
  182.6 3.5 %copy-start.8 = (f32[2,120,640]{2,1,0:T(8,128)S(1)}, f32[2,120,640]{2,1,0:T(8,128)}, u32[]{:S(2)}) copy-start(f32[2,120,640]{2,1,0:T(8,128)} %piece_of.9.refs_5_) | copy-start | bytes 1843204
  182.6 3.5 %copy-start.10 = (f32[2,16,1280]{2,1,0:T(8,128)S(1)}, f32[2,16,1280]{2,1,0:T(8,128)}, u32[]{:S(2)}) copy-start(f32[2,16,1280]{2,1,0:T(8,128)} %copy-done.9) | copy-start | bytes 491524
  182.6 14.9 %collective-permute-start.2 = (f32[3,32,1280]{2,1,0:T(8,128)S(1)}, f32[3,32,1280]{2,1,0:T(8,128)S(1)}, u32[]{:S(2)}, u32[]{:S(2)}) collective-permute-start(f32[3,32,1280]{2,1,0:T(8,128)S(1)} %get-tuple-element.42.refs_6_), channel_id=1, source_target_pairs={{0,4},{2,6},{4,0},{6,2},{8,12},{10,14},{12,8},{14,10},{16,20},{18,... | collective-permute-start | bytes 1474568 | tf_op jit(solution)/shard_map/ppermute | solution.py:385
  185.5 18.7 %collective-permute-start.7 = (f32[3,32,1280]{2,1,0:T(8,128)S(1)}, f32[3,32,1280]{2,1,0:T(8,128)S(1)}, u32[]{:S(2)}, u32[]{:S(2)}) collective-permute-start(f32[3,32,1280]{2,1,0:T(8,128)S(1)} %get-tuple-element.44.refs_6_), channel_id=1, source_target_pairs={{0,4},{2,6},{4,0},{6,2},{8,12},{10,14},{12,8},{14,10},{16,20},{18,... | collective-permute-start | bytes 1474568 | tf_op jit(solution)/shard_map/ppermute | solution.py:385
  186.1 1.9 copy-start.18
  197.5 32.7 %collective-permute-start.12 = (f32[3,64,1280]{2,1,0:T(8,128)S(1)}, f32[3,64,1280]{2,1,0:T(8,128)S(1)}, u32[]{:S(2)}, u32[]{:S(2)}) collective-permute-start(f32[3,64,1280]{2,1,0:T(8,128)S(1)} %get-tuple-element.26), channel_id=1, source_target_pairs={{0,2},{2,0},{4,6},{6,4},{8,10},{10,8},{12,14},{14,12},{16,18},{18,... | collective-permute-start | bytes 2949128 | tf_op jit(solution)/shard_map/ppermute | solution.py:407
  197.6 18.0 %collective-permute-start.3 = (f32[3,16,1280]{2,1,0:T(8,128)S(1)}, f32[3,16,1280]{2,1,0:T(8,128)S(1)}, u32[]{:S(2)}, u32[]{:S(2)}) collective-permute-start(f32[3,16,1280]{2,1,0:T(8,128)S(1)} %get-tuple-element.54.refs_5_), channel_id=1, source_target_pairs={{0,8},{2,10},{4,12},{6,14},{8,0},{10,2},{12,4},{14,6},{16,24},{18,... | collective-permute-start | bytes 737288 | tf_op jit(solution)/shard_map/ppermute | solution.py:385
  204.3 14.0 %collective-permute-start.8 = (f32[3,16,1280]{2,1,0:T(8,128)S(1)}, f32[3,16,1280]{2,1,0:T(8,128)S(1)}, u32[]{:S(2)}, u32[]{:S(2)}) collective-permute-start(f32[3,16,1280]{2,1,0:T(8,128)S(1)} %get-tuple-element.56.refs_6_), channel_id=1, source_target_pairs={{0,8},{2,10},{4,12},{6,14},{8,0},{10,2},{12,4},{14,6},{16,24},{18,... | collective-permute-start | bytes 737288 | tf_op jit(solution)/shard_map/ppermute | solution.py:385
  215.6 40.7 %collective-permute-start.22 = (f32[3,64,1280]{2,1,0:T(8,128)S(1)}, f32[3,64,1280]{2,1,0:T(8,128)S(1)}, u32[]{:S(2)}, u32[]{:S(2)}) collective-permute-start(f32[3,64,1280]{2,1,0:T(8,128)S(1)} %get-tuple-element.29), channel_id=1, source_target_pairs={{0,2},{2,0},{4,6},{6,4},{8,10},{10,8},{12,14},{14,12},{16,18},{18,... | collective-permute-start | bytes 2949128 | tf_op jit(solution)/shard_map/ppermute | solution.py:407
  215.7 11.9 %collective-permute-start.4 = (f32[3,8,1280]{2,1,0:T(8,128)S(1)}, f32[3,8,1280]{2,1,0:T(8,128)S(1)}, u32[]{:S(2)}, u32[]{:S(2)}) collective-permute-start(f32[3,8,1280]{2,1,0:T(8,128)S(1)} %dynamic-slice_add_fusion.24.refs_5_), channel_id=1, source_target_pairs={{0,16},{2,18},{4,20},{6,22},{8,24},{10,26},{12,28},{14,30},{16,0},... | collective-permute-start | bytes 368648 | tf_op jit(solution)/shard_map/ppermute | solution.py:385
  218.4 11.8 %collective-permute-start.9 = (f32[3,8,1280]{2,1,0:T(8,128)S(1)}, f32[3,8,1280]{2,1,0:T(8,128)S(1)}, u32[]{:S(2)}, u32[]{:S(2)}) collective-permute-start(f32[3,8,1280]{2,1,0:T(8,128)S(1)} %dynamic-slice_add_fusion.23), channel_id=1, source_target_pairs={{0,16},{2,18},{4,20},{6,22},{8,24},{10,26},{12,28},{14,30},{16,0},... | collective-permute-start | bytes 368648 | tf_op jit(solution)/shard_map/ppermute | solution.py:385
  230.3 13.3 %collective-permute-start.13 = (f32[3,32,1280]{2,1,0:T(8,128)S(1)}, f32[3,32,1280]{2,1,0:T(8,128)S(1)}, u32[]{:S(2)}, u32[]{:S(2)}) collective-permute-start(f32[3,32,1280]{2,1,0:T(8,128)S(1)} %get-tuple-element.46.refs_7_), channel_id=1, source_target_pairs={{0,4},{2,6},{4,0},{6,2},{8,12},{10,14},{12,8},{14,10},{16,20},{18,... | collective-permute-start | bytes 1474568 | tf_op jit(solution)/shard_map/ppermute | solution.py:385
  231.9 31.7 %collective-permute-start.10 = (f32[2,8,1280]{2,1,0:T(8,128)S(1)}, f32[2,8,1280]{2,1,0:T(8,128)S(1)}, u32[]{:S(2)}, u32[]{:S(2)}) collective-permute-start(f32[2,8,1280]{2,1,0:T(8,128)S(1)} %pad_maximum_fusion.1), channel_id=1, source_target_pairs={{0,1},{1,0},{2,3},{3,2},{4,5},{5,4},{6,7},{7,6},{8,9},{9,8},{10,11... | collective-permute-start | bytes 245768 | tf_op jit(solution)/shard_map/ppermute | solution.py:414
  243.6 9.8 %collective-permute-start.14 = (f32[3,16,1280]{2,1,0:T(8,128)S(1)}, f32[3,16,1280]{2,1,0:T(8,128)S(1)}, u32[]{:S(2)}, u32[]{:S(2)}) collective-permute-start(f32[3,16,1280]{2,1,0:T(8,128)S(1)} %get-tuple-element.58), channel_id=1, source_target_pairs={{0,8},{2,10},{4,12},{6,14},{8,0},{10,2},{12,4},{14,6},{16,24},{18,... | collective-permute-start | bytes 737288 | tf_op jit(solution)/shard_map/ppermute | solution.py:385
  253.3 3.8 %copy-start.5 = (f32[3,64,1280]{2,1,0:T(8,128)}, f32[3,64,1280]{2,1,0:T(8,128)S(1)}, u32[]{:S(2)}) copy-start(f32[3,64,1280]{2,1,0:T(8,128)S(1)} %get-tuple-element.31) | copy-start | bytes 2949124
  253.3 18.1 %collective-permute-start.27 = (f32[3,64,1280]{2,1,0:T(8,128)}, f32[3,64,1280]{2,1,0:T(8,128)S(1)}, u32[]{:S(2)}, u32[]{:S(2)}) collective-permute-start(f32[3,64,1280]{2,1,0:T(8,128)} %get-tuple-element.32), channel_id=1, source_target_pairs={{0,2},{2,0},{4,6},{6,4},{8,10},{10,8},{12,14},{14,12},{16,18},{18,... | collective-permute-start | bytes 2949128 | tf_op jit(solution)/shard_map/ppermute | solution.py:407
  253.4 9.4 %collective-permute-start.15 = (f32[3,8,1280]{2,1,0:T(8,128)S(1)}, f32[3,8,1280]{2,1,0:T(8,128)S(1)}, u32[]{:S(2)}, u32[]{:S(2)}) collective-permute-start(f32[3,8,1280]{2,1,0:T(8,128)S(1)} %dynamic-slice_add_fusion.22), channel_id=1, source_target_pairs={{0,16},{2,18},{4,20},{6,22},{8,24},{10,26},{12,28},{14,30},{16,0},... | collective-permute-start | bytes 368648 | tf_op jit(solution)/shard_map/ppermute | solution.py:385
  257.2 14.3 %copy-start.6 = (f32[3,64,1280]{2,1,0:T(8,128)S(1)}, f32[3,64,1280]{2,1,0:T(8,128)}, u32[]{:S(2)}) copy-start(f32[3,64,1280]{2,1,0:T(8,128)} %copy-done.5) | copy-start | bytes 2949124
  257.2 13.5 %collective-permute-start.23 = (f32[3,32,1280]{2,1,0:T(8,128)}, f32[3,32,1280]{2,1,0:T(8,128)S(1)}, u32[]{:S(2)}, u32[]{:S(2)}) collective-permute-start(f32[3,32,1280]{2,1,0:T(8,128)} %get-tuple-element.34), channel_id=1, source_target_pairs={{0,4},{2,6},{4,0},{6,2},{8,12},{10,14},{12,8},{14,10},{16,20},{18,... | collective-permute-start | bytes 1474568 | tf_op jit(solution)/shard_map/ppermute | solution.py:385
  262.9 0.7 collective-permute-start.16
  263.7 10.2 %collective-permute-start.17 = (f32[3,8,1280]{2,1,0:T(8,128)S(1)}, f32[3,8,1280]{2,1,0:T(8,128)S(1)}, u32[]{:S(2)}, u32[]{:S(2)}) collective-permute-start(f32[3,8,1280]{2,1,0:T(8,128)S(1)} %pad_maximum_fusion), channel_id=1, source_target_pairs={{0,16},{2,18},{4,20},{6,22},{8,24},{10,26},{12,28},{14,30},{16,0},... | collective-permute-start | bytes 368648 | tf_op jit(solution)/shard_map/ppermute | solution.py:388
  271.4 9.1 %collective-permute-start.24 = (f32[3,16,1280]{2,1,0:T(8,128)}, f32[3,16,1280]{2,1,0:T(8,128)S(1)}, u32[]{:S(2)}, u32[]{:S(2)}) collective-permute-start(f32[3,16,1280]{2,1,0:T(8,128)} %get-tuple-element.50), channel_id=1, source_target_pairs={{0,8},{2,10},{4,12},{6,14},{8,0},{10,2},{12,4},{14,6},{16,24},{18,... | collective-permute-start | bytes 737288 | tf_op jit(solution)/shard_map/ppermute | solution.py:385
  272.3 15.3 %collective-permute-start.28 = (f32[3,32,1280]{2,1,0:T(8,128)}, f32[3,32,1280]{2,1,0:T(8,128)S(1)}, u32[]{:S(2)}, u32[]{:S(2)}) collective-permute-start(f32[3,32,1280]{2,1,0:T(8,128)} %get-tuple-element.36), channel_id=1, source_target_pairs={{0,4},{2,6},{4,0},{6,2},{8,12},{10,14},{12,8},{14,10},{16,20},{18,... | collective-permute-start | bytes 1474568 | tf_op jit(solution)/shard_map/ppermute | solution.py:385
  273.9 12.2 %collective-permute-start.18 = (f32[3,16,1280]{2,1,0:T(8,128)S(1)}, f32[3,16,1280]{2,1,0:T(8,128)S(1)}, u32[]{:S(2)}, u32[]{:S(2)}) collective-permute-start(f32[3,16,1280]{2,1,0:T(8,128)S(1)} %maximum_select_fusion.7), channel_id=1, source_target_pairs={{0,8},{2,10},{4,12},{6,14},{8,0},{10,2},{12,4},{14,6},{16,24},{18,... | collective-permute-start | bytes 737288 | tf_op jit(solution)/shard_map/ppermute | solution.py:388
  280.5 5.5 %copy-start.20 = (f32[3,16,1280]{2,1,0:T(8,128)}, f32[3,16,1280]{2,1,0:T(8,128)S(1)}, u32[]{:S(2)}) copy-start(f32[3,16,1280]{2,1,0:T(8,128)S(1)} %collective-permute-done.24) | copy-start | bytes 737284
  280.6 7.8 %collective-permute-start.25 = (f32[3,8,1280]{2,1,0:T(8,128)S(1)}, f32[3,8,1280]{2,1,0:T(8,128)S(1)}, u32[]{:S(2)}, u32[]{:S(2)}) collective-permute-start(f32[3,8,1280]{2,1,0:T(8,128)S(1)} %dynamic-slice_add_fusion.21), channel_id=1, source_target_pairs={{0,16},{2,18},{4,20},{6,22},{8,24},{10,26},{12,28},{14,30},{16,0},... | collective-permute-start | bytes 368648 | tf_op jit(solution)/shard_map/ppermute | solution.py:385
  286.1 16.2 %collective-permute-start.19 = (f32[3,32,1280]{2,1,0:T(8,128)S(1)}, f32[3,32,1280]{2,1,0:T(8,128)S(1)}, u32[]{:S(2)}, u32[]{:S(2)}) collective-permute-start(f32[3,32,1280]{2,1,0:T(8,128)S(1)} %maximum_select_fusion.5), channel_id=1, source_target_pairs={{0,4},{2,6},{4,0},{6,2},{8,12},{10,14},{12,8},{14,10},{16,20},{18,... | collective-permute-start | bytes 1474568 | tf_op jit(solution)/shard_map/ppermute | solution.py:388
  287.7 6.3 %collective-permute-start.29 = (f32[3,16,1280]{2,1,0:T(8,128)S(1)}, f32[3,16,1280]{2,1,0:T(8,128)S(1)}, u32[]{:S(2)}, u32[]{:S(2)}) collective-permute-start(f32[3,16,1280]{2,1,0:T(8,128)S(1)} %get-tuple-element.52), channel_id=1, source_target_pairs={{0,8},{2,10},{4,12},{6,14},{8,0},{10,2},{12,4},{14,6},{16,24},{18,... | collective-permute-start | bytes 737288 | tf_op jit(solution)/shard_map/ppermute | solution.py:385
  294.0 8.1 %collective-permute-start.30 = (f32[3,8,1280]{2,1,0:T(8,128)S(1)}, f32[3,8,1280]{2,1,0:T(8,128)S(1)}, u32[]{:S(2)}, u32[]{:S(2)}) collective-permute-start(f32[3,8,1280]{2,1,0:T(8,128)S(1)} %dynamic-slice_add_fusion.20), channel_id=1, source_target_pairs={{0,16},{2,18},{4,20},{6,22},{8,24},{10,26},{12,28},{14,30},{16,0},... | collective-permute-start | bytes 368648 | tf_op jit(solution)/shard_map/ppermute | solution.py:385
  302.2 5.7 %collective-permute-start.31 = (f32[2,8,1280]{2,1,0:T(8,128)S(1)}, f32[2,8,1280]{2,1,0:T(8,128)S(1)}, u32[]{:S(2)}, u32[]{:S(2)}) collective-permute-start(f32[2,8,1280]{2,1,0:T(8,128)S(1)} %pad_maximum_fusion.2), channel_id=1, source_target_pairs={{0,16},{2,18},{4,20},{6,22},{8,24},{10,26},{12,28},{14,30},{16,0},... | collective-permute-start | bytes 245768 | tf_op jit(solution)/shard_map/ppermute | solution.py:388
  302.3 18.3 %collective-permute-start.20 = (f32[3,64,1280]{2,1,0:T(8,128)S(1)}, f32[3,64,1280]{2,1,0:T(8,128)}, u32[]{:S(2)}, u32[]{:S(2)}) collective-permute-start(f32[3,64,1280]{2,1,0:T(8,128)S(1)} %maximum_select_fusion.3), channel_id=1, source_target_pairs={{0,2},{2,0},{4,6},{6,4},{8,10},{10,8},{12,14},{14,12},{16,18},{18,... | collective-permute-start | bytes 2949128 | tf_op jit(solution)/shard_map/ppermute | solution.py:388
  307.9 5.4 %collective-permute-start.32 = (f32[2,16,1280]{2,1,0:T(8,128)S(1)}, f32[2,16,1280]{2,1,0:T(8,128)S(1)}, u32[]{:S(2)}, u32[]{:S(2)}) collective-permute-start(f32[2,16,1280]{2,1,0:T(8,128)S(1)} %maximum_select_fusion.8), channel_id=1, source_target_pairs={{0,8},{2,10},{4,12},{6,14},{8,0},{10,2},{12,4},{14,6},{16,24},{18,... | collective-permute-start | bytes 491528 | tf_op jit(solution)/shard_map/ppermute | solution.py:388
  313.3 7.1 %collective-permute-start.33 = (f32[2,32,1280]{2,1,0:T(8,128)S(1)}, f32[2,32,1280]{2,1,0:T(8,128)S(1)}, u32[]{:S(2)}, u32[]{:S(2)}) collective-permute-start(f32[2,32,1280]{2,1,0:T(8,128)S(1)} %maximum_select_fusion.6), channel_id=1, source_target_pairs={{0,4},{2,6},{4,0},{6,2},{8,12},{10,14},{12,8},{14,10},{16,20},{18,... | collective-permute-start | bytes 983048 | tf_op jit(solution)/shard_map/ppermute | solution.py:388
  320.5 2.9 collective-permute-start.34
  (8 other events, 8.9 us)

commit v4 on v3

--- a/solution.py
+++ b/solution.py
@@ -166,24 +166,20 @@
     )(jnp.stack([level, jnp.asarray(block, jnp.int32)]), spec)
 
 
-def piece_kernel(start_ref, from_ref, *refs):
-    out_ref, sem = refs[-2:]
-    start = pl.multiple_of(start_ref[0], SUB)
-    copy = pltpu.make_async_copy(from_ref.at[:, pl.ds(start, out_ref.shape[1])], out_ref, sem)
-    copy.start()
-    copy.wait()
-
-
-def piece_of(outgoing, start, rows, waits):
+def gate_kernel(*refs):
+    pass
+
+
+def gated(part, waits):
     return pl.pallas_call(
-        piece_kernel,
-        in_specs=[pl.BlockSpec(memory_space=pltpu.SMEM)] + [pl.BlockSpec(memory_space=pl.ANY)] * (1 + len(waits)),
+        gate_kernel,
+        in_specs=[pl.BlockSpec(memory_space=pl.ANY)] * (1 + len(waits)),
         out_specs=pl.BlockSpec(memory_space=pl.ANY),
-        out_shape=jax.ShapeDtypeStruct((2, rows, outgoing.shape[2]), jnp.float32),
-        scratch_shapes=[pltpu.SemaphoreType.DMA],
-        cost_estimate=pl.CostEstimate(flops=0, transcendentals=0, bytes_accessed=16 * rows * outgoing.shape[2]),
-        name="piece_of",
-    )(start.astype(jnp.int32).reshape(1), outgoing, *waits)
+        out_shape=jax.ShapeDtypeStruct(part.shape, part.dtype),
+        input_output_aliases={0: 0},
+        cost_estimate=pl.CostEstimate(flops=0, transcendentals=0, bytes_accessed=1024),
+        name="gated",
+    )(part, *waits)
 
 
 def east_of(x):
@@ -359,13 +355,15 @@
 
     lead = windows[0].rows
     outgoing = rows_first(spec, 1 - band, choose(1 - band, (nlat // LANE - 2, 0)), 2 * LANE)
-    piece = piece_of(outgoing, choose(1 - band, (2 * LANE - lead, 0)), lead, [])
+    piece = lax.dynamic_slice_in_dim(outgoing, choose(1 - band, (2 * LANE - lead, 0)), lead, axis=1)
     remotes = [lax.ppermute(piece, "band", swap)]
     outgoing = rows_first(spec, 1 - band, 0, nlat)
+    outgoing = [
+        lax.dynamic_slice_in_dim(outgoing, choose(1 - band, window.row_at), window.rows, axis=1) for window in windows
+    ]
 
     def fetch_rows(k, waits):
-        window = windows[k]
-        piece = piece_of(outgoing, choose(1 - band, window.row_at), window.rows, waits)
+        piece = gated(outgoing[k], waits) if waits else outgoing[k]
         remotes.append(lax.ppermute(piece, "band", swap))
         return piece
 

time: 327 us -> 228 us (0.70)
  Pallas kernels: 171 us -> 64.3 us
  local copies, waits for them, and re-layouts: 19.5 us -> 28.3 us
    pallas_call x5 -> x3, Pallas kernels: 105 us -> 0.01 us  [gated(): pl.pallas_call(gate_kernel, in_specs=[pl.BlockSpec(memory_space=pl.ANY)]...]
    unnamed x42 -> x46, local copies, waits for them, and re-layouts: 18.5 us -> 24.1 us
  transfers between devices with their start and end apart: 35 -> 35, of which waited for: 15 -> 16; matrix products, arithmetic and copies ran while one was open for 3% -> 4% of each run, Pallas kernels for 45% -> 27%
where the time goes in v4:
time: 228 us; the launch traced here: 227 us
  waiting for transfers between devices  95.4 us (42%)
  Pallas kernels  64.3 us (28%)
  starting transfers between devices  30.5 us (13%)
  local copies, waits for them, and re-layouts  28.3 us (12%)
  other arithmetic  7.59 us (3%)
    ppermute x15, waiting for transfers between devices, halved(): lax.ppermute(leaves, 'mem', pairs(members, bit))  54.8 us
    pallas_call x5, Pallas kernels, window_tensor(): pl.pallas_call(functools.partial(window_kernel, window, depth, len(waits)...  48.2 us
    ppermute x8, waiting for transfers between devices, doubled(): beside = lax.ppermute(part, 'mem', pairs(members, bit))  25.2 us
    unnamed x46, local copies, waits for them, and re-layouts  24.1 us
    ppermute x15, starting transfers between devices, halved(): lax.ppermute(leaves, 'mem', pairs(members, bit))  17.4 us
    pallas_call x3, Pallas kernels, rows_first(): pl.pallas_call(transpose_kernel, grid_spec=pltpu.PrefetchScalarGridSpec(n...  16.2 us
    ppermute x4, waiting for transfers between devices, fetch_rows(): remotes.append(lax.ppermute(piece, 'band', swap))  15 us
    add x15, other arithmetic, total(): sum((lax.dynamic_slice_in_dim(part, which * half, half, axis=1) for part...  5.65 us
  transfers between devices with their start and end apart: 35, of which 16 were waited for; matrix products, arithmetic and copies ran while one was open for 4% of the time, Pallas kernels for 27%

profile of v4, /device:TPU:0, one launch (start us, length us, event | category | flops | bytes accessed | tf_op | source)
XLA Modules:
  0.0 226.7 jit_solution(5209264078858984060)
XLA Ops:
  0.1 3.1 %rows_first.4 = f32[2,256,640]{2,1,0:T(8,128)S(1)} custom-call(s32[2]{0:T(128)S(1)} %pad_add_fusion.3.place, f32[2,2,640,640]{3,2,1,0:T(8,128)} %bitcast.24), custom_call_target="tpu_custom_call" | custom-call | bytes 10485760 | tf_op jit(solution)/shard_map/rows_first/pallas_call | solution.py:152
  4.1 2.9 %collective-permute-start = (f32[2,136,640]{2,1,0:T(8,128)}, f32[2,136,640]{2,1,0:T(8,128)}, u32[]{:S(2)}, u32[]{:S(2)}) collective-permute-start(f32[2,136,640]{2,1,0:T(8,128)} %constant_dynamic-slice_fusion.4), channel_id=1, source_target_pairs={{0,1},{1,0},{2,3},{3,2},{4,5},{5,4},{6,7},{7,6},{8,9},{9,8},{10,11... | collective-permute-start | bytes 2088968 | tf_op jit(solution)/shard_map/ppermute | solution.py:359
  7.1 6.6 %rows_first.5 = f32[2,640,640]{2,1,0:T(8,128)S(1)} custom-call(s32[2]{0:T(128)S(1)} %pad_add_fusion.place, f32[2,2,640,640]{3,2,1,0:T(8,128)} %bitcast.25), custom_call_target="tpu_custom_call" | custom-call | bytes 26214400 | tf_op jit(solution)/shard_map/rows_first/pallas_call | solution.py:152
  13.7 1.4 constant_dynamic-slice_fusion.1
  15.1 6.6 %rows_first.3.refs_1_ = f32[2,640,640]{2,1,0:T(8,128)S(1)} custom-call(s32[2]{0:T(128)S(1)} %get-tuple-element.64.place, f32[2,2,640,640]{3,2,1,0:T(8,128)} %bitcast.26), custom_call_target="tpu_custom_call" | custom-call | bytes 26214400 | tf_op jit(solution)/shard_map/rows_first/pallas_call | solution.py:152
  21.7 1.7 copy-done
  23.8 1.9 copy-done.1
  25.7 1.9 copy-done.14
  27.6 1.9 copy-done.17
  29.6 10.7 %window_tensor.5 = (f32[3,64,1280]{2,1,0:T(8,128)S(1)}, f32[3,64,1280]{2,1,0:T(8,128)}, f32[2,16,1280]{2,1,0:T(8,128)S(1)}) custom-call(s32[2]{0:T(128)S(1)} %get-tuple-element.65.refs_0_, f32[2,640,640]{2,1,0:T(8,128)S(1)} %copy-done.1, f32[2,136,640]{2,1,0:T(8,128)} %collective-permute-done.refs_1_.refs_2_, bf16[1280,1280]{1,0:T(8,128)(2,1)S(1)} %copy-done.17, ...), custom_call_target="tpu_custom_call" | custom-call | flops 13369344000 | bytes 9912320 | tf_op jit(solution)/shard_map/window_tensor/pallas_call | solution.py:313
  42.8 1.9 copy-done.2
  45.8 1.9 copy-done.15
  47.7 1.9 copy-done.18
  49.6 10.4 %window_tensor.6 = (f32[3,64,1280]{2,1,0:T(8,128)S(1)}, f32[3,64,1280]{2,1,0:T(8,128)}, f32[2,16,1280]{2,1,0:T(8,128)S(1)}) custom-call(s32[2]{0:T(128)S(1)} %get-tuple-element.65.refs_0_, f32[2,640,640]{2,1,0:T(8,128)S(1)} %copy-done.2, f32[2,128,640]{2,1,0:T(8,128)} %collective-permute-done.5.refs_1_.refs_2_, bf16[1280,1280]{1,0:T(8,128)(2,1)S(1)} %copy-done.18, ...), custom_call_target="tpu_custom_call" | custom-call | flops 12582912000 | bytes 9830400 | tf_op jit(solution)/shard_map/window_tensor/pallas_call | solution.py:313
  61.7 2.1 collective-permute-start.11
  64.6 15.0 %collective-permute-done.11.refs_1_.refs_2_ = f32[2,128,640]{2,1,0:T(8,128)} collective-permute-done((f32[2,128,640]{2,1,0:T(8,128)}, f32[2,128,640]{2,1,0:T(8,128)}, u32[]{:S(2)}, u32[]{:S(2)}) %collective-permute-start.11) | collective-permute-done | bytes 655392 | tf_op jit(solution)/shard_map/ppermute | solution.py:367
  79.6 1.9 collective-permute-start.26
  81.6 1.5 dynamic-slice_add_fusion.9
  83.1 1.6 collective-permute-start.2
  86.6 1.9 copy-done.16
  88.6 1.9 copy-done.19
  90.5 9.4 %window_tensor.7 = (f32[3,64,1280]{2,1,0:T(8,128)S(1)}, f32[3,64,1280]{2,1,0:T(8,128)S(1)}, f32[2,16,1280]{2,1,0:T(8,128)S(1)}) custom-call(s32[2]{0:T(128)S(1)} %get-tuple-element.65.refs_0_, f32[2,640,640]{2,1,0:T(8,128)S(1)} %copy-done.3, f32[2,128,640]{2,1,0:T(8,128)} %collective-permute-done.11.refs_1_.refs_2_, bf16[1280,1280]{1,0:T(8,128)(2,1)S(1)} %copy-done.19, ...), custom_call_target="tpu_custom_call" | custom-call | flops 12582912000 | bytes 9830400 | tf_op jit(solution)/shard_map/window_tensor/pallas_call | solution.py:313
  100.1 1.6 collective-permute-start.3
  101.7 4.2 %collective-permute-done.7 = f32[3,32,1280]{2,1,0:T(8,128)S(1)} collective-permute-done((f32[3,32,1280]{2,1,0:T(8,128)S(1)}, f32[3,32,1280]{2,1,0:T(8,128)S(1)}, u32[]{:S(2)}, u32[]{:S(2)}) %collective-permute-start.7) | collective-permute-done | bytes 491552 | tf_op jit(solution)/shard_map/ppermute | solution.py:383
  106.0 1.6 collective-permute-start.8
  107.6 9.0 %window_tensor.8 = (f32[3,64,1280]{2,1,0:T(8,128)S(1)}, f32[3,64,1280]{2,1,0:T(8,128)S(1)}, f32[2,16,1280]{2,1,0:T(8,128)S(1)}) custom-call(s32[2]{0:T(128)S(1)} %get-tuple-element.65.refs_0_, f32[2,640,640]{2,1,0:T(8,128)S(1)} %copy-done.3, f32[2,128,640]{2,1,0:T(8,128)S(1)} %collective-permute-done.21.refs_2_, bf16[1280,1280]{1,0:T(8,128)(2,1)S(1)} %copy-done.19, ...), custom_call_target="tpu_custom_call" | custom-call | flops 12582912000 | bytes 9830400 | tf_op jit(solution)/shard_map/window_tensor/pallas_call | solution.py:313
  116.8 2.6 %collective-permute-start.4 = (f32[3,8,1280]{2,1,0:T(8,128)S(1)}, f32[3,8,1280]{2,1,0:T(8,128)S(1)}, u32[]{:S(2)}, u32[]{:S(2)}) collective-permute-start(f32[3,8,1280]{2,1,0:T(8,128)S(1)} %dynamic-slice_add_fusion.24.refs_5_), channel_id=1, source_target_pairs={{0,16},{2,18},{4,20},{6,22},{8,24},{10,26},{12,28},{14,30},{16,0},... | collective-permute-start | bytes 368648 | tf_op jit(solution)/shard_map/ppermute | solution.py:383
  119.9 8.8 %collective-permute-done.4 = f32[3,8,1280]{2,1,0:T(8,128)S(1)} collective-permute-done((f32[3,8,1280]{2,1,0:T(8,128)S(1)}, f32[3,8,1280]{2,1,0:T(8,128)S(1)}, u32[]{:S(2)}, u32[]{:S(2)}) %collective-permute-start.4) | collective-permute-done | bytes 122912 | tf_op jit(solution)/shard_map/ppermute | solution.py:383
  128.7 2.5 %collective-permute-done.9 = f32[3,8,1280]{2,1,0:T(8,128)S(1)} collective-permute-done((f32[3,8,1280]{2,1,0:T(8,128)S(1)}, f32[3,8,1280]{2,1,0:T(8,128)S(1)}, u32[]{:S(2)}, u32[]{:S(2)}) %collective-permute-start.9) | collective-permute-done | bytes 122912 | tf_op jit(solution)/shard_map/ppermute | solution.py:383
  131.4 1.6 collective-permute-start.13
  133.7 11.0 %collective-permute-done.13 = f32[3,32,1280]{2,1,0:T(8,128)S(1)} collective-permute-done((f32[3,32,1280]{2,1,0:T(8,128)S(1)}, f32[3,32,1280]{2,1,0:T(8,128)S(1)}, u32[]{:S(2)}, u32[]{:S(2)}) %collective-permute-start.13) | collective-permute-done | bytes 491552 | tf_op jit(solution)/shard_map/ppermute | solution.py:383
  144.8 8.6 %window_tensor.9 = (f32[3,64,1280]{2,1,0:T(8,128)S(1)}, f32[3,64,1280]{2,1,0:T(8,128)S(1)}) custom-call(s32[2]{0:T(128)S(1)} %get-tuple-element.65.refs_0_, f32[2,640,640]{2,1,0:T(8,128)S(1)} %copy-done.3, f32[2,120,640]{2,1,0:T(8,128)S(1)} %collective-permute-done.26.refs_2_, bf16[1280,1280]{1,0:T(8,128)(2,1)S(1)} %copy-done.19, ...), custom_call_target="tpu_custom_call" | custom-call | flops 11796480000 | bytes 9748480 | tf_op jit(solution)/shard_map/window_tensor/pallas_call | solution.py:313
  153.6 2.8 %collective-permute-start.15 = (f32[3,8,1280]{2,1,0:T(8,128)S(1)}, f32[3,8,1280]{2,1,0:T(8,128)S(1)}, u32[]{:S(2)}, u32[]{:S(2)}) collective-permute-start(f32[3,8,1280]{2,1,0:T(8,128)S(1)} %dynamic-slice_add_fusion.22), channel_id=1, source_target_pairs={{0,16},{2,18},{4,20},{6,22},{8,24},{10,26},{12,28},{14,30},{16,0},... | collective-permute-start | bytes 368648 | tf_op jit(solution)/shard_map/ppermute | solution.py:383
  157.3 1.5 collective-permute-start.23
  158.8 4.2 %collective-permute-done.15 = f32[3,8,1280]{2,1,0:T(8,128)S(1)} collective-permute-done((f32[3,8,1280]{2,1,0:T(8,128)S(1)}, f32[3,8,1280]{2,1,0:T(8,128)S(1)}, u32[]{:S(2)}, u32[]{:S(2)}) %collective-permute-start.15) | collective-permute-done | bytes 122912 | tf_op jit(solution)/shard_map/ppermute | solution.py:383
  164.0 6.9 %collective-permute-done.23 = f32[3,32,1280]{2,1,0:T(8,128)S(1)} collective-permute-done((f32[3,32,1280]{2,1,0:T(8,128)}, f32[3,32,1280]{2,1,0:T(8,128)S(1)}, u32[]{:S(2)}, u32[]{:S(2)}) %collective-permute-start.23) | collective-permute-done | bytes 491552 | tf_op jit(solution)/shard_map/ppermute | solution.py:383
  171.0 1.4 dynamic-slice_add_fusion.1
  172.4 1.6 collective-permute-start.28
  174.0 2.1 collective-permute-start.18
  176.1 3.8 %collective-permute-done.24 = f32[3,16,1280]{2,1,0:T(8,128)S(1)} collective-permute-done((f32[3,16,1280]{2,1,0:T(8,128)S(1)}, f32[3,16,1280]{2,1,0:T(8,128)S(1)}, u32[]{:S(2)}, u32[]{:S(2)}) %collective-permute-start.24) | collective-permute-done | bytes 245792 | tf_op jit(solution)/shard_map/ppermute | solution.py:383
  180.2 6.0 %collective-permute-done.18 = f32[3,16,1280]{2,1,0:T(8,128)S(1)} collective-permute-done((f32[3,16,1280]{2,1,0:T(8,128)S(1)}, f32[3,16,1280]{2,1,0:T(8,128)S(1)}, u32[]{:S(2)}, u32[]{:S(2)}) %collective-permute-start.18) | collective-permute-done | bytes 245792 | tf_op jit(solution)/shard_map/ppermute | solution.py:386
  186.2 1.6 collective-permute-start.19
  188.0 7.1 %collective-permute-done.29 = f32[3,16,1280]{2,1,0:T(8,128)S(1)} collective-permute-done((f32[3,16,1280]{2,1,0:T(8,128)S(1)}, f32[3,16,1280]{2,1,0:T(8,128)S(1)}, u32[]{:S(2)}, u32[]{:S(2)}) %collective-permute-start.29) | collective-permute-done | bytes 245792 | tf_op jit(solution)/shard_map/ppermute | solution.py:383
  196.0 6.3 %collective-permute-done.30 = f32[3,8,1280]{2,1,0:T(8,128)S(1)} collective-permute-done((f32[3,8,1280]{2,1,0:T(8,128)S(1)}, f32[3,8,1280]{2,1,0:T(8,128)S(1)}, u32[]{:S(2)}, u32[]{:S(2)}) %collective-permute-start.30) | collective-permute-done | bytes 122912 | tf_op jit(solution)/shard_map/ppermute | solution.py:383
  202.6 5.5 %collective-permute-done.31 = f32[2,8,1280]{2,1,0:T(8,128)S(1)} collective-permute-done((f32[2,8,1280]{2,1,0:T(8,128)S(1)}, f32[2,8,1280]{2,1,0:T(8,128)S(1)}, u32[]{:S(2)}, u32[]{:S(2)}) %collective-permute-start.31) | collective-permute-done | bytes 81952 | tf_op jit(solution)/shard_map/ppermute | solution.py:386
  208.2 5.4 %collective-permute-done.32 = f32[2,16,1280]{2,1,0:T(8,128)S(1)} collective-permute-done((f32[2,16,1280]{2,1,0:T(8,128)S(1)}, f32[2,16,1280]{2,1,0:T(8,128)S(1)}, u32[]{:S(2)}, u32[]{:S(2)}) %collective-permute-start.32) | collective-permute-done | bytes 163872 | tf_op jit(solution)/shard_map/ppermute | solution.py:386
  214.2 7.5 %collective-permute-done.33 = f32[2,32,1280]{2,1,0:T(8,128)S(1)} collective-permute-done((f32[2,32,1280]{2,1,0:T(8,128)S(1)}, f32[2,32,1280]{2,1,0:T(8,128)S(1)}, u32[]{:S(2)}, u32[]{:S(2)}) %collective-permute-start.33) | collective-permute-done | bytes 327712 | tf_op jit(solution)/shard_map/ppermute | solution.py:386
  224.1 1.7 copy-done.20
  (127 shorter events, 19.0 us)
Async XLA Ops:
  4.1 19.7 %collective-permute-start = (f32[2,136,640]{2,1,0:T(8,128)}, f32[2,136,640]{2,1,0:T(8,128)}, u32[]{:S(2)}, u32[]{:S(2)}) collective-permute-start(f32[2,136,640]{2,1,0:T(8,128)} %constant_dynamic-slice_fusion.4), channel_id=1, source_target_pairs={{0,1},{1,0},{2,3},{3,2},{4,5},{5,4},{6,7},{7,6},{8,9},{9,8},{10,11... | collective-permute-start | bytes 2088968 | tf_op jit(solution)/shard_map/ppermute | solution.py:359
  15.0 26.8 %collective-permute-start.5 = (f32[2,128,640]{2,1,0:T(8,128)}, f32[2,128,640]{2,1,0:T(8,128)}, u32[]{:S(2)}, u32[]{:S(2)}) collective-permute-start(f32[2,128,640]{2,1,0:T(8,128)} %get-tuple-element.34), channel_id=1, source_target_pairs={{0,1},{1,0},{2,3},{3,2},{4,5},{5,4},{6,7},{7,6},{8,9},{9,8},{10,11... | collective-permute-start | bytes 1966088 | tf_op jit(solution)/shard_map/ppermute | solution.py:367
  23.8 1.9 copy-start.1
  25.7 1.9 copy-start.14
  27.6 1.9 copy-start.17
  41.9 39.7 %collective-permute-start.1 = (f32[3,64,1280]{2,1,0:T(8,128)}, f32[3,64,1280]{2,1,0:T(8,128)}, u32[]{:S(2)}, u32[]{:S(2)}) collective-permute-start(f32[3,64,1280]{2,1,0:T(8,128)} %get-tuple-element.20), channel_id=1, source_target_pairs={{0,2},{2,0},{4,6},{6,4},{8,10},{10,8},{12,14},{14,12},{16,18},{18,... | collective-permute-start | bytes 2949128 | tf_op jit(solution)/shard_map/ppermute | solution.py:405
  42.8 1.9 copy-start.2
  45.8 1.9 copy-start.15
  61.7 23.1 %collective-permute-start.6 = (f32[3,64,1280]{2,1,0:T(8,128)}, f32[3,64,1280]{2,1,0:T(8,128)}, u32[]{:S(2)}, u32[]{:S(2)}) collective-permute-start(f32[3,64,1280]{2,1,0:T(8,128)} %get-tuple-element.23), channel_id=1, source_target_pairs={{0,2},{2,0},{4,6},{6,4},{8,10},{10,8},{12,14},{14,12},{16,18},{18,... | collective-permute-start | bytes 2949128 | tf_op jit(solution)/shard_map/ppermute | solution.py:405
  61.7 18.0 %collective-permute-start.11 = (f32[2,128,640]{2,1,0:T(8,128)}, f32[2,128,640]{2,1,0:T(8,128)}, u32[]{:S(2)}, u32[]{:S(2)}) collective-permute-start(f32[2,128,640]{2,1,0:T(8,128)} %gated.3.refs_5_), channel_id=1, source_target_pairs={{0,1},{1,0},{2,3},{3,2},{4,5},{5,4},{6,7},{7,6},{8,9},{9,8},{10,11... | collective-permute-start | bytes 1966088 | tf_op jit(solution)/shard_map/ppermute | solution.py:367
  64.6 17.0 %copy-start.7 = (f32[3,64,1280]{2,1,0:T(8,128)S(1)}, f32[3,64,1280]{2,1,0:T(8,128)}, u32[]{:S(2)}) copy-start(f32[3,64,1280]{2,1,0:T(8,128)} %copy-done.6) | copy-start | bytes 2949124
  64.6 43.0 %collective-permute-start.21 = (f32[2,128,640]{2,1,0:T(8,128)}, f32[2,128,640]{2,1,0:T(8,128)S(1)}, u32[]{:S(2)}, u32[]{:S(2)}) collective-permute-start(f32[2,128,640]{2,1,0:T(8,128)} %gated.4.refs_5_), channel_id=1, source_target_pairs={{0,1},{1,0},{2,3},{3,2},{4,5},{5,4},{6,7},{7,6},{8,9},{9,8},{10,11... | collective-permute-start | bytes 1966088 | tf_op jit(solution)/shard_map/ppermute | solution.py:367
  79.6 5.1 %copy-start.9 = (f32[3,64,1280]{2,1,0:T(8,128)S(1)}, f32[3,64,1280]{2,1,0:T(8,128)}, u32[]{:S(2)}) copy-start(f32[3,64,1280]{2,1,0:T(8,128)} %copy-done.8) | copy-start | bytes 2949124
  79.6 65.2 %collective-permute-start.26 = (f32[2,120,640]{2,1,0:T(8,128)}, f32[2,120,640]{2,1,0:T(8,128)S(1)}, u32[]{:S(2)}, u32[]{:S(2)}) collective-permute-start(f32[2,120,640]{2,1,0:T(8,128)} %gated.5.refs_5_), channel_id=1, source_target_pairs={{0,1},{1,0},{2,3},{3,2},{4,5},{5,4},{6,7},{7,6},{8,9},{9,8},{10,11... | collective-permute-start | bytes 1843208 | tf_op jit(solution)/shard_map/ppermute | solution.py:367
  81.6 5.0 %copy-start.3 = (f32[2,640,640]{2,1,0:T(8,128)S(1)}, f32[2,640,640]{2,1,0:T(8,128)}, u32[]{:S(2)}) copy-start(f32[2,640,640]{2,1,0:T(8,128)} %copy-done) | copy-start | bytes 9830404
  83.1 3.5 %copy-start.5 = (f32[2,120,640]{2,1,0:T(8,128)S(1)}, f32[2,120,640]{2,1,0:T(8,128)}, u32[]{:S(2)}) copy-start(f32[2,120,640]{2,1,0:T(8,128)} %gated.5.refs_5_) | copy-start | bytes 1843204
  83.1 3.5 %copy-start.13 = (f32[2,16,1280]{2,1,0:T(8,128)S(1)}, f32[2,16,1280]{2,1,0:T(8,128)}, u32[]{:S(2)}) copy-start(f32[2,16,1280]{2,1,0:T(8,128)} %copy-done.12) | copy-start | bytes 491524
  83.1 16.9 %collective-permute-start.2 = (f32[3,32,1280]{2,1,0:T(8,128)S(1)}, f32[3,32,1280]{2,1,0:T(8,128)S(1)}, u32[]{:S(2)}, u32[]{:S(2)}) collective-permute-start(f32[3,32,1280]{2,1,0:T(8,128)S(1)} %get-tuple-element.45.refs_6_), channel_id=1, source_target_pairs={{0,4},{2,6},{4,0},{6,2},{8,12},{10,14},{12,8},{14,10},{16,20},{18,... | collective-permute-start | bytes 1474568 | tf_op jit(solution)/shard_map/ppermute | solution.py:383
  86.0 19.9 %collective-permute-start.7 = (f32[3,32,1280]{2,1,0:T(8,128)S(1)}, f32[3,32,1280]{2,1,0:T(8,128)S(1)}, u32[]{:S(2)}, u32[]{:S(2)}) collective-permute-start(f32[3,32,1280]{2,1,0:T(8,128)S(1)} %get-tuple-element.47.refs_6_), channel_id=1, source_target_pairs={{0,4},{2,6},{4,0},{6,2},{8,12},{10,14},{12,8},{14,10},{16,20},{18,... | collective-permute-start | bytes 1474568 | tf_op jit(solution)/shard_map/ppermute | solution.py:383
  86.6 1.9 copy-start.16
  99.9 31.4 %collective-permute-start.12 = (f32[3,64,1280]{2,1,0:T(8,128)S(1)}, f32[3,64,1280]{2,1,0:T(8,128)S(1)}, u32[]{:S(2)}, u32[]{:S(2)}) collective-permute-start(f32[3,64,1280]{2,1,0:T(8,128)S(1)} %get-tuple-element.26), channel_id=1, source_target_pairs={{0,2},{2,0},{4,6},{6,4},{8,10},{10,8},{12,14},{14,12},{16,18},{18,... | collective-permute-start | bytes 2949128 | tf_op jit(solution)/shard_map/ppermute | solution.py:405
  100.1 16.7 %collective-permute-start.3 = (f32[3,16,1280]{2,1,0:T(8,128)S(1)}, f32[3,16,1280]{2,1,0:T(8,128)S(1)}, u32[]{:S(2)}, u32[]{:S(2)}) collective-permute-start(f32[3,16,1280]{2,1,0:T(8,128)S(1)} %get-tuple-element.57.refs_5_), channel_id=1, source_target_pairs={{0,8},{2,10},{4,12},{6,14},{8,0},{10,2},{12,4},{14,6},{16,24},{18,... | collective-permute-start | bytes 737288 | tf_op jit(solution)/shard_map/ppermute | solution.py:383
  106.0 13.5 %collective-permute-start.8 = (f32[3,16,1280]{2,1,0:T(8,128)S(1)}, f32[3,16,1280]{2,1,0:T(8,128)S(1)}, u32[]{:S(2)}, u32[]{:S(2)}) collective-permute-start(f32[3,16,1280]{2,1,0:T(8,128)S(1)} %get-tuple-element.59.refs_6_), channel_id=1, source_target_pairs={{0,8},{2,10},{4,12},{6,14},{8,0},{10,2},{12,4},{14,6},{16,24},{18,... | collective-permute-start | bytes 737288 | tf_op jit(solution)/shard_map/ppermute | solution.py:383
  116.7 39.8 %collective-permute-start.22 = (f32[3,64,1280]{2,1,0:T(8,128)S(1)}, f32[3,64,1280]{2,1,0:T(8,128)S(1)}, u32[]{:S(2)}, u32[]{:S(2)}) collective-permute-start(f32[3,64,1280]{2,1,0:T(8,128)S(1)} %get-tuple-element.29), channel_id=1, source_target_pairs={{0,2},{2,0},{4,6},{6,4},{8,10},{10,8},{12,14},{14,12},{16,18},{18,... | collective-permute-start | bytes 2949128 | tf_op jit(solution)/shard_map/ppermute | solution.py:405
  116.8 11.9 %collective-permute-start.4 = (f32[3,8,1280]{2,1,0:T(8,128)S(1)}, f32[3,8,1280]{2,1,0:T(8,128)S(1)}, u32[]{:S(2)}, u32[]{:S(2)}) collective-permute-start(f32[3,8,1280]{2,1,0:T(8,128)S(1)} %dynamic-slice_add_fusion.24.refs_5_), channel_id=1, source_target_pairs={{0,16},{2,18},{4,20},{6,22},{8,24},{10,26},{12,28},{14,30},{16,0},... | collective-permute-start | bytes 368648 | tf_op jit(solution)/shard_map/ppermute | solution.py:383
  119.5 11.8 %collective-permute-start.9 = (f32[3,8,1280]{2,1,0:T(8,128)S(1)}, f32[3,8,1280]{2,1,0:T(8,128)S(1)}, u32[]{:S(2)}, u32[]{:S(2)}) collective-permute-start(f32[3,8,1280]{2,1,0:T(8,128)S(1)} %dynamic-slice_add_fusion.23), channel_id=1, source_target_pairs={{0,16},{2,18},{4,20},{6,22},{8,24},{10,26},{12,28},{14,30},{16,0},... | collective-permute-start | bytes 368648 | tf_op jit(solution)/shard_map/ppermute | solution.py:383
  131.4 13.3 %collective-permute-start.13 = (f32[3,32,1280]{2,1,0:T(8,128)S(1)}, f32[3,32,1280]{2,1,0:T(8,128)S(1)}, u32[]{:S(2)}, u32[]{:S(2)}) collective-permute-start(f32[3,32,1280]{2,1,0:T(8,128)S(1)} %get-tuple-element.49.refs_7_), channel_id=1, source_target_pairs={{0,4},{2,6},{4,0},{6,2},{8,12},{10,14},{12,8},{14,10},{16,20},{18,... | collective-permute-start | bytes 1474568 | tf_op jit(solution)/shard_map/ppermute | solution.py:383
  133.1 30.7 %collective-permute-start.10 = (f32[2,8,1280]{2,1,0:T(8,128)S(1)}, f32[2,8,1280]{2,1,0:T(8,128)S(1)}, u32[]{:S(2)}, u32[]{:S(2)}) collective-permute-start(f32[2,8,1280]{2,1,0:T(8,128)S(1)} %pad_maximum_fusion.1), channel_id=1, source_target_pairs={{0,1},{1,0},{2,3},{3,2},{4,5},{5,4},{6,7},{7,6},{8,9},{9,8},{10,11... | collective-permute-start | bytes 245768 | tf_op jit(solution)/shard_map/ppermute | solution.py:412
  144.7 8.8 %collective-permute-start.14 = (f32[3,16,1280]{2,1,0:T(8,128)S(1)}, f32[3,16,1280]{2,1,0:T(8,128)S(1)}, u32[]{:S(2)}, u32[]{:S(2)}) collective-permute-start(f32[3,16,1280]{2,1,0:T(8,128)S(1)} %get-tuple-element.61), channel_id=1, source_target_pairs={{0,8},{2,10},{4,12},{6,14},{8,0},{10,2},{12,4},{14,6},{16,24},{18,... | collective-permute-start | bytes 737288 | tf_op jit(solution)/shard_map/ppermute | solution.py:383
  153.5 17.5 %collective-permute-start.27 = (f32[3,64,1280]{2,1,0:T(8,128)S(1)}, f32[3,64,1280]{2,1,0:T(8,128)}, u32[]{:S(2)}, u32[]{:S(2)}) collective-permute-start(f32[3,64,1280]{2,1,0:T(8,128)S(1)} %get-tuple-element.32), channel_id=1, source_target_pairs={{0,2},{2,0},{4,6},{6,4},{8,10},{10,8},{12,14},{14,12},{16,18},{18,... | collective-permute-start | bytes 2949128 | tf_op jit(solution)/shard_map/ppermute | solution.py:405
  153.6 9.4 %collective-permute-start.15 = (f32[3,8,1280]{2,1,0:T(8,128)S(1)}, f32[3,8,1280]{2,1,0:T(8,128)S(1)}, u32[]{:S(2)}, u32[]{:S(2)}) collective-permute-start(f32[3,8,1280]{2,1,0:T(8,128)S(1)} %dynamic-slice_add_fusion.22), channel_id=1, source_target_pairs={{0,16},{2,18},{4,20},{6,22},{8,24},{10,26},{12,28},{14,30},{16,0},... | collective-permute-start | bytes 368648 | tf_op jit(solution)/shard_map/ppermute | solution.py:383
  157.3 13.5 %collective-permute-start.23 = (f32[3,32,1280]{2,1,0:T(8,128)}, f32[3,32,1280]{2,1,0:T(8,128)S(1)}, u32[]{:S(2)}, u32[]{:S(2)}) collective-permute-start(f32[3,32,1280]{2,1,0:T(8,128)} %get-tuple-element.37), channel_id=1, source_target_pairs={{0,4},{2,6},{4,0},{6,2},{8,12},{10,14},{12,8},{14,10},{16,20},{18,... | collective-permute-start | bytes 1474568 | tf_op jit(solution)/shard_map/ppermute | solution.py:383
  163.1 0.7 collective-permute-start.16
  163.8 7.1 %copy-start.21 = (f32[8,1280]{1,0:T(8,128)}, f32[8,1280]{1,0:T(8,128)S(1)}, u32[]{:S(2)}) copy-start(f32[8,1280]{1,0:T(8,128)S(1)} %collective-permute-done.16) | copy-start | bytes 122884
  163.8 10.2 %collective-permute-start.17 = (f32[3,8,1280]{2,1,0:T(8,128)S(1)}, f32[3,8,1280]{2,1,0:T(8,128)S(1)}, u32[]{:S(2)}, u32[]{:S(2)}) collective-permute-start(f32[3,8,1280]{2,1,0:T(8,128)S(1)} %pad_maximum_fusion), channel_id=1, source_target_pairs={{0,16},{2,18},{4,20},{6,22},{8,24},{10,26},{12,28},{14,30},{16,0},... | collective-permute-start | bytes 368648 | tf_op jit(solution)/shard_map/ppermute | solution.py:386
  170.9 3.1 %copy-start.22 = (f32[8,1280]{1,0:T(8,128)S(1)}, f32[8,1280]{1,0:T(8,128)}, u32[]{:S(2)}) copy-start(f32[8,1280]{1,0:T(8,128)} %copy-done.21) | copy-start | bytes 122884
  170.9 9.0 %collective-permute-start.24 = (f32[3,16,1280]{2,1,0:T(8,128)S(1)}, f32[3,16,1280]{2,1,0:T(8,128)S(1)}, u32[]{:S(2)}, u32[]{:S(2)}) collective-permute-start(f32[3,16,1280]{2,1,0:T(8,128)S(1)} %get-tuple-element.53), channel_id=1, source_target_pairs={{0,8},{2,10},{4,12},{6,14},{8,0},{10,2},{12,4},{14,6},{16,24},{18,... | collective-permute-start | bytes 737288 | tf_op jit(solution)/shard_map/ppermute | solution.py:383
  172.4 15.4 %collective-permute-start.28 = (f32[3,32,1280]{2,1,0:T(8,128)S(1)}, f32[3,32,1280]{2,1,0:T(8,128)S(1)}, u32[]{:S(2)}, u32[]{:S(2)}) collective-permute-start(f32[3,32,1280]{2,1,0:T(8,128)S(1)} %get-tuple-element.39), channel_id=1, source_target_pairs={{0,4},{2,6},{4,0},{6,2},{8,12},{10,14},{12,8},{14,10},{16,20},{18,... | collective-permute-start | bytes 1474568 | tf_op jit(solution)/shard_map/ppermute | solution.py:383
  174.0 12.2 %collective-permute-start.18 = (f32[3,16,1280]{2,1,0:T(8,128)S(1)}, f32[3,16,1280]{2,1,0:T(8,128)S(1)}, u32[]{:S(2)}, u32[]{:S(2)}) collective-permute-start(f32[3,16,1280]{2,1,0:T(8,128)S(1)} %maximum_select_fusion.7), channel_id=1, source_target_pairs={{0,8},{2,10},{4,12},{6,14},{8,0},{10,2},{12,4},{14,6},{16,24},{18,... | collective-permute-start | bytes 737288 | tf_op jit(solution)/shard_map/ppermute | solution.py:386
  179.9 8.1 %collective-permute-start.25 = (f32[3,8,1280]{2,1,0:T(8,128)S(1)}, f32[3,8,1280]{2,1,0:T(8,128)S(1)}, u32[]{:S(2)}, u32[]{:S(2)}) collective-permute-start(f32[3,8,1280]{2,1,0:T(8,128)S(1)} %dynamic-slice_add_fusion.21), channel_id=1, source_target_pairs={{0,16},{2,18},{4,20},{6,22},{8,24},{10,26},{12,28},{14,30},{16,0},... | collective-permute-start | bytes 368648 | tf_op jit(solution)/shard_map/ppermute | solution.py:383
  186.2 16.2 %collective-permute-start.19 = (f32[3,32,1280]{2,1,0:T(8,128)S(1)}, f32[3,32,1280]{2,1,0:T(8,128)S(1)}, u32[]{:S(2)}, u32[]{:S(2)}) collective-permute-start(f32[3,32,1280]{2,1,0:T(8,128)S(1)} %maximum_select_fusion.5), channel_id=1, source_target_pairs={{0,4},{2,6},{4,0},{6,2},{8,12},{10,14},{12,8},{14,10},{16,20},{18,... | collective-permute-start | bytes 1474568 | tf_op jit(solution)/shard_map/ppermute | solution.py:386
  187.9 7.2 %collective-permute-start.29 = (f32[3,16,1280]{2,1,0:T(8,128)S(1)}, f32[3,16,1280]{2,1,0:T(8,128)S(1)}, u32[]{:S(2)}, u32[]{:S(2)}) collective-permute-start(f32[3,16,1280]{2,1,0:T(8,128)S(1)} %get-tuple-element.55), channel_id=1, source_target_pairs={{0,8},{2,10},{4,12},{6,14},{8,0},{10,2},{12,4},{14,6},{16,24},{18,... | collective-permute-start | bytes 737288 | tf_op jit(solution)/shard_map/ppermute | solution.py:383
  195.1 7.2 %collective-permute-start.30 = (f32[3,8,1280]{2,1,0:T(8,128)S(1)}, f32[3,8,1280]{2,1,0:T(8,128)S(1)}, u32[]{:S(2)}, u32[]{:S(2)}) collective-permute-start(f32[3,8,1280]{2,1,0:T(8,128)S(1)} %dynamic-slice_add_fusion.20), channel_id=1, source_target_pairs={{0,16},{2,18},{4,20},{6,22},{8,24},{10,26},{12,28},{14,30},{16,0},... | collective-permute-start | bytes 368648 | tf_op jit(solution)/shard_map/ppermute | solution.py:383
  202.4 5.8 %collective-permute-start.31 = (f32[2,8,1280]{2,1,0:T(8,128)S(1)}, f32[2,8,1280]{2,1,0:T(8,128)S(1)}, u32[]{:S(2)}, u32[]{:S(2)}) collective-permute-start(f32[2,8,1280]{2,1,0:T(8,128)S(1)} %pad_maximum_fusion.2), channel_id=1, source_target_pairs={{0,16},{2,18},{4,20},{6,22},{8,24},{10,26},{12,28},{14,30},{16,0},... | collective-permute-start | bytes 245768 | tf_op jit(solution)/shard_map/ppermute | solution.py:386
  202.5 19.3 %collective-permute-start.20 = (f32[3,64,1280]{2,1,0:T(8,128)S(1)}, f32[3,64,1280]{2,1,0:T(8,128)S(1)}, u32[]{:S(2)}, u32[]{:S(2)}) collective-permute-start(f32[3,64,1280]{2,1,0:T(8,128)S(1)} %maximum_select_fusion.3), channel_id=1, source_target_pairs={{0,2},{2,0},{4,6},{6,4},{8,10},{10,8},{12,14},{14,12},{16,18},{18,... | collective-permute-start | bytes 2949128 | tf_op jit(solution)/shard_map/ppermute | solution.py:386
  208.2 5.5 %collective-permute-start.32 = (f32[2,16,1280]{2,1,0:T(8,128)S(1)}, f32[2,16,1280]{2,1,0:T(8,128)S(1)}, u32[]{:S(2)}, u32[]{:S(2)}) collective-permute-start(f32[2,16,1280]{2,1,0:T(8,128)S(1)} %maximum_select_fusion.8), channel_id=1, source_target_pairs={{0,8},{2,10},{4,12},{6,14},{8,0},{10,2},{12,4},{14,6},{16,24},{18,... | collective-permute-start | bytes 491528 | tf_op jit(solution)/shard_map/ppermute | solution.py:386
  213.7 8.1 %collective-permute-start.33 = (f32[2,32,1280]{2,1,0:T(8,128)S(1)}, f32[2,32,1280]{2,1,0:T(8,128)S(1)}, u32[]{:S(2)}, u32[]{:S(2)}) collective-permute-start(f32[2,32,1280]{2,1,0:T(8,128)S(1)} %maximum_select_fusion.6), channel_id=1, source_target_pairs={{0,4},{2,6},{4,0},{6,2},{8,12},{10,14},{12,8},{14,10},{16,20},{18,... | collective-permute-start | bytes 983048 | tf_op jit(solution)/shard_map/ppermute | solution.py:386
  221.8 2.2 collective-permute-start.34
  (10 other events, 12.5 us)

commit v5 on v4

--- a/solution.py
+++ b/solution.py
@@ -15,6 +15,7 @@
 SUB = 8
 LANE = 128
 VMEM_LIMIT = 24 * 1024 * 1024
+KERNEL_WORK = 8
 
 
 def padded(cells, sides, width):
@@ -106,17 +107,37 @@
     return lax.all_gather(exponent_of(summed, members), "mem", axis=2, tiled=True)
 
 
+def by_parity(waves_local):
+    half = waves_local // 2
+    whole = 2 * LANE - half
+    runs = []
+    for parity in range(2):
+        runs += [(parity, half, 2), (waves_local + parity, whole, 2)]
+    for parity in range(2):
+        runs.append((waves_local + parity + 2 * whole, half - whole, 2))
+    return runs
+
+
 @functools.lru_cache(maxsize=None)
 def wave_table(bands, waves_local):
-    wave = np.arange(bands * waves_local, dtype=np.int64)
-    phase = (wave[:, None] * np.arange(NLON, dtype=np.int64)[None, :]) % NLON
-    angle = phase.astype(np.float64) * (2.0 * np.pi / NLON)
-    weight = np.where(wave == 0, 1.0, 2.0)[:, None]
-    table = np.stack([weight * np.cos(angle), -weight * np.sin(angle)])
-    table = table.reshape(2, bands, waves_local, NLON).transpose(1, 0, 2, 3).reshape(-1, NLON)
-    high = table.astype(ml_dtypes.bfloat16)
-    low = (table - high.astype(np.float64)).astype(ml_dtypes.bfloat16)
-    return high, low
+    order = np.concatenate([start + step * np.arange(count) for start, count, step in by_parity(waves_local)])
+    wave, part = order % waves_local, order // waves_local
+    wave = wave[None, :] + waves_local * np.arange(bands)[:, None]
+    part = np.broadcast_to(part, wave.shape)
+    cut = [0, 2 * LANE, 4 * LANE, 4 * LANE + LANE // 2, 5 * LANE]
+    result = []
+    for parity in range(2):
+        picks = [(band, slice(cut[parity], cut[parity + 1])) for band in range(bands)]
+        picks += [(band, slice(cut[parity + 2], cut[parity + 3])) for band in range(bands)]
+        waves = np.concatenate([wave[pick] for pick in picks])
+        parts = np.concatenate([part[pick] for pick in picks])
+        phase = (waves[:, None] * np.arange(NLON // 2)[None, :]) % NLON
+        angle = phase.astype(np.float64) * (2.0 * np.pi / NLON)
+        weight = np.where(waves == 0, 1.0, 2.0)[:, None]
+        table = weight * np.where(parts[:, None] == 0, np.cos(angle), -np.sin(angle))
+        high = table.astype(ml_dtypes.bfloat16)
+        result += [high, (table - high.astype(np.float64)).astype(ml_dtypes.bfloat16)]
+    return np.stack(result)
 
 
 class Window:
@@ -144,7 +165,8 @@
 
 
 def transpose_kernel(place, spec_ref, out_ref):
-    out_ref[0] = spec_ref[0, 0].T
+    runs = by_parity(spec_ref.shape[2] // 2)
+    out_ref[0] = jnp.concatenate([spec_ref[0, 0, pl.ds(start, count, step), :] for start, count, step in runs]).T
 
 
 def rows_first(spec, level, block, width):
@@ -195,27 +217,39 @@
 
 def window_kernel(window, depth, waits, *refs):
     refs = list(refs)
-    place_ref, local_ref, remote_ref, high_ref, low_ref = refs[:5]
-    refs = refs[5 + waits :]
+    place_ref, local_ref, remote_ref, table_ref = refs[:4]
+    refs = refs[4 + waits :]
     carry_ref = None if window.first else refs.pop(0)
-    keep_ref, send_ref = refs.pop(0), refs.pop(0)
+    out_refs = [refs.pop(0) for _ in range(4)]
     carried_ref = None if window.last else refs.pop(0)
-    local_buf, lhs, lhs_high, lhs_low, wind, second, third, shift, sem = refs
-    band, core = place_ref[0], place_ref[1]
+    table, local_buf, lhs_high, lhs_low, wind, second, third, shift, sems = refs
+    band, core, side = place_ref[0], place_ref[1], place_ref[2]
     rows, extended = window.rows, window.extended
 
     def at(pair):
         return pl.multiple_of(choose(band, pair).astype(jnp.int32), SUB)
 
-    fetch = pltpu.make_async_copy(local_ref.at[:, pl.ds(at(window.row_at), rows)], local_buf, sem)
+    fetch = pltpu.make_async_copy(local_ref.at[:, pl.ds(at(window.row_at), rows)], local_buf, sems.at[0])
     fetch.start()
+    tables = pltpu.make_async_copy(table_ref, table, sems.at[1])
+    tables.start()
+    fetch.wait()
+    lane = lax.broadcasted_iota(jnp.int32, (rows, LANE), 1)
+    even, odd = [], []
     for c in range(2):
-        lhs[c * rows : (c + 1) * rows, pl.ds(pl.multiple_of((1 - band) * depth, LANE), depth)] = remote_ref[c]
-    fetch.wait()
-    for c in range(2):
-        lhs[c * rows : (c + 1) * rows, pl.ds(pl.multiple_of(band * depth, LANE), depth)] = local_buf[c]
-    lhs_high[...] = lhs[...].astype(jnp.bfloat16)
-    lhs_low[...] = (lhs[...] - lhs_high[...].astype(jnp.float32)).astype(jnp.bfloat16)
+        mine, theirs = local_buf[c], remote_ref[c]
+        low, high = jnp.where(band == 0, mine, theirs), jnp.where(band == 0, theirs, mine)
+        low_rest, high_rest = low[:, 4 * LANE :], high[:, 4 * LANE :]
+        turn = functools.partial(pltpu.roll, shift=LANE // 2, axis=1)
+        even_rest = jnp.where(lane < LANE // 2, low_rest, turn(high_rest))
+        odd_rest = jnp.where(lane < LANE // 2, turn(low_rest), high_rest)
+        even.append(jnp.concatenate([low[:, : 2 * LANE], high[:, : 2 * LANE], even_rest], axis=1))
+        odd.append(jnp.concatenate([low[:, 2 * LANE : 4 * LANE], high[:, 2 * LANE : 4 * LANE], odd_rest], axis=1))
+    for parity, parts in enumerate((even, odd)):
+        lhs = jnp.concatenate(parts)
+        lhs_high[parity] = lhs.astype(jnp.bfloat16)
+        lhs_low[parity] = (lhs - lhs_high[parity].astype(jnp.float32)).astype(jnp.bfloat16)
+    tables.wait()
 
     place = at(window.place)
     if window.first or window.last:
@@ -228,15 +262,20 @@
         for c in range(2):
             wind[c, pl.ds(at((extended - 2 * SUB, 0)), 2 * SUB), :] = carry_ref[c]
 
-    @pl.loop(0, NLON // 256)
-    def _(tile):
-        columns = pl.ds(pl.multiple_of(tile * 256, 256), 256)
-        dot = functools.partial(jnp.dot, preferred_element_type=jnp.float32)
-        total = dot(lhs_high[...], high_ref[:, columns])
-        total += dot(lhs_low[...], high_ref[:, columns])
-        total += dot(lhs_high[...], low_ref[:, columns])
+    dot = functools.partial(jnp.dot, preferred_element_type=jnp.float32)
+    for start in range(0, NLON // 2, 2 * LANE):
+        stop = min(start + 2 * LANE, NLON // 2)
+        columns = slice(start, stop)
+        sums = []
+        for parity in range(2):
+            total = dot(lhs_high[parity], table[2 * parity, :, columns])
+            total += dot(lhs_low[parity], table[2 * parity, :, columns])
+            total += dot(lhs_high[parity], table[2 * parity + 1, :, columns])
+            sums.append(total)
         for c in range(2):
-            wind[c, pl.ds(place, rows), columns] = total[c * rows : (c + 1) * rows]
+            even_sum, odd_sum = (total[c * rows : (c + 1) * rows] for total in sums)
+            wind[c, pl.ds(place, rows), start:stop] = even_sum + odd_sum
+            wind[c, pl.ds(place, rows), NLON // 2 + start : NLON // 2 + stop] = even_sum - odd_sum
 
     if not window.last:
         for c in range(2):
@@ -275,10 +314,10 @@
             both = second[c, rows_of(block), :] + third[c, rows_of(block), :]
             shift[c, rows_of(block), :] = (2.0 * both + (fourth - flow[c])) * (1.0 / 6.0)
 
-    half = window.width // 2 // SUB
+    quarter = window.width // 4 // SUB
 
     def entries(out_ref, base):
-        @pl.loop(0, half, unroll=4)
+        @pl.loop(0, quarter, unroll=4)
         def _(block):
             (e0, n0), (e1, n1) = derivatives(shift, base + block + 1)
             g_xx, g_xy, g_yx, g_yy = 1.0 + 0.5 * e0, 0.5 * n0, 0.5 * e1, 1.0 + 0.5 * n1
@@ -286,8 +325,11 @@
             out_ref[1, rows_of(block), :] = g_xx * g_xy + g_yx * g_yy
             out_ref[2, rows_of(block), :] = g_xy * g_xy + g_yy * g_yy
 
-    entries(keep_ref, core * half)
-    entries(send_ref, (1 - core) * half)
+    for out_ref, (a, b) in zip(out_refs, QUARTERS):
+        entries(out_ref, (2 * (core + a - 2 * core * a) + (side + b - 2 * side * b)) * quarter)
+
+
+QUARTERS = ((0, 0), (0, 1), (1, 0), (1, 1))
 
 
 def window_tensor(window, place, local, remote, table, waits, carry):
@@ -297,44 +339,43 @@
         pl.BlockSpec(memory_space=pltpu.SMEM),
         pl.BlockSpec(memory_space=pl.ANY),
         vmem,
-        vmem,
-        vmem,
+        pl.BlockSpec(memory_space=pl.ANY),
     ]
     in_specs += [pl.BlockSpec(memory_space=pl.ANY)] * len(waits)
-    operands = [place, local, remote, *table, *waits]
+    operands = [place, local, remote, table, *waits]
     if not window.first:
         in_specs.append(vmem)
         operands.append(carry)
-    out_shape = [jax.ShapeDtypeStruct((3, window.width // 2, NLON), jnp.float32)] * 2
+    out_shape = [jax.ShapeDtypeStruct((3, window.width // 4, NLON), jnp.float32)] * 4
     if not window.last:
         out_shape.append(jax.ShapeDtypeStruct((2, 2 * SUB, NLON), jnp.float32))
     field = pltpu.VMEM((2, window.extended, NLON), jnp.float32)
-    lhs_shape = (2 * window.rows, 2 * depth)
+    lhs_shape = (2, 2 * window.rows, depth)
     out = pl.pallas_call(
         functools.partial(window_kernel, window, depth, len(waits)),
         out_shape=out_shape,
         in_specs=in_specs,
         out_specs=[vmem] * len(out_shape),
         scratch_shapes=[
+            pltpu.VMEM(table.shape, table.dtype),
             pltpu.VMEM((2, window.rows, depth), jnp.float32),
-            pltpu.VMEM(lhs_shape, jnp.float32),
             pltpu.VMEM(lhs_shape, jnp.bfloat16),
             pltpu.VMEM(lhs_shape, jnp.bfloat16),
             field,
             field,
             field,
             field,
-            pltpu.SemaphoreType.DMA,
+            pltpu.SemaphoreType.DMA((2,)),
         ],
-        compiler_params=pltpu.CompilerParams(vmem_limit_bytes=VMEM_LIMIT),
+        compiler_params=pltpu.CompilerParams(vmem_limit_bytes=2 * VMEM_LIMIT),
         cost_estimate=pl.CostEstimate(
-            flops=5 * 3 * 2 * lhs_shape[0] * lhs_shape[1] * NLON,
+            flops=KERNEL_WORK * 3 * 2 * 2 * window.rows * depth * NLON,
             transcendentals=0,
-            bytes_accessed=4 * NLON * lhs_shape[1] + 8 * lhs_shape[0] * depth + 12 * window.width * NLON,
+            bytes_accessed=2 * table.size + 4 * window.rows * depth * 4 + 12 * window.width * NLON,
         ),
         name="window_tensor",
     )(*operands)
-    return out[0], out[1], (None if window.last else out[2])
+    return out[:4], (None if window.last else out[4])
 
 
 def pairs(members, bit):
@@ -347,10 +388,10 @@
     members = lax.axis_size("mem")
     band = lax.axis_index("band").astype(jnp.int32)
     member = lax.axis_index("mem").astype(jnp.int32)
-    place = jnp.stack([band, member % 2])
+    place = jnp.stack([band, member % 2, member // 2 % 2])
     spec = spec.reshape(levels, 2, parts * waves_local, nlat)
     windows = plan(nlat, [LANE] * (nlat // LANE))
-    table = [jnp.asarray(part) for part in wave_table(levels, waves_local)]
+    table = jnp.asarray(wave_table(levels, waves_local))
     swap = [(0, 1), (1, 0)]
 
     lead = windows[0].rows
@@ -382,6 +423,13 @@
         leaves = total(1 - mine)
         return [total(mine), lax.ppermute(leaves, "mem", pairs(members, bit)), leaves]
 
+    def advanced(parts_of, bit):
+        if len(parts_of) == 3:
+            return halved(parts_of, bit)
+        keep, leaves, keep_more, leaves_more = parts_of
+        leaves = leaves + leaves_more
+        return [keep + keep_more, lax.ppermute(leaves, "mem", pairs(members, bit)), leaves]
+
     def doubled(part, bit):
         beside = lax.ppermute(part, "mem", pairs(members, bit))
         mine = (member // bit) % 2
@@ -399,14 +447,16 @@
         if k + 2 < len(windows):
             waits.append(fetch_rows(k + 2, [remotes[k]] if carry is None else [remotes[k], carry]))
         for j in range(k - 1):
-            sums[j] = halved(sums[j], bits[k - 1 - j])
-            waits.append(sums[j][2])
-        keep, send, carry = window_tensor(window, place, local, remotes[k], table, waits, carry)
-        sums.append([keep, lax.ppermute(send, "mem", pairs(members, bits[0]))])
+            sums[j] = advanced(sums[j], bits[k - 1 - j])
+            waits.append(sums[j][-1])
+        quarters, carry = window_tensor(window, place, local, remotes[k], table, waits, carry)
+        first = lax.ppermute(quarters[3], "mem", pairs(members, bits[0]))
+        second = lax.ppermute(quarters[2], "mem", pairs(members, bits[0]))
+        sums.append([quarters[0], quarters[1], second, first])
     pieces = {"own": [], "both": [], "other": []}
     for k, window in enumerate(windows):
         for bit in bits[max(len(windows) - 1 - k, 1) :]:
-            sums[k] = halved(sums[k], bit)
+            sums[k] = advanced(sums[k], bit)
         pieces[window.side].append(exponent_of(sums[k][0] + sums[k][1], members))
 
     other = lax.ppermute(jnp.stack(pieces["other"]), "band", swap)
@@ -438,7 +488,7 @@
     _, levels, _, _, _, nlat = coeffs.shape
     members = lax.axis_size("mem")
     rows = nlat // lax.axis_size("band")
-    if levels == lax.axis_size("band") == 2 and members == 16 and nlat % (2 * LANE) == LANE and rows > LANE:
+    if coeffs.shape[4] == 5 * LANE // 2 and levels == lax.axis_size("band") == 2 and members == 16 and nlat % (2 * LANE) == LANE and rows > LANE:
         return by_levels(coeffs)
     return by_rows(coeffs)
 

time: 228 us -> 194 us (0.85)
  waiting for transfers between devices: 95.4 us -> 64.8 us
  local copies, waits for them, and re-layouts: 28.3 us -> 16.4 us
  starting transfers between devices: 30.5 us -> 35.6 us
  other arithmetic: 7.59 us -> 11.9 us
    ppermute x15 -> x10, waiting for transfers between devices: 54.8 us -> 31.8 us  [halved(): lax.ppermute(leaves, 'mem', pairs(members, bit))]
    ppermute x4, waiting for transfers between devices: 15 us -> 0.01 us  [fetch_rows(): remotes.append(lax.ppermute(piece, 'band', swap))]
    unnamed x46 -> x32, local copies, waits for them, and re-layouts: 24.1 us -> 12.2 us
    ppermute x5 -> x15, starting transfers between devices: 0.22 us -> 9.74 us  [the longest x5 5.13 us: advanced(): lax.ppermute(leaves, 'mem', pairs(members, bit))]
    ppermute x5 -> x15, waiting for transfers between devices: 0.01 us -> 9.02 us  [the longest x5 8.99 us: advanced(): lax.ppermute(leaves, 'mem', pairs(members, bit))]
    add x0 -> x10, other arithmetic: none -> 6.01 us  [the longest x5 3.44 us: advanced(): keep + keep_more]
    ppermute x8, starting transfers between devices: 4.69 us -> 0.81 us  [doubled(): beside = lax.ppermute(part, 'mem', pairs(members, bit))]
    add x15 -> x10, other arithmetic: 5.65 us -> 2.57 us  [total(): sum((lax.dynamic_slice_in_dim(part, which * half, half, axis=1) for part...]
  transfers between devices with their start and end apart: 35 -> 40, of which waited for: 16 -> 17; matrix products, arithmetic and copies ran while one was open for 4% -> 7% of each run, Pallas kernels for 27% -> 31%
where the time goes in v5:
time: 194 us; the launch traced here: 193 us
  waiting for transfers between devices  64.8 us (33%)
  Pallas kernels  63.6 us (33%)
  starting transfers between devices  35.6 us (18%)
  local copies, waits for them, and re-layouts  16.4 us (8%)
  other arithmetic  11.9 us (6%)
    pallas_call x5, Pallas kernels, window_tensor(): pl.pallas_call(functools.partial(window_kernel, window, depth, len(waits)...  47.4 us
    ppermute x10, waiting for transfers between devices, halved(): lax.ppermute(leaves, 'mem', pairs(members, bit))  31.8 us
    ppermute x8, waiting for transfers between devices, doubled(): beside = lax.ppermute(part, 'mem', pairs(members, bit))  23.6 us
    pallas_call x3, Pallas kernels, rows_first(): pl.pallas_call(transpose_kernel, grid_spec=pltpu.PrefetchScalarGridSpec(n...  16.2 us
    ppermute x10, starting transfers between devices, halved(): lax.ppermute(leaves, 'mem', pairs(members, bit))  15.7 us
    unnamed x32, local copies, waits for them, and re-layouts  12.2 us
    ppermute x5, waiting for transfers between devices, advanced(): lax.ppermute(leaves, 'mem', pairs(members, bit))  8.99 us
    ppermute x5, starting transfers between devices, advanced(): lax.ppermute(leaves, 'mem', pairs(members, bit))  5.13 us
  transfers between devices with their start and end apart: 40, of which 17 were waited for; matrix products, arithmetic and copies ran while one was open for 7% of the time, Pallas kernels for 31%

profile of v5, /device:TPU:0, one launch (start us, length us, event | category | flops | bytes accessed | tf_op | source)
XLA Modules:
  0.0 192.8 jit_solution(4996512216651500039)
XLA Ops:
  0.1 3.1 %rows_first.4 = f32[2,256,640]{2,1,0:T(8,128)S(1)} custom-call(s32[2]{0:T(128)S(1)} %pad_add_fusion.3.place, f32[2,2,640,640]{3,2,1,0:T(8,128)} %bitcast.25), custom_call_target="tpu_custom_call" | custom-call | bytes 10485760 | tf_op jit(solution)/shard_map/rows_first/pallas_call | solution.py:174
  4.0 2.9 %collective-permute-start = (f32[2,136,640]{2,1,0:T(8,128)}, f32[2,136,640]{2,1,0:T(8,128)}, u32[]{:S(2)}, u32[]{:S(2)}) collective-permute-start(f32[2,136,640]{2,1,0:T(8,128)} %constant_dynamic-slice_fusion.4), channel_id=1, source_target_pairs={{0,1},{1,0},{2,3},{3,2},{4,5},{5,4},{6,7},{7,6},{8,9},{9,8},{10,11... | collective-permute-start | bytes 2088968 | tf_op jit(solution)/shard_map/ppermute | solution.py:400
  7.1 6.6 %rows_first.5 = f32[2,640,640]{2,1,0:T(8,128)S(1)} custom-call(s32[2]{0:T(128)S(1)} %pad_add_fusion.place, f32[2,2,640,640]{3,2,1,0:T(8,128)} %bitcast.26), custom_call_target="tpu_custom_call" | custom-call | bytes 26214400 | tf_op jit(solution)/shard_map/rows_first/pallas_call | solution.py:174
  13.6 1.4 constant_dynamic-slice_fusion.1
  15.1 6.6 %rows_first.3.refs_1_ = f32[2,640,640]{2,1,0:T(8,128)S(1)} custom-call(s32[2]{0:T(128)S(1)} %pad_add_fusion.1.place, f32[2,2,640,640]{3,2,1,0:T(8,128)} %bitcast.27), custom_call_target="tpu_custom_call" | custom-call | bytes 26214400 | tf_op jit(solution)/shard_map/rows_first/pallas_call | solution.py:174
  21.6 1.7 copy-done
  23.7 2.1 %collective-permute-start.13 = (f32[2,128,640]{2,1,0:T(8,128)}, f32[2,128,640]{2,1,0:T(8,128)}, u32[]{:S(2)}, u32[]{:S(2)}) collective-permute-start(f32[2,128,640]{2,1,0:T(8,128)} %gated.3.refs_4_), channel_id=1, source_target_pairs={{0,1},{1,0},{2,3},{3,2},{4,5},{5,4},{6,7},{7,6},{8,9},{9,8},{10,11... | collective-permute-start | bytes 1966088 | tf_op jit(solution)/shard_map/ppermute | solution.py:408
  25.8 1.1 copy-done.2
  26.9 10.4 %window_tensor.5 = (f32[3,32,1280]{2,1,0:T(8,128)S(1)}, f32[3,32,1280]{2,1,0:T(8,128)S(1)}, f32[3,32,1280]{2,1,0:T(8,128)}, f32[3,32,1280]{2,1,0:T(8,128)}, f32[2,16,1280]{2,1,0:T(8,128)S(1)}) custom-call(s32[3]{0:T(128)S(1)} %pad_add_fusion.2.refs_0_, f32[2,640,640]{2,1,0:T(8,128)} %copy-done, f32[2,136,640]{2,1,0:T(8,128)} %collective-permute-done.refs_1_.refs_2_, ...), custom_call_target="tpu_custom_call" | custom-call | flops 10695475200 | bytes 6635520 | tf_op jit(solution)/shard_map/window_tensor/pallas_call | solution.py:354
  40.5 1.1 copy-done.1
  41.6 10.2 %window_tensor.6 = (f32[3,32,1280]{2,1,0:T(8,128)S(1)}, f32[3,32,1280]{2,1,0:T(8,128)S(1)}, f32[3,32,1280]{2,1,0:T(8,128)}, f32[3,32,1280]{2,1,0:T(8,128)}, f32[2,16,1280]{2,1,0:T(8,128)S(1)}) custom-call(s32[3]{0:T(128)S(1)} %pad_add_fusion.2.refs_0_, f32[2,640,640]{2,1,0:T(8,128)} %copy-done, f32[2,128,640]{2,1,0:T(8,128)} %collective-permute-done.6.refs_1_.refs_2_, ...), custom_call_target="tpu_custom_call" | custom-call | flops 10066329600 | bytes 6553600 | tf_op jit(solution)/shard_map/window_tensor/pallas_call | solution.py:354
  55.5 1.3 add.287.refs_5_
  56.8 2.1 %collective-permute-start.3 = (f32[3,32,1280]{2,1,0:T(8,128)S(1)}, f32[3,32,1280]{2,1,0:T(8,128)}, u32[]{:S(2)}, u32[]{:S(2)}) collective-permute-start(f32[3,32,1280]{2,1,0:T(8,128)S(1)} %add.287.refs_5_), channel_id=1, source_target_pairs={{0,4},{2,6},{4,0},{6,2},{8,12},{10,14},{12,8},{14,10},{16,20},{18,... | collective-permute-start | bytes 1474568 | tf_op jit(solution)/shard_map/ppermute | solution.py:431
  58.8 1.1 add.301.refs_5_
  60.1 1.1 add.285
  61.2 1.1 add.300
  62.4 2.0 %collective-permute-start.30 = (f32[2,120,640]{2,1,0:T(8,128)}, f32[2,120,640]{2,1,0:T(8,128)S(1)}, u32[]{:S(2)}, u32[]{:S(2)}) collective-permute-start(f32[2,120,640]{2,1,0:T(8,128)} %gated.5.refs_4_), channel_id=1, source_target_pairs={{0,1},{1,0},{2,3},{3,2},{4,5},{5,4},{6,7},{7,6},{8,9},{9,8},{10,11... | collective-permute-start | bytes 1843208 | tf_op jit(solution)/shard_map/ppermute | solution.py:408
  64.4 1.1 copy-done.3
  65.5 9.5 %window_tensor.7 = (f32[3,32,1280]{2,1,0:T(8,128)S(1)}, f32[3,32,1280]{2,1,0:T(8,128)S(1)}, f32[3,32,1280]{2,1,0:T(8,128)S(1)}, f32[3,32,1280]{2,1,0:T(8,128)S(1)}, f32[2,16,1280]{2,1,0:T(8,128)S(1)}) custom-call(s32[3]{0:T(128)S(1)} %pad_add_fusion.2.refs_0_, f32[2,640,640]{2,1,0:T(8,128)} %copy-done, ...), custom_call_target="tpu_custom_call" | custom-call | flops 10066329600 | bytes 6553600 | tf_op jit(solution)/shard_map/window_tensor/pallas_call | solution.py:354
  75.5 1.1 dynamic-slice_add_fusion.9
  76.6 4.5 %collective-permute-done.9 = f32[3,32,1280]{2,1,0:T(8,128)} collective-permute-done((f32[3,32,1280]{2,1,0:T(8,128)S(1)}, f32[3,32,1280]{2,1,0:T(8,128)}, u32[]{:S(2)}, u32[]{:S(2)}) %collective-permute-start.9) | collective-permute-done | bytes 491552 | tf_op jit(solution)/shard_map/ppermute | solution.py:431
  81.1 1.8 collective-permute-start.4
  82.9 1.1 dynamic-slice_add_fusion.7
  84.3 8.7 %window_tensor.8 = (f32[3,32,1280]{2,1,0:T(8,128)S(1)}, f32[3,32,1280]{2,1,0:T(8,128)S(1)}, f32[3,32,1280]{2,1,0:T(8,128)S(1)}, f32[3,32,1280]{2,1,0:T(8,128)S(1)}, f32[2,16,1280]{2,1,0:T(8,128)S(1)}) custom-call(s32[3]{0:T(128)S(1)} %pad_add_fusion.2.refs_0_, f32[2,640,640]{2,1,0:T(8,128)} %copy-done, f32[2,128,640]{2,1,0:T(8,128)S(1)} %collective-permute-done.24.refs_2_, ...), custom_call_target="tpu_custom_call" | custom-call | flops 10066329600 | bytes 6553600 | tf_op jit(solution)/shard_map/window_tensor/pallas_call | solution.py:354
  93.8 1.8 collective-permute-start.16
  95.7 2.7 %collective-permute-start.5 = (f32[3,8,1280]{2,1,0:T(8,128)S(1)}, f32[3,8,1280]{2,1,0:T(8,128)S(1)}, u32[]{:S(2)}, u32[]{:S(2)}) collective-permute-start(f32[3,8,1280]{2,1,0:T(8,128)S(1)} %dynamic-slice_add_fusion.14.refs_4_), channel_id=1, source_target_pairs={{0,16},{2,18},{4,20},{6,22},{8,24},{10,26},{12,28},{14,30},{16,0},... | collective-permute-start | bytes 368648 | tf_op jit(solution)/shard_map/ppermute | solution.py:424
  98.8 8.7 %window_tensor.9 = (f32[3,32,1280]{2,1,0:T(8,128)S(1)}, f32[3,32,1280]{2,1,0:T(8,128)S(1)}, f32[3,32,1280]{2,1,0:T(8,128)S(1)}, f32[3,32,1280]{2,1,0:T(8,128)S(1)}) custom-call(s32[3]{0:T(128)S(1)} %pad_add_fusion.2.refs_0_, f32[2,640,640]{2,1,0:T(8,128)} %copy-done, f32[2,120,640]{2,1,0:T(8,128)S(1)} %collective-permute-done.30.refs_2_, ...), custom_call_target="tpu_custom_call" | custom-call | flops 9437184000 | bytes 6471680 | tf_op jit(solution)/shard_map/window_tensor/pallas_call | solution.py:354
  108.1 1.4 collective-permute-done.11
  110.4 6.3 %collective-permute-done.17 = f32[3,16,1280]{2,1,0:T(8,128)S(1)} collective-permute-done((f32[3,16,1280]{2,1,0:T(8,128)S(1)}, f32[3,16,1280]{2,1,0:T(8,128)S(1)}, u32[]{:S(2)}, u32[]{:S(2)}) %collective-permute-start.17) | collective-permute-done | bytes 245792 | tf_op jit(solution)/shard_map/ppermute | solution.py:424
  116.7 3.3 %collective-permute-start.18 = (f32[3,8,1280]{2,1,0:T(8,128)S(1)}, f32[3,8,1280]{2,1,0:T(8,128)S(1)}, u32[]{:S(2)}, u32[]{:S(2)}) collective-permute-start(f32[3,8,1280]{2,1,0:T(8,128)S(1)} %dynamic-slice_add_fusion.12), channel_id=1, source_target_pairs={{0,16},{2,18},{4,20},{6,22},{8,24},{10,26},{12,28},{14,30},{16,0},... | collective-permute-start | bytes 368648 | tf_op jit(solution)/shard_map/ppermute | solution.py:424
  120.0 1.5 collective-permute-start.12
  122.1 3.5 %collective-permute-done.18 = f32[3,8,1280]{2,1,0:T(8,128)S(1)} collective-permute-done((f32[3,8,1280]{2,1,0:T(8,128)S(1)}, f32[3,8,1280]{2,1,0:T(8,128)S(1)}, u32[]{:S(2)}, u32[]{:S(2)}) %collective-permute-start.18) | collective-permute-done | bytes 122912 | tf_op jit(solution)/shard_map/ppermute | solution.py:424
  126.5 2.9 %collective-permute-start.31 = (f32[3,32,1280]{2,1,0:T(8,128)S(1)}, f32[3,32,1280]{2,1,0:T(8,128)}, u32[]{:S(2)}, u32[]{:S(2)}) collective-permute-start(f32[3,32,1280]{2,1,0:T(8,128)S(1)} %get-tuple-element.50), channel_id=1, source_target_pairs={{0,2},{2,0},{4,6},{6,4},{8,10},{10,8},{12,14},{14,12},{16,18},{18,... | collective-permute-start | bytes 1474568 | tf_op jit(solution)/shard_map/ppermute | solution.py:454
  130.4 4.5 %collective-permute-done.27 = f32[3,32,1280]{2,1,0:T(8,128)S(1)} collective-permute-done((f32[3,32,1280]{2,1,0:T(8,128)S(1)}, f32[3,32,1280]{2,1,0:T(8,128)S(1)}, u32[]{:S(2)}, u32[]{:S(2)}) %collective-permute-start.27) | collective-permute-done | bytes 491552 | tf_op jit(solution)/shard_map/ppermute | solution.py:431
  135.0 2.2 %collective-permute-start.28 = (f32[3,16,1280]{2,1,0:T(8,128)S(1)}, f32[3,16,1280]{2,1,0:T(8,128)S(1)}, u32[]{:S(2)}, u32[]{:S(2)}) collective-permute-start(f32[3,16,1280]{2,1,0:T(8,128)S(1)} %get-tuple-element.63), channel_id=1, source_target_pairs={{0,8},{2,10},{4,12},{6,14},{8,0},{10,2},{12,4},{14,6},{16,24},{18,... | collective-permute-start | bytes 737288 | tf_op jit(solution)/shard_map/ppermute | solution.py:424
  138.3 1.7 collective-permute-done.20
  140.2 3.4 %collective-permute-done.28 = f32[3,16,1280]{2,1,0:T(8,128)S(1)} collective-permute-done((f32[3,16,1280]{2,1,0:T(8,128)S(1)}, f32[3,16,1280]{2,1,0:T(8,128)S(1)}, u32[]{:S(2)}, u32[]{:S(2)}) %collective-permute-start.28) | collective-permute-done | bytes 245792 | tf_op jit(solution)/shard_map/ppermute | solution.py:424
  144.7 2.5 %collective-permute-start.34 = (f32[3,16,1280]{2,1,0:T(8,128)S(1)}, f32[3,16,1280]{2,1,0:T(8,128)S(1)}, u32[]{:S(2)}, u32[]{:S(2)}) collective-permute-start(f32[3,16,1280]{2,1,0:T(8,128)S(1)} %get-tuple-element.65), channel_id=1, source_target_pairs={{0,8},{2,10},{4,12},{6,14},{8,0},{10,2},{12,4},{14,6},{16,24},{18,... | collective-permute-start | bytes 737288 | tf_op jit(solution)/shard_map/ppermute | solution.py:424
  147.2 4.6 %collective-permute-done.29 = f32[3,8,1280]{2,1,0:T(8,128)S(1)} collective-permute-done((f32[3,8,1280]{2,1,0:T(8,128)S(1)}, f32[3,8,1280]{2,1,0:T(8,128)S(1)}, u32[]{:S(2)}, u32[]{:S(2)}) %collective-permute-start.29) | collective-permute-done | bytes 122912 | tf_op jit(solution)/shard_map/ppermute | solution.py:424
  151.9 4.5 %collective-permute-done.34 = f32[3,16,1280]{2,1,0:T(8,128)S(1)} collective-permute-done((f32[3,16,1280]{2,1,0:T(8,128)S(1)}, f32[3,16,1280]{2,1,0:T(8,128)S(1)}, u32[]{:S(2)}, u32[]{:S(2)}) %collective-permute-start.34) | collective-permute-done | bytes 245792 | tf_op jit(solution)/shard_map/ppermute | solution.py:424
  157.1 7.6 %collective-permute-done.35 = f32[3,8,1280]{2,1,0:T(8,128)S(1)} collective-permute-done((f32[3,8,1280]{2,1,0:T(8,128)S(1)}, f32[3,8,1280]{2,1,0:T(8,128)S(1)}, u32[]{:S(2)}, u32[]{:S(2)}) %collective-permute-start.35) | collective-permute-done | bytes 122912 | tf_op jit(solution)/shard_map/ppermute | solution.py:424
  165.0 5.5 %collective-permute-done.36 = f32[2,8,1280]{2,1,0:T(8,128)S(1)} collective-permute-done((f32[2,8,1280]{2,1,0:T(8,128)S(1)}, f32[2,8,1280]{2,1,0:T(8,128)S(1)}, u32[]{:S(2)}, u32[]{:S(2)}) %collective-permute-start.36) | collective-permute-done | bytes 81952 | tf_op jit(solution)/shard_map/ppermute | solution.py:434
  170.6 5.6 %collective-permute-done.37 = f32[2,16,1280]{2,1,0:T(8,128)S(1)} collective-permute-done((f32[2,16,1280]{2,1,0:T(8,128)S(1)}, f32[2,16,1280]{2,1,0:T(8,128)S(1)}, u32[]{:S(2)}, u32[]{:S(2)}) %collective-permute-start.37) | collective-permute-done | bytes 163872 | tf_op jit(solution)/shard_map/ppermute | solution.py:434
  176.4 2.4 %collective-permute-done.22 = f32[3,32,1280]{2,1,0:T(8,128)S(1)} collective-permute-done((f32[3,32,1280]{2,1,0:T(8,128)S(1)}, f32[3,32,1280]{2,1,0:T(8,128)S(1)}, u32[]{:S(2)}, u32[]{:S(2)}) %collective-permute-start.22) | collective-permute-done | bytes 491552 | tf_op jit(solution)/shard_map/ppermute | solution.py:434
  178.9 6.3 %collective-permute-done.38 = f32[2,32,1280]{2,1,0:T(8,128)S(1)} collective-permute-done((f32[2,32,1280]{2,1,0:T(8,128)S(1)}, f32[2,32,1280]{2,1,0:T(8,128)S(1)}, u32[]{:S(2)}, u32[]{:S(2)}) %collective-permute-start.38) | collective-permute-done | bytes 327712 | tf_op jit(solution)/shard_map/ppermute | solution.py:434
  185.3 2.2 %collective-permute-done.39 = f32[2,64,1280]{2,1,0:T(8,128)} collective-permute-done((f32[2,64,1280]{2,1,0:T(8,128)S(1)}, f32[2,64,1280]{2,1,0:T(8,128)}, u32[]{:S(2)}, u32[]{:S(2)}) %collective-permute-start.39) | collective-permute-done | bytes 655392 | tf_op jit(solution)/shard_map/ppermute | solution.py:434
  187.5 1.4 maximum_select_fusion.2
  190.2 1.7 copy-done.15
  (129 shorter events, 20.7 us)
Async XLA Ops:
  4.0 19.7 %collective-permute-start = (f32[2,136,640]{2,1,0:T(8,128)}, f32[2,136,640]{2,1,0:T(8,128)}, u32[]{:S(2)}, u32[]{:S(2)}) collective-permute-start(f32[2,136,640]{2,1,0:T(8,128)} %constant_dynamic-slice_fusion.4), channel_id=1, source_target_pairs={{0,1},{1,0},{2,3},{3,2},{4,5},{5,4},{6,7},{7,6},{8,9},{9,8},{10,11... | collective-permute-start | bytes 2088968 | tf_op jit(solution)/shard_map/ppermute | solution.py:400
  15.0 24.6 %collective-permute-start.6 = (f32[2,128,640]{2,1,0:T(8,128)}, f32[2,128,640]{2,1,0:T(8,128)}, u32[]{:S(2)}, u32[]{:S(2)}) collective-permute-start(f32[2,128,640]{2,1,0:T(8,128)} %get-tuple-element.54), channel_id=1, source_target_pairs={{0,1},{1,0},{2,3},{3,2},{4,5},{5,4},{6,7},{7,6},{8,9},{9,8},{10,11... | collective-permute-start | bytes 1966088 | tf_op jit(solution)/shard_map/ppermute | solution.py:408
  21.6 1.7 copy-start
  23.7 38.6 %collective-permute-start.13 = (f32[2,128,640]{2,1,0:T(8,128)}, f32[2,128,640]{2,1,0:T(8,128)}, u32[]{:S(2)}, u32[]{:S(2)}) collective-permute-start(f32[2,128,640]{2,1,0:T(8,128)} %gated.3.refs_4_), channel_id=1, source_target_pairs={{0,1},{1,0},{2,3},{3,2},{4,5},{5,4},{6,7},{7,6},{8,9},{9,8},{10,11... | collective-permute-start | bytes 1966088 | tf_op jit(solution)/shard_map/ppermute | solution.py:408
  25.8 1.1 copy-start.2
  39.6 15.9 %collective-permute-start.2 = (f32[3,32,1280]{2,1,0:T(8,128)}, f32[3,32,1280]{2,1,0:T(8,128)}, u32[]{:S(2)}, u32[]{:S(2)}) collective-permute-start(f32[3,32,1280]{2,1,0:T(8,128)} %get-tuple-element.32), channel_id=1, source_target_pairs={{0,2},{2,0},{4,6},{6,4},{8,10},{10,8},{12,14},{14,12},{16,18},{18,... | collective-permute-start | bytes 1474568 | tf_op jit(solution)/shard_map/ppermute | solution.py:453
  54.1 2.7 %collective-permute-start.8 = (f32[3,32,1280]{2,1,0:T(8,128)}, f32[3,32,1280]{2,1,0:T(8,128)}, u32[]{:S(2)}, u32[]{:S(2)}) collective-permute-start(f32[3,32,1280]{2,1,0:T(8,128)} %get-tuple-element.37), channel_id=1, source_target_pairs={{0,2},{2,0},{4,6},{6,4},{8,10},{10,8},{12,14},{14,12},{16,18},{18,... | collective-permute-start | bytes 1474568 | tf_op jit(solution)/shard_map/ppermute | solution.py:453
  54.1 5.9 %collective-permute-start.1 = (f32[3,32,1280]{2,1,0:T(8,128)}, f32[3,32,1280]{2,1,0:T(8,128)}, u32[]{:S(2)}, u32[]{:S(2)}) collective-permute-start(f32[3,32,1280]{2,1,0:T(8,128)} %get-tuple-element.30), channel_id=1, source_target_pairs={{0,2},{2,0},{4,6},{6,4},{8,10},{10,8},{12,14},{14,12},{16,18},{18,... | collective-permute-start | bytes 1474568 | tf_op jit(solution)/shard_map/ppermute | solution.py:454
  54.6 6.6 %collective-permute-start.7 = (f32[3,32,1280]{2,1,0:T(8,128)}, f32[3,32,1280]{2,1,0:T(8,128)}, u32[]{:S(2)}, u32[]{:S(2)}) collective-permute-start(f32[3,32,1280]{2,1,0:T(8,128)} %get-tuple-element.35), channel_id=1, source_target_pairs={{0,2},{2,0},{4,6},{6,4},{8,10},{10,8},{12,14},{14,12},{16,18},{18,... | collective-permute-start | bytes 1474568 | tf_op jit(solution)/shard_map/ppermute | solution.py:454
  54.6 4.3 %copy-start.10 = (f32[3,32,1280]{2,1,0:T(8,128)S(1)}, f32[3,32,1280]{2,1,0:T(8,128)}, u32[]{:S(2)}) copy-start(f32[3,32,1280]{2,1,0:T(8,128)} %copy-done.9) | copy-start | bytes 1474564
  55.4 4.6 %copy-start.5 = (f32[3,32,1280]{2,1,0:T(8,128)S(1)}, f32[3,32,1280]{2,1,0:T(8,128)}, u32[]{:S(2)}) copy-start(f32[3,32,1280]{2,1,0:T(8,128)} %copy-done.4) | copy-start | bytes 1474564
  55.4 28.6 %collective-permute-start.24 = (f32[2,128,640]{2,1,0:T(8,128)}, f32[2,128,640]{2,1,0:T(8,128)S(1)}, u32[]{:S(2)}, u32[]{:S(2)}) collective-permute-start(f32[2,128,640]{2,1,0:T(8,128)} %gated.4.refs_4_), channel_id=1, source_target_pairs={{0,1},{1,0},{2,3},{3,2},{4,5},{5,4},{6,7},{7,6},{8,9},{9,8},{10,11... | collective-permute-start | bytes 1966088 | tf_op jit(solution)/shard_map/ppermute | solution.py:408
  56.8 4.4 %copy-start.7 = (f32[3,32,1280]{2,1,0:T(8,128)S(1)}, f32[3,32,1280]{2,1,0:T(8,128)}, u32[]{:S(2)}) copy-start(f32[3,32,1280]{2,1,0:T(8,128)} %copy-done.6) | copy-start | bytes 1474564
  56.8 18.2 %collective-permute-start.3 = (f32[3,32,1280]{2,1,0:T(8,128)S(1)}, f32[3,32,1280]{2,1,0:T(8,128)}, u32[]{:S(2)}, u32[]{:S(2)}) collective-permute-start(f32[3,32,1280]{2,1,0:T(8,128)S(1)} %add.287.refs_5_), channel_id=1, source_target_pairs={{0,4},{2,6},{4,0},{6,2},{8,12},{10,14},{12,8},{14,10},{16,20},{18,... | collective-permute-start | bytes 1474568 | tf_op jit(solution)/shard_map/ppermute | solution.py:431
  59.9 21.2 %collective-permute-start.9 = (f32[3,32,1280]{2,1,0:T(8,128)S(1)}, f32[3,32,1280]{2,1,0:T(8,128)}, u32[]{:S(2)}, u32[]{:S(2)}) collective-permute-start(f32[3,32,1280]{2,1,0:T(8,128)S(1)} %add.301.refs_5_), channel_id=1, source_target_pairs={{0,4},{2,6},{4,0},{6,2},{8,12},{10,14},{12,8},{14,10},{16,20},{18,... | collective-permute-start | bytes 1474568 | tf_op jit(solution)/shard_map/ppermute | solution.py:431
  61.2 3.2 %copy-start.14 = (f32[2,16,1280]{2,1,0:T(8,128)S(1)}, f32[2,16,1280]{2,1,0:T(8,128)}, u32[]{:S(2)}) copy-start(f32[2,16,1280]{2,1,0:T(8,128)} %copy-done.13) | copy-start | bytes 491524
  62.4 36.0 %collective-permute-start.30 = (f32[2,120,640]{2,1,0:T(8,128)}, f32[2,120,640]{2,1,0:T(8,128)S(1)}, u32[]{:S(2)}, u32[]{:S(2)}) collective-permute-start(f32[2,120,640]{2,1,0:T(8,128)} %gated.5.refs_4_), channel_id=1, source_target_pairs={{0,1},{1,0},{2,3},{3,2},{4,5},{5,4},{6,7},{7,6},{8,9},{9,8},{10,11... | collective-permute-start | bytes 1843208 | tf_op jit(solution)/shard_map/ppermute | solution.py:408
  64.4 1.1 copy-start.3
  74.9 18.1 %collective-permute-start.14 = (f32[3,32,1280]{2,1,0:T(8,128)S(1)}, f32[3,32,1280]{2,1,0:T(8,128)S(1)}, u32[]{:S(2)}, u32[]{:S(2)}) collective-permute-start(f32[3,32,1280]{2,1,0:T(8,128)S(1)} %get-tuple-element.40), channel_id=1, source_target_pairs={{0,2},{2,0},{4,6},{6,4},{8,10},{10,8},{12,14},{14,12},{16,18},{18,... | collective-permute-start | bytes 1474568 | tf_op jit(solution)/shard_map/ppermute | solution.py:454
  75.0 18.2 %collective-permute-start.15 = (f32[3,32,1280]{2,1,0:T(8,128)S(1)}, f32[3,32,1280]{2,1,0:T(8,128)S(1)}, u32[]{:S(2)}, u32[]{:S(2)}) collective-permute-start(f32[3,32,1280]{2,1,0:T(8,128)S(1)} %get-tuple-element.42), channel_id=1, source_target_pairs={{0,2},{2,0},{4,6},{6,4},{8,10},{10,8},{12,14},{14,12},{16,18},{18,... | collective-permute-start | bytes 1474568 | tf_op jit(solution)/shard_map/ppermute | solution.py:453
  81.1 12.7 %collective-permute-start.4 = (f32[3,16,1280]{2,1,0:T(8,128)S(1)}, f32[3,16,1280]{2,1,0:T(8,128)S(1)}, u32[]{:S(2)}, u32[]{:S(2)}) collective-permute-start(f32[3,16,1280]{2,1,0:T(8,128)S(1)} %get-tuple-element.67.refs_4_), channel_id=1, source_target_pairs={{0,8},{2,10},{4,12},{6,14},{8,0},{10,2},{12,4},{14,6},{16,24},{18,... | collective-permute-start | bytes 737288 | tf_op jit(solution)/shard_map/ppermute | solution.py:424
  84.0 11.6 %collective-permute-start.10 = (f32[3,16,1280]{2,1,0:T(8,128)S(1)}, f32[3,16,1280]{2,1,0:T(8,128)S(1)}, u32[]{:S(2)}, u32[]{:S(2)}) collective-permute-start(f32[3,16,1280]{2,1,0:T(8,128)S(1)} %get-tuple-element.69.refs_5_), channel_id=1, source_target_pairs={{0,8},{2,10},{4,12},{6,14},{8,0},{10,2},{12,4},{14,6},{16,24},{18,... | collective-permute-start | bytes 737288 | tf_op jit(solution)/shard_map/ppermute | solution.py:424
  93.1 33.5 %collective-permute-start.25 = (f32[3,32,1280]{2,1,0:T(8,128)S(1)}, f32[3,32,1280]{2,1,0:T(8,128)S(1)}, u32[]{:S(2)}, u32[]{:S(2)}) collective-permute-start(f32[3,32,1280]{2,1,0:T(8,128)S(1)} %get-tuple-element.45), channel_id=1, source_target_pairs={{0,2},{2,0},{4,6},{6,4},{8,10},{10,8},{12,14},{14,12},{16,18},{18,... | collective-permute-start | bytes 1474568 | tf_op jit(solution)/shard_map/ppermute | solution.py:454
  93.2 28.2 %collective-permute-start.26 = (f32[3,32,1280]{2,1,0:T(8,128)S(1)}, f32[3,32,1280]{2,1,0:T(8,128)S(1)}, u32[]{:S(2)}, u32[]{:S(2)}) collective-permute-start(f32[3,32,1280]{2,1,0:T(8,128)S(1)} %get-tuple-element.47), channel_id=1, source_target_pairs={{0,2},{2,0},{4,6},{6,4},{8,10},{10,8},{12,14},{14,12},{16,18},{18,... | collective-permute-start | bytes 1474568 | tf_op jit(solution)/shard_map/ppermute | solution.py:453
  93.8 15.7 %collective-permute-start.16 = (f32[3,32,1280]{2,1,0:T(8,128)S(1)}, f32[3,32,1280]{2,1,0:T(8,128)S(1)}, u32[]{:S(2)}, u32[]{:S(2)}) collective-permute-start(f32[3,32,1280]{2,1,0:T(8,128)S(1)} %add.312.refs_6_), channel_id=1, source_target_pairs={{0,4},{2,6},{4,0},{6,2},{8,12},{10,14},{12,8},{14,10},{16,20},{18,... | collective-permute-start | bytes 1474568 | tf_op jit(solution)/shard_map/ppermute | solution.py:431
  95.7 12.3 %collective-permute-start.5 = (f32[3,8,1280]{2,1,0:T(8,128)S(1)}, f32[3,8,1280]{2,1,0:T(8,128)S(1)}, u32[]{:S(2)}, u32[]{:S(2)}) collective-permute-start(f32[3,8,1280]{2,1,0:T(8,128)S(1)} %dynamic-slice_add_fusion.14.refs_4_), channel_id=1, source_target_pairs={{0,16},{2,18},{4,20},{6,22},{8,24},{10,26},{12,28},{14,30},{16,0},... | collective-permute-start | bytes 368648 | tf_op jit(solution)/shard_map/ppermute | solution.py:424
  98.4 11.1 %collective-permute-start.11 = (f32[3,8,1280]{2,1,0:T(8,128)S(1)}, f32[3,8,1280]{2,1,0:T(8,128)S(1)}, u32[]{:S(2)}, u32[]{:S(2)}) collective-permute-start(f32[3,8,1280]{2,1,0:T(8,128)S(1)} %dynamic-slice_add_fusion.13), channel_id=1, source_target_pairs={{0,16},{2,18},{4,20},{6,22},{8,24},{10,26},{12,28},{14,30},{16,0},... | collective-permute-start | bytes 368648 | tf_op jit(solution)/shard_map/ppermute | solution.py:424
  108.0 21.5 %collective-permute-start.32 = (f32[3,32,1280]{2,1,0:T(8,128)S(1)}, f32[3,32,1280]{2,1,0:T(8,128)S(1)}, u32[]{:S(2)}, u32[]{:S(2)}) collective-permute-start(f32[3,32,1280]{2,1,0:T(8,128)S(1)} %get-tuple-element.52), channel_id=1, source_target_pairs={{0,2},{2,0},{4,6},{6,4},{8,10},{10,8},{12,14},{14,12},{16,18},{18,... | collective-permute-start | bytes 1474568 | tf_op jit(solution)/shard_map/ppermute | solution.py:453
  109.6 7.0 %collective-permute-start.17 = (f32[3,16,1280]{2,1,0:T(8,128)S(1)}, f32[3,16,1280]{2,1,0:T(8,128)S(1)}, u32[]{:S(2)}, u32[]{:S(2)}) collective-permute-start(f32[3,16,1280]{2,1,0:T(8,128)S(1)} %get-tuple-element.71), channel_id=1, source_target_pairs={{0,8},{2,10},{4,12},{6,14},{8,0},{10,2},{12,4},{14,6},{16,24},{18,... | collective-permute-start | bytes 737288 | tf_op jit(solution)/shard_map/ppermute | solution.py:424
  116.7 8.9 %collective-permute-start.18 = (f32[3,8,1280]{2,1,0:T(8,128)S(1)}, f32[3,8,1280]{2,1,0:T(8,128)S(1)}, u32[]{:S(2)}, u32[]{:S(2)}) collective-permute-start(f32[3,8,1280]{2,1,0:T(8,128)S(1)} %dynamic-slice_add_fusion.12), channel_id=1, source_target_pairs={{0,16},{2,18},{4,20},{6,22},{8,24},{10,26},{12,28},{14,30},{16,0},... | collective-permute-start | bytes 368648 | tf_op jit(solution)/shard_map/ppermute | solution.py:424
  120.0 10.2 %collective-permute-start.12 = (f32[2,8,1280]{2,1,0:T(8,128)S(1)}, f32[2,8,1280]{2,1,0:T(8,128)S(1)}, u32[]{:S(2)}, u32[]{:S(2)}) collective-permute-start(f32[2,8,1280]{2,1,0:T(8,128)S(1)} %pad_maximum_fusion.1), channel_id=1, source_target_pairs={{0,1},{1,0},{2,3},{3,2},{4,5},{5,4},{6,7},{7,6},{8,9},{9,8},{10,11... | collective-permute-start | bytes 245768 | tf_op jit(solution)/shard_map/ppermute | solution.py:462
  121.5 13.4 %collective-permute-start.27 = (f32[3,32,1280]{2,1,0:T(8,128)S(1)}, f32[3,32,1280]{2,1,0:T(8,128)S(1)}, u32[]{:S(2)}, u32[]{:S(2)}) collective-permute-start(f32[3,32,1280]{2,1,0:T(8,128)S(1)} %add.324), channel_id=1, source_target_pairs={{0,4},{2,6},{4,0},{6,2},{8,12},{10,14},{12,8},{14,10},{16,20},{18,... | collective-permute-start | bytes 1474568 | tf_op jit(solution)/shard_map/ppermute | solution.py:431
  125.6 4.5 %collective-permute-start.19 = (f32[8,1280]{1,0:T(8,128)S(1)}, f32[8,1280]{1,0:T(8,128)S(1)}, u32[]{:S(2)}, u32[]{:S(2)}) collective-permute-start(f32[8,1280]{1,0:T(8,128)S(1)} %fusion.18), channel_id=1, source_target_pairs={{0,0},{1,2},{2,1},{3,3},{4,4},{5,6},{6,5},{7,7},{8,8},{9,10},{10,9... | collective-permute-start | bytes 122888 | tf_op jit(solution)/shard_map/ppermute | solution.py:468
  126.5 10.7 %collective-permute-start.31 = (f32[3,32,1280]{2,1,0:T(8,128)S(1)}, f32[3,32,1280]{2,1,0:T(8,128)}, u32[]{:S(2)}, u32[]{:S(2)}) collective-permute-start(f32[3,32,1280]{2,1,0:T(8,128)S(1)} %get-tuple-element.50), channel_id=1, source_target_pairs={{0,2},{2,0},{4,6},{6,4},{8,10},{10,8},{12,14},{14,12},{16,18},{18,... | collective-permute-start | bytes 1474568 | tf_op jit(solution)/shard_map/ppermute | solution.py:454
  129.6 15.0 %collective-permute-start.33 = (f32[3,32,1280]{2,1,0:T(8,128)S(1)}, f32[3,32,1280]{2,1,0:T(8,128)S(1)}, u32[]{:S(2)}, u32[]{:S(2)}) collective-permute-start(f32[3,32,1280]{2,1,0:T(8,128)S(1)} %add.335), channel_id=1, source_target_pairs={{0,4},{2,6},{4,0},{6,2},{8,12},{10,14},{12,8},{14,10},{16,20},{18,... | collective-permute-start | bytes 1474568 | tf_op jit(solution)/shard_map/ppermute | solution.py:431
  130.2 9.9 %collective-permute-start.20 = (f32[3,8,1280]{2,1,0:T(8,128)S(1)}, f32[3,8,1280]{2,1,0:T(8,128)S(1)}, u32[]{:S(2)}, u32[]{:S(2)}) collective-permute-start(f32[3,8,1280]{2,1,0:T(8,128)S(1)} %pad_maximum_fusion), channel_id=1, source_target_pairs={{0,16},{2,18},{4,20},{6,22},{8,24},{10,26},{12,28},{14,30},{16,0},... | collective-permute-start | bytes 368648 | tf_op jit(solution)/shard_map/ppermute | solution.py:434
  135.0 8.6 %collective-permute-start.28 = (f32[3,16,1280]{2,1,0:T(8,128)S(1)}, f32[3,16,1280]{2,1,0:T(8,128)S(1)}, u32[]{:S(2)}, u32[]{:S(2)}) collective-permute-start(f32[3,16,1280]{2,1,0:T(8,128)S(1)} %get-tuple-element.63), channel_id=1, source_target_pairs={{0,8},{2,10},{4,12},{6,14},{8,0},{10,2},{12,4},{14,6},{16,24},{18,... | collective-permute-start | bytes 737288 | tf_op jit(solution)/shard_map/ppermute | solution.py:424
  140.1 24.8 %collective-permute-start.21 = (f32[3,16,1280]{2,1,0:T(8,128)S(1)}, f32[3,16,1280]{2,1,0:T(8,128)S(1)}, u32[]{:S(2)}, u32[]{:S(2)}) collective-permute-start(f32[3,16,1280]{2,1,0:T(8,128)S(1)} %maximum_select_fusion.7), channel_id=1, source_target_pairs={{0,8},{2,10},{4,12},{6,14},{8,0},{10,2},{12,4},{14,6},{16,24},{18,... | collective-permute-start | bytes 737288 | tf_op jit(solution)/shard_map/ppermute | solution.py:434
  143.6 8.3 %collective-permute-start.29 = (f32[3,8,1280]{2,1,0:T(8,128)S(1)}, f32[3,8,1280]{2,1,0:T(8,128)S(1)}, u32[]{:S(2)}, u32[]{:S(2)}) collective-permute-start(f32[3,8,1280]{2,1,0:T(8,128)S(1)} %dynamic-slice_add_fusion.11), channel_id=1, source_target_pairs={{0,16},{2,18},{4,20},{6,22},{8,24},{10,26},{12,28},{14,30},{16,0},... | collective-permute-start | bytes 368648 | tf_op jit(solution)/shard_map/ppermute | solution.py:424
  144.7 11.7 %collective-permute-start.34 = (f32[3,16,1280]{2,1,0:T(8,128)S(1)}, f32[3,16,1280]{2,1,0:T(8,128)S(1)}, u32[]{:S(2)}, u32[]{:S(2)}) collective-permute-start(f32[3,16,1280]{2,1,0:T(8,128)S(1)} %get-tuple-element.65), channel_id=1, source_target_pairs={{0,8},{2,10},{4,12},{6,14},{8,0},{10,2},{12,4},{14,6},{16,24},{18,... | collective-permute-start | bytes 737288 | tf_op jit(solution)/shard_map/ppermute | solution.py:424
  156.4 8.3 %collective-permute-start.35 = (f32[3,8,1280]{2,1,0:T(8,128)S(1)}, f32[3,8,1280]{2,1,0:T(8,128)S(1)}, u32[]{:S(2)}, u32[]{:S(2)}) collective-permute-start(f32[3,8,1280]{2,1,0:T(8,128)S(1)} %dynamic-slice_add_fusion.10), channel_id=1, source_target_pairs={{0,16},{2,18},{4,20},{6,22},{8,24},{10,26},{12,28},{14,30},{16,0},... | collective-permute-start | bytes 368648 | tf_op jit(solution)/shard_map/ppermute | solution.py:424
  164.8 5.7 %collective-permute-start.36 = (f32[2,8,1280]{2,1,0:T(8,128)S(1)}, f32[2,8,1280]{2,1,0:T(8,128)S(1)}, u32[]{:S(2)}, u32[]{:S(2)}) collective-permute-start(f32[2,8,1280]{2,1,0:T(8,128)S(1)} %pad_maximum_fusion.2), channel_id=1, source_target_pairs={{0,16},{2,18},{4,20},{6,22},{8,24},{10,26},{12,28},{14,30},{16,0},... | collective-permute-start | bytes 245768 | tf_op jit(solution)/shard_map/ppermute | solution.py:434
  164.9 13.8 %collective-permute-start.22 = (f32[3,32,1280]{2,1,0:T(8,128)S(1)}, f32[3,32,1280]{2,1,0:T(8,128)S(1)}, u32[]{:S(2)}, u32[]{:S(2)}) collective-permute-start(f32[3,32,1280]{2,1,0:T(8,128)S(1)} %maximum_select_fusion.5), channel_id=1, source_target_pairs={{0,4},{2,6},{4,0},{6,2},{8,12},{10,14},{12,8},{14,10},{16,20},{18,... | collective-permute-start | bytes 1474568 | tf_op jit(solution)/shard_map/ppermute | solution.py:434
  170.5 5.7 %collective-permute-start.37 = (f32[2,16,1280]{2,1,0:T(8,128)S(1)}, f32[2,16,1280]{2,1,0:T(8,128)S(1)}, u32[]{:S(2)}, u32[]{:S(2)}) collective-permute-start(f32[2,16,1280]{2,1,0:T(8,128)S(1)} %maximum_select_fusion.8), channel_id=1, source_target_pairs={{0,8},{2,10},{4,12},{6,14},{8,0},{10,2},{12,4},{14,6},{16,24},{18,... | collective-permute-start | bytes 491528 | tf_op jit(solution)/shard_map/ppermute | solution.py:434
  176.2 8.9 %collective-permute-start.38 = (f32[2,32,1280]{2,1,0:T(8,128)S(1)}, f32[2,32,1280]{2,1,0:T(8,128)S(1)}, u32[]{:S(2)}, u32[]{:S(2)}) collective-permute-start(f32[2,32,1280]{2,1,0:T(8,128)S(1)} %maximum_select_fusion.6), channel_id=1, source_target_pairs={{0,4},{2,6},{4,0},{6,2},{8,12},{10,14},{12,8},{14,10},{16,20},{18,... | collective-permute-start | bytes 983048 | tf_op jit(solution)/shard_map/ppermute | solution.py:434
  178.8 10.1 %collective-permute-start.23 = (f32[3,64,1280]{2,1,0:T(8,128)S(1)}, f32[3,64,1280]{2,1,0:T(8,128)S(1)}, u32[]{:S(2)}, u32[]{:S(2)}) collective-permute-start(f32[3,64,1280]{2,1,0:T(8,128)S(1)} %maximum_select_fusion.3), channel_id=1, source_target_pairs={{0,2},{2,0},{4,6},{6,4},{8,10},{10,8},{12,14},{14,12},{16,18},{18,... | collective-permute-start | bytes 2949128 | tf_op jit(solution)/shard_map/ppermute | solution.py:434
  185.2 2.3 %collective-permute-start.39 = (f32[2,64,1280]{2,1,0:T(8,128)S(1)}, f32[2,64,1280]{2,1,0:T(8,128)}, u32[]{:S(2)}, u32[]{:S(2)}) collective-permute-start(f32[2,64,1280]{2,1,0:T(8,128)S(1)} %maximum_select_fusion.4), channel_id=1, source_target_pairs={{0,2},{2,0},{4,6},{6,4},{8,10},{10,8},{12,14},{14,12},{16,18},{18,... | collective-permute-start | bytes 1966088 | tf_op jit(solution)/shard_map/ppermute | solution.py:434
  190.2 1.7 copy-start.15
  (8 other events, 6.6 us)

commit v6 on v5

--- a/solution.py
+++ b/solution.py
@@ -14,7 +14,7 @@
 STEPS = 1
 SUB = 8
 LANE = 128
-VMEM_LIMIT = 24 * 1024 * 1024
+VMEM_LIMIT = 60 * 1024 * 1024
 KERNEL_WORK = 8
 
 
@@ -141,51 +141,86 @@
 
 
 class Window:
-    def __init__(self, index, count, start, width, nlat):
+    def __init__(self, index, count):
         self.first = index == 0
         self.last = index == count - 1
-        self.width = width
-        self.extended = width + 2 * SUB
-        low = 0 if self.first else start + SUB
-        high = nlat if self.last else start + width + SUB
-        self.rows = high - low
-        self.row_at = (nlat - high, low)
-        base_up, base_down = start - SUB, nlat - start - width - SUB
-        self.place = (nlat - high - base_down, low - base_up)
-        self.side = "other" if 2 * (start + width) <= nlat else "own" if 2 * start >= nlat else "both"
-
-
-def plan(nlat, widths):
-    starts = np.cumsum([0] + widths[:-1])
-    return [Window(k, len(widths), int(starts[k]), widths[k], nlat) for k in range(len(widths))]
+        self.index = index
+        self.width = LANE
+        self.extended = LANE + 2 * SUB
+        self.main = LANE if self.first else LANE - SUB
+        self.rim = 0 if self.last else SUB
+        self.rows = self.main + self.rim
+        up = SUB if self.first else 2 * SUB
+        self.place = (self.extended - up - self.rows, up)
+        self.side = "other" if 2 * (index + 1) <= count else "own" if 2 * index >= count else "both"
 
 
 def choose(band, pair):
     return jnp.where(band == 0, pair[0], pair[1])
 
 
-def transpose_kernel(place, spec_ref, out_ref):
+def multiple(value, of):
+    return pl.multiple_of(value.astype(jnp.int32), of)
+
+
+def pieces_kernel(windows, slots, count, level_ref, spec_ref, *refs):
+    out_refs, (taken, turned, in_sems, out_sems) = refs[: len(windows)], refs[len(windows) :]
+    level = level_ref[0]
     runs = by_parity(spec_ref.shape[2] // 2)
-    out_ref[0] = jnp.concatenate([spec_ref[0, 0, pl.ds(start, count, step), :] for start, count, step in runs]).T
-
-
-def rows_first(spec, level, block, width):
+
+    def arrival(c, n):
+        tile = choose(level, (count - 1 - slots[n], slots[n]))
+        lanes = pl.ds(multiple(tile * LANE, LANE), LANE)
+        return pltpu.make_async_copy(spec_ref.at[level, c, :, lanes], taken.at[c, n], in_sems.at[c, n])
+
+    def departures(c, k):
+        window, n = windows[k], slots.index(windows[k].index)
+        rows = pl.ds(multiple(choose(level, (0, LANE - window.main)), SUB), window.main)
+        at = pl.ds(multiple(choose(level, (window.rim, 0)), SUB), window.main)
+        yield pltpu.make_async_copy(turned.at[c, n, rows], out_refs[k].at[c, at], out_sems.at[k, c, 0])
+        if window.rim:
+            rows = pl.ds(multiple(choose(level, (LANE - SUB, 0)), SUB), SUB)
+            at = pl.ds(multiple(choose(level, (0, window.main)), SUB), SUB)
+            yield pltpu.make_async_copy(turned.at[c, n + 1, rows], out_refs[k].at[c, at], out_sems.at[k, c, 1])
+
+    for n in range(len(slots)):
+        for c in range(2):
+            arrival(c, n).start()
+    for n in range(len(slots)):
+        for c in range(2):
+            arrival(c, n).wait()
+            turned[c, n] = jnp.concatenate([taken[c, n, pl.ds(start, rows, step), :] for start, rows, step in runs]).T
+        for k, window in enumerate(windows):
+            if slots[n] == window.index + (1 if window.rim else 0):
+                for c in range(2):
+                    for copy in departures(c, k):
+                        copy.start()
+    for k in range(len(windows)):
+        for c in range(2):
+            for copy in departures(c, k):
+                copy.wait()
+
+
+def pieces_of(spec, level, windows, count):
     depth = spec.shape[2]
+    slots = sorted({w.index for w in windows} | {w.index + 1 for w in windows if w.rim})
     return pl.pallas_call(
-        transpose_kernel,
-        grid_spec=pltpu.PrefetchScalarGridSpec(
-            num_scalar_prefetch=1,
-            grid=(2, width // LANE),
-            in_specs=[pl.BlockSpec((1, 1, depth, LANE), lambda c, t, place: (place[0], c, 0, place[1] + t))],
-            out_specs=pl.BlockSpec((1, LANE, depth), lambda c, t, place: (c, t, 0)),
+        functools.partial(pieces_kernel, windows, slots, count),
+        in_specs=[pl.BlockSpec(memory_space=pltpu.SMEM), pl.BlockSpec(memory_space=pl.ANY)],
+        out_specs=[pl.BlockSpec(memory_space=pl.ANY)] * len(windows),
+        out_shape=[jax.ShapeDtypeStruct((2, w.rows, depth), jnp.float32) for w in windows],
+        scratch_shapes=[
+            pltpu.VMEM((2, len(slots), depth, LANE), jnp.float32),
+            pltpu.VMEM((2, len(slots), LANE, depth), jnp.float32),
+            pltpu.SemaphoreType.DMA((2, len(slots))),
+            pltpu.SemaphoreType.DMA((len(windows), 2, 2)),
+        ],
+        compiler_params=pltpu.CompilerParams(vmem_limit_bytes=VMEM_LIMIT),
+        cost_estimate=pl.CostEstimate(
+            flops=0, transcendentals=0, bytes_accessed=4 * 2 * len(slots) * LANE * depth * 4
         ),
-        out_shape=jax.ShapeDtypeStruct((2, width, depth), jnp.float32),
-        compiler_params=pltpu.CompilerParams(vmem_limit_bytes=2 * VMEM_LIMIT),
-        cost_estimate=pl.CostEstimate(
-            flops=0, transcendentals=0, bytes_accessed=8 * 2 * width * depth * 4
-        ),
-        name="rows_first",
-    )(jnp.stack([level, jnp.asarray(block, jnp.int32)]), spec)
+        name="pieces_of",
+    )(level.reshape(1), spec)
 
 
 def gate_kernel(*refs):
@@ -222,22 +257,19 @@
     carry_ref = None if window.first else refs.pop(0)
     out_refs = [refs.pop(0) for _ in range(4)]
     carried_ref = None if window.last else refs.pop(0)
-    table, local_buf, lhs_high, lhs_low, wind, second, third, shift, sems = refs
+    table, lhs_high, lhs_low, wind, second, third, shift, results, carried, table_sem, out_sems = refs
     band, core, side = place_ref[0], place_ref[1], place_ref[2]
     rows, extended = window.rows, window.extended
 
     def at(pair):
-        return pl.multiple_of(choose(band, pair).astype(jnp.int32), SUB)
-
-    fetch = pltpu.make_async_copy(local_ref.at[:, pl.ds(at(window.row_at), rows)], local_buf, sems.at[0])
-    fetch.start()
-    tables = pltpu.make_async_copy(table_ref, table, sems.at[1])
+        return multiple(choose(band, pair), SUB)
+
+    tables = pltpu.make_async_copy(table_ref, table, table_sem)
     tables.start()
-    fetch.wait()
     lane = lax.broadcasted_iota(jnp.int32, (rows, LANE), 1)
     even, odd = [], []
     for c in range(2):
-        mine, theirs = local_buf[c], remote_ref[c]
+        mine, theirs = local_ref[c], remote_ref[c]
         low, high = jnp.where(band == 0, mine, theirs), jnp.where(band == 0, theirs, mine)
         low_rest, high_rest = low[:, 4 * LANE :], high[:, 4 * LANE :]
         turn = functools.partial(pltpu.roll, shift=LANE // 2, axis=1)
@@ -279,7 +311,9 @@
 
     if not window.last:
         for c in range(2):
-            carried_ref[c] = wind[c, pl.ds(at((0, extended - 2 * SUB)), 2 * SUB), :]
+            carried[c] = wind[c, pl.ds(at((0, extended - 2 * SUB)), 2 * SUB), :]
+        carry_on = pltpu.make_async_copy(carried, carried_ref, out_sems.at[4])
+        carry_on.start()
 
     blocks = extended // SUB
 
@@ -316,17 +350,24 @@
 
     quarter = window.width // 4 // SUB
 
-    def entries(out_ref, base):
+    def entries(out, base):
         @pl.loop(0, quarter, unroll=4)
         def _(block):
             (e0, n0), (e1, n1) = derivatives(shift, base + block + 1)
             g_xx, g_xy, g_yx, g_yy = 1.0 + 0.5 * e0, 0.5 * n0, 0.5 * e1, 1.0 + 0.5 * n1
-            out_ref[0, rows_of(block), :] = g_xx * g_xx + g_yx * g_yx
-            out_ref[1, rows_of(block), :] = g_xx * g_xy + g_yx * g_yy
-            out_ref[2, rows_of(block), :] = g_xy * g_xy + g_yy * g_yy
-
-    for out_ref, (a, b) in zip(out_refs, QUARTERS):
-        entries(out_ref, (2 * (core + a - 2 * core * a) + (side + b - 2 * side * b)) * quarter)
+            out[0, rows_of(block), :] = g_xx * g_xx + g_yx * g_yx
+            out[1, rows_of(block), :] = g_xx * g_xy + g_yx * g_yy
+            out[2, rows_of(block), :] = g_xy * g_xy + g_yy * g_yy
+
+    copies = []
+    for n, (a, b) in reversed(list(enumerate(QUARTERS))):
+        entries(results.at[n], (2 * (core + a - 2 * core * a) + (side + b - 2 * side * b)) * quarter)
+        copies.append(pltpu.make_async_copy(results.at[n], out_refs[n], out_sems.at[n]))
+        copies[-1].start()
+    for copy in copies:
+        copy.wait()
+    if not window.last:
+        carry_on.wait()
 
 
 QUARTERS = ((0, 0), (0, 1), (1, 0), (1, 1))
@@ -337,7 +378,7 @@
     vmem = pl.BlockSpec(memory_space=pltpu.VMEM)
     in_specs = [
         pl.BlockSpec(memory_space=pltpu.SMEM),
-        pl.BlockSpec(memory_space=pl.ANY),
+        vmem,
         vmem,
         pl.BlockSpec(memory_space=pl.ANY),
     ]
@@ -355,19 +396,21 @@
         functools.partial(window_kernel, window, depth, len(waits)),
         out_shape=out_shape,
         in_specs=in_specs,
-        out_specs=[vmem] * len(out_shape),
+        out_specs=[pl.BlockSpec(memory_space=pl.ANY)] * len(out_shape),
         scratch_shapes=[
             pltpu.VMEM(table.shape, table.dtype),
-            pltpu.VMEM((2, window.rows, depth), jnp.float32),
             pltpu.VMEM(lhs_shape, jnp.bfloat16),
             pltpu.VMEM(lhs_shape, jnp.bfloat16),
             field,
             field,
             field,
             field,
-            pltpu.SemaphoreType.DMA((2,)),
+            pltpu.VMEM((4, 3, window.width // 4, NLON), jnp.float32),
+            pltpu.VMEM((2, 2 * SUB, NLON), jnp.float32),
+            pltpu.SemaphoreType.DMA,
+            pltpu.SemaphoreType.DMA((5,)),
         ],
-        compiler_params=pltpu.CompilerParams(vmem_limit_bytes=2 * VMEM_LIMIT),
+        compiler_params=pltpu.CompilerParams(vmem_limit_bytes=VMEM_LIMIT),
         cost_estimate=pl.CostEstimate(
             flops=KERNEL_WORK * 3 * 2 * 2 * window.rows * depth * NLON,
             transcendentals=0,
@@ -382,26 +425,64 @@
     return [(member, member ^ bit) for member in range(members)]
 
 
+def put_kernel(count, place_ref, *refs):
+    parts, out_ref, sem = refs[:4], refs[-2], refs[-1]
+    core, side, along = place_ref[0], place_ref[1], place_ref[2]
+    around = parts[0].shape[1]
+    copies = []
+    for a, part in enumerate(parts):
+        half = core if a < 2 else 1 - core
+        quarter = side if a % 2 == 0 else 1 - side
+        for w in range(count):
+            level, row = place_ref[3 + 4 * w + half], place_ref[5 + 4 * w + half]
+            for n in range(around):
+                piece = lax.rem(along + 1 + n, around)
+                at = multiple(row + (quarter * around + piece) * SUB, SUB)
+                copies.append(pltpu.make_async_copy(part.at[w, n], out_ref.at[level, pl.ds(at, SUB)], sem.at[a, w, n]))
+                copies[-1].start()
+    for copy in copies:
+        copy.wait()
+
+
+def put(out, shape, places, parts):
+    count = parts[0].shape[0]
+    extra = [] if out is None else [out]
+    return pl.pallas_call(
+        functools.partial(put_kernel, count),
+        in_specs=[pl.BlockSpec(memory_space=pltpu.SMEM)]
+        + [pl.BlockSpec(memory_space=pltpu.VMEM)] * 4
+        + [pl.BlockSpec(memory_space=pl.ANY)] * len(extra),
+        out_specs=pl.BlockSpec(memory_space=pl.ANY),
+        out_shape=jax.ShapeDtypeStruct(shape, jnp.float32),
+        input_output_aliases={5: 0} if extra else {},
+        scratch_shapes=[pltpu.SemaphoreType.DMA((4, count, parts[0].shape[1]))],
+        compiler_params=pltpu.CompilerParams(vmem_limit_bytes=VMEM_LIMIT),
+        cost_estimate=pl.CostEstimate(flops=0, transcendentals=0, bytes_accessed=8 * 4 * parts[0].size),
+        name="put",
+    )(places.astype(jnp.int32), *parts, *extra)
+
+
+def pairs(members, bit):
+    return [(member, member ^ bit) for member in range(members)]
+
+
 def by_levels(coeffs):
     spec = coeffs[0]
     levels, _, parts, waves_local, nlat = spec.shape
     members = lax.axis_size("mem")
     band = lax.axis_index("band").astype(jnp.int32)
     member = lax.axis_index("mem").astype(jnp.int32)
-    place = jnp.stack([band, member % 2, member // 2 % 2])
+    core, side, along = member % 2, member // 2 % 2, member // 4
+    place = jnp.stack([band, core, side])
     spec = spec.reshape(levels, 2, parts * waves_local, nlat)
-    windows = plan(nlat, [LANE] * (nlat // LANE))
+    count = nlat // LANE
+    windows = [Window(k, count) for k in range(count)]
     table = jnp.asarray(wave_table(levels, waves_local))
     swap = [(0, 1), (1, 0)]
 
-    lead = windows[0].rows
-    outgoing = rows_first(spec, 1 - band, choose(1 - band, (nlat // LANE - 2, 0)), 2 * LANE)
-    piece = lax.dynamic_slice_in_dim(outgoing, choose(1 - band, (2 * LANE - lead, 0)), lead, axis=1)
+    (piece,) = pieces_of(spec, 1 - band, windows[:1], count)
     remotes = [lax.ppermute(piece, "band", swap)]
-    outgoing = rows_first(spec, 1 - band, 0, nlat)
-    outgoing = [
-        lax.dynamic_slice_in_dim(outgoing, choose(1 - band, window.row_at), window.rows, axis=1) for window in windows
-    ]
+    outgoing = [None, *pieces_of(spec, 1 - band, windows[1:], count)]
 
     def fetch_rows(k, waits):
         piece = gated(outgoing[k], waits) if waits else outgoing[k]
@@ -409,55 +490,43 @@
         return piece
 
     fetch_rows(1, [])
-    local = rows_first(spec, band, 0, nlat)
-
-    bits = [1 << n for n in range(members.bit_length() - 1)]
-
-    def halved(parts_of, bit):
-        half = parts_of[0].shape[1] // 2
-        mine = (member // bit) % 2
-
-        def total(which):
-            return sum(lax.dynamic_slice_in_dim(part, which * half, half, axis=1) for part in parts_of[:2])
-
-        leaves = total(1 - mine)
-        return [total(mine), lax.ppermute(leaves, "mem", pairs(members, bit)), leaves]
-
-    def advanced(parts_of, bit):
-        if len(parts_of) == 3:
-            return halved(parts_of, bit)
-        keep, leaves, keep_more, leaves_more = parts_of
-        leaves = leaves + leaves_more
-        return [keep + keep_more, lax.ppermute(leaves, "mem", pairs(members, bit)), leaves]
-
-    def doubled(part, bit):
-        beside = lax.ppermute(part, "mem", pairs(members, bit))
-        mine = (member // bit) % 2
-        return jnp.where(mine == 0, jnp.concatenate([part, beside], axis=1), jnp.concatenate([beside, part], axis=1))
-
-    def gathered(part):
-        for bit in reversed(bits):
-            part = doubled(part, bit)
-        return part
+    local = pieces_of(spec, band, windows, count)
+
+    around = members // 4
+    shifts = [[(m, (m + 4 * d) % members) for m in range(members)] for d in range(around)]
+
+    def across(kept, passed, kept_more, passed_more):
+        leaves = passed + passed_more
+        return [kept, kept_more, lax.ppermute(leaves, "mem", pairs(members, 2))], leaves
+
+    def onward(*parts_of):
+        rows = parts_of[0].shape[1] // around
+
+        def total(d):
+            first = (along + d) % around * rows
+            return sum(lax.dynamic_slice_in_dim(part, first, rows, axis=1) for part in parts_of)
+
+        leaves = [total(d) for d in range(1, around)]
+        return [total(0), *(lax.ppermute(leaves[d - 1], "mem", shifts[d]) for d in range(1, around))], leaves[0]
 
     carry = None
-    sums = []
+    sums, steps = [], [across, onward]
     for k, window in enumerate(windows):
         waits = []
-        if k + 2 < len(windows):
+        if k + 2 < count:
             waits.append(fetch_rows(k + 2, [remotes[k]] if carry is None else [remotes[k], carry]))
-        for j in range(k - 1):
-            sums[j] = advanced(sums[j], bits[k - 1 - j])
-            waits.append(sums[j][-1])
-        quarters, carry = window_tensor(window, place, local, remotes[k], table, waits, carry)
-        first = lax.ppermute(quarters[3], "mem", pairs(members, bits[0]))
-        second = lax.ppermute(quarters[2], "mem", pairs(members, bits[0]))
+        for j in range(max(0, k - len(steps)), k):
+            sums[j], left = steps[k - 1 - j](*sums[j])
+            waits.append(left)
+        quarters, carry = window_tensor(window, place, local[k], remotes[k], table, waits, carry)
+        first = lax.ppermute(quarters[3], "mem", pairs(members, 1))
+        second = lax.ppermute(quarters[2], "mem", pairs(members, 1))
         sums.append([quarters[0], quarters[1], second, first])
     pieces = {"own": [], "both": [], "other": []}
     for k, window in enumerate(windows):
-        for bit in bits[max(len(windows) - 1 - k, 1) :]:
-            sums[k] = advanced(sums[k], bit)
-        pieces[window.side].append(exponent_of(sums[k][0] + sums[k][1], members))
+        for step in steps[min(count - 1 - k, len(steps)) :]:
+            sums[k], _ = step(*sums[k])
+        pieces[window.side].append(exponent_of(sum(sums[k]), members))
 
     other = lax.ppermute(jnp.stack(pieces["other"]), "band", swap)
     trades = []
@@ -467,28 +536,38 @@
             trades.append((m * 2 + b, mate[0] * 2 + mate[1]))
     both = lax.ppermute(pieces["both"][0], ("mem", "band"), trades)
 
-    early = gathered(jnp.concatenate([other, both[None]]))
-    other, both = early[:-1], early[-1]
-    middle = both.shape[0] // 2
-    low, high = both[:middle], both[middle:]
-    rest = jnp.zeros((nlat // 2 - middle, NLON), jnp.float32)
-    down = jnp.stack([jnp.concatenate([rest, low]), jnp.concatenate([*other, high])])
-    up = jnp.stack([jnp.concatenate([low, *other[::-1]]), jnp.concatenate([high, rest])])
-    out = jnp.where(band == 0, down, up)
-
-    own = gathered(jnp.stack(pieces["own"]))
-    for k, block in enumerate(own):
-        width = block.shape[0]
-        row = choose(band, (nlat // 2 - middle - (k + 1) * width, middle + k * width))
-        out = lax.dynamic_update_slice(out, block[None], (band, row.astype(jnp.int32), jnp.int32(0)))
-    return out
+    def gathered(stack):
+        line = [lax.ppermute(stack, "mem", shifts[d]) for d in range(around - 1, 0, -1)] + [stack]
+        mine = jnp.stack(line, axis=1)
+        beside = lax.ppermute(mine, "mem", pairs(members, 2))
+        return [mine, beside, *(lax.ppermute(part, "mem", pairs(members, 1)) for part in (mine, beside))]
+
+    def places(rows):
+        return jnp.stack([core, side, along] + [jnp.asarray(value, jnp.int32) for pair in rows for value in pair])
+
+    height = nlat // 2
+    half, far = LANE // 2, 1 - band
+    early = []
+    for k in range(len(pieces["other"])):
+        row = choose(band, (k * LANE, height - (k + 1) * LANE))
+        early.append((far, far, row, row + half))
+    row = choose(band, (height - half, 0))
+    early.append((0, 1, row, row))
+    late = []
+    for k in range(len(pieces["own"])):
+        row = choose(band, (height - half - (k + 1) * LANE, half + k * LANE))
+        late.append((band, band, row, row + half))
+    shape = (levels, height, NLON)
+    out = put(None, shape, places(early), gathered(jnp.concatenate([other, both[None]])))
+    return put(out, shape, places(late), gathered(jnp.stack(pieces["own"])))
 
 
 def per_device(coeffs):
     _, levels, _, _, _, nlat = coeffs.shape
     members = lax.axis_size("mem")
     rows = nlat // lax.axis_size("band")
-    if coeffs.shape[4] == 5 * LANE // 2 and levels == lax.axis_size("band") == 2 and members == 16 and nlat % (2 * LANE) == LANE and rows > LANE:
+    fits = coeffs.shape[4] == 5 * LANE // 2 and nlat % (2 * LANE) == LANE and rows > LANE
+    if fits and levels == lax.axis_size("band") == 2 and members == 16:
         return by_levels(coeffs)
     return by_rows(coeffs)
 

time: 194 us -> 212 us (1.093)
  starting transfers between devices: 35.6 us -> 59.9 us
  local copies, waits for them, and re-layouts: 16.4 us -> 8.5 us
  waiting for transfers between devices: 64.8 us -> 60.9 us
  Pallas kernels: 63.6 us -> 67.1 us
    ppermute x33 -> x42, starting transfers between devices: 26.2 us -> 50 us  [the longest x15 30.5 us: onward(): lax.ppermute(leaves[d - 1], 'mem', shifts[d])]
    ppermute x33 -> x42, waiting for transfers between devices: 64.5 us -> 52.5 us  [the longest x5 26.6 us: across(): lax.ppermute(leaves, 'mem', pairs(members, 2))]
    unnamed x32 -> x40, local copies, waits for them, and re-layouts: 12.2 us -> 3.98 us
    ppermute x1, waiting for transfers between devices: 0.32 us -> 8.37 us  [by_levels(): remotes = [lax.ppermute(piece, 'band', swap)]]
    pallas_call x5, Pallas kernels: 47.4 us -> 51.2 us  [window_tensor(): pl.pallas_call(functools.partial(window_kernel, window, depth, len(waits)...]
    dynamic_slice x3 -> x0, local copies, waits for them, and re-layouts: 3.12 us -> none  [the longest x2 2.21 us: by_levels(): lax.dynamic_slice_in_dim(outgoing, choose(1 - band, window.row_at), windo...]
    ppermute x0 -> x3, local copies, waits for them, and re-layouts: none -> 2.47 us  [the longest x2 1.65 us: gathered(): lax.ppermute(part, 'mem', pairs(members, 1))]
    select_n x9 -> x0, other arithmetic: 2.19 us -> none  [the longest x8 1.8 us: doubled(): jnp.where(mine == 0, jnp.concatenate([part, beside], axis=1), jnp.concate...]
  transfers between devices with their start and end apart: 40 -> 49, of which waited for: 17 -> 15; matrix products, arithmetic and copies ran while one was open for 7% -> 9% of each run, Pallas kernels for 31% -> 29%
where the time goes in v6:
time: 212 us; the launch traced here: 211 us
  Pallas kernels  67.1 us (32%)
  waiting for transfers between devices  60.9 us (29%)
  starting transfers between devices  59.9 us (28%)
  other arithmetic  13.7 us (6%)
  local copies, waits for them, and re-layouts  8.5 us (4%)
    pallas_call x5, Pallas kernels, window_tensor(): pl.pallas_call(functools.partial(window_kernel, window, depth, len(waits)...  51.2 us
    ppermute x15, starting transfers between devices, onward(): lax.ppermute(leaves[d - 1], 'mem', shifts[d])  30.5 us
    ppermute x5, waiting for transfers between devices, across(): lax.ppermute(leaves, 'mem', pairs(members, 2))  26.6 us
    ppermute x15, waiting for transfers between devices, onward(): lax.ppermute(leaves[d - 1], 'mem', shifts[d])  11.4 us
    pallas_call x3, Pallas kernels, pieces_of(): pl.pallas_call(functools.partial(pieces_kernel, windows, slots, count), i...  10.2 us
    ppermute x6, waiting for transfers between devices, gathered(): lax.ppermute(stack, 'mem', shifts[d])  9.33 us
    ppermute x1, waiting for transfers between devices, by_levels(): remotes = [lax.ppermute(piece, 'band', swap)]  8.37 us
    add x5, other arithmetic, across(): leaves = passed + passed_more  7.87 us
  transfers between devices with their start and end apart: 49, of which 15 were waited for; matrix products, arithmetic and copies ran while one was open for 9% of the time, Pallas kernels for 29%

profile of v6, /device:TPU:0, one launch (start us, length us, event | category | flops | bytes accessed | tf_op | source)
XLA Modules:
  0.0 210.7 jit_solution(9594705586893431374)
XLA Ops:
  0.0 2.6 %pieces_of.5 = f32[2,136,640]{2,1,0:T(8,128)} custom-call(s32[1]{0:T(128)} %bitcast.9.level_ref, f32[2,2,640,640]{3,2,1,0:T(8,128)} %bitcast.30), custom_call_target="tpu_custom_call" | custom-call | bytes 5242880 | tf_op jit(solution)/shard_map/pieces_of/pallas_call | solution.py:207
  2.6 3.0 %collective-permute-start.1 = (f32[2,136,640]{2,1,0:T(8,128)}, f32[2,136,640]{2,1,0:T(8,128)S(1)}, u32[]{:S(2)}, u32[]{:S(2)}) collective-permute-start(f32[2,136,640]{2,1,0:T(8,128)} %pieces_of.5), channel_id=1, source_target_pairs={{0,1},{1,0},{2,3},{3,2},{4,5},{5,4},{6,7},{7,6},{8,9},{9,8},{10,11... | collective-permute-start | bytes 2088968 | tf_op jit(solution)/shard_map/ppermute | solution.py:484
  5.6 3.6 %pieces_of.4 = (f32[2,128,640]{2,1,0:T(8,128)}, f32[2,128,640]{2,1,0:T(8,128)}, f32[2,128,640]{2,1,0:T(8,128)}, f32[2,120,640]{2,1,0:T(8,128)}) custom-call(s32[1]{0:T(128)} %bitcast.9.level_ref, f32[2,2,640,640]{3,2,1,0:T(8,128)} %bitcast.31), custom_call_target="tpu_custom_call" | custom-call | bytes 10485760 | tf_op jit(solution)/shard_map/pieces_of/pallas_call | solution.py:207
  9.3 4.0 %pieces_of.3 = (f32[2,136,640]{2,1,0:T(8,128)}, f32[2,128,640]{2,1,0:T(8,128)}, f32[2,128,640]{2,1,0:T(8,128)}, f32[2,128,640]{2,1,0:T(8,128)}, f32[2,120,640]{2,1,0:T(8,128)}) custom-call(s32[1]{0:T(128)} %bitcast.3.level_ref, f32[2,2,640,640]{3,2,1,0:T(8,128)} %bitcast.32), custom_call_target="tpu_custom_call" | custom-call | bytes 13107200 | tf_op jit(solution)/shard_map/pieces_of/pallas_call | solution.py:207
  13.9 8.4 %collective-permute-done.1.refs_1_.refs_2_ = f32[2,136,640]{2,1,0:T(8,128)S(1)} collective-permute-done((f32[2,136,640]{2,1,0:T(8,128)}, f32[2,136,640]{2,1,0:T(8,128)S(1)}, u32[]{:S(2)}, u32[]{:S(2)}) %collective-permute-start.1) | collective-permute-done | bytes 696352 | tf_op jit(solution)/shard_map/ppermute | solution.py:484
  23.1 10.4 %window_tensor.5 = (f32[3,32,1280]{2,1,0:T(8,128)}, f32[3,32,1280]{2,1,0:T(8,128)}, f32[3,32,1280]{2,1,0:T(8,128)}, f32[3,32,1280]{2,1,0:T(8,128)}, f32[2,16,1280]{2,1,0:T(8,128)}) custom-call(s32[3]{0:T(128)} %pad_add_fusion.refs_0_, f32[2,136,640]{2,1,0:T(8,128)} %get-tuple-element.41.refs_1_, f32[2,136,640]{2,1,0:T(8,128)} %copy-done.1, ...), custom_call_target="tpu_custom_call" | custom-call | flops 10695475200 | bytes 6635520 | tf_op jit(solution)/shard_map/window_tensor/pallas_call | solution.py:395
  33.6 2.1 %collective-permute-start.7 = (f32[2,128,640]{2,1,0:T(8,128)S(1)}, f32[2,128,640]{2,1,0:T(8,128)S(1)}, u32[]{:S(2)}, u32[]{:S(2)}) collective-permute-start(f32[2,128,640]{2,1,0:T(8,128)S(1)} %copy-done.5), channel_id=1, source_target_pairs={{0,1},{1,0},{2,3},{3,2},{4,5},{5,4},{6,7},{7,6},{8,9},{9,8},{10,11... | collective-permute-start | bytes 1966088 | tf_op jit(solution)/shard_map/ppermute | solution.py:489
  36.7 1.9 add.398.refs_5_
  38.6 1.5 collective-permute-start.9
  40.1 10.3 %window_tensor.6 = (f32[3,32,1280]{2,1,0:T(8,128)}, f32[3,32,1280]{2,1,0:T(8,128)}, f32[3,32,1280]{2,1,0:T(8,128)}, f32[3,32,1280]{2,1,0:T(8,128)}, f32[2,16,1280]{2,1,0:T(8,128)}) custom-call(s32[3]{0:T(128)} %pad_add_fusion.refs_0_, f32[2,128,640]{2,1,0:T(8,128)} %get-tuple-element.44.refs_1_, f32[2,128,640]{2,1,0:T(8,128)} %copy-done.3, ...), custom_call_target="tpu_custom_call" | custom-call | flops 10066329600 | bytes 6553600 | tf_op jit(solution)/shard_map/window_tensor/pallas_call | solution.py:395
  50.6 1.4 collective-permute-start.2
  53.7 1.6 collective-permute-start.32
  55.3 2.6 %collective-permute-start.33 = (f32[3,8,1280]{2,1,0:T(8,128)}, f32[3,8,1280]{2,1,0:T(8,128)S(1)}, u32[]{:S(2)}, u32[]{:S(2)}) collective-permute-start(f32[3,8,1280]{2,1,0:T(8,128)} %get-tuple-element.71), channel_id=1, source_target_pairs={{0,16},{2,18},{4,20},{6,22},{8,24},{10,26},{12,28},{14,30},{16,0},... | collective-permute-start | bytes 368648 | tf_op jit(solution)/shard_map/ppermute | solution.py:510
  57.9 1.3 collective-permute-start.34
  59.2 1.9 add.403.refs_6_
  61.1 10.2 %window_tensor.7 = (f32[3,32,1280]{2,1,0:T(8,128)}, f32[3,32,1280]{2,1,0:T(8,128)}, f32[3,32,1280]{2,1,0:T(8,128)}, f32[3,32,1280]{2,1,0:T(8,128)}, f32[2,16,1280]{2,1,0:T(8,128)}) custom-call(s32[3]{0:T(128)} %pad_add_fusion.refs_0_, f32[2,128,640]{2,1,0:T(8,128)} %get-tuple-element.51.refs_1_, f32[2,128,640]{2,1,0:T(8,128)} %copy-done.2, ...), custom_call_target="tpu_custom_call" | custom-call | flops 10066329600 | bytes 6553600 | tf_op jit(solution)/shard_map/window_tensor/pallas_call | solution.py:395
  72.2 1.5 collective-permute-start.6
  75.3 9.0 %collective-permute-done.6 = f32[3,32,1280]{2,1,0:T(8,128)S(1)} collective-permute-done((f32[3,32,1280]{2,1,0:T(8,128)}, f32[3,32,1280]{2,1,0:T(8,128)S(1)}, u32[]{:S(2)}, u32[]{:S(2)}) %collective-permute-start.6) | collective-permute-done | bytes 491552 | tf_op jit(solution)/shard_map/ppermute | solution.py:500
  84.4 1.7 dynamic-slice_add_fusion.3
  87.2 1.9 add.407.refs_5_
  89.0 2.8 %collective-permute-start.37 = (f32[3,8,1280]{2,1,0:T(8,128)S(1)}, f32[3,8,1280]{2,1,0:T(8,128)}, u32[]{:S(2)}, u32[]{:S(2)}) collective-permute-start(f32[3,8,1280]{2,1,0:T(8,128)S(1)} %get-tuple-element.75), channel_id=1, source_target_pairs={{0,24},{2,26},{4,28},{6,30},{8,0},{10,2},{12,4},{14,6},{16,8},{18,... | collective-permute-start | bytes 368648 | tf_op jit(solution)/shard_map/ppermute | solution.py:510
  91.9 10.2 %window_tensor.8 = (f32[3,32,1280]{2,1,0:T(8,128)}, f32[3,32,1280]{2,1,0:T(8,128)}, f32[3,32,1280]{2,1,0:T(8,128)}, f32[3,32,1280]{2,1,0:T(8,128)}, f32[2,16,1280]{2,1,0:T(8,128)}) custom-call(s32[3]{0:T(128)} %pad_add_fusion.refs_0_, f32[2,128,640]{2,1,0:T(8,128)} %get-tuple-element.38.refs_1_, f32[2,128,640]{2,1,0:T(8,128)} %collective-permute-done.2.refs_2_, ...), custom_call_target="tpu_custom_call" | custom-call | flops 10066329600 | bytes 6553600 | tf_op jit(solution)/shard_map/window_tensor/pallas_call | solution.py:395
  102.1 1.3 collective-permute-start.19
  104.5 8.2 %collective-permute-done.19 = f32[3,32,1280]{2,1,0:T(8,128)S(1)} collective-permute-done((f32[3,32,1280]{2,1,0:T(8,128)S(1)}, f32[3,32,1280]{2,1,0:T(8,128)S(1)}, u32[]{:S(2)}, u32[]{:S(2)}) %collective-permute-start.19) | collective-permute-done | bytes 491552 | tf_op jit(solution)/shard_map/ppermute | solution.py:500
  113.4 1.2 collective-permute-start.40
  114.7 2.8 %collective-permute-start.41 = (f32[3,8,1280]{2,1,0:T(8,128)S(1)}, f32[3,8,1280]{2,1,0:T(8,128)S(1)}, u32[]{:S(2)}, u32[]{:S(2)}) collective-permute-start(f32[3,8,1280]{2,1,0:T(8,128)S(1)} %get-tuple-element.78), channel_id=1, source_target_pairs={{0,24},{2,26},{4,28},{6,30},{8,0},{10,2},{12,4},{14,6},{16,8},{18,... | collective-permute-start | bytes 368648 | tf_op jit(solution)/shard_map/ppermute | solution.py:510
  119.7 1.5 collective-permute-start.38
  121.2 1.2 collective-permute-done.40
  124.2 10.1 %window_tensor.9 = (f32[3,32,1280]{2,1,0:T(8,128)}, f32[3,32,1280]{2,1,0:T(8,128)}, f32[3,32,1280]{2,1,0:T(8,128)}, f32[3,32,1280]{2,1,0:T(8,128)}) custom-call(s32[3]{0:T(128)} %pad_add_fusion.refs_0_, f32[2,120,640]{2,1,0:T(8,128)} %get-tuple-element.63.refs_1_, f32[2,120,640]{2,1,0:T(8,128)} %collective-permute-done.17.refs_2_, ...), custom_call_target="tpu_custom_call" | custom-call | flops 9437184000 | bytes 6471680 | tf_op jit(solution)/shard_map/window_tensor/pallas_call | solution.py:395
  134.3 2.3 %collective-permute-start.21 = (f32[3,32,1280]{2,1,0:T(8,128)}, f32[3,32,1280]{2,1,0:T(8,128)S(1)}, u32[]{:S(2)}, u32[]{:S(2)}) collective-permute-start(f32[3,32,1280]{2,1,0:T(8,128)} %get-tuple-element.70), channel_id=1, source_target_pairs={{0,2},{2,0},{4,6},{6,4},{8,10},{10,8},{12,14},{14,12},{16,18},{18,... | collective-permute-start | bytes 1474568 | tf_op jit(solution)/shard_map/ppermute | solution.py:522
  136.7 2.6 %collective-permute-start.43 = (f32[3,8,1280]{2,1,0:T(8,128)S(1)}, f32[3,8,1280]{2,1,0:T(8,128)S(1)}, u32[]{:S(2)}, u32[]{:S(2)}) collective-permute-start(f32[3,8,1280]{2,1,0:T(8,128)S(1)} %get-tuple-element.86), channel_id=1, source_target_pairs={{0,24},{2,26},{4,28},{6,30},{8,0},{10,2},{12,4},{14,6},{16,8},{18,... | collective-permute-start | bytes 368648 | tf_op jit(solution)/shard_map/ppermute | solution.py:540
  140.2 2.8 %collective-permute-start.14 = (f32[3,8,1280]{2,1,0:T(8,128)S(1)}, f32[3,8,1280]{2,1,0:T(8,128)S(1)}, u32[]{:S(2)}, u32[]{:S(2)}) collective-permute-start(f32[3,8,1280]{2,1,0:T(8,128)S(1)} %get-tuple-element.80), channel_id=1, source_target_pairs={{0,8},{2,10},{4,12},{6,14},{8,16},{10,18},{12,20},{14,22},{16,24},... | collective-permute-start | bytes 368648 | tf_op jit(solution)/shard_map/ppermute | solution.py:510
  144.0 8.9 %collective-permute-start.15 = (f32[3,8,1280]{2,1,0:T(8,128)S(1)}, f32[3,8,1280]{2,1,0:T(8,128)S(1)}, u32[]{:S(2)}, u32[]{:S(2)}) collective-permute-start(f32[3,8,1280]{2,1,0:T(8,128)S(1)} %get-tuple-element.82), channel_id=1, source_target_pairs={{0,16},{2,18},{4,20},{6,22},{8,24},{10,26},{12,28},{14,30},{16,0},... | collective-permute-start | bytes 368648 | tf_op jit(solution)/shard_map/ppermute | solution.py:510
  152.9 3.1 %collective-permute-done.44 = f32[3,8,1280]{2,1,0:T(8,128)S(1)} collective-permute-done((f32[3,8,1280]{2,1,0:T(8,128)S(1)}, f32[3,8,1280]{2,1,0:T(8,128)S(1)}, u32[]{:S(2)}, u32[]{:S(2)}) %collective-permute-start.44) | collective-permute-done | bytes 122912 | tf_op jit(solution)/shard_map/ppermute | solution.py:540
  156.3 2.1 collective-permute-start.22
  158.5 1.4 collective-permute-done.15
  161.1 9.4 %collective-permute-done.22 = f32[3,32,1280]{2,1,0:T(8,128)S(1)} collective-permute-done((f32[3,32,1280]{2,1,0:T(8,128)S(1)}, f32[3,32,1280]{2,1,0:T(8,128)S(1)}, u32[]{:S(2)}, u32[]{:S(2)}) %collective-permute-start.22) | collective-permute-done | bytes 491552 | tf_op jit(solution)/shard_map/ppermute | solution.py:500
  170.6 2.1 %collective-permute-start.23 = (f32[3,8,1280]{2,1,0:T(8,128)S(1)}, f32[3,8,1280]{2,1,0:T(8,128)S(1)}, u32[]{:S(2)}, u32[]{:S(2)}) collective-permute-start(f32[3,8,1280]{2,1,0:T(8,128)S(1)} %get-tuple-element.83), channel_id=1, source_target_pairs={{0,8},{2,10},{4,12},{6,14},{8,16},{10,18},{12,20},{14,22},{16,24},... | collective-permute-start | bytes 368648 | tf_op jit(solution)/shard_map/ppermute | solution.py:510
  172.7 2.4 %collective-permute-start.25 = (f32[3,8,1280]{2,1,0:T(8,128)S(1)}, f32[3,8,1280]{2,1,0:T(8,128)S(1)}, u32[]{:S(2)}, u32[]{:S(2)}) collective-permute-start(f32[3,8,1280]{2,1,0:T(8,128)S(1)} %get-tuple-element.84), channel_id=1, source_target_pairs={{0,24},{2,26},{4,28},{6,30},{8,0},{10,2},{12,4},{14,6},{16,8},{18,... | collective-permute-start | bytes 368648 | tf_op jit(solution)/shard_map/ppermute | solution.py:510
  175.2 2.9 %collective-permute-done.23 = f32[3,8,1280]{2,1,0:T(8,128)S(1)} collective-permute-done((f32[3,8,1280]{2,1,0:T(8,128)S(1)}, f32[3,8,1280]{2,1,0:T(8,128)S(1)}, u32[]{:S(2)}, u32[]{:S(2)}) %collective-permute-start.23) | collective-permute-done | bytes 122912 | tf_op jit(solution)/shard_map/ppermute | solution.py:510
  178.1 3.7 %collective-permute-done.24 = f32[3,8,1280]{2,1,0:T(8,128)S(1)} collective-permute-done((f32[3,8,1280]{2,1,0:T(8,128)S(1)}, f32[3,8,1280]{2,1,0:T(8,128)S(1)}, u32[]{:S(2)}, u32[]{:S(2)}) %collective-permute-start.24) | collective-permute-done | bytes 122912 | tf_op jit(solution)/shard_map/ppermute | solution.py:510
  181.9 2.7 %collective-permute-start.26 = (f32[2,8,1280]{2,1,0:T(8,128)S(1)}, f32[2,8,1280]{2,1,0:T(8,128)S(1)}, u32[]{:S(2)}, u32[]{:S(2)}) collective-permute-start(f32[2,8,1280]{2,1,0:T(8,128)S(1)} %get-tuple-element.88), channel_id=1, source_target_pairs={{0,24},{2,26},{4,28},{6,30},{8,0},{10,2},{12,4},{14,6},{16,8},{18,... | collective-permute-start | bytes 245768 | tf_op jit(solution)/shard_map/ppermute | solution.py:540
  185.3 2.0 collective-permute-done.26
  187.3 3.2 %collective-permute-done.27 = f32[2,8,1280]{2,1,0:T(8,128)S(1)} collective-permute-done((f32[2,8,1280]{2,1,0:T(8,128)S(1)}, f32[2,8,1280]{2,1,0:T(8,128)S(1)}, u32[]{:S(2)}, u32[]{:S(2)}) %collective-permute-start.27) | collective-permute-done | bytes 81952 | tf_op jit(solution)/shard_map/ppermute | solution.py:540
  191.6 1.5 collective-permute-start.29
  193.6 5.1 %collective-permute-done.29.refs_1_ = f32[2,4,8,1280]{3,2,1,0:T(8,128)S(1)} collective-permute-done((f32[2,4,8,1280]{3,2,1,0:T(8,128)S(1)}, f32[2,4,8,1280]{3,2,1,0:T(8,128)S(1)}, u32[]{:S(2)}, u32[]{:S(2)}) %collective-permute-start.29) | collective-permute-done | bytes 327712 | tf_op jit(solution)/shard_map/ppermute | solution.py:542
  203.3 3.2 %put.2.refs_4_ = f32[2,320,1280]{2,1,0:T(8,128)} custom-call(s32[15]{0:T(128)} %stack.111.place_ref, f32[3,4,8,1280]{3,2,1,0:T(8,128)} %copy.10.refs_0_, f32[3,4,8,1280]{3,2,1,0:T(8,128)} %copy.11.refs_1_, f32[3,4,8,1280]{3,2,1,0:T(8,128)} %copy.12.refs_2_, f32[3,4,8,1280]{3,2,1,0:T(8,128)} %copy.13.refs_3_), custom_call_target="tpu_custom_call" | custom-call | bytes 3932160 | tf_op jit(solution)/shard_map/put/pallas_call | solution.py:450
  207.9 2.6 %put.3 = f32[2,320,1280]{2,1,0:T(8,128)} custom-call(s32[11]{0:T(128)} %stack.102.place_ref, f32[2,4,8,1280]{3,2,1,0:T(8,128)} %copy-done, f32[2,4,8,1280]{3,2,1,0:T(8,128)} %copy-done.15, f32[2,4,8,1280]{3,2,1,0:T(8,128)} %copy-done.16, f32[2,4,8,1280]{3,2,1,0:T(8,128)} %copy-done.17, f32[2,320,1280]{2,1,0:T(8,128)} %put.2.refs_4_), custom_call_target="tpu_custom_call", output_to_operand_aliasing={{}: (5, {})} | custom-call | bytes 2621440 | tf_op jit(solution)/shard_map/put/pallas_call | solution.py:450
  (135 shorter events, 25.8 us)
Async XLA Ops:
  2.6 19.7 %collective-permute-start.1 = (f32[2,136,640]{2,1,0:T(8,128)}, f32[2,136,640]{2,1,0:T(8,128)S(1)}, u32[]{:S(2)}, u32[]{:S(2)}) collective-permute-start(f32[2,136,640]{2,1,0:T(8,128)} %pieces_of.5), channel_id=1, source_target_pairs={{0,1},{1,0},{2,3},{3,2},{4,5},{5,4},{6,7},{7,6},{8,9},{9,8},{10,11... | collective-permute-start | bytes 2088968 | tf_op jit(solution)/shard_map/ppermute | solution.py:484
  9.2 26.7 %collective-permute-start = (f32[2,128,640]{2,1,0:T(8,128)}, f32[2,128,640]{2,1,0:T(8,128)S(1)}, u32[]{:S(2)}, u32[]{:S(2)}) collective-permute-start(f32[2,128,640]{2,1,0:T(8,128)} %get-tuple-element.40), channel_id=1, source_target_pairs={{0,1},{1,0},{2,3},{3,2},{4,5},{5,4},{6,7},{7,6},{8,9},{9,8},{10,11... | collective-permute-start | bytes 1966088 | tf_op jit(solution)/shard_map/ppermute | solution.py:489
  33.6 18.4 %collective-permute-start.7 = (f32[2,128,640]{2,1,0:T(8,128)S(1)}, f32[2,128,640]{2,1,0:T(8,128)S(1)}, u32[]{:S(2)}, u32[]{:S(2)}) collective-permute-start(f32[2,128,640]{2,1,0:T(8,128)S(1)} %copy-done.5), channel_id=1, source_target_pairs={{0,1},{1,0},{2,3},{3,2},{4,5},{5,4},{6,7},{7,6},{8,9},{9,8},{10,11... | collective-permute-start | bytes 1966088 | tf_op jit(solution)/shard_map/ppermute | solution.py:489
  35.7 17.1 %collective-permute-start.8 = (f32[3,32,1280]{2,1,0:T(8,128)}, f32[3,32,1280]{2,1,0:T(8,128)S(1)}, u32[]{:S(2)}, u32[]{:S(2)}) collective-permute-start(f32[3,32,1280]{2,1,0:T(8,128)} %get-tuple-element.55), channel_id=1, source_target_pairs={{0,2},{2,0},{4,6},{6,4},{8,10},{10,8},{12,14},{14,12},{16,18},{18,... | collective-permute-start | bytes 1474568 | tf_op jit(solution)/shard_map/ppermute | solution.py:523
  38.6 14.2 %collective-permute-start.9 = (f32[3,32,1280]{2,1,0:T(8,128)}, f32[3,32,1280]{2,1,0:T(8,128)S(1)}, u32[]{:S(2)}, u32[]{:S(2)}) collective-permute-start(f32[3,32,1280]{2,1,0:T(8,128)} %add.398.refs_5_), channel_id=1, source_target_pairs={{0,4},{2,6},{4,0},{6,2},{8,12},{10,14},{12,8},{14,10},{16,20},{18,... | collective-permute-start | bytes 1474568 | tf_op jit(solution)/shard_map/ppermute | solution.py:500
  50.4 7.4 %collective-permute-start.5 = (f32[3,32,1280]{2,1,0:T(8,128)}, f32[3,32,1280]{2,1,0:T(8,128)}, u32[]{:S(2)}, u32[]{:S(2)}) collective-permute-start(f32[3,32,1280]{2,1,0:T(8,128)} %get-tuple-element.50), channel_id=1, source_target_pairs={{0,2},{2,0},{4,6},{6,4},{8,10},{10,8},{12,14},{14,12},{16,18},{18,... | collective-permute-start | bytes 1474568 | tf_op jit(solution)/shard_map/ppermute | solution.py:522
  50.6 38.4 %collective-permute-start.2 = (f32[2,128,640]{2,1,0:T(8,128)S(1)}, f32[2,128,640]{2,1,0:T(8,128)}, u32[]{:S(2)}, u32[]{:S(2)}) collective-permute-start(f32[2,128,640]{2,1,0:T(8,128)S(1)} %copy-done.4), channel_id=1, source_target_pairs={{0,1},{1,0},{2,3},{3,2},{4,5},{5,4},{6,7},{7,6},{8,9},{9,8},{10,11... | collective-permute-start | bytes 1966088 | tf_op jit(solution)/shard_map/ppermute | solution.py:489
  52.0 22.8 %collective-permute-start.4 = (f32[3,32,1280]{2,1,0:T(8,128)}, f32[3,32,1280]{2,1,0:T(8,128)}, u32[]{:S(2)}, u32[]{:S(2)}) collective-permute-start(f32[3,32,1280]{2,1,0:T(8,128)} %get-tuple-element.48), channel_id=1, source_target_pairs={{0,2},{2,0},{4,6},{6,4},{8,10},{10,8},{12,14},{14,12},{16,18},{18,... | collective-permute-start | bytes 1474568 | tf_op jit(solution)/shard_map/ppermute | solution.py:523
  53.7 17.7 %collective-permute-start.32 = (f32[3,8,1280]{2,1,0:T(8,128)}, f32[3,8,1280]{2,1,0:T(8,128)S(1)}, u32[]{:S(2)}, u32[]{:S(2)}) collective-permute-start(f32[3,8,1280]{2,1,0:T(8,128)} %get-tuple-element.73.refs_5_), channel_id=1, source_target_pairs={{0,8},{2,10},{4,12},{6,14},{8,16},{10,18},{12,20},{14,22},{16,24},... | collective-permute-start | bytes 368648 | tf_op jit(solution)/shard_map/ppermute | solution.py:510
  55.3 17.0 %collective-permute-start.33 = (f32[3,8,1280]{2,1,0:T(8,128)}, f32[3,8,1280]{2,1,0:T(8,128)S(1)}, u32[]{:S(2)}, u32[]{:S(2)}) collective-permute-start(f32[3,8,1280]{2,1,0:T(8,128)} %get-tuple-element.71), channel_id=1, source_target_pairs={{0,16},{2,18},{4,20},{6,22},{8,24},{10,26},{12,28},{14,30},{16,0},... | collective-permute-start | bytes 368648 | tf_op jit(solution)/shard_map/ppermute | solution.py:510
  57.9 15.9 %collective-permute-start.34 = (f32[3,8,1280]{2,1,0:T(8,128)}, f32[3,8,1280]{2,1,0:T(8,128)}, u32[]{:S(2)}, u32[]{:S(2)}) collective-permute-start(f32[3,8,1280]{2,1,0:T(8,128)} %get-tuple-element.72), channel_id=1, source_target_pairs={{0,24},{2,26},{4,28},{6,30},{8,0},{10,2},{12,4},{14,6},{16,8},{18,... | collective-permute-start | bytes 368648 | tf_op jit(solution)/shard_map/ppermute | solution.py:510
  71.4 52.8 %collective-permute-start.17 = (f32[2,120,640]{2,1,0:T(8,128)S(1)}, f32[2,120,640]{2,1,0:T(8,128)}, u32[]{:S(2)}, u32[]{:S(2)}) collective-permute-start(f32[2,120,640]{2,1,0:T(8,128)S(1)} %copy-done.6), channel_id=1, source_target_pairs={{0,1},{1,0},{2,3},{3,2},{4,5},{5,4},{6,7},{7,6},{8,9},{9,8},{10,11... | collective-permute-start | bytes 1843208 | tf_op jit(solution)/shard_map/ppermute | solution.py:489
  72.2 12.1 %collective-permute-start.6 = (f32[3,32,1280]{2,1,0:T(8,128)}, f32[3,32,1280]{2,1,0:T(8,128)S(1)}, u32[]{:S(2)}, u32[]{:S(2)}) collective-permute-start(f32[3,32,1280]{2,1,0:T(8,128)} %add.403.refs_6_), channel_id=1, source_target_pairs={{0,4},{2,6},{4,0},{6,2},{8,12},{10,14},{12,8},{14,10},{16,20},{18,... | collective-permute-start | bytes 1474568 | tf_op jit(solution)/shard_map/ppermute | solution.py:500
  73.8 13.1 %collective-permute-start.10 = (f32[3,32,1280]{2,1,0:T(8,128)}, f32[3,32,1280]{2,1,0:T(8,128)S(1)}, u32[]{:S(2)}, u32[]{:S(2)}) collective-permute-start(f32[3,32,1280]{2,1,0:T(8,128)} %get-tuple-element.57), channel_id=1, source_target_pairs={{0,2},{2,0},{4,6},{6,4},{8,10},{10,8},{12,14},{14,12},{16,18},{18,... | collective-permute-start | bytes 1474568 | tf_op jit(solution)/shard_map/ppermute | solution.py:522
  74.8 29.7 %collective-permute-start.18 = (f32[3,32,1280]{2,1,0:T(8,128)}, f32[3,32,1280]{2,1,0:T(8,128)S(1)}, u32[]{:S(2)}, u32[]{:S(2)}) collective-permute-start(f32[3,32,1280]{2,1,0:T(8,128)} %get-tuple-element.65), channel_id=1, source_target_pairs={{0,2},{2,0},{4,6},{6,4},{8,10},{10,8},{12,14},{14,12},{16,18},{18,... | collective-permute-start | bytes 1474568 | tf_op jit(solution)/shard_map/ppermute | solution.py:523
  86.1 15.9 %collective-permute-start.35 = (f32[3,8,1280]{2,1,0:T(8,128)S(1)}, f32[3,8,1280]{2,1,0:T(8,128)S(1)}, u32[]{:S(2)}, u32[]{:S(2)}) collective-permute-start(f32[3,8,1280]{2,1,0:T(8,128)S(1)} %get-tuple-element.76.refs_4_), channel_id=1, source_target_pairs={{0,8},{2,10},{4,12},{6,14},{8,16},{10,18},{12,20},{14,22},{16,24},... | collective-permute-start | bytes 368648 | tf_op jit(solution)/shard_map/ppermute | solution.py:510
  86.8 16.6 %collective-permute-start.36 = (f32[3,8,1280]{2,1,0:T(8,128)}, f32[3,8,1280]{2,1,0:T(8,128)S(1)}, u32[]{:S(2)}, u32[]{:S(2)}) collective-permute-start(f32[3,8,1280]{2,1,0:T(8,128)} %get-tuple-element.74), channel_id=1, source_target_pairs={{0,16},{2,18},{4,20},{6,22},{8,24},{10,26},{12,28},{14,30},{16,0},... | collective-permute-start | bytes 368648 | tf_op jit(solution)/shard_map/ppermute | solution.py:510
  89.0 14.4 %collective-permute-start.37 = (f32[3,8,1280]{2,1,0:T(8,128)S(1)}, f32[3,8,1280]{2,1,0:T(8,128)}, u32[]{:S(2)}, u32[]{:S(2)}) collective-permute-start(f32[3,8,1280]{2,1,0:T(8,128)S(1)} %get-tuple-element.75), channel_id=1, source_target_pairs={{0,24},{2,26},{4,28},{6,30},{8,0},{10,2},{12,4},{14,6},{16,8},{18,... | collective-permute-start | bytes 368648 | tf_op jit(solution)/shard_map/ppermute | solution.py:510
  102.1 10.6 %collective-permute-start.19 = (f32[3,32,1280]{2,1,0:T(8,128)S(1)}, f32[3,32,1280]{2,1,0:T(8,128)S(1)}, u32[]{:S(2)}, u32[]{:S(2)}) collective-permute-start(f32[3,32,1280]{2,1,0:T(8,128)S(1)} %copy-done.14), channel_id=1, source_target_pairs={{0,4},{2,6},{4,0},{6,2},{8,12},{10,14},{12,8},{14,10},{16,20},{18,... | collective-permute-start | bytes 1474568 | tf_op jit(solution)/shard_map/ppermute | solution.py:500
  103.4 14.1 %collective-permute-start.12 = (f32[3,32,1280]{2,1,0:T(8,128)}, f32[3,32,1280]{2,1,0:T(8,128)S(1)}, u32[]{:S(2)}, u32[]{:S(2)}) collective-permute-start(f32[3,32,1280]{2,1,0:T(8,128)} %get-tuple-element.62), channel_id=1, source_target_pairs={{0,2},{2,0},{4,6},{6,4},{8,10},{10,8},{12,14},{14,12},{16,18},{18,... | collective-permute-start | bytes 1474568 | tf_op jit(solution)/shard_map/ppermute | solution.py:522
  112.8 6.9 %collective-permute-start.39 = (f32[3,8,1280]{2,1,0:T(8,128)S(1)}, f32[3,8,1280]{2,1,0:T(8,128)S(1)}, u32[]{:S(2)}, u32[]{:S(2)}) collective-permute-start(f32[3,8,1280]{2,1,0:T(8,128)S(1)} %get-tuple-element.79.refs_4_), channel_id=1, source_target_pairs={{0,8},{2,10},{4,12},{6,14},{8,16},{10,18},{12,20},{14,22},{16,24},... | collective-permute-start | bytes 368648 | tf_op jit(solution)/shard_map/ppermute | solution.py:510
  113.4 8.9 %collective-permute-start.40 = (f32[3,8,1280]{2,1,0:T(8,128)S(1)}, f32[3,8,1280]{2,1,0:T(8,128)S(1)}, u32[]{:S(2)}, u32[]{:S(2)}) collective-permute-start(f32[3,8,1280]{2,1,0:T(8,128)S(1)} %get-tuple-element.77), channel_id=1, source_target_pairs={{0,16},{2,18},{4,20},{6,22},{8,24},{10,26},{12,28},{14,30},{16,0},... | collective-permute-start | bytes 368648 | tf_op jit(solution)/shard_map/ppermute | solution.py:510
  114.7 8.5 %collective-permute-start.41 = (f32[3,8,1280]{2,1,0:T(8,128)S(1)}, f32[3,8,1280]{2,1,0:T(8,128)S(1)}, u32[]{:S(2)}, u32[]{:S(2)}) collective-permute-start(f32[3,8,1280]{2,1,0:T(8,128)S(1)} %get-tuple-element.78), channel_id=1, source_target_pairs={{0,24},{2,26},{4,28},{6,30},{8,0},{10,2},{12,4},{14,6},{16,8},{18,... | collective-permute-start | bytes 368648 | tf_op jit(solution)/shard_map/ppermute | solution.py:510
  117.5 21.7 %collective-permute-start.11 = (f32[3,32,1280]{2,1,0:T(8,128)}, f32[3,32,1280]{2,1,0:T(8,128)S(1)}, u32[]{:S(2)}, u32[]{:S(2)}) collective-permute-start(f32[3,32,1280]{2,1,0:T(8,128)} %get-tuple-element.60), channel_id=1, source_target_pairs={{0,2},{2,0},{4,6},{6,4},{8,10},{10,8},{12,14},{14,12},{16,18},{18,... | collective-permute-start | bytes 1474568 | tf_op jit(solution)/shard_map/ppermute | solution.py:523
  119.7 16.9 %collective-permute-start.38 = (f32[2,8,1280]{2,1,0:T(8,128)S(1)}, f32[2,8,1280]{2,1,0:T(8,128)S(1)}, u32[]{:S(2)}, u32[]{:S(2)}) collective-permute-start(f32[2,8,1280]{2,1,0:T(8,128)S(1)} %pad_maximum_fusion.4), channel_id=1, source_target_pairs={{0,1},{1,0},{2,3},{3,2},{4,5},{5,4},{6,7},{7,6},{8,9},{9,8},{10,11... | collective-permute-start | bytes 245768 | tf_op jit(solution)/shard_map/ppermute | solution.py:531
  122.4 17.7 %collective-permute-start.13 = (f32[3,32,1280]{2,1,0:T(8,128)S(1)}, f32[3,32,1280]{2,1,0:T(8,128)S(1)}, u32[]{:S(2)}, u32[]{:S(2)}) collective-permute-start(f32[3,32,1280]{2,1,0:T(8,128)S(1)} %add.411.refs_5_), channel_id=1, source_target_pairs={{0,4},{2,6},{4,0},{6,2},{8,12},{10,14},{12,8},{14,10},{16,20},{18,... | collective-permute-start | bytes 1474568 | tf_op jit(solution)/shard_map/ppermute | solution.py:500
  123.3 13.4 %collective-permute-start.42 = (f32[8,1280]{1,0:T(8,128)S(1)}, f32[8,1280]{1,0:T(8,128)S(1)}, u32[]{:S(2)}, u32[]{:S(2)}) collective-permute-start(f32[8,1280]{1,0:T(8,128)S(1)} %fusion.6), channel_id=1, source_target_pairs={{0,0},{1,2},{2,1},{3,3},{4,4},{5,6},{6,5},{7,7},{8,8},{9,10},{10,9... | collective-permute-start | bytes 122888 | tf_op jit(solution)/shard_map/ppermute | solution.py:537
  134.3 5.8 %collective-permute-start.21 = (f32[3,32,1280]{2,1,0:T(8,128)}, f32[3,32,1280]{2,1,0:T(8,128)S(1)}, u32[]{:S(2)}, u32[]{:S(2)}) collective-permute-start(f32[3,32,1280]{2,1,0:T(8,128)} %get-tuple-element.70), channel_id=1, source_target_pairs={{0,2},{2,0},{4,6},{6,4},{8,10},{10,8},{12,14},{14,12},{16,18},{18,... | collective-permute-start | bytes 1474568 | tf_op jit(solution)/shard_map/ppermute | solution.py:522
  136.6 24.5 %collective-permute-start.20 = (f32[3,32,1280]{2,1,0:T(8,128)}, f32[3,32,1280]{2,1,0:T(8,128)S(1)}, u32[]{:S(2)}, u32[]{:S(2)}) collective-permute-start(f32[3,32,1280]{2,1,0:T(8,128)} %get-tuple-element.68), channel_id=1, source_target_pairs={{0,2},{2,0},{4,6},{6,4},{8,10},{10,8},{12,14},{14,12},{16,18},{18,... | collective-permute-start | bytes 1474568 | tf_op jit(solution)/shard_map/ppermute | solution.py:523
  136.7 7.3 %collective-permute-start.43 = (f32[3,8,1280]{2,1,0:T(8,128)S(1)}, f32[3,8,1280]{2,1,0:T(8,128)S(1)}, u32[]{:S(2)}, u32[]{:S(2)}) collective-permute-start(f32[3,8,1280]{2,1,0:T(8,128)S(1)} %get-tuple-element.86), channel_id=1, source_target_pairs={{0,24},{2,26},{4,28},{6,30},{8,0},{10,2},{12,4},{14,6},{16,8},{18,... | collective-permute-start | bytes 368648 | tf_op jit(solution)/shard_map/ppermute | solution.py:540
  139.3 16.7 %collective-permute-start.44 = (f32[3,8,1280]{2,1,0:T(8,128)S(1)}, f32[3,8,1280]{2,1,0:T(8,128)S(1)}, u32[]{:S(2)}, u32[]{:S(2)}) collective-permute-start(f32[3,8,1280]{2,1,0:T(8,128)S(1)} %get-tuple-element.86), channel_id=1, source_target_pairs={{0,16},{2,18},{4,20},{6,22},{8,24},{10,26},{12,28},{14,30},{16,0},... | collective-permute-start | bytes 368648 | tf_op jit(solution)/shard_map/ppermute | solution.py:540
  140.0 16.2 %collective-permute-start.45 = (f32[3,8,1280]{2,1,0:T(8,128)S(1)}, f32[3,8,1280]{2,1,0:T(8,128)S(1)}, u32[]{:S(2)}, u32[]{:S(2)}) collective-permute-start(f32[3,8,1280]{2,1,0:T(8,128)S(1)} %get-tuple-element.86), channel_id=1, source_target_pairs={{0,8},{2,10},{4,12},{6,14},{8,16},{10,18},{12,20},{14,22},{16,24},... | collective-permute-start | bytes 368648 | tf_op jit(solution)/shard_map/ppermute | solution.py:540
  140.2 18.3 %collective-permute-start.14 = (f32[3,8,1280]{2,1,0:T(8,128)S(1)}, f32[3,8,1280]{2,1,0:T(8,128)S(1)}, u32[]{:S(2)}, u32[]{:S(2)}) collective-permute-start(f32[3,8,1280]{2,1,0:T(8,128)S(1)} %get-tuple-element.80), channel_id=1, source_target_pairs={{0,8},{2,10},{4,12},{6,14},{8,16},{10,18},{12,20},{14,22},{16,24},... | collective-permute-start | bytes 368648 | tf_op jit(solution)/shard_map/ppermute | solution.py:510
  144.0 15.9 %collective-permute-start.15 = (f32[3,8,1280]{2,1,0:T(8,128)S(1)}, f32[3,8,1280]{2,1,0:T(8,128)S(1)}, u32[]{:S(2)}, u32[]{:S(2)}) collective-permute-start(f32[3,8,1280]{2,1,0:T(8,128)S(1)} %get-tuple-element.82), channel_id=1, source_target_pairs={{0,16},{2,18},{4,20},{6,22},{8,24},{10,26},{12,28},{14,30},{16,0},... | collective-permute-start | bytes 368648 | tf_op jit(solution)/shard_map/ppermute | solution.py:510
  156.0 5.1 %collective-permute-start.16 = (f32[3,8,1280]{2,1,0:T(8,128)S(1)}, f32[3,8,1280]{2,1,0:T(8,128)S(1)}, u32[]{:S(2)}, u32[]{:S(2)}) collective-permute-start(f32[3,8,1280]{2,1,0:T(8,128)S(1)} %get-tuple-element.81), channel_id=1, source_target_pairs={{0,24},{2,26},{4,28},{6,30},{8,0},{10,2},{12,4},{14,6},{16,8},{18,... | collective-permute-start | bytes 368648 | tf_op jit(solution)/shard_map/ppermute | solution.py:510
  156.3 14.2 %collective-permute-start.22 = (f32[3,32,1280]{2,1,0:T(8,128)S(1)}, f32[3,32,1280]{2,1,0:T(8,128)S(1)}, u32[]{:S(2)}, u32[]{:S(2)}) collective-permute-start(f32[3,32,1280]{2,1,0:T(8,128)S(1)} %add.435), channel_id=1, source_target_pairs={{0,4},{2,6},{4,0},{6,2},{8,12},{10,14},{12,8},{14,10},{16,20},{18,... | collective-permute-start | bytes 1474568 | tf_op jit(solution)/shard_map/ppermute | solution.py:500
  158.4 34.7 %collective-permute-start.46 = (f32[3,4,8,1280]{3,2,0,1:T(8,128)S(1)}, f32[3,4,8,1280]{3,2,0,1:T(8,128)S(1)}, u32[]{:S(2)}, u32[]{:S(2)}) collective-permute-start(f32[3,4,8,1280]{3,2,0,1:T(8,128)S(1)} %pad_maximum_fusion), channel_id=1, source_target_pairs={{0,4},{2,6},{4,0},{6,2},{8,12},{10,14},{12,8},{14,10},{16,20},{18,... | collective-permute-start | bytes 1474568 | tf_op jit(solution)/shard_map/ppermute | solution.py:542
  170.6 7.5 %collective-permute-start.23 = (f32[3,8,1280]{2,1,0:T(8,128)S(1)}, f32[3,8,1280]{2,1,0:T(8,128)S(1)}, u32[]{:S(2)}, u32[]{:S(2)}) collective-permute-start(f32[3,8,1280]{2,1,0:T(8,128)S(1)} %get-tuple-element.83), channel_id=1, source_target_pairs={{0,8},{2,10},{4,12},{6,14},{8,16},{10,18},{12,20},{14,22},{16,24},... | collective-permute-start | bytes 368648 | tf_op jit(solution)/shard_map/ppermute | solution.py:510
  172.7 9.1 %collective-permute-start.24 = (f32[3,8,1280]{2,1,0:T(8,128)S(1)}, f32[3,8,1280]{2,1,0:T(8,128)S(1)}, u32[]{:S(2)}, u32[]{:S(2)}) collective-permute-start(f32[3,8,1280]{2,1,0:T(8,128)S(1)} %get-tuple-element.85), channel_id=1, source_target_pairs={{0,16},{2,18},{4,20},{6,22},{8,24},{10,26},{12,28},{14,30},{16,0},... | collective-permute-start | bytes 368648 | tf_op jit(solution)/shard_map/ppermute | solution.py:510
  172.7 9.1 %collective-permute-start.25 = (f32[3,8,1280]{2,1,0:T(8,128)S(1)}, f32[3,8,1280]{2,1,0:T(8,128)S(1)}, u32[]{:S(2)}, u32[]{:S(2)}) collective-permute-start(f32[3,8,1280]{2,1,0:T(8,128)S(1)} %get-tuple-element.84), channel_id=1, source_target_pairs={{0,24},{2,26},{4,28},{6,30},{8,0},{10,2},{12,4},{14,6},{16,8},{18,... | collective-permute-start | bytes 368648 | tf_op jit(solution)/shard_map/ppermute | solution.py:510
  181.9 5.4 %collective-permute-start.26 = (f32[2,8,1280]{2,1,0:T(8,128)S(1)}, f32[2,8,1280]{2,1,0:T(8,128)S(1)}, u32[]{:S(2)}, u32[]{:S(2)}) collective-permute-start(f32[2,8,1280]{2,1,0:T(8,128)S(1)} %get-tuple-element.88), channel_id=1, source_target_pairs={{0,24},{2,26},{4,28},{6,30},{8,0},{10,2},{12,4},{14,6},{16,8},{18,... | collective-permute-start | bytes 245768 | tf_op jit(solution)/shard_map/ppermute | solution.py:540
  184.6 5.9 %collective-permute-start.27 = (f32[2,8,1280]{2,1,0:T(8,128)S(1)}, f32[2,8,1280]{2,1,0:T(8,128)S(1)}, u32[]{:S(2)}, u32[]{:S(2)}) collective-permute-start(f32[2,8,1280]{2,1,0:T(8,128)S(1)} %get-tuple-element.88), channel_id=1, source_target_pairs={{0,16},{2,18},{4,20},{6,22},{8,24},{10,26},{12,28},{14,30},{16,0},... | collective-permute-start | bytes 245768 | tf_op jit(solution)/shard_map/ppermute | solution.py:540
  185.3 6.2 %collective-permute-start.28 = (f32[2,8,1280]{2,1,0:T(8,128)S(1)}, f32[2,8,1280]{2,1,0:T(8,128)S(1)}, u32[]{:S(2)}, u32[]{:S(2)}) collective-permute-start(f32[2,8,1280]{2,1,0:T(8,128)S(1)} %get-tuple-element.88), channel_id=1, source_target_pairs={{0,8},{2,10},{4,12},{6,14},{8,16},{10,18},{12,20},{14,22},{16,24},... | collective-permute-start | bytes 245768 | tf_op jit(solution)/shard_map/ppermute | solution.py:540
  191.6 7.1 %collective-permute-start.29 = (f32[2,4,8,1280]{3,2,1,0:T(8,128)S(1)}, f32[2,4,8,1280]{3,2,1,0:T(8,128)S(1)}, u32[]{:S(2)}, u32[]{:S(2)}) collective-permute-start(f32[2,4,8,1280]{3,2,1,0:T(8,128)S(1)} %pad_maximum_fusion.1.refs_0_), channel_id=1, source_target_pairs={{0,4},{2,6},{4,0},{6,2},{8,12},{10,14},{12,8},{14,10},{16,20},{18,... | collective-permute-start | bytes 983048 | tf_op jit(solution)/shard_map/ppermute | solution.py:542
  193.1 8.5 %collective-permute-start.47 = (f32[3,4,8,1280]{3,2,0,1:T(8,128)S(1)}, f32[3,4,8,1280]{3,2,0,1:T(8,128)S(1)}, u32[]{:S(2)}, u32[]{:S(2)}) collective-permute-start(f32[3,4,8,1280]{3,2,0,1:T(8,128)S(1)} %pad_maximum_fusion), channel_id=1, source_target_pairs={{0,2},{2,0},{4,6},{6,4},{8,10},{10,8},{12,14},{14,12},{16,18},{18,... | collective-permute-start | bytes 1474568 | tf_op jit(solution)/shard_map/ppermute | solution.py:543
  193.1 9.4 %collective-permute-start.48 = (f32[3,4,8,1280]{3,2,0,1:T(8,128)S(1)}, f32[3,4,8,1280]{3,2,0,1:T(8,128)S(1)}, u32[]{:S(2)}, u32[]{:S(2)}) collective-permute-start(f32[3,4,8,1280]{3,2,0,1:T(8,128)S(1)} %collective-permute-done.46), channel_id=1, source_target_pairs={{0,2},{2,0},{4,6},{6,4},{8,10},{10,8},{12,14},{14,12},{16,18},{18,... | collective-permute-start | bytes 1474568 | tf_op jit(solution)/shard_map/ppermute | solution.py:543
  193.6 12.9 %collective-permute-start.30 = (f32[2,4,8,1280]{3,2,1,0:T(8,128)S(1)}, f32[2,4,8,1280]{3,2,1,0:T(8,128)S(1)}, u32[]{:S(2)}, u32[]{:S(2)}) collective-permute-start(f32[2,4,8,1280]{3,2,1,0:T(8,128)S(1)} %pad_maximum_fusion.1.refs_0_), channel_id=1, source_target_pairs={{0,2},{2,0},{4,6},{6,4},{8,10},{10,8},{12,14},{14,12},{16,18},{18,... | collective-permute-start | bytes 983048 | tf_op jit(solution)/shard_map/ppermute | solution.py:543
  198.7 7.7 %collective-permute-start.31 = (f32[2,4,8,1280]{3,2,1,0:T(8,128)S(1)}, f32[2,4,8,1280]{3,2,1,0:T(8,128)S(1)}, u32[]{:S(2)}, u32[]{:S(2)}) collective-permute-start(f32[2,4,8,1280]{3,2,1,0:T(8,128)S(1)} %collective-permute-done.29.refs_1_), channel_id=1, source_target_pairs={{0,2},{2,0},{4,6},{6,4},{8,10},{10,8},{12,14},{14,12},{16,18},{18,... | collective-permute-start | bytes 983048 | tf_op jit(solution)/shard_map/ppermute | solution.py:543
  (21 other events, 209.8 us)

commit v7 on v5

v7 whole, which is shorter than its diff:
```python
import functools
import math

import jax
import jax.numpy as jnp
import ml_dtypes
import numpy as np
from jax import lax
from jax.experimental import pallas as pl
from jax.experimental.pallas import tpu as pltpu
from jax.sharding import PartitionSpec as P

NLON = 1280
STEPS = 1
SUB = 8
LANE = 128
VMEM_LIMIT = 60 * 1024 * 1024
KERNEL_WORK = 8
LAG = 1


def padded(cells, sides, width):
    for axis, dim in sides:
        count = lax.axis_size(axis)
        ends = count - 1
        head = lax.slice_in_dim(cells, 0, width, axis=dim)
        tail = lax.slice_in_dim(cells, cells.shape[dim] - width, cells.shape[dim], axis=dim)
        cells = jnp.concatenate(
            [
                lax.ppermute(tail, axis, [(i, (i + 1) % count) for i in range(ends)]),
                cells,
                lax.ppermute(head, axis, [((i + 1) % count, i) for i in range(ends)]),
            ],
            axis=dim,
        )
    return cells


def slope(extended, winds):
    center = extended[:, 1:-1]
    north = (extended[:, 2:] - extended[:, :-2]) * 0.5
    east = (jnp.roll(center, -1, 2) - jnp.roll(center, 1, 2)) * 0.5
    return -winds - (winds[0] * east + winds[1] * north)


def rimmed(field):
    return padded(field, (("band", 1),), 1)


def tensor(extended):
    center = extended[:, 1:-1]
    north = (extended[:, 2:] - extended[:, :-2]) * 0.5
    east = (jnp.roll(center, -1, 2) - jnp.roll(center, 1, 2)) * 0.5
    g_xx = 1.0 + east[0]
    g_xy = north[0]
    g_yx = east[1]
    g_yy = 1.0 + north[1]
    return jnp.stack(
        [g_xx * g_xx + g_yx * g_yx, g_xx * g_xy + g_yx * g_yy, g_xy * g_xy + g_yy * g_yy]
    )


def integrate(shift, flow, extend):
    first = slope(extend(shift), flow)
    second = slope(extend(0.5 * first), flow)
    third = slope(extend(0.5 * second), flow)
    fourth = slope(extend(third), flow)
    return (first + 2.0 * second + 2.0 * third + fourth) / 6.0


def exponent_of(summed, members):
    mean = summed / members
    first, cross, second = (mean[..., 0, :, :], mean[..., 1, :, :], mean[..., 2, :, :])
    half = (first + second) * 0.5
    differ = (first - second) * 0.5
    largest = half + jnp.sqrt(differ * differ + cross * cross)
    return jnp.log(largest + 1e-06) / (2.0 * STEPS)


def by_rows(coeffs):
    spec = coeffs[0]
    levels = spec.shape[0]
    nlat = spec.shape[4]
    waves = spec.shape[3] * lax.axis_size("band")
    members = lax.axis_size("mem")
    stacked = spec.reshape(levels * 2, 2, spec.shape[3], nlat)
    wave_index = lax.iota(jnp.int32, waves)
    column = lax.iota(jnp.int32, NLON)
    phase = wave_index[:, None] * column[None, :] % NLON
    angle = phase.astype(jnp.float32) * (2.0 * math.pi / NLON)
    weight = jnp.where(wave_index == 0, 1.0, 2.0).astype(jnp.float32)[:, None]
    table = jnp.stack([weight * jnp.cos(angle), -weight * jnp.sin(angle)], axis=0)
    winds = jnp.einsum(
        "crwh,rwn->chn",
        lax.all_to_all(stacked, "band", split_axis=3, concat_axis=2, tiled=True),
        table,
        precision=lax.Precision.HIGHEST,
        preferred_element_type=jnp.float32,
    )
    height = winds.shape[1]
    winds = winds.reshape(levels, 2, height, NLON)
    partials = []
    for level in range(levels):
        flow = winds[level]
        shift = integrate(jnp.zeros_like(flow), flow, rimmed)
        partials.append(tensor(rimmed(shift)))
    summed = lax.psum_scatter(jnp.stack(partials), "mem", scatter_dimension=3, tiled=True)
    return lax.all_gather(exponent_of(summed, members), "mem", axis=2, tiled=True)


def by_parity(waves_local):
    half = waves_local // 2
    whole = 2 * LANE - half
    runs = []
    for parity in range(2):
        runs += [(parity, half, 2), (waves_local + parity, whole, 2)]
    for parity in range(2):
        runs.append((waves_local + parity + 2 * whole, half - whole, 2))
    return runs


@functools.lru_cache(maxsize=None)
def wave_table(bands, waves_local):
    order = np.concatenate([start + step * np.arange(count) for start, count, step in by_parity(waves_local)])
    wave, part = order % waves_local, order // waves_local
    wave = wave[None, :] + waves_local * np.arange(bands)[:, None]
    part = np.broadcast_to(part, wave.shape)
    cut = [0, 2 * LANE, 4 * LANE, 4 * LANE + LANE // 2, 5 * LANE]
    result = []
    for parity in range(2):
        picks = [(band, slice(cut[parity], cut[parity + 1])) for band in range(bands)]
        picks += [(band, slice(cut[parity + 2], cut[parity + 3])) for band in range(bands)]
        waves = np.concatenate([wave[pick] for pick in picks])
        parts = np.concatenate([part[pick] for pick in picks])
        phase = (waves[:, None] * np.arange(NLON // 2)[None, :]) % NLON
        angle = phase.astype(np.float64) * (2.0 * np.pi / NLON)
        weight = np.where(waves == 0, 1.0, 2.0)[:, None]
        table = weight * np.where(parts[:, None] == 0, np.cos(angle), -np.sin(angle))
        high = table.astype(ml_dtypes.bfloat16)
        result += [high, (table - high.astype(np.float64)).astype(ml_dtypes.bfloat16)]
    return np.stack(result)


class Piece:
    def __init__(self, index, count):
        self.index = index
        self.main = LANE if index == 0 else LANE - SUB
        self.rim = 0 if index == count - 1 else SUB
        self.rows = self.main + self.rim


class Window:
    def __init__(self, pieces, count):
        self.pieces = pieces
        self.first = pieces[0].index == 0
        self.last = pieces[-1].index == count - 1
        self.width = LANE * len(pieces)
        self.extended = self.width + 2 * SUB
        self.spread = self.extended // SUB
        self.places = []
        up = SUB if self.first else 2 * SUB
        for piece in pieces:
            self.places.append((self.extended - up - piece.rows, up))
            up += piece.rows
        self.side = "other" if 2 * (pieces[-1].index + 1) <= count else "own" if 2 * pieces[0].index >= count else "both"


def choose(band, pair):
    return jnp.where(band == 0, pair[0], pair[1])


def multiple(value, of):
    return pl.multiple_of(value.astype(jnp.int32), of)


def pieces_kernel(pieces, slots, count, level_ref, spec_ref, *refs):
    out_refs, (taken, turned, in_sems, out_sems) = refs[: len(pieces)], refs[len(pieces) :]
    level = level_ref[0]
    runs = by_parity(spec_ref.shape[2] // 2)

    def arrival(c, n):
        tile = choose(level, (count - 1 - slots[n], slots[n]))
        lanes = pl.ds(multiple(tile * LANE, LANE), LANE)
        return pltpu.make_async_copy(spec_ref.at[level, c, :, lanes], taken.at[c, n], in_sems.at[c, n])

    def departures(c, k):
        piece, n = pieces[k], slots.index(pieces[k].index)
        rows = pl.ds(multiple(choose(level, (0, LANE - piece.main)), SUB), piece.main)
        at = pl.ds(multiple(choose(level, (piece.rim, 0)), SUB), piece.main)
        yield pltpu.make_async_copy(turned.at[c, n, rows], out_refs[k].at[c, at], out_sems.at[k, c, 0])
        if piece.rim:
            rows = pl.ds(multiple(choose(level, (LANE - SUB, 0)), SUB), SUB)
            at = pl.ds(multiple(choose(level, (0, piece.main)), SUB), SUB)
            yield pltpu.make_async_copy(turned.at[c, n + 1, rows], out_refs[k].at[c, at], out_sems.at[k, c, 1])

    for n in range(len(slots)):
        for c in range(2):
            arrival(c, n).start()
    for n in range(len(slots)):
        for c in range(2):
            arrival(c, n).wait()
            turned[c, n] = jnp.concatenate([taken[c, n, pl.ds(start, rows, step), :] for start, rows, step in runs]).T
        for k, piece in enumerate(pieces):
            if slots[n] == piece.index + (1 if piece.rim else 0):
                for c in range(2):
                    for copy in departures(c, k):
                        copy.start()
    for k in range(len(pieces)):
        for c in range(2):
            for copy in departures(c, k):
                copy.wait()


def pieces_of(spec, level, pieces, count):
    depth = spec.shape[2]
    slots = sorted({w.index for w in pieces} | {w.index + 1 for w in pieces if w.rim})
    return pl.pallas_call(
        functools.partial(pieces_kernel, pieces, slots, count),
        in_specs=[pl.BlockSpec(memory_space=pltpu.SMEM), pl.BlockSpec(memory_space=pl.ANY)],
        out_specs=[pl.BlockSpec(memory_space=pl.ANY)] * len(pieces),
        out_shape=[jax.ShapeDtypeStruct((2, w.rows, depth), jnp.float32) for w in pieces],
        scratch_shapes=[
            pltpu.VMEM((2, len(slots), depth, LANE), jnp.float32),
            pltpu.VMEM((2, len(slots), LANE, depth), jnp.float32),
            pltpu.SemaphoreType.DMA((2, len(slots))),
            pltpu.SemaphoreType.DMA((len(pieces), 2, 2)),
        ],
        compiler_params=pltpu.CompilerParams(vmem_limit_bytes=VMEM_LIMIT),
        cost_estimate=pl.CostEstimate(
            flops=0, transcendentals=0, bytes_accessed=4 * 2 * len(slots) * LANE * depth * 4
        ),
        name="pieces_of",
    )(level.reshape(1), spec)


def gate_kernel(*refs):
    pass


def gated(part, waits):
    return pl.pallas_call(
        gate_kernel,
        in_specs=[pl.BlockSpec(memory_space=pl.ANY)] * (1 + len(waits)),
        out_specs=pl.BlockSpec(memory_space=pl.ANY),
        out_shape=jax.ShapeDtypeStruct(part.shape, part.dtype),
        input_output_aliases={0: 0},
        cost_estimate=pl.CostEstimate(flops=0, transcendentals=0, bytes_accessed=1024),
        name="gated",
    )(part, *waits)


def east_of(x):
    return pltpu.roll(x, NLON - 1, axis=1) - pltpu.roll(x, 1, axis=1)


def window_kernel(window, waits, *refs):
    refs = list(refs)
    pieces, extended, spread = window.pieces, window.extended, window.spread
    place_ref, table_ref = refs[:2]
    local_refs, remote_refs = refs[2 : 2 + len(pieces)], refs[2 + len(pieces) : 2 + 2 * len(pieces)]
    refs = refs[2 + 2 * len(pieces) + waits :]
    carry_ref = None if window.first else refs.pop(0)
    out_refs = [refs.pop(0) for _ in range(4)]
    carried_ref = None if window.last else refs.pop(0)
    table, lhs_high, lhs_low, natural, wind, second, third, shift, results, carried, table_sem, out_sems = refs
    band, core, side = place_ref[0], place_ref[1], place_ref[2]

    def at(pair):
        return multiple(choose(band, pair), SUB)

    tables = pltpu.make_async_copy(table_ref, table, table_sem)
    tables.start()
    even, odd = [], []
    for local_ref, remote_ref, piece in zip(local_refs, remote_refs, pieces):
        lane = lax.broadcasted_iota(jnp.int32, (piece.rows, LANE), 1)
        turn = functools.partial(pltpu.roll, shift=LANE // 2, axis=1)
        for c in range(2):
            mine, theirs = local_ref[c], remote_ref[c]
            low, high = jnp.where(band == 0, mine, theirs), jnp.where(band == 0, theirs, mine)
            low_rest, high_rest = low[:, 4 * LANE :], high[:, 4 * LANE :]
            even_rest = jnp.where(lane < LANE // 2, low_rest, turn(high_rest))
            odd_rest = jnp.where(lane < LANE // 2, turn(low_rest), high_rest)
            even.append(jnp.concatenate([low[:, : 2 * LANE], high[:, : 2 * LANE], even_rest], axis=1))
            odd.append(jnp.concatenate([low[:, 2 * LANE : 4 * LANE], high[:, 2 * LANE : 4 * LANE], odd_rest], axis=1))
    for parity, parts in enumerate((even, odd)):
        lhs = jnp.concatenate(parts)
        lhs_high[parity] = lhs.astype(jnp.bfloat16)
        lhs_low[parity] = (lhs - lhs_high[parity].astype(jnp.float32)).astype(jnp.bfloat16)

    tiles = NLON // LANE
    for c in range(2):
        for t in range(tiles):
            if window.first:
                natural[c, t, pl.ds(at((extended - SUB, 0)), SUB), :] = jnp.zeros((SUB, LANE), jnp.float32)
            else:
                natural[c, t, pl.ds(at((extended - 2 * SUB, 0)), 2 * SUB), :] = carry_ref[c, t]
            if window.last:
                natural[c, t, pl.ds(at((0, extended - SUB)), SUB), :] = jnp.zeros((SUB, LANE), jnp.float32)
    tables.wait()

    dot = functools.partial(jnp.dot, preferred_element_type=jnp.float32)
    for start in range(0, tiles // 2, 2):
        stop = min(start + 2, tiles // 2)
        columns = slice(start * LANE, stop * LANE)
        sums = []
        for parity in range(2):
            total = dot(lhs_high[parity], table[2 * parity, :, columns])
            total += dot(lhs_low[parity], table[2 * parity, :, columns])
            total += dot(lhs_high[parity], table[2 * parity + 1, :, columns])
            sums.append(total)
        row = 0
        for piece, place in zip(pieces, window.places):
            rows = pl.ds(at(place), piece.rows)
            for c in range(2):
                even_sum, odd_sum = (total[row : row + piece.rows] for total in sums)
                row += piece.rows
                for t in range(start, stop):
                    lanes = slice((t - start) * LANE, (t - start + 1) * LANE)
                    natural[c, t, rows, :] = even_sum[:, lanes] + odd_sum[:, lanes]
                    natural[c, tiles // 2 + t, rows, :] = even_sum[:, lanes] - odd_sum[:, lanes]

    if not window.last:
        for c in range(2):
            for t in range(tiles):
                carried[c, t] = natural[c, t, pl.ds(at((0, extended - 2 * SUB)), 2 * SUB), :]
        carry_on = pltpu.make_async_copy(carried, carried_ref, out_sems.at[4])
        carry_on.start()

    def closed(field):
        for c in range(2):
            field[c, 0] = pltpu.roll(field[c, spread], 1, axis=0)
            field[c, spread + 1] = pltpu.roll(field[c, 1], SUB - 1, axis=0)

    def slopes(field, block):
        return [(east_of(field[c, block]), field[c, block + 1] - field[c, block - 1]) for c in range(2)]

    def each_block(body):
        @pl.loop(0, spread // 2)
        def _(pair):
            body(2 * pair + 1)
            body(2 * pair + 2)

    def spread_out(block):
        for c in range(2):
            rows = pl.ds(block - 1, SUB, spread)
            wind[c, block] = jnp.concatenate([natural[c, t, rows, :] for t in range(tiles)], axis=1)

    each_block(spread_out)
    closed(wind)

    def second_slope(block):
        u, v = wind[0, block], wind[1, block]
        for c, (east, north) in enumerate(slopes(wind, block)):
            second[c, block] = 0.25 * (u * east + v * north) - (u, v)[c]

    each_block(second_slope)
    closed(second)

    def third_slope(block):
        u, v = wind[0, block], wind[1, block]
        for c, (east, north) in enumerate(slopes(second, block)):
            third[c, block] = -(u, v)[c] - 0.25 * (u * east + v * north)

    each_block(third_slope)
    closed(third)

    def whole_step(block):
        u, v = wind[0, block], wind[1, block]
        for c, (east, north) in enumerate(slopes(third, block)):
            fourth = -(u, v)[c] - 0.5 * (u * east + v * north)
            both = second[c, block] + third[c, block]
            shift[c, block] = (2.0 * both + (fourth - (u, v)[c])) * (1.0 / 6.0)

    each_block(whole_step)
    closed(shift)

    def entries(block):
        (e0, n0), (e1, n1) = slopes(shift, block)
        g_xx, g_xy, g_yx, g_yy = 1.0 + 0.5 * e0, 0.5 * n0, 0.5 * e1, 1.0 + 0.5 * n1
        rows = pl.ds(block - 1, SUB, spread)
        for n, entry in enumerate((g_xx * g_xx + g_yx * g_yx, g_xx * g_xy + g_yx * g_yy, g_xy * g_xy + g_yy * g_yy)):
            for t in range(tiles):
                results[n, t, rows, :] = entry[:, t * LANE : (t + 1) * LANE]

    each_block(entries)

    quarter = window.width // 4
    copies = []
    for n, (a, b) in enumerate(QUARTERS):
        base = (2 * (core + a - 2 * core * a) + (side + b - 2 * side * b)) * quarter + SUB
        rows = pl.ds(multiple(base, SUB), quarter)
        copies.append(pltpu.make_async_copy(results.at[:, :, rows], out_refs[n], out_sems.at[n]))
        copies[-1].start()
    for copy in copies:
        copy.wait()
    if not window.last:
        carry_on.wait()


QUARTERS = ((0, 0), (0, 1), (1, 0), (1, 1))


def window_tensor(window, place, table, local, remote, waits, carry):
    depth, tiles = local[0].shape[2], NLON // LANE
    vmem, hbm = pl.BlockSpec(memory_space=pltpu.VMEM), pl.BlockSpec(memory_space=pl.ANY)
    in_specs = [pl.BlockSpec(memory_space=pltpu.SMEM), hbm]
    in_specs += [vmem] * (len(local) + len(remote)) + [hbm] * len(waits)
    operands = [place, table, *local, *remote, *waits]
    if not window.first:
        in_specs.append(vmem)
        operands.append(carry)
    out_shape = [jax.ShapeDtypeStruct((3, tiles, window.width // 4, LANE), jnp.float32)] * 4
    carried = (2, tiles, 2 * SUB, LANE)
    if not window.last:
        out_shape.append(jax.ShapeDtypeStruct(carried, jnp.float32))
    field = pltpu.VMEM((2, window.spread + 2, SUB, NLON), jnp.float32)
    rows = sum(piece.rows for piece in window.pieces)
    lhs_shape = (2, 2 * rows, depth)
    out = pl.pallas_call(
        functools.partial(window_kernel, window, len(waits)),
        out_shape=out_shape,
        in_specs=in_specs,
        out_specs=[hbm] * len(out_shape),
        scratch_shapes=[
            pltpu.VMEM(table.shape, table.dtype),
            pltpu.VMEM(lhs_shape, jnp.bfloat16),
            pltpu.VMEM(lhs_shape, jnp.bfloat16),
            pltpu.VMEM((2, tiles, window.extended, LANE), jnp.float32),
            field,
            field,
            field,
            field,
            pltpu.VMEM((3, tiles, window.extended, LANE), jnp.float32),
            pltpu.VMEM(carried, jnp.float32),
            pltpu.SemaphoreType.DMA,
            pltpu.SemaphoreType.DMA((5,)),
        ],
        compiler_params=pltpu.CompilerParams(vmem_limit_bytes=VMEM_LIMIT),
        cost_estimate=pl.CostEstimate(
            flops=KERNEL_WORK * 3 * 2 * 2 * rows * depth * NLON,
            transcendentals=0,
            bytes_accessed=2 * table.size + 4 * rows * depth * 4 + 12 * window.width * NLON,
        ),
        name="window_tensor",
    )(*operands)
    return out[:4], (None if window.last else out[4])


def pairs(members, bit):
    return [(member, member ^ bit) for member in range(members)]


def by_levels(coeffs):
    spec = coeffs[0]
    levels, _, parts, waves_local, nlat = spec.shape
    members = lax.axis_size("mem")
    band = lax.axis_index("band").astype(jnp.int32)
    member = lax.axis_index("mem").astype(jnp.int32)
    core, side = member % 2, member // 2 % 2
    place = jnp.stack([band, core, side])
    spec = spec.reshape(levels, 2, parts * waves_local, nlat)
    count = nlat // LANE
    pieces = [Piece(k, count) for k in range(count)]
    windows = [Window(pieces[:2], count)] + [Window([piece], count) for piece in pieces[2:]]
    table = jnp.asarray(wave_table(levels, waves_local))
    swap = [(0, 1), (1, 0)]

    (outgoing,) = pieces_of(spec, 1 - band, pieces[:1], count)
    remotes = [lax.ppermute(outgoing, "band", swap)]
    outgoing = [None, *pieces_of(spec, 1 - band, pieces[1:], count)]

    def fetch_rows(k, waits):
        piece = gated(outgoing[k], waits) if waits else outgoing[k]
        remotes.append(lax.ppermute(piece, "band", swap))
        return piece

    fetch_rows(1, [])
    local = pieces_of(spec, band, pieces, count)

    bits = [1 << n for n in range(members.bit_length() - 1)]

    def halved(parts_of, bit):
        half = parts_of[0].shape[2] // 2
        mine = (member // bit) % 2

        def total(which):
            return sum(lax.dynamic_slice_in_dim(part, which * half, half, axis=2) for part in parts_of)

        leaves = total(1 - mine)
        return [total(mine), lax.ppermute(leaves, "mem", pairs(members, bit))], leaves

    def across(parts_of, bit):
        kept, passed, kept_more, passed_more = parts_of
        leaves = passed + passed_more
        return [kept, kept_more, lax.ppermute(leaves, "mem", pairs(members, bit))], leaves

    def advanced(parts_of, bit):
        return (across if len(parts_of) == 4 else halved)(parts_of, bit)

    def doubled(part, bit):
        beside = lax.ppermute(part, "mem", pairs(members, bit))
        mine = (member // bit) % 2
        return jnp.where(mine == 0, jnp.concatenate([part, beside], axis=0), jnp.concatenate([beside, part], axis=0))

    def gathered(part):
        for bit in reversed(bits):
            part = doubled(part, bit)
        return part

    carry = None
    sums, done = [], []
    for k, window in enumerate(windows):
        waits, last = [], window.pieces[-1].index
        while len(remotes) < min(last + 3, count):
            before = len(remotes) - 2
            waits.append(fetch_rows(len(remotes), [remotes[before]] if carry is None else [remotes[before], carry]))
        for j in range(k - LAG):
            sums[j], left = advanced(sums[j], bits[done[j]])
            done[j] += 1
            waits.append(left)
        here = [piece.index for piece in window.pieces]
        quarters, carry = window_tensor(
            window, place, table, [local[p] for p in here], [remotes[p] for p in here], waits, carry
        )
        first = lax.ppermute(quarters[3], "mem", pairs(members, bits[0]))
        second = lax.ppermute(quarters[2], "mem", pairs(members, bits[0]))
        sums.append([quarters[0], quarters[1], second, first])
        done.append(1)
    results = {}
    for k, window in enumerate(windows):
        for bit in bits[done[k] :]:
            sums[k], _ = advanced(sums[k], bit)
        summed = sum(sums[k])
        rows = summed.shape[2]
        summed = summed.transpose(0, 2, 1, 3).reshape(3, rows, NLON)
        results.setdefault(window.side, []).append(exponent_of(summed, members))

    (other,), (both,) = results["other"], results["both"]
    other = lax.ppermute(other, "band", swap)
    trades = []
    for m in range(members):
        for b in range(2):
            mate = (m, b) if m % 2 == b else (m ^ 1, 1 - b)
            trades.append((m * 2 + b, mate[0] * 2 + mate[1]))
    both = lax.ppermute(both, ("mem", "band"), trades)

    def whole(parts):
        heights = [part.shape[0] for part in parts]
        stack = jnp.concatenate(parts, axis=0)[None]
        stack = gathered(stack)
        cuts = np.cumsum([0] + heights)
        return [stack[:, cuts[n] : cuts[n + 1]].reshape(-1, NLON) for n in range(len(parts))]

    other, both = whole([other, both])
    middle = both.shape[0] // 2
    low, high = both[:middle], both[middle:]
    rest = jnp.zeros((nlat // 2 - middle, NLON), jnp.float32)
    down = jnp.stack([jnp.concatenate([rest, low]), jnp.concatenate([other, high])])
    up = jnp.stack([jnp.concatenate([low, other]), jnp.concatenate([high, rest])])
    out = jnp.where(band == 0, down, up)
    for k, block in enumerate(whole(results["own"])):
        width = block.shape[0]
        row = choose(band, (nlat // 2 - middle - (k + 1) * width, middle + k * width))
        out = lax.dynamic_update_slice(out, block[None], (band, row.astype(jnp.int32), jnp.int32(0)))
    return out


def per_device(coeffs):
    _, levels, _, _, _, nlat = coeffs.shape
    members = lax.axis_size("mem")
    rows = nlat // lax.axis_size("band")
    fits = coeffs.shape[4] == 5 * LANE // 2 and nlat % (2 * LANE) == LANE and rows > LANE
    if fits and levels == lax.axis_size("band") == 2 and members == 16:
        return by_levels(coeffs)
    return by_rows(coeffs)


def solution(mesh):
    placed = (P("mem", None, None, None, "band", None),)
    return jax.shard_map(
        per_device, mesh=mesh, in_specs=placed, out_specs=P(None, "band", None), check_vma=False
    )
```

time: 194 us -> 220 us (1.13)
  waiting for transfers between devices: 64.8 us -> 95.9 us
  local copies, waits for them, and re-layouts: 16.4 us -> 5.42 us
  Pallas kernels: 63.6 us -> 68.5 us
  other arithmetic: 11.9 us -> 15.1 us
    ppermute x4, waiting for transfers between devices: 0.01 us -> 27.7 us  [fetch_rows(): remotes.append(lax.ppermute(piece, 'band', swap))]
    ppermute x8 -> x7, waiting for transfers between devices: 9.31 us -> 22.1 us  [the longest x4 20.1 us: across(): lax.ppermute(leaves, 'mem', pairs(members, bit))]
    unnamed x32 -> x27, local copies, waits for them, and re-layouts: 12.2 us -> 4.28 us
    ppermute x10 -> x8, waiting for transfers between devices: 31.8 us -> 24 us  [halved(): lax.ppermute(leaves, 'mem', pairs(members, bit))]
    pallas_call x8 -> x7, Pallas kernels: 63.6 us -> 68.5 us  [the longest x4 58.3 us: window_tensor(): pl.pallas_call(functools.partial(window_kernel, window, len(waits)), out_...]
    ppermute x8, starting transfers between devices: 0.81 us -> 4.95 us  [doubled(): beside = lax.ppermute(part, 'mem', pairs(members, bit))]
    dynamic_slice x3 -> x0, local copies, waits for them, and re-layouts: 3.12 us -> none  [the longest x2 2.21 us: by_levels(): lax.dynamic_slice_in_dim(outgoing, choose(1 - band, window.row_at), windo...]
    add x20 -> x12, other arithmetic: 8.58 us -> 10.9 us  [the longest x8 7.7 us: total(): sum((lax.dynamic_slice_in_dim(part, which * half, half, axis=2) for part...]
  transfers between devices with their start and end apart: 40 -> 35, of which waited for: 17 -> 15; matrix products, arithmetic and copies ran while one was open for 7% -> 6% of each run, Pallas kernels for 31% -> 30%
where the time goes in v7:
time: 220 us; the launch traced here: 219 us
  waiting for transfers between devices  95.9 us (44%)
  Pallas kernels  68.5 us (31%)
  starting transfers between devices  33.9 us (15%)
  other arithmetic  15.1 us (7%)
  local copies, waits for them, and re-layouts  5.42 us (2%)
    pallas_call x4, Pallas kernels, window_tensor(): pl.pallas_call(functools.partial(window_kernel, window, len(waits)), out_...  58.3 us
    ppermute x4, waiting for transfers between devices, fetch_rows(): remotes.append(lax.ppermute(piece, 'band', swap))  27.7 us
    ppermute x8, waiting for transfers between devices, halved(): lax.ppermute(leaves, 'mem', pairs(members, bit))  24 us
    ppermute x8, waiting for transfers between devices, doubled(): beside = lax.ppermute(part, 'mem', pairs(members, bit))  21.6 us
    ppermute x4, waiting for transfers between devices, across(): lax.ppermute(leaves, 'mem', pairs(members, bit))  20.1 us
    ppermute x8, starting transfers between devices, halved(): lax.ppermute(leaves, 'mem', pairs(members, bit))  13.9 us
    pallas_call x3, Pallas kernels, pieces_of(): pl.pallas_call(functools.partial(pieces_kernel, pieces, slots, count), in...  10.2 us
    add x8, other arithmetic, total(): sum((lax.dynamic_slice_in_dim(part, which * half, half, axis=2) for part...  7.7 us
  transfers between devices with their start and end apart: 35, of which 15 were waited for; matrix products, arithmetic and copies ran while one was open for 6% of the time, Pallas kernels for 30%

profile of v7, /device:TPU:0, one launch (start us, length us, event | category | flops | bytes accessed | tf_op | source)
XLA Modules:
  0.0 219.3 jit_solution(13037202645023416256)
XLA Ops:
  0.0 2.6 %pieces_of.4 = f32[2,136,640]{2,1,0:T(8,128)} custom-call(s32[1]{0:T(128)} %bitcast.4.level_ref, f32[2,2,640,640]{3,2,1,0:T(8,128)} %bitcast.49), custom_call_target="tpu_custom_call" | custom-call | bytes 5242880 | tf_op jit(solution)/shard_map/pieces_of/pallas_call | solution.py:217
  2.6 3.0 %collective-permute-start = (f32[2,136,640]{2,1,0:T(8,128)}, f32[2,136,640]{2,1,0:T(8,128)S(1)}, u32[]{:S(2)}, u32[]{:S(2)}) collective-permute-start(f32[2,136,640]{2,1,0:T(8,128)} %pieces_of.4), channel_id=1, source_target_pairs={{0,1},{1,0},{2,3},{3,2},{4,5},{5,4},{6,7},{7,6},{8,9},{9,8},{10,11... | collective-permute-start | bytes 2088968 | tf_op jit(solution)/shard_map/ppermute | solution.py:469
  5.6 3.7 %pieces_of.5 = (f32[2,128,640]{2,1,0:T(8,128)}, f32[2,128,640]{2,1,0:T(8,128)}, f32[2,128,640]{2,1,0:T(8,128)}, f32[2,120,640]{2,1,0:T(8,128)}) custom-call(s32[1]{0:T(128)} %bitcast.4.level_ref, f32[2,2,640,640]{3,2,1,0:T(8,128)} %bitcast.50), custom_call_target="tpu_custom_call" | custom-call | bytes 10485760 | tf_op jit(solution)/shard_map/pieces_of/pallas_call | solution.py:217
  9.3 4.0 %pieces_of.3 = (f32[2,136,640]{2,1,0:T(8,128)}, f32[2,128,640]{2,1,0:T(8,128)}, f32[2,128,640]{2,1,0:T(8,128)}, f32[2,128,640]{2,1,0:T(8,128)}, f32[2,120,640]{2,1,0:T(8,128)}) custom-call(s32[1]{0:T(128)} %bitcast.level_ref, f32[2,2,640,640]{3,2,1,0:T(8,128)} %bitcast.51), custom_call_target="tpu_custom_call" | custom-call | bytes 13107200 | tf_op jit(solution)/shard_map/pieces_of/pallas_call | solution.py:217
  14.1 21.4 %collective-permute-done.1.refs_1_.refs_5_ = f32[2,128,640]{2,1,0:T(8,128)S(1)} collective-permute-done((f32[2,128,640]{2,1,0:T(8,128)}, f32[2,128,640]{2,1,0:T(8,128)S(1)}, u32[]{:S(2)}, u32[]{:S(2)}) %collective-permute-start.1) | collective-permute-done | bytes 655392 | tf_op jit(solution)/shard_map/ppermute | solution.py:474
  35.4 0.8 copy-done.6
  36.3 1.7 collective-permute-start.19
  38.0 0.9 copy-done.4
  39.2 20.9 %window_tensor.4 = (f32[3,10,64,128]{3,2,1,0:T(8,128)}, f32[3,10,64,128]{3,2,1,0:T(8,128)}, f32[3,10,64,128]{3,2,1,0:T(8,128)}, f32[3,10,64,128]{3,2,1,0:T(8,128)}, f32[2,10,16,128]{3,2,1,0:T(8,128)}) custom-call(s32[3]{0:T(128)} %pad_add_fusion.refs_0_, bf16[4,640,640]{2,1,0:T(8,128)(2,1)} %constant.167.clone.refs_1_, ...), custom_call_target="tpu_custom_call" | custom-call | flops 20761804800 | bytes 9912320 | tf_op jit(solution)/shard_map/window_tensor/pallas_call | solution.py:419
  60.1 6.3 %collective-permute-done.8.refs_1_.refs_3_ = f32[2,128,640]{2,1,0:T(8,128)S(1)} collective-permute-done((f32[2,128,640]{2,1,0:T(8,128)}, f32[2,128,640]{2,1,0:T(8,128)S(1)}, u32[]{:S(2)}, u32[]{:S(2)}) %collective-permute-start.8) | collective-permute-done | bytes 655392 | tf_op jit(solution)/shard_map/ppermute | solution.py:474
  67.3 12.5 %window_tensor.5 = (f32[3,10,32,128]{3,2,1,0:T(8,128)}, f32[3,10,32,128]{3,2,1,0:T(8,128)}, f32[3,10,32,128]{3,2,1,0:T(8,128)}, f32[3,10,32,128]{3,2,1,0:T(8,128)}, f32[2,10,16,128]{3,2,1,0:T(8,128)}) custom-call(s32[3]{0:T(128)} %pad_add_fusion.refs_0_, bf16[4,640,640]{2,1,0:T(8,128)(2,1)} %constant.167.clone.refs_1_, ...), custom_call_target="tpu_custom_call" | custom-call | flops 10066329600 | bytes 6553600 | tf_op jit(solution)/shard_map/window_tensor/pallas_call | solution.py:419
  80.4 1.1 add.258.refs_4_
  82.0 1.5 collective-permute-start.11
  83.5 12.5 %window_tensor.6 = (f32[3,10,32,128]{3,2,1,0:T(8,128)}, f32[3,10,32,128]{3,2,1,0:T(8,128)}, f32[3,10,32,128]{3,2,1,0:T(8,128)}, f32[3,10,32,128]{3,2,1,0:T(8,128)}, f32[2,10,16,128]{3,2,1,0:T(8,128)}) custom-call(s32[3]{0:T(128)} %pad_add_fusion.refs_0_, bf16[4,640,640]{2,1,0:T(8,128)(2,1)} %constant.167.clone.refs_1_, ...), custom_call_target="tpu_custom_call" | custom-call | flops 10066329600 | bytes 6553600 | tf_op jit(solution)/shard_map/window_tensor/pallas_call | solution.py:419
  97.3 1.3 dynamic-slice_add_fusion.7
  98.6 1.6 collective-permute-start.12
  100.2 2.0 add.290
  102.1 1.5 collective-permute-start.22
  103.7 2.6 %collective-permute-done.12 = f32[3,10,16,128]{3,2,1,0:T(8,128)S(1)} collective-permute-done((f32[3,10,16,128]{3,2,1,0:T(8,128)S(1)}, f32[3,10,16,128]{3,2,1,0:T(8,128)S(1)}, u32[]{:S(2)}, u32[]{:S(2)}) %collective-permute-start.12) | collective-permute-done | bytes 245792 | tf_op jit(solution)/shard_map/ppermute | solution.py:490
  106.3 1.4 collective-permute-start.25
  108.4 2.6 %collective-permute-start.13 = (f32[3,10,8,128]{3,2,1,0:T(8,128)}, f32[3,10,8,128]{3,2,1,0:T(8,128)}, u32[]{:S(2)}, u32[]{:S(2)}) collective-permute-start(f32[3,10,8,128]{3,2,1,0:T(8,128)} %dynamic-slice_add_fusion.11), channel_id=1, source_target_pairs={{0,16},{2,18},{4,20},{6,22},{8,24},{10,26},{12,28},{14,30},{16,0},... | collective-permute-start | bytes 368648 | tf_op jit(solution)/shard_map/ppermute | solution.py:490
  111.0 20.1 %collective-permute-done.22 = f32[3,10,32,128]{3,2,1,0:T(8,128)} collective-permute-done((f32[3,10,32,128]{3,2,1,0:T(8,128)}, f32[3,10,32,128]{3,2,1,0:T(8,128)}, u32[]{:S(2)}, u32[]{:S(2)}) %collective-permute-start.22) | collective-permute-done | bytes 491552 | tf_op jit(solution)/shard_map/ppermute | solution.py:495
  131.1 2.3 %dynamic-slice_add_fusion.5 = (f32[3,10,16,128]{3,2,1,0:T(8,128)S(1)}, f32[3,10,16,128]{3,2,1,0:T(8,128)}) fusion(f32[3,10,32,128]{3,2,1,0:T(8,128)} %collective-permute-done.22, s32[]{:T(128)S(6)} %select_n.228, f32[3,10,32,128]{3,2,1,0:T(8,128)} %collective-permute-done.20, f32[3,10,32,128]{3,2,1,0:T(8,128)} %get-tuple-element.51, s32[]{:T(128)S(6)} %select_n.230), kind=kLoop, calls=%fused_computation.23 | loop fusion | flops 245760 | bytes 1966088 | tf_op jit(solution)/shard_map/add | solution.py:487
  133.3 1.6 collective-permute-start.23
  134.9 2.3 %dynamic-slice_add_fusion.1 = (f32[3,10,32,128]{3,2,1,0:T(8,128)S(1)}, f32[3,10,32,128]{3,2,1,0:T(8,128)}) fusion(f32[3,10,64,128]{3,2,1,0:T(8,128)} %collective-permute-done.4, s32[]{:T(128)S(6)} %select_n.224, f32[3,10,64,128]{3,2,1,0:T(8,128)S(1)} %collective-permute-done.2, f32[3,10,64,128]{3,2,1,0:T(8,128)S(1)} %copy-done.1, s32[]{:T(128)S(6)} %select_n.226), kind=kLoop, calls=%fused_computation.15 | loop fusion | flops 491520 | bytes 3932168 | tf_op jit(solution)/shard_map/add | solution.py:487
  137.7 12.4 %window_tensor.7 = (f32[3,10,32,128]{3,2,1,0:T(8,128)}, f32[3,10,32,128]{3,2,1,0:T(8,128)}, f32[3,10,32,128]{3,2,1,0:T(8,128)}, f32[3,10,32,128]{3,2,1,0:T(8,128)}) custom-call(s32[3]{0:T(128)} %pad_add_fusion.refs_0_, bf16[4,640,640]{2,1,0:T(8,128)(2,1)} %constant.167.clone.refs_1_, f32[2,120,640]{2,1,0:T(8,128)} %get-tuple-element.55.refs_2_, ...), custom_call_target="tpu_custom_call" | custom-call | flops 9437184000 | bytes 6471680 | tf_op jit(solution)/shard_map/window_tensor/pallas_call | solution.py:419
  150.6 0.9 multiply_bitcast_fusion.3
  151.6 2.7 %collective-permute-start.6 = (f32[3,10,16,128]{3,2,1,0:T(8,128)S(1)}, f32[3,10,16,128]{3,2,1,0:T(8,128)S(1)}, u32[]{:S(2)}, u32[]{:S(2)}) collective-permute-start(f32[3,10,16,128]{3,2,1,0:T(8,128)S(1)} %dynamic-slice_add_fusion.8), channel_id=1, source_target_pairs={{0,16},{2,18},{4,20},{6,22},{8,24},{10,26},{12,28},{14,30},{16,0},... | collective-permute-start | bytes 737288 | tf_op jit(solution)/shard_map/ppermute | solution.py:490
  154.3 0.9 collective-permute-start.14
  155.2 0.9 dynamic-slice_add_fusion.10
  157.3 12.0 %collective-permute-done.6 = f32[3,10,16,128]{3,2,1,0:T(8,128)S(1)} collective-permute-done((f32[3,10,16,128]{3,2,1,0:T(8,128)S(1)}, f32[3,10,16,128]{3,2,1,0:T(8,128)S(1)}, u32[]{:S(2)}, u32[]{:S(2)}) %collective-permute-start.6) | collective-permute-done | bytes 245792 | tf_op jit(solution)/shard_map/ppermute | solution.py:490
  169.5 1.6 collective-permute-start.7
  171.1 0.9 multiply_bitcast_fusion.2
  172.1 2.0 collective-permute-done.7
  174.4 3.3 %collective-permute-start.29 = (f32[3,10,16,128]{3,2,1,0:T(8,128)S(1)}, f32[3,10,16,128]{3,2,1,0:T(8,128)S(1)}, u32[]{:S(2)}, u32[]{:S(2)}) collective-permute-start(f32[3,10,16,128]{3,2,1,0:T(8,128)S(1)} %get-tuple-element.68), channel_id=1, source_target_pairs={{0,8},{2,10},{4,12},{6,14},{8,0},{10,2},{12,4},{14,6},{16,24},{18,... | collective-permute-start | bytes 737288 | tf_op jit(solution)/shard_map/ppermute | solution.py:490
  177.7 5.9 %collective-permute-done.29 = f32[3,10,16,128]{3,2,1,0:T(8,128)S(1)} collective-permute-done((f32[3,10,16,128]{3,2,1,0:T(8,128)S(1)}, f32[3,10,16,128]{3,2,1,0:T(8,128)S(1)}, u32[]{:S(2)}, u32[]{:S(2)}) %collective-permute-start.29) | collective-permute-done | bytes 245792 | tf_op jit(solution)/shard_map/ppermute | solution.py:490
  183.6 1.4 collective-permute-start.30
  185.1 2.1 collective-permute-start.16
  187.2 3.4 %collective-permute-done.30 = f32[3,10,8,128]{3,2,1,0:T(8,128)S(1)} collective-permute-done((f32[3,10,8,128]{3,2,1,0:T(8,128)S(1)}, f32[3,10,8,128]{3,2,1,0:T(8,128)S(1)}, u32[]{:S(2)}, u32[]{:S(2)}) %collective-permute-start.30) | collective-permute-done | bytes 122912 | tf_op jit(solution)/shard_map/ppermute | solution.py:490
  190.7 1.6 collective-permute-start.31
  192.3 2.2 %collective-permute-done.16 = f32[2,24,1280]{2,1,0:T(8,128)S(1)} collective-permute-done((f32[2,24,1280]{2,1,0:T(8,128)S(1)}, f32[2,24,1280]{2,1,0:T(8,128)S(1)}, u32[]{:S(2)}, u32[]{:S(2)}) %collective-permute-start.16) | collective-permute-done | bytes 245792 | tf_op jit(solution)/shard_map/ppermute | solution.py:501
  195.0 2.1 collective-permute-done.31
  197.2 5.2 %collective-permute-done.32 = f32[2,16,1280]{2,1,0:T(8,128)S(1)} collective-permute-done((f32[2,16,1280]{2,1,0:T(8,128)S(1)}, f32[2,16,1280]{2,1,0:T(8,128)S(1)}, u32[]{:S(2)}, u32[]{:S(2)}) %collective-permute-start.32) | collective-permute-done | bytes 163872 | tf_op jit(solution)/shard_map/ppermute | solution.py:501
  202.9 5.8 %collective-permute-done.17 = f32[4,24,1280]{2,1,0:T(8,128)S(1)} collective-permute-done((f32[4,24,1280]{2,1,0:T(8,128)S(1)}, f32[4,24,1280]{2,1,0:T(8,128)S(1)}, u32[]{:S(2)}, u32[]{:S(2)}) %collective-permute-start.17) | collective-permute-done | bytes 491552 | tf_op jit(solution)/shard_map/ppermute | solution.py:501
  208.9 4.2 %collective-permute-done.33 = f32[4,16,1280]{2,1,0:T(8,128)S(1)} collective-permute-done((f32[4,16,1280]{2,1,0:T(8,128)S(1)}, f32[4,16,1280]{2,1,0:T(8,128)S(1)}, u32[]{:S(2)}, u32[]{:S(2)}) %collective-permute-start.33) | collective-permute-done | bytes 327712 | tf_op jit(solution)/shard_map/ppermute | solution.py:501
  213.2 2.1 collective-permute-done.34
  216.7 1.7 copy-done
  218.4 0.9 fusion
  (97 shorter events, 10.5 us)
Async XLA Ops:
  2.6 35.5 %collective-permute-start = (f32[2,136,640]{2,1,0:T(8,128)}, f32[2,136,640]{2,1,0:T(8,128)S(1)}, u32[]{:S(2)}, u32[]{:S(2)}) collective-permute-start(f32[2,136,640]{2,1,0:T(8,128)} %pieces_of.4), channel_id=1, source_target_pairs={{0,1},{1,0},{2,3},{3,2},{4,5},{5,4},{6,7},{7,6},{8,9},{9,8},{10,11... | collective-permute-start | bytes 2088968 | tf_op jit(solution)/shard_map/ppermute | solution.py:469
  9.2 26.2 %collective-permute-start.1 = (f32[2,128,640]{2,1,0:T(8,128)}, f32[2,128,640]{2,1,0:T(8,128)S(1)}, u32[]{:S(2)}, u32[]{:S(2)}) collective-permute-start(f32[2,128,640]{2,1,0:T(8,128)} %get-tuple-element.35), channel_id=1, source_target_pairs={{0,1},{1,0},{2,3},{3,2},{4,5},{5,4},{6,7},{7,6},{8,9},{9,8},{10,11... | collective-permute-start | bytes 1966088 | tf_op jit(solution)/shard_map/ppermute | solution.py:474
  35.4 0.8 copy-start.6
  36.3 47.3 %collective-permute-start.19 = (f32[2,128,640]{2,1,0:T(8,128)}, f32[2,128,640]{2,1,0:T(8,128)}, u32[]{:S(2)}, u32[]{:S(2)}) collective-permute-start(f32[2,128,640]{2,1,0:T(8,128)} %gated.4.refs_7_), channel_id=1, source_target_pairs={{0,1},{1,0},{2,3},{3,2},{4,5},{5,4},{6,7},{7,6},{8,9},{9,8},{10,11... | collective-permute-start | bytes 1966088 | tf_op jit(solution)/shard_map/ppermute | solution.py:474
  38.0 0.9 copy-start.4
  38.9 27.6 %collective-permute-start.8 = (f32[2,128,640]{2,1,0:T(8,128)}, f32[2,128,640]{2,1,0:T(8,128)S(1)}, u32[]{:S(2)}, u32[]{:S(2)}) collective-permute-start(f32[2,128,640]{2,1,0:T(8,128)} %gated.3.refs_6_), channel_id=1, source_target_pairs={{0,1},{1,0},{2,3},{3,2},{4,5},{5,4},{6,7},{7,6},{8,9},{9,8},{10,11... | collective-permute-start | bytes 1966088 | tf_op jit(solution)/shard_map/ppermute | solution.py:474
  60.0 20.3 %collective-permute-start.3 = (f32[3,10,64,128]{3,2,1,0:T(8,128)}, f32[3,10,64,128]{3,2,1,0:T(8,128)S(1)}, u32[]{:S(2)}, u32[]{:S(2)}) collective-permute-start(f32[3,10,64,128]{3,2,1,0:T(8,128)} %get-tuple-element.41), channel_id=1, source_target_pairs={{0,2},{2,0},{4,6},{6,4},{8,10},{10,8},{12,14},{14,12},{16,18},{18,... | collective-permute-start | bytes 2949128 | tf_op jit(solution)/shard_map/ppermute | solution.py:525
  66.4 0.8 copy-start.5
  67.3 13.1 %copy-start.3 = (f32[3,10,64,128]{3,2,1,0:T(8,128)S(1)}, f32[3,10,64,128]{3,2,1,0:T(8,128)}, u32[]{:S(2)}) copy-start(f32[3,10,64,128]{3,2,1,0:T(8,128)} %get-tuple-element.40) | copy-start | bytes 2949124
  79.8 2.2 copy-start.12
  79.8 2.1 collective-permute-start.10
  79.9 17.4 %collective-permute-start.9 = (f32[3,10,32,128]{3,2,1,0:T(8,128)}, f32[3,10,32,128]{3,2,1,0:T(8,128)S(1)}, u32[]{:S(2)}, u32[]{:S(2)}) collective-permute-start(f32[3,10,32,128]{3,2,1,0:T(8,128)} %get-tuple-element.46), channel_id=1, source_target_pairs={{0,2},{2,0},{4,6},{6,4},{8,10},{10,8},{12,14},{14,12},{16,18},{18,... | collective-permute-start | bytes 1474568 | tf_op jit(solution)/shard_map/ppermute | solution.py:526
  82.0 14.1 %copy-start.7 = (f32[3,10,32,128]{3,2,1,0:T(8,128)}, f32[3,10,32,128]{3,2,1,0:T(8,128)S(1)}, u32[]{:S(2)}) copy-start(f32[3,10,32,128]{3,2,1,0:T(8,128)S(1)} %add.275.refs_5_) | copy-start | bytes 1474564
  82.0 15.2 %collective-permute-start.11 = (f32[3,10,32,128]{3,2,1,0:T(8,128)S(1)}, f32[3,10,32,128]{3,2,1,0:T(8,128)}, u32[]{:S(2)}, u32[]{:S(2)}) collective-permute-start(f32[3,10,32,128]{3,2,1,0:T(8,128)S(1)} %add.275.refs_5_), channel_id=1, source_target_pairs={{0,4},{2,6},{4,0},{6,2},{8,12},{10,14},{12,8},{14,10},{16,20},{18,... | collective-permute-start | bytes 1474568 | tf_op jit(solution)/shard_map/ppermute | solution.py:495
  83.5 13.1 %copy-start.2 = (f32[3,10,64,128]{3,2,1,0:T(8,128)S(1)}, f32[3,10,64,128]{3,2,1,0:T(8,128)}, u32[]{:S(2)}) copy-start(f32[3,10,64,128]{3,2,1,0:T(8,128)} %add.258.refs_4_) | copy-start | bytes 2949124
  83.5 13.7 %copy-start.8 = (f32[3,10,32,128]{3,2,1,0:T(8,128)S(1)}, f32[3,10,32,128]{3,2,1,0:T(8,128)}, u32[]{:S(2)}) copy-start(f32[3,10,32,128]{3,2,1,0:T(8,128)} %get-tuple-element.45) | copy-start | bytes 1474564
  96.1 4.0 %collective-permute-start.21 = (f32[3,10,32,128]{3,2,1,0:T(8,128)}, f32[3,10,32,128]{3,2,1,0:T(8,128)}, u32[]{:S(2)}, u32[]{:S(2)}) collective-permute-start(f32[3,10,32,128]{3,2,1,0:T(8,128)} %get-tuple-element.54), channel_id=1, source_target_pairs={{0,2},{2,0},{4,6},{6,4},{8,10},{10,8},{12,14},{14,12},{16,18},{18,... | collective-permute-start | bytes 1474568 | tf_op jit(solution)/shard_map/ppermute | solution.py:525
  96.2 38.7 %collective-permute-start.2 = (f32[3,10,64,128]{3,2,1,0:T(8,128)}, f32[3,10,64,128]{3,2,1,0:T(8,128)S(1)}, u32[]{:S(2)}, u32[]{:S(2)}) collective-permute-start(f32[3,10,64,128]{3,2,1,0:T(8,128)} %get-tuple-element.39), channel_id=1, source_target_pairs={{0,2},{2,0},{4,6},{6,4},{8,10},{10,8},{12,14},{14,12},{16,18},{18,... | collective-permute-start | bytes 2949128 | tf_op jit(solution)/shard_map/ppermute | solution.py:526
  96.7 38.2 %collective-permute-start.4 = (f32[3,10,64,128]{3,2,1,0:T(8,128)S(1)}, f32[3,10,64,128]{3,2,1,0:T(8,128)}, u32[]{:S(2)}, u32[]{:S(2)}) collective-permute-start(f32[3,10,64,128]{3,2,1,0:T(8,128)S(1)} %copy-done.2), channel_id=1, source_target_pairs={{0,4},{2,6},{4,0},{6,2},{8,12},{10,14},{12,8},{14,10},{16,20},{18,... | collective-permute-start | bytes 2949128 | tf_op jit(solution)/shard_map/ppermute | solution.py:495
  97.3 2.9 %copy-start.10 = (f32[3,10,32,128]{3,2,1,0:T(8,128)S(1)}, f32[3,10,32,128]{3,2,1,0:T(8,128)}, u32[]{:S(2)}) copy-start(f32[3,10,32,128]{3,2,1,0:T(8,128)} %get-tuple-element.53) | copy-start | bytes 1474564
  98.6 7.7 %collective-permute-start.12 = (f32[3,10,16,128]{3,2,1,0:T(8,128)S(1)}, f32[3,10,16,128]{3,2,1,0:T(8,128)S(1)}, u32[]{:S(2)}, u32[]{:S(2)}) collective-permute-start(f32[3,10,16,128]{3,2,1,0:T(8,128)S(1)} %get-tuple-element.70), channel_id=1, source_target_pairs={{0,8},{2,10},{4,12},{6,14},{8,0},{10,2},{12,4},{14,6},{16,24},{18,... | collective-permute-start | bytes 737288 | tf_op jit(solution)/shard_map/ppermute | solution.py:490
  100.1 8.2 %collective-permute-start.20 = (f32[3,10,32,128]{3,2,1,0:T(8,128)}, f32[3,10,32,128]{3,2,1,0:T(8,128)}, u32[]{:S(2)}, u32[]{:S(2)}) collective-permute-start(f32[3,10,32,128]{3,2,1,0:T(8,128)} %get-tuple-element.52), channel_id=1, source_target_pairs={{0,2},{2,0},{4,6},{6,4},{8,10},{10,8},{12,14},{14,12},{16,18},{18,... | collective-permute-start | bytes 1474568 | tf_op jit(solution)/shard_map/ppermute | solution.py:526
  100.2 34.8 %copy-start.1 = (f32[3,10,64,128]{3,2,1,0:T(8,128)S(1)}, f32[3,10,64,128]{3,2,1,0:T(8,128)}, u32[]{:S(2)}) copy-start(f32[3,10,64,128]{3,2,1,0:T(8,128)} %get-tuple-element.38) | copy-start | bytes 2949124
  102.1 28.9 %collective-permute-start.22 = (f32[3,10,32,128]{3,2,1,0:T(8,128)}, f32[3,10,32,128]{3,2,1,0:T(8,128)}, u32[]{:S(2)}, u32[]{:S(2)}) collective-permute-start(f32[3,10,32,128]{3,2,1,0:T(8,128)} %add.290), channel_id=1, source_target_pairs={{0,4},{2,6},{4,0},{6,2},{8,12},{10,14},{12,8},{14,10},{16,20},{18,... | collective-permute-start | bytes 1474568 | tf_op jit(solution)/shard_map/ppermute | solution.py:495
  106.3 31.4 %collective-permute-start.25 = (f32[2,120,640]{2,1,0:T(8,128)}, f32[2,120,640]{2,1,0:T(8,128)}, u32[]{:S(2)}, u32[]{:S(2)}) collective-permute-start(f32[2,120,640]{2,1,0:T(8,128)} %gated.5.refs_4_), channel_id=1, source_target_pairs={{0,1},{1,0},{2,3},{3,2},{4,5},{5,4},{6,7},{7,6},{8,9},{9,8},{10,11... | collective-permute-start | bytes 1843208 | tf_op jit(solution)/shard_map/ppermute | solution.py:474
  108.4 42.3 %collective-permute-start.13 = (f32[3,10,8,128]{3,2,1,0:T(8,128)}, f32[3,10,8,128]{3,2,1,0:T(8,128)}, u32[]{:S(2)}, u32[]{:S(2)}) collective-permute-start(f32[3,10,8,128]{3,2,1,0:T(8,128)} %dynamic-slice_add_fusion.11), channel_id=1, source_target_pairs={{0,16},{2,18},{4,20},{6,22},{8,24},{10,26},{12,28},{14,30},{16,0},... | collective-permute-start | bytes 368648 | tf_op jit(solution)/shard_map/ppermute | solution.py:490
  133.3 21.9 %collective-permute-start.23 = (f32[3,10,16,128]{3,2,1,0:T(8,128)}, f32[3,10,16,128]{3,2,1,0:T(8,128)}, u32[]{:S(2)}, u32[]{:S(2)}) collective-permute-start(f32[3,10,16,128]{3,2,1,0:T(8,128)} %get-tuple-element.66), channel_id=1, source_target_pairs={{0,8},{2,10},{4,12},{6,14},{8,0},{10,2},{12,4},{14,6},{16,24},{18,... | collective-permute-start | bytes 737288 | tf_op jit(solution)/shard_map/ppermute | solution.py:490
  137.2 14.4 %collective-permute-start.5 = (f32[3,10,32,128]{3,2,1,0:T(8,128)}, f32[3,10,32,128]{3,2,1,0:T(8,128)S(1)}, u32[]{:S(2)}, u32[]{:S(2)}) collective-permute-start(f32[3,10,32,128]{3,2,1,0:T(8,128)} %get-tuple-element.62.refs_4_), channel_id=1, source_target_pairs={{0,8},{2,10},{4,12},{6,14},{8,0},{10,2},{12,4},{14,6},{16,24},{18,... | collective-permute-start | bytes 1474568 | tf_op jit(solution)/shard_map/ppermute | solution.py:490
  150.1 6.5 %copy-start.11 = (f32[3,10,32,128]{3,2,1,0:T(8,128)S(1)}, f32[3,10,32,128]{3,2,1,0:T(8,128)}, u32[]{:S(2)}) copy-start(f32[3,10,32,128]{3,2,1,0:T(8,128)} %get-tuple-element.59) | copy-start | bytes 1474564
  150.1 6.5 %collective-permute-start.27 = (f32[3,10,32,128]{3,2,1,0:T(8,128)}, f32[3,10,32,128]{3,2,1,0:T(8,128)S(1)}, u32[]{:S(2)}, u32[]{:S(2)}) collective-permute-start(f32[3,10,32,128]{3,2,1,0:T(8,128)} %get-tuple-element.60), channel_id=1, source_target_pairs={{0,2},{2,0},{4,6},{6,4},{8,10},{10,8},{12,14},{14,12},{16,18},{18,... | collective-permute-start | bytes 1474568 | tf_op jit(solution)/shard_map/ppermute | solution.py:525
  150.1 24.0 %collective-permute-start.26 = (f32[3,10,32,128]{3,2,1,0:T(8,128)}, f32[3,10,32,128]{3,2,1,0:T(8,128)S(1)}, u32[]{:S(2)}, u32[]{:S(2)}) collective-permute-start(f32[3,10,32,128]{3,2,1,0:T(8,128)} %get-tuple-element.58), channel_id=1, source_target_pairs={{0,2},{2,0},{4,6},{6,4},{8,10},{10,8},{12,14},{14,12},{16,18},{18,... | collective-permute-start | bytes 1474568 | tf_op jit(solution)/shard_map/ppermute | solution.py:526
  151.6 17.7 %collective-permute-start.6 = (f32[3,10,16,128]{3,2,1,0:T(8,128)S(1)}, f32[3,10,16,128]{3,2,1,0:T(8,128)S(1)}, u32[]{:S(2)}, u32[]{:S(2)}) collective-permute-start(f32[3,10,16,128]{3,2,1,0:T(8,128)S(1)} %dynamic-slice_add_fusion.8), channel_id=1, source_target_pairs={{0,16},{2,18},{4,20},{6,22},{8,24},{10,26},{12,28},{14,30},{16,0},... | collective-permute-start | bytes 737288 | tf_op jit(solution)/shard_map/ppermute | solution.py:490
  154.3 17.7 %collective-permute-start.14 = (f32[8,1280]{1,0:T(8,128)S(1)}, f32[8,1280]{1,0:T(8,128)S(1)}, u32[]{:S(2)}, u32[]{:S(2)}) collective-permute-start(f32[8,1280]{1,0:T(8,128)S(1)} %fusion.28), channel_id=1, source_target_pairs={{0,0},{1,2},{2,1},{3,3},{4,4},{5,6},{6,5},{7,7},{8,8},{9,10},{10,9... | collective-permute-start | bytes 122888 | tf_op jit(solution)/shard_map/ppermute | solution.py:545
  156.2 14.9 %collective-permute-start.24 = (f32[3,10,8,128]{3,2,1,0:T(8,128)S(1)}, f32[3,10,8,128]{3,2,1,0:T(8,128)S(1)}, u32[]{:S(2)}, u32[]{:S(2)}) collective-permute-start(f32[3,10,8,128]{3,2,1,0:T(8,128)S(1)} %dynamic-slice_add_fusion.10), channel_id=1, source_target_pairs={{0,16},{2,18},{4,20},{6,22},{8,24},{10,26},{12,28},{14,30},{16,0},... | collective-permute-start | bytes 368648 | tf_op jit(solution)/shard_map/ppermute | solution.py:490
  156.6 17.6 %copy-start.9 = (f32[3,10,32,128]{3,2,1,0:T(8,128)S(1)}, f32[3,10,32,128]{3,2,1,0:T(8,128)}, u32[]{:S(2)}) copy-start(f32[3,10,32,128]{3,2,1,0:T(8,128)} %get-tuple-element.57) | copy-start | bytes 1474564
  156.7 17.5 %collective-permute-start.28 = (f32[3,10,32,128]{3,2,1,0:T(8,128)S(1)}, f32[3,10,32,128]{3,2,1,0:T(8,128)S(1)}, u32[]{:S(2)}, u32[]{:S(2)}) collective-permute-start(f32[3,10,32,128]{3,2,1,0:T(8,128)S(1)} %add.302), channel_id=1, source_target_pairs={{0,4},{2,6},{4,0},{6,2},{8,12},{10,14},{12,8},{14,10},{16,20},{18,... | collective-permute-start | bytes 1474568 | tf_op jit(solution)/shard_map/ppermute | solution.py:495
  169.5 4.5 %collective-permute-start.7 = (f32[16,1280]{1,0:T(8,128)S(1)}, f32[16,1280]{1,0:T(8,128)S(1)}, u32[]{:S(2)}, u32[]{:S(2)}) collective-permute-start(f32[16,1280]{1,0:T(8,128)S(1)} %bitcast.54), channel_id=1, source_target_pairs={{0,1},{1,0},{2,3},{3,2},{4,5},{5,4},{6,7},{7,6},{8,9},{9,8},{10,11... | collective-permute-start | bytes 245768 | tf_op jit(solution)/shard_map/ppermute | solution.py:539
  174.1 11.0 %collective-permute-start.15 = (f32[1,24,1280]{2,1,0:T(8,128)S(1)}, f32[1,24,1280]{2,1,0:T(8,128)S(1)}, u32[]{:S(2)}, u32[]{:S(2)}) collective-permute-start(f32[1,24,1280]{2,1,0:T(8,128)S(1)} %maximum_bitcast_fusion.2), channel_id=1, source_target_pairs={{0,16},{2,18},{4,20},{6,22},{8,24},{10,26},{12,28},{14,30},{16,0},... | collective-permute-start | bytes 368648 | tf_op jit(solution)/shard_map/ppermute | solution.py:501
  174.4 9.3 %collective-permute-start.29 = (f32[3,10,16,128]{3,2,1,0:T(8,128)S(1)}, f32[3,10,16,128]{3,2,1,0:T(8,128)S(1)}, u32[]{:S(2)}, u32[]{:S(2)}) collective-permute-start(f32[3,10,16,128]{3,2,1,0:T(8,128)S(1)} %get-tuple-element.68), channel_id=1, source_target_pairs={{0,8},{2,10},{4,12},{6,14},{8,0},{10,2},{12,4},{14,6},{16,24},{18,... | collective-permute-start | bytes 737288 | tf_op jit(solution)/shard_map/ppermute | solution.py:490
  183.6 7.0 %collective-permute-start.30 = (f32[3,10,8,128]{3,2,1,0:T(8,128)S(1)}, f32[3,10,8,128]{3,2,1,0:T(8,128)S(1)}, u32[]{:S(2)}, u32[]{:S(2)}) collective-permute-start(f32[3,10,8,128]{3,2,1,0:T(8,128)S(1)} %dynamic-slice_add_fusion.9), channel_id=1, source_target_pairs={{0,16},{2,18},{4,20},{6,22},{8,24},{10,26},{12,28},{14,30},{16,0},... | collective-permute-start | bytes 368648 | tf_op jit(solution)/shard_map/ppermute | solution.py:490
  185.1 9.4 %collective-permute-start.16 = (f32[2,24,1280]{2,1,0:T(8,128)S(1)}, f32[2,24,1280]{2,1,0:T(8,128)S(1)}, u32[]{:S(2)}, u32[]{:S(2)}) collective-permute-start(f32[2,24,1280]{2,1,0:T(8,128)S(1)} %maximum_select_fusion.7), channel_id=1, source_target_pairs={{0,8},{2,10},{4,12},{6,14},{8,0},{10,2},{12,4},{14,6},{16,24},{18,... | collective-permute-start | bytes 737288 | tf_op jit(solution)/shard_map/ppermute | solution.py:501
  190.7 6.4 %collective-permute-start.31 = (f32[1,16,1280]{2,1,0:T(8,128)S(1)}, f32[1,16,1280]{2,1,0:T(8,128)S(1)}, u32[]{:S(2)}, u32[]{:S(2)}) collective-permute-start(f32[1,16,1280]{2,1,0:T(8,128)S(1)} %maximum_bitcast_fusion.3), channel_id=1, source_target_pairs={{0,16},{2,18},{4,20},{6,22},{8,24},{10,26},{12,28},{14,30},{16,0},... | collective-permute-start | bytes 245768 | tf_op jit(solution)/shard_map/ppermute | solution.py:501
  194.5 14.2 %collective-permute-start.17 = (f32[4,24,1280]{2,1,0:T(8,128)S(1)}, f32[4,24,1280]{2,1,0:T(8,128)S(1)}, u32[]{:S(2)}, u32[]{:S(2)}) collective-permute-start(f32[4,24,1280]{2,1,0:T(8,128)S(1)} %maximum_select_fusion.5), channel_id=1, source_target_pairs={{0,4},{2,6},{4,0},{6,2},{8,12},{10,14},{12,8},{14,10},{16,20},{18,... | collective-permute-start | bytes 1474568 | tf_op jit(solution)/shard_map/ppermute | solution.py:501
  197.1 5.4 %collective-permute-start.32 = (f32[2,16,1280]{2,1,0:T(8,128)S(1)}, f32[2,16,1280]{2,1,0:T(8,128)S(1)}, u32[]{:S(2)}, u32[]{:S(2)}) collective-permute-start(f32[2,16,1280]{2,1,0:T(8,128)S(1)} %maximum_select_fusion.8), channel_id=1, source_target_pairs={{0,8},{2,10},{4,12},{6,14},{8,0},{10,2},{12,4},{14,6},{16,24},{18,... | collective-permute-start | bytes 491528 | tf_op jit(solution)/shard_map/ppermute | solution.py:501
  202.5 10.5 %collective-permute-start.33 = (f32[4,16,1280]{2,1,0:T(8,128)S(1)}, f32[4,16,1280]{2,1,0:T(8,128)S(1)}, u32[]{:S(2)}, u32[]{:S(2)}) collective-permute-start(f32[4,16,1280]{2,1,0:T(8,128)S(1)} %maximum_select_fusion.6), channel_id=1, source_target_pairs={{0,4},{2,6},{4,0},{6,2},{8,12},{10,14},{12,8},{14,10},{16,20},{18,... | collective-permute-start | bytes 983048 | tf_op jit(solution)/shard_map/ppermute | solution.py:501
  208.8 6.6 %collective-permute-start.18 = (f32[8,24,1280]{2,1,0:T(8,128)S(1)}, f32[8,24,1280]{2,1,0:T(8,128)S(1)}, u32[]{:S(2)}, u32[]{:S(2)}) collective-permute-start(f32[8,24,1280]{2,1,0:T(8,128)S(1)} %maximum_select_fusion.3), channel_id=1, source_target_pairs={{0,2},{2,0},{4,6},{6,4},{8,10},{10,8},{12,14},{14,12},{16,18},{18,... | collective-permute-start | bytes 2949128 | tf_op jit(solution)/shard_map/ppermute | solution.py:501
  213.1 2.2 collective-permute-start.34
  216.7 1.7 copy-start

commit v8 on v7

--- a/solution.py
+++ b/solution.py
@@ -16,7 +16,8 @@
 LANE = 128
 VMEM_LIMIT = 60 * 1024 * 1024
 KERNEL_WORK = 8
-LAG = 1
+GROUP = 9
+AHEAD = ((), (0,), (1,), (2, 0))
 
 
 def padded(cells, sides, width):
@@ -156,7 +157,6 @@
         self.last = pieces[-1].index == count - 1
         self.width = LANE * len(pieces)
         self.extended = self.width + 2 * SUB
-        self.spread = self.extended // SUB
         self.places = []
         up = SUB if self.first else 2 * SUB
         for piece in pieces:
@@ -255,15 +255,16 @@
 
 def window_kernel(window, waits, *refs):
     refs = list(refs)
-    pieces, extended, spread = window.pieces, window.extended, window.spread
+    pieces, extended = window.pieces, window.extended
     place_ref, table_ref = refs[:2]
     local_refs, remote_refs = refs[2 : 2 + len(pieces)], refs[2 + len(pieces) : 2 + 2 * len(pieces)]
     refs = refs[2 + 2 * len(pieces) + waits :]
     carry_ref = None if window.first else refs.pop(0)
-    out_refs = [refs.pop(0) for _ in range(4)]
+    out_refs = [refs.pop(0) for _ in PARTS]
     carried_ref = None if window.last else refs.pop(0)
-    table, lhs_high, lhs_low, natural, wind, second, third, shift, results, carried, table_sem, out_sems = refs
+    table, lhs, wind, second, third, shift, results, carried, table_sem, out_sems = refs
     band, core, side = place_ref[0], place_ref[1], place_ref[2]
+    half = lhs.shape[1] // 2
 
     def at(pair):
         return multiple(choose(band, pair), SUB)
@@ -283,113 +284,114 @@
             even.append(jnp.concatenate([low[:, : 2 * LANE], high[:, : 2 * LANE], even_rest], axis=1))
             odd.append(jnp.concatenate([low[:, 2 * LANE : 4 * LANE], high[:, 2 * LANE : 4 * LANE], odd_rest], axis=1))
     for parity, parts in enumerate((even, odd)):
-        lhs = jnp.concatenate(parts)
-        lhs_high[parity] = lhs.astype(jnp.bfloat16)
-        lhs_low[parity] = (lhs - lhs_high[parity].astype(jnp.float32)).astype(jnp.bfloat16)
-
-    tiles = NLON // LANE
+        whole = jnp.concatenate(parts)
+        high = whole.astype(jnp.bfloat16)
+        lhs[parity, :half] = high
+        lhs[parity, half:] = (whole - high.astype(jnp.float32)).astype(jnp.bfloat16)
+
     for c in range(2):
-        for t in range(tiles):
-            if window.first:
-                natural[c, t, pl.ds(at((extended - SUB, 0)), SUB), :] = jnp.zeros((SUB, LANE), jnp.float32)
-            else:
-                natural[c, t, pl.ds(at((extended - 2 * SUB, 0)), 2 * SUB), :] = carry_ref[c, t]
-            if window.last:
-                natural[c, t, pl.ds(at((0, extended - SUB)), SUB), :] = jnp.zeros((SUB, LANE), jnp.float32)
+        if window.first:
+            wind[c, pl.ds(at((extended - SUB, 0)), SUB), :] = jnp.zeros((SUB, NLON), jnp.float32)
+        else:
+            wind[c, pl.ds(at((extended - 2 * SUB, 0)), 2 * SUB), :] = carry_ref[c]
+        if window.last:
+            wind[c, pl.ds(at((0, extended - SUB)), SUB), :] = jnp.zeros((SUB, NLON), jnp.float32)
     tables.wait()
 
     dot = functools.partial(jnp.dot, preferred_element_type=jnp.float32)
-    for start in range(0, tiles // 2, 2):
-        stop = min(start + 2, tiles // 2)
-        columns = slice(start * LANE, stop * LANE)
+    for start in range(0, NLON // 2, 2 * LANE):
+        stop = min(start + 2 * LANE, NLON // 2)
         sums = []
         for parity in range(2):
-            total = dot(lhs_high[parity], table[2 * parity, :, columns])
-            total += dot(lhs_low[parity], table[2 * parity, :, columns])
-            total += dot(lhs_high[parity], table[2 * parity + 1, :, columns])
-            sums.append(total)
+            both = dot(lhs[parity], table[2 * parity, :, start:stop])
+            sums.append(both[:half] + both[half:] + dot(lhs[parity, :half], table[2 * parity + 1, :, start:stop]))
         row = 0
         for piece, place in zip(pieces, window.places):
             rows = pl.ds(at(place), piece.rows)
             for c in range(2):
                 even_sum, odd_sum = (total[row : row + piece.rows] for total in sums)
                 row += piece.rows
-                for t in range(start, stop):
-                    lanes = slice((t - start) * LANE, (t - start + 1) * LANE)
-                    natural[c, t, rows, :] = even_sum[:, lanes] + odd_sum[:, lanes]
-                    natural[c, tiles // 2 + t, rows, :] = even_sum[:, lanes] - odd_sum[:, lanes]
+                wind[c, rows, start:stop] = even_sum + odd_sum
+                wind[c, rows, NLON // 2 + start : NLON // 2 + stop] = even_sum - odd_sum
 
     if not window.last:
         for c in range(2):
-            for t in range(tiles):
-                carried[c, t] = natural[c, t, pl.ds(at((0, extended - 2 * SUB)), 2 * SUB), :]
-        carry_on = pltpu.make_async_copy(carried, carried_ref, out_sems.at[4])
+            carried[c] = wind[c, pl.ds(at((0, extended - 2 * SUB)), 2 * SUB), :]
+        carry_on = pltpu.make_async_copy(carried, carried_ref, out_sems.at[len(PARTS)])
         carry_on.start()
 
-    def closed(field):
+    blocks = extended // SUB
+
+    def rows_of(block):
+        return pl.ds(multiple(block * SUB, SUB), SUB)
+
+    def slopes(field, first, number):
+        row = lax.broadcasted_iota(jnp.int32, (SUB, NLON), 0)
+        runs = []
         for c in range(2):
-            field[c, 0] = pltpu.roll(field[c, spread], 1, axis=0)
-            field[c, spread + 1] = pltpu.roll(field[c, 1], SUB - 1, axis=0)
-
-    def slopes(field, block):
-        return [(east_of(field[c, block]), field[c, block + 1] - field[c, block - 1]) for c in range(2)]
-
-    def each_block(body):
-        @pl.loop(0, spread // 2)
-        def _(pair):
-            body(2 * pair + 1)
-            body(2 * pair + 2)
-
-    def spread_out(block):
-        for c in range(2):
-            rows = pl.ds(block - 1, SUB, spread)
-            wind[c, block] = jnp.concatenate([natural[c, t, rows, :] for t in range(tiles)], axis=1)
-
-    each_block(spread_out)
-    closed(wind)
-
-    def second_slope(block):
-        u, v = wind[0, block], wind[1, block]
-        for c, (east, north) in enumerate(slopes(wind, block)):
-            second[c, block] = 0.25 * (u * east + v * north) - (u, v)[c]
-
-    each_block(second_slope)
-    closed(second)
-
-    def third_slope(block):
-        u, v = wind[0, block], wind[1, block]
-        for c, (east, north) in enumerate(slopes(second, block)):
-            third[c, block] = -(u, v)[c] - 0.25 * (u * east + v * north)
-
-    each_block(third_slope)
-    closed(third)
-
-    def whole_step(block):
-        u, v = wind[0, block], wind[1, block]
-        for c, (east, north) in enumerate(slopes(third, block)):
-            fourth = -(u, v)[c] - 0.5 * (u * east + v * north)
-            both = second[c, block] + third[c, block]
-            shift[c, block] = (2.0 * both + (fourth - (u, v)[c])) * (1.0 / 6.0)
-
-    each_block(whole_step)
-    closed(shift)
-
-    def entries(block):
-        (e0, n0), (e1, n1) = slopes(shift, block)
-        g_xx, g_xy, g_yx, g_yy = 1.0 + 0.5 * e0, 0.5 * n0, 0.5 * e1, 1.0 + 0.5 * n1
-        rows = pl.ds(block - 1, SUB, spread)
-        for n, entry in enumerate((g_xx * g_xx + g_yx * g_yx, g_xx * g_xy + g_yx * g_yy, g_xy * g_xy + g_yy * g_yy)):
-            for t in range(tiles):
-                results[n, t, rows, :] = entry[:, t * LANE : (t + 1) * LANE]
-
-    each_block(entries)
+            here = [field[c, rows_of(first + n), :] for n in range(number)]
+            before = field[c, rows_of(jnp.maximum(first - 1, 0)), :]
+            after = field[c, rows_of(jnp.minimum(first + number, blocks - 1)), :]
+            up = [pltpu.roll(x, SUB - 1, axis=0) for x in [*here, after]]
+            down = [pltpu.roll(x, 1, axis=0) for x in [before, *here]]
+            runs.append(
+                [
+                    (
+                        east_of(here[n]),
+                        jnp.where(row == SUB - 1, up[n + 1], up[n]) - jnp.where(row == 0, down[n], down[n + 1]),
+                    )
+                    for n in range(number)
+                ]
+            )
+        return zip(*runs)
+
+    def each_run(count, number, body):
+        @pl.loop(0, count // number)
+        def _(run):
+            body(run * number, number)
+
+    group = max(n for n in range(1, GROUP + 1) if blocks % n == 0)
+
+    def second_slope(first, number):
+        for n, pair in enumerate(slopes(wind, first, number)):
+            flow = [wind[c, rows_of(first + n), :] for c in range(2)]
+            for c, (east, north) in enumerate(pair):
+                second[c, rows_of(first + n), :] = 0.25 * (flow[0] * east + flow[1] * north) - flow[c]
+
+    def third_slope(first, number):
+        for n, pair in enumerate(slopes(second, first, number)):
+            flow = [wind[c, rows_of(first + n), :] for c in range(2)]
+            for c, (east, north) in enumerate(pair):
+                third[c, rows_of(first + n), :] = -flow[c] - 0.25 * (flow[0] * east + flow[1] * north)
+
+    def whole_step(first, number):
+        for n, pair in enumerate(slopes(third, first, number)):
+            here = rows_of(first + n)
+            flow = [wind[c, here, :] for c in range(2)]
+            for c, (east, north) in enumerate(pair):
+                fourth = -flow[c] - 0.5 * (flow[0] * east + flow[1] * north)
+                both = second[c, here, :] + third[c, here, :]
+                shift[c, here, :] = (2.0 * both + (fourth - flow[c])) * (1.0 / 6.0)
+
+    for body in (second_slope, third_slope, whole_step):
+        each_run(blocks, group, body)
+
+    def entries(first, number):
+        for n, ((e0, n0), (e1, n1)) in enumerate(slopes(shift, first + 1, number)):
+            g_xx, g_xy, g_yx, g_yy = 1.0 + 0.5 * e0, 0.5 * n0, 0.5 * e1, 1.0 + 0.5 * n1
+            here = rows_of(first + n)
+            results[0, here, :] = g_xx * g_xx + g_yx * g_yx
+            results[1, here, :] = g_xx * g_xy + g_yx * g_yy
+            results[2, here, :] = g_xy * g_xy + g_yy * g_yy
+
+    each_run(blocks - 2, 8, entries)
 
     quarter = window.width // 4
     copies = []
-    for n, (a, b) in enumerate(QUARTERS):
-        base = (2 * (core + a - 2 * core * a) + (side + b - 2 * side * b)) * quarter + SUB
-        rows = pl.ds(multiple(base, SUB), quarter)
-        copies.append(pltpu.make_async_copy(results.at[:, :, rows], out_refs[n], out_sems.at[n]))
+    for n, (a, b, p, of) in enumerate(PARTS):
+        base = (2 * (core + a - 2 * core * a) + (side + b - 2 * side * b)) * quarter + p * (quarter // of)
+        rows = pl.ds(multiple(base, SUB), quarter // of)
+        copies.append(pltpu.make_async_copy(results.at[:, rows], out_refs[n], out_sems.at[n]))
         copies[-1].start()
     for copy in copies:
         copy.wait()
@@ -397,11 +399,11 @@
         carry_on.wait()
 
 
-QUARTERS = ((0, 0), (0, 1), (1, 0), (1, 1))
+PARTS = ((0, 0, 0, 1), (0, 1, 0, 1), (1, 0, 0, 1), (1, 1, 0, 2), (1, 1, 1, 2))
 
 
 def window_tensor(window, place, table, local, remote, waits, carry):
-    depth, tiles = local[0].shape[2], NLON // LANE
+    depth = local[0].shape[2]
     vmem, hbm = pl.BlockSpec(memory_space=pltpu.VMEM), pl.BlockSpec(memory_space=pl.ANY)
     in_specs = [pl.BlockSpec(memory_space=pltpu.SMEM), hbm]
     in_specs += [vmem] * (len(local) + len(remote)) + [hbm] * len(waits)
@@ -409,13 +411,12 @@
     if not window.first:
         in_specs.append(vmem)
         operands.append(carry)
-    out_shape = [jax.ShapeDtypeStruct((3, tiles, window.width // 4, LANE), jnp.float32)] * 4
-    carried = (2, tiles, 2 * SUB, LANE)
+    out_shape = [jax.ShapeDtypeStruct((3, window.width // 4 // of, NLON), jnp.float32) for _, _, _, of in PARTS]
+    carried = (2, 2 * SUB, NLON)
     if not window.last:
         out_shape.append(jax.ShapeDtypeStruct(carried, jnp.float32))
-    field = pltpu.VMEM((2, window.spread + 2, SUB, NLON), jnp.float32)
+    field = pltpu.VMEM((2, window.extended, NLON), jnp.float32)
     rows = sum(piece.rows for piece in window.pieces)
-    lhs_shape = (2, 2 * rows, depth)
     out = pl.pallas_call(
         functools.partial(window_kernel, window, len(waits)),
         out_shape=out_shape,
@@ -423,17 +424,15 @@
         out_specs=[hbm] * len(out_shape),
         scratch_shapes=[
             pltpu.VMEM(table.shape, table.dtype),
-            pltpu.VMEM(lhs_shape, jnp.bfloat16),
-            pltpu.VMEM(lhs_shape, jnp.bfloat16),
-            pltpu.VMEM((2, tiles, window.extended, LANE), jnp.float32),
+            pltpu.VMEM((2, 4 * rows, depth), jnp.bfloat16),
             field,
             field,
             field,
             field,
-            pltpu.VMEM((3, tiles, window.extended, LANE), jnp.float32),
+            pltpu.VMEM((3, window.width, NLON), jnp.float32),
             pltpu.VMEM(carried, jnp.float32),
             pltpu.SemaphoreType.DMA,
-            pltpu.SemaphoreType.DMA((5,)),
+            pltpu.SemaphoreType.DMA((len(PARTS) + 1,)),
         ],
         compiler_params=pltpu.CompilerParams(vmem_limit_bytes=VMEM_LIMIT),
         cost_estimate=pl.CostEstimate(
@@ -443,7 +442,7 @@
         ),
         name="window_tensor",
     )(*operands)
-    return out[:4], (None if window.last else out[4])
+    return out[: len(PARTS)], (None if window.last else out[len(PARTS)])
 
 
 def pairs(members, bit):
@@ -480,11 +479,11 @@
     bits = [1 << n for n in range(members.bit_length() - 1)]
 
     def halved(parts_of, bit):
-        half = parts_of[0].shape[2] // 2
+        half = parts_of[0].shape[1] // 2
         mine = (member // bit) % 2
 
         def total(which):
-            return sum(lax.dynamic_slice_in_dim(part, which * half, half, axis=2) for part in parts_of)
+            return sum(lax.dynamic_slice_in_dim(part, which * half, half, axis=1) for part in parts_of)
 
         leaves = total(1 - mine)
         return [total(mine), lax.ppermute(leaves, "mem", pairs(members, bit))], leaves
@@ -514,26 +513,22 @@
         while len(remotes) < min(last + 3, count):
             before = len(remotes) - 2
             waits.append(fetch_rows(len(remotes), [remotes[before]] if carry is None else [remotes[before], carry]))
-        for j in range(k - LAG):
+        for j in AHEAD[k]:
             sums[j], left = advanced(sums[j], bits[done[j]])
             done[j] += 1
             waits.append(left)
         here = [piece.index for piece in window.pieces]
-        quarters, carry = window_tensor(
+        parts, carry = window_tensor(
             window, place, table, [local[p] for p in here], [remotes[p] for p in here], waits, carry
         )
-        first = lax.ppermute(quarters[3], "mem", pairs(members, bits[0]))
-        second = lax.ppermute(quarters[2], "mem", pairs(members, bits[0]))
-        sums.append([quarters[0], quarters[1], second, first])
+        swapped = [lax.ppermute(part, "mem", pairs(members, bits[0])) for part in reversed(parts[2:])]
+        sums.append([parts[0], parts[1], swapped[2], jnp.concatenate(swapped[1::-1], axis=1)])
         done.append(1)
     results = {}
     for k, window in enumerate(windows):
         for bit in bits[done[k] :]:
             sums[k], _ = advanced(sums[k], bit)
-        summed = sum(sums[k])
-        rows = summed.shape[2]
-        summed = summed.transpose(0, 2, 1, 3).reshape(3, rows, NLON)
-        results.setdefault(window.side, []).append(exponent_of(summed, members))
+        results.setdefault(window.side, []).append(exponent_of(sum(sums[k]), members))
 
     (other,), (both,) = results["other"], results["both"]
     other = lax.ppermute(other, "band", swap)

time: 220 us -> 233 us (1.059)
  waiting for transfers between devices: 95.9 us -> 115 us
  Pallas kernels: 68.5 us -> 63.9 us
    ppermute x4, waiting for transfers between devices: 27.7 us -> 45.4 us  [fetch_rows(): remotes.append(lax.ppermute(piece, 'band', swap))]
    ppermute x4, waiting for transfers between devices: 20.1 us -> 7.98 us  [across(): lax.ppermute(leaves, 'mem', pairs(members, bit))]
    ppermute x8, waiting for transfers between devices: 21.6 us -> 31.3 us  [doubled(): beside = lax.ppermute(part, 'mem', pairs(members, bit))]
    pallas_call x4, Pallas kernels: 58.3 us -> 53.7 us  [window_tensor(): pl.pallas_call(functools.partial(window_kernel, window, len(waits)), out_...]
    add x4, other arithmetic: 3.22 us -> 6.33 us  [across(): leaves = passed + passed_more]
    add x8, other arithmetic: 7.7 us -> 4.76 us  [total(): sum((lax.dynamic_slice_in_dim(part, which * half, half, axis=1) for part...]
    unnamed x27 -> x26, local copies, waits for them, and re-layouts: 4.28 us -> 5.97 us
  transfers between devices with their start and end apart: 35 -> 39, of which waited for: 15 -> 19; matrix products, arithmetic and copies ran while one was open for 6% -> 5% of each run, Pallas kernels for 30% -> 13%
where the time goes in v8:
time: 233 us
  waiting for transfers between devices  115 us (49%)
  Pallas kernels  63.9 us (27%)
  starting transfers between devices  33.2 us (14%)
  other arithmetic  13.4 us (6%)
  local copies, waits for them, and re-layouts  7.07 us (3%)
    pallas_call x4, Pallas kernels, window_tensor(): pl.pallas_call(functools.partial(window_kernel, window, len(waits)), out_...  53.7 us
    ppermute x4, waiting for transfers between devices, fetch_rows(): remotes.append(lax.ppermute(piece, 'band', swap))  45.4 us
    ppermute x8, waiting for transfers between devices, doubled(): beside = lax.ppermute(part, 'mem', pairs(members, bit))  31.3 us
    ppermute x8, waiting for transfers between devices, halved(): lax.ppermute(leaves, 'mem', pairs(members, bit))  25 us
    ppermute x8, starting transfers between devices, halved(): lax.ppermute(leaves, 'mem', pairs(members, bit))  11.9 us
    pallas_call x3, Pallas kernels, pieces_of(): pl.pallas_call(functools.partial(pieces_kernel, pieces, slots, count), in...  10.2 us
    ppermute x4, waiting for transfers between devices, across(): lax.ppermute(leaves, 'mem', pairs(members, bit))  7.98 us
    add x4, other arithmetic, across(): leaves = passed + passed_more  6.33 us
  transfers between devices with their start and end apart: 39, of which 19 were waited for; matrix products, arithmetic and copies ran while one was open for 5% of the time, Pallas kernels for 13%

profile of v8, /device:TPU:0, one launch (start us, length us, event | category | flops | bytes accessed | tf_op | source)
XLA Modules:
  0.0 232.8 jit_solution(11848327817528320932)
XLA Ops:
  0.0 2.6 %pieces_of.4 = f32[2,136,640]{2,1,0:T(8,128)} custom-call(s32[1]{0:T(128)} %bitcast.4.level_ref, f32[2,2,640,640]{3,2,1,0:T(8,128)} %bitcast.38), custom_call_target="tpu_custom_call" | custom-call | bytes 5242880 | tf_op jit(solution)/shard_map/pieces_of/pallas_call | solution.py:217
  2.6 3.0 %collective-permute-start = (f32[2,136,640]{2,1,0:T(8,128)}, f32[2,136,640]{2,1,0:T(8,128)S(1)}, u32[]{:S(2)}, u32[]{:S(2)}) collective-permute-start(f32[2,136,640]{2,1,0:T(8,128)} %pieces_of.4), channel_id=1, source_target_pairs={{0,1},{1,0},{2,3},{3,2},{4,5},{5,4},{6,7},{7,6},{8,9},{9,8},{10,11... | collective-permute-start | bytes 2088968 | tf_op jit(solution)/shard_map/ppermute | solution.py:468
  5.6 3.6 %pieces_of.5 = (f32[2,128,640]{2,1,0:T(8,128)}, f32[2,128,640]{2,1,0:T(8,128)}, f32[2,128,640]{2,1,0:T(8,128)}, f32[2,120,640]{2,1,0:T(8,128)}) custom-call(s32[1]{0:T(128)} %bitcast.4.level_ref, f32[2,2,640,640]{3,2,1,0:T(8,128)} %bitcast.39), custom_call_target="tpu_custom_call" | custom-call | bytes 10485760 | tf_op jit(solution)/shard_map/pieces_of/pallas_call | solution.py:217
  9.3 4.0 %pieces_of.3 = (f32[2,136,640]{2,1,0:T(8,128)}, f32[2,128,640]{2,1,0:T(8,128)}, f32[2,128,640]{2,1,0:T(8,128)}, f32[2,128,640]{2,1,0:T(8,128)}, f32[2,120,640]{2,1,0:T(8,128)}) custom-call(s32[1]{0:T(128)} %bitcast.level_ref, f32[2,2,640,640]{3,2,1,0:T(8,128)} %bitcast.40), custom_call_target="tpu_custom_call" | custom-call | bytes 13107200 | tf_op jit(solution)/shard_map/pieces_of/pallas_call | solution.py:217
  14.0 21.5 %collective-permute-done.1.refs_1_.refs_5_ = f32[2,128,640]{2,1,0:T(8,128)S(1)} collective-permute-done((f32[2,128,640]{2,1,0:T(8,128)}, f32[2,128,640]{2,1,0:T(8,128)S(1)}, u32[]{:S(2)}, u32[]{:S(2)}) %collective-permute-start.1) | collective-permute-done | bytes 655392 | tf_op jit(solution)/shard_map/ppermute | solution.py:473
  35.4 0.9 copy-done.6
  36.3 0.8 copy-done.3
  37.2 20.2 %window_tensor.4 = (f32[3,64,1280]{2,1,0:T(8,128)}, f32[3,64,1280]{2,1,0:T(8,128)}, f32[3,64,1280]{2,1,0:T(8,128)}, f32[3,32,1280]{2,1,0:T(8,128)}, f32[3,32,1280]{2,1,0:T(8,128)}, /*index=5*/f32[2,16,1280]{2,1,0:T(8,128)}) custom-call(s32[3]{0:T(128)} %pad_add_fusion.refs_0_, bf16[4,640,640]{2,1,0:T(8,128)(2,1)} %constant.167.clone.refs_1_, ...), custom_call_target="tpu_custom_call" | custom-call | flops 20761804800 | bytes 9912320 | tf_op jit(solution)/shard_map/window_tensor/pallas_call | solution.py:420
  58.0 1.7 collective-permute-start.9
  60.2 2.3 maximum_add_fusion.refs_5_
  62.5 12.2 %collective-permute-done.9.refs_1_.refs_3_ = f32[2,128,640]{2,1,0:T(8,128)S(1)} collective-permute-done((f32[2,128,640]{2,1,0:T(8,128)S(1)}, f32[2,128,640]{2,1,0:T(8,128)S(1)}, u32[]{:S(2)}, u32[]{:S(2)}) %collective-permute-start.9) | collective-permute-done | bytes 655392 | tf_op jit(solution)/shard_map/ppermute | solution.py:473
  75.5 11.1 %window_tensor.5 = (f32[3,32,1280]{2,1,0:T(8,128)}, f32[3,32,1280]{2,1,0:T(8,128)}, f32[3,32,1280]{2,1,0:T(8,128)}, f32[3,16,1280]{2,1,0:T(8,128)}, f32[3,16,1280]{2,1,0:T(8,128)}, /*index=5*/f32[2,16,1280]{2,1,0:T(8,128)}) custom-call(s32[3]{0:T(128)} %pad_add_fusion.refs_0_, bf16[4,640,640]{2,1,0:T(8,128)(2,1)} %constant.167.clone.refs_1_, ...), custom_call_target="tpu_custom_call" | custom-call | flops 10066329600 | bytes 6553600 | tf_op jit(solution)/shard_map/window_tensor/pallas_call | solution.py:420
  87.2 1.8 collective-permute-start.21
  89.0 1.5 collective-permute-start.5
  90.5 1.9 maximum_add_fusion.1.refs_4_
  92.4 11.8 %collective-permute-done.21.refs_3_ = f32[2,128,640]{2,1,0:T(8,128)S(1)} collective-permute-done((f32[2,128,640]{2,1,0:T(8,128)}, f32[2,128,640]{2,1,0:T(8,128)S(1)}, u32[]{:S(2)}, u32[]{:S(2)}) %collective-permute-start.21) | collective-permute-done | bytes 655392 | tf_op jit(solution)/shard_map/ppermute | solution.py:473
  105.0 11.3 %window_tensor.6 = (f32[3,32,1280]{2,1,0:T(8,128)}, f32[3,32,1280]{2,1,0:T(8,128)}, f32[3,32,1280]{2,1,0:T(8,128)}, f32[3,16,1280]{2,1,0:T(8,128)}, f32[3,16,1280]{2,1,0:T(8,128)}, /*index=5*/f32[2,16,1280]{2,1,0:T(8,128)}) custom-call(s32[3]{0:T(128)} %pad_add_fusion.refs_0_, bf16[4,640,640]{2,1,0:T(8,128)(2,1)} %constant.167.clone.refs_1_, ...), custom_call_target="tpu_custom_call" | custom-call | flops 10066329600 | bytes 6553600 | tf_op jit(solution)/shard_map/window_tensor/pallas_call | solution.py:420
  117.0 1.3 collective-permute-done.23
  118.2 1.8 collective-permute-start.13
  120.0 1.5 collective-permute-start.28
  121.5 2.1 maximum_add_fusion.2.refs_4_
  123.6 8.0 %collective-permute-done.13 = f32[3,32,1280]{2,1,0:T(8,128)} collective-permute-done((f32[3,32,1280]{2,1,0:T(8,128)S(1)}, f32[3,32,1280]{2,1,0:T(8,128)}, u32[]{:S(2)}, u32[]{:S(2)}) %collective-permute-start.13) | collective-permute-done | bytes 491552 | tf_op jit(solution)/shard_map/ppermute | solution.py:494
  131.6 1.7 collective-permute-start.25
  133.4 2.2 dynamic-slice_add_fusion.7
  135.6 1.6 collective-permute-start.14
  137.2 1.0 dynamic-slice_add_fusion.1
  139.4 11.1 %window_tensor.7 = (f32[3,32,1280]{2,1,0:T(8,128)}, f32[3,32,1280]{2,1,0:T(8,128)}, f32[3,32,1280]{2,1,0:T(8,128)}, f32[3,16,1280]{2,1,0:T(8,128)}, f32[3,16,1280]{2,1,0:T(8,128)}) custom-call(s32[3]{0:T(128)} %pad_add_fusion.refs_0_, bf16[4,640,640]{2,1,0:T(8,128)(2,1)} %constant.167.clone.refs_1_, f32[2,120,640]{2,1,0:T(8,128)} %get-tuple-element.62.refs_2_, ...), custom_call_target="tpu_custom_call" | custom-call | flops 9437184000 | bytes 6471680 | tf_op jit(solution)/shard_map/window_tensor/pallas_call | solution.py:420
  151.3 2.6 %collective-permute-start.15 = (f32[3,8,1280]{2,1,0:T(8,128)S(1)}, f32[3,8,1280]{2,1,0:T(8,128)S(1)}, u32[]{:S(2)}, u32[]{:S(2)}) collective-permute-start(f32[3,8,1280]{2,1,0:T(8,128)S(1)} %dynamic-slice_add_fusion.11), channel_id=1, source_target_pairs={{0,16},{2,18},{4,20},{6,22},{8,24},{10,26},{12,28},{14,30},{16,0},... | collective-permute-start | bytes 368648 | tf_op jit(solution)/shard_map/ppermute | solution.py:489
  153.9 1.4 dynamic-slice_add_fusion.5
  155.3 1.6 collective-permute-start.26
  157.6 3.0 %collective-permute-done.15 = f32[3,8,1280]{2,1,0:T(8,128)S(1)} collective-permute-done((f32[3,8,1280]{2,1,0:T(8,128)S(1)}, f32[3,8,1280]{2,1,0:T(8,128)S(1)}, u32[]{:S(2)}, u32[]{:S(2)}) %collective-permute-start.15) | collective-permute-done | bytes 122912 | tf_op jit(solution)/shard_map/ppermute | solution.py:489
  161.4 3.5 %collective-permute-done.26 = f32[3,16,1280]{2,1,0:T(8,128)S(1)} collective-permute-done((f32[3,16,1280]{2,1,0:T(8,128)S(1)}, f32[3,16,1280]{2,1,0:T(8,128)S(1)}, u32[]{:S(2)}, u32[]{:S(2)}) %collective-permute-start.26) | collective-permute-done | bytes 245792 | tf_op jit(solution)/shard_map/ppermute | solution.py:489
  165.5 2.5 %collective-permute-start.7 = (f32[3,16,1280]{2,1,0:T(8,128)S(1)}, f32[3,16,1280]{2,1,0:T(8,128)S(1)}, u32[]{:S(2)}, u32[]{:S(2)}) collective-permute-start(f32[3,16,1280]{2,1,0:T(8,128)S(1)} %dynamic-slice_add_fusion.8), channel_id=1, source_target_pairs={{0,16},{2,18},{4,20},{6,22},{8,24},{10,26},{12,28},{14,30},{16,0},... | collective-permute-start | bytes 737288 | tf_op jit(solution)/shard_map/ppermute | solution.py:489
  168.0 11.3 %collective-permute-done.27 = f32[3,8,1280]{2,1,0:T(8,128)S(1)} collective-permute-done((f32[3,8,1280]{2,1,0:T(8,128)S(1)}, f32[3,8,1280]{2,1,0:T(8,128)S(1)}, u32[]{:S(2)}, u32[]{:S(2)}) %collective-permute-start.27) | collective-permute-done | bytes 122912 | tf_op jit(solution)/shard_map/ppermute | solution.py:489
  179.6 4.3 %collective-permute-done.7 = f32[3,16,1280]{2,1,0:T(8,128)S(1)} collective-permute-done((f32[3,16,1280]{2,1,0:T(8,128)S(1)}, f32[3,16,1280]{2,1,0:T(8,128)S(1)}, u32[]{:S(2)}, u32[]{:S(2)}) %collective-permute-start.7) | collective-permute-done | bytes 245792 | tf_op jit(solution)/shard_map/ppermute | solution.py:489
  184.0 1.2 collective-permute-start.8
  185.3 3.3 %collective-permute-done.8 = f32[16,1280]{1,0:T(8,128)S(1)} collective-permute-done((f32[16,1280]{1,0:T(8,128)S(1)}, f32[16,1280]{1,0:T(8,128)S(1)}, u32[]{:S(2)}, u32[]{:S(2)}) %collective-permute-start.8) | collective-permute-done | bytes 81952 | tf_op jit(solution)/shard_map/ppermute | solution.py:534
  189.1 2.5 %collective-permute-start.34 = (f32[3,8,1280]{2,1,0:T(8,128)S(1)}, f32[3,8,1280]{2,1,0:T(8,128)S(1)}, u32[]{:S(2)}, u32[]{:S(2)}) collective-permute-start(f32[3,8,1280]{2,1,0:T(8,128)S(1)} %dynamic-slice_add_fusion.9), channel_id=1, source_target_pairs={{0,16},{2,18},{4,20},{6,22},{8,24},{10,26},{12,28},{14,30},{16,0},... | collective-permute-start | bytes 368648 | tf_op jit(solution)/shard_map/ppermute | solution.py:489
  191.6 6.6 %collective-permute-done.17 = f32[1,24,1280]{2,1,0:T(8,128)S(1)} collective-permute-done((f32[1,24,1280]{2,1,0:T(8,128)S(1)}, f32[1,24,1280]{2,1,0:T(8,128)S(1)}, u32[]{:S(2)}, u32[]{:S(2)}) %collective-permute-start.17) | collective-permute-done | bytes 122912 | tf_op jit(solution)/shard_map/ppermute | solution.py:500
  198.4 2.3 collective-permute-done.34
  201.5 6.2 %collective-permute-done.18 = f32[2,24,1280]{2,1,0:T(8,128)S(1)} collective-permute-done((f32[2,24,1280]{2,1,0:T(8,128)S(1)}, f32[2,24,1280]{2,1,0:T(8,128)S(1)}, u32[]{:S(2)}, u32[]{:S(2)}) %collective-permute-start.18) | collective-permute-done | bytes 245792 | tf_op jit(solution)/shard_map/ppermute | solution.py:500
  208.4 5.3 %collective-permute-done.36 = f32[2,16,1280]{2,1,0:T(8,128)S(1)} collective-permute-done((f32[2,16,1280]{2,1,0:T(8,128)S(1)}, f32[2,16,1280]{2,1,0:T(8,128)S(1)}, u32[]{:S(2)}, u32[]{:S(2)}) %collective-permute-start.36) | collective-permute-done | bytes 163872 | tf_op jit(solution)/shard_map/ppermute | solution.py:500
  213.8 1.6 collective-permute-start.37
  215.3 6.6 %collective-permute-done.19 = f32[4,24,1280]{2,1,0:T(8,128)S(1)} collective-permute-done((f32[4,24,1280]{2,1,0:T(8,128)S(1)}, f32[4,24,1280]{2,1,0:T(8,128)S(1)}, u32[]{:S(2)}, u32[]{:S(2)}) %collective-permute-start.19) | collective-permute-done | bytes 491552 | tf_op jit(solution)/shard_map/ppermute | solution.py:500
  222.1 4.5 %collective-permute-done.37 = f32[4,16,1280]{2,1,0:T(8,128)S(1)} collective-permute-done((f32[4,16,1280]{2,1,0:T(8,128)S(1)}, f32[4,16,1280]{2,1,0:T(8,128)S(1)}, u32[]{:S(2)}, u32[]{:S(2)}) %collective-permute-start.37) | collective-permute-done | bytes 327712 | tf_op jit(solution)/shard_map/ppermute | solution.py:500
  226.7 2.1 collective-permute-done.38
  230.3 1.7 copy-done
  232.0 0.9 fusion
  (103 shorter events, 12.9 us)
Async XLA Ops:
  2.6 33.8 %collective-permute-start = (f32[2,136,640]{2,1,0:T(8,128)}, f32[2,136,640]{2,1,0:T(8,128)S(1)}, u32[]{:S(2)}, u32[]{:S(2)}) collective-permute-start(f32[2,136,640]{2,1,0:T(8,128)} %pieces_of.4), channel_id=1, source_target_pairs={{0,1},{1,0},{2,3},{3,2},{4,5},{5,4},{6,7},{7,6},{8,9},{9,8},{10,11... | collective-permute-start | bytes 2088968 | tf_op jit(solution)/shard_map/ppermute | solution.py:468
  9.2 26.3 %collective-permute-start.1 = (f32[2,128,640]{2,1,0:T(8,128)}, f32[2,128,640]{2,1,0:T(8,128)S(1)}, u32[]{:S(2)}, u32[]{:S(2)}) collective-permute-start(f32[2,128,640]{2,1,0:T(8,128)} %get-tuple-element.39), channel_id=1, source_target_pairs={{0,1},{1,0},{2,3},{3,2},{4,5},{5,4},{6,7},{7,6},{8,9},{9,8},{10,11... | collective-permute-start | bytes 1966088 | tf_op jit(solution)/shard_map/ppermute | solution.py:473
  35.4 0.9 copy-start.6
  37.2 20.8 %copy-start.4 = (f32[2,128,640]{2,1,0:T(8,128)S(1)}, f32[2,128,640]{2,1,0:T(8,128)}, u32[]{:S(2)}) copy-start(f32[2,128,640]{2,1,0:T(8,128)} %gated.3.refs_6_) | copy-start | bytes 1966084
  57.4 2.3 collective-permute-start.3
  57.5 2.8 %collective-permute-start.4 = (f32[3,32,1280]{2,1,0:T(8,128)}, f32[3,32,1280]{2,1,0:T(8,128)S(1)}, u32[]{:S(2)}, u32[]{:S(2)}) collective-permute-start(f32[3,32,1280]{2,1,0:T(8,128)} %get-tuple-element.46), channel_id=1, source_target_pairs={{0,2},{2,0},{4,6},{6,4},{8,10},{10,8},{12,14},{14,12},{16,18},{18,... | collective-permute-start | bytes 1474568 | tf_op jit(solution)/shard_map/ppermute | solution.py:524
  58.0 16.7 %collective-permute-start.9 = (f32[2,128,640]{2,1,0:T(8,128)S(1)}, f32[2,128,640]{2,1,0:T(8,128)S(1)}, u32[]{:S(2)}, u32[]{:S(2)}) collective-permute-start(f32[2,128,640]{2,1,0:T(8,128)S(1)} %copy-done.4), channel_id=1, source_target_pairs={{0,1},{1,0},{2,3},{3,2},{4,5},{5,4},{6,7},{7,6},{8,9},{9,8},{10,11... | collective-permute-start | bytes 1966088 | tf_op jit(solution)/shard_map/ppermute | solution.py:473
  75.5 13.5 %copy-start.2 = (f32[3,64,1280]{2,1,0:T(8,128)S(1)}, f32[3,64,1280]{2,1,0:T(8,128)}, u32[]{:S(2)}) copy-start(f32[3,64,1280]{2,1,0:T(8,128)} %maximum_add_fusion.refs_5_) | copy-start | bytes 2949124
  86.6 3.9 %collective-permute-start.11 = (f32[3,16,1280]{2,1,0:T(8,128)}, f32[3,16,1280]{2,1,0:T(8,128)S(1)}, u32[]{:S(2)}, u32[]{:S(2)}) collective-permute-start(f32[3,16,1280]{2,1,0:T(8,128)} %get-tuple-element.53), channel_id=1, source_target_pairs={{0,2},{2,0},{4,6},{6,4},{8,10},{10,8},{12,14},{14,12},{16,18},{18,... | collective-permute-start | bytes 737288 | tf_op jit(solution)/shard_map/ppermute | solution.py:524
  86.7 3.8 %collective-permute-start.12 = (f32[3,16,1280]{2,1,0:T(8,128)}, f32[3,16,1280]{2,1,0:T(8,128)S(1)}, u32[]{:S(2)}, u32[]{:S(2)}) collective-permute-start(f32[3,16,1280]{2,1,0:T(8,128)} %get-tuple-element.54), channel_id=1, source_target_pairs={{0,2},{2,0},{4,6},{6,4},{8,10},{10,8},{12,14},{14,12},{16,18},{18,... | collective-permute-start | bytes 737288 | tf_op jit(solution)/shard_map/ppermute | solution.py:524
  87.2 16.9 %collective-permute-start.21 = (f32[2,128,640]{2,1,0:T(8,128)}, f32[2,128,640]{2,1,0:T(8,128)S(1)}, u32[]{:S(2)}, u32[]{:S(2)}) collective-permute-start(f32[2,128,640]{2,1,0:T(8,128)} %gated.4.refs_7_), channel_id=1, source_target_pairs={{0,1},{1,0},{2,3},{3,2},{4,5},{5,4},{6,7},{7,6},{8,9},{9,8},{10,11... | collective-permute-start | bytes 1966088 | tf_op jit(solution)/shard_map/ppermute | solution.py:473
  89.0 46.6 %collective-permute-start.2 = (f32[3,64,1280]{2,1,0:T(8,128)}, f32[3,64,1280]{2,1,0:T(8,128)S(1)}, u32[]{:S(2)}, u32[]{:S(2)}) collective-permute-start(f32[3,64,1280]{2,1,0:T(8,128)} %get-tuple-element.43), channel_id=1, source_target_pairs={{0,2},{2,0},{4,6},{6,4},{8,10},{10,8},{12,14},{14,12},{16,18},{18,... | collective-permute-start | bytes 2949128 | tf_op jit(solution)/shard_map/ppermute | solution.py:524
  89.0 48.2 %collective-permute-start.5 = (f32[3,64,1280]{2,1,0:T(8,128)S(1)}, f32[3,64,1280]{2,1,0:T(8,128)S(1)}, u32[]{:S(2)}, u32[]{:S(2)}) collective-permute-start(f32[3,64,1280]{2,1,0:T(8,128)S(1)} %copy-done.2), channel_id=1, source_target_pairs={{0,4},{2,6},{4,0},{6,2},{8,12},{10,14},{12,8},{14,10},{16,20},{18,... | collective-permute-start | bytes 2949128 | tf_op jit(solution)/shard_map/ppermute | solution.py:494
  105.0 13.2 %copy-start.8 = (f32[3,32,1280]{2,1,0:T(8,128)S(1)}, f32[3,32,1280]{2,1,0:T(8,128)}, u32[]{:S(2)}) copy-start(f32[3,32,1280]{2,1,0:T(8,128)} %maximum_add_fusion.1.refs_4_) | copy-start | bytes 1474564
  116.3 1.9 collective-permute-start.23
  116.4 3.6 %collective-permute-start.24 = (f32[3,16,1280]{2,1,0:T(8,128)}, f32[3,16,1280]{2,1,0:T(8,128)}, u32[]{:S(2)}, u32[]{:S(2)}) collective-permute-start(f32[3,16,1280]{2,1,0:T(8,128)} %get-tuple-element.61), channel_id=1, source_target_pairs={{0,2},{2,0},{4,6},{6,4},{8,10},{10,8},{12,14},{14,12},{16,18},{18,... | collective-permute-start | bytes 737288 | tf_op jit(solution)/shard_map/ppermute | solution.py:524
  116.9 6.8 %collective-permute-start.10 = (f32[3,32,1280]{2,1,0:T(8,128)}, f32[3,32,1280]{2,1,0:T(8,128)}, u32[]{:S(2)}, u32[]{:S(2)}) collective-permute-start(f32[3,32,1280]{2,1,0:T(8,128)} %get-tuple-element.51), channel_id=1, source_target_pairs={{0,2},{2,0},{4,6},{6,4},{8,10},{10,8},{12,14},{14,12},{16,18},{18,... | collective-permute-start | bytes 1474568 | tf_op jit(solution)/shard_map/ppermute | solution.py:524
  118.2 13.4 %collective-permute-start.13 = (f32[3,32,1280]{2,1,0:T(8,128)S(1)}, f32[3,32,1280]{2,1,0:T(8,128)}, u32[]{:S(2)}, u32[]{:S(2)}) collective-permute-start(f32[3,32,1280]{2,1,0:T(8,128)S(1)} %copy-done.8), channel_id=1, source_target_pairs={{0,4},{2,6},{4,0},{6,2},{8,12},{10,14},{12,8},{14,10},{16,20},{18,... | collective-permute-start | bytes 1474568 | tf_op jit(solution)/shard_map/ppermute | solution.py:494
  120.0 18.6 %collective-permute-start.28 = (f32[2,120,640]{2,1,0:T(8,128)}, f32[2,120,640]{2,1,0:T(8,128)S(1)}, u32[]{:S(2)}, u32[]{:S(2)}) collective-permute-start(f32[2,120,640]{2,1,0:T(8,128)} %gated.5.refs_4_), channel_id=1, source_target_pairs={{0,1},{1,0},{2,3},{3,2},{4,5},{5,4},{6,7},{7,6},{8,9},{9,8},{10,11... | collective-permute-start | bytes 1843208 | tf_op jit(solution)/shard_map/ppermute | solution.py:473
  121.5 15.7 %copy-start.1 = (f32[3,64,1280]{2,1,0:T(8,128)S(1)}, f32[3,64,1280]{2,1,0:T(8,128)}, u32[]{:S(2)}) copy-start(f32[3,64,1280]{2,1,0:T(8,128)} %get-tuple-element.42) | copy-start | bytes 2949124
  123.6 27.5 %collective-permute-start.22 = (f32[3,32,1280]{2,1,0:T(8,128)}, f32[3,32,1280]{2,1,0:T(8,128)}, u32[]{:S(2)}, u32[]{:S(2)}) collective-permute-start(f32[3,32,1280]{2,1,0:T(8,128)} %get-tuple-element.58), channel_id=1, source_target_pairs={{0,2},{2,0},{4,6},{6,4},{8,10},{10,8},{12,14},{14,12},{16,18},{18,... | collective-permute-start | bytes 1474568 | tf_op jit(solution)/shard_map/ppermute | solution.py:524
  131.6 19.7 %collective-permute-start.25 = (f32[3,32,1280]{2,1,0:T(8,128)}, f32[3,32,1280]{2,1,0:T(8,128)}, u32[]{:S(2)}, u32[]{:S(2)}) collective-permute-start(f32[3,32,1280]{2,1,0:T(8,128)} %maximum_add_fusion.2.refs_4_), channel_id=1, source_target_pairs={{0,4},{2,6},{4,0},{6,2},{8,12},{10,14},{12,8},{14,10},{16,20},{18,... | collective-permute-start | bytes 1474568 | tf_op jit(solution)/shard_map/ppermute | solution.py:494
  135.6 15.1 %collective-permute-start.14 = (f32[3,16,1280]{2,1,0:T(8,128)}, f32[3,16,1280]{2,1,0:T(8,128)S(1)}, u32[]{:S(2)}, u32[]{:S(2)}) collective-permute-start(f32[3,16,1280]{2,1,0:T(8,128)} %get-tuple-element.78), channel_id=1, source_target_pairs={{0,8},{2,10},{4,12},{6,14},{8,0},{10,2},{12,4},{14,6},{16,24},{18,... | collective-permute-start | bytes 737288 | tf_op jit(solution)/shard_map/ppermute | solution.py:489
  138.2 27.3 %collective-permute-start.6 = (f32[3,32,1280]{2,1,0:T(8,128)}, f32[3,32,1280]{2,1,0:T(8,128)S(1)}, u32[]{:S(2)}, u32[]{:S(2)}) collective-permute-start(f32[3,32,1280]{2,1,0:T(8,128)} %get-tuple-element.70.refs_5_), channel_id=1, source_target_pairs={{0,8},{2,10},{4,12},{6,14},{8,0},{10,2},{12,4},{14,6},{16,24},{18,... | collective-permute-start | bytes 1474568 | tf_op jit(solution)/shard_map/ppermute | solution.py:489
  139.4 14.5 %copy-start.7 = (f32[3,32,1280]{2,1,0:T(8,128)S(1)}, f32[3,32,1280]{2,1,0:T(8,128)}, u32[]{:S(2)}) copy-start(f32[3,32,1280]{2,1,0:T(8,128)} %get-tuple-element.57) | copy-start | bytes 1474564
  150.6 6.4 %copy-start.10 = (f32[3,32,1280]{2,1,0:T(8,128)S(1)}, f32[3,32,1280]{2,1,0:T(8,128)}, u32[]{:S(2)}) copy-start(f32[3,32,1280]{2,1,0:T(8,128)} %get-tuple-element.66) | copy-start | bytes 1474564
  150.6 4.7 %collective-permute-start.30 = (f32[3,16,1280]{2,1,0:T(8,128)}, f32[3,16,1280]{2,1,0:T(8,128)S(1)}, u32[]{:S(2)}, u32[]{:S(2)}) collective-permute-start(f32[3,16,1280]{2,1,0:T(8,128)} %get-tuple-element.67), channel_id=1, source_target_pairs={{0,2},{2,0},{4,6},{6,4},{8,10},{10,8},{12,14},{14,12},{16,18},{18,... | collective-permute-start | bytes 737288 | tf_op jit(solution)/shard_map/ppermute | solution.py:524
  150.7 6.3 %collective-permute-start.31 = (f32[3,16,1280]{2,1,0:T(8,128)}, f32[3,16,1280]{2,1,0:T(8,128)S(1)}, u32[]{:S(2)}, u32[]{:S(2)}) collective-permute-start(f32[3,16,1280]{2,1,0:T(8,128)} %get-tuple-element.68), channel_id=1, source_target_pairs={{0,2},{2,0},{4,6},{6,4},{8,10},{10,8},{12,14},{14,12},{16,18},{18,... | collective-permute-start | bytes 737288 | tf_op jit(solution)/shard_map/ppermute | solution.py:524
  151.2 28.2 %collective-permute-start.29 = (f32[3,32,1280]{2,1,0:T(8,128)}, f32[3,32,1280]{2,1,0:T(8,128)S(1)}, u32[]{:S(2)}, u32[]{:S(2)}) collective-permute-start(f32[3,32,1280]{2,1,0:T(8,128)} %get-tuple-element.65), channel_id=1, source_target_pairs={{0,2},{2,0},{4,6},{6,4},{8,10},{10,8},{12,14},{14,12},{16,18},{18,... | collective-permute-start | bytes 1474568 | tf_op jit(solution)/shard_map/ppermute | solution.py:524
  151.3 9.3 %collective-permute-start.15 = (f32[3,8,1280]{2,1,0:T(8,128)S(1)}, f32[3,8,1280]{2,1,0:T(8,128)S(1)}, u32[]{:S(2)}, u32[]{:S(2)}) collective-permute-start(f32[3,8,1280]{2,1,0:T(8,128)S(1)} %dynamic-slice_add_fusion.11), channel_id=1, source_target_pairs={{0,16},{2,18},{4,20},{6,22},{8,24},{10,26},{12,28},{14,30},{16,0},... | collective-permute-start | bytes 368648 | tf_op jit(solution)/shard_map/ppermute | solution.py:489
  155.3 9.6 %collective-permute-start.26 = (f32[3,16,1280]{2,1,0:T(8,128)S(1)}, f32[3,16,1280]{2,1,0:T(8,128)S(1)}, u32[]{:S(2)}, u32[]{:S(2)}) collective-permute-start(f32[3,16,1280]{2,1,0:T(8,128)S(1)} %get-tuple-element.74), channel_id=1, source_target_pairs={{0,8},{2,10},{4,12},{6,14},{8,0},{10,2},{12,4},{14,6},{16,24},{18,... | collective-permute-start | bytes 737288 | tf_op jit(solution)/shard_map/ppermute | solution.py:489
  157.0 22.5 %copy-start.9 = (f32[3,32,1280]{2,1,0:T(8,128)S(1)}, f32[3,32,1280]{2,1,0:T(8,128)}, u32[]{:S(2)}) copy-start(f32[3,32,1280]{2,1,0:T(8,128)} %get-tuple-element.64) | copy-start | bytes 1474564
  157.0 22.4 %collective-permute-start.32 = (f32[3,32,1280]{2,1,0:T(8,128)S(1)}, f32[3,32,1280]{2,1,0:T(8,128)S(1)}, u32[]{:S(2)}, u32[]{:S(2)}) collective-permute-start(f32[3,32,1280]{2,1,0:T(8,128)S(1)} %maximum_add_fusion.3), channel_id=1, source_target_pairs={{0,4},{2,6},{4,0},{6,2},{8,12},{10,14},{12,8},{14,10},{16,20},{18,... | collective-permute-start | bytes 1474568 | tf_op jit(solution)/shard_map/ppermute | solution.py:494
  160.7 24.6 %collective-permute-start.16 = (f32[8,1280]{1,0:T(8,128)S(1)}, f32[8,1280]{1,0:T(8,128)S(1)}, u32[]{:S(2)}, u32[]{:S(2)}) collective-permute-start(f32[8,1280]{1,0:T(8,128)S(1)} %fusion.29), channel_id=1, source_target_pairs={{0,0},{1,2},{2,1},{3,3},{4,4},{5,6},{6,5},{7,7},{8,8},{9,10},{10,9... | collective-permute-start | bytes 122888 | tf_op jit(solution)/shard_map/ppermute | solution.py:540
  164.9 14.4 %collective-permute-start.27 = (f32[3,8,1280]{2,1,0:T(8,128)S(1)}, f32[3,8,1280]{2,1,0:T(8,128)S(1)}, u32[]{:S(2)}, u32[]{:S(2)}) collective-permute-start(f32[3,8,1280]{2,1,0:T(8,128)S(1)} %dynamic-slice_add_fusion.10), channel_id=1, source_target_pairs={{0,16},{2,18},{4,20},{6,22},{8,24},{10,26},{12,28},{14,30},{16,0},... | collective-permute-start | bytes 368648 | tf_op jit(solution)/shard_map/ppermute | solution.py:489
  165.5 18.4 %collective-permute-start.7 = (f32[3,16,1280]{2,1,0:T(8,128)S(1)}, f32[3,16,1280]{2,1,0:T(8,128)S(1)}, u32[]{:S(2)}, u32[]{:S(2)}) collective-permute-start(f32[3,16,1280]{2,1,0:T(8,128)S(1)} %dynamic-slice_add_fusion.8), channel_id=1, source_target_pairs={{0,16},{2,18},{4,20},{6,22},{8,24},{10,26},{12,28},{14,30},{16,0},... | collective-permute-start | bytes 737288 | tf_op jit(solution)/shard_map/ppermute | solution.py:489
  179.5 9.5 %collective-permute-start.33 = (f32[3,16,1280]{2,1,0:T(8,128)S(1)}, f32[3,16,1280]{2,1,0:T(8,128)S(1)}, u32[]{:S(2)}, u32[]{:S(2)}) collective-permute-start(f32[3,16,1280]{2,1,0:T(8,128)S(1)} %get-tuple-element.76), channel_id=1, source_target_pairs={{0,8},{2,10},{4,12},{6,14},{8,0},{10,2},{12,4},{14,6},{16,24},{18,... | collective-permute-start | bytes 737288 | tf_op jit(solution)/shard_map/ppermute | solution.py:489
  184.0 4.5 %collective-permute-start.8 = (f32[16,1280]{1,0:T(8,128)S(1)}, f32[16,1280]{1,0:T(8,128)S(1)}, u32[]{:S(2)}, u32[]{:S(2)}) collective-permute-start(f32[16,1280]{1,0:T(8,128)S(1)} %fusion.8), channel_id=1, source_target_pairs={{0,1},{1,0},{2,3},{3,2},{4,5},{5,4},{6,7},{7,6},{8,9},{9,8},{10,11... | collective-permute-start | bytes 245768 | tf_op jit(solution)/shard_map/ppermute | solution.py:534
  188.6 9.7 %collective-permute-start.17 = (f32[1,24,1280]{2,1,0:T(8,128)S(1)}, f32[1,24,1280]{2,1,0:T(8,128)S(1)}, u32[]{:S(2)}, u32[]{:S(2)}) collective-permute-start(f32[1,24,1280]{2,1,0:T(8,128)S(1)} %maximum_bitcast_fusion.2), channel_id=1, source_target_pairs={{0,16},{2,18},{4,20},{6,22},{8,24},{10,26},{12,28},{14,30},{16,0},... | collective-permute-start | bytes 368648 | tf_op jit(solution)/shard_map/ppermute | solution.py:500
  189.1 11.6 %collective-permute-start.34 = (f32[3,8,1280]{2,1,0:T(8,128)S(1)}, f32[3,8,1280]{2,1,0:T(8,128)S(1)}, u32[]{:S(2)}, u32[]{:S(2)}) collective-permute-start(f32[3,8,1280]{2,1,0:T(8,128)S(1)} %dynamic-slice_add_fusion.9), channel_id=1, source_target_pairs={{0,16},{2,18},{4,20},{6,22},{8,24},{10,26},{12,28},{14,30},{16,0},... | collective-permute-start | bytes 368648 | tf_op jit(solution)/shard_map/ppermute | solution.py:489
  198.3 9.4 %collective-permute-start.18 = (f32[2,24,1280]{2,1,0:T(8,128)S(1)}, f32[2,24,1280]{2,1,0:T(8,128)S(1)}, u32[]{:S(2)}, u32[]{:S(2)}) collective-permute-start(f32[2,24,1280]{2,1,0:T(8,128)S(1)} %maximum_select_fusion.7), channel_id=1, source_target_pairs={{0,8},{2,10},{4,12},{6,14},{8,0},{10,2},{12,4},{14,6},{16,24},{18,... | collective-permute-start | bytes 737288 | tf_op jit(solution)/shard_map/ppermute | solution.py:500
  200.8 7.5 %collective-permute-start.35 = (f32[1,16,1280]{2,1,0:T(8,128)S(1)}, f32[1,16,1280]{2,1,0:T(8,128)S(1)}, u32[]{:S(2)}, u32[]{:S(2)}) collective-permute-start(f32[1,16,1280]{2,1,0:T(8,128)S(1)} %maximum_bitcast_fusion.3), channel_id=1, source_target_pairs={{0,16},{2,18},{4,20},{6,22},{8,24},{10,26},{12,28},{14,30},{16,0},... | collective-permute-start | bytes 245768 | tf_op jit(solution)/shard_map/ppermute | solution.py:500
  207.8 14.2 %collective-permute-start.19 = (f32[4,24,1280]{2,1,0:T(8,128)S(1)}, f32[4,24,1280]{2,1,0:T(8,128)S(1)}, u32[]{:S(2)}, u32[]{:S(2)}) collective-permute-start(f32[4,24,1280]{2,1,0:T(8,128)S(1)} %maximum_select_fusion.5), channel_id=1, source_target_pairs={{0,4},{2,6},{4,0},{6,2},{8,12},{10,14},{12,8},{14,10},{16,20},{18,... | collective-permute-start | bytes 1474568 | tf_op jit(solution)/shard_map/ppermute | solution.py:500
  208.3 5.4 %collective-permute-start.36 = (f32[2,16,1280]{2,1,0:T(8,128)S(1)}, f32[2,16,1280]{2,1,0:T(8,128)S(1)}, u32[]{:S(2)}, u32[]{:S(2)}) collective-permute-start(f32[2,16,1280]{2,1,0:T(8,128)S(1)} %maximum_select_fusion.8), channel_id=1, source_target_pairs={{0,8},{2,10},{4,12},{6,14},{8,0},{10,2},{12,4},{14,6},{16,24},{18,... | collective-permute-start | bytes 491528 | tf_op jit(solution)/shard_map/ppermute | solution.py:500
  213.8 12.8 %collective-permute-start.37 = (f32[4,16,1280]{2,1,0:T(8,128)S(1)}, f32[4,16,1280]{2,1,0:T(8,128)S(1)}, u32[]{:S(2)}, u32[]{:S(2)}) collective-permute-start(f32[4,16,1280]{2,1,0:T(8,128)S(1)} %maximum_select_fusion.6), channel_id=1, source_target_pairs={{0,4},{2,6},{4,0},{6,2},{8,12},{10,14},{12,8},{14,10},{16,20},{18,... | collective-permute-start | bytes 983048 | tf_op jit(solution)/shard_map/ppermute | solution.py:500
  222.1 6.9 %collective-permute-start.20 = (f32[8,24,1280]{2,1,0:T(8,128)S(1)}, f32[8,24,1280]{2,1,0:T(8,128)S(1)}, u32[]{:S(2)}, u32[]{:S(2)}) collective-permute-start(f32[8,24,1280]{2,1,0:T(8,128)S(1)} %maximum_select_fusion.3), channel_id=1, source_target_pairs={{0,2},{2,0},{4,6},{6,4},{8,10},{10,8},{12,14},{14,12},{16,18},{18,... | collective-permute-start | bytes 2949128 | tf_op jit(solution)/shard_map/ppermute | solution.py:500
  226.6 2.2 collective-permute-start.38
  230.2 1.7 copy-start
  (4 other events, 3.4 us)

commit v9 on v6

--- a/solution.py
+++ b/solution.py
@@ -16,6 +16,7 @@
 LANE = 128
 VMEM_LIMIT = 60 * 1024 * 1024
 KERNEL_WORK = 8
+AHEAD = ((), (), (0,), (1, 0), (2, 1, 0))
 
 
 def padded(cells, sides, width):
@@ -221,22 +222,6 @@
         ),
         name="pieces_of",
     )(level.reshape(1), spec)
-
-
-def gate_kernel(*refs):
-    pass
-
-
-def gated(part, waits):
-    return pl.pallas_call(
-        gate_kernel,
-        in_specs=[pl.BlockSpec(memory_space=pl.ANY)] * (1 + len(waits)),
-        out_specs=pl.BlockSpec(memory_space=pl.ANY),
-        out_shape=jax.ShapeDtypeStruct(part.shape, part.dtype),
-        input_output_aliases={0: 0},
-        cost_estimate=pl.CostEstimate(flops=0, transcendentals=0, bytes_accessed=1024),
-        name="gated",
-    )(part, *waits)
 
 
 def east_of(x):
@@ -425,6 +410,10 @@
     return [(member, member ^ bit) for member in range(members)]
 
 
+def pairs(members, bit):
+    return [(member, member ^ bit) for member in range(members)]
+
+
 def put_kernel(count, place_ref, *refs):
     parts, out_ref, sem = refs[:4], refs[-2], refs[-1]
     core, side, along = place_ref[0], place_ref[1], place_ref[2]
@@ -472,7 +461,7 @@
     members = lax.axis_size("mem")
     band = lax.axis_index("band").astype(jnp.int32)
     member = lax.axis_index("mem").astype(jnp.int32)
-    core, side, along = member % 2, member // 2 % 2, member // 4
+    core, side = member % 2, member // 2 % 2
     place = jnp.stack([band, core, side])
     spec = spec.reshape(levels, 2, parts * waves_local, nlat)
     count = nlat // LANE
@@ -482,50 +471,57 @@
 
     (piece,) = pieces_of(spec, 1 - band, windows[:1], count)
     remotes = [lax.ppermute(piece, "band", swap)]
-    outgoing = [None, *pieces_of(spec, 1 - band, windows[1:], count)]
-
-    def fetch_rows(k, waits):
-        piece = gated(outgoing[k], waits) if waits else outgoing[k]
-        remotes.append(lax.ppermute(piece, "band", swap))
-        return piece
-
-    fetch_rows(1, [])
+    outgoing = pieces_of(spec, 1 - band, windows[1:], count)
+    remotes += [lax.ppermute(piece, "band", swap) for piece in outgoing]
     local = pieces_of(spec, band, windows, count)
 
-    around = members // 4
-    shifts = [[(m, (m + 4 * d) % members) for m in range(members)] for d in range(around)]
-
-    def across(kept, passed, kept_more, passed_more):
+    bits = [1 << n for n in range(members.bit_length() - 1)]
+
+    def halved(parts_of, bit):
+        half = parts_of[0].shape[1] // 2
+        mine = (member // bit) % 2
+
+        def total(which):
+            return sum(lax.dynamic_slice_in_dim(part, which * half, half, axis=1) for part in parts_of)
+
+        leaves = total(1 - mine)
+        return [total(mine), lax.ppermute(leaves, "mem", pairs(members, bit))], leaves
+
+    def across(parts_of, bit):
+        kept, passed, kept_more, passed_more = parts_of
         leaves = passed + passed_more
-        return [kept, kept_more, lax.ppermute(leaves, "mem", pairs(members, 2))], leaves
-
-    def onward(*parts_of):
-        rows = parts_of[0].shape[1] // around
-
-        def total(d):
-            first = (along + d) % around * rows
-            return sum(lax.dynamic_slice_in_dim(part, first, rows, axis=1) for part in parts_of)
-
-        leaves = [total(d) for d in range(1, around)]
-        return [total(0), *(lax.ppermute(leaves[d - 1], "mem", shifts[d]) for d in range(1, around))], leaves[0]
+        return [kept, kept_more, lax.ppermute(leaves, "mem", pairs(members, bit))], leaves
+
+    def advanced(parts_of, bit):
+        return (across if len(parts_of) == 4 else halved)(parts_of, bit)
+
+    def doubled(part, bit):
+        beside = lax.ppermute(part, "mem", pairs(members, bit))
+        mine = (member // bit) % 2
+        return jnp.where(mine == 0, jnp.concatenate([part, beside], axis=1), jnp.concatenate([beside, part], axis=1))
+
+    def gathered(part):
+        for bit in reversed(bits):
+            part = doubled(part, bit)
+        return part
 
     carry = None
-    sums, steps = [], [across, onward]
+    sums, done = [], []
     for k, window in enumerate(windows):
         waits = []
-        if k + 2 < count:
-            waits.append(fetch_rows(k + 2, [remotes[k]] if carry is None else [remotes[k], carry]))
-        for j in range(max(0, k - len(steps)), k):
-            sums[j], left = steps[k - 1 - j](*sums[j])
+        for j in AHEAD[k]:
+            sums[j], left = advanced(sums[j], bits[done[j]])
+            done[j] += 1
             waits.append(left)
         quarters, carry = window_tensor(window, place, local[k], remotes[k], table, waits, carry)
-        first = lax.ppermute(quarters[3], "mem", pairs(members, 1))
-        second = lax.ppermute(quarters[2], "mem", pairs(members, 1))
+        first = lax.ppermute(quarters[3], "mem", pairs(members, bits[0]))
+        second = lax.ppermute(quarters[2], "mem", pairs(members, bits[0]))
         sums.append([quarters[0], quarters[1], second, first])
+        done.append(1)
     pieces = {"own": [], "both": [], "other": []}
     for k, window in enumerate(windows):
-        for step in steps[min(count - 1 - k, len(steps)) :]:
-            sums[k], _ = step(*sums[k])
+        for bit in bits[done[k] :]:
+            sums[k], _ = advanced(sums[k], bit)
         pieces[window.side].append(exponent_of(sum(sums[k]), members))
 
     other = lax.ppermute(jnp.stack(pieces["other"]), "band", swap)
@@ -536,30 +532,21 @@
             trades.append((m * 2 + b, mate[0] * 2 + mate[1]))
     both = lax.ppermute(pieces["both"][0], ("mem", "band"), trades)
 
-    def gathered(stack):
-        line = [lax.ppermute(stack, "mem", shifts[d]) for d in range(around - 1, 0, -1)] + [stack]
-        mine = jnp.stack(line, axis=1)
-        beside = lax.ppermute(mine, "mem", pairs(members, 2))
-        return [mine, beside, *(lax.ppermute(part, "mem", pairs(members, 1)) for part in (mine, beside))]
-
-    def places(rows):
-        return jnp.stack([core, side, along] + [jnp.asarray(value, jnp.int32) for pair in rows for value in pair])
-
-    height = nlat // 2
-    half, far = LANE // 2, 1 - band
-    early = []
-    for k in range(len(pieces["other"])):
-        row = choose(band, (k * LANE, height - (k + 1) * LANE))
-        early.append((far, far, row, row + half))
-    row = choose(band, (height - half, 0))
-    early.append((0, 1, row, row))
-    late = []
-    for k in range(len(pieces["own"])):
-        row = choose(band, (height - half - (k + 1) * LANE, half + k * LANE))
-        late.append((band, band, row, row + half))
-    shape = (levels, height, NLON)
-    out = put(None, shape, places(early), gathered(jnp.concatenate([other, both[None]])))
-    return put(out, shape, places(late), gathered(jnp.stack(pieces["own"])))
+    early = gathered(jnp.concatenate([other, both[None]]))
+    other, both = early[:-1], early[-1]
+    middle = both.shape[0] // 2
+    low, high = both[:middle], both[middle:]
+    rest = jnp.zeros((nlat // 2 - middle, NLON), jnp.float32)
+    down = jnp.stack([jnp.concatenate([rest, low]), jnp.concatenate([*other, high])])
+    up = jnp.stack([jnp.concatenate([low, *other[::-1]]), jnp.concatenate([high, rest])])
+    out = jnp.where(band == 0, down, up)
+
+    own = gathered(jnp.stack(pieces["own"]))
+    for k, block in enumerate(own):
+        width = block.shape[0]
+        row = choose(band, (nlat // 2 - middle - (k + 1) * width, middle + k * width))
+        out = lax.dynamic_update_slice(out, block[None], (band, row.astype(jnp.int32), jnp.int32(0)))
+    return out
 
 
 def per_device(coeffs):

time: 212 us -> 192 us (0.906)
  starting transfers between devices: 59.9 us -> 36.4 us
  waiting for transfers between devices: 60.9 us -> 81 us
  other arithmetic: 13.7 us -> 7 us
  Pallas kernels: 67.1 us -> 61.5 us
  local copies, waits for them, and re-layouts: 8.5 us -> 4.75 us
    ppermute x46 -> x37, waiting for transfers between devices: 52.5 us -> 76.7 us  [the longest x10 42.3 us: halved(): lax.ppermute(leaves, 'mem', pairs(members, bit))]
    ppermute x46 -> x37, starting transfers between devices: 54.5 us -> 30.9 us  [the longest x10 12.3 us: halved(): lax.ppermute(leaves, 'mem', pairs(members, bit))]
    add x5, other arithmetic: 7.87 us -> 1.06 us  [across(): leaves = passed + passed_more]
    pallas_call x5 -> x0, Pallas kernels: 5.76 us -> none  [the longest x2 5.76 us: put(): pl.pallas_call(functools.partial(put_kernel, count), in_specs=[pl.BlockSp...]
    ppermute x1, waiting for transfers between devices: 8.37 us -> 4.26 us  [by_levels(): remotes = [lax.ppermute(piece, 'band', swap)]]
    ppermute x3 -> x0, local copies, waits for them, and re-layouts: 2.47 us -> none  [the longest x2 1.65 us: gathered(): lax.ppermute(part, 'mem', pairs(members, 1))]
  transfers between devices with their start and end apart: 49 -> 40, of which waited for: 15 -> 18; matrix products, arithmetic and copies ran while one was open for 9% -> 4% of each run, Pallas kernels for 29% -> 31%
where the time goes in v9:
time: 192 us; the launch traced here: 191 us
  waiting for transfers between devices  81 us (42%)
  Pallas kernels  61.5 us (32%)
  starting transfers between devices  36.4 us (19%)
  other arithmetic  7 us (4%)
  local copies, waits for them, and re-layouts  4.75 us (2%)
    pallas_call x5, Pallas kernels, window_tensor(): pl.pallas_call(functools.partial(window_kernel, window, depth, len(waits)...  51.4 us
    ppermute x10, waiting for transfers between devices, halved(): lax.ppermute(leaves, 'mem', pairs(members, bit))  42.3 us
    ppermute x8, waiting for transfers between devices, doubled(): beside = lax.ppermute(part, 'mem', pairs(members, bit))  28.9 us
    ppermute x10, starting transfers between devices, halved(): lax.ppermute(leaves, 'mem', pairs(members, bit))  12.3 us
    pallas_call x3, Pallas kernels, pieces_of(): pl.pallas_call(functools.partial(pieces_kernel, windows, slots, count), i...  10.1 us
    ppermute x5, starting transfers between devices, across(): lax.ppermute(leaves, 'mem', pairs(members, bit))  6.84 us
    ppermute x4, waiting for transfers between devices, by_levels(): remotes += [lax.ppermute(piece, 'band', swap) for piece in outgoing]  4.94 us
    ppermute x1, waiting for transfers between devices, by_levels(): remotes = [lax.ppermute(piece, 'band', swap)]  4.26 us
  transfers between devices with their start and end apart: 40, of which 18 were waited for; matrix products, arithmetic and copies ran while one was open for 4% of the time, Pallas kernels for 31%

profile of v9, /device:TPU:0, one launch (start us, length us, event | category | flops | bytes accessed | tf_op | source)
XLA Modules:
  0.0 191.2 jit_solution(1010015975493750359)
XLA Ops:
  0.0 2.6 %pieces_of.4 = f32[2,136,640]{2,1,0:T(8,128)} custom-call(s32[1]{0:T(128)} %bitcast.4.level_ref, f32[2,2,640,640]{3,2,1,0:T(8,128)} %bitcast.24), custom_call_target="tpu_custom_call" | custom-call | bytes 5242880 | tf_op jit(solution)/shard_map/pieces_of/pallas_call | solution.py:208
  2.6 3.0 %collective-permute-start = (f32[2,136,640]{2,1,0:T(8,128)}, f32[2,136,640]{2,1,0:T(8,128)S(1)}, u32[]{:S(2)}, u32[]{:S(2)}) collective-permute-start(f32[2,136,640]{2,1,0:T(8,128)} %pieces_of.4), channel_id=1, source_target_pairs={{0,1},{1,0},{2,3},{3,2},{4,5},{5,4},{6,7},{7,6},{8,9},{9,8},{10,11... | collective-permute-start | bytes 2088968 | tf_op jit(solution)/shard_map/ppermute | solution.py:473
  5.6 3.6 %pieces_of.5 = (f32[2,128,640]{2,1,0:T(8,128)}, f32[2,128,640]{2,1,0:T(8,128)}, f32[2,128,640]{2,1,0:T(8,128)}, f32[2,120,640]{2,1,0:T(8,128)}) custom-call(s32[1]{0:T(128)} %bitcast.4.level_ref, f32[2,2,640,640]{3,2,1,0:T(8,128)} %bitcast.25), custom_call_target="tpu_custom_call" | custom-call | bytes 10485760 | tf_op jit(solution)/shard_map/pieces_of/pallas_call | solution.py:208
  9.3 2.0 %collective-permute-start.13 = (f32[2,128,640]{2,1,0:T(8,128)}, f32[2,128,640]{2,1,0:T(8,128)S(1)}, u32[]{:S(2)}, u32[]{:S(2)}) collective-permute-start(f32[2,128,640]{2,1,0:T(8,128)} %get-tuple-element.51), channel_id=1, source_target_pairs={{0,1},{1,0},{2,3},{3,2},{4,5},{5,4},{6,7},{7,6},{8,9},{9,8},{10,11... | collective-permute-start | bytes 1966088 | tf_op jit(solution)/shard_map/ppermute | solution.py:475
  11.3 1.9 %collective-permute-start.30 = (f32[2,120,640]{2,1,0:T(8,128)}, f32[2,120,640]{2,1,0:T(8,128)}, u32[]{:S(2)}, u32[]{:S(2)}) collective-permute-start(f32[2,120,640]{2,1,0:T(8,128)} %get-tuple-element.65), channel_id=1, source_target_pairs={{0,1},{1,0},{2,3},{3,2},{4,5},{5,4},{6,7},{7,6},{8,9},{9,8},{10,11... | collective-permute-start | bytes 1843208 | tf_op jit(solution)/shard_map/ppermute | solution.py:475
  13.3 4.0 %pieces_of.3 = (f32[2,136,640]{2,1,0:T(8,128)}, f32[2,128,640]{2,1,0:T(8,128)}, f32[2,128,640]{2,1,0:T(8,128)}, f32[2,128,640]{2,1,0:T(8,128)}, f32[2,120,640]{2,1,0:T(8,128)}) custom-call(s32[1]{0:T(128)} %bitcast.level_ref, f32[2,2,640,640]{3,2,1,0:T(8,128)} %bitcast.26), custom_call_target="tpu_custom_call" | custom-call | bytes 13107200 | tf_op jit(solution)/shard_map/pieces_of/pallas_call | solution.py:208
  18.0 4.3 %collective-permute-done.refs_2_ = f32[2,136,640]{2,1,0:T(8,128)S(1)} collective-permute-done((f32[2,136,640]{2,1,0:T(8,128)}, f32[2,136,640]{2,1,0:T(8,128)S(1)}, u32[]{:S(2)}, u32[]{:S(2)}) %collective-permute-start) | collective-permute-done | bytes 696352 | tf_op jit(solution)/shard_map/ppermute | solution.py:473
  22.2 0.9 copy-done.14
  23.1 10.5 %window_tensor.5 = (f32[3,32,1280]{2,1,0:T(8,128)}, f32[3,32,1280]{2,1,0:T(8,128)}, f32[3,32,1280]{2,1,0:T(8,128)}, f32[3,32,1280]{2,1,0:T(8,128)}, f32[2,16,1280]{2,1,0:T(8,128)}) custom-call(s32[3]{0:T(128)} %pad_add_fusion.refs_0_, f32[2,136,640]{2,1,0:T(8,128)} %get-tuple-element.38.refs_1_, f32[2,136,640]{2,1,0:T(8,128)} %copy-done.14, ...), custom_call_target="tpu_custom_call" | custom-call | flops 10695475200 | bytes 6635520 | tf_op jit(solution)/shard_map/window_tensor/pallas_call | solution.py:380
  33.7 2.6 %collective-permute-done.6.refs_2_ = f32[2,128,640]{2,1,0:T(8,128)S(1)} collective-permute-done((f32[2,128,640]{2,1,0:T(8,128)}, f32[2,128,640]{2,1,0:T(8,128)S(1)}, u32[]{:S(2)}, u32[]{:S(2)}) %collective-permute-start.6) | collective-permute-done | bytes 655392 | tf_op jit(solution)/shard_map/ppermute | solution.py:475
  36.3 0.8 copy-done.17
  37.1 10.2 %window_tensor.6 = (f32[3,32,1280]{2,1,0:T(8,128)}, f32[3,32,1280]{2,1,0:T(8,128)}, f32[3,32,1280]{2,1,0:T(8,128)}, f32[3,32,1280]{2,1,0:T(8,128)}, f32[2,16,1280]{2,1,0:T(8,128)}) custom-call(s32[3]{0:T(128)} %pad_add_fusion.refs_0_, f32[2,128,640]{2,1,0:T(8,128)} %get-tuple-element.43.refs_1_, f32[2,128,640]{2,1,0:T(8,128)} %copy-done.17, ...), custom_call_target="tpu_custom_call" | custom-call | flops 10066329600 | bytes 6553600 | tf_op jit(solution)/shard_map/window_tensor/pallas_call | solution.py:380
  48.0 2.3 %collective-permute-done.13.refs_2_ = f32[2,128,640]{2,1,0:T(8,128)S(1)} collective-permute-done((f32[2,128,640]{2,1,0:T(8,128)}, f32[2,128,640]{2,1,0:T(8,128)S(1)}, u32[]{:S(2)}, u32[]{:S(2)}) %collective-permute-start.13) | collective-permute-done | bytes 655392 | tf_op jit(solution)/shard_map/ppermute | solution.py:475
  50.3 2.1 %collective-permute-start.3 = (f32[3,32,1280]{2,1,0:T(8,128)S(1)}, f32[3,32,1280]{2,1,0:T(8,128)S(1)}, u32[]{:S(2)}, u32[]{:S(2)}) collective-permute-start(f32[3,32,1280]{2,1,0:T(8,128)S(1)} %add.307.refs_4_), channel_id=1, source_target_pairs={{0,4},{2,6},{4,0},{6,2},{8,12},{10,14},{12,8},{14,10},{16,20},{18,... | collective-permute-start | bytes 1474568 | tf_op jit(solution)/shard_map/ppermute | solution.py:493
  52.4 10.4 %window_tensor.7 = (f32[3,32,1280]{2,1,0:T(8,128)}, f32[3,32,1280]{2,1,0:T(8,128)}, f32[3,32,1280]{2,1,0:T(8,128)}, f32[3,32,1280]{2,1,0:T(8,128)}, f32[2,16,1280]{2,1,0:T(8,128)}) custom-call(s32[3]{0:T(128)} %pad_add_fusion.refs_0_, f32[2,128,640]{2,1,0:T(8,128)} %get-tuple-element.50.refs_1_, f32[2,128,640]{2,1,0:T(8,128)} %copy-done.16, ...), custom_call_target="tpu_custom_call" | custom-call | flops 10066329600 | bytes 6553600 | tf_op jit(solution)/shard_map/window_tensor/pallas_call | solution.py:380
  63.0 0.9 add.322.refs_4_
  65.6 1.6 collective-permute-start.4
  67.2 10.2 %window_tensor.8 = (f32[3,32,1280]{2,1,0:T(8,128)}, f32[3,32,1280]{2,1,0:T(8,128)}, f32[3,32,1280]{2,1,0:T(8,128)}, f32[3,32,1280]{2,1,0:T(8,128)}, f32[2,16,1280]{2,1,0:T(8,128)}) custom-call(s32[3]{0:T(128)} %pad_add_fusion.refs_0_, f32[2,128,640]{2,1,0:T(8,128)} %get-tuple-element.57.refs_1_, f32[2,128,640]{2,1,0:T(8,128)} %copy-done.15, ...), custom_call_target="tpu_custom_call" | custom-call | flops 10066329600 | bytes 6553600 | tf_op jit(solution)/shard_map/window_tensor/pallas_call | solution.py:380
  78.5 1.8 dynamic-slice_add_fusion.7
  80.3 0.9 collective-permute-start.10
  81.8 1.2 collective-permute-start.16
  83.0 10.1 %window_tensor.9 = (f32[3,32,1280]{2,1,0:T(8,128)}, f32[3,32,1280]{2,1,0:T(8,128)}, f32[3,32,1280]{2,1,0:T(8,128)}, f32[3,32,1280]{2,1,0:T(8,128)}) custom-call(s32[3]{0:T(128)} %pad_add_fusion.refs_0_, f32[2,120,640]{2,1,0:T(8,128)} %get-tuple-element.64.refs_1_, f32[2,120,640]{2,1,0:T(8,128)} %collective-permute-done.30.refs_2_, ...), custom_call_target="tpu_custom_call" | custom-call | flops 9437184000 | bytes 6471680 | tf_op jit(solution)/shard_map/window_tensor/pallas_call | solution.py:380
  93.1 2.7 %collective-permute-start.5 = (f32[3,8,1280]{2,1,0:T(8,128)S(1)}, f32[3,8,1280]{2,1,0:T(8,128)S(1)}, u32[]{:S(2)}, u32[]{:S(2)}) collective-permute-start(f32[3,8,1280]{2,1,0:T(8,128)S(1)} %copy-done.13), channel_id=1, source_target_pairs={{0,16},{2,18},{4,20},{6,22},{8,24},{10,26},{12,28},{14,30},{16,0},... | collective-permute-start | bytes 368648 | tf_op jit(solution)/shard_map/ppermute | solution.py:488
  95.8 5.9 %collective-permute-done.5 = f32[3,8,1280]{2,1,0:T(8,128)S(1)} collective-permute-done((f32[3,8,1280]{2,1,0:T(8,128)S(1)}, f32[3,8,1280]{2,1,0:T(8,128)S(1)}, u32[]{:S(2)}, u32[]{:S(2)}) %collective-permute-start.5) | collective-permute-done | bytes 122912 | tf_op jit(solution)/shard_map/ppermute | solution.py:488
  101.8 8.0 %collective-permute-done.11 = f32[3,8,1280]{2,1,0:T(8,128)S(1)} collective-permute-done((f32[3,8,1280]{2,1,0:T(8,128)S(1)}, f32[3,8,1280]{2,1,0:T(8,128)S(1)}, u32[]{:S(2)}, u32[]{:S(2)}) %collective-permute-start.11) | collective-permute-done | bytes 122912 | tf_op jit(solution)/shard_map/ppermute | solution.py:488
  110.2 8.3 %collective-permute-done.17 = f32[3,16,1280]{2,1,0:T(8,128)S(1)} collective-permute-done((f32[3,16,1280]{2,1,0:T(8,128)S(1)}, f32[3,16,1280]{2,1,0:T(8,128)S(1)}, u32[]{:S(2)}, u32[]{:S(2)}) %collective-permute-start.17) | collective-permute-done | bytes 245792 | tf_op jit(solution)/shard_map/ppermute | solution.py:488
  118.6 1.6 collective-permute-start.12
  120.2 1.4 collective-permute-start.27
  121.6 5.4 %collective-permute-done.18 = f32[3,8,1280]{2,1,0:T(8,128)S(1)} collective-permute-done((f32[3,8,1280]{2,1,0:T(8,128)S(1)}, f32[3,8,1280]{2,1,0:T(8,128)S(1)}, u32[]{:S(2)}, u32[]{:S(2)}) %collective-permute-start.18) | collective-permute-done | bytes 122912 | tf_op jit(solution)/shard_map/ppermute | solution.py:488
  127.0 0.9 collective-permute-start.19
  128.0 2.9 %collective-permute-start.31 = (f32[3,32,1280]{2,1,0:T(8,128)}, f32[3,32,1280]{2,1,0:T(8,128)S(1)}, u32[]{:S(2)}, u32[]{:S(2)}) collective-permute-start(f32[3,32,1280]{2,1,0:T(8,128)} %get-tuple-element.68), channel_id=1, source_target_pairs={{0,2},{2,0},{4,6},{6,4},{8,10},{10,8},{12,14},{14,12},{16,18},{18,... | collective-permute-start | bytes 1474568 | tf_op jit(solution)/shard_map/ppermute | solution.py:518
  131.0 1.4 collective-permute-start.33
  132.9 3.3 %collective-permute-start.28 = (f32[3,16,1280]{2,1,0:T(8,128)S(1)}, f32[3,16,1280]{2,1,0:T(8,128)S(1)}, u32[]{:S(2)}, u32[]{:S(2)}) collective-permute-start(f32[3,16,1280]{2,1,0:T(8,128)S(1)} %get-tuple-element.76), channel_id=1, source_target_pairs={{0,8},{2,10},{4,12},{6,14},{8,0},{10,2},{12,4},{14,6},{16,24},{18,... | collective-permute-start | bytes 737288 | tf_op jit(solution)/shard_map/ppermute | solution.py:488
  136.2 4.0 %collective-permute-done.20 = f32[3,8,1280]{2,1,0:T(8,128)S(1)} collective-permute-done((f32[3,8,1280]{2,1,0:T(8,128)S(1)}, f32[3,8,1280]{2,1,0:T(8,128)S(1)}, u32[]{:S(2)}, u32[]{:S(2)}) %collective-permute-start.20) | collective-permute-done | bytes 122912 | tf_op jit(solution)/shard_map/ppermute | solution.py:499
  140.3 3.6 %collective-permute-done.28 = f32[3,16,1280]{2,1,0:T(8,128)S(1)} collective-permute-done((f32[3,16,1280]{2,1,0:T(8,128)S(1)}, f32[3,16,1280]{2,1,0:T(8,128)S(1)}, u32[]{:S(2)}, u32[]{:S(2)}) %collective-permute-start.28) | collective-permute-done | bytes 245792 | tf_op jit(solution)/shard_map/ppermute | solution.py:488
  144.3 2.5 %collective-permute-start.34 = (f32[3,16,1280]{2,1,0:T(8,128)S(1)}, f32[3,16,1280]{2,1,0:T(8,128)S(1)}, u32[]{:S(2)}, u32[]{:S(2)}) collective-permute-start(f32[3,16,1280]{2,1,0:T(8,128)S(1)} %get-tuple-element.78), channel_id=1, source_target_pairs={{0,8},{2,10},{4,12},{6,14},{8,0},{10,2},{12,4},{14,6},{16,24},{18,... | collective-permute-start | bytes 737288 | tf_op jit(solution)/shard_map/ppermute | solution.py:488
  146.7 4.5 %collective-permute-done.21 = f32[3,16,1280]{2,1,0:T(8,128)S(1)} collective-permute-done((f32[3,16,1280]{2,1,0:T(8,128)S(1)}, f32[3,16,1280]{2,1,0:T(8,128)S(1)}, u32[]{:S(2)}, u32[]{:S(2)}) %collective-permute-start.21) | collective-permute-done | bytes 245792 | tf_op jit(solution)/shard_map/ppermute | solution.py:499
  151.3 1.4 collective-permute-start.22
  152.6 4.0 %collective-permute-done.34 = f32[3,16,1280]{2,1,0:T(8,128)S(1)} collective-permute-done((f32[3,16,1280]{2,1,0:T(8,128)S(1)}, f32[3,16,1280]{2,1,0:T(8,128)S(1)}, u32[]{:S(2)}, u32[]{:S(2)}) %collective-permute-start.34) | collective-permute-done | bytes 245792 | tf_op jit(solution)/shard_map/ppermute | solution.py:488
  156.6 1.0 collective-permute-start.35
  157.6 7.2 %collective-permute-done.35 = f32[3,8,1280]{2,1,0:T(8,128)S(1)} collective-permute-done((f32[3,8,1280]{2,1,0:T(8,128)S(1)}, f32[3,8,1280]{2,1,0:T(8,128)S(1)}, u32[]{:S(2)}, u32[]{:S(2)}) %collective-permute-start.35) | collective-permute-done | bytes 122912 | tf_op jit(solution)/shard_map/ppermute | solution.py:488
  165.2 6.0 %collective-permute-done.36 = f32[2,8,1280]{2,1,0:T(8,128)S(1)} collective-permute-done((f32[2,8,1280]{2,1,0:T(8,128)S(1)}, f32[2,8,1280]{2,1,0:T(8,128)S(1)}, u32[]{:S(2)}, u32[]{:S(2)}) %collective-permute-start.36) | collective-permute-done | bytes 81952 | tf_op jit(solution)/shard_map/ppermute | solution.py:499
  171.3 6.1 %collective-permute-done.37 = f32[2,16,1280]{2,1,0:T(8,128)S(1)} collective-permute-done((f32[2,16,1280]{2,1,0:T(8,128)S(1)}, f32[2,16,1280]{2,1,0:T(8,128)S(1)}, u32[]{:S(2)}, u32[]{:S(2)}) %collective-permute-start.37) | collective-permute-done | bytes 163872 | tf_op jit(solution)/shard_map/ppermute | solution.py:499
  177.4 1.3 collective-permute-start.38
  178.7 7.5 %collective-permute-done.38 = f32[2,32,1280]{2,1,0:T(8,128)S(1)} collective-permute-done((f32[2,32,1280]{2,1,0:T(8,128)S(1)}, f32[2,32,1280]{2,1,0:T(8,128)S(1)}, u32[]{:S(2)}, u32[]{:S(2)}) %collective-permute-start.38) | collective-permute-done | bytes 327712 | tf_op jit(solution)/shard_map/ppermute | solution.py:499
  187.6 0.8 collective-permute-done.39
  188.6 1.7 copy-done
  190.3 0.9 slice_dynamic-update-slice_fusion
  (119 shorter events, 8.8 us)
Async XLA Ops:
  2.6 19.6 %collective-permute-start = (f32[2,136,640]{2,1,0:T(8,128)}, f32[2,136,640]{2,1,0:T(8,128)S(1)}, u32[]{:S(2)}, u32[]{:S(2)}) collective-permute-start(f32[2,136,640]{2,1,0:T(8,128)} %pieces_of.4), channel_id=1, source_target_pairs={{0,1},{1,0},{2,3},{3,2},{4,5},{5,4},{6,7},{7,6},{8,9},{9,8},{10,11... | collective-permute-start | bytes 2088968 | tf_op jit(solution)/shard_map/ppermute | solution.py:473
  9.2 27.1 %collective-permute-start.6 = (f32[2,128,640]{2,1,0:T(8,128)}, f32[2,128,640]{2,1,0:T(8,128)S(1)}, u32[]{:S(2)}, u32[]{:S(2)}) collective-permute-start(f32[2,128,640]{2,1,0:T(8,128)} %get-tuple-element.44), channel_id=1, source_target_pairs={{0,1},{1,0},{2,3},{3,2},{4,5},{5,4},{6,7},{7,6},{8,9},{9,8},{10,11... | collective-permute-start | bytes 1966088 | tf_op jit(solution)/shard_map/ppermute | solution.py:475
  9.3 41.0 %collective-permute-start.13 = (f32[2,128,640]{2,1,0:T(8,128)}, f32[2,128,640]{2,1,0:T(8,128)S(1)}, u32[]{:S(2)}, u32[]{:S(2)}) collective-permute-start(f32[2,128,640]{2,1,0:T(8,128)} %get-tuple-element.51), channel_id=1, source_target_pairs={{0,1},{1,0},{2,3},{3,2},{4,5},{5,4},{6,7},{7,6},{8,9},{9,8},{10,11... | collective-permute-start | bytes 1966088 | tf_op jit(solution)/shard_map/ppermute | solution.py:475
  11.3 54.4 %collective-permute-start.24 = (f32[2,128,640]{2,1,0:T(8,128)}, f32[2,128,640]{2,1,0:T(8,128)S(1)}, u32[]{:S(2)}, u32[]{:S(2)}) collective-permute-start(f32[2,128,640]{2,1,0:T(8,128)} %get-tuple-element.58), channel_id=1, source_target_pairs={{0,1},{1,0},{2,3},{3,2},{4,5},{5,4},{6,7},{7,6},{8,9},{9,8},{10,11... | collective-permute-start | bytes 1966088 | tf_op jit(solution)/shard_map/ppermute | solution.py:475
  11.3 70.5 %collective-permute-start.30 = (f32[2,120,640]{2,1,0:T(8,128)}, f32[2,120,640]{2,1,0:T(8,128)}, u32[]{:S(2)}, u32[]{:S(2)}) collective-permute-start(f32[2,120,640]{2,1,0:T(8,128)} %get-tuple-element.65), channel_id=1, source_target_pairs={{0,1},{1,0},{2,3},{3,2},{4,5},{5,4},{6,7},{7,6},{8,9},{9,8},{10,11... | collective-permute-start | bytes 1843208 | tf_op jit(solution)/shard_map/ppermute | solution.py:475
  33.6 13.7 %collective-permute-start.2 = (f32[3,32,1280]{2,1,0:T(8,128)}, f32[3,32,1280]{2,1,0:T(8,128)S(1)}, u32[]{:S(2)}, u32[]{:S(2)}) collective-permute-start(f32[3,32,1280]{2,1,0:T(8,128)} %get-tuple-element.42), channel_id=1, source_target_pairs={{0,2},{2,0},{4,6},{6,4},{8,10},{10,8},{12,14},{14,12},{16,18},{18,... | collective-permute-start | bytes 1474568 | tf_op jit(solution)/shard_map/ppermute | solution.py:517
  37.1 26.7 %collective-permute-start.1 = (f32[3,32,1280]{2,1,0:T(8,128)}, f32[3,32,1280]{2,1,0:T(8,128)S(1)}, u32[]{:S(2)}, u32[]{:S(2)}) collective-permute-start(f32[3,32,1280]{2,1,0:T(8,128)} %get-tuple-element.40), channel_id=1, source_target_pairs={{0,2},{2,0},{4,6},{6,4},{8,10},{10,8},{12,14},{14,12},{16,18},{18,... | collective-permute-start | bytes 1474568 | tf_op jit(solution)/shard_map/ppermute | solution.py:518
  37.1 10.8 %copy-start.12 = (f32[3,32,1280]{2,1,0:T(8,128)S(1)}, f32[3,32,1280]{2,1,0:T(8,128)}, u32[]{:S(2)}) copy-start(f32[3,32,1280]{2,1,0:T(8,128)} %get-tuple-element.41) | copy-start | bytes 1474564
  47.3 15.5 %collective-permute-start.8 = (f32[3,32,1280]{2,1,0:T(8,128)}, f32[3,32,1280]{2,1,0:T(8,128)S(1)}, u32[]{:S(2)}, u32[]{:S(2)}) collective-permute-start(f32[3,32,1280]{2,1,0:T(8,128)} %get-tuple-element.49), channel_id=1, source_target_pairs={{0,2},{2,0},{4,6},{6,4},{8,10},{10,8},{12,14},{14,12},{16,18},{18,... | collective-permute-start | bytes 1474568 | tf_op jit(solution)/shard_map/ppermute | solution.py:517
  50.3 14.3 %collective-permute-start.3 = (f32[3,32,1280]{2,1,0:T(8,128)S(1)}, f32[3,32,1280]{2,1,0:T(8,128)S(1)}, u32[]{:S(2)}, u32[]{:S(2)}) collective-permute-start(f32[3,32,1280]{2,1,0:T(8,128)S(1)} %add.307.refs_4_), channel_id=1, source_target_pairs={{0,4},{2,6},{4,0},{6,2},{8,12},{10,14},{12,8},{14,10},{16,20},{18,... | collective-permute-start | bytes 1474568 | tf_op jit(solution)/shard_map/ppermute | solution.py:493
  52.4 10.5 %copy-start.10 = (f32[3,32,1280]{2,1,0:T(8,128)S(1)}, f32[3,32,1280]{2,1,0:T(8,128)}, u32[]{:S(2)}) copy-start(f32[3,32,1280]{2,1,0:T(8,128)} %get-tuple-element.48) | copy-start | bytes 1474564
  62.9 14.7 %collective-permute-start.7 = (f32[3,32,1280]{2,1,0:T(8,128)}, f32[3,32,1280]{2,1,0:T(8,128)S(1)}, u32[]{:S(2)}, u32[]{:S(2)}) collective-permute-start(f32[3,32,1280]{2,1,0:T(8,128)} %get-tuple-element.47), channel_id=1, source_target_pairs={{0,2},{2,0},{4,6},{6,4},{8,10},{10,8},{12,14},{14,12},{16,18},{18,... | collective-permute-start | bytes 1474568 | tf_op jit(solution)/shard_map/ppermute | solution.py:518
  63.8 14.3 %collective-permute-start.9 = (f32[3,32,1280]{2,1,0:T(8,128)}, f32[3,32,1280]{2,1,0:T(8,128)}, u32[]{:S(2)}, u32[]{:S(2)}) collective-permute-start(f32[3,32,1280]{2,1,0:T(8,128)} %add.322.refs_4_), channel_id=1, source_target_pairs={{0,4},{2,6},{4,0},{6,2},{8,12},{10,14},{12,8},{14,10},{16,20},{18,... | collective-permute-start | bytes 1474568 | tf_op jit(solution)/shard_map/ppermute | solution.py:493
  64.7 12.8 %collective-permute-start.15 = (f32[3,32,1280]{2,1,0:T(8,128)}, f32[3,32,1280]{2,1,0:T(8,128)S(1)}, u32[]{:S(2)}, u32[]{:S(2)}) collective-permute-start(f32[3,32,1280]{2,1,0:T(8,128)} %get-tuple-element.56), channel_id=1, source_target_pairs={{0,2},{2,0},{4,6},{6,4},{8,10},{10,8},{12,14},{14,12},{16,18},{18,... | collective-permute-start | bytes 1474568 | tf_op jit(solution)/shard_map/ppermute | solution.py:517
  65.6 14.6 %collective-permute-start.4 = (f32[3,16,1280]{2,1,0:T(8,128)}, f32[3,16,1280]{2,1,0:T(8,128)S(1)}, u32[]{:S(2)}, u32[]{:S(2)}) collective-permute-start(f32[3,16,1280]{2,1,0:T(8,128)} %get-tuple-element.80.refs_5_), channel_id=1, source_target_pairs={{0,8},{2,10},{4,12},{6,14},{8,0},{10,2},{12,4},{14,6},{16,24},{18,... | collective-permute-start | bytes 737288 | tf_op jit(solution)/shard_map/ppermute | solution.py:488
  67.2 10.3 %copy-start.9 = (f32[3,32,1280]{2,1,0:T(8,128)S(1)}, f32[3,32,1280]{2,1,0:T(8,128)}, u32[]{:S(2)}) copy-start(f32[3,32,1280]{2,1,0:T(8,128)} %get-tuple-element.55) | copy-start | bytes 1474564
  77.4 32.5 %collective-permute-start.14 = (f32[3,32,1280]{2,1,0:T(8,128)}, f32[3,32,1280]{2,1,0:T(8,128)S(1)}, u32[]{:S(2)}, u32[]{:S(2)}) collective-permute-start(f32[3,32,1280]{2,1,0:T(8,128)} %get-tuple-element.54), channel_id=1, source_target_pairs={{0,2},{2,0},{4,6},{6,4},{8,10},{10,8},{12,14},{14,12},{16,18},{18,... | collective-permute-start | bytes 1474568 | tf_op jit(solution)/shard_map/ppermute | solution.py:518
  77.6 42.5 %collective-permute-start.26 = (f32[3,32,1280]{2,1,0:T(8,128)}, f32[3,32,1280]{2,1,0:T(8,128)S(1)}, u32[]{:S(2)}, u32[]{:S(2)}) collective-permute-start(f32[3,32,1280]{2,1,0:T(8,128)} %get-tuple-element.63), channel_id=1, source_target_pairs={{0,2},{2,0},{4,6},{6,4},{8,10},{10,8},{12,14},{14,12},{16,18},{18,... | collective-permute-start | bytes 1474568 | tf_op jit(solution)/shard_map/ppermute | solution.py:517
  78.2 54.3 %collective-permute-start.25 = (f32[3,32,1280]{2,1,0:T(8,128)}, f32[3,32,1280]{2,1,0:T(8,128)S(1)}, u32[]{:S(2)}, u32[]{:S(2)}) collective-permute-start(f32[3,32,1280]{2,1,0:T(8,128)} %get-tuple-element.61), channel_id=1, source_target_pairs={{0,2},{2,0},{4,6},{6,4},{8,10},{10,8},{12,14},{14,12},{16,18},{18,... | collective-permute-start | bytes 1474568 | tf_op jit(solution)/shard_map/ppermute | solution.py:518
  80.3 12.8 %collective-permute-start.10 = (f32[3,16,1280]{2,1,0:T(8,128)}, f32[3,16,1280]{2,1,0:T(8,128)S(1)}, u32[]{:S(2)}, u32[]{:S(2)}) collective-permute-start(f32[3,16,1280]{2,1,0:T(8,128)} %get-tuple-element.82.refs_5_), channel_id=1, source_target_pairs={{0,8},{2,10},{4,12},{6,14},{8,0},{10,2},{12,4},{14,6},{16,24},{18,... | collective-permute-start | bytes 737288 | tf_op jit(solution)/shard_map/ppermute | solution.py:488
  81.8 28.1 %collective-permute-start.16 = (f32[3,32,1280]{2,1,0:T(8,128)S(1)}, f32[3,32,1280]{2,1,0:T(8,128)S(1)}, u32[]{:S(2)}, u32[]{:S(2)}) collective-permute-start(f32[3,32,1280]{2,1,0:T(8,128)S(1)} %add.334.refs_4_), channel_id=1, source_target_pairs={{0,4},{2,6},{4,0},{6,2},{8,12},{10,14},{12,8},{14,10},{16,20},{18,... | collective-permute-start | bytes 1474568 | tf_op jit(solution)/shard_map/ppermute | solution.py:493
  93.1 16.8 %copy-start.3 = (f32[3,32,1280]{2,1,0:T(8,128)S(1)}, f32[3,32,1280]{2,1,0:T(8,128)}, u32[]{:S(2)}) copy-start(f32[3,32,1280]{2,1,0:T(8,128)} %get-tuple-element.53) | copy-start | bytes 1474564
  93.1 8.5 %collective-permute-start.5 = (f32[3,8,1280]{2,1,0:T(8,128)S(1)}, f32[3,8,1280]{2,1,0:T(8,128)S(1)}, u32[]{:S(2)}, u32[]{:S(2)}) collective-permute-start(f32[3,8,1280]{2,1,0:T(8,128)S(1)} %copy-done.13), channel_id=1, source_target_pairs={{0,16},{2,18},{4,20},{6,22},{8,24},{10,26},{12,28},{14,30},{16,0},... | collective-permute-start | bytes 368648 | tf_op jit(solution)/shard_map/ppermute | solution.py:488
  101.7 8.2 %collective-permute-start.11 = (f32[3,8,1280]{2,1,0:T(8,128)S(1)}, f32[3,8,1280]{2,1,0:T(8,128)S(1)}, u32[]{:S(2)}, u32[]{:S(2)}) collective-permute-start(f32[3,8,1280]{2,1,0:T(8,128)S(1)} %dynamic-slice_add_fusion.13), channel_id=1, source_target_pairs={{0,16},{2,18},{4,20},{6,22},{8,24},{10,26},{12,28},{14,30},{16,0},... | collective-permute-start | bytes 368648 | tf_op jit(solution)/shard_map/ppermute | solution.py:488
  101.8 18.4 %copy-start.4 = (f32[3,32,1280]{2,1,0:T(8,128)S(1)}, f32[3,32,1280]{2,1,0:T(8,128)}, u32[]{:S(2)}) copy-start(f32[3,32,1280]{2,1,0:T(8,128)} %get-tuple-element.62) | copy-start | bytes 1474564
  109.9 18.1 %collective-permute-start.32 = (f32[3,32,1280]{2,1,0:T(8,128)}, f32[3,32,1280]{2,1,0:T(8,128)S(1)}, u32[]{:S(2)}, u32[]{:S(2)}) collective-permute-start(f32[3,32,1280]{2,1,0:T(8,128)} %get-tuple-element.70), channel_id=1, source_target_pairs={{0,2},{2,0},{4,6},{6,4},{8,10},{10,8},{12,14},{14,12},{16,18},{18,... | collective-permute-start | bytes 1474568 | tf_op jit(solution)/shard_map/ppermute | solution.py:517
  110.0 20.9 %copy-start.5 = (f32[3,32,1280]{2,1,0:T(8,128)S(1)}, f32[3,32,1280]{2,1,0:T(8,128)}, u32[]{:S(2)}) copy-start(f32[3,32,1280]{2,1,0:T(8,128)} %get-tuple-element.69) | copy-start | bytes 1474564
  110.0 8.4 %collective-permute-start.17 = (f32[3,16,1280]{2,1,0:T(8,128)S(1)}, f32[3,16,1280]{2,1,0:T(8,128)S(1)}, u32[]{:S(2)}, u32[]{:S(2)}) collective-permute-start(f32[3,16,1280]{2,1,0:T(8,128)S(1)} %get-tuple-element.84), channel_id=1, source_target_pairs={{0,8},{2,10},{4,12},{6,14},{8,0},{10,2},{12,4},{14,6},{16,24},{18,... | collective-permute-start | bytes 737288 | tf_op jit(solution)/shard_map/ppermute | solution.py:488
  118.5 8.5 %collective-permute-start.18 = (f32[3,8,1280]{2,1,0:T(8,128)S(1)}, f32[3,8,1280]{2,1,0:T(8,128)S(1)}, u32[]{:S(2)}, u32[]{:S(2)}) collective-permute-start(f32[3,8,1280]{2,1,0:T(8,128)S(1)} %dynamic-slice_add_fusion.12), channel_id=1, source_target_pairs={{0,16},{2,18},{4,20},{6,22},{8,24},{10,26},{12,28},{14,30},{16,0},... | collective-permute-start | bytes 368648 | tf_op jit(solution)/shard_map/ppermute | solution.py:488
  118.6 12.4 %collective-permute-start.12 = (f32[2,8,1280]{2,1,0:T(8,128)S(1)}, f32[2,8,1280]{2,1,0:T(8,128)S(1)}, u32[]{:S(2)}, u32[]{:S(2)}) collective-permute-start(f32[2,8,1280]{2,1,0:T(8,128)S(1)} %pad_maximum_fusion.1), channel_id=1, source_target_pairs={{0,1},{1,0},{2,3},{3,2},{4,5},{5,4},{6,7},{7,6},{8,9},{9,8},{10,11... | collective-permute-start | bytes 245768 | tf_op jit(solution)/shard_map/ppermute | solution.py:527
  120.1 12.7 %copy-start.1 = (f32[3,32,1280]{2,1,0:T(8,128)S(1)}, f32[3,32,1280]{2,1,0:T(8,128)}, u32[]{:S(2)}) copy-start(f32[3,32,1280]{2,1,0:T(8,128)} %get-tuple-element.60) | copy-start | bytes 1474564
  120.2 12.6 %collective-permute-start.27 = (f32[3,32,1280]{2,1,0:T(8,128)S(1)}, f32[3,32,1280]{2,1,0:T(8,128)S(1)}, u32[]{:S(2)}, u32[]{:S(2)}) collective-permute-start(f32[3,32,1280]{2,1,0:T(8,128)S(1)} %add.347), channel_id=1, source_target_pairs={{0,4},{2,6},{4,0},{6,2},{8,12},{10,14},{12,8},{14,10},{16,20},{18,... | collective-permute-start | bytes 1474568 | tf_op jit(solution)/shard_map/ppermute | solution.py:493
  127.0 5.3 %collective-permute-start.19 = (f32[8,1280]{1,0:T(8,128)S(1)}, f32[8,1280]{1,0:T(8,128)S(1)}, u32[]{:S(2)}, u32[]{:S(2)}) collective-permute-start(f32[8,1280]{1,0:T(8,128)S(1)} %fusion.18), channel_id=1, source_target_pairs={{0,0},{1,2},{2,1},{3,3},{4,4},{5,6},{6,5},{7,7},{8,8},{9,10},{10,9... | collective-permute-start | bytes 122888 | tf_op jit(solution)/shard_map/ppermute | solution.py:533
  128.0 16.1 %collective-permute-start.31 = (f32[3,32,1280]{2,1,0:T(8,128)}, f32[3,32,1280]{2,1,0:T(8,128)S(1)}, u32[]{:S(2)}, u32[]{:S(2)}) collective-permute-start(f32[3,32,1280]{2,1,0:T(8,128)} %get-tuple-element.68), channel_id=1, source_target_pairs={{0,2},{2,0},{4,6},{6,4},{8,10},{10,8},{12,14},{14,12},{16,18},{18,... | collective-permute-start | bytes 1474568 | tf_op jit(solution)/shard_map/ppermute | solution.py:518
  130.9 13.2 %copy-start.2 = (f32[3,32,1280]{2,1,0:T(8,128)S(1)}, f32[3,32,1280]{2,1,0:T(8,128)}, u32[]{:S(2)}) copy-start(f32[3,32,1280]{2,1,0:T(8,128)} %get-tuple-element.67) | copy-start | bytes 1474564
  131.0 13.2 %collective-permute-start.33 = (f32[3,32,1280]{2,1,0:T(8,128)S(1)}, f32[3,32,1280]{2,1,0:T(8,128)S(1)}, u32[]{:S(2)}, u32[]{:S(2)}) collective-permute-start(f32[3,32,1280]{2,1,0:T(8,128)S(1)} %add.359), channel_id=1, source_target_pairs={{0,4},{2,6},{4,0},{6,2},{8,12},{10,14},{12,8},{14,10},{16,20},{18,... | collective-permute-start | bytes 1474568 | tf_op jit(solution)/shard_map/ppermute | solution.py:493
  132.3 7.9 %collective-permute-start.20 = (f32[3,8,1280]{2,1,0:T(8,128)S(1)}, f32[3,8,1280]{2,1,0:T(8,128)S(1)}, u32[]{:S(2)}, u32[]{:S(2)}) collective-permute-start(f32[3,8,1280]{2,1,0:T(8,128)S(1)} %pad_maximum_fusion), channel_id=1, source_target_pairs={{0,16},{2,18},{4,20},{6,22},{8,24},{10,26},{12,28},{14,30},{16,0},... | collective-permute-start | bytes 368648 | tf_op jit(solution)/shard_map/ppermute | solution.py:499
  132.9 11.0 %collective-permute-start.28 = (f32[3,16,1280]{2,1,0:T(8,128)S(1)}, f32[3,16,1280]{2,1,0:T(8,128)S(1)}, u32[]{:S(2)}, u32[]{:S(2)}) collective-permute-start(f32[3,16,1280]{2,1,0:T(8,128)S(1)} %get-tuple-element.76), channel_id=1, source_target_pairs={{0,8},{2,10},{4,12},{6,14},{8,0},{10,2},{12,4},{14,6},{16,24},{18,... | collective-permute-start | bytes 737288 | tf_op jit(solution)/shard_map/ppermute | solution.py:488
  140.3 11.0 %collective-permute-start.21 = (f32[3,16,1280]{2,1,0:T(8,128)S(1)}, f32[3,16,1280]{2,1,0:T(8,128)S(1)}, u32[]{:S(2)}, u32[]{:S(2)}) collective-permute-start(f32[3,16,1280]{2,1,0:T(8,128)S(1)} %maximum_select_fusion.7), channel_id=1, source_target_pairs={{0,8},{2,10},{4,12},{6,14},{8,0},{10,2},{12,4},{14,6},{16,24},{18,... | collective-permute-start | bytes 737288 | tf_op jit(solution)/shard_map/ppermute | solution.py:499
  143.9 8.7 %collective-permute-start.29 = (f32[3,8,1280]{2,1,0:T(8,128)S(1)}, f32[3,8,1280]{2,1,0:T(8,128)S(1)}, u32[]{:S(2)}, u32[]{:S(2)}) collective-permute-start(f32[3,8,1280]{2,1,0:T(8,128)S(1)} %dynamic-slice_add_fusion.11), channel_id=1, source_target_pairs={{0,16},{2,18},{4,20},{6,22},{8,24},{10,26},{12,28},{14,30},{16,0},... | collective-permute-start | bytes 368648 | tf_op jit(solution)/shard_map/ppermute | solution.py:488
  144.3 12.3 %collective-permute-start.34 = (f32[3,16,1280]{2,1,0:T(8,128)S(1)}, f32[3,16,1280]{2,1,0:T(8,128)S(1)}, u32[]{:S(2)}, u32[]{:S(2)}) collective-permute-start(f32[3,16,1280]{2,1,0:T(8,128)S(1)} %get-tuple-element.78), channel_id=1, source_target_pairs={{0,8},{2,10},{4,12},{6,14},{8,0},{10,2},{12,4},{14,6},{16,24},{18,... | collective-permute-start | bytes 737288 | tf_op jit(solution)/shard_map/ppermute | solution.py:488
  151.3 13.8 %collective-permute-start.22 = (f32[3,32,1280]{2,1,0:T(8,128)S(1)}, f32[3,32,1280]{2,1,0:T(8,128)S(1)}, u32[]{:S(2)}, u32[]{:S(2)}) collective-permute-start(f32[3,32,1280]{2,1,0:T(8,128)S(1)} %maximum_select_fusion.5), channel_id=1, source_target_pairs={{0,4},{2,6},{4,0},{6,2},{8,12},{10,14},{12,8},{14,10},{16,20},{18,... | collective-permute-start | bytes 1474568 | tf_op jit(solution)/shard_map/ppermute | solution.py:499
  156.6 8.2 %collective-permute-start.35 = (f32[3,8,1280]{2,1,0:T(8,128)S(1)}, f32[3,8,1280]{2,1,0:T(8,128)S(1)}, u32[]{:S(2)}, u32[]{:S(2)}) collective-permute-start(f32[3,8,1280]{2,1,0:T(8,128)S(1)} %dynamic-slice_add_fusion.10), channel_id=1, source_target_pairs={{0,16},{2,18},{4,20},{6,22},{8,24},{10,26},{12,28},{14,30},{16,0},... | collective-permute-start | bytes 368648 | tf_op jit(solution)/shard_map/ppermute | solution.py:488
  164.9 6.2 %collective-permute-start.36 = (f32[2,8,1280]{2,1,0:T(8,128)S(1)}, f32[2,8,1280]{2,1,0:T(8,128)S(1)}, u32[]{:S(2)}, u32[]{:S(2)}) collective-permute-start(f32[2,8,1280]{2,1,0:T(8,128)S(1)} %pad_maximum_fusion.2), channel_id=1, source_target_pairs={{0,16},{2,18},{4,20},{6,22},{8,24},{10,26},{12,28},{14,30},{16,0},... | collective-permute-start | bytes 245768 | tf_op jit(solution)/shard_map/ppermute | solution.py:499
  165.1 21.3 %collective-permute-start.23 = (f32[3,64,1280]{2,1,0:T(8,128)S(1)}, f32[3,64,1280]{2,1,0:T(8,128)S(1)}, u32[]{:S(2)}, u32[]{:S(2)}) collective-permute-start(f32[3,64,1280]{2,1,0:T(8,128)S(1)} %maximum_select_fusion.3), channel_id=1, source_target_pairs={{0,2},{2,0},{4,6},{6,4},{8,10},{10,8},{12,14},{14,12},{16,18},{18,... | collective-permute-start | bytes 2949128 | tf_op jit(solution)/shard_map/ppermute | solution.py:499
  171.2 6.2 %collective-permute-start.37 = (f32[2,16,1280]{2,1,0:T(8,128)S(1)}, f32[2,16,1280]{2,1,0:T(8,128)S(1)}, u32[]{:S(2)}, u32[]{:S(2)}) collective-permute-start(f32[2,16,1280]{2,1,0:T(8,128)S(1)} %maximum_select_fusion.8), channel_id=1, source_target_pairs={{0,8},{2,10},{4,12},{6,14},{8,0},{10,2},{12,4},{14,6},{16,24},{18,... | collective-permute-start | bytes 491528 | tf_op jit(solution)/shard_map/ppermute | solution.py:499
  177.4 8.9 %collective-permute-start.38 = (f32[2,32,1280]{2,1,0:T(8,128)S(1)}, f32[2,32,1280]{2,1,0:T(8,128)S(1)}, u32[]{:S(2)}, u32[]{:S(2)}) collective-permute-start(f32[2,32,1280]{2,1,0:T(8,128)S(1)} %maximum_select_fusion.6), channel_id=1, source_target_pairs={{0,4},{2,6},{4,0},{6,2},{8,12},{10,14},{12,8},{14,10},{16,20},{18,... | collective-permute-start | bytes 983048 | tf_op jit(solution)/shard_map/ppermute | solution.py:499
  186.3 2.2 %collective-permute-start.39 = (f32[2,64,1280]{2,1,0:T(8,128)S(1)}, f32[2,64,1280]{2,1,0:T(8,128)S(1)}, u32[]{:S(2)}, u32[]{:S(2)}) collective-permute-start(f32[2,64,1280]{2,1,0:T(8,128)S(1)} %maximum_select_fusion.4), channel_id=1, source_target_pairs={{0,2},{2,0},{4,6},{6,4},{8,10},{10,8},{12,14},{14,12},{16,18},{18,... | collective-permute-start | bytes 1966088 | tf_op jit(solution)/shard_map/ppermute | solution.py:499
  (10 other events, 30.2 us)

commit v10 on v9

--- a/solution.py
+++ b/solution.py
@@ -16,7 +16,7 @@
 LANE = 128
 VMEM_LIMIT = 60 * 1024 * 1024
 KERNEL_WORK = 8
-AHEAD = ((), (), (0,), (1, 0), (2, 1, 0))
+AHEAD = ((), (), (0,), (1, 0), (3, 2, 1, 0))
 
 
 def padded(cells, sides, width):
@@ -222,6 +222,22 @@
         ),
         name="pieces_of",
     )(level.reshape(1), spec)
+
+
+def gate_kernel(*refs):
+    pass
+
+
+def gated(part, waits):
+    return pl.pallas_call(
+        gate_kernel,
+        in_specs=[pl.BlockSpec(memory_space=pl.ANY)] * (1 + len(waits)),
+        out_specs=pl.BlockSpec(memory_space=pl.ANY),
+        out_shape=jax.ShapeDtypeStruct(part.shape, part.dtype),
+        input_output_aliases={0: 0},
+        cost_estimate=pl.CostEstimate(flops=0, transcendentals=0, bytes_accessed=1024),
+        name="gated",
+    )(part, *waits)
 
 
 def east_of(x):
@@ -498,12 +514,8 @@
     def doubled(part, bit):
         beside = lax.ppermute(part, "mem", pairs(members, bit))
         mine = (member // bit) % 2
-        return jnp.where(mine == 0, jnp.concatenate([part, beside], axis=1), jnp.concatenate([beside, part], axis=1))
-
-    def gathered(part):
-        for bit in reversed(bits):
-            part = doubled(part, bit)
-        return part
+        low, high = jnp.concatenate([part, beside], axis=1), jnp.concatenate([beside, part], axis=1)
+        return jnp.where(mine == 0, low, high), beside
 
     carry = None
     sums, done = [], []
@@ -514,25 +526,53 @@
             done[j] += 1
             waits.append(left)
         quarters, carry = window_tensor(window, place, local[k], remotes[k], table, waits, carry)
-        first = lax.ppermute(quarters[3], "mem", pairs(members, bits[0]))
+        sent = quarters[3] if k + 1 < len(windows) else gated(quarters[3], [sums[2][-1], sums[3][-1]])
+        first = lax.ppermute(sent, "mem", pairs(members, bits[0]))
         second = lax.ppermute(quarters[2], "mem", pairs(members, bits[0]))
         sums.append([quarters[0], quarters[1], second, first])
         done.append(1)
-    pieces = {"own": [], "both": [], "other": []}
-    for k, window in enumerate(windows):
-        for bit in bits[done[k] :]:
-            sums[k], _ = advanced(sums[k], bit)
-        pieces[window.side].append(exponent_of(sum(sums[k]), members))
-
-    other = lax.ppermute(jnp.stack(pieces["other"]), "band", swap)
+    parts_of_last = quarters[0]
+
+    def step(k, waits=()):
+        if waits:
+            sums[k] = [gated(sums[k][0], list(waits)), *sums[k][1:]]
+        sums[k], left = advanced(sums[k], bits[done[k]])
+        done[k] += 1
+        return left
+
+    def exponent(k):
+        return exponent_of(sum(sums[k]), members)
+
+    def arrival(k):
+        return sums[k][-1]
+
+    made = [parts_of_last]
+    step(1, made)
+    step(2, made)
+    step(3, made)
+    step(4)
+    left = step(4, [arrival(3)])
+    for k in range(2):
+        sums[k] = [gated(sums[k][0], [left]), *sums[k][1:]]
+    swapped = lax.ppermute(jnp.stack([exponent(0), exponent(1)]), "band", swap)
+    step(2, [left])
+    step(3, [left])
+    both = exponent(2)
     trades = []
     for m in range(members):
         for b in range(2):
             mate = (m, b) if m % 2 == b else (m ^ 1, 1 - b)
             trades.append((m * 2 + b, mate[0] * 2 + mate[1]))
-    both = lax.ppermute(pieces["both"][0], ("mem", "band"), trades)
-
-    early = gathered(jnp.concatenate([other, both[None]]))
+    both = lax.ppermute(both, ("mem", "band"), trades)
+    early = jnp.concatenate([swapped, both[None]])
+    orders = [arrival(4)]
+    step(4)
+    orders.append(arrival(4))
+    late = jnp.stack([exponent(3), exponent(4)])
+    for n, bit in enumerate(reversed(bits)):
+        early, _ = doubled(gated(early, [orders[n]]), bit)
+        late, beside = doubled(late, bit)
+        orders.append(beside)
     other, both = early[:-1], early[-1]
     middle = both.shape[0] // 2
     low, high = both[:middle], both[middle:]
@@ -541,8 +581,7 @@
     up = jnp.stack([jnp.concatenate([low, *other[::-1]]), jnp.concatenate([high, rest])])
     out = jnp.where(band == 0, down, up)
 
-    own = gathered(jnp.stack(pieces["own"]))
-    for k, block in enumerate(own):
+    for k, block in enumerate(late):
         width = block.shape[0]
         row = choose(band, (nlat // 2 - middle - (k + 1) * width, middle + k * width))
         out = lax.dynamic_update_slice(out, block[None], (band, row.astype(jnp.int32), jnp.int32(0)))

time: 192 us -> 213 us (1.11)
  other arithmetic: 7 us -> 26 us
  local copies, waits for them, and re-layouts: 4.75 us -> 8.33 us
  waiting for transfers between devices: 81 us -> 78.7 us
    ppermute x10, waiting for transfers between devices: 42.3 us -> 21.6 us  [halved(): lax.ppermute(leaves, 'mem', pairs(members, bit))]
    ppermute x4, waiting for transfers between devices: 4.94 us -> 16.6 us  [by_levels(): remotes += [lax.ppermute(piece, 'band', swap) for piece in outgoing]]
    add x10, other arithmetic: 3.55 us -> 10.5 us  [total(): sum((lax.dynamic_slice_in_dim(part, which * half, half, axis=1) for part...]
    select_n x8, other arithmetic: 0.48 us -> 7.11 us  [doubled(): return (jnp.where(mine == 0, low, high), beside)]
    ppermute x5, waiting for transfers between devices: 0.5 us -> 6.07 us  [across(): lax.ppermute(leaves, 'mem', pairs(members, bit))]
    div x5, other arithmetic: 0.12 us -> 3.87 us  [exponent_of(): mean = summed / members]
    unnamed x36 -> x60, local copies, waits for them, and re-layouts: 3.68 us -> 7.27 us
    ppermute x10, starting transfers between devices: 12.3 us -> 15.4 us  [halved(): lax.ppermute(leaves, 'mem', pairs(members, bit))]
  transfers between devices with their start and end apart: 40 -> 40, of which waited for: 18 -> 16; matrix products, arithmetic and copies ran while one was open for 4% -> 12% of each run, Pallas kernels for 31% -> 28%
where the time goes in v10:
time: 213 us; the launch traced here: 212 us
  waiting for transfers between devices  78.7 us (37%)
  Pallas kernels  61.6 us (29%)
  starting transfers between devices  36.7 us (17%)
  other arithmetic  26 us (12%)
  local copies, waits for them, and re-layouts  8.33 us (4%)
    pallas_call x5, Pallas kernels, window_tensor(): pl.pallas_call(functools.partial(window_kernel, window, depth, len(waits)...  51.3 us
    ppermute x8, waiting for transfers between devices, doubled(): beside = lax.ppermute(part, 'mem', pairs(members, bit))  30.2 us
    ppermute x10, waiting for transfers between devices, halved(): lax.ppermute(leaves, 'mem', pairs(members, bit))  21.6 us
    ppermute x4, waiting for transfers between devices, by_levels(): remotes += [lax.ppermute(piece, 'band', swap) for piece in outgoing]  16.6 us
    ppermute x10, starting transfers between devices, halved(): lax.ppermute(leaves, 'mem', pairs(members, bit))  15.4 us
    add x10, other arithmetic, total(): sum((lax.dynamic_slice_in_dim(part, which * half, half, axis=1) for part...  10.5 us
    pallas_call x3, Pallas kernels, pieces_of(): pl.pallas_call(functools.partial(pieces_kernel, windows, slots, count), i...  10.2 us
    unnamed x60, local copies, waits for them, and re-layouts  7.27 us
  transfers between devices with their start and end apart: 40, of which 16 were waited for; matrix products, arithmetic and copies ran while one was open for 12% of the time, Pallas kernels for 28%

profile of v10, /device:TPU:0, one launch (start us, length us, event | category | flops | bytes accessed | tf_op | source)
XLA Modules:
  0.0 212.0 jit_solution(7035551487784954799)
XLA Ops:
  0.0 2.6 %pieces_of.4 = f32[2,136,640]{2,1,0:T(8,128)} custom-call(s32[1]{0:T(128)} %bitcast.4.level_ref, f32[2,2,640,640]{3,2,1,0:T(8,128)} %bitcast.24), custom_call_target="tpu_custom_call" | custom-call | bytes 5242880 | tf_op jit(solution)/shard_map/pieces_of/pallas_call | solution.py:208
  2.6 3.0 %collective-permute-start = (f32[2,136,640]{2,1,0:T(8,128)}, f32[2,136,640]{2,1,0:T(8,128)S(1)}, u32[]{:S(2)}, u32[]{:S(2)}) collective-permute-start(f32[2,136,640]{2,1,0:T(8,128)} %pieces_of.4), channel_id=1, source_target_pairs={{0,1},{1,0},{2,3},{3,2},{4,5},{5,4},{6,7},{7,6},{8,9},{9,8},{10,11... | collective-permute-start | bytes 2088968 | tf_op jit(solution)/shard_map/ppermute | solution.py:489
  5.6 3.6 %pieces_of.5 = (f32[2,128,640]{2,1,0:T(8,128)}, f32[2,128,640]{2,1,0:T(8,128)}, f32[2,128,640]{2,1,0:T(8,128)}, f32[2,120,640]{2,1,0:T(8,128)}) custom-call(s32[1]{0:T(128)} %bitcast.4.level_ref, f32[2,2,640,640]{3,2,1,0:T(8,128)} %bitcast.25), custom_call_target="tpu_custom_call" | custom-call | bytes 10485760 | tf_op jit(solution)/shard_map/pieces_of/pallas_call | solution.py:208
  9.4 2.0 collective-permute-start.7
  11.5 1.9 collective-permute-start.6
  13.4 4.0 %pieces_of.3 = (f32[2,136,640]{2,1,0:T(8,128)}, f32[2,128,640]{2,1,0:T(8,128)}, f32[2,128,640]{2,1,0:T(8,128)}, f32[2,128,640]{2,1,0:T(8,128)}, f32[2,120,640]{2,1,0:T(8,128)}) custom-call(s32[1]{0:T(128)} %bitcast.level_ref, f32[2,2,640,640]{3,2,1,0:T(8,128)} %bitcast.26), custom_call_target="tpu_custom_call" | custom-call | bytes 13107200 | tf_op jit(solution)/shard_map/pieces_of/pallas_call | solution.py:208
  18.1 4.2 %collective-permute-done.refs_2_ = f32[2,136,640]{2,1,0:T(8,128)S(1)} collective-permute-done((f32[2,136,640]{2,1,0:T(8,128)}, f32[2,136,640]{2,1,0:T(8,128)S(1)}, u32[]{:S(2)}, u32[]{:S(2)}) %collective-permute-start) | collective-permute-done | bytes 696352 | tf_op jit(solution)/shard_map/ppermute | solution.py:489
  23.2 10.5 %window_tensor.5 = (f32[3,32,1280]{2,1,0:T(8,128)}, f32[3,32,1280]{2,1,0:T(8,128)}, f32[3,32,1280]{2,1,0:T(8,128)}, f32[3,32,1280]{2,1,0:T(8,128)}, f32[2,16,1280]{2,1,0:T(8,128)}) custom-call(s32[3]{0:T(128)} %pad_add_fusion.refs_0_, f32[2,136,640]{2,1,0:T(8,128)} %get-tuple-element.38.refs_1_, f32[2,136,640]{2,1,0:T(8,128)} %copy-done.27, ...), custom_call_target="tpu_custom_call" | custom-call | flops 10695475200 | bytes 6635520 | tf_op jit(solution)/shard_map/window_tensor/pallas_call | solution.py:396
  33.8 16.6 %collective-permute-done.7.refs_2_ = f32[2,128,640]{2,1,0:T(8,128)S(1)} collective-permute-done((f32[2,128,640]{2,1,0:T(8,128)}, f32[2,128,640]{2,1,0:T(8,128)S(1)}, u32[]{:S(2)}, u32[]{:S(2)}) %collective-permute-start.7) | collective-permute-done | bytes 655392 | tf_op jit(solution)/shard_map/ppermute | solution.py:491
  51.2 10.2 %window_tensor.6 = (f32[3,32,1280]{2,1,0:T(8,128)}, f32[3,32,1280]{2,1,0:T(8,128)}, f32[3,32,1280]{2,1,0:T(8,128)}, f32[3,32,1280]{2,1,0:T(8,128)}, f32[2,16,1280]{2,1,0:T(8,128)}) custom-call(s32[3]{0:T(128)} %pad_add_fusion.refs_0_, f32[2,128,640]{2,1,0:T(8,128)} %get-tuple-element.47.refs_1_, f32[2,128,640]{2,1,0:T(8,128)} %copy-done.29, ...), custom_call_target="tpu_custom_call" | custom-call | flops 10066329600 | bytes 6553600 | tf_op jit(solution)/shard_map/window_tensor/pallas_call | solution.py:396
  62.8 2.1 collective-permute-start.3
  64.9 10.4 %window_tensor.7 = (f32[3,32,1280]{2,1,0:T(8,128)}, f32[3,32,1280]{2,1,0:T(8,128)}, f32[3,32,1280]{2,1,0:T(8,128)}, f32[3,32,1280]{2,1,0:T(8,128)}, f32[2,16,1280]{2,1,0:T(8,128)}) custom-call(s32[3]{0:T(128)} %pad_add_fusion.refs_0_, f32[2,128,640]{2,1,0:T(8,128)} %get-tuple-element.52.refs_1_, f32[2,128,640]{2,1,0:T(8,128)} %copy-done.28, ...), custom_call_target="tpu_custom_call" | custom-call | flops 10066329600 | bytes 6553600 | tf_op jit(solution)/shard_map/window_tensor/pallas_call | solution.py:396
  76.6 1.7 collective-permute-start.13
  79.1 10.2 %window_tensor.8 = (f32[3,32,1280]{2,1,0:T(8,128)}, f32[3,32,1280]{2,1,0:T(8,128)}, f32[3,32,1280]{2,1,0:T(8,128)}, f32[3,32,1280]{2,1,0:T(8,128)}, f32[2,16,1280]{2,1,0:T(8,128)}) custom-call(s32[3]{0:T(128)} %pad_add_fusion.refs_0_, f32[2,128,640]{2,1,0:T(8,128)} %get-tuple-element.45.refs_1_, f32[2,128,640]{2,1,0:T(8,128)} %collective-permute-done.6.refs_2_, ...), custom_call_target="tpu_custom_call" | custom-call | flops 10066329600 | bytes 6553600 | tf_op jit(solution)/shard_map/window_tensor/pallas_call | solution.py:396
  89.4 1.6 collective-permute-start.4
  91.1 1.1 add.316.refs_5_
  93.7 4.2 %collective-permute-done.4 = f32[3,16,1280]{2,1,0:T(8,128)} collective-permute-done((f32[3,16,1280]{2,1,0:T(8,128)S(1)}, f32[3,16,1280]{2,1,0:T(8,128)}, u32[]{:S(2)}, u32[]{:S(2)}) %collective-permute-start.4) | collective-permute-done | bytes 245792 | tf_op jit(solution)/shard_map/ppermute | solution.py:504
  97.9 1.7 dynamic-slice_add_fusion.16
  100.5 10.1 %window_tensor.9 = (f32[3,32,1280]{2,1,0:T(8,128)}, f32[3,32,1280]{2,1,0:T(8,128)}, f32[3,32,1280]{2,1,0:T(8,128)}, f32[3,32,1280]{2,1,0:T(8,128)}) custom-call(s32[3]{0:T(128)} %pad_add_fusion.refs_0_, f32[2,120,640]{2,1,0:T(8,128)} %get-tuple-element.43.refs_1_, f32[2,120,640]{2,1,0:T(8,128)} %collective-permute-done.5.refs_2_, ...), custom_call_target="tpu_custom_call" | custom-call | flops 9437184000 | bytes 6471680 | tf_op jit(solution)/shard_map/window_tensor/pallas_call | solution.py:396
  110.5 5.5 %collective-permute-done.15.refs_2_ = f32[3,32,1280]{2,1,0:T(8,128)S(1)} collective-permute-done((f32[3,32,1280]{2,1,0:T(8,128)S(1)}, f32[3,32,1280]{2,1,0:T(8,128)S(1)}, u32[]{:S(2)}, u32[]{:S(2)}) %collective-permute-start.15) | collective-permute-done | bytes 491552 | tf_op jit(solution)/shard_map/ppermute | solution.py:509
  117.9 2.6 %collective-permute-start.21 = (f32[3,8,1280]{2,1,0:T(8,128)}, f32[3,8,1280]{2,1,0:T(8,128)}, u32[]{:S(2)}, u32[]{:S(2)}) collective-permute-start(f32[3,8,1280]{2,1,0:T(8,128)} %get-tuple-element.88.refs_7_), channel_id=1, source_target_pairs={{0,16},{2,18},{4,20},{6,22},{8,24},{10,26},{12,28},{14,30},{16,0},... | collective-permute-start | bytes 368648 | tf_op jit(solution)/shard_map/ppermute | solution.py:504
  122.4 1.6 collective-permute-start.16
  124.7 4.4 %collective-permute-done.22 = f32[3,16,1280]{2,1,0:T(8,128)} collective-permute-done((f32[3,16,1280]{2,1,0:T(8,128)}, f32[3,16,1280]{2,1,0:T(8,128)}, u32[]{:S(2)}, u32[]{:S(2)}) %collective-permute-start.22) | collective-permute-done | bytes 245792 | tf_op jit(solution)/shard_map/ppermute | solution.py:504
  129.1 1.8 dynamic-slice_add_fusion.13
  130.9 3.4 %collective-permute-done.16.refs_1_ = f32[3,16,1280]{2,1,0:T(8,128)S(1)} collective-permute-done((f32[3,16,1280]{2,1,0:T(8,128)S(1)}, f32[3,16,1280]{2,1,0:T(8,128)S(1)}, u32[]{:S(2)}, u32[]{:S(2)}) %collective-permute-start.16) | collective-permute-done | bytes 245792 | tf_op jit(solution)/shard_map/ppermute | solution.py:504
  134.3 2.6 %collective-permute-start.23 = (f32[3,8,1280]{2,1,0:T(8,128)S(1)}, f32[3,8,1280]{2,1,0:T(8,128)S(1)}, u32[]{:S(2)}, u32[]{:S(2)}) collective-permute-start(f32[3,8,1280]{2,1,0:T(8,128)S(1)} %get-tuple-element.89), channel_id=1, source_target_pairs={{0,16},{2,18},{4,20},{6,22},{8,24},{10,26},{12,28},{14,30},{16,0},... | collective-permute-start | bytes 368648 | tf_op jit(solution)/shard_map/ppermute | solution.py:504
  136.9 1.1 dynamic-slice_add_fusion.1
  138.7 3.4 %collective-permute-done.26 = f32[3,16,1280]{2,1,0:T(8,128)S(1)} collective-permute-done((f32[3,16,1280]{2,1,0:T(8,128)S(1)}, f32[3,16,1280]{2,1,0:T(8,128)S(1)}, u32[]{:S(2)}, u32[]{:S(2)}) %collective-permute-start.26) | collective-permute-done | bytes 245792 | tf_op jit(solution)/shard_map/ppermute | solution.py:504
  143.2 1.0 add_multiply_fusion.3
  144.2 1.0 add_multiply_fusion.4
  145.3 1.6 collective-permute-start.24
  147.8 2.9 %collective-permute-start.33 = (f32[3,8,1280]{2,1,0:T(8,128)S(1)}, f32[3,8,1280]{2,1,0:T(8,128)S(1)}, u32[]{:S(2)}, u32[]{:S(2)}) collective-permute-start(f32[3,8,1280]{2,1,0:T(8,128)S(1)} %dynamic-slice_add_fusion.10), channel_id=1, source_target_pairs={{0,16},{2,18},{4,20},{6,22},{8,24},{10,26},{12,28},{14,30},{16,0},... | collective-permute-start | bytes 368648 | tf_op jit(solution)/shard_map/ppermute | solution.py:504
  151.7 5.3 %collective-permute-done.33 = f32[3,8,1280]{2,1,0:T(8,128)S(1)} collective-permute-done((f32[3,8,1280]{2,1,0:T(8,128)S(1)}, f32[3,8,1280]{2,1,0:T(8,128)S(1)}, u32[]{:S(2)}, u32[]{:S(2)}) %collective-permute-start.33) | collective-permute-done | bytes 122912 | tf_op jit(solution)/shard_map/ppermute | solution.py:504
  160.3 3.0 %collective-permute-start.31 = (f32[3,8,1280]{2,1,0:T(8,128)S(1)}, f32[3,8,1280]{2,1,0:T(8,128)S(1)}, u32[]{:S(2)}, u32[]{:S(2)}) collective-permute-start(f32[3,8,1280]{2,1,0:T(8,128)S(1)} %dynamic-slice_add_fusion.11), channel_id=1, source_target_pairs={{0,16},{2,18},{4,20},{6,22},{8,24},{10,26},{12,28},{14,30},{16,0},... | collective-permute-start | bytes 368648 | tf_op jit(solution)/shard_map/ppermute | solution.py:504
  163.3 7.4 %collective-permute-done.30 = f32[3,8,1280]{2,1,0:T(8,128)S(1)} collective-permute-done((f32[3,8,1280]{2,1,0:T(8,128)}, f32[3,8,1280]{2,1,0:T(8,128)S(1)}, u32[]{:S(2)}, u32[]{:S(2)}) %collective-permute-start.30) | collective-permute-done | bytes 122912 | tf_op jit(solution)/shard_map/ppermute | solution.py:515
  170.7 1.7 maximum_select_fusion.7.refs_0_
  173.9 1.0 add_multiply_fusion
  174.9 2.2 %collective-permute-start.34 = (f32[2,8,1280]{2,1,0:T(8,128)S(1)}, f32[2,8,1280]{2,1,0:T(8,128)S(1)}, u32[]{:S(2)}, u32[]{:S(2)}) collective-permute-start(f32[2,8,1280]{2,1,0:T(8,128)S(1)} %pad_maximum_fusion.2), channel_id=1, source_target_pairs={{0,16},{2,18},{4,20},{6,22},{8,24},{10,26},{12,28},{14,30},{16,0},... | collective-permute-start | bytes 245768 | tf_op jit(solution)/shard_map/ppermute | solution.py:515
  177.1 6.6 %collective-permute-done.32 = f32[3,16,1280]{2,1,0:T(8,128)S(1)} collective-permute-done((f32[3,16,1280]{2,1,0:T(8,128)}, f32[3,16,1280]{2,1,0:T(8,128)S(1)}, u32[]{:S(2)}, u32[]{:S(2)}) %collective-permute-start.32) | collective-permute-done | bytes 245792 | tf_op jit(solution)/shard_map/ppermute | solution.py:515
  183.7 1.9 maximum_select_fusion.5.refs_0_
  186.8 1.0 maximum_select_fusion.8
  187.8 5.3 %collective-permute-done.36.refs_1_ = f32[2,16,1280]{2,1,0:T(8,128)S(1)} collective-permute-done((f32[2,16,1280]{2,1,0:T(8,128)S(1)}, f32[2,16,1280]{2,1,0:T(8,128)S(1)}, u32[]{:S(2)}, u32[]{:S(2)}) %collective-permute-start.36) | collective-permute-done | bytes 163872 | tf_op jit(solution)/shard_map/ppermute | solution.py:515
  193.2 1.6 collective-permute-start.38
  194.7 5.9 %collective-permute-done.35 = f32[3,32,1280]{2,1,0:T(8,128)S(1)} collective-permute-done((f32[3,32,1280]{2,1,0:T(8,128)}, f32[3,32,1280]{2,1,0:T(8,128)S(1)}, u32[]{:S(2)}, u32[]{:S(2)}) %collective-permute-start.35) | collective-permute-done | bytes 491552 | tf_op jit(solution)/shard_map/ppermute | solution.py:515
  200.6 2.2 %maximum_select_fusion.3.refs_0_ = f32[3,64,1280]{2,1,0:T(8,128)} fusion(f32[3,32,1280]{2,1,0:T(8,128)S(1)} %collective-permute-done.35, f32[3,32,1280]{2,1,0:T(8,128)} %gated.24, pred[]{:T(512)S(6)} %eq.44), kind=kLoop, calls=%fused_computation.7 | loop fusion | flops 737280 | bytes 1966081 | tf_op jit(solution)/shard_map/jit(_where)/select_n | solution.py:518
  202.8 3.0 %collective-permute-done.38 = f32[2,32,1280]{2,1,0:T(8,128)S(1)} collective-permute-done((f32[2,32,1280]{2,1,0:T(8,128)S(1)}, f32[2,32,1280]{2,1,0:T(8,128)S(1)}, u32[]{:S(2)}, u32[]{:S(2)}) %collective-permute-start.38) | collective-permute-done | bytes 327712 | tf_op jit(solution)/shard_map/ppermute | solution.py:515
  205.9 2.1 collective-permute-done.39
  209.4 1.7 copy-done.2
  (156 shorter events, 24.9 us)
Async XLA Ops:
  2.6 19.6 %collective-permute-start = (f32[2,136,640]{2,1,0:T(8,128)}, f32[2,136,640]{2,1,0:T(8,128)S(1)}, u32[]{:S(2)}, u32[]{:S(2)}) collective-permute-start(f32[2,136,640]{2,1,0:T(8,128)} %pieces_of.4), channel_id=1, source_target_pairs={{0,1},{1,0},{2,3},{3,2},{4,5},{5,4},{6,7},{7,6},{8,9},{9,8},{10,11... | collective-permute-start | bytes 2088968 | tf_op jit(solution)/shard_map/ppermute | solution.py:489
  9.3 53.5 %collective-permute-start.9 = (f32[2,128,640]{2,1,0:T(8,128)}, f32[2,128,640]{2,1,0:T(8,128)S(1)}, u32[]{:S(2)}, u32[]{:S(2)}) collective-permute-start(f32[2,128,640]{2,1,0:T(8,128)} %get-tuple-element.53), channel_id=1, source_target_pairs={{0,1},{1,0},{2,3},{3,2},{4,5},{5,4},{6,7},{7,6},{8,9},{9,8},{10,11... | collective-permute-start | bytes 1966088 | tf_op jit(solution)/shard_map/ppermute | solution.py:491
  9.4 41.0 %collective-permute-start.7 = (f32[2,128,640]{2,1,0:T(8,128)}, f32[2,128,640]{2,1,0:T(8,128)S(1)}, u32[]{:S(2)}, u32[]{:S(2)}) collective-permute-start(f32[2,128,640]{2,1,0:T(8,128)} %get-tuple-element.48), channel_id=1, source_target_pairs={{0,1},{1,0},{2,3},{3,2},{4,5},{5,4},{6,7},{7,6},{8,9},{9,8},{10,11... | collective-permute-start | bytes 1966088 | tf_op jit(solution)/shard_map/ppermute | solution.py:491
  11.4 88.7 %collective-permute-start.5 = (f32[2,120,640]{2,1,0:T(8,128)}, f32[2,120,640]{2,1,0:T(8,128)}, u32[]{:S(2)}, u32[]{:S(2)}) collective-permute-start(f32[2,120,640]{2,1,0:T(8,128)} %get-tuple-element.44), channel_id=1, source_target_pairs={{0,1},{1,0},{2,3},{3,2},{4,5},{5,4},{6,7},{7,6},{8,9},{9,8},{10,11... | collective-permute-start | bytes 1843208 | tf_op jit(solution)/shard_map/ppermute | solution.py:491
  11.5 67.7 %collective-permute-start.6 = (f32[2,128,640]{2,1,0:T(8,128)}, f32[2,128,640]{2,1,0:T(8,128)}, u32[]{:S(2)}, u32[]{:S(2)}) collective-permute-start(f32[2,128,640]{2,1,0:T(8,128)} %get-tuple-element.46), channel_id=1, source_target_pairs={{0,1},{1,0},{2,3},{3,2},{4,5},{5,4},{6,7},{7,6},{8,9},{9,8},{10,11... | collective-permute-start | bytes 1966088 | tf_op jit(solution)/shard_map/ppermute | solution.py:491
  33.7 27.8 %collective-permute-start.2 = (f32[3,32,1280]{2,1,0:T(8,128)}, f32[3,32,1280]{2,1,0:T(8,128)S(1)}, u32[]{:S(2)}, u32[]{:S(2)}) collective-permute-start(f32[3,32,1280]{2,1,0:T(8,128)} %get-tuple-element.42), channel_id=1, source_target_pairs={{0,2},{2,0},{4,6},{6,4},{8,10},{10,8},{12,14},{14,12},{16,18},{18,... | collective-permute-start | bytes 1474568 | tf_op jit(solution)/shard_map/ppermute | solution.py:530
  51.2 10.8 %copy-start.23 = (f32[3,32,1280]{2,1,0:T(8,128)S(1)}, f32[3,32,1280]{2,1,0:T(8,128)}, u32[]{:S(2)}) copy-start(f32[3,32,1280]{2,1,0:T(8,128)} %get-tuple-element.41) | copy-start | bytes 1474564
  61.4 13.9 %collective-permute-start.8 = (f32[3,32,1280]{2,1,0:T(8,128)}, f32[3,32,1280]{2,1,0:T(8,128)S(1)}, u32[]{:S(2)}, u32[]{:S(2)}) collective-permute-start(f32[3,32,1280]{2,1,0:T(8,128)} %get-tuple-element.51), channel_id=1, source_target_pairs={{0,2},{2,0},{4,6},{6,4},{8,10},{10,8},{12,14},{14,12},{16,18},{18,... | collective-permute-start | bytes 1474568 | tf_op jit(solution)/shard_map/ppermute | solution.py:530
  61.5 14.0 %collective-permute-start.1 = (f32[3,32,1280]{2,1,0:T(8,128)}, f32[3,32,1280]{2,1,0:T(8,128)S(1)}, u32[]{:S(2)}, u32[]{:S(2)}) collective-permute-start(f32[3,32,1280]{2,1,0:T(8,128)} %get-tuple-element.40), channel_id=1, source_target_pairs={{0,2},{2,0},{4,6},{6,4},{8,10},{10,8},{12,14},{14,12},{16,18},{18,... | collective-permute-start | bytes 1474568 | tf_op jit(solution)/shard_map/ppermute | solution.py:531
  62.8 13.8 %collective-permute-start.3 = (f32[3,32,1280]{2,1,0:T(8,128)}, f32[3,32,1280]{2,1,0:T(8,128)S(1)}, u32[]{:S(2)}, u32[]{:S(2)}) collective-permute-start(f32[3,32,1280]{2,1,0:T(8,128)} %add.307.refs_4_), channel_id=1, source_target_pairs={{0,4},{2,6},{4,0},{6,2},{8,12},{10,14},{12,8},{14,10},{16,20},{18,... | collective-permute-start | bytes 1474568 | tf_op jit(solution)/shard_map/ppermute | solution.py:509
  64.9 10.5 %copy-start.22 = (f32[3,32,1280]{2,1,0:T(8,128)S(1)}, f32[3,32,1280]{2,1,0:T(8,128)}, u32[]{:S(2)}) copy-start(f32[3,32,1280]{2,1,0:T(8,128)} %get-tuple-element.50) | copy-start | bytes 1474564
  75.4 16.8 %collective-permute-start.12 = (f32[3,32,1280]{2,1,0:T(8,128)}, f32[3,32,1280]{2,1,0:T(8,128)S(1)}, u32[]{:S(2)}, u32[]{:S(2)}) collective-permute-start(f32[3,32,1280]{2,1,0:T(8,128)} %get-tuple-element.61), channel_id=1, source_target_pairs={{0,2},{2,0},{4,6},{6,4},{8,10},{10,8},{12,14},{14,12},{16,18},{18,... | collective-permute-start | bytes 1474568 | tf_op jit(solution)/shard_map/ppermute | solution.py:531
  75.5 13.9 %collective-permute-start.11 = (f32[3,32,1280]{2,1,0:T(8,128)}, f32[3,32,1280]{2,1,0:T(8,128)}, u32[]{:S(2)}, u32[]{:S(2)}) collective-permute-start(f32[3,32,1280]{2,1,0:T(8,128)} %get-tuple-element.59), channel_id=1, source_target_pairs={{0,2},{2,0},{4,6},{6,4},{8,10},{10,8},{12,14},{14,12},{16,18},{18,... | collective-permute-start | bytes 1474568 | tf_op jit(solution)/shard_map/ppermute | solution.py:530
  76.6 16.2 %collective-permute-start.13 = (f32[3,32,1280]{2,1,0:T(8,128)S(1)}, f32[3,32,1280]{2,1,0:T(8,128)S(1)}, u32[]{:S(2)}, u32[]{:S(2)}) collective-permute-start(f32[3,32,1280]{2,1,0:T(8,128)S(1)} %add.314.refs_4_), channel_id=1, source_target_pairs={{0,4},{2,6},{4,0},{6,2},{8,12},{10,14},{12,8},{14,10},{16,20},{18,... | collective-permute-start | bytes 1474568 | tf_op jit(solution)/shard_map/ppermute | solution.py:509
  79.1 10.3 %copy-start.26 = (f32[3,16,1280]{2,1,0:T(8,128)S(1)}, f32[3,16,1280]{2,1,0:T(8,128)}, u32[]{:S(2)}) copy-start(f32[3,16,1280]{2,1,0:T(8,128)} %get-tuple-element.84.refs_5_) | copy-start | bytes 737284
  79.1 12.0 %copy-start.16 = (f32[3,32,1280]{2,1,0:T(8,128)S(1)}, f32[3,32,1280]{2,1,0:T(8,128)}, u32[]{:S(2)}) copy-start(f32[3,32,1280]{2,1,0:T(8,128)} %get-tuple-element.58) | copy-start | bytes 1474564
  89.3 10.3 %collective-permute-start.10 = (f32[3,32,1280]{2,1,0:T(8,128)}, f32[3,32,1280]{2,1,0:T(8,128)S(1)}, u32[]{:S(2)}, u32[]{:S(2)}) collective-permute-start(f32[3,32,1280]{2,1,0:T(8,128)} %get-tuple-element.57), channel_id=1, source_target_pairs={{0,2},{2,0},{4,6},{6,4},{8,10},{10,8},{12,14},{14,12},{16,18},{18,... | collective-permute-start | bytes 1474568 | tf_op jit(solution)/shard_map/ppermute | solution.py:530
  89.4 8.5 %collective-permute-start.4 = (f32[3,16,1280]{2,1,0:T(8,128)S(1)}, f32[3,16,1280]{2,1,0:T(8,128)}, u32[]{:S(2)}, u32[]{:S(2)}) collective-permute-start(f32[3,16,1280]{2,1,0:T(8,128)S(1)} %copy-done.26), channel_id=1, source_target_pairs={{0,8},{2,10},{4,12},{6,14},{8,0},{10,2},{12,4},{14,6},{16,24},{18,... | collective-permute-start | bytes 737288 | tf_op jit(solution)/shard_map/ppermute | solution.py:504
  92.2 7.5 %copy-start.20 = (f32[3,32,1280]{2,1,0:T(8,128)}, f32[3,32,1280]{2,1,0:T(8,128)S(1)}, u32[]{:S(2)}) copy-start(f32[3,32,1280]{2,1,0:T(8,128)S(1)} %add.316.refs_5_) | copy-start | bytes 1474564
  92.2 18.3 %collective-permute-start.18 = (f32[3,32,1280]{2,1,0:T(8,128)S(1)}, f32[3,32,1280]{2,1,0:T(8,128)S(1)}, u32[]{:S(2)}, u32[]{:S(2)}) collective-permute-start(f32[3,32,1280]{2,1,0:T(8,128)S(1)} %add.316.refs_5_), channel_id=1, source_target_pairs={{0,4},{2,6},{4,0},{6,2},{8,12},{10,14},{12,8},{14,10},{16,20},{18,... | collective-permute-start | bytes 1474568 | tf_op jit(solution)/shard_map/ppermute | solution.py:509
  99.7 16.4 %collective-permute-start.15 = (f32[3,32,1280]{2,1,0:T(8,128)S(1)}, f32[3,32,1280]{2,1,0:T(8,128)S(1)}, u32[]{:S(2)}, u32[]{:S(2)}) collective-permute-start(f32[3,32,1280]{2,1,0:T(8,128)S(1)} %add.315.refs_4_), channel_id=1, source_target_pairs={{0,4},{2,6},{4,0},{6,2},{8,12},{10,14},{12,8},{14,10},{16,20},{18,... | collective-permute-start | bytes 1474568 | tf_op jit(solution)/shard_map/ppermute | solution.py:509
  116.9 3.6 %collective-permute-start.19 = (f32[3,32,1280]{2,1,0:T(8,128)}, f32[3,32,1280]{2,1,0:T(8,128)S(1)}, u32[]{:S(2)}, u32[]{:S(2)}) collective-permute-start(f32[3,32,1280]{2,1,0:T(8,128)} %gated.15), channel_id=1, source_target_pairs={{0,2},{2,0},{4,6},{6,4},{8,10},{10,8},{12,14},{14,12},{16,18},{18,... | collective-permute-start | bytes 1474568 | tf_op jit(solution)/shard_map/ppermute | solution.py:530
  116.9 3.7 %collective-permute-start.14 = (f32[3,32,1280]{2,1,0:T(8,128)}, f32[3,32,1280]{2,1,0:T(8,128)S(1)}, u32[]{:S(2)}, u32[]{:S(2)}) collective-permute-start(f32[3,32,1280]{2,1,0:T(8,128)} %get-tuple-element.65), channel_id=1, source_target_pairs={{0,2},{2,0},{4,6},{6,4},{8,10},{10,8},{12,14},{14,12},{16,18},{18,... | collective-permute-start | bytes 1474568 | tf_op jit(solution)/shard_map/ppermute | solution.py:531
  117.4 5.0 %collective-permute-start.25 = (f32[3,32,1280]{2,1,0:T(8,128)}, f32[3,32,1280]{2,1,0:T(8,128)S(1)}, u32[]{:S(2)}, u32[]{:S(2)}) collective-permute-start(f32[3,32,1280]{2,1,0:T(8,128)} %get-tuple-element.70), channel_id=1, source_target_pairs={{0,2},{2,0},{4,6},{6,4},{8,10},{10,8},{12,14},{14,12},{16,18},{18,... | collective-permute-start | bytes 1474568 | tf_op jit(solution)/shard_map/ppermute | solution.py:531
  117.4 11.7 %collective-permute-start.22 = (f32[3,16,1280]{2,1,0:T(8,128)}, f32[3,16,1280]{2,1,0:T(8,128)}, u32[]{:S(2)}, u32[]{:S(2)}) collective-permute-start(f32[3,16,1280]{2,1,0:T(8,128)} %get-tuple-element.80.refs_6_), channel_id=1, source_target_pairs={{0,8},{2,10},{4,12},{6,14},{8,0},{10,2},{12,4},{14,6},{16,24},{18,... | collective-permute-start | bytes 737288 | tf_op jit(solution)/shard_map/ppermute | solution.py:504
  117.9 26.4 %collective-permute-start.21 = (f32[3,8,1280]{2,1,0:T(8,128)}, f32[3,8,1280]{2,1,0:T(8,128)}, u32[]{:S(2)}, u32[]{:S(2)}) collective-permute-start(f32[3,8,1280]{2,1,0:T(8,128)} %get-tuple-element.88.refs_7_), channel_id=1, source_target_pairs={{0,16},{2,18},{4,20},{6,22},{8,24},{10,26},{12,28},{14,30},{16,0},... | collective-permute-start | bytes 368648 | tf_op jit(solution)/shard_map/ppermute | solution.py:504
  120.5 16.4 %collective-permute-start.17 = (f32[3,32,1280]{2,1,0:T(8,128)}, f32[3,32,1280]{2,1,0:T(8,128)S(1)}, u32[]{:S(2)}, u32[]{:S(2)}) collective-permute-start(f32[3,32,1280]{2,1,0:T(8,128)} %get-tuple-element.66), channel_id=1, source_target_pairs={{0,2},{2,0},{4,6},{6,4},{8,10},{10,8},{12,14},{14,12},{16,18},{18,... | collective-permute-start | bytes 1474568 | tf_op jit(solution)/shard_map/ppermute | solution.py:531
  120.6 16.2 %collective-permute-start.20 = (f32[3,32,1280]{2,1,0:T(8,128)S(1)}, f32[3,32,1280]{2,1,0:T(8,128)S(1)}, u32[]{:S(2)}, u32[]{:S(2)}) collective-permute-start(f32[3,32,1280]{2,1,0:T(8,128)S(1)} %add.324), channel_id=1, source_target_pairs={{0,4},{2,6},{4,0},{6,2},{8,12},{10,14},{12,8},{14,10},{16,20},{18,... | collective-permute-start | bytes 1474568 | tf_op jit(solution)/shard_map/ppermute | solution.py:509
  122.4 11.9 %collective-permute-start.16 = (f32[3,16,1280]{2,1,0:T(8,128)S(1)}, f32[3,16,1280]{2,1,0:T(8,128)S(1)}, u32[]{:S(2)}, u32[]{:S(2)}) collective-permute-start(f32[3,16,1280]{2,1,0:T(8,128)S(1)} %get-tuple-element.76), channel_id=1, source_target_pairs={{0,8},{2,10},{4,12},{6,14},{8,0},{10,2},{12,4},{14,6},{16,24},{18,... | collective-permute-start | bytes 737288 | tf_op jit(solution)/shard_map/ppermute | solution.py:504
  129.1 13.1 %collective-permute-start.26 = (f32[3,16,1280]{2,1,0:T(8,128)S(1)}, f32[3,16,1280]{2,1,0:T(8,128)S(1)}, u32[]{:S(2)}, u32[]{:S(2)}) collective-permute-start(f32[3,16,1280]{2,1,0:T(8,128)S(1)} %get-tuple-element.82), channel_id=1, source_target_pairs={{0,8},{2,10},{4,12},{6,14},{8,0},{10,2},{12,4},{14,6},{16,24},{18,... | collective-permute-start | bytes 737288 | tf_op jit(solution)/shard_map/ppermute | solution.py:504
  134.3 8.9 %collective-permute-start.23 = (f32[3,8,1280]{2,1,0:T(8,128)S(1)}, f32[3,8,1280]{2,1,0:T(8,128)S(1)}, u32[]{:S(2)}, u32[]{:S(2)}) collective-permute-start(f32[3,8,1280]{2,1,0:T(8,128)S(1)} %get-tuple-element.89), channel_id=1, source_target_pairs={{0,16},{2,18},{4,20},{6,22},{8,24},{10,26},{12,28},{14,30},{16,0},... | collective-permute-start | bytes 368648 | tf_op jit(solution)/shard_map/ppermute | solution.py:504
  138.0 20.6 %collective-permute-start.29 = (f32[3,16,1280]{2,1,0:T(8,128)S(1)}, f32[3,16,1280]{2,1,0:T(8,128)S(1)}, u32[]{:S(2)}, u32[]{:S(2)}) collective-permute-start(f32[3,16,1280]{2,1,0:T(8,128)S(1)} %get-tuple-element.78.refs_1_), channel_id=1, source_target_pairs={{0,8},{2,10},{4,12},{6,14},{8,0},{10,2},{12,4},{14,6},{16,24},{18,... | collective-permute-start | bytes 737288 | tf_op jit(solution)/shard_map/ppermute | solution.py:504
  138.7 8.1 %copy-start.11 = (f32[3,16,1280]{2,1,0:T(8,128)S(1)}, f32[3,16,1280]{2,1,0:T(8,128)}, u32[]{:S(2)}) copy-start(f32[3,16,1280]{2,1,0:T(8,128)} %copy-done.10) | copy-start | bytes 737284
  143.1 7.6 %collective-permute-start.27 = (f32[3,8,1280]{2,1,0:T(8,128)S(1)}, f32[3,8,1280]{2,1,0:T(8,128)S(1)}, u32[]{:S(2)}, u32[]{:S(2)}) collective-permute-start(f32[3,8,1280]{2,1,0:T(8,128)S(1)} %dynamic-slice_add_fusion.12), channel_id=1, source_target_pairs={{0,16},{2,18},{4,20},{6,22},{8,24},{10,26},{12,28},{14,30},{16,0},... | collective-permute-start | bytes 368648 | tf_op jit(solution)/shard_map/ppermute | solution.py:504
  143.2 7.5 %copy-start.3 = (f32[3,16,1280]{2,1,0:T(8,128)S(1)}, f32[3,16,1280]{2,1,0:T(8,128)}, u32[]{:S(2)}) copy-start(f32[3,16,1280]{2,1,0:T(8,128)} %gated.20) | copy-start | bytes 737284
  145.3 12.7 %collective-permute-start.24 = (f32[2,8,1280]{2,1,0:T(8,128)S(1)}, f32[2,8,1280]{2,1,0:T(8,128)S(1)}, u32[]{:S(2)}, u32[]{:S(2)}) collective-permute-start(f32[2,8,1280]{2,1,0:T(8,128)S(1)} %pad_maximum_fusion.1), channel_id=1, source_target_pairs={{0,1},{1,0},{2,3},{3,2},{4,5},{5,4},{6,7},{7,6},{8,9},{9,8},{10,11... | collective-permute-start | bytes 245768 | tf_op jit(solution)/shard_map/ppermute | solution.py:557
  147.8 9.2 %collective-permute-start.33 = (f32[3,8,1280]{2,1,0:T(8,128)S(1)}, f32[3,8,1280]{2,1,0:T(8,128)S(1)}, u32[]{:S(2)}, u32[]{:S(2)}) collective-permute-start(f32[3,8,1280]{2,1,0:T(8,128)S(1)} %dynamic-slice_add_fusion.10), channel_id=1, source_target_pairs={{0,16},{2,18},{4,20},{6,22},{8,24},{10,26},{12,28},{14,30},{16,0},... | collective-permute-start | bytes 368648 | tf_op jit(solution)/shard_map/ppermute | solution.py:504
  150.8 7.2 %collective-permute-start.28 = (f32[8,1280]{1,0:T(8,128)S(1)}, f32[8,1280]{1,0:T(8,128)S(1)}, u32[]{:S(2)}, u32[]{:S(2)}) collective-permute-start(f32[8,1280]{1,0:T(8,128)S(1)} %fusion.18), channel_id=1, source_target_pairs={{0,0},{1,2},{2,1},{3,3},{4,4},{5,6},{6,5},{7,7},{8,8},{9,10},{10,9... | collective-permute-start | bytes 122888 | tf_op jit(solution)/shard_map/ppermute | solution.py:566
  159.3 11.3 %collective-permute-start.30 = (f32[3,8,1280]{2,1,0:T(8,128)}, f32[3,8,1280]{2,1,0:T(8,128)S(1)}, u32[]{:S(2)}, u32[]{:S(2)}) collective-permute-start(f32[3,8,1280]{2,1,0:T(8,128)} %gated.21), channel_id=1, source_target_pairs={{0,16},{2,18},{4,20},{6,22},{8,24},{10,26},{12,28},{14,30},{16,0},... | collective-permute-start | bytes 368648 | tf_op jit(solution)/shard_map/ppermute | solution.py:515
  160.3 12.9 %collective-permute-start.31 = (f32[3,8,1280]{2,1,0:T(8,128)S(1)}, f32[3,8,1280]{2,1,0:T(8,128)S(1)}, u32[]{:S(2)}, u32[]{:S(2)}) collective-permute-start(f32[3,8,1280]{2,1,0:T(8,128)S(1)} %dynamic-slice_add_fusion.11), channel_id=1, source_target_pairs={{0,16},{2,18},{4,20},{6,22},{8,24},{10,26},{12,28},{14,30},{16,0},... | collective-permute-start | bytes 368648 | tf_op jit(solution)/shard_map/ppermute | solution.py:504
  173.9 9.8 %collective-permute-start.32 = (f32[3,16,1280]{2,1,0:T(8,128)}, f32[3,16,1280]{2,1,0:T(8,128)S(1)}, u32[]{:S(2)}, u32[]{:S(2)}) collective-permute-start(f32[3,16,1280]{2,1,0:T(8,128)} %gated.22), channel_id=1, source_target_pairs={{0,8},{2,10},{4,12},{6,14},{8,0},{10,2},{12,4},{14,6},{16,24},{18,... | collective-permute-start | bytes 737288 | tf_op jit(solution)/shard_map/ppermute | solution.py:515
  174.9 10.7 %collective-permute-start.34 = (f32[2,8,1280]{2,1,0:T(8,128)S(1)}, f32[2,8,1280]{2,1,0:T(8,128)S(1)}, u32[]{:S(2)}, u32[]{:S(2)}) collective-permute-start(f32[2,8,1280]{2,1,0:T(8,128)S(1)} %pad_maximum_fusion.2), channel_id=1, source_target_pairs={{0,16},{2,18},{4,20},{6,22},{8,24},{10,26},{12,28},{14,30},{16,0},... | collective-permute-start | bytes 245768 | tf_op jit(solution)/shard_map/ppermute | solution.py:515
  186.2 14.4 %collective-permute-start.35 = (f32[3,32,1280]{2,1,0:T(8,128)}, f32[3,32,1280]{2,1,0:T(8,128)S(1)}, u32[]{:S(2)}, u32[]{:S(2)}) collective-permute-start(f32[3,32,1280]{2,1,0:T(8,128)} %gated.24), channel_id=1, source_target_pairs={{0,4},{2,6},{4,0},{6,2},{8,12},{10,14},{12,8},{14,10},{16,20},{18,... | collective-permute-start | bytes 1474568 | tf_op jit(solution)/shard_map/ppermute | solution.py:515
  187.7 5.4 %collective-permute-start.36 = (f32[2,16,1280]{2,1,0:T(8,128)S(1)}, f32[2,16,1280]{2,1,0:T(8,128)S(1)}, u32[]{:S(2)}, u32[]{:S(2)}) collective-permute-start(f32[2,16,1280]{2,1,0:T(8,128)S(1)} %maximum_select_fusion.8), channel_id=1, source_target_pairs={{0,8},{2,10},{4,12},{6,14},{8,0},{10,2},{12,4},{14,6},{16,24},{18,... | collective-permute-start | bytes 491528 | tf_op jit(solution)/shard_map/ppermute | solution.py:515
  193.1 9.7 %copy-start.13 = (f32[2,16,1280]{2,1,0:T(8,128)}, f32[2,16,1280]{2,1,0:T(8,128)S(1)}, u32[]{:S(2)}) copy-start(f32[2,16,1280]{2,1,0:T(8,128)S(1)} %collective-permute-done.36.refs_1_) | copy-start | bytes 491524
  193.2 12.6 %collective-permute-start.38 = (f32[2,32,1280]{2,1,0:T(8,128)S(1)}, f32[2,32,1280]{2,1,0:T(8,128)S(1)}, u32[]{:S(2)}, u32[]{:S(2)}) collective-permute-start(f32[2,32,1280]{2,1,0:T(8,128)S(1)} %maximum_select_fusion.6), channel_id=1, source_target_pairs={{0,4},{2,6},{4,0},{6,2},{8,12},{10,14},{12,8},{14,10},{16,20},{18,... | collective-permute-start | bytes 983048 | tf_op jit(solution)/shard_map/ppermute | solution.py:515
  202.8 5.3 %collective-permute-start.37 = (f32[3,64,1280]{2,1,0:T(8,128)}, f32[3,64,1280]{2,1,0:T(8,128)S(1)}, u32[]{:S(2)}, u32[]{:S(2)}) collective-permute-start(f32[3,64,1280]{2,1,0:T(8,128)} %gated.25), channel_id=1, source_target_pairs={{0,2},{2,0},{4,6},{6,4},{8,10},{10,8},{12,14},{14,12},{16,18},{18,... | collective-permute-start | bytes 2949128 | tf_op jit(solution)/shard_map/ppermute | solution.py:515
  205.8 2.2 %collective-permute-start.39 = (f32[2,64,1280]{2,1,0:T(8,128)S(1)}, f32[2,64,1280]{2,1,0:T(8,128)S(1)}, u32[]{:S(2)}, u32[]{:S(2)}) collective-permute-start(f32[2,64,1280]{2,1,0:T(8,128)S(1)} %maximum_select_fusion.4), channel_id=1, source_target_pairs={{0,2},{2,0},{4,6},{6,4},{8,10},{10,8},{12,14},{14,12},{16,18},{18,... | collective-permute-start | bytes 1966088 | tf_op jit(solution)/shard_map/ppermute | solution.py:515
  (22 other events, 50.4 us)

commit v11 on v9

--- a/solution.py
+++ b/solution.py
@@ -16,6 +16,7 @@
 LANE = 128
 VMEM_LIMIT = 60 * 1024 * 1024
 KERNEL_WORK = 8
+ORDER = ((2, 4, 8), (4, 8, 2))
 AHEAD = ((), (), (0,), (1, 0), (2, 1, 0))
 
 
@@ -224,6 +225,22 @@
     )(level.reshape(1), spec)
 
 
+def gate_kernel(*refs):
+    pass
+
+
+def gated(part, waits):
+    return pl.pallas_call(
+        gate_kernel,
+        in_specs=[pl.BlockSpec(memory_space=pl.ANY)] * (1 + len(waits)),
+        out_specs=pl.BlockSpec(memory_space=pl.ANY),
+        out_shape=jax.ShapeDtypeStruct(part.shape, part.dtype),
+        input_output_aliases={0: 0},
+        cost_estimate=pl.CostEstimate(flops=0, transcendentals=0, bytes_accessed=1024),
+        name="gated",
+    )(part, *waits)
+
+
 def east_of(x):
     return pltpu.roll(x, NLON - 1, axis=1) - pltpu.roll(x, 1, axis=1)
 
@@ -243,7 +260,7 @@
     out_refs = [refs.pop(0) for _ in range(4)]
     carried_ref = None if window.last else refs.pop(0)
     table, lhs_high, lhs_low, wind, second, third, shift, results, carried, table_sem, out_sems = refs
-    band, core, side = place_ref[0], place_ref[1], place_ref[2]
+    band, core, sides = place_ref[0], place_ref[1], (place_ref[2], place_ref[3])
     rows, extended = window.rows, window.extended
 
     def at(pair):
@@ -346,6 +363,7 @@
 
     copies = []
     for n, (a, b) in reversed(list(enumerate(QUARTERS))):
+        side = sides[a]
         entries(results.at[n], (2 * (core + a - 2 * core * a) + (side + b - 2 * side * b)) * quarter)
         copies.append(pltpu.make_async_copy(results.at[n], out_refs[n], out_sems.at[n]))
         copies[-1].start()
@@ -406,14 +424,6 @@
     return out[:4], (None if window.last else out[4])
 
 
-def pairs(members, bit):
-    return [(member, member ^ bit) for member in range(members)]
-
-
-def pairs(members, bit):
-    return [(member, member ^ bit) for member in range(members)]
-
-
 def put_kernel(count, place_ref, *refs):
     parts, out_ref, sem = refs[:4], refs[-2], refs[-1]
     core, side, along = place_ref[0], place_ref[1], place_ref[2]
@@ -451,18 +461,16 @@
     )(places.astype(jnp.int32), *parts, *extra)
 
 
-def pairs(members, bit):
-    return [(member, member ^ bit) for member in range(members)]
-
-
 def by_levels(coeffs):
     spec = coeffs[0]
     levels, _, parts, waves_local, nlat = spec.shape
     members = lax.axis_size("mem")
     band = lax.axis_index("band").astype(jnp.int32)
     member = lax.axis_index("mem").astype(jnp.int32)
-    core, side = member % 2, member // 2 % 2
-    place = jnp.stack([band, core, side])
+    core = member % 2
+    half_of = [choose(core, [member // bits[step] % 2 for bits in ORDER]) for step in range(len(ORDER[0]))]
+    half_beside = choose(1 - core, [member // bits[0] % 2 for bits in ORDER])
+    place = jnp.stack([band, core, half_of[0], half_beside])
     spec = spec.reshape(levels, 2, parts * waves_local, nlat)
     count = nlat // LANE
     windows = [Window(k, count) for k in range(count)]
@@ -471,38 +479,41 @@
 
     (piece,) = pieces_of(spec, 1 - band, windows[:1], count)
     remotes = [lax.ppermute(piece, "band", swap)]
-    outgoing = pieces_of(spec, 1 - band, windows[1:], count)
-    remotes += [lax.ppermute(piece, "band", swap) for piece in outgoing]
+    for k, piece in enumerate(pieces_of(spec, 1 - band, windows[1:], count), 1):
+        if k > 1:
+            piece = gated(piece, [remotes[k - 2]])
+        remotes.append(lax.ppermute(piece, "band", swap))
     local = pieces_of(spec, band, windows, count)
 
-    bits = [1 << n for n in range(members.bit_length() - 1)]
-
-    def halved(parts_of, bit):
+    cores = [(m, m ^ 1) for m in range(members)]
+    ways = [[(m, m ^ ORDER[m % 2][step]) for m in range(members)] for step in range(len(ORDER[0]))]
+
+    def halved(parts_of, step):
         half = parts_of[0].shape[1] // 2
-        mine = (member // bit) % 2
+        mine = half_of[step]
 
         def total(which):
             return sum(lax.dynamic_slice_in_dim(part, which * half, half, axis=1) for part in parts_of)
 
         leaves = total(1 - mine)
-        return [total(mine), lax.ppermute(leaves, "mem", pairs(members, bit))], leaves
-
-    def across(parts_of, bit):
+        return [total(mine), lax.ppermute(leaves, "mem", ways[step])], leaves
+
+    def across(parts_of, step):
         kept, passed, kept_more, passed_more = parts_of
         leaves = passed + passed_more
-        return [kept, kept_more, lax.ppermute(leaves, "mem", pairs(members, bit))], leaves
-
-    def advanced(parts_of, bit):
-        return (across if len(parts_of) == 4 else halved)(parts_of, bit)
-
-    def doubled(part, bit):
-        beside = lax.ppermute(part, "mem", pairs(members, bit))
-        mine = (member // bit) % 2
+        return [kept, kept_more, lax.ppermute(leaves, "mem", ways[step])], leaves
+
+    def advanced(parts_of, step):
+        return (across if step == 0 else halved)(parts_of, step)
+
+    def doubled(part, step):
+        beside = lax.ppermute(part, "mem", cores if step < 0 else ways[step])
+        mine = core if step < 0 else half_of[step]
         return jnp.where(mine == 0, jnp.concatenate([part, beside], axis=1), jnp.concatenate([beside, part], axis=1))
 
     def gathered(part):
-        for bit in reversed(bits):
-            part = doubled(part, bit)
+        for step in range(len(ways) - 1, -2, -1):
+            part = doubled(part, step)
         return part
 
     carry = None
@@ -510,26 +521,31 @@
     for k, window in enumerate(windows):
         waits = []
         for j in AHEAD[k]:
-            sums[j], left = advanced(sums[j], bits[done[j]])
+            sums[j], left = advanced(sums[j], done[j])
             done[j] += 1
             waits.append(left)
         quarters, carry = window_tensor(window, place, local[k], remotes[k], table, waits, carry)
-        first = lax.ppermute(quarters[3], "mem", pairs(members, bits[0]))
-        second = lax.ppermute(quarters[2], "mem", pairs(members, bits[0]))
+        first = lax.ppermute(quarters[3], "mem", cores)
+        second = lax.ppermute(quarters[2], "mem", cores)
         sums.append([quarters[0], quarters[1], second, first])
-        done.append(1)
+        done.append(0)
     pieces = {"own": [], "both": [], "other": []}
     for k, window in enumerate(windows):
-        for bit in bits[done[k] :]:
-            sums[k], _ = advanced(sums[k], bit)
+        for step in range(done[k], len(ways)):
+            sums[k], _ = advanced(sums[k], step)
         pieces[window.side].append(exponent_of(sum(sums[k]), members))
 
     other = lax.ppermute(jnp.stack(pieces["other"]), "band", swap)
-    trades = []
+    place_of = {}
     for m in range(members):
         for b in range(2):
-            mate = (m, b) if m % 2 == b else (m ^ 1, 1 - b)
-            trades.append((m * 2 + b, mate[0] * 2 + mate[1]))
+            bits = ORDER[m % 2]
+            piece = functools.reduce(lambda value, bit: 2 * value + m // bit % 2, bits, m % 2)
+            place_of[piece, b] = m * 2 + b
+    trades, half = [], members // 2
+    for (piece, b), index in place_of.items():
+        mate = (piece, b) if (piece < half) == (b == 0) else ((piece + half) % members, 1 - b)
+        trades.append((index, place_of[mate]))
     both = lax.ppermute(pieces["both"][0], ("mem", "band"), trades)
 
     early = gathered(jnp.concatenate([other, both[None]]))

time: 192 us -> 184 us (0.958)
  waiting for transfers between devices: 81 us -> 72.4 us
    ppermute x37, waiting for transfers between devices: 76.7 us -> 64.1 us  [the longest x10 39.4 us: halved(): return ([total(mine), lax.ppermute(leaves, 'mem', ways[step])], leaves)]
    ppermute x1, waiting for transfers between devices: 4.26 us -> 8.2 us  [by_levels(): remotes = [lax.ppermute(piece, 'band', swap)]]
  transfers between devices with their start and end apart: 40 -> 40, of which waited for: 18 -> 13; matrix products, arithmetic and copies ran while one was open for 4% -> 4% of each run, Pallas kernels for 31% -> 32%
where the time goes in v11:
time: 184 us
  waiting for transfers between devices  72.4 us (39%)
  Pallas kernels  61.5 us (33%)
  starting transfers between devices  36.2 us (20%)
  other arithmetic  8.53 us (5%)
  local copies, waits for them, and re-layouts  4.56 us (2%)
    pallas_call x5, Pallas kernels, window_tensor(): pl.pallas_call(functools.partial(window_kernel, window, depth, len(waits)...  51.3 us
    ppermute x10, waiting for transfers between devices, halved(): return ([total(mine), lax.ppermute(leaves, 'mem', ways[step])], leaves)  39.4 us
    ppermute x8, waiting for transfers between devices, doubled(): beside = lax.ppermute(part, 'mem', cores if step < 0 else ways[step])  24.3 us
    ppermute x10, starting transfers between devices, halved(): return ([total(mine), lax.ppermute(leaves, 'mem', ways[step])], leaves)  10.8 us
    pallas_call x3, Pallas kernels, pieces_of(): pl.pallas_call(functools.partial(pieces_kernel, windows, slots, count), i...  10.2 us
    ppermute x1, waiting for transfers between devices, by_levels(): remotes = [lax.ppermute(piece, 'band', swap)]  8.2 us
    ppermute x5, starting transfers between devices, across(): return ([kept, kept_more, lax.ppermute(leaves, 'mem', ways[step])], leaves)  6.04 us
    ppermute x4, starting transfers between devices, by_levels(): remotes.append(lax.ppermute(piece, 'band', swap))  5.09 us
  transfers between devices with their start and end apart: 40, of which 13 were waited for; matrix products, arithmetic and copies ran while one was open for 4% of the time, Pallas kernels for 32%

profile of v11, /device:TPU:0, one launch (start us, length us, event | category | flops | bytes accessed | tf_op | source)
XLA Modules:
  0.0 183.8 jit_solution(13931986443851125507)
XLA Ops:
  0.0 2.6 %pieces_of.4 = f32[2,136,640]{2,1,0:T(8,128)} custom-call(s32[1]{0:T(128)} %bitcast.5.level_ref, f32[2,2,640,640]{3,2,1,0:T(8,128)} %bitcast.25), custom_call_target="tpu_custom_call" | custom-call | bytes 5242880 | tf_op jit(solution)/shard_map/pieces_of/pallas_call | solution.py:209
  2.6 3.0 %collective-permute-start = (f32[2,136,640]{2,1,0:T(8,128)}, f32[2,136,640]{2,1,0:T(8,128)S(1)}, u32[]{:S(2)}, u32[]{:S(2)}) collective-permute-start(f32[2,136,640]{2,1,0:T(8,128)} %pieces_of.4), channel_id=1, source_target_pairs={{0,1},{1,0},{2,3},{3,2},{4,5},{5,4},{6,7},{7,6},{8,9},{9,8},{10,11... | collective-permute-start | bytes 2088968 | tf_op jit(solution)/shard_map/ppermute | solution.py:481
  5.6 3.6 %pieces_of.5 = (f32[2,128,640]{2,1,0:T(8,128)}, f32[2,128,640]{2,1,0:T(8,128)}, f32[2,128,640]{2,1,0:T(8,128)}, f32[2,120,640]{2,1,0:T(8,128)}) custom-call(s32[1]{0:T(128)} %bitcast.5.level_ref, f32[2,2,640,640]{3,2,1,0:T(8,128)} %bitcast.26), custom_call_target="tpu_custom_call" | custom-call | bytes 10485760 | tf_op jit(solution)/shard_map/pieces_of/pallas_call | solution.py:209
  9.4 4.0 %pieces_of.3 = (f32[2,136,640]{2,1,0:T(8,128)}, f32[2,128,640]{2,1,0:T(8,128)}, f32[2,128,640]{2,1,0:T(8,128)}, f32[2,128,640]{2,1,0:T(8,128)}, f32[2,120,640]{2,1,0:T(8,128)}) custom-call(s32[1]{0:T(128)} %bitcast.level_ref, f32[2,2,640,640]{3,2,1,0:T(8,128)} %bitcast.27), custom_call_target="tpu_custom_call" | custom-call | bytes 13107200 | tf_op jit(solution)/shard_map/pieces_of/pallas_call | solution.py:209
  14.0 8.2 %collective-permute-done.refs_2_.refs_1_ = f32[2,136,640]{2,1,0:T(8,128)S(1)} collective-permute-done((f32[2,136,640]{2,1,0:T(8,128)}, f32[2,136,640]{2,1,0:T(8,128)S(1)}, u32[]{:S(2)}, u32[]{:S(2)}) %collective-permute-start) | collective-permute-done | bytes 696352 | tf_op jit(solution)/shard_map/ppermute | solution.py:481
  22.2 0.9 copy-done.1
  23.1 10.5 %window_tensor.5 = (f32[3,32,1280]{2,1,0:T(8,128)}, f32[3,32,1280]{2,1,0:T(8,128)}, f32[3,32,1280]{2,1,0:T(8,128)}, f32[3,32,1280]{2,1,0:T(8,128)}, f32[2,16,1280]{2,1,0:T(8,128)}) custom-call(s32[4]{0:T(128)} %pad_add_fusion.refs_0_, f32[2,136,640]{2,1,0:T(8,128)} %get-tuple-element.38.refs_1_, f32[2,136,640]{2,1,0:T(8,128)} %copy-done.1, ...), custom_call_target="tpu_custom_call" | custom-call | flops 10695475200 | bytes 6635520 | tf_op jit(solution)/shard_map/window_tensor/pallas_call | solution.py:398
  33.8 2.1 %collective-permute-start.13 = (f32[2,128,640]{2,1,0:T(8,128)}, f32[2,128,640]{2,1,0:T(8,128)S(1)}, u32[]{:S(2)}, u32[]{:S(2)}) collective-permute-start(f32[2,128,640]{2,1,0:T(8,128)} %gated.3), channel_id=1, source_target_pairs={{0,1},{1,0},{2,3},{3,2},{4,5},{5,4},{6,7},{7,6},{8,9},{9,8},{10,11... | collective-permute-start | bytes 1966088 | tf_op jit(solution)/shard_map/ppermute | solution.py:485
  35.9 0.8 copy-done.3
  36.7 10.1 %window_tensor.6 = (f32[3,32,1280]{2,1,0:T(8,128)}, f32[3,32,1280]{2,1,0:T(8,128)}, f32[3,32,1280]{2,1,0:T(8,128)}, f32[3,32,1280]{2,1,0:T(8,128)}, f32[2,16,1280]{2,1,0:T(8,128)}) custom-call(s32[4]{0:T(128)} %pad_add_fusion.refs_0_, f32[2,128,640]{2,1,0:T(8,128)} %get-tuple-element.43.refs_1_, f32[2,128,640]{2,1,0:T(8,128)} %copy-done.3, ...), custom_call_target="tpu_custom_call" | custom-call | flops 10066329600 | bytes 6553600 | tf_op jit(solution)/shard_map/window_tensor/pallas_call | solution.py:398
  47.1 1.3 collective-permute-start.24
  48.9 0.8 add.295.refs_4_
  49.7 1.5 collective-permute-start.3
  51.7 2.0 %collective-permute-start.9 = (f32[3,32,1280]{2,1,0:T(8,128)S(1)}, f32[3,32,1280]{2,1,0:T(8,128)}, u32[]{:S(2)}, u32[]{:S(2)}) collective-permute-start(f32[3,32,1280]{2,1,0:T(8,128)S(1)} %add.310.refs_4_), channel_id=1, source_target_pairs={{0,4},{2,10},{4,0},{6,14},{8,12},{10,2},{12,8},{14,6},{16,20},{18,... | collective-permute-start | bytes 1474568 | tf_op jit(solution)/shard_map/ppermute | solution.py:504
  53.7 10.4 %window_tensor.7 = (f32[3,32,1280]{2,1,0:T(8,128)}, f32[3,32,1280]{2,1,0:T(8,128)}, f32[3,32,1280]{2,1,0:T(8,128)}, f32[3,32,1280]{2,1,0:T(8,128)}, f32[2,16,1280]{2,1,0:T(8,128)}) custom-call(s32[4]{0:T(128)} %pad_add_fusion.refs_0_, f32[2,128,640]{2,1,0:T(8,128)} %get-tuple-element.50.refs_1_, f32[2,128,640]{2,1,0:T(8,128)} %copy-done.2, ...), custom_call_target="tpu_custom_call" | custom-call | flops 10066329600 | bytes 6553600 | tf_op jit(solution)/shard_map/window_tensor/pallas_call | solution.py:398
  64.2 1.6 collective-permute-start.30
  65.7 1.8 dynamic-slice_add_fusion.9
  67.7 1.6 collective-permute-start.4
  69.3 1.4 dynamic-slice_add_fusion.7
  71.2 10.2 %window_tensor.8 = (f32[3,32,1280]{2,1,0:T(8,128)}, f32[3,32,1280]{2,1,0:T(8,128)}, f32[3,32,1280]{2,1,0:T(8,128)}, f32[3,32,1280]{2,1,0:T(8,128)}, f32[2,16,1280]{2,1,0:T(8,128)}) custom-call(s32[4]{0:T(128)} %pad_add_fusion.refs_0_, f32[2,128,640]{2,1,0:T(8,128)} %get-tuple-element.57.refs_1_, f32[2,128,640]{2,1,0:T(8,128)} %collective-permute-done.24.refs_2_, ...), custom_call_target="tpu_custom_call" | custom-call | flops 10066329600 | bytes 6553600 | tf_op jit(solution)/shard_map/window_tensor/pallas_call | solution.py:398
  81.4 0.8 collective-permute-start.26
  82.4 0.7 dynamic-slice_add_fusion.14.refs_6_
  83.1 0.8 collective-permute-start.16
  83.9 2.7 %collective-permute-start.5 = (f32[3,8,1280]{2,1,0:T(8,128)}, f32[3,8,1280]{2,1,0:T(8,128)}, u32[]{:S(2)}, u32[]{:S(2)}) collective-permute-start(f32[3,8,1280]{2,1,0:T(8,128)} %dynamic-slice_add_fusion.14.refs_6_), channel_id=1, source_target_pairs={{0,16},{2,6},{4,20},{6,2},{8,24},{10,14},{12,28},{14,10},{16,0},{1... | collective-permute-start | bytes 368648 | tf_op jit(solution)/shard_map/ppermute | solution.py:499
  86.6 10.1 %window_tensor.9 = (f32[3,32,1280]{2,1,0:T(8,128)}, f32[3,32,1280]{2,1,0:T(8,128)}, f32[3,32,1280]{2,1,0:T(8,128)}, f32[3,32,1280]{2,1,0:T(8,128)}) custom-call(s32[4]{0:T(128)} %pad_add_fusion.refs_0_, f32[2,120,640]{2,1,0:T(8,128)} %get-tuple-element.64.refs_1_, f32[2,120,640]{2,1,0:T(8,128)} %collective-permute-done.30.refs_2_, ...), custom_call_target="tpu_custom_call" | custom-call | flops 9437184000 | bytes 6471680 | tf_op jit(solution)/shard_map/window_tensor/pallas_call | solution.py:398
  97.1 0.9 add_multiply_fusion.4
  98.1 5.8 %collective-permute-done.11 = f32[3,8,1280]{2,1,0:T(8,128)S(1)} collective-permute-done((f32[3,8,1280]{2,1,0:T(8,128)S(1)}, f32[3,8,1280]{2,1,0:T(8,128)S(1)}, u32[]{:S(2)}, u32[]{:S(2)}) %collective-permute-start.11) | collective-permute-done | bytes 122912 | tf_op jit(solution)/shard_map/ppermute | solution.py:499
  104.5 7.4 %collective-permute-done.17 = f32[3,16,1280]{2,1,0:T(8,128)S(1)} collective-permute-done((f32[3,16,1280]{2,1,0:T(8,128)S(1)}, f32[3,16,1280]{2,1,0:T(8,128)S(1)}, u32[]{:S(2)}, u32[]{:S(2)}) %collective-permute-start.17) | collective-permute-done | bytes 245792 | tf_op jit(solution)/shard_map/ppermute | solution.py:499
  112.0 0.9 collective-permute-start.12
  113.0 1.3 collective-permute-start.27
  114.3 4.7 %collective-permute-done.18 = f32[3,8,1280]{2,1,0:T(8,128)S(1)} collective-permute-done((f32[3,8,1280]{2,1,0:T(8,128)S(1)}, f32[3,8,1280]{2,1,0:T(8,128)S(1)}, u32[]{:S(2)}, u32[]{:S(2)}) %collective-permute-start.18) | collective-permute-done | bytes 122912 | tf_op jit(solution)/shard_map/ppermute | solution.py:499
  119.1 0.9 collective-permute-start.19
  120.0 2.5 %collective-permute-start.31 = (f32[3,32,1280]{2,1,0:T(8,128)}, f32[3,32,1280]{2,1,0:T(8,128)S(1)}, u32[]{:S(2)}, u32[]{:S(2)}) collective-permute-start(f32[3,32,1280]{2,1,0:T(8,128)} %get-tuple-element.68), channel_id=1, source_target_pairs={{0,2},{2,0},{4,6},{6,4},{8,10},{10,8},{12,14},{14,12},{16,18},{18,... | collective-permute-start | bytes 1474568 | tf_op jit(solution)/shard_map/ppermute | solution.py:529
  123.0 2.1 %collective-permute-start.20 = (f32[3,8,1280]{2,1,0:T(8,128)S(1)}, f32[3,8,1280]{2,1,0:T(8,128)S(1)}, u32[]{:S(2)}, u32[]{:S(2)}) collective-permute-start(f32[3,8,1280]{2,1,0:T(8,128)S(1)} %pad_maximum_fusion), channel_id=1, source_target_pairs={{0,16},{2,6},{4,20},{6,2},{8,24},{10,14},{12,28},{14,10},{16,0},{1... | collective-permute-start | bytes 368648 | tf_op jit(solution)/shard_map/ppermute | solution.py:510
  125.2 1.3 collective-permute-start.28
  126.5 2.8 %collective-permute-done.20 = f32[3,8,1280]{2,1,0:T(8,128)S(1)} collective-permute-done((f32[3,8,1280]{2,1,0:T(8,128)S(1)}, f32[3,8,1280]{2,1,0:T(8,128)S(1)}, u32[]{:S(2)}, u32[]{:S(2)}) %collective-permute-start.20) | collective-permute-done | bytes 122912 | tf_op jit(solution)/shard_map/ppermute | solution.py:510
  129.3 2.6 %collective-permute-start.21 = (f32[3,16,1280]{2,1,0:T(8,128)S(1)}, f32[3,16,1280]{2,1,0:T(8,128)S(1)}, u32[]{:S(2)}, u32[]{:S(2)}) collective-permute-start(f32[3,16,1280]{2,1,0:T(8,128)S(1)} %maximum_select_fusion.7), channel_id=1, source_target_pairs={{0,8},{2,18},{4,12},{6,22},{8,0},{10,26},{12,4},{14,30},{16,24},{1... | collective-permute-start | bytes 737288 | tf_op jit(solution)/shard_map/ppermute | solution.py:510
  131.8 7.8 %collective-permute-done.28 = f32[3,16,1280]{2,1,0:T(8,128)S(1)} collective-permute-done((f32[3,16,1280]{2,1,0:T(8,128)S(1)}, f32[3,16,1280]{2,1,0:T(8,128)S(1)}, u32[]{:S(2)}, u32[]{:S(2)}) %collective-permute-start.28) | collective-permute-done | bytes 245792 | tf_op jit(solution)/shard_map/ppermute | solution.py:499
  139.6 0.7 collective-permute-start.29
  140.5 2.5 %collective-permute-start.34 = (f32[3,16,1280]{2,1,0:T(8,128)S(1)}, f32[3,16,1280]{2,1,0:T(8,128)S(1)}, u32[]{:S(2)}, u32[]{:S(2)}) collective-permute-start(f32[3,16,1280]{2,1,0:T(8,128)S(1)} %get-tuple-element.78), channel_id=1, source_target_pairs={{0,8},{2,18},{4,12},{6,22},{8,0},{10,26},{12,4},{14,30},{16,24},{1... | collective-permute-start | bytes 737288 | tf_op jit(solution)/shard_map/ppermute | solution.py:499
  143.0 7.4 %collective-permute-done.29 = f32[3,8,1280]{2,1,0:T(8,128)S(1)} collective-permute-done((f32[3,8,1280]{2,1,0:T(8,128)S(1)}, f32[3,8,1280]{2,1,0:T(8,128)S(1)}, u32[]{:S(2)}, u32[]{:S(2)}) %collective-permute-start.29) | collective-permute-done | bytes 122912 | tf_op jit(solution)/shard_map/ppermute | solution.py:499
  151.1 6.3 %collective-permute-done.35 = f32[3,8,1280]{2,1,0:T(8,128)S(1)} collective-permute-done((f32[3,8,1280]{2,1,0:T(8,128)S(1)}, f32[3,8,1280]{2,1,0:T(8,128)S(1)}, u32[]{:S(2)}, u32[]{:S(2)}) %collective-permute-start.35) | collective-permute-done | bytes 122912 | tf_op jit(solution)/shard_map/ppermute | solution.py:499
  157.8 6.2 %collective-permute-done.36 = f32[2,8,1280]{2,1,0:T(8,128)S(1)} collective-permute-done((f32[2,8,1280]{2,1,0:T(8,128)S(1)}, f32[2,8,1280]{2,1,0:T(8,128)S(1)}, u32[]{:S(2)}, u32[]{:S(2)}) %collective-permute-start.36) | collective-permute-done | bytes 81952 | tf_op jit(solution)/shard_map/ppermute | solution.py:510
  164.0 6.4 %collective-permute-done.37 = f32[2,16,1280]{2,1,0:T(8,128)S(1)} collective-permute-done((f32[2,16,1280]{2,1,0:T(8,128)S(1)}, f32[2,16,1280]{2,1,0:T(8,128)S(1)}, u32[]{:S(2)}, u32[]{:S(2)}) %collective-permute-start.37) | collective-permute-done | bytes 163872 | tf_op jit(solution)/shard_map/ppermute | solution.py:510
  170.7 6.9 %collective-permute-done.38 = f32[2,32,1280]{2,1,0:T(8,128)S(1)} collective-permute-done((f32[2,32,1280]{2,1,0:T(8,128)S(1)}, f32[2,32,1280]{2,1,0:T(8,128)S(1)}, u32[]{:S(2)}, u32[]{:S(2)}) %collective-permute-start.38) | collective-permute-done | bytes 327712 | tf_op jit(solution)/shard_map/ppermute | solution.py:510
  177.7 2.1 %collective-permute-done.39 = f32[2,64,1280]{2,1,0:T(8,128)S(1)} collective-permute-done((f32[2,64,1280]{2,1,0:T(8,128)S(1)}, f32[2,64,1280]{2,1,0:T(8,128)S(1)}, u32[]{:S(2)}, u32[]{:S(2)}) %collective-permute-start.39) | collective-permute-done | bytes 655392 | tf_op jit(solution)/shard_map/ppermute | solution.py:510
  181.2 1.7 copy-done
  182.9 0.9 slice_dynamic-update-slice_fusion
  (120 shorter events, 7.7 us)
Async XLA Ops:
  2.6 19.6 %collective-permute-start = (f32[2,136,640]{2,1,0:T(8,128)}, f32[2,136,640]{2,1,0:T(8,128)S(1)}, u32[]{:S(2)}, u32[]{:S(2)}) collective-permute-start(f32[2,136,640]{2,1,0:T(8,128)} %pieces_of.4), channel_id=1, source_target_pairs={{0,1},{1,0},{2,3},{3,2},{4,5},{5,4},{6,7},{7,6},{8,9},{9,8},{10,11... | collective-permute-start | bytes 2088968 | tf_op jit(solution)/shard_map/ppermute | solution.py:481
  9.2 26.7 %collective-permute-start.6 = (f32[2,128,640]{2,1,0:T(8,128)}, f32[2,128,640]{2,1,0:T(8,128)S(1)}, u32[]{:S(2)}, u32[]{:S(2)}) collective-permute-start(f32[2,128,640]{2,1,0:T(8,128)} %get-tuple-element.44), channel_id=1, source_target_pairs={{0,1},{1,0},{2,3},{3,2},{4,5},{5,4},{6,7},{7,6},{8,9},{9,8},{10,11... | collective-permute-start | bytes 1966088 | tf_op jit(solution)/shard_map/ppermute | solution.py:485
  33.7 14.8 %collective-permute-start.2 = (f32[3,32,1280]{2,1,0:T(8,128)}, f32[3,32,1280]{2,1,0:T(8,128)S(1)}, u32[]{:S(2)}, u32[]{:S(2)}) collective-permute-start(f32[3,32,1280]{2,1,0:T(8,128)} %get-tuple-element.42), channel_id=1, source_target_pairs={{0,2},{2,0},{4,6},{6,4},{8,10},{10,8},{12,14},{14,12},{16,18},{18,... | collective-permute-start | bytes 1474568 | tf_op jit(solution)/shard_map/ppermute | solution.py:528
  33.8 17.9 %collective-permute-start.13 = (f32[2,128,640]{2,1,0:T(8,128)}, f32[2,128,640]{2,1,0:T(8,128)S(1)}, u32[]{:S(2)}, u32[]{:S(2)}) collective-permute-start(f32[2,128,640]{2,1,0:T(8,128)} %gated.3), channel_id=1, source_target_pairs={{0,1},{1,0},{2,3},{3,2},{4,5},{5,4},{6,7},{7,6},{8,9},{9,8},{10,11... | collective-permute-start | bytes 1966088 | tf_op jit(solution)/shard_map/ppermute | solution.py:485
  46.8 2.9 %collective-permute-start.8 = (f32[3,32,1280]{2,1,0:T(8,128)}, f32[3,32,1280]{2,1,0:T(8,128)S(1)}, u32[]{:S(2)}, u32[]{:S(2)}) collective-permute-start(f32[3,32,1280]{2,1,0:T(8,128)} %get-tuple-element.49), channel_id=1, source_target_pairs={{0,2},{2,0},{4,6},{6,4},{8,10},{10,8},{12,14},{14,12},{16,18},{18,... | collective-permute-start | bytes 1474568 | tf_op jit(solution)/shard_map/ppermute | solution.py:528
  47.1 23.6 %collective-permute-start.24 = (f32[2,128,640]{2,1,0:T(8,128)}, f32[2,128,640]{2,1,0:T(8,128)}, u32[]{:S(2)}, u32[]{:S(2)}) collective-permute-start(f32[2,128,640]{2,1,0:T(8,128)} %gated.4), channel_id=1, source_target_pairs={{0,1},{1,0},{2,3},{3,2},{4,5},{5,4},{6,7},{7,6},{8,9},{9,8},{10,11... | collective-permute-start | bytes 1966088 | tf_op jit(solution)/shard_map/ppermute | solution.py:485
  48.4 15.7 %collective-permute-start.1 = (f32[3,32,1280]{2,1,0:T(8,128)}, f32[3,32,1280]{2,1,0:T(8,128)S(1)}, u32[]{:S(2)}, u32[]{:S(2)}) collective-permute-start(f32[3,32,1280]{2,1,0:T(8,128)} %get-tuple-element.40), channel_id=1, source_target_pairs={{0,2},{2,0},{4,6},{6,4},{8,10},{10,8},{12,14},{14,12},{16,18},{18,... | collective-permute-start | bytes 1474568 | tf_op jit(solution)/shard_map/ppermute | solution.py:529
  48.5 19.1 %collective-permute-start.7 = (f32[3,32,1280]{2,1,0:T(8,128)}, f32[3,32,1280]{2,1,0:T(8,128)}, u32[]{:S(2)}, u32[]{:S(2)}) collective-permute-start(f32[3,32,1280]{2,1,0:T(8,128)} %get-tuple-element.47), channel_id=1, source_target_pairs={{0,2},{2,0},{4,6},{6,4},{8,10},{10,8},{12,14},{14,12},{16,18},{18,... | collective-permute-start | bytes 1474568 | tf_op jit(solution)/shard_map/ppermute | solution.py:529
  49.7 14.4 %collective-permute-start.3 = (f32[3,32,1280]{2,1,0:T(8,128)}, f32[3,32,1280]{2,1,0:T(8,128)}, u32[]{:S(2)}, u32[]{:S(2)}) collective-permute-start(f32[3,32,1280]{2,1,0:T(8,128)} %add.295.refs_4_), channel_id=1, source_target_pairs={{0,4},{2,10},{4,0},{6,14},{8,12},{10,2},{12,8},{14,6},{16,20},{18,... | collective-permute-start | bytes 1474568 | tf_op jit(solution)/shard_map/ppermute | solution.py:504
  51.3 12.7 %copy-start.13 = (f32[3,32,1280]{2,1,0:T(8,128)}, f32[3,32,1280]{2,1,0:T(8,128)S(1)}, u32[]{:S(2)}) copy-start(f32[3,32,1280]{2,1,0:T(8,128)S(1)} %add.310.refs_4_) | copy-start | bytes 1474564
  51.7 16.0 %collective-permute-start.9 = (f32[3,32,1280]{2,1,0:T(8,128)S(1)}, f32[3,32,1280]{2,1,0:T(8,128)}, u32[]{:S(2)}, u32[]{:S(2)}) collective-permute-start(f32[3,32,1280]{2,1,0:T(8,128)S(1)} %add.310.refs_4_), channel_id=1, source_target_pairs={{0,4},{2,10},{4,0},{6,14},{8,12},{10,2},{12,8},{14,6},{16,20},{18,... | collective-permute-start | bytes 1474568 | tf_op jit(solution)/shard_map/ppermute | solution.py:504
  64.1 17.3 %collective-permute-start.15 = (f32[3,32,1280]{2,1,0:T(8,128)}, f32[3,32,1280]{2,1,0:T(8,128)S(1)}, u32[]{:S(2)}, u32[]{:S(2)}) collective-permute-start(f32[3,32,1280]{2,1,0:T(8,128)} %get-tuple-element.56), channel_id=1, source_target_pairs={{0,2},{2,0},{4,6},{6,4},{8,10},{10,8},{12,14},{14,12},{16,18},{18,... | collective-permute-start | bytes 1474568 | tf_op jit(solution)/shard_map/ppermute | solution.py:528
  64.2 19.7 %collective-permute-start.30 = (f32[2,120,640]{2,1,0:T(8,128)}, f32[2,120,640]{2,1,0:T(8,128)}, u32[]{:S(2)}, u32[]{:S(2)}) collective-permute-start(f32[2,120,640]{2,1,0:T(8,128)} %gated.5), channel_id=1, source_target_pairs={{0,1},{1,0},{2,3},{3,2},{4,5},{5,4},{6,7},{7,6},{8,9},{9,8},{10,11... | collective-permute-start | bytes 1843208 | tf_op jit(solution)/shard_map/ppermute | solution.py:485
  67.6 36.3 %collective-permute-start.14 = (f32[3,32,1280]{2,1,0:T(8,128)}, f32[3,32,1280]{2,1,0:T(8,128)S(1)}, u32[]{:S(2)}, u32[]{:S(2)}) collective-permute-start(f32[3,32,1280]{2,1,0:T(8,128)} %get-tuple-element.54), channel_id=1, source_target_pairs={{0,2},{2,0},{4,6},{6,4},{8,10},{10,8},{12,14},{14,12},{16,18},{18,... | collective-permute-start | bytes 1474568 | tf_op jit(solution)/shard_map/ppermute | solution.py:529
  67.7 14.5 %collective-permute-start.4 = (f32[3,16,1280]{2,1,0:T(8,128)}, f32[3,16,1280]{2,1,0:T(8,128)S(1)}, u32[]{:S(2)}, u32[]{:S(2)}) collective-permute-start(f32[3,16,1280]{2,1,0:T(8,128)} %get-tuple-element.80.refs_5_), channel_id=1, source_target_pairs={{0,8},{2,18},{4,12},{6,22},{8,0},{10,26},{12,4},{14,30},{16,24},{1... | collective-permute-start | bytes 737288 | tf_op jit(solution)/shard_map/ppermute | solution.py:499
  70.7 10.7 %copy-start.16 = (f32[3,16,1280]{2,1,0:T(8,128)}, f32[3,16,1280]{2,1,0:T(8,128)S(1)}, u32[]{:S(2)}) copy-start(f32[3,16,1280]{2,1,0:T(8,128)S(1)} %get-tuple-element.82.refs_5_) | copy-start | bytes 737284
  70.7 12.3 %collective-permute-start.10 = (f32[3,16,1280]{2,1,0:T(8,128)S(1)}, f32[3,16,1280]{2,1,0:T(8,128)S(1)}, u32[]{:S(2)}, u32[]{:S(2)}) collective-permute-start(f32[3,16,1280]{2,1,0:T(8,128)S(1)} %get-tuple-element.82.refs_5_), channel_id=1, source_target_pairs={{0,8},{2,18},{4,12},{6,22},{8,0},{10,26},{12,4},{14,30},{16,24},{1... | collective-permute-start | bytes 737288 | tf_op jit(solution)/shard_map/ppermute | solution.py:499
  71.2 11.0 %copy-start.14 = (f32[3,32,1280]{2,1,0:T(8,128)S(1)}, f32[3,32,1280]{2,1,0:T(8,128)}, u32[]{:S(2)}) copy-start(f32[3,32,1280]{2,1,0:T(8,128)} %get-tuple-element.55) | copy-start | bytes 1474564
  81.4 31.5 %collective-permute-start.26 = (f32[3,32,1280]{2,1,0:T(8,128)}, f32[3,32,1280]{2,1,0:T(8,128)S(1)}, u32[]{:S(2)}, u32[]{:S(2)}) collective-permute-start(f32[3,32,1280]{2,1,0:T(8,128)} %get-tuple-element.63), channel_id=1, source_target_pairs={{0,2},{2,0},{4,6},{6,4},{8,10},{10,8},{12,14},{14,12},{16,18},{18,... | collective-permute-start | bytes 1474568 | tf_op jit(solution)/shard_map/ppermute | solution.py:528
  82.3 42.8 %collective-permute-start.25 = (f32[3,32,1280]{2,1,0:T(8,128)}, f32[3,32,1280]{2,1,0:T(8,128)S(1)}, u32[]{:S(2)}, u32[]{:S(2)}) collective-permute-start(f32[3,32,1280]{2,1,0:T(8,128)} %get-tuple-element.61), channel_id=1, source_target_pairs={{0,2},{2,0},{4,6},{6,4},{8,10},{10,8},{12,14},{14,12},{16,18},{18,... | collective-permute-start | bytes 1474568 | tf_op jit(solution)/shard_map/ppermute | solution.py:529
  83.1 20.9 %collective-permute-start.16 = (f32[3,32,1280]{2,1,0:T(8,128)S(1)}, f32[3,32,1280]{2,1,0:T(8,128)S(1)}, u32[]{:S(2)}, u32[]{:S(2)}) collective-permute-start(f32[3,32,1280]{2,1,0:T(8,128)S(1)} %add.322.refs_4_), channel_id=1, source_target_pairs={{0,4},{2,10},{4,0},{6,14},{8,12},{10,2},{12,8},{14,6},{16,20},{18,... | collective-permute-start | bytes 1474568 | tf_op jit(solution)/shard_map/ppermute | solution.py:504
  83.9 12.8 %collective-permute-start.5 = (f32[3,8,1280]{2,1,0:T(8,128)}, f32[3,8,1280]{2,1,0:T(8,128)}, u32[]{:S(2)}, u32[]{:S(2)}) collective-permute-start(f32[3,8,1280]{2,1,0:T(8,128)} %dynamic-slice_add_fusion.14.refs_6_), channel_id=1, source_target_pairs={{0,16},{2,6},{4,20},{6,2},{8,24},{10,14},{12,28},{14,10},{16,0},{1... | collective-permute-start | bytes 368648 | tf_op jit(solution)/shard_map/ppermute | solution.py:499
  86.6 17.4 %copy-start.8 = (f32[3,32,1280]{2,1,0:T(8,128)S(1)}, f32[3,32,1280]{2,1,0:T(8,128)}, u32[]{:S(2)}) copy-start(f32[3,32,1280]{2,1,0:T(8,128)} %get-tuple-element.53) | copy-start | bytes 1474564
  96.7 7.2 %collective-permute-start.11 = (f32[3,8,1280]{2,1,0:T(8,128)S(1)}, f32[3,8,1280]{2,1,0:T(8,128)S(1)}, u32[]{:S(2)}, u32[]{:S(2)}) collective-permute-start(f32[3,8,1280]{2,1,0:T(8,128)S(1)} %dynamic-slice_add_fusion.13), channel_id=1, source_target_pairs={{0,16},{2,6},{4,20},{6,2},{8,24},{10,14},{12,28},{14,10},{16,0},{1... | collective-permute-start | bytes 368648 | tf_op jit(solution)/shard_map/ppermute | solution.py:499
  98.0 14.9 %copy-start.11 = (f32[3,32,1280]{2,1,0:T(8,128)S(1)}, f32[3,32,1280]{2,1,0:T(8,128)}, u32[]{:S(2)}) copy-start(f32[3,32,1280]{2,1,0:T(8,128)} %get-tuple-element.62) | copy-start | bytes 1474564
  103.9 16.1 %collective-permute-start.32 = (f32[3,32,1280]{2,1,0:T(8,128)}, f32[3,32,1280]{2,1,0:T(8,128)S(1)}, u32[]{:S(2)}, u32[]{:S(2)}) collective-permute-start(f32[3,32,1280]{2,1,0:T(8,128)} %get-tuple-element.70), channel_id=1, source_target_pairs={{0,2},{2,0},{4,6},{6,4},{8,10},{10,8},{12,14},{14,12},{16,18},{18,... | collective-permute-start | bytes 1474568 | tf_op jit(solution)/shard_map/ppermute | solution.py:528
  104.0 18.5 %copy-start.12 = (f32[3,32,1280]{2,1,0:T(8,128)S(1)}, f32[3,32,1280]{2,1,0:T(8,128)}, u32[]{:S(2)}) copy-start(f32[3,32,1280]{2,1,0:T(8,128)} %get-tuple-element.69) | copy-start | bytes 1474564
  104.0 7.9 %collective-permute-start.17 = (f32[3,16,1280]{2,1,0:T(8,128)S(1)}, f32[3,16,1280]{2,1,0:T(8,128)S(1)}, u32[]{:S(2)}, u32[]{:S(2)}) collective-permute-start(f32[3,16,1280]{2,1,0:T(8,128)S(1)} %get-tuple-element.84), channel_id=1, source_target_pairs={{0,8},{2,18},{4,12},{6,22},{8,0},{10,26},{12,4},{14,30},{16,24},{1... | collective-permute-start | bytes 737288 | tf_op jit(solution)/shard_map/ppermute | solution.py:499
  111.9 7.1 %collective-permute-start.18 = (f32[3,8,1280]{2,1,0:T(8,128)S(1)}, f32[3,8,1280]{2,1,0:T(8,128)S(1)}, u32[]{:S(2)}, u32[]{:S(2)}) collective-permute-start(f32[3,8,1280]{2,1,0:T(8,128)S(1)} %dynamic-slice_add_fusion.12), channel_id=1, source_target_pairs={{0,16},{2,6},{4,20},{6,2},{8,24},{10,14},{12,28},{14,10},{16,0},{1... | collective-permute-start | bytes 368648 | tf_op jit(solution)/shard_map/ppermute | solution.py:499
  112.0 10.5 %collective-permute-start.12 = (f32[2,8,1280]{2,1,0:T(8,128)S(1)}, f32[2,8,1280]{2,1,0:T(8,128)S(1)}, u32[]{:S(2)}, u32[]{:S(2)}) collective-permute-start(f32[2,8,1280]{2,1,0:T(8,128)S(1)} %pad_maximum_fusion.1), channel_id=1, source_target_pairs={{0,1},{1,0},{2,3},{3,2},{4,5},{5,4},{6,7},{7,6},{8,9},{9,8},{10,11... | collective-permute-start | bytes 245768 | tf_op jit(solution)/shard_map/ppermute | solution.py:538
  112.9 12.1 %copy-start.6 = (f32[3,32,1280]{2,1,0:T(8,128)S(1)}, f32[3,32,1280]{2,1,0:T(8,128)}, u32[]{:S(2)}) copy-start(f32[3,32,1280]{2,1,0:T(8,128)} %get-tuple-element.60) | copy-start | bytes 1474564
  113.0 12.1 %collective-permute-start.27 = (f32[3,32,1280]{2,1,0:T(8,128)S(1)}, f32[3,32,1280]{2,1,0:T(8,128)S(1)}, u32[]{:S(2)}, u32[]{:S(2)}) collective-permute-start(f32[3,32,1280]{2,1,0:T(8,128)S(1)} %add.335), channel_id=1, source_target_pairs={{0,4},{2,10},{4,0},{6,14},{8,12},{10,2},{12,8},{14,6},{16,20},{18,... | collective-permute-start | bytes 1474568 | tf_op jit(solution)/shard_map/ppermute | solution.py:504
  119.1 3.9 %collective-permute-start.19 = (f32[8,1280]{1,0:T(8,128)S(1)}, f32[8,1280]{1,0:T(8,128)S(1)}, u32[]{:S(2)}, u32[]{:S(2)}) collective-permute-start(f32[8,1280]{1,0:T(8,128)S(1)} %fusion.18), channel_id=1, source_target_pairs={{0,0},{1,2},{2,1},{3,3},{4,4},{5,10},{6,17},{7,7},{8,8},{9,18},{10... | collective-permute-start | bytes 122888 | tf_op jit(solution)/shard_map/ppermute | solution.py:549
  120.0 20.4 %collective-permute-start.31 = (f32[3,32,1280]{2,1,0:T(8,128)}, f32[3,32,1280]{2,1,0:T(8,128)S(1)}, u32[]{:S(2)}, u32[]{:S(2)}) collective-permute-start(f32[3,32,1280]{2,1,0:T(8,128)} %get-tuple-element.68), channel_id=1, source_target_pairs={{0,2},{2,0},{4,6},{6,4},{8,10},{10,8},{12,14},{14,12},{16,18},{18,... | collective-permute-start | bytes 1474568 | tf_op jit(solution)/shard_map/ppermute | solution.py:529
  122.5 17.8 %copy-start.7 = (f32[3,32,1280]{2,1,0:T(8,128)S(1)}, f32[3,32,1280]{2,1,0:T(8,128)}, u32[]{:S(2)}) copy-start(f32[3,32,1280]{2,1,0:T(8,128)} %get-tuple-element.67) | copy-start | bytes 1474564
  122.6 17.8 %collective-permute-start.33 = (f32[3,32,1280]{2,1,0:T(8,128)S(1)}, f32[3,32,1280]{2,1,0:T(8,128)S(1)}, u32[]{:S(2)}, u32[]{:S(2)}) collective-permute-start(f32[3,32,1280]{2,1,0:T(8,128)S(1)} %add.347), channel_id=1, source_target_pairs={{0,4},{2,10},{4,0},{6,14},{8,12},{10,2},{12,8},{14,6},{16,20},{18,... | collective-permute-start | bytes 1474568 | tf_op jit(solution)/shard_map/ppermute | solution.py:504
  123.0 6.2 %collective-permute-start.20 = (f32[3,8,1280]{2,1,0:T(8,128)S(1)}, f32[3,8,1280]{2,1,0:T(8,128)S(1)}, u32[]{:S(2)}, u32[]{:S(2)}) collective-permute-start(f32[3,8,1280]{2,1,0:T(8,128)S(1)} %pad_maximum_fusion), channel_id=1, source_target_pairs={{0,16},{2,6},{4,20},{6,2},{8,24},{10,14},{12,28},{14,10},{16,0},{1... | collective-permute-start | bytes 368648 | tf_op jit(solution)/shard_map/ppermute | solution.py:510
  125.2 14.4 %collective-permute-start.28 = (f32[3,16,1280]{2,1,0:T(8,128)S(1)}, f32[3,16,1280]{2,1,0:T(8,128)S(1)}, u32[]{:S(2)}, u32[]{:S(2)}) collective-permute-start(f32[3,16,1280]{2,1,0:T(8,128)S(1)} %get-tuple-element.76), channel_id=1, source_target_pairs={{0,8},{2,18},{4,12},{6,22},{8,0},{10,26},{12,4},{14,30},{16,24},{1... | collective-permute-start | bytes 737288 | tf_op jit(solution)/shard_map/ppermute | solution.py:499
  129.3 28.4 %collective-permute-start.21 = (f32[3,16,1280]{2,1,0:T(8,128)S(1)}, f32[3,16,1280]{2,1,0:T(8,128)S(1)}, u32[]{:S(2)}, u32[]{:S(2)}) collective-permute-start(f32[3,16,1280]{2,1,0:T(8,128)S(1)} %maximum_select_fusion.7), channel_id=1, source_target_pairs={{0,8},{2,18},{4,12},{6,22},{8,0},{10,26},{12,4},{14,30},{16,24},{1... | collective-permute-start | bytes 737288 | tf_op jit(solution)/shard_map/ppermute | solution.py:510
  139.6 10.8 %collective-permute-start.29 = (f32[3,8,1280]{2,1,0:T(8,128)S(1)}, f32[3,8,1280]{2,1,0:T(8,128)S(1)}, u32[]{:S(2)}, u32[]{:S(2)}) collective-permute-start(f32[3,8,1280]{2,1,0:T(8,128)S(1)} %dynamic-slice_add_fusion.11), channel_id=1, source_target_pairs={{0,16},{2,6},{4,20},{6,2},{8,24},{10,14},{12,28},{14,10},{16,0},{1... | collective-permute-start | bytes 368648 | tf_op jit(solution)/shard_map/ppermute | solution.py:499
  140.5 10.0 %collective-permute-start.34 = (f32[3,16,1280]{2,1,0:T(8,128)S(1)}, f32[3,16,1280]{2,1,0:T(8,128)S(1)}, u32[]{:S(2)}, u32[]{:S(2)}) collective-permute-start(f32[3,16,1280]{2,1,0:T(8,128)S(1)} %get-tuple-element.78), channel_id=1, source_target_pairs={{0,8},{2,18},{4,12},{6,22},{8,0},{10,26},{12,4},{14,30},{16,24},{1... | collective-permute-start | bytes 737288 | tf_op jit(solution)/shard_map/ppermute | solution.py:499
  150.5 6.9 %collective-permute-start.35 = (f32[3,8,1280]{2,1,0:T(8,128)S(1)}, f32[3,8,1280]{2,1,0:T(8,128)S(1)}, u32[]{:S(2)}, u32[]{:S(2)}) collective-permute-start(f32[3,8,1280]{2,1,0:T(8,128)S(1)} %dynamic-slice_add_fusion.10), channel_id=1, source_target_pairs={{0,16},{2,6},{4,20},{6,2},{8,24},{10,14},{12,28},{14,10},{16,0},{1... | collective-permute-start | bytes 368648 | tf_op jit(solution)/shard_map/ppermute | solution.py:499
  157.5 6.4 %collective-permute-start.36 = (f32[2,8,1280]{2,1,0:T(8,128)S(1)}, f32[2,8,1280]{2,1,0:T(8,128)S(1)}, u32[]{:S(2)}, u32[]{:S(2)}) collective-permute-start(f32[2,8,1280]{2,1,0:T(8,128)S(1)} %pad_maximum_fusion.2), channel_id=1, source_target_pairs={{0,16},{2,6},{4,20},{6,2},{8,24},{10,14},{12,28},{14,10},{16,0},{1... | collective-permute-start | bytes 245768 | tf_op jit(solution)/shard_map/ppermute | solution.py:510
  157.7 12.9 %collective-permute-start.22 = (f32[3,32,1280]{2,1,0:T(8,128)S(1)}, f32[3,32,1280]{2,1,0:T(8,128)S(1)}, u32[]{:S(2)}, u32[]{:S(2)}) collective-permute-start(f32[3,32,1280]{2,1,0:T(8,128)S(1)} %maximum_select_fusion.5), channel_id=1, source_target_pairs={{0,4},{2,10},{4,0},{6,14},{8,12},{10,2},{12,8},{14,6},{16,20},{18,... | collective-permute-start | bytes 1474568 | tf_op jit(solution)/shard_map/ppermute | solution.py:510
  163.9 6.5 %collective-permute-start.37 = (f32[2,16,1280]{2,1,0:T(8,128)S(1)}, f32[2,16,1280]{2,1,0:T(8,128)S(1)}, u32[]{:S(2)}, u32[]{:S(2)}) collective-permute-start(f32[2,16,1280]{2,1,0:T(8,128)S(1)} %maximum_select_fusion.8), channel_id=1, source_target_pairs={{0,8},{2,18},{4,12},{6,22},{8,0},{10,26},{12,4},{14,30},{16,24},{1... | collective-permute-start | bytes 491528 | tf_op jit(solution)/shard_map/ppermute | solution.py:510
  170.5 7.1 %collective-permute-start.38 = (f32[2,32,1280]{2,1,0:T(8,128)S(1)}, f32[2,32,1280]{2,1,0:T(8,128)S(1)}, u32[]{:S(2)}, u32[]{:S(2)}) collective-permute-start(f32[2,32,1280]{2,1,0:T(8,128)S(1)} %maximum_select_fusion.6), channel_id=1, source_target_pairs={{0,4},{2,10},{4,0},{6,14},{8,12},{10,2},{12,8},{14,6},{16,20},{18,... | collective-permute-start | bytes 983048 | tf_op jit(solution)/shard_map/ppermute | solution.py:510
  170.6 9.3 %collective-permute-start.23 = (f32[3,64,1280]{2,1,0:T(8,128)S(1)}, f32[3,64,1280]{2,1,0:T(8,128)S(1)}, u32[]{:S(2)}, u32[]{:S(2)}) collective-permute-start(f32[3,64,1280]{2,1,0:T(8,128)S(1)} %maximum_select_fusion.3), channel_id=1, source_target_pairs={{0,2},{2,0},{4,6},{6,4},{8,10},{10,8},{12,14},{14,12},{16,18},{18,... | collective-permute-start | bytes 2949128 | tf_op jit(solution)/shard_map/ppermute | solution.py:510
  177.7 2.2 %collective-permute-start.39 = (f32[2,64,1280]{2,1,0:T(8,128)S(1)}, f32[2,64,1280]{2,1,0:T(8,128)S(1)}, u32[]{:S(2)}, u32[]{:S(2)}) collective-permute-start(f32[2,64,1280]{2,1,0:T(8,128)S(1)} %maximum_select_fusion.4), channel_id=1, source_target_pairs={{0,2},{2,0},{4,6},{6,4},{8,10},{10,8},{12,14},{14,12},{16,18},{18,... | collective-permute-start | bytes 1966088 | tf_op jit(solution)/shard_map/ppermute | solution.py:510
  (9 other events, 23.0 us)

commit v12 on v11

--- a/solution.py
+++ b/solution.py
@@ -17,7 +17,7 @@
 VMEM_LIMIT = 60 * 1024 * 1024
 KERNEL_WORK = 8
 ORDER = ((2, 4, 8), (4, 8, 2))
-AHEAD = ((), (), (0,), (1, 0), (2, 1, 0))
+AHEAD = ((), (), (0,), (1, 0), (3, 2, 1, 0))
 
 
 def padded(cells, sides, width):
@@ -424,43 +424,6 @@
     return out[:4], (None if window.last else out[4])
 
 
-def put_kernel(count, place_ref, *refs):
-    parts, out_ref, sem = refs[:4], refs[-2], refs[-1]
-    core, side, along = place_ref[0], place_ref[1], place_ref[2]
-    around = parts[0].shape[1]
-    copies = []
-    for a, part in enumerate(parts):
-        half = core if a < 2 else 1 - core
-        quarter = side if a % 2 == 0 else 1 - side
-        for w in range(count):
-            level, row = place_ref[3 + 4 * w + half], place_ref[5 + 4 * w + half]
-            for n in range(around):
-                piece = lax.rem(along + 1 + n, around)
-                at = multiple(row + (quarter * around + piece) * SUB, SUB)
-                copies.append(pltpu.make_async_copy(part.at[w, n], out_ref.at[level, pl.ds(at, SUB)], sem.at[a, w, n]))
-                copies[-1].start()
-    for copy in copies:
-        copy.wait()
-
-
-def put(out, shape, places, parts):
-    count = parts[0].shape[0]
-    extra = [] if out is None else [out]
-    return pl.pallas_call(
-        functools.partial(put_kernel, count),
-        in_specs=[pl.BlockSpec(memory_space=pltpu.SMEM)]
-        + [pl.BlockSpec(memory_space=pltpu.VMEM)] * 4
-        + [pl.BlockSpec(memory_space=pl.ANY)] * len(extra),
-        out_specs=pl.BlockSpec(memory_space=pl.ANY),
-        out_shape=jax.ShapeDtypeStruct(shape, jnp.float32),
-        input_output_aliases={5: 0} if extra else {},
-        scratch_shapes=[pltpu.SemaphoreType.DMA((4, count, parts[0].shape[1]))],
-        compiler_params=pltpu.CompilerParams(vmem_limit_bytes=VMEM_LIMIT),
-        cost_estimate=pl.CostEstimate(flops=0, transcendentals=0, bytes_accessed=8 * 4 * parts[0].size),
-        name="put",
-    )(places.astype(jnp.int32), *parts, *extra)
-
-
 def by_levels(coeffs):
     spec = coeffs[0]
     levels, _, parts, waves_local, nlat = spec.shape
@@ -511,11 +474,6 @@
         mine = core if step < 0 else half_of[step]
         return jnp.where(mine == 0, jnp.concatenate([part, beside], axis=1), jnp.concatenate([beside, part], axis=1))
 
-    def gathered(part):
-        for step in range(len(ways) - 1, -2, -1):
-            part = doubled(part, step)
-        return part
-
     carry = None
     sums, done = [], []
     for k, window in enumerate(windows):
@@ -525,17 +483,35 @@
             done[j] += 1
             waits.append(left)
         quarters, carry = window_tensor(window, place, local[k], remotes[k], table, waits, carry)
-        first = lax.ppermute(quarters[3], "mem", cores)
+        sent = quarters[3] if k + 1 < count else gated(quarters[3], [sums[k - 2][-1], sums[k - 1][-1]])
+        first = lax.ppermute(sent, "mem", cores)
         second = lax.ppermute(quarters[2], "mem", cores)
         sums.append([quarters[0], quarters[1], second, first])
         done.append(0)
-    pieces = {"own": [], "both": [], "other": []}
-    for k, window in enumerate(windows):
-        for step in range(done[k], len(ways)):
-            sums[k], _ = advanced(sums[k], step)
-        pieces[window.side].append(exponent_of(sum(sums[k]), members))
-
-    other = lax.ppermute(jnp.stack(pieces["other"]), "band", swap)
+    def step(k, waits):
+        gate = 1 if done[k] == 0 else 0
+        sums[k][gate] = gated(sums[k][gate], waits)
+        sums[k], left = advanced(sums[k], done[k])
+        done[k] += 1
+        return left
+
+    def exponents(some, waits):
+        for k in some:
+            sums[k] = [gated(sums[k][0], waits), *sums[k][1:]]
+        return jnp.stack([exponent_of(sum(sums[k]), members) for k in some])
+
+    left = step(2, [quarters[0]])
+    left = step(3, [left])
+    left = step(1, [left])
+    left = step(4, [left])
+    left = step(4, [left])
+    far = exponents([0, 1], [left])
+    swapped = lax.ppermute(far, "band", swap)
+    left = step(2, [far])
+    left = step(3, [left])
+    left = step(4, [left])
+    far = gated(swapped, [left])
+    both = exponents([2], [far])
     place_of = {}
     for m in range(members):
         for b in range(2):
@@ -546,22 +522,29 @@
     for (piece, b), index in place_of.items():
         mate = (piece, b) if (piece < half) == (b == 0) else ((piece + half) % members, 1 - b)
         trades.append((index, place_of[mate]))
-    both = lax.ppermute(pieces["both"][0], ("mem", "band"), trades)
-
-    early = gathered(jnp.concatenate([other, both[None]]))
-    other, both = early[:-1], early[-1]
-    middle = both.shape[0] // 2
-    low, high = both[:middle], both[middle:]
-    rest = jnp.zeros((nlat // 2 - middle, NLON), jnp.float32)
-    down = jnp.stack([jnp.concatenate([rest, low]), jnp.concatenate([*other, high])])
-    up = jnp.stack([jnp.concatenate([low, *other[::-1]]), jnp.concatenate([high, rest])])
+    traded = lax.ppermute(both, ("mem", "band"), trades)
+    near = jnp.concatenate([traded, exponents([3, 4], [both])])
+    for n in (2, 1, 0):
+        far = gated(doubled(far, n), [near])
+        near = gated(doubled(near, n), [far])
+    far, near = doubled(far, -1), doubled(near, -1)
+
+    middle = near.shape[1] // 2
+    rest = jnp.zeros((nlat // 2, NLON), jnp.float32)
+    down = jnp.stack([rest, jnp.concatenate([*far, rest[:middle]])])
+    up = jnp.stack([jnp.concatenate([rest[:middle], *far[::-1]]), rest])
     out = jnp.where(band == 0, down, up)
 
-    own = gathered(jnp.stack(pieces["own"]))
-    for k, block in enumerate(own):
-        width = block.shape[0]
-        row = choose(band, (nlat // 2 - middle - (k + 1) * width, middle + k * width))
-        out = lax.dynamic_update_slice(out, block[None], (band, row.astype(jnp.int32), jnp.int32(0)))
+    def put(block, level, pair):
+        return lax.dynamic_update_slice(
+            out, block[None], (level, choose(band, pair).astype(jnp.int32), jnp.int32(0))
+        )
+
+    edge = nlat // 2 - middle
+    out = put(near[0, :middle], 0, (edge, 0))
+    out = put(near[0, middle:], 1, (edge, 0))
+    for k, block in enumerate(near[1:]):
+        out = put(block, band, (edge - (k + 1) * LANE, middle + k * LANE))
     return out
 
 

time: 184 us -> 195 us (1.060)
  the two profiles are of different devices: /device:TPU:0 before, /device:TPU:3 now
where the time goes in v12:
time: 195 us; the launch traced here: 194 us
  Pallas kernels  61.5 us (32%)
  starting transfers between devices  56.3 us (29%)
  other arithmetic  34.9 us (18%)
  waiting for transfers between devices  33.2 us (17%)
  local copies, waits for them, and re-layouts  8.01 us (4%)
    pallas_call x5, Pallas kernels, window_tensor(): pl.pallas_call(functools.partial(window_kernel, window, depth, len(waits)...  51.2 us
    ppermute x8, starting transfers between devices, doubled(): beside = lax.ppermute(part, 'mem', cores if step < 0 else ways[step])  26.4 us
    add x10, other arithmetic, total(): sum((lax.dynamic_slice_in_dim(part, which * half, half, axis=1) for part...  16.8 us
    ppermute x10, starting transfers between devices, halved(): return ([total(mine), lax.ppermute(leaves, 'mem', ways[step])], leaves)  14 us
    ppermute x5, waiting for transfers between devices, across(): return ([kept, kept_more, lax.ppermute(leaves, 'mem', ways[step])], leaves)  13.8 us
    pallas_call x3, Pallas kernels, pieces_of(): pl.pallas_call(functools.partial(pieces_kernel, windows, slots, count), i...  10.2 us
    ppermute x8, waiting for transfers between devices, doubled(): beside = lax.ppermute(part, 'mem', cores if step < 0 else ways[step])  8.68 us
    select_n x8, other arithmetic, doubled(): jnp.where(mine == 0, jnp.concatenate([part, beside], axis=1), jnp.concate...  7.23 us
  transfers between devices with their start and end apart: 40, of which 10 were waited for; matrix products, arithmetic and copies ran while one was open for 18% of the time, Pallas kernels for 30%

profile of v12, /device:TPU:3, one launch (start us, length us, event | category | flops | bytes accessed | tf_op | source)
XLA Modules:
  0.0 194.5 jit_solution(13156948139548918819)
XLA Ops:
  0.0 2.6 %pieces_of.4 = f32[2,136,640]{2,1,0:T(8,128)} custom-call(s32[1]{0:T(128)} %bitcast.5.level_ref, f32[2,2,640,640]{3,2,1,0:T(8,128)} %bitcast.14), custom_call_target="tpu_custom_call" | custom-call | bytes 5242880 | tf_op jit(solution)/shard_map/pieces_of/pallas_call | solution.py:209
  2.7 3.6 %pieces_of.5 = (f32[2,128,640]{2,1,0:T(8,128)}, f32[2,128,640]{2,1,0:T(8,128)}, f32[2,128,640]{2,1,0:T(8,128)}, f32[2,120,640]{2,1,0:T(8,128)}) custom-call(s32[1]{0:T(128)} %bitcast.5.level_ref, f32[2,2,640,640]{3,2,1,0:T(8,128)} %bitcast.15), custom_call_target="tpu_custom_call" | custom-call | bytes 10485760 | tf_op jit(solution)/shard_map/pieces_of/pallas_call | solution.py:209
  6.3 1.5 collective-permute-start.7
  7.8 4.0 %pieces_of.3 = (f32[2,136,640]{2,1,0:T(8,128)}, f32[2,128,640]{2,1,0:T(8,128)}, f32[2,128,640]{2,1,0:T(8,128)}, f32[2,128,640]{2,1,0:T(8,128)}, f32[2,120,640]{2,1,0:T(8,128)}) custom-call(s32[1]{0:T(128)} %bitcast.level_ref, f32[2,2,640,640]{3,2,1,0:T(8,128)} %bitcast.16), custom_call_target="tpu_custom_call" | custom-call | bytes 13107200 | tf_op jit(solution)/shard_map/pieces_of/pallas_call | solution.py:209
  12.4 6.9 %collective-permute-done.refs_2_.refs_1_ = f32[2,136,640]{2,1,0:T(8,128)S(1)} collective-permute-done((f32[2,136,640]{2,1,0:T(8,128)}, f32[2,136,640]{2,1,0:T(8,128)S(1)}, u32[]{:S(2)}, u32[]{:S(2)}) %collective-permute-start) | collective-permute-done | bytes 696352 | tf_op jit(solution)/shard_map/ppermute | solution.py:444
  20.5 10.5 %window_tensor.5 = (f32[3,32,1280]{2,1,0:T(8,128)}, f32[3,32,1280]{2,1,0:T(8,128)}, f32[3,32,1280]{2,1,0:T(8,128)}, f32[3,32,1280]{2,1,0:T(8,128)}, f32[2,16,1280]{2,1,0:T(8,128)}) custom-call(s32[4]{0:T(128)} %pad_add_fusion.refs_0_, f32[2,136,640]{2,1,0:T(8,128)} %get-tuple-element.38.refs_1_, f32[2,136,640]{2,1,0:T(8,128)} %copy-done.15, ...), custom_call_target="tpu_custom_call" | custom-call | flops 10695475200 | bytes 6635520 | tf_op jit(solution)/shard_map/window_tensor/pallas_call | solution.py:398
  31.1 2.4 %collective-permute-start.2 = (f32[3,32,1280]{2,1,0:T(8,128)}, f32[3,32,1280]{2,1,0:T(8,128)S(1)}, u32[]{:S(2)}, u32[]{:S(2)}) collective-permute-start(f32[3,32,1280]{2,1,0:T(8,128)} %get-tuple-element.42), channel_id=1, source_target_pairs={{0,2},{2,0},{4,6},{6,4},{8,10},{10,8},{12,14},{14,12},{16,18},{18,... | collective-permute-start | bytes 1474568 | tf_op jit(solution)/shard_map/ppermute | solution.py:487
  34.4 10.1 %window_tensor.6 = (f32[3,32,1280]{2,1,0:T(8,128)}, f32[3,32,1280]{2,1,0:T(8,128)}, f32[3,32,1280]{2,1,0:T(8,128)}, f32[3,32,1280]{2,1,0:T(8,128)}, f32[2,16,1280]{2,1,0:T(8,128)}) custom-call(s32[4]{0:T(128)} %pad_add_fusion.refs_0_, f32[2,128,640]{2,1,0:T(8,128)} %get-tuple-element.49.refs_1_, f32[2,128,640]{2,1,0:T(8,128)} %copy-done.17, ...), custom_call_target="tpu_custom_call" | custom-call | flops 10066329600 | bytes 6553600 | tf_op jit(solution)/shard_map/window_tensor/pallas_call | solution.py:398
  44.5 2.6 %collective-permute-start.9 = (f32[3,32,1280]{2,1,0:T(8,128)}, f32[3,32,1280]{2,1,0:T(8,128)S(1)}, u32[]{:S(2)}, u32[]{:S(2)}) collective-permute-start(f32[3,32,1280]{2,1,0:T(8,128)} %get-tuple-element.52), channel_id=1, source_target_pairs={{0,2},{2,0},{4,6},{6,4},{8,10},{10,8},{12,14},{14,12},{16,18},{18,... | collective-permute-start | bytes 1474568 | tf_op jit(solution)/shard_map/ppermute | solution.py:487
  48.8 1.3 collective-permute-start.3
  51.1 10.4 %window_tensor.7 = (f32[3,32,1280]{2,1,0:T(8,128)}, f32[3,32,1280]{2,1,0:T(8,128)}, f32[3,32,1280]{2,1,0:T(8,128)}, f32[3,32,1280]{2,1,0:T(8,128)}, f32[2,16,1280]{2,1,0:T(8,128)}) custom-call(s32[4]{0:T(128)} %pad_add_fusion.refs_0_, f32[2,128,640]{2,1,0:T(8,128)} %get-tuple-element.53.refs_1_, f32[2,128,640]{2,1,0:T(8,128)} %copy-done.16, ...), custom_call_target="tpu_custom_call" | custom-call | flops 10066329600 | bytes 6553600 | tf_op jit(solution)/shard_map/window_tensor/pallas_call | solution.py:398
  61.5 1.2 collective-permute-start.6
  63.7 1.8 dynamic-slice_add_fusion.9
  65.5 10.2 %window_tensor.8 = (f32[3,32,1280]{2,1,0:T(8,128)}, f32[3,32,1280]{2,1,0:T(8,128)}, f32[3,32,1280]{2,1,0:T(8,128)}, f32[3,32,1280]{2,1,0:T(8,128)}, f32[2,16,1280]{2,1,0:T(8,128)}) custom-call(s32[4]{0:T(128)} %pad_add_fusion.refs_0_, f32[2,128,640]{2,1,0:T(8,128)} %get-tuple-element.46.refs_1_, f32[2,128,640]{2,1,0:T(8,128)} %collective-permute-done.8.refs_2_, ...), custom_call_target="tpu_custom_call" | custom-call | flops 10066329600 | bytes 6553600 | tf_op jit(solution)/shard_map/window_tensor/pallas_call | solution.py:398
  75.8 2.4 %collective-permute-start.4 = (f32[3,16,1280]{2,1,0:T(8,128)}, f32[3,16,1280]{2,1,0:T(8,128)}, u32[]{:S(2)}, u32[]{:S(2)}) collective-permute-start(f32[3,16,1280]{2,1,0:T(8,128)} %get-tuple-element.80.refs_5_), channel_id=1, source_target_pairs={{0,8},{2,18},{4,12},{6,22},{8,0},{10,26},{12,4},{14,30},{16,24},{1... | collective-permute-start | bytes 737288 | tf_op jit(solution)/shard_map/ppermute | solution.py:462
  80.3 1.1 add.306.refs_5_
  81.4 3.4 %collective-permute-done.4 = f32[3,16,1280]{2,1,0:T(8,128)} collective-permute-done((f32[3,16,1280]{2,1,0:T(8,128)}, f32[3,16,1280]{2,1,0:T(8,128)}, u32[]{:S(2)}, u32[]{:S(2)}) %collective-permute-start.4) | collective-permute-done | bytes 245792 | tf_op jit(solution)/shard_map/ppermute | solution.py:462
  84.8 2.3 %collective-permute-start.18 = (f32[3,16,1280]{2,1,0:T(8,128)S(1)}, f32[3,16,1280]{2,1,0:T(8,128)}, u32[]{:S(2)}, u32[]{:S(2)}) collective-permute-start(f32[3,16,1280]{2,1,0:T(8,128)S(1)} %get-tuple-element.82.refs_6_), channel_id=1, source_target_pairs={{0,8},{2,18},{4,12},{6,22},{8,0},{10,26},{12,4},{14,30},{16,24},{1... | collective-permute-start | bytes 737288 | tf_op jit(solution)/shard_map/ppermute | solution.py:462
  87.0 1.7 dynamic-slice_add_fusion.19
  88.7 1.3 collective-permute-start.15
  90.0 1.9 add.305.refs_4_
  92.1 10.0 %window_tensor.9 = (f32[3,32,1280]{2,1,0:T(8,128)}, f32[3,32,1280]{2,1,0:T(8,128)}, f32[3,32,1280]{2,1,0:T(8,128)}, f32[3,32,1280]{2,1,0:T(8,128)}) custom-call(s32[4]{0:T(128)} %pad_add_fusion.refs_0_, f32[2,120,640]{2,1,0:T(8,128)} %get-tuple-element.43.refs_1_, f32[2,120,640]{2,1,0:T(8,128)} %collective-permute-done.6.refs_2_, ...), custom_call_target="tpu_custom_call" | custom-call | flops 9437184000 | bytes 6471680 | tf_op jit(solution)/shard_map/window_tensor/pallas_call | solution.py:398
  102.6 1.2 collective-permute-done.17.refs_2_
  104.7 2.0 %dynamic-slice_add_fusion = (f32[3,16,1280]{2,1,0:T(8,128)}, f32[3,16,1280]{2,1,0:T(8,128)}) fusion(f32[3,32,1280]{2,1,0:T(8,128)} %copy-done.10, s32[]{:T(128)S(6)} %select_n.221, f32[3,32,1280]{2,1,0:T(8,128)S(1)} %collective-permute-done.14, f32[3,32,1280]{2,1,0:T(8,128)S(1)} %copy-done.6, s32[]{:T(128)S(6)} %select_n.223), kind=kLoop, calls=%fused_computation.16 | loop fusion | flops 245760 | bytes 1966088 | tf_op jit(solution)/shard_map/add | solution.py:459
  106.7 1.9 dynamic-slice_add_fusion.1
  108.6 1.9 dynamic-slice_add_fusion.17
  110.5 1.1 add.318.refs_1_
  111.6 1.4 collective-permute-start.21
  114.0 2.3 %collective-permute-start.25 = (f32[3,16,1280]{2,1,0:T(8,128)S(1)}, f32[3,16,1280]{2,1,0:T(8,128)S(1)}, u32[]{:S(2)}, u32[]{:S(2)}) collective-permute-start(f32[3,16,1280]{2,1,0:T(8,128)S(1)} %copy-done.11), channel_id=1, source_target_pairs={{0,8},{2,18},{4,12},{6,22},{8,0},{10,26},{12,4},{14,30},{16,24},{1... | collective-permute-start | bytes 737288 | tf_op jit(solution)/shard_map/ppermute | solution.py:462
  117.0 12.6 %collective-permute-done.21 = f32[3,32,1280]{2,1,0:T(8,128)S(1)} collective-permute-done((f32[3,32,1280]{2,1,0:T(8,128)S(1)}, f32[3,32,1280]{2,1,0:T(8,128)S(1)}, u32[]{:S(2)}, u32[]{:S(2)}) %collective-permute-start.21) | collective-permute-done | bytes 491552 | tf_op jit(solution)/shard_map/ppermute | solution.py:467
  129.6 1.8 dynamic-slice_add_fusion.2
  131.5 2.6 %collective-permute-start.27 = (f32[3,16,1280]{2,1,0:T(8,128)S(1)}, f32[3,16,1280]{2,1,0:T(8,128)S(1)}, u32[]{:S(2)}, u32[]{:S(2)}) collective-permute-start(f32[3,16,1280]{2,1,0:T(8,128)S(1)} %get-tuple-element.78.refs_1_), channel_id=1, source_target_pairs={{0,8},{2,18},{4,12},{6,22},{8,0},{10,26},{12,4},{14,30},{16,24},{1... | collective-permute-start | bytes 737288 | tf_op jit(solution)/shard_map/ppermute | solution.py:462
  136.7 1.6 dynamic-slice_add_fusion.12
  138.3 1.4 collective-permute-start.29
  139.7 1.6 dynamic-slice_add_fusion.11
  142.0 1.6 dynamic-slice_add_fusion.10
  151.7 1.8 collective-permute-done.34
  154.6 1.6 collective-permute-done.33
  156.3 1.7 maximum_select_fusion.5.refs_0_
  158.0 7.4 %collective-permute-start.35 = (f32[2,32,1280]{2,1,0:T(8,128)}, f32[2,32,1280]{2,1,0:T(8,128)S(1)}, u32[]{:S(2)}, u32[]{:S(2)}) collective-permute-start(f32[2,32,1280]{2,1,0:T(8,128)} %gated.44.refs_1_), channel_id=1, source_target_pairs={{0,4},{2,10},{4,0},{6,14},{8,12},{10,2},{12,8},{14,6},{16,20},{18,... | collective-permute-start | bytes 983048 | tf_op jit(solution)/shard_map/ppermute | solution.py:473
  165.4 2.0 %collective-permute-done.36 = f32[3,16,1280]{2,1,0:T(8,128)S(1)} collective-permute-done((f32[3,16,1280]{2,1,0:T(8,128)}, f32[3,16,1280]{2,1,0:T(8,128)S(1)}, u32[]{:S(2)}, u32[]{:S(2)}) %collective-permute-start.36) | collective-permute-done | bytes 245792 | tf_op jit(solution)/shard_map/ppermute | solution.py:473
  167.4 1.9 maximum_select_fusion.4.refs_0_
  169.3 1.5 collective-permute-done.35
  171.8 9.3 %collective-permute-start.37 = (f32[2,64,1280]{2,1,0:T(8,128)}, f32[2,64,1280]{2,1,0:T(8,128)S(1)}, u32[]{:S(2)}, u32[]{:S(2)}) collective-permute-start(f32[2,64,1280]{2,1,0:T(8,128)} %gated.46.refs_1_), channel_id=1, source_target_pairs={{0,2},{2,0},{4,6},{6,4},{8,10},{10,8},{12,14},{14,12},{16,18},{18,... | collective-permute-start | bytes 1966088 | tf_op jit(solution)/shard_map/ppermute | solution.py:473
  181.1 1.0 maximum_select_fusion.2.refs_0_
  182.1 7.1 %collective-permute-start.39 = (f32[3,64,1280]{2,1,0:T(8,128)}, f32[3,64,1280]{2,1,0:T(8,128)S(1)}, u32[]{:S(2)}, u32[]{:S(2)}) collective-permute-start(f32[3,64,1280]{2,1,0:T(8,128)} %gated.47), channel_id=1, source_target_pairs={{0,2},{2,0},{4,6},{6,4},{8,10},{10,8},{12,14},{14,12},{16,18},{18,... | collective-permute-start | bytes 2949128 | tf_op jit(solution)/shard_map/ppermute | solution.py:473
  189.9 1.7 collective-permute-done.39
  191.9 1.7 copy-done.4
  (180 shorter events, 26.7 us)
Async XLA Ops:
  2.6 16.8 %collective-permute-start = (f32[2,136,640]{2,1,0:T(8,128)}, f32[2,136,640]{2,1,0:T(8,128)S(1)}, u32[]{:S(2)}, u32[]{:S(2)}) collective-permute-start(f32[2,136,640]{2,1,0:T(8,128)} %pieces_of.4), channel_id=1, source_target_pairs={{0,1},{1,0},{2,3},{3,2},{4,5},{5,4},{6,7},{7,6},{8,9},{9,8},{10,11... | collective-permute-start | bytes 2088968 | tf_op jit(solution)/shard_map/ppermute | solution.py:444
  6.3 27.2 %collective-permute-start.7 = (f32[2,128,640]{2,1,0:T(8,128)}, f32[2,128,640]{2,1,0:T(8,128)S(1)}, u32[]{:S(2)}, u32[]{:S(2)}) collective-permute-start(f32[2,128,640]{2,1,0:T(8,128)} %get-tuple-element.48), channel_id=1, source_target_pairs={{0,1},{1,0},{2,3},{3,2},{4,5},{5,4},{6,7},{7,6},{8,9},{9,8},{10,11... | collective-permute-start | bytes 1966088 | tf_op jit(solution)/shard_map/ppermute | solution.py:448
  20.2 30.0 %collective-permute-start.5 = (f32[2,128,640]{2,1,0:T(8,128)}, f32[2,128,640]{2,1,0:T(8,128)S(1)}, u32[]{:S(2)}, u32[]{:S(2)}) collective-permute-start(f32[2,128,640]{2,1,0:T(8,128)} %gated.24), channel_id=1, source_target_pairs={{0,1},{1,0},{2,3},{3,2},{4,5},{5,4},{6,7},{7,6},{8,9},{9,8},{10,11... | collective-permute-start | bytes 1966088 | tf_op jit(solution)/shard_map/ppermute | solution.py:448
  31.1 16.3 %collective-permute-start.2 = (f32[3,32,1280]{2,1,0:T(8,128)}, f32[3,32,1280]{2,1,0:T(8,128)S(1)}, u32[]{:S(2)}, u32[]{:S(2)}) collective-permute-start(f32[3,32,1280]{2,1,0:T(8,128)} %get-tuple-element.42), channel_id=1, source_target_pairs={{0,2},{2,0},{4,6},{6,4},{8,10},{10,8},{12,14},{14,12},{16,18},{18,... | collective-permute-start | bytes 1474568 | tf_op jit(solution)/shard_map/ppermute | solution.py:487
  44.5 4.3 %collective-permute-start.9 = (f32[3,32,1280]{2,1,0:T(8,128)}, f32[3,32,1280]{2,1,0:T(8,128)S(1)}, u32[]{:S(2)}, u32[]{:S(2)}) collective-permute-start(f32[3,32,1280]{2,1,0:T(8,128)} %get-tuple-element.52), channel_id=1, source_target_pairs={{0,2},{2,0},{4,6},{6,4},{8,10},{10,8},{12,14},{14,12},{16,18},{18,... | collective-permute-start | bytes 1474568 | tf_op jit(solution)/shard_map/ppermute | solution.py:487
  47.1 18.4 %collective-permute-start.8 = (f32[2,128,640]{2,1,0:T(8,128)}, f32[2,128,640]{2,1,0:T(8,128)}, u32[]{:S(2)}, u32[]{:S(2)}) collective-permute-start(f32[2,128,640]{2,1,0:T(8,128)} %gated.26), channel_id=1, source_target_pairs={{0,1},{1,0},{2,3},{3,2},{4,5},{5,4},{6,7},{7,6},{8,9},{9,8},{10,11... | collective-permute-start | bytes 1966088 | tf_op jit(solution)/shard_map/ppermute | solution.py:448
  47.1 14.4 %collective-permute-start.1 = (f32[3,32,1280]{2,1,0:T(8,128)}, f32[3,32,1280]{2,1,0:T(8,128)}, u32[]{:S(2)}, u32[]{:S(2)}) collective-permute-start(f32[3,32,1280]{2,1,0:T(8,128)} %get-tuple-element.40), channel_id=1, source_target_pairs={{0,2},{2,0},{4,6},{6,4},{8,10},{10,8},{12,14},{14,12},{16,18},{18,... | collective-permute-start | bytes 1474568 | tf_op jit(solution)/shard_map/ppermute | solution.py:488
  47.3 28.4 %collective-permute-start.12 = (f32[3,32,1280]{2,1,0:T(8,128)}, f32[3,32,1280]{2,1,0:T(8,128)S(1)}, u32[]{:S(2)}, u32[]{:S(2)}) collective-permute-start(f32[3,32,1280]{2,1,0:T(8,128)} %get-tuple-element.61), channel_id=1, source_target_pairs={{0,2},{2,0},{4,6},{6,4},{8,10},{10,8},{12,14},{14,12},{16,18},{18,... | collective-permute-start | bytes 1474568 | tf_op jit(solution)/shard_map/ppermute | solution.py:488
  48.8 13.9 %collective-permute-start.3 = (f32[3,32,1280]{2,1,0:T(8,128)}, f32[3,32,1280]{2,1,0:T(8,128)S(1)}, u32[]{:S(2)}, u32[]{:S(2)}) collective-permute-start(f32[3,32,1280]{2,1,0:T(8,128)} %add.297.refs_4_), channel_id=1, source_target_pairs={{0,4},{2,10},{4,0},{6,14},{8,12},{10,2},{12,8},{14,6},{16,20},{18,... | collective-permute-start | bytes 1474568 | tf_op jit(solution)/shard_map/ppermute | solution.py:467
  50.2 11.3 %copy-start.25 = (f32[3,32,1280]{2,1,0:T(8,128)}, f32[3,32,1280]{2,1,0:T(8,128)S(1)}, u32[]{:S(2)}) copy-start(f32[3,32,1280]{2,1,0:T(8,128)S(1)} %add.304.refs_4_) | copy-start | bytes 1474564
  50.2 28.0 %collective-permute-start.13 = (f32[3,32,1280]{2,1,0:T(8,128)S(1)}, f32[3,32,1280]{2,1,0:T(8,128)S(1)}, u32[]{:S(2)}, u32[]{:S(2)}) collective-permute-start(f32[3,32,1280]{2,1,0:T(8,128)S(1)} %add.304.refs_4_), channel_id=1, source_target_pairs={{0,4},{2,10},{4,0},{6,14},{8,12},{10,2},{12,8},{14,6},{16,20},{18,... | collective-permute-start | bytes 1474568 | tf_op jit(solution)/shard_map/ppermute | solution.py:467
  61.5 30.4 %collective-permute-start.6 = (f32[2,120,640]{2,1,0:T(8,128)}, f32[2,120,640]{2,1,0:T(8,128)}, u32[]{:S(2)}, u32[]{:S(2)}) collective-permute-start(f32[2,120,640]{2,1,0:T(8,128)} %gated.25), channel_id=1, source_target_pairs={{0,1},{1,0},{2,3},{3,2},{4,5},{5,4},{6,7},{7,6},{8,9},{9,8},{10,11... | collective-permute-start | bytes 1843208 | tf_op jit(solution)/shard_map/ppermute | solution.py:448
  62.7 16.2 %collective-permute-start.11 = (f32[3,32,1280]{2,1,0:T(8,128)}, f32[3,32,1280]{2,1,0:T(8,128)S(1)}, u32[]{:S(2)}, u32[]{:S(2)}) collective-permute-start(f32[3,32,1280]{2,1,0:T(8,128)} %get-tuple-element.59), channel_id=1, source_target_pairs={{0,2},{2,0},{4,6},{6,4},{8,10},{10,8},{12,14},{14,12},{16,18},{18,... | collective-permute-start | bytes 1474568 | tf_op jit(solution)/shard_map/ppermute | solution.py:487
  65.5 12.7 %copy-start.20 = (f32[3,32,1280]{2,1,0:T(8,128)S(1)}, f32[3,32,1280]{2,1,0:T(8,128)}, u32[]{:S(2)}) copy-start(f32[3,32,1280]{2,1,0:T(8,128)} %get-tuple-element.60) | copy-start | bytes 1474564
  75.7 13.0 %collective-permute-start.10 = (f32[3,32,1280]{2,1,0:T(8,128)}, f32[3,32,1280]{2,1,0:T(8,128)}, u32[]{:S(2)}, u32[]{:S(2)}) collective-permute-start(f32[3,32,1280]{2,1,0:T(8,128)} %get-tuple-element.57), channel_id=1, source_target_pairs={{0,2},{2,0},{4,6},{6,4},{8,10},{10,8},{12,14},{14,12},{16,18},{18,... | collective-permute-start | bytes 1474568 | tf_op jit(solution)/shard_map/ppermute | solution.py:487
  75.8 9.0 %collective-permute-start.4 = (f32[3,16,1280]{2,1,0:T(8,128)}, f32[3,16,1280]{2,1,0:T(8,128)}, u32[]{:S(2)}, u32[]{:S(2)}) collective-permute-start(f32[3,16,1280]{2,1,0:T(8,128)} %get-tuple-element.80.refs_5_), channel_id=1, source_target_pairs={{0,8},{2,18},{4,12},{6,22},{8,0},{10,26},{12,4},{14,30},{16,24},{1... | collective-permute-start | bytes 737288 | tf_op jit(solution)/shard_map/ppermute | solution.py:462
  78.2 26.5 %collective-permute-start.14 = (f32[3,32,1280]{2,1,0:T(8,128)}, f32[3,32,1280]{2,1,0:T(8,128)S(1)}, u32[]{:S(2)}, u32[]{:S(2)}) collective-permute-start(f32[3,32,1280]{2,1,0:T(8,128)} %get-tuple-element.67), channel_id=1, source_target_pairs={{0,2},{2,0},{4,6},{6,4},{8,10},{10,8},{12,14},{14,12},{16,18},{18,... | collective-permute-start | bytes 1474568 | tf_op jit(solution)/shard_map/ppermute | solution.py:488
  78.2 11.8 %copy-start.26 = (f32[3,32,1280]{2,1,0:T(8,128)S(1)}, f32[3,32,1280]{2,1,0:T(8,128)}, u32[]{:S(2)}) copy-start(f32[3,32,1280]{2,1,0:T(8,128)} %get-tuple-element.56) | copy-start | bytes 1474564
  79.0 13.1 %copy-start.34 = (f32[3,16,1280]{2,1,0:T(8,128)}, f32[3,16,1280]{2,1,0:T(8,128)S(1)}, u32[]{:S(2)}) copy-start(f32[3,16,1280]{2,1,0:T(8,128)S(1)} %get-tuple-element.82.refs_6_) | copy-start | bytes 737284
  79.8 26.9 %collective-permute-start.16 = (f32[3,32,1280]{2,1,0:T(8,128)}, f32[3,32,1280]{2,1,0:T(8,128)S(1)}, u32[]{:S(2)}, u32[]{:S(2)}) collective-permute-start(f32[3,32,1280]{2,1,0:T(8,128)} %get-tuple-element.68), channel_id=1, source_target_pairs={{0,2},{2,0},{4,6},{6,4},{8,10},{10,8},{12,14},{14,12},{16,18},{18,... | collective-permute-start | bytes 1474568 | tf_op jit(solution)/shard_map/ppermute | solution.py:488
  81.4 10.7 %copy-start.28 = (f32[3,32,1280]{2,1,0:T(8,128)}, f32[3,32,1280]{2,1,0:T(8,128)S(1)}, u32[]{:S(2)}) copy-start(f32[3,32,1280]{2,1,0:T(8,128)S(1)} %add.306.refs_5_) | copy-start | bytes 1474564
  84.8 23.9 %collective-permute-start.18 = (f32[3,16,1280]{2,1,0:T(8,128)S(1)}, f32[3,16,1280]{2,1,0:T(8,128)}, u32[]{:S(2)}, u32[]{:S(2)}) collective-permute-start(f32[3,16,1280]{2,1,0:T(8,128)S(1)} %get-tuple-element.82.refs_6_), channel_id=1, source_target_pairs={{0,8},{2,18},{4,12},{6,22},{8,0},{10,26},{12,4},{14,30},{16,24},{1... | collective-permute-start | bytes 737288 | tf_op jit(solution)/shard_map/ppermute | solution.py:462
  88.7 13.4 %collective-permute-start.15 = (f32[3,32,1280]{2,1,0:T(8,128)S(1)}, f32[3,32,1280]{2,1,0:T(8,128)S(1)}, u32[]{:S(2)}, u32[]{:S(2)}) collective-permute-start(f32[3,32,1280]{2,1,0:T(8,128)S(1)} %add.306.refs_5_), channel_id=1, source_target_pairs={{0,4},{2,10},{4,0},{6,14},{8,12},{10,2},{12,8},{14,6},{16,20},{18,... | collective-permute-start | bytes 1474568 | tf_op jit(solution)/shard_map/ppermute | solution.py:467
  91.9 12.0 %collective-permute-start.17 = (f32[3,32,1280]{2,1,0:T(8,128)}, f32[3,32,1280]{2,1,0:T(8,128)S(1)}, u32[]{:S(2)}, u32[]{:S(2)}) collective-permute-start(f32[3,32,1280]{2,1,0:T(8,128)} %add.305.refs_4_), channel_id=1, source_target_pairs={{0,4},{2,10},{4,0},{6,14},{8,12},{10,2},{12,8},{14,6},{16,20},{18,... | collective-permute-start | bytes 1474568 | tf_op jit(solution)/shard_map/ppermute | solution.py:467
  102.2 14.3 %collective-permute-start.20 = (f32[3,32,1280]{2,1,0:T(8,128)}, f32[3,32,1280]{2,1,0:T(8,128)S(1)}, u32[]{:S(2)}, u32[]{:S(2)}) collective-permute-start(f32[3,32,1280]{2,1,0:T(8,128)} %get-tuple-element.70), channel_id=1, source_target_pairs={{0,2},{2,0},{4,6},{6,4},{8,10},{10,8},{12,14},{14,12},{16,18},{18,... | collective-permute-start | bytes 1474568 | tf_op jit(solution)/shard_map/ppermute | solution.py:488
  104.7 5.8 %collective-permute-start.19 = (f32[3,32,1280]{2,1,0:T(8,128)}, f32[3,32,1280]{2,1,0:T(8,128)S(1)}, u32[]{:S(2)}, u32[]{:S(2)}) collective-permute-start(f32[3,32,1280]{2,1,0:T(8,128)} %gated.31), channel_id=1, source_target_pairs={{0,2},{2,0},{4,6},{6,4},{8,10},{10,8},{12,14},{14,12},{16,18},{18,... | collective-permute-start | bytes 1474568 | tf_op jit(solution)/shard_map/ppermute | solution.py:487
  111.6 18.0 %collective-permute-start.21 = (f32[3,32,1280]{2,1,0:T(8,128)S(1)}, f32[3,32,1280]{2,1,0:T(8,128)S(1)}, u32[]{:S(2)}, u32[]{:S(2)}) collective-permute-start(f32[3,32,1280]{2,1,0:T(8,128)S(1)} %add.318.refs_1_), channel_id=1, source_target_pairs={{0,4},{2,10},{4,0},{6,14},{8,12},{10,2},{12,8},{14,6},{16,20},{18,... | collective-permute-start | bytes 1474568 | tf_op jit(solution)/shard_map/ppermute | solution.py:467
  113.1 22.0 %collective-permute-start.22 = (f32[3,8,1280]{2,1,0:T(8,128)S(1)}, f32[3,8,1280]{2,1,0:T(8,128)S(1)}, u32[]{:S(2)}, u32[]{:S(2)}) collective-permute-start(f32[3,8,1280]{2,1,0:T(8,128)S(1)} %copy-done.35), channel_id=1, source_target_pairs={{0,16},{2,6},{4,20},{6,2},{8,24},{10,14},{12,28},{14,10},{16,0},{1... | collective-permute-start | bytes 368648 | tf_op jit(solution)/shard_map/ppermute | solution.py:462
  114.0 22.6 %collective-permute-start.25 = (f32[3,16,1280]{2,1,0:T(8,128)S(1)}, f32[3,16,1280]{2,1,0:T(8,128)S(1)}, u32[]{:S(2)}, u32[]{:S(2)}) collective-permute-start(f32[3,16,1280]{2,1,0:T(8,128)S(1)} %copy-done.11), channel_id=1, source_target_pairs={{0,8},{2,18},{4,12},{6,22},{8,0},{10,26},{12,4},{14,30},{16,24},{1... | collective-permute-start | bytes 737288 | tf_op jit(solution)/shard_map/ppermute | solution.py:462
  116.4 23.3 %collective-permute-start.26 = (f32[3,16,1280]{2,1,0:T(8,128)S(1)}, f32[3,16,1280]{2,1,0:T(8,128)S(1)}, u32[]{:S(2)}, u32[]{:S(2)}) collective-permute-start(f32[3,16,1280]{2,1,0:T(8,128)S(1)} %copy-done.12), channel_id=1, source_target_pairs={{0,8},{2,18},{4,12},{6,22},{8,0},{10,26},{12,4},{14,30},{16,24},{1... | collective-permute-start | bytes 737288 | tf_op jit(solution)/shard_map/ppermute | solution.py:462
  116.5 17.6 %collective-permute-start.23 = (f32[3,8,1280]{2,1,0:T(8,128)S(1)}, f32[3,8,1280]{2,1,0:T(8,128)S(1)}, u32[]{:S(2)}, u32[]{:S(2)}) collective-permute-start(f32[3,8,1280]{2,1,0:T(8,128)S(1)} %copy-done.29), channel_id=1, source_target_pairs={{0,16},{2,6},{4,20},{6,2},{8,24},{10,14},{12,28},{14,10},{16,0},{1... | collective-permute-start | bytes 368648 | tf_op jit(solution)/shard_map/ppermute | solution.py:462
  131.5 10.5 %collective-permute-start.27 = (f32[3,16,1280]{2,1,0:T(8,128)S(1)}, f32[3,16,1280]{2,1,0:T(8,128)S(1)}, u32[]{:S(2)}, u32[]{:S(2)}) collective-permute-start(f32[3,16,1280]{2,1,0:T(8,128)S(1)} %get-tuple-element.78.refs_1_), channel_id=1, source_target_pairs={{0,8},{2,18},{4,12},{6,22},{8,0},{10,26},{12,4},{14,30},{16,24},{1... | collective-permute-start | bytes 737288 | tf_op jit(solution)/shard_map/ppermute | solution.py:462
  136.1 8.4 %collective-permute-start.24 = (f32[2,8,1280]{2,1,0:T(8,128)S(1)}, f32[2,8,1280]{2,1,0:T(8,128)S(1)}, u32[]{:S(2)}, u32[]{:S(2)}) collective-permute-start(f32[2,8,1280]{2,1,0:T(8,128)S(1)} %pad_maximum_fusion.1.refs_1_), channel_id=1, source_target_pairs={{0,1},{1,0},{2,3},{3,2},{4,5},{5,4},{6,7},{7,6},{8,9},{9,8},{10,11... | collective-permute-start | bytes 245768 | tf_op jit(solution)/shard_map/ppermute | solution.py:509
  138.3 7.4 %collective-permute-start.29 = (f32[3,8,1280]{2,1,0:T(8,128)S(1)}, f32[3,8,1280]{2,1,0:T(8,128)S(1)}, u32[]{:S(2)}, u32[]{:S(2)}) collective-permute-start(f32[3,8,1280]{2,1,0:T(8,128)S(1)} %get-tuple-element.88.refs_1_), channel_id=1, source_target_pairs={{0,16},{2,6},{4,20},{6,2},{8,24},{10,14},{12,28},{14,10},{16,0},{1... | collective-permute-start | bytes 368648 | tf_op jit(solution)/shard_map/ppermute | solution.py:462
  141.3 6.1 %collective-permute-start.31 = (f32[3,8,1280]{2,1,0:T(8,128)S(1)}, f32[3,8,1280]{2,1,0:T(8,128)S(1)}, u32[]{:S(2)}, u32[]{:S(2)}) collective-permute-start(f32[3,8,1280]{2,1,0:T(8,128)S(1)} %get-tuple-element.86.refs_1_), channel_id=1, source_target_pairs={{0,16},{2,6},{4,20},{6,2},{8,24},{10,14},{12,28},{14,10},{16,0},{1... | collective-permute-start | bytes 368648 | tf_op jit(solution)/shard_map/ppermute | solution.py:462
  143.6 4.8 %collective-permute-start.32 = (f32[3,8,1280]{2,1,0:T(8,128)S(1)}, f32[3,8,1280]{2,1,0:T(8,128)S(1)}, u32[]{:S(2)}, u32[]{:S(2)}) collective-permute-start(f32[3,8,1280]{2,1,0:T(8,128)S(1)} %get-tuple-element.90.refs_1_), channel_id=1, source_target_pairs={{0,16},{2,6},{4,20},{6,2},{8,24},{10,14},{12,28},{14,10},{16,0},{1... | collective-permute-start | bytes 368648 | tf_op jit(solution)/shard_map/ppermute | solution.py:462
  145.1 5.2 %collective-permute-start.28 = (f32[2,8,1280]{2,1,0:T(8,128)}, f32[2,8,1280]{2,1,0:T(8,128)S(1)}, u32[]{:S(2)}, u32[]{:S(2)}) collective-permute-start(f32[2,8,1280]{2,1,0:T(8,128)} %gated.38.refs_1_), channel_id=1, source_target_pairs={{0,16},{2,6},{4,20},{6,2},{8,24},{10,14},{12,28},{14,10},{16,0},{1... | collective-permute-start | bytes 245768 | tf_op jit(solution)/shard_map/ppermute | solution.py:473
  146.7 2.7 %collective-permute-start.30 = (f32[1,8,1280]{2,1,0:T(8,128)S(1)}, f32[1,8,1280]{2,1,0:T(8,128)S(1)}, u32[]{:S(2)}, u32[]{:S(2)}) collective-permute-start(f32[1,8,1280]{2,1,0:T(8,128)S(1)} %fusion.17.refs_1_), channel_id=1, source_target_pairs={{0,0},{1,2},{2,1},{3,3},{4,4},{5,10},{6,17},{7,7},{8,8},{9,18},{10... | collective-permute-start | bytes 122888 | tf_op jit(solution)/shard_map/ppermute | solution.py:525
  149.4 4.1 %collective-permute-start.34 = (f32[3,8,1280]{2,1,0:T(8,128)S(1)}, f32[3,8,1280]{2,1,0:T(8,128)S(1)}, u32[]{:S(2)}, u32[]{:S(2)}) collective-permute-start(f32[3,8,1280]{2,1,0:T(8,128)S(1)} %pad_maximum_fusion.refs_1_), channel_id=1, source_target_pairs={{0,16},{2,6},{4,20},{6,2},{8,24},{10,14},{12,28},{14,10},{16,0},{1... | collective-permute-start | bytes 368648 | tf_op jit(solution)/shard_map/ppermute | solution.py:473
  151.0 5.3 %collective-permute-start.33 = (f32[2,16,1280]{2,1,0:T(8,128)}, f32[2,16,1280]{2,1,0:T(8,128)S(1)}, u32[]{:S(2)}, u32[]{:S(2)}) collective-permute-start(f32[2,16,1280]{2,1,0:T(8,128)} %gated.42.refs_1_), channel_id=1, source_target_pairs={{0,8},{2,18},{4,12},{6,22},{8,0},{10,26},{12,4},{14,30},{16,24},{1... | collective-permute-start | bytes 491528 | tf_op jit(solution)/shard_map/ppermute | solution.py:473
  154.2 13.3 %collective-permute-start.36 = (f32[3,16,1280]{2,1,0:T(8,128)}, f32[3,16,1280]{2,1,0:T(8,128)S(1)}, u32[]{:S(2)}, u32[]{:S(2)}) collective-permute-start(f32[3,16,1280]{2,1,0:T(8,128)} %gated.43.refs_1_), channel_id=1, source_target_pairs={{0,8},{2,18},{4,12},{6,22},{8,0},{10,26},{12,4},{14,30},{16,24},{1... | collective-permute-start | bytes 737288 | tf_op jit(solution)/shard_map/ppermute | solution.py:473
  158.0 12.9 %copy-start.3 = (f32[2,32,1280]{2,1,0:T(8,128)S(1)}, f32[2,32,1280]{2,1,0:T(8,128)}, u32[]{:S(2)}) copy-start(f32[2,32,1280]{2,1,0:T(8,128)} %gated.44.refs_1_) | copy-start | bytes 983044
  158.0 12.9 %collective-permute-start.35 = (f32[2,32,1280]{2,1,0:T(8,128)}, f32[2,32,1280]{2,1,0:T(8,128)S(1)}, u32[]{:S(2)}, u32[]{:S(2)}) collective-permute-start(f32[2,32,1280]{2,1,0:T(8,128)} %gated.44.refs_1_), channel_id=1, source_target_pairs={{0,4},{2,10},{4,0},{6,14},{8,12},{10,2},{12,8},{14,6},{16,20},{18,... | collective-permute-start | bytes 983048 | tf_op jit(solution)/shard_map/ppermute | solution.py:473
  169.3 11.7 %copy-start.2 = (f32[3,32,1280]{2,1,0:T(8,128)S(1)}, f32[3,32,1280]{2,1,0:T(8,128)}, u32[]{:S(2)}) copy-start(f32[3,32,1280]{2,1,0:T(8,128)} %gated.45.refs_1_) | copy-start | bytes 1474564
  169.3 11.7 %collective-permute-start.38 = (f32[3,32,1280]{2,1,0:T(8,128)}, f32[3,32,1280]{2,1,0:T(8,128)S(1)}, u32[]{:S(2)}, u32[]{:S(2)}) collective-permute-start(f32[3,32,1280]{2,1,0:T(8,128)} %gated.45.refs_1_), channel_id=1, source_target_pairs={{0,4},{2,10},{4,0},{6,14},{8,12},{10,2},{12,8},{14,6},{16,20},{18,... | collective-permute-start | bytes 1474568 | tf_op jit(solution)/shard_map/ppermute | solution.py:473
  171.8 17.4 %collective-permute-start.37 = (f32[2,64,1280]{2,1,0:T(8,128)}, f32[2,64,1280]{2,1,0:T(8,128)S(1)}, u32[]{:S(2)}, u32[]{:S(2)}) collective-permute-start(f32[2,64,1280]{2,1,0:T(8,128)} %gated.46.refs_1_), channel_id=1, source_target_pairs={{0,2},{2,0},{4,6},{6,4},{8,10},{10,8},{12,14},{14,12},{16,18},{18,... | collective-permute-start | bytes 1966088 | tf_op jit(solution)/shard_map/ppermute | solution.py:473
  181.0 8.1 %copy-start = (f32[2,64,1280]{2,1,0:T(8,128)S(1)}, f32[2,64,1280]{2,1,0:T(8,128)}, u32[]{:S(2)}) copy-start(f32[2,64,1280]{2,1,0:T(8,128)} %gated.46.refs_1_) | copy-start | bytes 1966084
  182.1 9.5 %collective-permute-start.39 = (f32[3,64,1280]{2,1,0:T(8,128)}, f32[3,64,1280]{2,1,0:T(8,128)S(1)}, u32[]{:S(2)}, u32[]{:S(2)}) collective-permute-start(f32[3,64,1280]{2,1,0:T(8,128)} %gated.47), channel_id=1, source_target_pairs={{0,2},{2,0},{4,6},{6,4},{8,10},{10,8},{12,14},{14,12},{16,18},{18,... | collective-permute-start | bytes 2949128 | tf_op jit(solution)/shard_map/ppermute | solution.py:473
  (28 other events, 72.3 us)

commit v13 on v12

--- a/solution.py
+++ b/solution.py
@@ -17,7 +17,7 @@
 VMEM_LIMIT = 60 * 1024 * 1024
 KERNEL_WORK = 8
 ORDER = ((2, 4, 8), (4, 8, 2))
-AHEAD = ((), (), (0,), (1, 0), (3, 2, 1, 0))
+AHEAD = ((), (), (), (0,), (1, 0))
 
 
 def padded(cells, sides, width):
@@ -252,15 +252,15 @@
     return above - below
 
 
-def window_kernel(window, depth, waits, *refs):
+def window_kernel(window, slot, waits, *refs):
     refs = list(refs)
     place_ref, local_ref, remote_ref, table_ref = refs[:4]
-    refs = refs[4 + waits :]
+    refs = refs[4 + waits + (len(PARTS) if slot else 0) :]
     carry_ref = None if window.first else refs.pop(0)
     out_refs = [refs.pop(0) for _ in range(4)]
     carried_ref = None if window.last else refs.pop(0)
-    table, lhs_high, lhs_low, wind, second, third, shift, results, carried, table_sem, out_sems = refs
-    band, core, sides = place_ref[0], place_ref[1], (place_ref[2], place_ref[3])
+    table, lhs_high, lhs_low, wind, second, third, shift, results, carried, table_sem, carry_sem, out_sems = refs
+    band = place_ref[0]
     rows, extended = window.rows, window.extended
 
     def at(pair):
@@ -314,7 +314,7 @@
     if not window.last:
         for c in range(2):
             carried[c] = wind[c, pl.ds(at((0, extended - 2 * SUB)), 2 * SUB), :]
-        carry_on = pltpu.make_async_copy(carried, carried_ref, out_sems.at[4])
+        carry_on = pltpu.make_async_copy(carried, carried_ref, carry_sem)
         carry_on.start()
 
     blocks = extended // SUB
@@ -362,21 +362,37 @@
             out[2, rows_of(block), :] = g_xy * g_xy + g_yy * g_yy
 
     copies = []
-    for n, (a, b) in reversed(list(enumerate(QUARTERS))):
-        side = sides[a]
-        entries(results.at[n], (2 * (core + a - 2 * core * a) + (side + b - 2 * side * b)) * quarter)
-        copies.append(pltpu.make_async_copy(results.at[n], out_refs[n], out_sems.at[n]))
-        copies[-1].start()
+    for n, (a, b) in reversed(list(enumerate(PARTS))):
+        entries(results.at[n], block_of(place_ref, a, b, 0, 0) // 4 * 4)
+        for at_part, (e, f) in enumerate(WITHIN):
+            rows = pl.ds(multiple(block_of(place_ref, a, b, e, f) % 4 * SUB, SUB), SUB)
+            copies.append(
+                pltpu.make_async_copy(
+                    results.at[n, :, rows],
+                    out_refs[n].at[slot, :, pl.ds(at_part * SUB, SUB)],
+                    out_sems.at[n, at_part],
+                )
+            )
+            copies[-1].start()
     for copy in copies:
         copy.wait()
     if not window.last:
         carry_on.wait()
 
 
-QUARTERS = ((0, 0), (0, 1), (1, 0), (1, 1))
-
-
-def window_tensor(window, place, local, remote, table, waits, carry):
+PARTS = ((0, 0), (0, 1), (1, 0), (1, 1))
+WITHIN = ((0, 0), (0, 1), (1, 0), (1, 1))
+
+
+def block_of(place_ref, core, *steps):
+    block = place_ref[1] + core - 2 * core * place_ref[1]
+    for n, differs in enumerate(steps):
+        half = place_ref[2 + 3 * core + n]
+        block = 2 * block + half + differs - 2 * differs * half
+    return block
+
+
+def window_tensor(window, slot, slots, place, local, remote, table, parts, waits, carry):
     depth = local.shape[2]
     vmem = pl.BlockSpec(memory_space=pltpu.VMEM)
     in_specs = [
@@ -387,16 +403,21 @@
     ]
     in_specs += [pl.BlockSpec(memory_space=pl.ANY)] * len(waits)
     operands = [place, local, remote, table, *waits]
+    aliases = {}
+    if slot:
+        aliases = {len(operands) + n: n for n in range(len(PARTS))}
+        in_specs += [pl.BlockSpec(memory_space=pl.ANY)] * len(PARTS)
+        operands += parts
     if not window.first:
         in_specs.append(vmem)
         operands.append(carry)
-    out_shape = [jax.ShapeDtypeStruct((3, window.width // 4, NLON), jnp.float32)] * 4
+    out_shape = [jax.ShapeDtypeStruct((slots, 3, window.width // 4, NLON), jnp.float32)] * len(PARTS)
     if not window.last:
         out_shape.append(jax.ShapeDtypeStruct((2, 2 * SUB, NLON), jnp.float32))
     field = pltpu.VMEM((2, window.extended, NLON), jnp.float32)
     lhs_shape = (2, 2 * window.rows, depth)
     out = pl.pallas_call(
-        functools.partial(window_kernel, window, depth, len(waits)),
+        functools.partial(window_kernel, window, slot, len(waits)),
         out_shape=out_shape,
         in_specs=in_specs,
         out_specs=[pl.BlockSpec(memory_space=pl.ANY)] * len(out_shape),
@@ -411,8 +432,10 @@
             pltpu.VMEM((4, 3, window.width // 4, NLON), jnp.float32),
             pltpu.VMEM((2, 2 * SUB, NLON), jnp.float32),
             pltpu.SemaphoreType.DMA,
-            pltpu.SemaphoreType.DMA((5,)),
+            pltpu.SemaphoreType.DMA,
+            pltpu.SemaphoreType.DMA((len(PARTS), len(WITHIN))),
         ],
+        input_output_aliases=aliases,
         compiler_params=pltpu.CompilerParams(vmem_limit_bytes=VMEM_LIMIT),
         cost_estimate=pl.CostEstimate(
             flops=KERNEL_WORK * 3 * 2 * 2 * window.rows * depth * NLON,
@@ -421,7 +444,60 @@
         ),
         name="window_tensor",
     )(*operands)
-    return out[:4], (None if window.last else out[4])
+    return list(out[: len(PARTS)]), (None if window.last else out[len(PARTS)])
+
+
+def put_kernel(kinds, place_ref, mine_ref, beside_ref, *refs):
+    out_ref, held, in_sems, out_sems = refs[-4:]
+    band, height = place_ref[0], out_ref.shape[1]
+    half = LANE // 2
+    arrivals, departures = [], []
+    for core, ref in enumerate((mine_ref, beside_ref)):
+        for w in range(len(kinds)):
+            arrivals.append(pltpu.make_async_copy(ref.at[w], held.at[core, w], in_sems.at[core, w]))
+            arrivals[-1].start()
+    for core in range(2):
+        for w, (kind, k) in enumerate(kinds):
+            arrivals[core * len(kinds) + w].wait()
+            for n in range(SUB):
+                block = block_of(place_ref, core, n // 4, n // 2 % 2, n % 2)
+                if kind == "other":
+                    level, row = 1 - band, choose(band, (k * LANE, height - (k + 1) * LANE)) + block * SUB
+                elif kind == "both":
+                    level, row = block // SUB, choose(band, (height - half, 0)) + block % SUB * SUB
+                else:
+                    row = choose(band, (height - half - (k + 1) * LANE, half + k * LANE)) + block * SUB
+                    level = band
+                departures.append(
+                    pltpu.make_async_copy(
+                        held.at[core, w, pl.ds(n * SUB, SUB)],
+                        out_ref.at[level, pl.ds(multiple(row, SUB), SUB)],
+                        out_sems.at[core, w, n],
+                    )
+                )
+                departures[-1].start()
+    for copy in departures:
+        copy.wait()
+
+
+def put(out, shape, place, kinds, mine, beside):
+    extra = [] if out is None else [out]
+    hbm = pl.BlockSpec(memory_space=pl.ANY)
+    return pl.pallas_call(
+        functools.partial(put_kernel, kinds),
+        in_specs=[pl.BlockSpec(memory_space=pltpu.SMEM), hbm, hbm] + [hbm] * len(extra),
+        out_specs=hbm,
+        out_shape=jax.ShapeDtypeStruct(shape, jnp.float32),
+        input_output_aliases={3: 0} if extra else {},
+        scratch_shapes=[
+            pltpu.VMEM((2, *mine.shape), jnp.float32),
+            pltpu.SemaphoreType.DMA((2, len(kinds))),
+            pltpu.SemaphoreType.DMA((2, len(kinds), SUB)),
+        ],
+        compiler_params=pltpu.CompilerParams(vmem_limit_bytes=VMEM_LIMIT),
+        cost_estimate=pl.CostEstimate(flops=0, transcendentals=0, bytes_accessed=16 * mine.size),
+        name="put",
+    )(place, mine, beside, *extra)
 
 
 def by_levels(coeffs):
@@ -431,14 +507,15 @@
     band = lax.axis_index("band").astype(jnp.int32)
     member = lax.axis_index("mem").astype(jnp.int32)
     core = member % 2
-    half_of = [choose(core, [member // bits[step] % 2 for bits in ORDER]) for step in range(len(ORDER[0]))]
-    half_beside = choose(1 - core, [member // bits[0] % 2 for bits in ORDER])
-    place = jnp.stack([band, core, half_of[0], half_beside])
+    halves = [[member // bit % 2 for bit in bits] for bits in ORDER]
+    place = jnp.stack([band, core] + [choose(c, pair) for c in (core, 1 - core) for pair in zip(*halves)])
     spec = spec.reshape(levels, 2, parts * waves_local, nlat)
     count = nlat // LANE
     windows = [Window(k, count) for k in range(count)]
     table = jnp.asarray(wave_table(levels, waves_local))
     swap = [(0, 1), (1, 0)]
+    cores = [(m, m ^ 1) for m in range(members)]
+    ways = [[(m, m ^ ORDER[m % 2][step]) for m in range(members)] for step in range(len(ORDER[0]))]
 
     (piece,) = pieces_of(spec, 1 - band, windows[:1], count)
     remotes = [lax.ppermute(piece, "band", swap)]
@@ -448,70 +525,59 @@
         remotes.append(lax.ppermute(piece, "band", swap))
     local = pieces_of(spec, band, windows, count)
 
-    cores = [(m, m ^ 1) for m in range(members)]
-    ways = [[(m, m ^ ORDER[m % 2][step]) for m in range(members)] for step in range(len(ORDER[0]))]
-
-    def halved(parts_of, step):
-        half = parts_of[0].shape[1] // 2
-        mine = half_of[step]
-
-        def total(which):
-            return sum(lax.dynamic_slice_in_dim(part, which * half, half, axis=1) for part in parts_of)
-
-        leaves = total(1 - mine)
-        return [total(mine), lax.ppermute(leaves, "mem", ways[step])], leaves
-
-    def across(parts_of, step):
-        kept, passed, kept_more, passed_more = parts_of
-        leaves = passed + passed_more
-        return [kept, kept_more, lax.ppermute(leaves, "mem", ways[step])], leaves
-
-    def advanced(parts_of, step):
-        return (across if step == 0 else halved)(parts_of, step)
-
-    def doubled(part, step):
-        beside = lax.ppermute(part, "mem", cores if step < 0 else ways[step])
-        mine = core if step < 0 else half_of[step]
-        return jnp.where(mine == 0, jnp.concatenate([part, beside], axis=1), jnp.concatenate([beside, part], axis=1))
+    batches = [(0, 1), (2, 3), (4,)]
+    sums, done = {}, {}
+
+    def step(n, waits=()):
+        terms, at = sums[n], done[n]
+        gate = 1 if at == 0 else 0
+        if waits:
+            terms[gate] = gated(terms[gate], list(waits))
+        if at == 0:
+            kept, passed, kept_more, passed_more = terms
+            kept, leaves = [kept, kept_more], passed + passed_more
+        else:
+            half = terms[0].shape[2] // 2
+            leaves = sum(term[:, :, half:] for term in terms)
+            kept = [sum(term[:, :, :half] for term in terms)]
+        sums[n], done[n] = [*kept, lax.ppermute(leaves, "mem", ways[at])], at + 1
+        return leaves
+
+    def exponents(n, waits):
+        sums[n][0] = gated(sums[n][0], waits)
+        return exponent_of(sum(sums[n]), members)
+
+    def doubled(part, at):
+        return jnp.concatenate([part, lax.ppermute(part, "mem", ways[at])], axis=1)
 
     carry = None
-    sums, done = [], []
-    for k, window in enumerate(windows):
-        waits = []
-        for j in AHEAD[k]:
-            sums[j], left = advanced(sums[j], done[j])
-            done[j] += 1
-            waits.append(left)
-        quarters, carry = window_tensor(window, place, local[k], remotes[k], table, waits, carry)
-        sent = quarters[3] if k + 1 < count else gated(quarters[3], [sums[k - 2][-1], sums[k - 1][-1]])
+    for n, batch in enumerate(batches):
+        made = None
+        for slot, k in enumerate(batch):
+            waits = [step(j) for j in AHEAD[k]]
+            made, carry = window_tensor(
+                windows[k], slot, len(batch), place, local[k], remotes[k], table, made, waits, carry
+            )
+        sent = made[3]
+        if batch[-1] + 1 == count:
+            sent = gated(sent, [sums[n - 1][-1]])
+        elif batch[-1] + 2 == count:
+            sent = gated(sent, [remotes[-1]])
         first = lax.ppermute(sent, "mem", cores)
-        second = lax.ppermute(quarters[2], "mem", cores)
-        sums.append([quarters[0], quarters[1], second, first])
-        done.append(0)
-    def step(k, waits):
-        gate = 1 if done[k] == 0 else 0
-        sums[k][gate] = gated(sums[k][gate], waits)
-        sums[k], left = advanced(sums[k], done[k])
-        done[k] += 1
-        return left
-
-    def exponents(some, waits):
-        for k in some:
-            sums[k] = [gated(sums[k][0], waits), *sums[k][1:]]
-        return jnp.stack([exponent_of(sum(sums[k]), members) for k in some])
-
-    left = step(2, [quarters[0]])
-    left = step(3, [left])
+        second = lax.ppermute(made[2], "mem", cores)
+        sums[n], done[n] = [made[0], made[1], second, first], 0
+        last_made = made[0]
+
+    left = step(0, [last_made])
     left = step(1, [left])
-    left = step(4, [left])
-    left = step(4, [left])
-    far = exponents([0, 1], [left])
+    left = step(2, [left])
+    left = step(2, [left])
+    far = exponents(0, [left])
     swapped = lax.ppermute(far, "band", swap)
-    left = step(2, [far])
-    left = step(3, [left])
-    left = step(4, [left])
+    left = step(1, [far])
+    left = step(2, [left])
     far = gated(swapped, [left])
-    both = exponents([2], [far])
+    near = exponents(1, [far])
     place_of = {}
     for m in range(members):
         for b in range(2):
@@ -522,30 +588,15 @@
     for (piece, b), index in place_of.items():
         mate = (piece, b) if (piece < half) == (b == 0) else ((piece + half) % members, 1 - b)
         trades.append((index, place_of[mate]))
-    traded = lax.ppermute(both, ("mem", "band"), trades)
-    near = jnp.concatenate([traded, exponents([3, 4], [both])])
-    for n in (2, 1, 0):
-        far = gated(doubled(far, n), [near])
-        near = gated(doubled(near, n), [far])
-    far, near = doubled(far, -1), doubled(near, -1)
-
-    middle = near.shape[1] // 2
-    rest = jnp.zeros((nlat // 2, NLON), jnp.float32)
-    down = jnp.stack([rest, jnp.concatenate([*far, rest[:middle]])])
-    up = jnp.stack([jnp.concatenate([rest[:middle], *far[::-1]]), rest])
-    out = jnp.where(band == 0, down, up)
-
-    def put(block, level, pair):
-        return lax.dynamic_update_slice(
-            out, block[None], (level, choose(band, pair).astype(jnp.int32), jnp.int32(0))
-        )
-
-    edge = nlat // 2 - middle
-    out = put(near[0, :middle], 0, (edge, 0))
-    out = put(near[0, middle:], 1, (edge, 0))
-    for k, block in enumerate(near[1:]):
-        out = put(block, band, (edge - (k + 1) * LANE, middle + k * LANE))
-    return out
+    traded = lax.ppermute(near[:1], ("mem", "band"), trades)
+    near = jnp.concatenate([traded, near[1:], exponents(2, [near])])
+    for at in (2, 1, 0):
+        far = gated(doubled(far, at), [near])
+        near = gated(doubled(near, at), [far])
+    shape = (levels, nlat // 2, NLON)
+    out = put(None, shape, place, [("other", 0), ("other", 1)], far, lax.ppermute(far, "mem", cores))
+    kinds = [("both", 0), ("own", 0), ("own", 1)]
+    return put(out, shape, place, kinds, near, lax.ppermute(near, "mem", cores))
 
 
 def per_device(coeffs):

time: 195 us -> 202 us (1.036)
  the two profiles are of different devices: /device:TPU:3 before, /device:TPU:7 now
where the time goes in v13:
time: 202 us; the launch traced here: 201 us
  Pallas kernels  68.3 us (34%)
  waiting for transfers between devices  57.7 us (29%)
  starting transfers between devices  40.6 us (20%)
  other arithmetic  25.6 us (13%)
  local copies, waits for them, and re-layouts  8.35 us (4%)
    pallas_call x5, Pallas kernels, window_tensor(): pl.pallas_call(functools.partial(window_kernel, window, slot, len(waits))...  51.7 us
    ppermute x9, waiting for transfers between devices, step(): sums[n], done[n] = ([*kept, lax.ppermute(leaves, 'mem', ways[at])], at + 1)  28.3 us
    ppermute x6, waiting for transfers between devices, doubled(): return jnp.concatenate([part, lax.ppermute(part, 'mem', ways[at])], axis=1)  12.4 us
    ppermute x9, starting transfers between devices, step(): sums[n], done[n] = ([*kept, lax.ppermute(leaves, 'mem', ways[at])], at + 1)  11.4 us
    add x5, other arithmetic, step(): kept = [sum((term[:, :, :half] for term in terms))]  11.1 us
    ppermute x6, starting transfers between devices, doubled(): return jnp.concatenate([part, lax.ppermute(part, 'mem', ways[at])], axis=1)  10.6 us
    ppermute x1, starting transfers between devices, by_levels(): return put(out, shape, place, kinds, near, lax.ppermute(near, 'mem', cores))  10.2 us
    pallas_call x3, Pallas kernels, pieces_of(): pl.pallas_call(functools.partial(pieces_kernel, windows, slots, count), i...  10.2 us
  transfers between devices with their start and end apart: 30, of which 12 were waited for; matrix products, arithmetic and copies ran while one was open for 13% of the time, Pallas kernels for 31%

profile of v13, /device:TPU:7, one launch (start us, length us, event | category | flops | bytes accessed | tf_op | source)
XLA Modules:
  0.0 201.0 jit_solution(13635513550932838795)
XLA Ops:
  0.0 2.6 %pieces_of.5 = f32[2,136,640]{2,1,0:T(8,128)} custom-call(s32[1]{0:T(128)} %bitcast.9.level_ref, f32[2,2,640,640]{3,2,1,0:T(8,128)} %bitcast.20), custom_call_target="tpu_custom_call" | custom-call | bytes 5242880 | tf_op jit(solution)/shard_map/pieces_of/pallas_call | solution.py:209
  2.9 3.6 %pieces_of.4 = (f32[2,128,640]{2,1,0:T(8,128)}, f32[2,128,640]{2,1,0:T(8,128)}, f32[2,128,640]{2,1,0:T(8,128)}, f32[2,120,640]{2,1,0:T(8,128)}) custom-call(s32[1]{0:T(128)} %bitcast.9.level_ref, f32[2,2,640,640]{3,2,1,0:T(8,128)} %bitcast.21), custom_call_target="tpu_custom_call" | custom-call | bytes 10485760 | tf_op jit(solution)/shard_map/pieces_of/pallas_call | solution.py:209
  6.5 1.3 collective-permute-start
  7.8 4.0 %pieces_of.3 = (f32[2,136,640]{2,1,0:T(8,128)}, f32[2,128,640]{2,1,0:T(8,128)}, f32[2,128,640]{2,1,0:T(8,128)}, f32[2,128,640]{2,1,0:T(8,128)}, f32[2,120,640]{2,1,0:T(8,128)}) custom-call(s32[1]{0:T(128)} %bitcast.level_ref, f32[2,2,640,640]{3,2,1,0:T(8,128)} %bitcast.22), custom_call_target="tpu_custom_call" | custom-call | bytes 13107200 | tf_op jit(solution)/shard_map/pieces_of/pallas_call | solution.py:209
  12.5 6.8 %collective-permute-done.2.refs_2_.refs_1_ = f32[2,136,640]{2,1,0:T(8,128)S(1)} collective-permute-done((f32[2,136,640]{2,1,0:T(8,128)}, f32[2,136,640]{2,1,0:T(8,128)S(1)}, u32[]{:S(2)}, u32[]{:S(2)}) %collective-permute-start.2) | collective-permute-done | bytes 696352 | tf_op jit(solution)/shard_map/ppermute | solution.py:521
  20.4 10.6 %window_tensor.5 = (f32[2,3,32,1280]{3,2,1,0:T(8,128)}, f32[2,3,32,1280]{3,2,1,0:T(8,128)}, f32[2,3,32,1280]{3,2,1,0:T(8,128)}, f32[2,3,32,1280]{3,2,1,0:T(8,128)}, f32[2,16,1280]{2,1,0:T(8,128)}) custom-call(s32[8]{0:T(128)} %stack.35.refs_0_.place_ref, f32[2,136,640]{2,1,0:T(8,128)} %get-tuple-element.42.refs_1_, f32[2,136,640]{2,1,0:T(8,128)} %copy-done.14, ...), custom_call_target="tpu_custom_call" | custom-call | flops 10695475200 | bytes 6635520 | tf_op jit(solution)/shard_map/window_tensor/pallas_call | solution.py:419
  31.0 2.4 %collective-permute-done.refs_1_.refs_2_ = f32[2,128,640]{2,1,0:T(8,128)S(1)} collective-permute-done((f32[2,128,640]{2,1,0:T(8,128)}, f32[2,128,640]{2,1,0:T(8,128)S(1)}, u32[]{:S(2)}, u32[]{:S(2)}) %collective-permute-start) | collective-permute-done | bytes 655392 | tf_op jit(solution)/shard_map/ppermute | solution.py:525
  34.2 10.2 %window_tensor.6 = (f32[2,3,32,1280]{3,2,1,0:T(8,128)}, f32[2,3,32,1280]{3,2,1,0:T(8,128)}, f32[2,3,32,1280]{3,2,1,0:T(8,128)}, f32[2,3,32,1280]{3,2,1,0:T(8,128)}, f32[2,16,1280]{2,1,0:T(8,128)}) custom-call(s32[8]{0:T(128)} %stack.35.refs_0_.place_ref, ...), custom_call_target="tpu_custom_call", output_to_operand_aliasing={{0}: (4, {}), {1}: (5, {}), {2}: (6, {}), {3}: (7, {})} | custom-call | flops 10066329600 | bytes 6553600 | tf_op jit(solution)/shard_map/window_tensor/pallas_call | solution.py:419
  44.5 2.8 %collective-permute-start.3 = (f32[2,3,32,1280]{3,2,1,0:T(8,128)}, f32[2,3,32,1280]{3,2,1,0:T(8,128)S(1)}, u32[]{:S(2)}, u32[]{:S(2)}) collective-permute-start(f32[2,3,32,1280]{3,2,1,0:T(8,128)} %get-tuple-element.49), channel_id=1, source_target_pairs={{0,2},{2,0},{4,6},{6,4},{8,10},{10,8},{12,14},{14,12},{16,18},{18,... | collective-permute-start | bytes 2949128 | tf_op jit(solution)/shard_map/ppermute | solution.py:566
  48.7 1.2 collective-permute-start.7
  49.9 10.3 %window_tensor.7 = (f32[2,3,32,1280]{3,2,1,0:T(8,128)}, f32[2,3,32,1280]{3,2,1,0:T(8,128)}, f32[2,3,32,1280]{3,2,1,0:T(8,128)}, f32[2,3,32,1280]{3,2,1,0:T(8,128)}, f32[2,16,1280]{2,1,0:T(8,128)}) custom-call(s32[8]{0:T(128)} %stack.35.refs_0_.place_ref, f32[2,128,640]{2,1,0:T(8,128)} %get-tuple-element.50.refs_1_, f32[2,128,640]{2,1,0:T(8,128)} %copy-done.15, ...), custom_call_target="tpu_custom_call" | custom-call | flops 10066329600 | bytes 6553600 | tf_op jit(solution)/shard_map/window_tensor/pallas_call | solution.py:419
  60.4 1.4 collective-permute-start.6
  61.7 2.1 %collective-permute-done.1.refs_2_ = f32[2,128,640]{2,1,0:T(8,128)} collective-permute-done((f32[2,128,640]{2,1,0:T(8,128)}, f32[2,128,640]{2,1,0:T(8,128)}, u32[]{:S(2)}, u32[]{:S(2)}) %collective-permute-start.1) | collective-permute-done | bytes 655392 | tf_op jit(solution)/shard_map/ppermute | solution.py:525
  63.8 10.4 %window_tensor.8 = (f32[2,3,32,1280]{3,2,1,0:T(8,128)}, f32[2,3,32,1280]{3,2,1,0:T(8,128)}, f32[2,3,32,1280]{3,2,1,0:T(8,128)}, f32[2,3,32,1280]{3,2,1,0:T(8,128)}, f32[2,16,1280]{2,1,0:T(8,128)}) custom-call(s32[8]{0:T(128)} %stack.35.refs_0_.place_ref, ...), custom_call_target="tpu_custom_call", output_to_operand_aliasing={{0}: (5, {}), {1}: (6, {}), {2}: (7, {}), {3}: (8, {})} | custom-call | flops 10066329600 | bytes 6553600 | tf_op jit(solution)/shard_map/window_tensor/pallas_call | solution.py:419
  74.3 2.7 %collective-permute-done.7.refs_1_.refs_2_ = f32[2,120,640]{2,1,0:T(8,128)} collective-permute-done((f32[2,120,640]{2,1,0:T(8,128)}, f32[2,120,640]{2,1,0:T(8,128)}, u32[]{:S(2)}, u32[]{:S(2)}) %collective-permute-start.7) | collective-permute-done | bytes 614432 | tf_op jit(solution)/shard_map/ppermute | solution.py:525
  77.9 2.4 %slice_add_fusion.6 = (f32[2,3,16,1280]{3,2,1,0:T(8,128)}, f32[2,3,16,1280]{3,2,1,0:T(8,128)S(1)}) fusion(f32[2,3,32,1280]{3,2,1,0:T(8,128)S(1)} %collective-permute-done.6, f32[2,3,32,1280]{3,2,1,0:T(8,128)} %collective-permute-done.5, f32[2,3,32,1280]{3,2,1,0:T(8,128)} %get-tuple-element.59), kind=kLoop, calls=%fused_computation.8 | loop fusion | flops 491520 | bytes 3932160 | tf_op jit(solution)/shard_map/add | solution.py:542
  80.3 2.3 %collective-permute-start.9 = (f32[2,3,16,1280]{3,2,1,0:T(8,128)S(1)}, f32[2,3,16,1280]{3,2,1,0:T(8,128)}, u32[]{:S(2)}, u32[]{:S(2)}) collective-permute-start(f32[2,3,16,1280]{3,2,1,0:T(8,128)S(1)} %get-tuple-element.74.refs_5_), channel_id=1, source_target_pairs={{0,8},{2,18},{4,12},{6,22},{8,0},{10,26},{12,4},{14,30},{16,24},{1... | collective-permute-start | bytes 1474568 | tf_op jit(solution)/shard_map/ppermute | solution.py:543
  82.7 1.4 collective-permute-start.11
  84.1 10.2 %window_tensor.9 = (f32[1,3,32,1280]{3,2,1,0:T(8,128)}, f32[1,3,32,1280]{3,2,1,0:T(8,128)}, f32[1,3,32,1280]{3,2,1,0:T(8,128)}, f32[1,3,32,1280]{3,2,1,0:T(8,128)}) custom-call(s32[8]{0:T(128)} %stack.35.refs_0_.place_ref, f32[2,120,640]{2,1,0:T(8,128)} %get-tuple-element.61.refs_1_, f32[2,120,640]{2,1,0:T(8,128)} %collective-permute-done.7.refs_1_.refs_2_, ...), custom_call_target="tpu_custom_call" | custom-call | flops 9437184000 | bytes 6471680 | tf_op jit(solution)/shard_map/window_tensor/pallas_call | solution.py:419
  94.4 2.2 %slice_add_fusion.14 = (f32[2,3,8,1280]{3,2,1,0:T(8,128)}, f32[2,3,8,1280]{3,2,1,0:T(8,128)}) fusion(f32[2,3,16,1280]{3,2,1,0:T(8,128)} %collective-permute-done.9, f32[2,3,16,1280]{3,2,1,0:T(8,128)} %gated.25), kind=kLoop, calls=%fused_computation.18 | loop fusion | flops 122880 | bytes 1474560 | tf_op jit(solution)/shard_map/add | solution.py:542
  96.6 8.1 %collective-permute-done.11.refs_1_ = f32[2,3,32,1280]{3,2,1,0:T(8,128)S(1)} collective-permute-done((f32[2,3,32,1280]{3,2,1,0:T(8,128)S(1)}, f32[2,3,32,1280]{3,2,1,0:T(8,128)S(1)}, u32[]{:S(2)}, u32[]{:S(2)}) %collective-permute-start.11) | collective-permute-done | bytes 983072 | tf_op jit(solution)/shard_map/ppermute | solution.py:543
  105.6 2.9 %slice_add_fusion.2 = (f32[2,3,16,1280]{3,2,1,0:T(8,128)}, f32[2,3,16,1280]{3,2,1,0:T(8,128)}) fusion(f32[2,3,32,1280]{3,2,1,0:T(8,128)} %copy-done.2, f32[2,3,32,1280]{3,2,1,0:T(8,128)} %collective-permute-done.10, f32[2,3,32,1280]{3,2,1,0:T(8,128)} %gated.26), kind=kLoop, calls=%fused_computation.4 | loop fusion | flops 491520 | bytes 3932160 | tf_op jit(solution)/shard_map/add | solution.py:542
  108.5 1.1 add.190.refs_1_
  109.6 1.4 collective-permute-start.14
  111.3 2.3 %collective-permute-start.16 = (f32[2,3,16,1280]{3,2,1,0:T(8,128)}, f32[2,3,16,1280]{3,2,1,0:T(8,128)S(1)}, u32[]{:S(2)}, u32[]{:S(2)}) collective-permute-start(f32[2,3,16,1280]{3,2,1,0:T(8,128)} %get-tuple-element.72.refs_1_), channel_id=1, source_target_pairs={{0,8},{2,18},{4,12},{6,22},{8,0},{10,26},{12,4},{14,30},{16,24},{1... | collective-permute-start | bytes 1474568 | tf_op jit(solution)/shard_map/ppermute | solution.py:543
  113.6 14.7 %collective-permute-done.14 = f32[1,3,32,1280]{3,2,1,0:T(8,128)S(1)} collective-permute-done((f32[1,3,32,1280]{3,2,1,0:T(8,128)S(1)}, f32[1,3,32,1280]{3,2,1,0:T(8,128)S(1)}, u32[]{:S(2)}, u32[]{:S(2)}) %collective-permute-start.14) | collective-permute-done | bytes 491552 | tf_op jit(solution)/shard_map/ppermute | solution.py:543
  128.2 1.8 slice_add_fusion.9
  130.1 2.4 %collective-permute-start.18 = (f32[1,3,16,1280]{3,2,1,0:T(8,128)S(1)}, f32[1,3,16,1280]{3,2,1,0:T(8,128)S(1)}, u32[]{:S(2)}, u32[]{:S(2)}) collective-permute-start(f32[1,3,16,1280]{3,2,1,0:T(8,128)S(1)} %get-tuple-element.76.refs_1_), channel_id=1, source_target_pairs={{0,8},{2,18},{4,12},{6,22},{8,0},{10,26},{12,4},{14,30},{16,24},{1... | collective-permute-start | bytes 737288 | tf_op jit(solution)/shard_map/ppermute | solution.py:543
  132.5 1.0 add_multiply_fusion.1
  134.1 1.8 slice_add_fusion.11
  136.7 5.6 %collective-permute-done.18 = f32[1,3,16,1280]{3,2,1,0:T(8,128)S(1)} collective-permute-done((f32[1,3,16,1280]{3,2,1,0:T(8,128)S(1)}, f32[1,3,16,1280]{3,2,1,0:T(8,128)S(1)}, u32[]{:S(2)}, u32[]{:S(2)}) %collective-permute-start.18) | collective-permute-done | bytes 245792 | tf_op jit(solution)/shard_map/ppermute | solution.py:543
  142.2 1.6 slice_add_fusion.17
  146.0 1.0 add_multiply_fusion
  150.8 2.4 %collective-permute-done.22 = f32[3,8,1280]{2,1,0:T(8,128)S(1)} collective-permute-done((f32[3,8,1280]{2,1,0:T(8,128)S(1)}, f32[3,8,1280]{2,1,0:T(8,128)S(1)}, u32[]{:S(2)}, u32[]{:S(2)}) %collective-permute-start.22) | collective-permute-done | bytes 122912 | tf_op jit(solution)/shard_map/ppermute | solution.py:551
  154.0 2.4 %collective-permute-done.25 = f32[2,16,1280]{2,1,0:T(8,128)S(1)} collective-permute-done((f32[2,16,1280]{2,1,0:T(8,128)}, f32[2,16,1280]{2,1,0:T(8,128)S(1)}, u32[]{:S(2)}, u32[]{:S(2)}) %collective-permute-start.25) | collective-permute-done | bytes 163872 | tf_op jit(solution)/shard_map/ppermute | solution.py:551
  156.4 1.7 pad_maximum_fusion.3.refs_0_
  158.1 7.2 %collective-permute-start.27 = (f32[2,32,1280]{2,1,0:T(8,128)}, f32[2,32,1280]{2,1,0:T(8,128)S(1)}, u32[]{:S(2)}, u32[]{:S(2)}) collective-permute-start(f32[2,32,1280]{2,1,0:T(8,128)} %gated.38.refs_1_), channel_id=1, source_target_pairs={{0,4},{2,10},{4,0},{6,14},{8,12},{10,2},{12,8},{14,6},{16,20},{18,... | collective-permute-start | bytes 983048 | tf_op jit(solution)/shard_map/ppermute | solution.py:551
  165.3 1.8 pad_maximum_fusion.2.refs_0_
  167.0 1.9 collective-permute-start.26
  168.9 1.5 collective-permute-done.27
  170.4 1.9 pad_maximum_fusion.1.refs_0_
  172.3 6.0 %collective-permute-done.26 = f32[3,32,1280]{2,1,0:T(8,128)S(1)} collective-permute-done((f32[3,32,1280]{2,1,0:T(8,128)}, f32[3,32,1280]{2,1,0:T(8,128)S(1)}, u32[]{:S(2)}, u32[]{:S(2)}) %collective-permute-start.26) | collective-permute-done | bytes 491552 | tf_op jit(solution)/shard_map/ppermute | solution.py:551
  178.3 1.0 pad_maximum_fusion.refs_0_
  179.4 10.2 %collective-permute-start.28 = (f32[3,64,1280]{2,1,0:T(8,128)}, f32[3,64,1280]{2,1,0:T(8,128)S(1)}, u32[]{:S(2)}, u32[]{:S(2)}) collective-permute-start(f32[3,64,1280]{2,1,0:T(8,128)} %gated.41.mine_ref), channel_id=1, source_target_pairs={{0,2},{2,0},{4,6},{6,4},{8,10},{10,8},{12,14},{14,12},{16,18},{18,... | collective-permute-start | bytes 2949128 | tf_op jit(solution)/shard_map/ppermute | solution.py:599
  189.6 3.0 %collective-permute-done.29.beside_ref = f32[2,64,1280]{2,1,0:T(8,128)S(1)} collective-permute-done((f32[2,64,1280]{2,1,0:T(8,128)S(1)}, f32[2,64,1280]{2,1,0:T(8,128)S(1)}, u32[]{:S(2)}, u32[]{:S(2)}) %collective-permute-start.29) | collective-permute-done | bytes 655392 | tf_op jit(solution)/shard_map/ppermute | solution.py:597
  193.4 3.0 %put.2.refs_0_ = f32[2,320,1280]{2,1,0:T(8,128)} custom-call(s32[8]{0:T(128)} %stack.35.refs_0_.place_ref, f32[2,64,1280]{2,1,0:T(8,128)} %gated.40.refs_1_.mine_ref, f32[2,64,1280]{2,1,0:T(8,128)} %copy-done.16), custom_call_target="tpu_custom_call" | custom-call | bytes 2621440 | tf_op jit(solution)/shard_map/put/pallas_call | solution.py:486
  196.4 1.0 copy-done.8
  197.4 3.4 %put.3 = f32[2,320,1280]{2,1,0:T(8,128)} custom-call(s32[8]{0:T(128)} %stack.35.refs_0_.place_ref, f32[3,64,1280]{2,1,0:T(8,128)} %gated.41.mine_ref, f32[3,64,1280]{2,1,0:T(8,128)} %copy-done.8, f32[2,320,1280]{2,1,0:T(8,128)} %put.2.refs_0_), custom_call_target="tpu_custom_call", output_to_operand_aliasing={{}: (3, {})} | custom-call | bytes 3932160 | tf_op jit(solution)/shard_map/put/pallas_call | solution.py:486
  (112 shorter events, 15.7 us)
Async XLA Ops:
  2.6 16.8 %collective-permute-start.2 = (f32[2,136,640]{2,1,0:T(8,128)}, f32[2,136,640]{2,1,0:T(8,128)S(1)}, u32[]{:S(2)}, u32[]{:S(2)}) collective-permute-start(f32[2,136,640]{2,1,0:T(8,128)} %pieces_of.5), channel_id=1, source_target_pairs={{0,1},{1,0},{2,3},{3,2},{4,5},{5,4},{6,7},{7,6},{8,9},{9,8},{10,11... | collective-permute-start | bytes 2088968 | tf_op jit(solution)/shard_map/ppermute | solution.py:521
  6.5 26.8 %collective-permute-start = (f32[2,128,640]{2,1,0:T(8,128)}, f32[2,128,640]{2,1,0:T(8,128)S(1)}, u32[]{:S(2)}, u32[]{:S(2)}) collective-permute-start(f32[2,128,640]{2,1,0:T(8,128)} %get-tuple-element.40), channel_id=1, source_target_pairs={{0,1},{1,0},{2,3},{3,2},{4,5},{5,4},{6,7},{7,6},{8,9},{9,8},{10,11... | collective-permute-start | bytes 1966088 | tf_op jit(solution)/shard_map/ppermute | solution.py:525
  19.3 0.9 copy-start.14
  20.2 27.7 %collective-permute-start.4 = (f32[2,128,640]{2,1,0:T(8,128)}, f32[2,128,640]{2,1,0:T(8,128)S(1)}, u32[]{:S(2)}, u32[]{:S(2)}) collective-permute-start(f32[2,128,640]{2,1,0:T(8,128)} %gated.22), channel_id=1, source_target_pairs={{0,1},{1,0},{2,3},{3,2},{4,5},{5,4},{6,7},{7,6},{8,9},{9,8},{10,11... | collective-permute-start | bytes 1966088 | tf_op jit(solution)/shard_map/ppermute | solution.py:525
  33.4 0.9 copy-start.17
  44.5 15.8 %collective-permute-start.3 = (f32[2,3,32,1280]{3,2,1,0:T(8,128)}, f32[2,3,32,1280]{3,2,1,0:T(8,128)S(1)}, u32[]{:S(2)}, u32[]{:S(2)}) collective-permute-start(f32[2,3,32,1280]{3,2,1,0:T(8,128)} %get-tuple-element.49), channel_id=1, source_target_pairs={{0,2},{2,0},{4,6},{6,4},{8,10},{10,8},{12,14},{14,12},{16,18},{18,... | collective-permute-start | bytes 2949128 | tf_op jit(solution)/shard_map/ppermute | solution.py:566
  47.2 16.6 %collective-permute-start.1 = (f32[2,128,640]{2,1,0:T(8,128)}, f32[2,128,640]{2,1,0:T(8,128)}, u32[]{:S(2)}, u32[]{:S(2)}) collective-permute-start(f32[2,128,640]{2,1,0:T(8,128)} %gated.21), channel_id=1, source_target_pairs={{0,1},{1,0},{2,3},{3,2},{4,5},{5,4},{6,7},{7,6},{8,9},{9,8},{10,11... | collective-permute-start | bytes 1966088 | tf_op jit(solution)/shard_map/ppermute | solution.py:525
  47.5 30.4 %collective-permute-start.5 = (f32[2,3,32,1280]{3,2,1,0:T(8,128)}, f32[2,3,32,1280]{3,2,1,0:T(8,128)}, u32[]{:S(2)}, u32[]{:S(2)}) collective-permute-start(f32[2,3,32,1280]{3,2,1,0:T(8,128)} %get-tuple-element.60), channel_id=1, source_target_pairs={{0,2},{2,0},{4,6},{6,4},{8,10},{10,8},{12,14},{14,12},{16,18},{18,... | collective-permute-start | bytes 2949128 | tf_op jit(solution)/shard_map/ppermute | solution.py:567
  47.8 0.8 copy-start.15
  48.7 28.3 %collective-permute-start.7 = (f32[2,120,640]{2,1,0:T(8,128)}, f32[2,120,640]{2,1,0:T(8,128)}, u32[]{:S(2)}, u32[]{:S(2)}) collective-permute-start(f32[2,120,640]{2,1,0:T(8,128)} %gated.23), channel_id=1, source_target_pairs={{0,1},{1,0},{2,3},{3,2},{4,5},{5,4},{6,7},{7,6},{8,9},{9,8},{10,11... | collective-permute-start | bytes 1843208 | tf_op jit(solution)/shard_map/ppermute | solution.py:525
  49.9 10.4 %copy-start.7 = (f32[2,3,32,1280]{3,2,1,0:T(8,128)S(1)}, f32[2,3,32,1280]{3,2,1,0:T(8,128)}, u32[]{:S(2)}) copy-start(f32[2,3,32,1280]{3,2,1,0:T(8,128)} %get-tuple-element.48) | copy-start | bytes 2949124
  60.4 3.5 %copy-start.4 = (f32[2,3,32,1280]{3,2,1,0:T(8,128)}, f32[2,3,32,1280]{3,2,1,0:T(8,128)S(1)}, u32[]{:S(2)}) copy-start(f32[2,3,32,1280]{3,2,1,0:T(8,128)S(1)} %add.178.refs_4_) | copy-start | bytes 2949124
  60.4 17.5 %collective-permute-start.6 = (f32[2,3,32,1280]{3,2,1,0:T(8,128)S(1)}, f32[2,3,32,1280]{3,2,1,0:T(8,128)S(1)}, u32[]{:S(2)}, u32[]{:S(2)}) collective-permute-start(f32[2,3,32,1280]{3,2,1,0:T(8,128)S(1)} %add.178.refs_4_), channel_id=1, source_target_pairs={{0,4},{2,10},{4,0},{6,14},{8,12},{10,2},{12,8},{14,6},{16,20},{18,... | collective-permute-start | bytes 2949128 | tf_op jit(solution)/shard_map/ppermute | solution.py:543
  74.3 8.3 %copy-start.6 = (f32[2,3,32,1280]{3,2,1,0:T(8,128)S(1)}, f32[2,3,32,1280]{3,2,1,0:T(8,128)}, u32[]{:S(2)}) copy-start(f32[2,3,32,1280]{3,2,1,0:T(8,128)} %get-tuple-element.63) | copy-start | bytes 2949124
  77.0 5.6 %collective-permute-start.8 = (f32[2,3,32,1280]{3,2,1,0:T(8,128)}, f32[2,3,32,1280]{3,2,1,0:T(8,128)S(1)}, u32[]{:S(2)}, u32[]{:S(2)}) collective-permute-start(f32[2,3,32,1280]{3,2,1,0:T(8,128)} %gated.24), channel_id=1, source_target_pairs={{0,2},{2,0},{4,6},{6,4},{8,10},{10,8},{12,14},{14,12},{16,18},{18,... | collective-permute-start | bytes 2949128 | tf_op jit(solution)/shard_map/ppermute | solution.py:566
  77.9 27.8 %collective-permute-start.10 = (f32[2,3,32,1280]{3,2,1,0:T(8,128)}, f32[2,3,32,1280]{3,2,1,0:T(8,128)}, u32[]{:S(2)}, u32[]{:S(2)}) collective-permute-start(f32[2,3,32,1280]{3,2,1,0:T(8,128)} %get-tuple-element.67), channel_id=1, source_target_pairs={{0,2},{2,0},{4,6},{6,4},{8,10},{10,8},{12,14},{14,12},{16,18},{18,... | collective-permute-start | bytes 2949128 | tf_op jit(solution)/shard_map/ppermute | solution.py:567
  80.3 3.8 %copy-start.18 = (f32[2,3,16,1280]{3,2,1,0:T(8,128)}, f32[2,3,16,1280]{3,2,1,0:T(8,128)S(1)}, u32[]{:S(2)}) copy-start(f32[2,3,16,1280]{3,2,1,0:T(8,128)S(1)} %get-tuple-element.74.refs_5_) | copy-start | bytes 1474564
  80.3 14.1 %collective-permute-start.9 = (f32[2,3,16,1280]{3,2,1,0:T(8,128)S(1)}, f32[2,3,16,1280]{3,2,1,0:T(8,128)}, u32[]{:S(2)}, u32[]{:S(2)}) collective-permute-start(f32[2,3,16,1280]{3,2,1,0:T(8,128)S(1)} %get-tuple-element.74.refs_5_), channel_id=1, source_target_pairs={{0,8},{2,18},{4,12},{6,22},{8,0},{10,26},{12,4},{14,30},{16,24},{1... | collective-permute-start | bytes 1474568 | tf_op jit(solution)/shard_map/ppermute | solution.py:543
  82.7 1.4 copy-start.5
  82.7 21.9 %collective-permute-start.11 = (f32[2,3,32,1280]{3,2,1,0:T(8,128)S(1)}, f32[2,3,32,1280]{3,2,1,0:T(8,128)S(1)}, u32[]{:S(2)}, u32[]{:S(2)}) collective-permute-start(f32[2,3,32,1280]{3,2,1,0:T(8,128)S(1)} %add.181.refs_4_), channel_id=1, source_target_pairs={{0,4},{2,10},{4,0},{6,14},{8,12},{10,2},{12,8},{14,6},{16,20},{18,... | collective-permute-start | bytes 2949128 | tf_op jit(solution)/shard_map/ppermute | solution.py:543
  94.3 19.3 %collective-permute-start.13 = (f32[1,3,32,1280]{3,2,1,0:T(8,128)}, f32[1,3,32,1280]{3,2,1,0:T(8,128)S(1)}, u32[]{:S(2)}, u32[]{:S(2)}) collective-permute-start(f32[1,3,32,1280]{3,2,1,0:T(8,128)} %get-tuple-element.70), channel_id=1, source_target_pairs={{0,2},{2,0},{4,6},{6,4},{8,10},{10,8},{12,14},{14,12},{16,18},{18,... | collective-permute-start | bytes 1474568 | tf_op jit(solution)/shard_map/ppermute | solution.py:567
  104.7 0.9 copy-start.2
  105.6 5.5 %copy-start.9 = (f32[2,3,8,1280]{3,2,1,0:T(8,128)S(1)}, f32[2,3,8,1280]{3,2,1,0:T(8,128)}, u32[]{:S(2)}) copy-start(f32[2,3,8,1280]{3,2,1,0:T(8,128)} %get-tuple-element.80.refs_1_) | copy-start | bytes 737284
  105.6 2.9 %collective-permute-start.12 = (f32[1,3,32,1280]{3,2,1,0:T(8,128)}, f32[1,3,32,1280]{3,2,1,0:T(8,128)S(1)}, u32[]{:S(2)}, u32[]{:S(2)}) collective-permute-start(f32[1,3,32,1280]{3,2,1,0:T(8,128)} %gated.28), channel_id=1, source_target_pairs={{0,2},{2,0},{4,6},{6,4},{8,10},{10,8},{12,14},{14,12},{16,18},{18,... | collective-permute-start | bytes 1474568 | tf_op jit(solution)/shard_map/ppermute | solution.py:566
  109.6 3.9 %copy-start.3 = (f32[1,3,32,1280]{3,2,1,0:T(8,128)}, f32[1,3,32,1280]{3,2,1,0:T(8,128)S(1)}, u32[]{:S(2)}) copy-start(f32[1,3,32,1280]{3,2,1,0:T(8,128)S(1)} %add.190.refs_1_) | copy-start | bytes 1474564
  109.6 18.6 %collective-permute-start.14 = (f32[1,3,32,1280]{3,2,1,0:T(8,128)S(1)}, f32[1,3,32,1280]{3,2,1,0:T(8,128)S(1)}, u32[]{:S(2)}, u32[]{:S(2)}) collective-permute-start(f32[1,3,32,1280]{3,2,1,0:T(8,128)S(1)} %add.190.refs_1_), channel_id=1, source_target_pairs={{0,4},{2,10},{4,0},{6,14},{8,12},{10,2},{12,8},{14,6},{16,20},{18,... | collective-permute-start | bytes 1474568 | tf_op jit(solution)/shard_map/ppermute | solution.py:543
  111.1 21.4 %collective-permute-start.15 = (f32[2,3,8,1280]{3,2,1,0:T(8,128)S(1)}, f32[2,3,8,1280]{3,2,1,0:T(8,128)S(1)}, u32[]{:S(2)}, u32[]{:S(2)}) collective-permute-start(f32[2,3,8,1280]{3,2,1,0:T(8,128)S(1)} %copy-done.9), channel_id=1, source_target_pairs={{0,16},{2,6},{4,20},{6,2},{8,24},{10,14},{12,28},{14,10},{16,0},{1... | collective-permute-start | bytes 737288 | tf_op jit(solution)/shard_map/ppermute | solution.py:543
  111.3 22.8 %collective-permute-start.16 = (f32[2,3,16,1280]{3,2,1,0:T(8,128)}, f32[2,3,16,1280]{3,2,1,0:T(8,128)S(1)}, u32[]{:S(2)}, u32[]{:S(2)}) collective-permute-start(f32[2,3,16,1280]{3,2,1,0:T(8,128)} %get-tuple-element.72.refs_1_), channel_id=1, source_target_pairs={{0,8},{2,18},{4,12},{6,22},{8,0},{10,26},{12,4},{14,30},{16,24},{1... | collective-permute-start | bytes 1474568 | tf_op jit(solution)/shard_map/ppermute | solution.py:543
  130.1 2.4 %copy-start.10 = (f32[1,3,16,1280]{3,2,1,0:T(8,128)}, f32[1,3,16,1280]{3,2,1,0:T(8,128)S(1)}, u32[]{:S(2)}) copy-start(f32[1,3,16,1280]{3,2,1,0:T(8,128)S(1)} %get-tuple-element.76.refs_1_) | copy-start | bytes 737284
  130.1 12.2 %collective-permute-start.18 = (f32[1,3,16,1280]{3,2,1,0:T(8,128)S(1)}, f32[1,3,16,1280]{3,2,1,0:T(8,128)S(1)}, u32[]{:S(2)}, u32[]{:S(2)}) collective-permute-start(f32[1,3,16,1280]{3,2,1,0:T(8,128)S(1)} %get-tuple-element.76.refs_1_), channel_id=1, source_target_pairs={{0,8},{2,18},{4,12},{6,22},{8,0},{10,26},{12,4},{14,30},{16,24},{1... | collective-permute-start | bytes 737288 | tf_op jit(solution)/shard_map/ppermute | solution.py:543
  133.5 10.4 %collective-permute-start.17 = (f32[2,8,1280]{2,1,0:T(8,128)S(1)}, f32[2,8,1280]{2,1,0:T(8,128)S(1)}, u32[]{:S(2)}, u32[]{:S(2)}) collective-permute-start(f32[2,8,1280]{2,1,0:T(8,128)S(1)} %fusion.12.refs_1_), channel_id=1, source_target_pairs={{0,1},{1,0},{2,3},{3,2},{4,5},{5,4},{6,7},{7,6},{8,9},{9,8},{10,11... | collective-permute-start | bytes 245768 | tf_op jit(solution)/shard_map/ppermute | solution.py:576
  136.0 10.0 %collective-permute-start.19 = (f32[2,3,8,1280]{3,2,1,0:T(8,128)S(1)}, f32[2,3,8,1280]{3,2,1,0:T(8,128)S(1)}, u32[]{:S(2)}, u32[]{:S(2)}) collective-permute-start(f32[2,3,8,1280]{3,2,1,0:T(8,128)S(1)} %get-tuple-element.78.refs_1_), channel_id=1, source_target_pairs={{0,16},{2,6},{4,20},{6,2},{8,24},{10,14},{12,28},{14,10},{16,0},{1... | collective-permute-start | bytes 737288 | tf_op jit(solution)/shard_map/ppermute | solution.py:543
  143.9 4.5 %collective-permute-start.21 = (f32[1,3,8,1280]{3,2,1,0:T(8,128)S(1)}, f32[1,3,8,1280]{3,2,1,0:T(8,128)S(1)}, u32[]{:S(2)}, u32[]{:S(2)}) collective-permute-start(f32[1,3,8,1280]{3,2,1,0:T(8,128)S(1)} %get-tuple-element.81.refs_1_), channel_id=1, source_target_pairs={{0,16},{2,6},{4,20},{6,2},{8,24},{10,14},{12,28},{14,10},{16,0},{1... | collective-permute-start | bytes 368648 | tf_op jit(solution)/shard_map/ppermute | solution.py:543
  145.2 5.0 %copy-start.13 = (f32[2,8,1280]{2,1,0:T(8,128)S(1)}, f32[2,8,1280]{2,1,0:T(8,128)}, u32[]{:S(2)}) copy-start(f32[2,8,1280]{2,1,0:T(8,128)} %gated.33.refs_1_) | copy-start | bytes 245764
  145.2 5.0 %collective-permute-start.23 = (f32[2,8,1280]{2,1,0:T(8,128)}, f32[2,8,1280]{2,1,0:T(8,128)S(1)}, u32[]{:S(2)}, u32[]{:S(2)}) collective-permute-start(f32[2,8,1280]{2,1,0:T(8,128)} %gated.33.refs_1_), channel_id=1, source_target_pairs={{0,16},{2,6},{4,20},{6,2},{8,24},{10,14},{12,28},{14,10},{16,0},{1... | collective-permute-start | bytes 245768 | tf_op jit(solution)/shard_map/ppermute | solution.py:551
  147.7 1.7 collective-permute-start.20
  149.4 1.4 copy-start.20
  149.4 3.8 %collective-permute-start.22 = (f32[3,8,1280]{2,1,0:T(8,128)S(1)}, f32[3,8,1280]{2,1,0:T(8,128)S(1)}, u32[]{:S(2)}, u32[]{:S(2)}) collective-permute-start(f32[3,8,1280]{2,1,0:T(8,128)S(1)} %pad_maximum_fusion.6.refs_1_), channel_id=1, source_target_pairs={{0,16},{2,6},{4,20},{6,2},{8,24},{10,14},{12,28},{14,10},{16,0},{1... | collective-permute-start | bytes 368648 | tf_op jit(solution)/shard_map/ppermute | solution.py:551
  150.8 5.6 %collective-permute-start.25 = (f32[2,16,1280]{2,1,0:T(8,128)}, f32[2,16,1280]{2,1,0:T(8,128)S(1)}, u32[]{:S(2)}, u32[]{:S(2)}) collective-permute-start(f32[2,16,1280]{2,1,0:T(8,128)} %gated.36.refs_1_), channel_id=1, source_target_pairs={{0,8},{2,18},{4,12},{6,22},{8,0},{10,26},{12,4},{14,30},{16,24},{1... | collective-permute-start | bytes 491528 | tf_op jit(solution)/shard_map/ppermute | solution.py:551
  154.0 11.3 %collective-permute-start.24 = (f32[3,16,1280]{2,1,0:T(8,128)}, f32[3,16,1280]{2,1,0:T(8,128)S(1)}, u32[]{:S(2)}, u32[]{:S(2)}) collective-permute-start(f32[3,16,1280]{2,1,0:T(8,128)} %gated.37.refs_1_), channel_id=1, source_target_pairs={{0,8},{2,18},{4,12},{6,22},{8,0},{10,26},{12,4},{14,30},{16,24},{1... | collective-permute-start | bytes 737288 | tf_op jit(solution)/shard_map/ppermute | solution.py:551
  158.1 12.4 %collective-permute-start.27 = (f32[2,32,1280]{2,1,0:T(8,128)}, f32[2,32,1280]{2,1,0:T(8,128)S(1)}, u32[]{:S(2)}, u32[]{:S(2)}) collective-permute-start(f32[2,32,1280]{2,1,0:T(8,128)} %gated.38.refs_1_), channel_id=1, source_target_pairs={{0,4},{2,10},{4,0},{6,14},{8,12},{10,2},{12,8},{14,6},{16,20},{18,... | collective-permute-start | bytes 983048 | tf_op jit(solution)/shard_map/ppermute | solution.py:551
  167.0 11.3 %copy-start.1 = (f32[3,32,1280]{2,1,0:T(8,128)S(1)}, f32[3,32,1280]{2,1,0:T(8,128)}, u32[]{:S(2)}) copy-start(f32[3,32,1280]{2,1,0:T(8,128)} %gated.39.refs_1_) | copy-start | bytes 1474564
  167.0 11.3 %collective-permute-start.26 = (f32[3,32,1280]{2,1,0:T(8,128)}, f32[3,32,1280]{2,1,0:T(8,128)S(1)}, u32[]{:S(2)}, u32[]{:S(2)}) collective-permute-start(f32[3,32,1280]{2,1,0:T(8,128)} %gated.39.refs_1_), channel_id=1, source_target_pairs={{0,4},{2,10},{4,0},{6,14},{8,12},{10,2},{12,8},{14,6},{16,20},{18,... | collective-permute-start | bytes 1474568 | tf_op jit(solution)/shard_map/ppermute | solution.py:551
  172.3 17.3 %copy-start = (f32[2,64,1280]{2,1,0:T(8,128)S(1)}, f32[2,64,1280]{2,1,0:T(8,128)}, u32[]{:S(2)}) copy-start(f32[2,64,1280]{2,1,0:T(8,128)} %gated.40.refs_1_.mine_ref) | copy-start | bytes 1966084
  179.4 17.0 %collective-permute-start.28 = (f32[3,64,1280]{2,1,0:T(8,128)}, f32[3,64,1280]{2,1,0:T(8,128)S(1)}, u32[]{:S(2)}, u32[]{:S(2)}) collective-permute-start(f32[3,64,1280]{2,1,0:T(8,128)} %gated.41.mine_ref), channel_id=1, source_target_pairs={{0,2},{2,0},{4,6},{6,4},{8,10},{10,8},{12,14},{14,12},{16,18},{18,... | collective-permute-start | bytes 2949128 | tf_op jit(solution)/shard_map/ppermute | solution.py:599
  189.6 3.0 %collective-permute-start.29 = (f32[2,64,1280]{2,1,0:T(8,128)S(1)}, f32[2,64,1280]{2,1,0:T(8,128)S(1)}, u32[]{:S(2)}, u32[]{:S(2)}) collective-permute-start(f32[2,64,1280]{2,1,0:T(8,128)S(1)} %copy-done), channel_id=1, source_target_pairs={{0,2},{2,0},{4,6},{6,4},{8,10},{10,8},{12,14},{14,12},{16,18},{18,... | collective-permute-start | bytes 1966088 | tf_op jit(solution)/shard_map/ppermute | solution.py:597
  192.6 0.8 copy-start.16
  196.4 1.0 copy-start.8
  (4 other events, 2.6 us)

commit v14 on v11

--- a/solution.py
+++ b/solution.py
@@ -17,7 +17,7 @@
 VMEM_LIMIT = 60 * 1024 * 1024
 KERNEL_WORK = 8
 ORDER = ((2, 4, 8), (4, 8, 2))
-AHEAD = ((), (), (0,), (1, 0), (2, 1, 0))
+AHEAD = ((), (), (0,), (1, 0), (3, 2, 1))
 
 
 def padded(cells, sides, width):
@@ -424,43 +424,6 @@
     return out[:4], (None if window.last else out[4])
 
 
-def put_kernel(count, place_ref, *refs):
-    parts, out_ref, sem = refs[:4], refs[-2], refs[-1]
-    core, side, along = place_ref[0], place_ref[1], place_ref[2]
-    around = parts[0].shape[1]
-    copies = []
-    for a, part in enumerate(parts):
-        half = core if a < 2 else 1 - core
-        quarter = side if a % 2 == 0 else 1 - side
-        for w in range(count):
-            level, row = place_ref[3 + 4 * w + half], place_ref[5 + 4 * w + half]
-            for n in range(around):
-                piece = lax.rem(along + 1 + n, around)
-                at = multiple(row + (quarter * around + piece) * SUB, SUB)
-                copies.append(pltpu.make_async_copy(part.at[w, n], out_ref.at[level, pl.ds(at, SUB)], sem.at[a, w, n]))
-                copies[-1].start()
-    for copy in copies:
-        copy.wait()
-
-
-def put(out, shape, places, parts):
-    count = parts[0].shape[0]
-    extra = [] if out is None else [out]
-    return pl.pallas_call(
-        functools.partial(put_kernel, count),
-        in_specs=[pl.BlockSpec(memory_space=pltpu.SMEM)]
-        + [pl.BlockSpec(memory_space=pltpu.VMEM)] * 4
-        + [pl.BlockSpec(memory_space=pl.ANY)] * len(extra),
-        out_specs=pl.BlockSpec(memory_space=pl.ANY),
-        out_shape=jax.ShapeDtypeStruct(shape, jnp.float32),
-        input_output_aliases={5: 0} if extra else {},
-        scratch_shapes=[pltpu.SemaphoreType.DMA((4, count, parts[0].shape[1]))],
-        compiler_params=pltpu.CompilerParams(vmem_limit_bytes=VMEM_LIMIT),
-        cost_estimate=pl.CostEstimate(flops=0, transcendentals=0, bytes_accessed=8 * 4 * parts[0].size),
-        name="put",
-    )(places.astype(jnp.int32), *parts, *extra)
-
-
 def by_levels(coeffs):
     spec = coeffs[0]
     levels, _, parts, waves_local, nlat = spec.shape
@@ -488,7 +451,7 @@
     cores = [(m, m ^ 1) for m in range(members)]
     ways = [[(m, m ^ ORDER[m % 2][step]) for m in range(members)] for step in range(len(ORDER[0]))]
 
-    def halved(parts_of, step):
+    def halved(parts_of, step, waits=()):
         half = parts_of[0].shape[1] // 2
         mine = half_of[step]
 
@@ -496,6 +459,8 @@
             return sum(lax.dynamic_slice_in_dim(part, which * half, half, axis=1) for part in parts_of)
 
         leaves = total(1 - mine)
+        if waits:
+            leaves = gated(leaves, list(waits))
         return [total(mine), lax.ppermute(leaves, "mem", ways[step])], leaves
 
     def across(parts_of, step):
@@ -525,17 +490,40 @@
             done[j] += 1
             waits.append(left)
         quarters, carry = window_tensor(window, place, local[k], remotes[k], table, waits, carry)
-        first = lax.ppermute(quarters[3], "mem", cores)
+        sent = quarters[3] if k + 1 < count else gated(quarters[3], [sums[k - 1][-1]])
+        first = lax.ppermute(sent, "mem", cores)
         second = lax.ppermute(quarters[2], "mem", cores)
         sums.append([quarters[0], quarters[1], second, first])
         done.append(0)
-    pieces = {"own": [], "both": [], "other": []}
-    for k, window in enumerate(windows):
-        for step in range(done[k], len(ways)):
-            sums[k], _ = advanced(sums[k], step)
-        pieces[window.side].append(exponent_of(sum(sums[k]), members))
-
-    other = lax.ppermute(jnp.stack(pieces["other"]), "band", swap)
+    def further(k, until, waits=()):
+        while done[k] < until:
+            last = done[k] + 1 == until
+            if done[k] == 0:
+                sums[k], _ = across(sums[k], 0)
+            else:
+                sums[k], _ = halved(sums[k], done[k], waits if last else ())
+            done[k] += 1
+
+    def exponent(k):
+        return exponent_of(sum(sums[k]), members)
+
+    further(0, 3, [first])
+    further(1, 3, [first])
+    further(2, 2, [first])
+    further(4, 1)
+    over = [sums[4][-1]]
+    further(2, 3, over)
+    further(4, 2)
+    over_two = [sums[4][-1]]
+    further(3, 3, over_two)
+    further(4, 3)
+    pieces = {
+        "other": gated(jnp.stack([exponent(0), exponent(1)]), over),
+        "both": exponent(2),
+        "own": jnp.stack([exponent(3), exponent(4)]),
+    }
+
+    other = lax.ppermute(pieces["other"], "band", swap)
     place_of = {}
     for m in range(members):
         for b in range(2):
@@ -546,9 +534,9 @@
     for (piece, b), index in place_of.items():
         mate = (piece, b) if (piece < half) == (b == 0) else ((piece + half) % members, 1 - b)
         trades.append((index, place_of[mate]))
-    both = lax.ppermute(pieces["both"][0], ("mem", "band"), trades)
-
-    early = gathered(jnp.concatenate([other, both[None]]))
+    both = lax.ppermute(pieces["both"], ("mem", "band"), trades)
+
+    early = gathered(gated(jnp.concatenate([other, both[None]]), over_two))
     other, both = early[:-1], early[-1]
     middle = both.shape[0] // 2
     low, high = both[:middle], both[middle:]
@@ -557,7 +545,7 @@
     up = jnp.stack([jnp.concatenate([low, *other[::-1]]), jnp.concatenate([high, rest])])
     out = jnp.where(band == 0, down, up)
 
-    own = gathered(jnp.stack(pieces["own"]))
+    own = gathered(pieces["own"])
     for k, block in enumerate(own):
         width = block.shape[0]
         row = choose(band, (nlat // 2 - middle - (k + 1) * width, middle + k * width))

time: 184 us -> 204 us (1.11)
  the two profiles are of different devices: /device:TPU:0 before, /device:TPU:3 now
where the time goes in v14:
time: 204 us; the launch traced here: 203 us
  Pallas kernels  61.4 us (30%)
  waiting for transfers between devices  61.3 us (30%)
  starting transfers between devices  47.4 us (23%)
  other arithmetic  24.1 us (12%)
  local copies, waits for them, and re-layouts  8.2 us (4%)
    pallas_call x5, Pallas kernels, window_tensor(): pl.pallas_call(functools.partial(window_kernel, window, depth, len(waits)...  51.2 us
    ppermute x8, waiting for transfers between devices, doubled(): beside = lax.ppermute(part, 'mem', cores if step < 0 else ways[step])  26.1 us
    ppermute x8, starting transfers between devices, doubled(): beside = lax.ppermute(part, 'mem', cores if step < 0 else ways[step])  20.1 us
    ppermute x10, waiting for transfers between devices, halved(): return ([total(mine), lax.ppermute(leaves, 'mem', ways[step])], leaves)  18.2 us
    add x10, other arithmetic, total(): sum((lax.dynamic_slice_in_dim(part, which * half, half, axis=1) for part...  14 us
    pallas_call x3, Pallas kernels, pieces_of(): pl.pallas_call(functools.partial(pieces_kernel, windows, slots, count), i...  10.2 us
    ppermute x5, waiting for transfers between devices, across(): return ([kept, kept_more, lax.ppermute(leaves, 'mem', ways[step])], leaves)  9.63 us
    ppermute x10, starting transfers between devices, halved(): return ([total(mine), lax.ppermute(leaves, 'mem', ways[step])], leaves)  9.47 us
  transfers between devices with their start and end apart: 40, of which 13 were waited for; matrix products, arithmetic and copies ran while one was open for 11% of the time, Pallas kernels for 29%

profile of v14, /device:TPU:3, one launch (start us, length us, event | category | flops | bytes accessed | tf_op | source)
XLA Modules:
  0.0 202.9 jit_solution(10962169470115123381)
XLA Ops:
  0.0 2.6 %pieces_of.4 = f32[2,136,640]{2,1,0:T(8,128)} custom-call(s32[1]{0:T(128)} %bitcast.5.level_ref, f32[2,2,640,640]{3,2,1,0:T(8,128)} %bitcast.25), custom_call_target="tpu_custom_call" | custom-call | bytes 5242880 | tf_op jit(solution)/shard_map/pieces_of/pallas_call | solution.py:209
  2.7 3.6 %pieces_of.5 = (f32[2,128,640]{2,1,0:T(8,128)}, f32[2,128,640]{2,1,0:T(8,128)}, f32[2,128,640]{2,1,0:T(8,128)}, f32[2,120,640]{2,1,0:T(8,128)}) custom-call(s32[1]{0:T(128)} %bitcast.5.level_ref, f32[2,2,640,640]{3,2,1,0:T(8,128)} %bitcast.26), custom_call_target="tpu_custom_call" | custom-call | bytes 10485760 | tf_op jit(solution)/shard_map/pieces_of/pallas_call | solution.py:209
  6.3 1.5 collective-permute-start.7
  7.8 4.0 %pieces_of.3 = (f32[2,136,640]{2,1,0:T(8,128)}, f32[2,128,640]{2,1,0:T(8,128)}, f32[2,128,640]{2,1,0:T(8,128)}, f32[2,128,640]{2,1,0:T(8,128)}, f32[2,120,640]{2,1,0:T(8,128)}) custom-call(s32[1]{0:T(128)} %bitcast.level_ref, f32[2,2,640,640]{3,2,1,0:T(8,128)} %bitcast.27), custom_call_target="tpu_custom_call" | custom-call | bytes 13107200 | tf_op jit(solution)/shard_map/pieces_of/pallas_call | solution.py:209
  12.4 7.0 %collective-permute-done.refs_2_.refs_1_ = f32[2,136,640]{2,1,0:T(8,128)S(1)} collective-permute-done((f32[2,136,640]{2,1,0:T(8,128)}, f32[2,136,640]{2,1,0:T(8,128)S(1)}, u32[]{:S(2)}, u32[]{:S(2)}) %collective-permute-start) | collective-permute-done | bytes 696352 | tf_op jit(solution)/shard_map/ppermute | solution.py:444
  20.2 10.5 %window_tensor.5 = (f32[3,32,1280]{2,1,0:T(8,128)}, f32[3,32,1280]{2,1,0:T(8,128)}, f32[3,32,1280]{2,1,0:T(8,128)}, f32[3,32,1280]{2,1,0:T(8,128)}, f32[2,16,1280]{2,1,0:T(8,128)}) custom-call(s32[4]{0:T(128)} %pad_add_fusion.refs_0_, f32[2,136,640]{2,1,0:T(8,128)} %get-tuple-element.38.refs_1_, f32[2,136,640]{2,1,0:T(8,128)} %copy-done.8, ...), custom_call_target="tpu_custom_call" | custom-call | flops 10695475200 | bytes 6635520 | tf_op jit(solution)/shard_map/window_tensor/pallas_call | solution.py:398
  30.7 2.8 %collective-permute-start.2 = (f32[3,32,1280]{2,1,0:T(8,128)}, f32[3,32,1280]{2,1,0:T(8,128)S(1)}, u32[]{:S(2)}, u32[]{:S(2)}) collective-permute-start(f32[3,32,1280]{2,1,0:T(8,128)} %get-tuple-element.42), channel_id=1, source_target_pairs={{0,2},{2,0},{4,6},{6,4},{8,10},{10,8},{12,14},{14,12},{16,18},{18,... | collective-permute-start | bytes 1474568 | tf_op jit(solution)/shard_map/ppermute | solution.py:494
  34.3 10.1 %window_tensor.6 = (f32[3,32,1280]{2,1,0:T(8,128)}, f32[3,32,1280]{2,1,0:T(8,128)}, f32[3,32,1280]{2,1,0:T(8,128)}, f32[3,32,1280]{2,1,0:T(8,128)}, f32[2,16,1280]{2,1,0:T(8,128)}) custom-call(s32[4]{0:T(128)} %pad_add_fusion.refs_0_, f32[2,128,640]{2,1,0:T(8,128)} %get-tuple-element.49.refs_1_, f32[2,128,640]{2,1,0:T(8,128)} %copy-done.10, ...), custom_call_target="tpu_custom_call" | custom-call | flops 10066329600 | bytes 6553600 | tf_op jit(solution)/shard_map/window_tensor/pallas_call | solution.py:398
  44.5 1.5 collective-permute-start.9
  47.7 1.3 collective-permute-start.3
  50.0 1.3 collective-permute-start.13
  51.3 10.3 %window_tensor.7 = (f32[3,32,1280]{2,1,0:T(8,128)}, f32[3,32,1280]{2,1,0:T(8,128)}, f32[3,32,1280]{2,1,0:T(8,128)}, f32[3,32,1280]{2,1,0:T(8,128)}, f32[2,16,1280]{2,1,0:T(8,128)}) custom-call(s32[4]{0:T(128)} %pad_add_fusion.refs_0_, f32[2,128,640]{2,1,0:T(8,128)} %get-tuple-element.53.refs_1_, f32[2,128,640]{2,1,0:T(8,128)} %copy-done.9, ...), custom_call_target="tpu_custom_call" | custom-call | flops 10066329600 | bytes 6553600 | tf_op jit(solution)/shard_map/window_tensor/pallas_call | solution.py:398
  61.6 1.6 collective-permute-start.11
  63.5 1.8 dynamic-slice_add_fusion.9
  65.4 10.2 %window_tensor.8 = (f32[3,32,1280]{2,1,0:T(8,128)}, f32[3,32,1280]{2,1,0:T(8,128)}, f32[3,32,1280]{2,1,0:T(8,128)}, f32[3,32,1280]{2,1,0:T(8,128)}, f32[2,16,1280]{2,1,0:T(8,128)}) custom-call(s32[4]{0:T(128)} %pad_add_fusion.refs_0_, f32[2,128,640]{2,1,0:T(8,128)} %get-tuple-element.46.refs_1_, f32[2,128,640]{2,1,0:T(8,128)} %collective-permute-done.8.refs_2_, ...), custom_call_target="tpu_custom_call" | custom-call | flops 10066329600 | bytes 6553600 | tf_op jit(solution)/shard_map/window_tensor/pallas_call | solution.py:398
  76.4 2.3 %collective-permute-start.4 = (f32[3,16,1280]{2,1,0:T(8,128)}, f32[3,16,1280]{2,1,0:T(8,128)}, u32[]{:S(2)}, u32[]{:S(2)}) collective-permute-start(f32[3,16,1280]{2,1,0:T(8,128)} %get-tuple-element.80.refs_5_), channel_id=1, source_target_pairs={{0,8},{2,18},{4,12},{6,22},{8,0},{10,26},{12,4},{14,30},{16,24},{1... | collective-permute-start | bytes 737288 | tf_op jit(solution)/shard_map/ppermute | solution.py:464
  80.4 1.3 collective-permute-start.22
  82.6 10.1 %window_tensor.9 = (f32[3,32,1280]{2,1,0:T(8,128)}, f32[3,32,1280]{2,1,0:T(8,128)}, f32[3,32,1280]{2,1,0:T(8,128)}, f32[3,32,1280]{2,1,0:T(8,128)}) custom-call(s32[4]{0:T(128)} %pad_add_fusion.refs_0_, f32[2,120,640]{2,1,0:T(8,128)} %get-tuple-element.43.refs_1_, f32[2,120,640]{2,1,0:T(8,128)} %collective-permute-done.6.refs_2_, ...), custom_call_target="tpu_custom_call" | custom-call | flops 9437184000 | bytes 6471680 | tf_op jit(solution)/shard_map/window_tensor/pallas_call | solution.py:398
  92.7 8.3 %collective-permute-done.14.refs_1_ = f32[3,32,1280]{2,1,0:T(8,128)S(1)} collective-permute-done((f32[3,32,1280]{2,1,0:T(8,128)S(1)}, f32[3,32,1280]{2,1,0:T(8,128)S(1)}, u32[]{:S(2)}, u32[]{:S(2)}) %collective-permute-start.14) | collective-permute-done | bytes 491552 | tf_op jit(solution)/shard_map/ppermute | solution.py:469
  101.9 1.6 dynamic-slice_add_fusion.14.refs_0_
  103.5 1.6 dynamic-slice_add_fusion.13.refs_0_
  105.6 2.1 %dynamic-slice_add_fusion.5 = (f32[3,16,1280]{2,1,0:T(8,128)S(1)}, f32[3,16,1280]{2,1,0:T(8,128)}) fusion(f32[3,32,1280]{2,1,0:T(8,128)} %collective-permute-done.22, s32[]{:T(128)S(6)} %select_n.215, f32[3,32,1280]{2,1,0:T(8,128)} %collective-permute-done.21, f32[3,32,1280]{2,1,0:T(8,128)S(1)} %copy-done.12, s32[]{:T(128)S(6)} %select_n.217), kind=kLoop, calls=%fused_computation.23 | loop fusion | flops 245760 | bytes 1966088 | tf_op jit(solution)/shard_map/add | solution.py:459
  109.1 1.8 dynamic-slice_add_fusion.2
  110.9 1.7 collective-permute-start.33
  112.7 2.0 collective-permute-start.19
  115.6 1.0 add_multiply_fusion.4
  116.7 3.3 %collective-permute-done.18 = f32[3,8,1280]{2,1,0:T(8,128)} collective-permute-done((f32[3,8,1280]{2,1,0:T(8,128)}, f32[3,8,1280]{2,1,0:T(8,128)}, u32[]{:S(2)}, u32[]{:S(2)}) %collective-permute-start.18) | collective-permute-done | bytes 122912 | tf_op jit(solution)/shard_map/ppermute | solution.py:464
  120.0 1.0 add_multiply_fusion.3
  121.7 8.9 %collective-permute-done.23 = f32[3,16,1280]{2,1,0:T(8,128)S(1)} collective-permute-done((f32[3,16,1280]{2,1,0:T(8,128)}, f32[3,16,1280]{2,1,0:T(8,128)S(1)}, u32[]{:S(2)}, u32[]{:S(2)}) %collective-permute-start.23) | collective-permute-done | bytes 245792 | tf_op jit(solution)/shard_map/ppermute | solution.py:464
  131.2 1.3 collective-permute-done.19.refs_1_
  133.8 1.1 dynamic-slice_add_fusion
  135.0 1.9 collective-permute-start.27
  138.8 1.6 dynamic-slice_add_fusion.11.refs_0_
  141.3 5.0 %collective-permute-done.27.refs_1_ = f32[3,16,1280]{2,1,0:T(8,128)S(1)} collective-permute-done((f32[3,16,1280]{2,1,0:T(8,128)S(1)}, f32[3,16,1280]{2,1,0:T(8,128)S(1)}, u32[]{:S(2)}, u32[]{:S(2)}) %collective-permute-start.27) | collective-permute-done | bytes 245792 | tf_op jit(solution)/shard_map/ppermute | solution.py:464
  148.5 1.0 collective-permute-start.35
  150.0 1.0 collective-permute-done.34
  151.0 0.9 add_multiply_fusion.1
  151.9 1.7 collective-permute-done.28
  153.6 1.0 maximum_select_fusion.7
  154.8 1.4 collective-permute-start.36
  156.2 13.4 %collective-permute-done.29 = f32[3,16,1280]{2,1,0:T(8,128)S(1)} collective-permute-done((f32[3,16,1280]{2,1,0:T(8,128)S(1)}, f32[3,16,1280]{2,1,0:T(8,128)S(1)}, u32[]{:S(2)}, u32[]{:S(2)}) %collective-permute-start.29) | collective-permute-done | bytes 245792 | tf_op jit(solution)/shard_map/ppermute | solution.py:475
  169.8 1.7 collective-permute-start.37
  171.5 9.3 %collective-permute-done.37 = f32[2,16,1280]{2,1,0:T(8,128)S(1)} collective-permute-done((f32[2,16,1280]{2,1,0:T(8,128)S(1)}, f32[2,16,1280]{2,1,0:T(8,128)S(1)}, u32[]{:S(2)}, u32[]{:S(2)}) %collective-permute-start.37) | collective-permute-done | bytes 163872 | tf_op jit(solution)/shard_map/ppermute | solution.py:475
  180.8 2.2 %collective-permute-start.38 = (f32[2,32,1280]{2,1,0:T(8,128)S(1)}, f32[2,32,1280]{2,1,0:T(8,128)S(1)}, u32[]{:S(2)}, u32[]{:S(2)}) collective-permute-start(f32[2,32,1280]{2,1,0:T(8,128)S(1)} %maximum_select_fusion.6), channel_id=1, source_target_pairs={{0,4},{2,10},{4,0},{6,14},{8,12},{10,2},{12,8},{14,6},{16,20},{18,... | collective-permute-start | bytes 983048 | tf_op jit(solution)/shard_map/ppermute | solution.py:475
  183.1 8.0 %collective-permute-start.31 = (f32[3,64,1280]{2,1,0:T(8,128)S(1)}, f32[3,64,1280]{2,1,0:T(8,128)S(1)}, u32[]{:S(2)}, u32[]{:S(2)}) collective-permute-start(f32[3,64,1280]{2,1,0:T(8,128)S(1)} %maximum_select_fusion.3), channel_id=1, source_target_pairs={{0,2},{2,0},{4,6},{6,4},{8,10},{10,8},{12,14},{14,12},{16,18},{18,... | collective-permute-start | bytes 2949128 | tf_op jit(solution)/shard_map/ppermute | solution.py:475
  191.1 6.0 %collective-permute-start.39 = (f32[2,64,1280]{2,1,0:T(8,128)S(1)}, f32[2,64,1280]{2,1,0:T(8,128)S(1)}, u32[]{:S(2)}, u32[]{:S(2)}) collective-permute-start(f32[2,64,1280]{2,1,0:T(8,128)S(1)} %maximum_select_fusion.4), channel_id=1, source_target_pairs={{0,2},{2,0},{4,6},{6,4},{8,10},{10,8},{12,14},{14,12},{16,18},{18,... | collective-permute-start | bytes 1966088 | tf_op jit(solution)/shard_map/ppermute | solution.py:475
  197.2 1.7 collective-permute-done.39
  200.3 1.7 copy-done.3
  (138 shorter events, 23.3 us)
Async XLA Ops:
  2.6 16.8 %collective-permute-start = (f32[2,136,640]{2,1,0:T(8,128)}, f32[2,136,640]{2,1,0:T(8,128)S(1)}, u32[]{:S(2)}, u32[]{:S(2)}) collective-permute-start(f32[2,136,640]{2,1,0:T(8,128)} %pieces_of.4), channel_id=1, source_target_pairs={{0,1},{1,0},{2,3},{3,2},{4,5},{5,4},{6,7},{7,6},{8,9},{9,8},{10,11... | collective-permute-start | bytes 2088968 | tf_op jit(solution)/shard_map/ppermute | solution.py:444
  6.3 27.2 %collective-permute-start.7 = (f32[2,128,640]{2,1,0:T(8,128)}, f32[2,128,640]{2,1,0:T(8,128)S(1)}, u32[]{:S(2)}, u32[]{:S(2)}) collective-permute-start(f32[2,128,640]{2,1,0:T(8,128)} %get-tuple-element.48), channel_id=1, source_target_pairs={{0,1},{1,0},{2,3},{3,2},{4,5},{5,4},{6,7},{7,6},{8,9},{9,8},{10,11... | collective-permute-start | bytes 1966088 | tf_op jit(solution)/shard_map/ppermute | solution.py:448
  30.7 16.1 %collective-permute-start.2 = (f32[3,32,1280]{2,1,0:T(8,128)}, f32[3,32,1280]{2,1,0:T(8,128)S(1)}, u32[]{:S(2)}, u32[]{:S(2)}) collective-permute-start(f32[3,32,1280]{2,1,0:T(8,128)} %get-tuple-element.42), channel_id=1, source_target_pairs={{0,2},{2,0},{4,6},{6,4},{8,10},{10,8},{12,14},{14,12},{16,18},{18,... | collective-permute-start | bytes 1474568 | tf_op jit(solution)/shard_map/ppermute | solution.py:494
  33.5 16.5 %collective-permute-start.5 = (f32[2,128,640]{2,1,0:T(8,128)}, f32[2,128,640]{2,1,0:T(8,128)S(1)}, u32[]{:S(2)}, u32[]{:S(2)}) collective-permute-start(f32[2,128,640]{2,1,0:T(8,128)} %gated.11), channel_id=1, source_target_pairs={{0,1},{1,0},{2,3},{3,2},{4,5},{5,4},{6,7},{7,6},{8,9},{9,8},{10,11... | collective-permute-start | bytes 1966088 | tf_op jit(solution)/shard_map/ppermute | solution.py:448
  44.5 3.3 %collective-permute-start.9 = (f32[3,32,1280]{2,1,0:T(8,128)}, f32[3,32,1280]{2,1,0:T(8,128)S(1)}, u32[]{:S(2)}, u32[]{:S(2)}) collective-permute-start(f32[3,32,1280]{2,1,0:T(8,128)} %get-tuple-element.52), channel_id=1, source_target_pairs={{0,2},{2,0},{4,6},{6,4},{8,10},{10,8},{12,14},{14,12},{16,18},{18,... | collective-permute-start | bytes 1474568 | tf_op jit(solution)/shard_map/ppermute | solution.py:494
  46.0 19.4 %collective-permute-start.8 = (f32[2,128,640]{2,1,0:T(8,128)}, f32[2,128,640]{2,1,0:T(8,128)}, u32[]{:S(2)}, u32[]{:S(2)}) collective-permute-start(f32[2,128,640]{2,1,0:T(8,128)} %gated.13), channel_id=1, source_target_pairs={{0,1},{1,0},{2,3},{3,2},{4,5},{5,4},{6,7},{7,6},{8,9},{9,8},{10,11... | collective-permute-start | bytes 1966088 | tf_op jit(solution)/shard_map/ppermute | solution.py:448
  46.3 15.3 %collective-permute-start.1 = (f32[3,32,1280]{2,1,0:T(8,128)}, f32[3,32,1280]{2,1,0:T(8,128)}, u32[]{:S(2)}, u32[]{:S(2)}) collective-permute-start(f32[3,32,1280]{2,1,0:T(8,128)} %get-tuple-element.40), channel_id=1, source_target_pairs={{0,2},{2,0},{4,6},{6,4},{8,10},{10,8},{12,14},{14,12},{16,18},{18,... | collective-permute-start | bytes 1474568 | tf_op jit(solution)/shard_map/ppermute | solution.py:495
  46.8 29.5 %collective-permute-start.12 = (f32[3,32,1280]{2,1,0:T(8,128)}, f32[3,32,1280]{2,1,0:T(8,128)S(1)}, u32[]{:S(2)}, u32[]{:S(2)}) collective-permute-start(f32[3,32,1280]{2,1,0:T(8,128)} %get-tuple-element.61), channel_id=1, source_target_pairs={{0,2},{2,0},{4,6},{6,4},{8,10},{10,8},{12,14},{14,12},{16,18},{18,... | collective-permute-start | bytes 1474568 | tf_op jit(solution)/shard_map/ppermute | solution.py:495
  47.7 15.6 %collective-permute-start.3 = (f32[3,32,1280]{2,1,0:T(8,128)}, f32[3,32,1280]{2,1,0:T(8,128)S(1)}, u32[]{:S(2)}, u32[]{:S(2)}) collective-permute-start(f32[3,32,1280]{2,1,0:T(8,128)} %add.295.refs_4_), channel_id=1, source_target_pairs={{0,4},{2,10},{4,0},{6,14},{8,12},{10,2},{12,8},{14,6},{16,20},{18,... | collective-permute-start | bytes 1474568 | tf_op jit(solution)/shard_map/ppermute | solution.py:469
  50.0 26.5 %collective-permute-start.13 = (f32[3,32,1280]{2,1,0:T(8,128)}, f32[3,32,1280]{2,1,0:T(8,128)S(1)}, u32[]{:S(2)}, u32[]{:S(2)}) collective-permute-start(f32[3,32,1280]{2,1,0:T(8,128)} %add.304.refs_4_), channel_id=1, source_target_pairs={{0,4},{2,10},{4,0},{6,14},{8,12},{10,2},{12,8},{14,6},{16,20},{18,... | collective-permute-start | bytes 1474568 | tf_op jit(solution)/shard_map/ppermute | solution.py:469
  61.6 17.9 %collective-permute-start.11 = (f32[3,32,1280]{2,1,0:T(8,128)}, f32[3,32,1280]{2,1,0:T(8,128)S(1)}, u32[]{:S(2)}, u32[]{:S(2)}) collective-permute-start(f32[3,32,1280]{2,1,0:T(8,128)} %get-tuple-element.59), channel_id=1, source_target_pairs={{0,2},{2,0},{4,6},{6,4},{8,10},{10,8},{12,14},{14,12},{16,18},{18,... | collective-permute-start | bytes 1474568 | tf_op jit(solution)/shard_map/ppermute | solution.py:494
  63.3 18.5 %collective-permute-start.6 = (f32[2,120,640]{2,1,0:T(8,128)}, f32[2,120,640]{2,1,0:T(8,128)}, u32[]{:S(2)}, u32[]{:S(2)}) collective-permute-start(f32[2,120,640]{2,1,0:T(8,128)} %gated.12), channel_id=1, source_target_pairs={{0,1},{1,0},{2,3},{3,2},{4,5},{5,4},{6,7},{7,6},{8,9},{9,8},{10,11... | collective-permute-start | bytes 1843208 | tf_op jit(solution)/shard_map/ppermute | solution.py:448
  65.4 13.4 %copy-start.11 = (f32[3,32,1280]{2,1,0:T(8,128)S(1)}, f32[3,32,1280]{2,1,0:T(8,128)}, u32[]{:S(2)}) copy-start(f32[3,32,1280]{2,1,0:T(8,128)} %get-tuple-element.60) | copy-start | bytes 1474564
  75.6 4.8 %collective-permute-start.10 = (f32[3,32,1280]{2,1,0:T(8,128)}, f32[3,32,1280]{2,1,0:T(8,128)S(1)}, u32[]{:S(2)}, u32[]{:S(2)}) collective-permute-start(f32[3,32,1280]{2,1,0:T(8,128)} %get-tuple-element.57), channel_id=1, source_target_pairs={{0,2},{2,0},{4,6},{6,4},{8,10},{10,8},{12,14},{14,12},{16,18},{18,... | collective-permute-start | bytes 1474568 | tf_op jit(solution)/shard_map/ppermute | solution.py:494
  76.3 29.3 %collective-permute-start.21 = (f32[3,32,1280]{2,1,0:T(8,128)}, f32[3,32,1280]{2,1,0:T(8,128)}, u32[]{:S(2)}, u32[]{:S(2)}) collective-permute-start(f32[3,32,1280]{2,1,0:T(8,128)} %get-tuple-element.66), channel_id=1, source_target_pairs={{0,2},{2,0},{4,6},{6,4},{8,10},{10,8},{12,14},{14,12},{16,18},{18,... | collective-permute-start | bytes 1474568 | tf_op jit(solution)/shard_map/ppermute | solution.py:495
  76.4 25.4 %collective-permute-start.4 = (f32[3,16,1280]{2,1,0:T(8,128)}, f32[3,16,1280]{2,1,0:T(8,128)}, u32[]{:S(2)}, u32[]{:S(2)}) collective-permute-start(f32[3,16,1280]{2,1,0:T(8,128)} %get-tuple-element.80.refs_5_), channel_id=1, source_target_pairs={{0,8},{2,18},{4,12},{6,22},{8,0},{10,26},{12,4},{14,30},{16,24},{1... | collective-permute-start | bytes 737288 | tf_op jit(solution)/shard_map/ppermute | solution.py:464
  79.5 24.0 %collective-permute-start.17 = (f32[3,16,1280]{2,1,0:T(8,128)}, f32[3,16,1280]{2,1,0:T(8,128)}, u32[]{:S(2)}, u32[]{:S(2)}) collective-permute-start(f32[3,16,1280]{2,1,0:T(8,128)} %get-tuple-element.82.refs_6_), channel_id=1, source_target_pairs={{0,8},{2,18},{4,12},{6,22},{8,0},{10,26},{12,4},{14,30},{16,24},{1... | collective-permute-start | bytes 737288 | tf_op jit(solution)/shard_map/ppermute | solution.py:464
  80.4 25.2 %collective-permute-start.22 = (f32[3,32,1280]{2,1,0:T(8,128)}, f32[3,32,1280]{2,1,0:T(8,128)}, u32[]{:S(2)}, u32[]{:S(2)}) collective-permute-start(f32[3,32,1280]{2,1,0:T(8,128)} %add.306.refs_5_), channel_id=1, source_target_pairs={{0,4},{2,10},{4,0},{6,14},{8,12},{10,2},{12,8},{14,6},{16,20},{18,... | collective-permute-start | bytes 1474568 | tf_op jit(solution)/shard_map/ppermute | solution.py:469
  81.8 19.2 %collective-permute-start.14 = (f32[3,32,1280]{2,1,0:T(8,128)S(1)}, f32[3,32,1280]{2,1,0:T(8,128)S(1)}, u32[]{:S(2)}, u32[]{:S(2)}) collective-permute-start(f32[3,32,1280]{2,1,0:T(8,128)S(1)} %add.305.refs_4_), channel_id=1, source_target_pairs={{0,4},{2,10},{4,0},{6,14},{8,12},{10,2},{12,8},{14,6},{16,20},{18,... | collective-permute-start | bytes 1474568 | tf_op jit(solution)/shard_map/ppermute | solution.py:469
  92.7 12.9 %copy-start.12 = (f32[3,32,1280]{2,1,0:T(8,128)S(1)}, f32[3,32,1280]{2,1,0:T(8,128)}, u32[]{:S(2)}) copy-start(f32[3,32,1280]{2,1,0:T(8,128)} %get-tuple-element.65) | copy-start | bytes 1474564
  101.0 8.1 %collective-permute-start.32 = (f32[3,32,1280]{2,1,0:T(8,128)}, f32[3,32,1280]{2,1,0:T(8,128)}, u32[]{:S(2)}, u32[]{:S(2)}) collective-permute-start(f32[3,32,1280]{2,1,0:T(8,128)} %get-tuple-element.70), channel_id=1, source_target_pairs={{0,2},{2,0},{4,6},{6,4},{8,10},{10,8},{12,14},{14,12},{16,18},{18,... | collective-permute-start | bytes 1474568 | tf_op jit(solution)/shard_map/ppermute | solution.py:495
  101.8 5.9 %collective-permute-start.15 = (f32[3,32,1280]{2,1,0:T(8,128)}, f32[3,32,1280]{2,1,0:T(8,128)S(1)}, u32[]{:S(2)}, u32[]{:S(2)}) collective-permute-start(f32[3,32,1280]{2,1,0:T(8,128)} %gated.14), channel_id=1, source_target_pairs={{0,2},{2,0},{4,6},{6,4},{8,10},{10,8},{12,14},{14,12},{16,18},{18,... | collective-permute-start | bytes 1474568 | tf_op jit(solution)/shard_map/ppermute | solution.py:494
  101.8 7.2 %copy-start.7 = (f32[3,32,1280]{2,1,0:T(8,128)S(1)}, f32[3,32,1280]{2,1,0:T(8,128)}, u32[]{:S(2)}) copy-start(f32[3,32,1280]{2,1,0:T(8,128)} %copy-done.6) | copy-start | bytes 1474564
  101.9 7.2 %copy-start.14 = (f32[3,32,1280]{2,1,0:T(8,128)S(1)}, f32[3,32,1280]{2,1,0:T(8,128)}, u32[]{:S(2)}) copy-start(f32[3,32,1280]{2,1,0:T(8,128)} %get-tuple-element.69) | copy-start | bytes 1474564
  105.1 28.7 %collective-permute-start.26 = (f32[3,32,1280]{2,1,0:T(8,128)}, f32[3,32,1280]{2,1,0:T(8,128)S(1)}, u32[]{:S(2)}, u32[]{:S(2)}) collective-permute-start(f32[3,32,1280]{2,1,0:T(8,128)} %get-tuple-element.68), channel_id=1, source_target_pairs={{0,2},{2,0},{4,6},{6,4},{8,10},{10,8},{12,14},{14,12},{16,18},{18,... | collective-permute-start | bytes 1474568 | tf_op jit(solution)/shard_map/ppermute | solution.py:495
  107.7 4.9 %copy-start.20 = (f32[3,32,1280]{2,1,0:T(8,128)S(1)}, f32[3,32,1280]{2,1,0:T(8,128)}, u32[]{:S(2)}) copy-start(f32[3,32,1280]{2,1,0:T(8,128)} %get-tuple-element.64) | copy-start | bytes 1474564
  108.5 4.1 %copy-start.1 = (f32[3,32,1280]{2,1,0:T(8,128)S(1)}, f32[3,32,1280]{2,1,0:T(8,128)}, u32[]{:S(2)}) copy-start(f32[3,32,1280]{2,1,0:T(8,128)} %copy-done) | copy-start | bytes 1474564
  108.5 7.1 %collective-permute-start.16 = (f32[3,8,1280]{2,1,0:T(8,128)}, f32[3,8,1280]{2,1,0:T(8,128)}, u32[]{:S(2)}, u32[]{:S(2)}) collective-permute-start(f32[3,8,1280]{2,1,0:T(8,128)} %gated.15), channel_id=1, source_target_pairs={{0,16},{2,6},{4,20},{6,2},{8,24},{10,14},{12,28},{14,10},{16,0},{1... | collective-permute-start | bytes 368648 | tf_op jit(solution)/shard_map/ppermute | solution.py:464
  110.9 27.9 %collective-permute-start.33 = (f32[3,16,1280]{2,1,0:T(8,128)}, f32[3,16,1280]{2,1,0:T(8,128)}, u32[]{:S(2)}, u32[]{:S(2)}) collective-permute-start(f32[3,16,1280]{2,1,0:T(8,128)} %get-tuple-element.76), channel_id=1, source_target_pairs={{0,8},{2,18},{4,12},{6,22},{8,0},{10,26},{12,4},{14,30},{16,24},{1... | collective-permute-start | bytes 737288 | tf_op jit(solution)/shard_map/ppermute | solution.py:464
  112.7 19.9 %collective-permute-start.19 = (f32[3,32,1280]{2,1,0:T(8,128)S(1)}, f32[3,32,1280]{2,1,0:T(8,128)S(1)}, u32[]{:S(2)}, u32[]{:S(2)}) collective-permute-start(f32[3,32,1280]{2,1,0:T(8,128)S(1)} %add.323), channel_id=1, source_target_pairs={{0,4},{2,10},{4,0},{6,14},{8,12},{10,2},{12,8},{14,6},{16,20},{18,... | collective-permute-start | bytes 1474568 | tf_op jit(solution)/shard_map/ppermute | solution.py:469
  114.6 5.4 %collective-permute-start.18 = (f32[3,8,1280]{2,1,0:T(8,128)}, f32[3,8,1280]{2,1,0:T(8,128)}, u32[]{:S(2)}, u32[]{:S(2)}) collective-permute-start(f32[3,8,1280]{2,1,0:T(8,128)} %gated.16), channel_id=1, source_target_pairs={{0,16},{2,6},{4,20},{6,2},{8,24},{10,14},{12,28},{14,10},{16,0},{1... | collective-permute-start | bytes 368648 | tf_op jit(solution)/shard_map/ppermute | solution.py:464
  115.5 18.3 %copy-start.15 = (f32[3,32,1280]{2,1,0:T(8,128)S(1)}, f32[3,32,1280]{2,1,0:T(8,128)}, u32[]{:S(2)}) copy-start(f32[3,32,1280]{2,1,0:T(8,128)} %get-tuple-element.67) | copy-start | bytes 1474564
  115.5 15.0 %collective-permute-start.23 = (f32[3,16,1280]{2,1,0:T(8,128)}, f32[3,16,1280]{2,1,0:T(8,128)S(1)}, u32[]{:S(2)}, u32[]{:S(2)}) collective-permute-start(f32[3,16,1280]{2,1,0:T(8,128)} %gated.18), channel_id=1, source_target_pairs={{0,8},{2,18},{4,12},{6,22},{8,0},{10,26},{12,4},{14,30},{16,24},{1... | collective-permute-start | bytes 737288 | tf_op jit(solution)/shard_map/ppermute | solution.py:464
  133.3 4.4 %collective-permute-start.24 = (f32[3,8,1280]{2,1,0:T(8,128)}, f32[3,8,1280]{2,1,0:T(8,128)S(1)}, u32[]{:S(2)}, u32[]{:S(2)}) collective-permute-start(f32[3,8,1280]{2,1,0:T(8,128)} %gated.19), channel_id=1, source_target_pairs={{0,16},{2,6},{4,20},{6,2},{8,24},{10,14},{12,28},{14,10},{16,0},{1... | collective-permute-start | bytes 368648 | tf_op jit(solution)/shard_map/ppermute | solution.py:464
  135.0 11.4 %collective-permute-start.27 = (f32[3,16,1280]{2,1,0:T(8,128)S(1)}, f32[3,16,1280]{2,1,0:T(8,128)S(1)}, u32[]{:S(2)}, u32[]{:S(2)}) collective-permute-start(f32[3,16,1280]{2,1,0:T(8,128)S(1)} %get-tuple-element.78), channel_id=1, source_target_pairs={{0,8},{2,18},{4,12},{6,22},{8,0},{10,26},{12,4},{14,30},{16,24},{1... | collective-permute-start | bytes 737288 | tf_op jit(solution)/shard_map/ppermute | solution.py:464
  136.8 3.8 %collective-permute-start.20 = (f32[2,8,1280]{2,1,0:T(8,128)}, f32[2,8,1280]{2,1,0:T(8,128)S(1)}, u32[]{:S(2)}, u32[]{:S(2)}) collective-permute-start(f32[2,8,1280]{2,1,0:T(8,128)} %gated.17), channel_id=1, source_target_pairs={{0,1},{1,0},{2,3},{3,2},{4,5},{5,4},{6,7},{7,6},{8,9},{9,8},{10,11... | collective-permute-start | bytes 245768 | tf_op jit(solution)/shard_map/ppermute | solution.py:526
  137.8 2.8 %collective-permute-start.25 = (f32[8,1280]{1,0:T(8,128)S(1)}, f32[8,1280]{1,0:T(8,128)S(1)}, u32[]{:S(2)}, u32[]{:S(2)}) collective-permute-start(f32[8,1280]{1,0:T(8,128)S(1)} %fusion.18), channel_id=1, source_target_pairs={{0,0},{1,2},{2,1},{3,3},{4,4},{5,10},{6,17},{7,7},{8,8},{9,18},{10... | collective-permute-start | bytes 122888 | tf_op jit(solution)/shard_map/ppermute | solution.py:537
  147.0 7.7 %copy-start.5 = (f32[3,16,1280]{2,1,0:T(8,128)S(1)}, f32[3,16,1280]{2,1,0:T(8,128)}, u32[]{:S(2)}) copy-start(f32[3,16,1280]{2,1,0:T(8,128)} %copy-done.4) | copy-start | bytes 737284
  147.0 3.9 %collective-permute-start.34 = (f32[3,8,1280]{2,1,0:T(8,128)}, f32[3,8,1280]{2,1,0:T(8,128)S(1)}, u32[]{:S(2)}, u32[]{:S(2)}) collective-permute-start(f32[3,8,1280]{2,1,0:T(8,128)} %gated.21), channel_id=1, source_target_pairs={{0,16},{2,6},{4,20},{6,2},{8,24},{10,14},{12,28},{14,10},{16,0},{1... | collective-permute-start | bytes 368648 | tf_op jit(solution)/shard_map/ppermute | solution.py:464
  148.5 6.2 %collective-permute-start.35 = (f32[3,8,1280]{2,1,0:T(8,128)S(1)}, f32[3,8,1280]{2,1,0:T(8,128)S(1)}, u32[]{:S(2)}, u32[]{:S(2)}) collective-permute-start(f32[3,8,1280]{2,1,0:T(8,128)S(1)} %dynamic-slice_add_fusion.10), channel_id=1, source_target_pairs={{0,16},{2,6},{4,20},{6,2},{8,24},{10,14},{12,28},{14,10},{16,0},{1... | collective-permute-start | bytes 368648 | tf_op jit(solution)/shard_map/ppermute | solution.py:464
  149.5 4.1 %collective-permute-start.28 = (f32[3,8,1280]{2,1,0:T(8,128)}, f32[3,8,1280]{2,1,0:T(8,128)S(1)}, u32[]{:S(2)}, u32[]{:S(2)}) collective-permute-start(f32[3,8,1280]{2,1,0:T(8,128)} %gated.20), channel_id=1, source_target_pairs={{0,16},{2,6},{4,20},{6,2},{8,24},{10,14},{12,28},{14,10},{16,0},{1... | collective-permute-start | bytes 368648 | tf_op jit(solution)/shard_map/ppermute | solution.py:475
  154.6 15.0 %collective-permute-start.29 = (f32[3,16,1280]{2,1,0:T(8,128)S(1)}, f32[3,16,1280]{2,1,0:T(8,128)S(1)}, u32[]{:S(2)}, u32[]{:S(2)}) collective-permute-start(f32[3,16,1280]{2,1,0:T(8,128)S(1)} %maximum_select_fusion.7), channel_id=1, source_target_pairs={{0,8},{2,18},{4,12},{6,22},{8,0},{10,26},{12,4},{14,30},{16,24},{1... | collective-permute-start | bytes 737288 | tf_op jit(solution)/shard_map/ppermute | solution.py:475
  154.8 14.9 %collective-permute-start.36 = (f32[2,8,1280]{2,1,0:T(8,128)S(1)}, f32[2,8,1280]{2,1,0:T(8,128)S(1)}, u32[]{:S(2)}, u32[]{:S(2)}) collective-permute-start(f32[2,8,1280]{2,1,0:T(8,128)S(1)} %pad_maximum_fusion.2), channel_id=1, source_target_pairs={{0,16},{2,6},{4,20},{6,2},{8,24},{10,14},{12,28},{14,10},{16,0},{1... | collective-permute-start | bytes 245768 | tf_op jit(solution)/shard_map/ppermute | solution.py:475
  169.7 13.3 %collective-permute-start.30 = (f32[3,32,1280]{2,1,0:T(8,128)S(1)}, f32[3,32,1280]{2,1,0:T(8,128)S(1)}, u32[]{:S(2)}, u32[]{:S(2)}) collective-permute-start(f32[3,32,1280]{2,1,0:T(8,128)S(1)} %maximum_select_fusion.5), channel_id=1, source_target_pairs={{0,4},{2,10},{4,0},{6,14},{8,12},{10,2},{12,8},{14,6},{16,20},{18,... | collective-permute-start | bytes 1474568 | tf_op jit(solution)/shard_map/ppermute | solution.py:475
  169.8 11.0 %collective-permute-start.37 = (f32[2,16,1280]{2,1,0:T(8,128)S(1)}, f32[2,16,1280]{2,1,0:T(8,128)S(1)}, u32[]{:S(2)}, u32[]{:S(2)}) collective-permute-start(f32[2,16,1280]{2,1,0:T(8,128)S(1)} %maximum_select_fusion.8), channel_id=1, source_target_pairs={{0,8},{2,18},{4,12},{6,22},{8,0},{10,26},{12,4},{14,30},{16,24},{1... | collective-permute-start | bytes 491528 | tf_op jit(solution)/shard_map/ppermute | solution.py:475
  180.8 10.3 %collective-permute-start.38 = (f32[2,32,1280]{2,1,0:T(8,128)S(1)}, f32[2,32,1280]{2,1,0:T(8,128)S(1)}, u32[]{:S(2)}, u32[]{:S(2)}) collective-permute-start(f32[2,32,1280]{2,1,0:T(8,128)S(1)} %maximum_select_fusion.6), channel_id=1, source_target_pairs={{0,4},{2,10},{4,0},{6,14},{8,12},{10,2},{12,8},{14,6},{16,20},{18,... | collective-permute-start | bytes 983048 | tf_op jit(solution)/shard_map/ppermute | solution.py:475
  183.1 15.9 %collective-permute-start.31 = (f32[3,64,1280]{2,1,0:T(8,128)S(1)}, f32[3,64,1280]{2,1,0:T(8,128)S(1)}, u32[]{:S(2)}, u32[]{:S(2)}) collective-permute-start(f32[3,64,1280]{2,1,0:T(8,128)S(1)} %maximum_select_fusion.3), channel_id=1, source_target_pairs={{0,2},{2,0},{4,6},{6,4},{8,10},{10,8},{12,14},{14,12},{16,18},{18,... | collective-permute-start | bytes 2949128 | tf_op jit(solution)/shard_map/ppermute | solution.py:475
  191.1 7.8 %collective-permute-start.39 = (f32[2,64,1280]{2,1,0:T(8,128)S(1)}, f32[2,64,1280]{2,1,0:T(8,128)S(1)}, u32[]{:S(2)}, u32[]{:S(2)}) collective-permute-start(f32[2,64,1280]{2,1,0:T(8,128)S(1)} %maximum_select_fusion.4), channel_id=1, source_target_pairs={{0,2},{2,0},{4,6},{6,4},{8,10},{10,8},{12,14},{14,12},{16,18},{18,... | collective-permute-start | bytes 1966088 | tf_op jit(solution)/shard_map/ppermute | solution.py:475
  (14 other events, 23.0 us)

commit v15 on v11

--- a/solution.py
+++ b/solution.py
@@ -14,7 +14,7 @@
 STEPS = 1
 SUB = 8
 LANE = 128
-VMEM_LIMIT = 60 * 1024 * 1024
+VMEM_LIMIT = 28 * 1024 * 1024
 KERNEL_WORK = 8
 ORDER = ((2, 4, 8), (4, 8, 2))
 AHEAD = ((), (), (0,), (1, 0), (2, 1, 0))
@@ -424,43 +424,6 @@
     return out[:4], (None if window.last else out[4])
 
 
-def put_kernel(count, place_ref, *refs):
-    parts, out_ref, sem = refs[:4], refs[-2], refs[-1]
-    core, side, along = place_ref[0], place_ref[1], place_ref[2]
-    around = parts[0].shape[1]
-    copies = []
-    for a, part in enumerate(parts):
-        half = core if a < 2 else 1 - core
-        quarter = side if a % 2 == 0 else 1 - side
-        for w in range(count):
-            level, row = place_ref[3 + 4 * w + half], place_ref[5 + 4 * w + half]
-            for n in range(around):
-                piece = lax.rem(along + 1 + n, around)
-                at = multiple(row + (quarter * around + piece) * SUB, SUB)
-                copies.append(pltpu.make_async_copy(part.at[w, n], out_ref.at[level, pl.ds(at, SUB)], sem.at[a, w, n]))
-                copies[-1].start()
-    for copy in copies:
-        copy.wait()
-
-
-def put(out, shape, places, parts):
-    count = parts[0].shape[0]
-    extra = [] if out is None else [out]
-    return pl.pallas_call(
-        functools.partial(put_kernel, count),
-        in_specs=[pl.BlockSpec(memory_space=pltpu.SMEM)]
-        + [pl.BlockSpec(memory_space=pltpu.VMEM)] * 4
-        + [pl.BlockSpec(memory_space=pl.ANY)] * len(extra),
-        out_specs=pl.BlockSpec(memory_space=pl.ANY),
-        out_shape=jax.ShapeDtypeStruct(shape, jnp.float32),
-        input_output_aliases={5: 0} if extra else {},
-        scratch_shapes=[pltpu.SemaphoreType.DMA((4, count, parts[0].shape[1]))],
-        compiler_params=pltpu.CompilerParams(vmem_limit_bytes=VMEM_LIMIT),
-        cost_estimate=pl.CostEstimate(flops=0, transcendentals=0, bytes_accessed=8 * 4 * parts[0].size),
-        name="put",
-    )(places.astype(jnp.int32), *parts, *extra)
-
-
 def by_levels(coeffs):
     spec = coeffs[0]
     levels, _, parts, waves_local, nlat = spec.shape

time: 184 us -> 191 us (1.038)
  local copies, waits for them, and re-layouts: 4.56 us -> 20.8 us
  Pallas kernels: 61.5 us -> 51.4 us
  starting transfers between devices: 36.2 us -> 33.3 us
  waiting for transfers between devices: 72.4 us -> 74.6 us
    unnamed x34 -> x58, local copies, waits for them, and re-layouts: 3.5 us -> 19.8 us
    pallas_call x5, Pallas kernels: 51.3 us -> 44.8 us  [window_tensor(): pl.pallas_call(functools.partial(window_kernel, window, depth, len(waits)...]
    pallas_call x3, Pallas kernels: 10.2 us -> 6.65 us  [pieces_of(): pl.pallas_call(functools.partial(pieces_kernel, windows, slots, count), i...]
    ppermute x1, waiting for transfers between devices: 8.2 us -> 5.35 us  [by_levels(): remotes = [lax.ppermute(piece, 'band', swap)]]
    ppermute x4, waiting for transfers between devices: 0.37 us -> 3.18 us  [by_levels(): remotes.append(lax.ppermute(piece, 'band', swap))]
  transfers between devices with their start and end apart: 40 -> 40, of which waited for: 13 -> 13; matrix products, arithmetic and copies ran while one was open for 4% -> 4% of each run, Pallas kernels for 32% -> 26%
where the time goes in v15:
time: 191 us; the launch traced here: 190 us
  waiting for transfers between devices  74.6 us (39%)
  Pallas kernels  51.4 us (27%)
  starting transfers between devices  33.3 us (17%)
  local copies, waits for them, and re-layouts  20.8 us (11%)
  other arithmetic  9.37 us (5%)
    pallas_call x5, Pallas kernels, window_tensor(): pl.pallas_call(functools.partial(window_kernel, window, depth, len(waits)...  44.8 us
    ppermute x10, waiting for transfers between devices, halved(): return ([total(mine), lax.ppermute(leaves, 'mem', ways[step])], leaves)  41.2 us
    ppermute x8, waiting for transfers between devices, doubled(): beside = lax.ppermute(part, 'mem', cores if step < 0 else ways[step])  24.8 us
    unnamed x58, local copies, waits for them, and re-layouts  19.8 us
    ppermute x10, starting transfers between devices, halved(): return ([total(mine), lax.ppermute(leaves, 'mem', ways[step])], leaves)  9.41 us
    pallas_call x3, Pallas kernels, pieces_of(): pl.pallas_call(functools.partial(pieces_kernel, windows, slots, count), i...  6.65 us
    ppermute x1, waiting for transfers between devices, by_levels(): remotes = [lax.ppermute(piece, 'band', swap)]  5.35 us
    ppermute x8, starting transfers between devices, doubled(): beside = lax.ppermute(part, 'mem', cores if step < 0 else ways[step])  5.16 us
  transfers between devices with their start and end apart: 40, of which 13 were waited for; matrix products, arithmetic and copies ran while one was open for 4% of the time, Pallas kernels for 26%

profile of v15, /device:TPU:0, one launch (start us, length us, event | category | flops | bytes accessed | tf_op | source)
XLA Modules:
  0.0 190.3 jit_solution(7768270511118196509)
XLA Ops:
  0.0 2.9 %copy-done = f32[1,2,2,2,320,640]{5,4,3,2,1,0:T(8,128)S(1)} copy-done((f32[1,2,2,2,320,640]{5,4,3,2,1,0:T(8,128)S(1)}, f32[1,2,2,2,320,640]{5,4,3,2,1,0:T(8,128)}, u32[]{:S(2)}) %copy-start) | copy-done | bytes 6553624
  2.9 1.1 pieces_of.4
  4.0 3.0 %collective-permute-start = (f32[2,136,640]{2,1,0:T(8,128)S(1)}, f32[2,136,640]{2,1,0:T(8,128)S(1)}, u32[]{:S(2)}, u32[]{:S(2)}) collective-permute-start(f32[2,136,640]{2,1,0:T(8,128)S(1)} %pieces_of.4), channel_id=1, source_target_pairs={{0,1},{1,0},{2,3},{3,2},{4,5},{5,4},{6,7},{7,6},{8,9},{9,8},{10,11... | collective-permute-start | bytes 2088968 | tf_op jit(solution)/shard_map/ppermute | solution.py:444
  7.0 2.3 %pieces_of.5 = (f32[2,128,640]{2,1,0:T(8,128)}, f32[2,128,640]{2,1,0:T(8,128)S(1)}, f32[2,128,640]{2,1,0:T(8,128)S(1)}, f32[2,120,640]{2,1,0:T(8,128)S(1)}) custom-call(s32[1]{0:T(128)} %bitcast.5.level_ref, f32[2,2,640,640]{3,2,1,0:T(8,128)S(1)} %bitcast.26), custom_call_target="tpu_custom_call" | custom-call | bytes 10485760 | tf_op jit(solution)/shard_map/pieces_of/pallas_call | solution.py:209
  11.8 2.9 %copy-done.1 = f32[1,2,2,2,320,640]{5,4,3,2,1,0:T(8,128)S(1)} copy-done((f32[1,2,2,2,320,640]{5,4,3,2,1,0:T(8,128)S(1)}, f32[1,2,2,2,320,640]{5,4,3,2,1,0:T(8,128)}, u32[]{:S(2)}) %copy-start.1) | copy-done | bytes 6553624
  14.7 3.2 %pieces_of.3 = (f32[2,136,640]{2,1,0:T(8,128)S(1)}, f32[2,128,640]{2,1,0:T(8,128)S(1)}, f32[2,128,640]{2,1,0:T(8,128)S(1)}, f32[2,128,640]{2,1,0:T(8,128)S(1)}, f32[2,120,640]{2,1,0:T(8,128)S(1)}) custom-call(s32[1]{0:T(128)} %bitcast.level_ref, f32[2,2,640,640]{3,2,1,0:T(8,128)S(1)} %bitcast.27), custom_call_target="tpu_custom_call" | custom-call | bytes 13107200 | tf_op jit(solution)/shard_map/pieces_of/pallas_call | solution.py:209
  18.1 5.3 %collective-permute-done.refs_2_.refs_1_ = f32[2,136,640]{2,1,0:T(8,128)S(1)} collective-permute-done((f32[2,136,640]{2,1,0:T(8,128)S(1)}, f32[2,136,640]{2,1,0:T(8,128)S(1)}, u32[]{:S(2)}, u32[]{:S(2)}) %collective-permute-start) | collective-permute-done | bytes 696352 | tf_op jit(solution)/shard_map/ppermute | solution.py:444
  23.4 8.6 %window_tensor.5 = (f32[3,32,1280]{2,1,0:T(8,128)S(1)}, f32[3,32,1280]{2,1,0:T(8,128)S(1)}, f32[3,32,1280]{2,1,0:T(8,128)}, f32[3,32,1280]{2,1,0:T(8,128)}, f32[2,16,1280]{2,1,0:T(8,128)S(1)}) custom-call(s32[4]{0:T(128)S(1)} %pad_add_fusion.refs_0_, f32[2,136,640]{2,1,0:T(8,128)S(1)} %get-tuple-element.38.refs_1_, ...), custom_call_target="tpu_custom_call" | custom-call | flops 10695475200 | bytes 6635520 | tf_op jit(solution)/shard_map/window_tensor/pallas_call | solution.py:398
  32.2 2.1 %collective-permute-start.13 = (f32[2,128,640]{2,1,0:T(8,128)}, f32[2,128,640]{2,1,0:T(8,128)S(1)}, u32[]{:S(2)}, u32[]{:S(2)}) collective-permute-start(f32[2,128,640]{2,1,0:T(8,128)} %gated.3), channel_id=1, source_target_pairs={{0,1},{1,0},{2,3},{3,2},{4,5},{5,4},{6,7},{7,6},{8,9},{9,8},{10,11... | collective-permute-start | bytes 1966088 | tf_op jit(solution)/shard_map/ppermute | solution.py:448
  34.3 3.2 %collective-permute-done.6.refs_2_.refs_1_ = f32[2,128,640]{2,1,0:T(8,128)S(1)} collective-permute-done((f32[2,128,640]{2,1,0:T(8,128)}, f32[2,128,640]{2,1,0:T(8,128)S(1)}, u32[]{:S(2)}, u32[]{:S(2)}) %collective-permute-start.6) | collective-permute-done | bytes 655392 | tf_op jit(solution)/shard_map/ppermute | solution.py:448
  37.5 1.3 copy-done.13
  38.8 1.9 %copy-done.19 = bf16[4,640,640]{2,1,0:T(8,128)(2,1)S(1)} copy-done((bf16[4,640,640]{2,1,0:T(8,128)(2,1)S(1)}, bf16[4,640,640]{2,1,0:T(8,128)(2,1)}, u32[]{:S(2)}) %copy-start.19) | copy-done | bytes 3276824
  40.7 0.9 copy-done.27
  41.6 8.5 %window_tensor.6 = (f32[3,32,1280]{2,1,0:T(8,128)S(1)}, f32[3,32,1280]{2,1,0:T(8,128)S(1)}, f32[3,32,1280]{2,1,0:T(8,128)}, f32[3,32,1280]{2,1,0:T(8,128)}, f32[2,16,1280]{2,1,0:T(8,128)S(1)}) custom-call(s32[4]{0:T(128)S(1)} %pad_add_fusion.refs_0_, f32[2,128,640]{2,1,0:T(8,128)S(1)} %copy-done.13, ...), custom_call_target="tpu_custom_call" | custom-call | flops 10066329600 | bytes 6553600 | tf_op jit(solution)/shard_map/window_tensor/pallas_call | solution.py:398
  50.4 1.8 collective-permute-start.24
  52.6 1.9 add.295.refs_4_
  54.5 1.5 collective-permute-start.3
  56.7 1.9 %copy-done.20 = bf16[4,640,640]{2,1,0:T(8,128)(2,1)S(1)} copy-done((bf16[4,640,640]{2,1,0:T(8,128)(2,1)S(1)}, bf16[4,640,640]{2,1,0:T(8,128)(2,1)}, u32[]{:S(2)}) %copy-start.20) | copy-done | bytes 3276824
  58.6 0.9 copy-done.25
  59.6 8.8 %window_tensor.7 = (f32[3,32,1280]{2,1,0:T(8,128)S(1)}, f32[3,32,1280]{2,1,0:T(8,128)S(1)}, f32[3,32,1280]{2,1,0:T(8,128)}, f32[3,32,1280]{2,1,0:T(8,128)S(1)}, f32[2,16,1280]{2,1,0:T(8,128)S(1)}) custom-call(s32[4]{0:T(128)S(1)} %pad_add_fusion.refs_0_, f32[2,128,640]{2,1,0:T(8,128)S(1)} %copy-done.11, ...), custom_call_target="tpu_custom_call" | custom-call | flops 10066329600 | bytes 6553600 | tf_op jit(solution)/shard_map/window_tensor/pallas_call | solution.py:398
  69.2 1.1 copy-done.17
  70.6 1.5 dynamic-slice_add_fusion.9
  72.4 1.8 collective-permute-start.4
  74.2 1.4 dynamic-slice_add_fusion.7
  75.9 0.9 copy-done.23
  76.9 9.7 %window_tensor.8 = (f32[3,32,1280]{2,1,0:T(8,128)S(1)}, f32[3,32,1280]{2,1,0:T(8,128)S(1)}, f32[3,32,1280]{2,1,0:T(8,128)S(1)}, f32[3,32,1280]{2,1,0:T(8,128)S(1)}, f32[2,16,1280]{2,1,0:T(8,128)S(1)}) custom-call(s32[4]{0:T(128)S(1)} %pad_add_fusion.refs_0_, f32[2,128,640]{2,1,0:T(8,128)S(1)} %copy-done.9, f32[2,128,640]{2,1,0:T(8,128)} %collective-permute-done.24.refs_2_, ...), custom_call_target="tpu_custom_call" | custom-call | flops 10066329600 | bytes 6553600 | tf_op jit(solution)/shard_map/window_tensor/pallas_call | solution.py:398
  87.7 1.6 collective-permute-start.16
  89.3 2.7 %collective-permute-start.5 = (f32[3,8,1280]{2,1,0:T(8,128)S(1)}, f32[3,8,1280]{2,1,0:T(8,128)S(1)}, u32[]{:S(2)}, u32[]{:S(2)}) collective-permute-start(f32[3,8,1280]{2,1,0:T(8,128)S(1)} %dynamic-slice_add_fusion.14.refs_6_), channel_id=1, source_target_pairs={{0,16},{2,6},{4,20},{6,2},{8,24},{10,14},{12,28},{14,10},{16,0},{1... | collective-permute-start | bytes 368648 | tf_op jit(solution)/shard_map/ppermute | solution.py:462
  92.0 9.1 %window_tensor.9 = (f32[3,32,1280]{2,1,0:T(8,128)S(1)}, f32[3,32,1280]{2,1,0:T(8,128)S(1)}, f32[3,32,1280]{2,1,0:T(8,128)S(1)}, f32[3,32,1280]{2,1,0:T(8,128)S(1)}) custom-call(s32[4]{0:T(128)S(1)} %pad_add_fusion.refs_0_, f32[2,120,640]{2,1,0:T(8,128)S(1)} %copy-done.15, f32[2,120,640]{2,1,0:T(8,128)S(1)} %collective-permute-done.30.refs_2_, ...), custom_call_target="tpu_custom_call" | custom-call | flops 9437184000 | bytes 6471680 | tf_op jit(solution)/shard_map/window_tensor/pallas_call | solution.py:398
  101.6 6.7 %collective-permute-done.11 = f32[3,8,1280]{2,1,0:T(8,128)S(1)} collective-permute-done((f32[3,8,1280]{2,1,0:T(8,128)S(1)}, f32[3,8,1280]{2,1,0:T(8,128)S(1)}, u32[]{:S(2)}, u32[]{:S(2)}) %collective-permute-start.11) | collective-permute-done | bytes 122912 | tf_op jit(solution)/shard_map/ppermute | solution.py:462
  108.9 7.4 %collective-permute-done.17 = f32[3,16,1280]{2,1,0:T(8,128)S(1)} collective-permute-done((f32[3,16,1280]{2,1,0:T(8,128)S(1)}, f32[3,16,1280]{2,1,0:T(8,128)S(1)}, u32[]{:S(2)}, u32[]{:S(2)}) %collective-permute-start.17) | collective-permute-done | bytes 245792 | tf_op jit(solution)/shard_map/ppermute | solution.py:462
  116.4 1.6 collective-permute-start.12
  118.6 4.7 %collective-permute-done.18 = f32[3,8,1280]{2,1,0:T(8,128)S(1)} collective-permute-done((f32[3,8,1280]{2,1,0:T(8,128)S(1)}, f32[3,8,1280]{2,1,0:T(8,128)S(1)}, u32[]{:S(2)}, u32[]{:S(2)}) %collective-permute-start.18) | collective-permute-done | bytes 122912 | tf_op jit(solution)/shard_map/ppermute | solution.py:462
  124.1 2.8 %collective-permute-start.31 = (f32[3,32,1280]{2,1,0:T(8,128)S(1)}, f32[3,32,1280]{2,1,0:T(8,128)S(1)}, u32[]{:S(2)}, u32[]{:S(2)}) collective-permute-start(f32[3,32,1280]{2,1,0:T(8,128)S(1)} %get-tuple-element.68), channel_id=1, source_target_pairs={{0,2},{2,0},{4,6},{6,4},{8,10},{10,8},{12,14},{14,12},{16,18},{18,... | collective-permute-start | bytes 1474568 | tf_op jit(solution)/shard_map/ppermute | solution.py:492
  128.1 2.5 %collective-permute-start.20 = (f32[3,8,1280]{2,1,0:T(8,128)S(1)}, f32[3,8,1280]{2,1,0:T(8,128)S(1)}, u32[]{:S(2)}, u32[]{:S(2)}) collective-permute-start(f32[3,8,1280]{2,1,0:T(8,128)S(1)} %pad_maximum_fusion), channel_id=1, source_target_pairs={{0,16},{2,6},{4,20},{6,2},{8,24},{10,14},{12,28},{14,10},{16,0},{1... | collective-permute-start | bytes 368648 | tf_op jit(solution)/shard_map/ppermute | solution.py:473
  131.2 3.9 %collective-permute-done.20 = f32[3,8,1280]{2,1,0:T(8,128)S(1)} collective-permute-done((f32[3,8,1280]{2,1,0:T(8,128)S(1)}, f32[3,8,1280]{2,1,0:T(8,128)S(1)}, u32[]{:S(2)}, u32[]{:S(2)}) %collective-permute-start.20) | collective-permute-done | bytes 122912 | tf_op jit(solution)/shard_map/ppermute | solution.py:473
  135.1 1.6 collective-permute-start.21
  136.7 8.3 %collective-permute-done.28 = f32[3,16,1280]{2,1,0:T(8,128)S(1)} collective-permute-done((f32[3,16,1280]{2,1,0:T(8,128)S(1)}, f32[3,16,1280]{2,1,0:T(8,128)S(1)}, u32[]{:S(2)}, u32[]{:S(2)}) %collective-permute-start.28) | collective-permute-done | bytes 245792 | tf_op jit(solution)/shard_map/ppermute | solution.py:462
  145.2 2.5 %collective-permute-start.34 = (f32[3,16,1280]{2,1,0:T(8,128)S(1)}, f32[3,16,1280]{2,1,0:T(8,128)S(1)}, u32[]{:S(2)}, u32[]{:S(2)}) collective-permute-start(f32[3,16,1280]{2,1,0:T(8,128)S(1)} %get-tuple-element.78), channel_id=1, source_target_pairs={{0,8},{2,18},{4,12},{6,22},{8,0},{10,26},{12,4},{14,30},{16,24},{1... | collective-permute-start | bytes 737288 | tf_op jit(solution)/shard_map/ppermute | solution.py:462
  147.8 8.0 %collective-permute-done.29 = f32[3,8,1280]{2,1,0:T(8,128)S(1)} collective-permute-done((f32[3,8,1280]{2,1,0:T(8,128)S(1)}, f32[3,8,1280]{2,1,0:T(8,128)S(1)}, u32[]{:S(2)}, u32[]{:S(2)}) %collective-permute-start.29) | collective-permute-done | bytes 122912 | tf_op jit(solution)/shard_map/ppermute | solution.py:462
  156.4 6.1 %collective-permute-done.35 = f32[3,8,1280]{2,1,0:T(8,128)S(1)} collective-permute-done((f32[3,8,1280]{2,1,0:T(8,128)S(1)}, f32[3,8,1280]{2,1,0:T(8,128)S(1)}, u32[]{:S(2)}, u32[]{:S(2)}) %collective-permute-start.35) | collective-permute-done | bytes 122912 | tf_op jit(solution)/shard_map/ppermute | solution.py:462
  163.5 5.5 %collective-permute-done.36 = f32[2,8,1280]{2,1,0:T(8,128)S(1)} collective-permute-done((f32[2,8,1280]{2,1,0:T(8,128)S(1)}, f32[2,8,1280]{2,1,0:T(8,128)S(1)}, u32[]{:S(2)}, u32[]{:S(2)}) %collective-permute-start.36) | collective-permute-done | bytes 81952 | tf_op jit(solution)/shard_map/ppermute | solution.py:473
  169.0 6.4 %collective-permute-done.37 = f32[2,16,1280]{2,1,0:T(8,128)S(1)} collective-permute-done((f32[2,16,1280]{2,1,0:T(8,128)S(1)}, f32[2,16,1280]{2,1,0:T(8,128)S(1)}, u32[]{:S(2)}, u32[]{:S(2)}) %collective-permute-start.37) | collective-permute-done | bytes 163872 | tf_op jit(solution)/shard_map/ppermute | solution.py:473
  175.7 6.9 %collective-permute-done.38 = f32[2,32,1280]{2,1,0:T(8,128)S(1)} collective-permute-done((f32[2,32,1280]{2,1,0:T(8,128)S(1)}, f32[2,32,1280]{2,1,0:T(8,128)S(1)}, u32[]{:S(2)}, u32[]{:S(2)}) %collective-permute-start.38) | collective-permute-done | bytes 327712 | tf_op jit(solution)/shard_map/ppermute | solution.py:473
  182.8 2.2 %collective-permute-done.39 = f32[2,64,1280]{2,1,0:T(8,128)} collective-permute-done((f32[2,64,1280]{2,1,0:T(8,128)S(1)}, f32[2,64,1280]{2,1,0:T(8,128)}, u32[]{:S(2)}, u32[]{:S(2)}) %collective-permute-start.39) | collective-permute-done | bytes 655392 | tf_op jit(solution)/shard_map/ppermute | solution.py:473
  185.0 1.4 maximum_select_fusion.2
  187.7 1.7 copy-done.28
  189.4 0.9 slice_dynamic-update-slice_fusion
  (144 shorter events, 14.6 us)
Async XLA Ops:
  4.0 19.4 %collective-permute-start = (f32[2,136,640]{2,1,0:T(8,128)S(1)}, f32[2,136,640]{2,1,0:T(8,128)S(1)}, u32[]{:S(2)}, u32[]{:S(2)}) collective-permute-start(f32[2,136,640]{2,1,0:T(8,128)S(1)} %pieces_of.4), channel_id=1, source_target_pairs={{0,1},{1,0},{2,3},{3,2},{4,5},{5,4},{6,7},{7,6},{8,9},{9,8},{10,11... | collective-permute-start | bytes 2088968 | tf_op jit(solution)/shard_map/ppermute | solution.py:444
  11.8 25.6 %collective-permute-start.6 = (f32[2,128,640]{2,1,0:T(8,128)}, f32[2,128,640]{2,1,0:T(8,128)S(1)}, u32[]{:S(2)}, u32[]{:S(2)}) collective-permute-start(f32[2,128,640]{2,1,0:T(8,128)} %get-tuple-element.44), channel_id=1, source_target_pairs={{0,1},{1,0},{2,3},{3,2},{4,5},{5,4},{6,7},{7,6},{8,9},{9,8},{10,11... | collective-permute-start | bytes 1966088 | tf_op jit(solution)/shard_map/ppermute | solution.py:448
  14.7 8.7 %copy-start.18 = (bf16[4,640,640]{2,1,0:T(8,128)(2,1)S(1)}, bf16[4,640,640]{2,1,0:T(8,128)(2,1)}, u32[]{:S(2)}) copy-start(bf16[4,640,640]{2,1,0:T(8,128)(2,1)} %constant.121.clone.refs_3_) | copy-start | bytes 9830404
  17.9 14.1 %copy-start.8 = (f32[2,128,640]{2,1,0:T(8,128)}, f32[2,128,640]{2,1,0:T(8,128)S(1)}, u32[]{:S(2)}) copy-start(f32[2,128,640]{2,1,0:T(8,128)S(1)} %get-tuple-element.57.refs_1_) | copy-start | bytes 1966084
  17.9 14.1 %copy-start.10 = (f32[2,128,640]{2,1,0:T(8,128)}, f32[2,128,640]{2,1,0:T(8,128)S(1)}, u32[]{:S(2)}) copy-start(f32[2,128,640]{2,1,0:T(8,128)S(1)} %get-tuple-element.50.refs_1_) | copy-start | bytes 1966084
  18.0 14.1 %copy-start.12 = (f32[2,128,640]{2,1,0:T(8,128)}, f32[2,128,640]{2,1,0:T(8,128)S(1)}, u32[]{:S(2)}) copy-start(f32[2,128,640]{2,1,0:T(8,128)S(1)} %get-tuple-element.43.refs_1_) | copy-start | bytes 1966084
  18.0 14.1 %copy-start.14 = (f32[2,120,640]{2,1,0:T(8,128)}, f32[2,120,640]{2,1,0:T(8,128)S(1)}, u32[]{:S(2)}) copy-start(f32[2,120,640]{2,1,0:T(8,128)S(1)} %get-tuple-element.64.refs_1_) | copy-start | bytes 1843204
  23.4 8.6 %copy-start.2 = (f32[2,136,640]{2,1,0:T(8,128)}, f32[2,136,640]{2,1,0:T(8,128)S(1)}, u32[]{:S(2)}) copy-start(f32[2,136,640]{2,1,0:T(8,128)S(1)} %collective-permute-done.refs_2_.refs_1_) | copy-start | bytes 2088964
  32.1 20.1 %collective-permute-start.2 = (f32[3,32,1280]{2,1,0:T(8,128)}, f32[3,32,1280]{2,1,0:T(8,128)}, u32[]{:S(2)}, u32[]{:S(2)}) collective-permute-start(f32[3,32,1280]{2,1,0:T(8,128)} %get-tuple-element.42), channel_id=1, source_target_pairs={{0,2},{2,0},{4,6},{6,4},{8,10},{10,8},{12,14},{14,12},{16,18},{18,... | collective-permute-start | bytes 1474568 | tf_op jit(solution)/shard_map/ppermute | solution.py:491
  32.2 24.0 %collective-permute-start.13 = (f32[2,128,640]{2,1,0:T(8,128)}, f32[2,128,640]{2,1,0:T(8,128)S(1)}, u32[]{:S(2)}, u32[]{:S(2)}) collective-permute-start(f32[2,128,640]{2,1,0:T(8,128)} %gated.3), channel_id=1, source_target_pairs={{0,1},{1,0},{2,3},{3,2},{4,5},{5,4},{6,7},{7,6},{8,9},{9,8},{10,11... | collective-permute-start | bytes 1966088 | tf_op jit(solution)/shard_map/ppermute | solution.py:448
  37.5 12.7 %copy-start.6 = (f32[2,128,640]{2,1,0:T(8,128)}, f32[2,128,640]{2,1,0:T(8,128)S(1)}, u32[]{:S(2)}) copy-start(f32[2,128,640]{2,1,0:T(8,128)S(1)} %collective-permute-done.6.refs_2_.refs_1_) | copy-start | bytes 1966084
  50.2 4.3 %collective-permute-start.8 = (f32[3,32,1280]{2,1,0:T(8,128)}, f32[3,32,1280]{2,1,0:T(8,128)S(1)}, u32[]{:S(2)}, u32[]{:S(2)}) collective-permute-start(f32[3,32,1280]{2,1,0:T(8,128)} %get-tuple-element.49), channel_id=1, source_target_pairs={{0,2},{2,0},{4,6},{6,4},{8,10},{10,8},{12,14},{14,12},{16,18},{18,... | collective-permute-start | bytes 1474568 | tf_op jit(solution)/shard_map/ppermute | solution.py:491
  50.4 25.3 %collective-permute-start.24 = (f32[2,128,640]{2,1,0:T(8,128)}, f32[2,128,640]{2,1,0:T(8,128)}, u32[]{:S(2)}, u32[]{:S(2)}) collective-permute-start(f32[2,128,640]{2,1,0:T(8,128)} %gated.4), channel_id=1, source_target_pairs={{0,1},{1,0},{2,3},{3,2},{4,5},{5,4},{6,7},{7,6},{8,9},{9,8},{10,11... | collective-permute-start | bytes 1966088 | tf_op jit(solution)/shard_map/ppermute | solution.py:448
  52.1 17.0 %collective-permute-start.1 = (f32[3,32,1280]{2,1,0:T(8,128)}, f32[3,32,1280]{2,1,0:T(8,128)}, u32[]{:S(2)}, u32[]{:S(2)}) collective-permute-start(f32[3,32,1280]{2,1,0:T(8,128)} %get-tuple-element.40), channel_id=1, source_target_pairs={{0,2},{2,0},{4,6},{6,4},{8,10},{10,8},{12,14},{14,12},{16,18},{18,... | collective-permute-start | bytes 1474568 | tf_op jit(solution)/shard_map/ppermute | solution.py:492
  52.2 20.0 %collective-permute-start.7 = (f32[3,32,1280]{2,1,0:T(8,128)}, f32[3,32,1280]{2,1,0:T(8,128)}, u32[]{:S(2)}, u32[]{:S(2)}) collective-permute-start(f32[3,32,1280]{2,1,0:T(8,128)} %get-tuple-element.47), channel_id=1, source_target_pairs={{0,2},{2,0},{4,6},{6,4},{8,10},{10,8},{12,14},{14,12},{16,18},{18,... | collective-permute-start | bytes 1474568 | tf_op jit(solution)/shard_map/ppermute | solution.py:492
  54.5 15.7 %collective-permute-start.3 = (f32[3,32,1280]{2,1,0:T(8,128)}, f32[3,32,1280]{2,1,0:T(8,128)}, u32[]{:S(2)}, u32[]{:S(2)}) collective-permute-start(f32[3,32,1280]{2,1,0:T(8,128)} %add.295.refs_4_), channel_id=1, source_target_pairs={{0,4},{2,10},{4,0},{6,14},{8,12},{10,2},{12,8},{14,6},{16,20},{18,... | collective-permute-start | bytes 1474568 | tf_op jit(solution)/shard_map/ppermute | solution.py:467
  56.1 12.2 %copy-start.3 = (f32[2,128,640]{2,1,0:T(8,128)}, f32[2,128,640]{2,1,0:T(8,128)S(1)}, u32[]{:S(2)}) copy-start(f32[2,128,640]{2,1,0:T(8,128)S(1)} %collective-permute-done.13.refs_2_.refs_1_) | copy-start | bytes 1966084
  56.1 16.3 %collective-permute-start.9 = (f32[3,32,1280]{2,1,0:T(8,128)S(1)}, f32[3,32,1280]{2,1,0:T(8,128)}, u32[]{:S(2)}, u32[]{:S(2)}) collective-permute-start(f32[3,32,1280]{2,1,0:T(8,128)S(1)} %add.310.refs_4_), channel_id=1, source_target_pairs={{0,4},{2,10},{4,0},{6,14},{8,12},{10,2},{12,8},{14,6},{16,20},{18,... | collective-permute-start | bytes 1474568 | tf_op jit(solution)/shard_map/ppermute | solution.py:467
  70.2 16.4 %collective-permute-start.15 = (f32[3,32,1280]{2,1,0:T(8,128)S(1)}, f32[3,32,1280]{2,1,0:T(8,128)S(1)}, u32[]{:S(2)}, u32[]{:S(2)}) collective-permute-start(f32[3,32,1280]{2,1,0:T(8,128)S(1)} %copy-done.17), channel_id=1, source_target_pairs={{0,2},{2,0},{4,6},{6,4},{8,10},{10,8},{12,14},{14,12},{16,18},{18,... | collective-permute-start | bytes 1474568 | tf_op jit(solution)/shard_map/ppermute | solution.py:491
  70.2 19.1 %collective-permute-start.30 = (f32[2,120,640]{2,1,0:T(8,128)}, f32[2,120,640]{2,1,0:T(8,128)S(1)}, u32[]{:S(2)}, u32[]{:S(2)}) collective-permute-start(f32[2,120,640]{2,1,0:T(8,128)} %gated.5), channel_id=1, source_target_pairs={{0,1},{1,0},{2,3},{3,2},{4,5},{5,4},{6,7},{7,6},{8,9},{9,8},{10,11... | collective-permute-start | bytes 1843208 | tf_op jit(solution)/shard_map/ppermute | solution.py:448
  72.2 36.2 %collective-permute-start.14 = (f32[3,32,1280]{2,1,0:T(8,128)}, f32[3,32,1280]{2,1,0:T(8,128)S(1)}, u32[]{:S(2)}, u32[]{:S(2)}) collective-permute-start(f32[3,32,1280]{2,1,0:T(8,128)} %get-tuple-element.54), channel_id=1, source_target_pairs={{0,2},{2,0},{4,6},{6,4},{8,10},{10,8},{12,14},{14,12},{16,18},{18,... | collective-permute-start | bytes 1474568 | tf_op jit(solution)/shard_map/ppermute | solution.py:492
  72.4 15.1 %collective-permute-start.4 = (f32[3,16,1280]{2,1,0:T(8,128)S(1)}, f32[3,16,1280]{2,1,0:T(8,128)S(1)}, u32[]{:S(2)}, u32[]{:S(2)}) collective-permute-start(f32[3,16,1280]{2,1,0:T(8,128)S(1)} %get-tuple-element.80.refs_5_), channel_id=1, source_target_pairs={{0,8},{2,18},{4,12},{6,22},{8,0},{10,26},{12,4},{14,30},{16,24},{1... | collective-permute-start | bytes 737288 | tf_op jit(solution)/shard_map/ppermute | solution.py:462
  75.6 12.0 %collective-permute-start.10 = (f32[3,16,1280]{2,1,0:T(8,128)S(1)}, f32[3,16,1280]{2,1,0:T(8,128)S(1)}, u32[]{:S(2)}, u32[]{:S(2)}) collective-permute-start(f32[3,16,1280]{2,1,0:T(8,128)S(1)} %get-tuple-element.82.refs_5_), channel_id=1, source_target_pairs={{0,8},{2,18},{4,12},{6,22},{8,0},{10,26},{12,4},{14,30},{16,24},{1... | collective-permute-start | bytes 737288 | tf_op jit(solution)/shard_map/ppermute | solution.py:462
  86.6 31.4 %collective-permute-start.26 = (f32[3,32,1280]{2,1,0:T(8,128)S(1)}, f32[3,32,1280]{2,1,0:T(8,128)S(1)}, u32[]{:S(2)}, u32[]{:S(2)}) collective-permute-start(f32[3,32,1280]{2,1,0:T(8,128)S(1)} %get-tuple-element.63), channel_id=1, source_target_pairs={{0,2},{2,0},{4,6},{6,4},{8,10},{10,8},{12,14},{14,12},{16,18},{18,... | collective-permute-start | bytes 1474568 | tf_op jit(solution)/shard_map/ppermute | solution.py:491
  87.5 43.0 %collective-permute-start.25 = (f32[3,32,1280]{2,1,0:T(8,128)S(1)}, f32[3,32,1280]{2,1,0:T(8,128)S(1)}, u32[]{:S(2)}, u32[]{:S(2)}) collective-permute-start(f32[3,32,1280]{2,1,0:T(8,128)S(1)} %get-tuple-element.61), channel_id=1, source_target_pairs={{0,2},{2,0},{4,6},{6,4},{8,10},{10,8},{12,14},{14,12},{16,18},{18,... | collective-permute-start | bytes 1474568 | tf_op jit(solution)/shard_map/ppermute | solution.py:492
  87.7 20.7 %collective-permute-start.16 = (f32[3,32,1280]{2,1,0:T(8,128)S(1)}, f32[3,32,1280]{2,1,0:T(8,128)S(1)}, u32[]{:S(2)}, u32[]{:S(2)}) collective-permute-start(f32[3,32,1280]{2,1,0:T(8,128)S(1)} %add.322.refs_4_), channel_id=1, source_target_pairs={{0,4},{2,10},{4,0},{6,14},{8,12},{10,2},{12,8},{14,6},{16,20},{18,... | collective-permute-start | bytes 1474568 | tf_op jit(solution)/shard_map/ppermute | solution.py:467
  89.3 11.8 %collective-permute-start.5 = (f32[3,8,1280]{2,1,0:T(8,128)S(1)}, f32[3,8,1280]{2,1,0:T(8,128)S(1)}, u32[]{:S(2)}, u32[]{:S(2)}) collective-permute-start(f32[3,8,1280]{2,1,0:T(8,128)S(1)} %dynamic-slice_add_fusion.14.refs_6_), channel_id=1, source_target_pairs={{0,16},{2,6},{4,20},{6,2},{8,24},{10,14},{12,28},{14,10},{16,0},{1... | collective-permute-start | bytes 368648 | tf_op jit(solution)/shard_map/ppermute | solution.py:462
  101.1 7.2 %collective-permute-start.11 = (f32[3,8,1280]{2,1,0:T(8,128)S(1)}, f32[3,8,1280]{2,1,0:T(8,128)S(1)}, u32[]{:S(2)}, u32[]{:S(2)}) collective-permute-start(f32[3,8,1280]{2,1,0:T(8,128)S(1)} %dynamic-slice_add_fusion.13), channel_id=1, source_target_pairs={{0,16},{2,6},{4,20},{6,2},{8,24},{10,14},{12,28},{14,10},{16,0},{1... | collective-permute-start | bytes 368648 | tf_op jit(solution)/shard_map/ppermute | solution.py:462
  108.3 15.8 %collective-permute-start.32 = (f32[3,32,1280]{2,1,0:T(8,128)S(1)}, f32[3,32,1280]{2,1,0:T(8,128)S(1)}, u32[]{:S(2)}, u32[]{:S(2)}) collective-permute-start(f32[3,32,1280]{2,1,0:T(8,128)S(1)} %get-tuple-element.70), channel_id=1, source_target_pairs={{0,2},{2,0},{4,6},{6,4},{8,10},{10,8},{12,14},{14,12},{16,18},{18,... | collective-permute-start | bytes 1474568 | tf_op jit(solution)/shard_map/ppermute | solution.py:491
  108.5 7.9 %collective-permute-start.17 = (f32[3,16,1280]{2,1,0:T(8,128)S(1)}, f32[3,16,1280]{2,1,0:T(8,128)S(1)}, u32[]{:S(2)}, u32[]{:S(2)}) collective-permute-start(f32[3,16,1280]{2,1,0:T(8,128)S(1)} %get-tuple-element.84), channel_id=1, source_target_pairs={{0,8},{2,18},{4,12},{6,22},{8,0},{10,26},{12,4},{14,30},{16,24},{1... | collective-permute-start | bytes 737288 | tf_op jit(solution)/shard_map/ppermute | solution.py:462
  116.3 7.0 %collective-permute-start.18 = (f32[3,8,1280]{2,1,0:T(8,128)S(1)}, f32[3,8,1280]{2,1,0:T(8,128)S(1)}, u32[]{:S(2)}, u32[]{:S(2)}) collective-permute-start(f32[3,8,1280]{2,1,0:T(8,128)S(1)} %dynamic-slice_add_fusion.12), channel_id=1, source_target_pairs={{0,16},{2,6},{4,20},{6,2},{8,24},{10,14},{12,28},{14,10},{16,0},{1... | collective-permute-start | bytes 368648 | tf_op jit(solution)/shard_map/ppermute | solution.py:462
  116.4 11.3 %collective-permute-start.12 = (f32[2,8,1280]{2,1,0:T(8,128)S(1)}, f32[2,8,1280]{2,1,0:T(8,128)S(1)}, u32[]{:S(2)}, u32[]{:S(2)}) collective-permute-start(f32[2,8,1280]{2,1,0:T(8,128)S(1)} %pad_maximum_fusion.1), channel_id=1, source_target_pairs={{0,1},{1,0},{2,3},{3,2},{4,5},{5,4},{6,7},{7,6},{8,9},{9,8},{10,11... | collective-permute-start | bytes 245768 | tf_op jit(solution)/shard_map/ppermute | solution.py:501
  118.1 12.5 %collective-permute-start.27 = (f32[3,32,1280]{2,1,0:T(8,128)S(1)}, f32[3,32,1280]{2,1,0:T(8,128)S(1)}, u32[]{:S(2)}, u32[]{:S(2)}) collective-permute-start(f32[3,32,1280]{2,1,0:T(8,128)S(1)} %add.335), channel_id=1, source_target_pairs={{0,4},{2,10},{4,0},{6,14},{8,12},{10,2},{12,8},{14,6},{16,20},{18,... | collective-permute-start | bytes 1474568 | tf_op jit(solution)/shard_map/ppermute | solution.py:467
  123.4 4.6 %collective-permute-start.19 = (f32[8,1280]{1,0:T(8,128)S(1)}, f32[8,1280]{1,0:T(8,128)S(1)}, u32[]{:S(2)}, u32[]{:S(2)}) collective-permute-start(f32[8,1280]{1,0:T(8,128)S(1)} %fusion.18), channel_id=1, source_target_pairs={{0,0},{1,2},{2,1},{3,3},{4,4},{5,10},{6,17},{7,7},{8,8},{9,18},{10... | collective-permute-start | bytes 122888 | tf_op jit(solution)/shard_map/ppermute | solution.py:512
  124.1 21.0 %collective-permute-start.31 = (f32[3,32,1280]{2,1,0:T(8,128)S(1)}, f32[3,32,1280]{2,1,0:T(8,128)S(1)}, u32[]{:S(2)}, u32[]{:S(2)}) collective-permute-start(f32[3,32,1280]{2,1,0:T(8,128)S(1)} %get-tuple-element.68), channel_id=1, source_target_pairs={{0,2},{2,0},{4,6},{6,4},{8,10},{10,8},{12,14},{14,12},{16,18},{18,... | collective-permute-start | bytes 1474568 | tf_op jit(solution)/shard_map/ppermute | solution.py:492
  127.8 17.4 %collective-permute-start.33 = (f32[3,32,1280]{2,1,0:T(8,128)}, f32[3,32,1280]{2,1,0:T(8,128)S(1)}, u32[]{:S(2)}, u32[]{:S(2)}) collective-permute-start(f32[3,32,1280]{2,1,0:T(8,128)} %add.347), channel_id=1, source_target_pairs={{0,4},{2,10},{4,0},{6,14},{8,12},{10,2},{12,8},{14,6},{16,20},{18,... | collective-permute-start | bytes 1474568 | tf_op jit(solution)/shard_map/ppermute | solution.py:467
  128.1 7.0 %collective-permute-start.20 = (f32[3,8,1280]{2,1,0:T(8,128)S(1)}, f32[3,8,1280]{2,1,0:T(8,128)S(1)}, u32[]{:S(2)}, u32[]{:S(2)}) collective-permute-start(f32[3,8,1280]{2,1,0:T(8,128)S(1)} %pad_maximum_fusion), channel_id=1, source_target_pairs={{0,16},{2,6},{4,20},{6,2},{8,24},{10,14},{12,28},{14,10},{16,0},{1... | collective-permute-start | bytes 368648 | tf_op jit(solution)/shard_map/ppermute | solution.py:473
  130.7 14.3 %collective-permute-start.28 = (f32[3,16,1280]{2,1,0:T(8,128)S(1)}, f32[3,16,1280]{2,1,0:T(8,128)S(1)}, u32[]{:S(2)}, u32[]{:S(2)}) collective-permute-start(f32[3,16,1280]{2,1,0:T(8,128)S(1)} %get-tuple-element.76), channel_id=1, source_target_pairs={{0,8},{2,18},{4,12},{6,22},{8,0},{10,26},{12,4},{14,30},{16,24},{1... | collective-permute-start | bytes 737288 | tf_op jit(solution)/shard_map/ppermute | solution.py:462
  135.1 27.6 %collective-permute-start.21 = (f32[3,16,1280]{2,1,0:T(8,128)S(1)}, f32[3,16,1280]{2,1,0:T(8,128)S(1)}, u32[]{:S(2)}, u32[]{:S(2)}) collective-permute-start(f32[3,16,1280]{2,1,0:T(8,128)S(1)} %maximum_select_fusion.7), channel_id=1, source_target_pairs={{0,8},{2,18},{4,12},{6,22},{8,0},{10,26},{12,4},{14,30},{16,24},{1... | collective-permute-start | bytes 737288 | tf_op jit(solution)/shard_map/ppermute | solution.py:473
  145.0 10.7 %collective-permute-start.29 = (f32[3,8,1280]{2,1,0:T(8,128)S(1)}, f32[3,8,1280]{2,1,0:T(8,128)S(1)}, u32[]{:S(2)}, u32[]{:S(2)}) collective-permute-start(f32[3,8,1280]{2,1,0:T(8,128)S(1)} %dynamic-slice_add_fusion.11), channel_id=1, source_target_pairs={{0,16},{2,6},{4,20},{6,2},{8,24},{10,14},{12,28},{14,10},{16,0},{1... | collective-permute-start | bytes 368648 | tf_op jit(solution)/shard_map/ppermute | solution.py:462
  145.2 10.5 %collective-permute-start.34 = (f32[3,16,1280]{2,1,0:T(8,128)S(1)}, f32[3,16,1280]{2,1,0:T(8,128)S(1)}, u32[]{:S(2)}, u32[]{:S(2)}) collective-permute-start(f32[3,16,1280]{2,1,0:T(8,128)S(1)} %get-tuple-element.78), channel_id=1, source_target_pairs={{0,8},{2,18},{4,12},{6,22},{8,0},{10,26},{12,4},{14,30},{16,24},{1... | collective-permute-start | bytes 737288 | tf_op jit(solution)/shard_map/ppermute | solution.py:462
  155.8 6.7 %collective-permute-start.35 = (f32[3,8,1280]{2,1,0:T(8,128)S(1)}, f32[3,8,1280]{2,1,0:T(8,128)S(1)}, u32[]{:S(2)}, u32[]{:S(2)}) collective-permute-start(f32[3,8,1280]{2,1,0:T(8,128)S(1)} %dynamic-slice_add_fusion.10), channel_id=1, source_target_pairs={{0,16},{2,6},{4,20},{6,2},{8,24},{10,14},{12,28},{14,10},{16,0},{1... | collective-permute-start | bytes 368648 | tf_op jit(solution)/shard_map/ppermute | solution.py:462
  162.6 6.3 %collective-permute-start.36 = (f32[2,8,1280]{2,1,0:T(8,128)S(1)}, f32[2,8,1280]{2,1,0:T(8,128)S(1)}, u32[]{:S(2)}, u32[]{:S(2)}) collective-permute-start(f32[2,8,1280]{2,1,0:T(8,128)S(1)} %pad_maximum_fusion.2), channel_id=1, source_target_pairs={{0,16},{2,6},{4,20},{6,2},{8,24},{10,14},{12,28},{14,10},{16,0},{1... | collective-permute-start | bytes 245768 | tf_op jit(solution)/shard_map/ppermute | solution.py:473
  162.7 12.8 %collective-permute-start.22 = (f32[3,32,1280]{2,1,0:T(8,128)S(1)}, f32[3,32,1280]{2,1,0:T(8,128)S(1)}, u32[]{:S(2)}, u32[]{:S(2)}) collective-permute-start(f32[3,32,1280]{2,1,0:T(8,128)S(1)} %maximum_select_fusion.5), channel_id=1, source_target_pairs={{0,4},{2,10},{4,0},{6,14},{8,12},{10,2},{12,8},{14,6},{16,20},{18,... | collective-permute-start | bytes 1474568 | tf_op jit(solution)/shard_map/ppermute | solution.py:473
  169.0 6.5 %collective-permute-start.37 = (f32[2,16,1280]{2,1,0:T(8,128)S(1)}, f32[2,16,1280]{2,1,0:T(8,128)S(1)}, u32[]{:S(2)}, u32[]{:S(2)}) collective-permute-start(f32[2,16,1280]{2,1,0:T(8,128)S(1)} %maximum_select_fusion.8), channel_id=1, source_target_pairs={{0,8},{2,18},{4,12},{6,22},{8,0},{10,26},{12,4},{14,30},{16,24},{1... | collective-permute-start | bytes 491528 | tf_op jit(solution)/shard_map/ppermute | solution.py:473
  175.5 7.1 %collective-permute-start.38 = (f32[2,32,1280]{2,1,0:T(8,128)S(1)}, f32[2,32,1280]{2,1,0:T(8,128)S(1)}, u32[]{:S(2)}, u32[]{:S(2)}) collective-permute-start(f32[2,32,1280]{2,1,0:T(8,128)S(1)} %maximum_select_fusion.6), channel_id=1, source_target_pairs={{0,4},{2,10},{4,0},{6,14},{8,12},{10,2},{12,8},{14,6},{16,20},{18,... | collective-permute-start | bytes 983048 | tf_op jit(solution)/shard_map/ppermute | solution.py:473
  175.7 10.7 %collective-permute-start.23 = (f32[3,64,1280]{2,1,0:T(8,128)S(1)}, f32[3,64,1280]{2,1,0:T(8,128)S(1)}, u32[]{:S(2)}, u32[]{:S(2)}) collective-permute-start(f32[3,64,1280]{2,1,0:T(8,128)S(1)} %maximum_select_fusion.3), channel_id=1, source_target_pairs={{0,2},{2,0},{4,6},{6,4},{8,10},{10,8},{12,14},{14,12},{16,18},{18,... | collective-permute-start | bytes 2949128 | tf_op jit(solution)/shard_map/ppermute | solution.py:473
  182.7 2.3 %collective-permute-start.39 = (f32[2,64,1280]{2,1,0:T(8,128)S(1)}, f32[2,64,1280]{2,1,0:T(8,128)}, u32[]{:S(2)}, u32[]{:S(2)}) collective-permute-start(f32[2,64,1280]{2,1,0:T(8,128)S(1)} %maximum_select_fusion.4), channel_id=1, source_target_pairs={{0,2},{2,0},{4,6},{6,4},{8,10},{10,8},{12,14},{14,12},{16,18},{18,... | collective-permute-start | bytes 1966088 | tf_op jit(solution)/shard_map/ppermute | solution.py:473
  (21 other events, 54.9 us)

commit v16 on v15

--- a/solution.py
+++ b/solution.py
@@ -14,7 +14,7 @@
 STEPS = 1
 SUB = 8
 LANE = 128
-VMEM_LIMIT = 28 * 1024 * 1024
+VMEM_LIMIT = 60 * 1024 * 1024
 KERNEL_WORK = 8
 ORDER = ((2, 4, 8), (4, 8, 2))
 AHEAD = ((), (), (0,), (1, 0), (2, 1, 0))
@@ -252,26 +252,34 @@
     return above - below
 
 
-def window_kernel(window, depth, waits, *refs):
+def window_kernel(window, waits, *refs):
     refs = list(refs)
     place_ref, local_ref, remote_ref, table_ref = refs[:4]
     refs = refs[4 + waits :]
     carry_ref = None if window.first else refs.pop(0)
     out_refs = [refs.pop(0) for _ in range(4)]
     carried_ref = None if window.last else refs.pop(0)
-    table, lhs_high, lhs_low, wind, second, third, shift, results, carried, table_sem, out_sems = refs
+    table, mine_buf, theirs_buf, lhs_high, lhs_low, wind, second, third, shift, results, carried, in_sems, out_sems = refs
     band, core, sides = place_ref[0], place_ref[1], (place_ref[2], place_ref[3])
     rows, extended = window.rows, window.extended
 
     def at(pair):
         return multiple(choose(band, pair), SUB)
 
-    tables = pltpu.make_async_copy(table_ref, table, table_sem)
-    tables.start()
+    inputs = [pltpu.make_async_copy(local_ref, mine_buf, in_sems.at[0])]
+    inputs.append(pltpu.make_async_copy(remote_ref, theirs_buf, in_sems.at[1]))
+    tables = pltpu.make_async_copy(table_ref, table, in_sems.at[2])
+    if not window.first:
+        rows_before = wind.at[:, pl.ds(at((extended - 2 * SUB, 0)), 2 * SUB)]
+        inputs.append(pltpu.make_async_copy(carry_ref, rows_before, in_sems.at[3]))
+    for copy in [*inputs, tables]:
+        copy.start()
+    for copy in inputs:
+        copy.wait()
     lane = lax.broadcasted_iota(jnp.int32, (rows, LANE), 1)
     even, odd = [], []
     for c in range(2):
-        mine, theirs = local_ref[c], remote_ref[c]
+        mine, theirs = mine_buf[c], theirs_buf[c]
         low, high = jnp.where(band == 0, mine, theirs), jnp.where(band == 0, theirs, mine)
         low_rest, high_rest = low[:, 4 * LANE :], high[:, 4 * LANE :]
         turn = functools.partial(pltpu.roll, shift=LANE // 2, axis=1)
@@ -283,7 +291,6 @@
         lhs = jnp.concatenate(parts)
         lhs_high[parity] = lhs.astype(jnp.bfloat16)
         lhs_low[parity] = (lhs - lhs_high[parity].astype(jnp.float32)).astype(jnp.bfloat16)
-    tables.wait()
 
     place = at(window.place)
     if window.first or window.last:
@@ -292,9 +299,7 @@
                 wind[c, pl.ds(at((extended - SUB, 0)), SUB), :] = jnp.zeros((SUB, NLON), jnp.float32)
             if window.last:
                 wind[c, pl.ds(at((0, extended - SUB)), SUB), :] = jnp.zeros((SUB, NLON), jnp.float32)
-    if not window.first:
-        for c in range(2):
-            wind[c, pl.ds(at((extended - 2 * SUB, 0)), 2 * SUB), :] = carry_ref[c]
+    tables.wait()
 
     dot = functools.partial(jnp.dot, preferred_element_type=jnp.float32)
     for start in range(0, NLON // 2, 2 * LANE):
@@ -378,30 +383,24 @@
 
 def window_tensor(window, place, local, remote, table, waits, carry):
     depth = local.shape[2]
-    vmem = pl.BlockSpec(memory_space=pltpu.VMEM)
-    in_specs = [
-        pl.BlockSpec(memory_space=pltpu.SMEM),
-        vmem,
-        vmem,
-        pl.BlockSpec(memory_space=pl.ANY),
-    ]
-    in_specs += [pl.BlockSpec(memory_space=pl.ANY)] * len(waits)
     operands = [place, local, remote, table, *waits]
     if not window.first:
-        in_specs.append(vmem)
         operands.append(carry)
+    in_specs = [pl.BlockSpec(memory_space=pltpu.SMEM)] + [pl.BlockSpec(memory_space=pl.ANY)] * (len(operands) - 1)
     out_shape = [jax.ShapeDtypeStruct((3, window.width // 4, NLON), jnp.float32)] * 4
     if not window.last:
         out_shape.append(jax.ShapeDtypeStruct((2, 2 * SUB, NLON), jnp.float32))
     field = pltpu.VMEM((2, window.extended, NLON), jnp.float32)
     lhs_shape = (2, 2 * window.rows, depth)
     out = pl.pallas_call(
-        functools.partial(window_kernel, window, depth, len(waits)),
+        functools.partial(window_kernel, window, len(waits)),
         out_shape=out_shape,
         in_specs=in_specs,
         out_specs=[pl.BlockSpec(memory_space=pl.ANY)] * len(out_shape),
         scratch_shapes=[
             pltpu.VMEM(table.shape, table.dtype),
+            pltpu.VMEM(local.shape, jnp.float32),
+            pltpu.VMEM(local.shape, jnp.float32),
             pltpu.VMEM(lhs_shape, jnp.bfloat16),
             pltpu.VMEM(lhs_shape, jnp.bfloat16),
             field,
@@ -410,7 +409,7 @@
             field,
             pltpu.VMEM((4, 3, window.width // 4, NLON), jnp.float32),
             pltpu.VMEM((2, 2 * SUB, NLON), jnp.float32),
-            pltpu.SemaphoreType.DMA,
+            pltpu.SemaphoreType.DMA((4,)),
             pltpu.SemaphoreType.DMA((5,)),
         ],
         compiler_params=pltpu.CompilerParams(vmem_limit_bytes=VMEM_LIMIT),
@@ -466,8 +465,12 @@
         leaves = passed + passed_more
         return [kept, kept_more, lax.ppermute(leaves, "mem", ways[step])], leaves
 
+    def shared(parts_of, step):
+        total = sum(parts_of)
+        return [total, lax.ppermute(total, "mem", ways[step])], total
+
     def advanced(parts_of, step):
-        return (across if step == 0 else halved)(parts_of, step)
+        return (across if step == 0 else halved if step + 1 < len(ways) else shared)(parts_of, step)
 
     def doubled(part, step):
         beside = lax.ppermute(part, "mem", cores if step < 0 else ways[step])
@@ -475,7 +478,7 @@
         return jnp.where(mine == 0, jnp.concatenate([part, beside], axis=1), jnp.concatenate([beside, part], axis=1))
 
     def gathered(part):
-        for step in range(len(ways) - 1, -2, -1):
+        for step in range(len(ways) - 2, -2, -1):
             part = doubled(part, step)
         return part
 
@@ -502,13 +505,13 @@
     place_of = {}
     for m in range(members):
         for b in range(2):
-            bits = ORDER[m % 2]
+            *bits, last = ORDER[m % 2]
             piece = functools.reduce(lambda value, bit: 2 * value + m // bit % 2, bits, m % 2)
-            place_of[piece, b] = m * 2 + b
-    trades, half = [], members // 2
-    for (piece, b), index in place_of.items():
-        mate = (piece, b) if (piece < half) == (b == 0) else ((piece + half) % members, 1 - b)
-        trades.append((index, place_of[mate]))
+            place_of[piece, m // last % 2, b] = m * 2 + b
+    trades, half = [], members // 4
+    for (piece, twin, b), index in place_of.items():
+        mate = (piece, b) if (piece < half) == (b == 0) else ((piece + half) % (2 * half), 1 - b)
+        trades.append((index, place_of[mate[0], twin, mate[1]]))
     both = lax.ppermute(pieces["both"][0], ("mem", "band"), trades)
 
     early = gathered(jnp.concatenate([other, both[None]]))

time: 191 us -> 202 us (1.058)
  starting transfers between devices: 33.3 us -> 52.5 us
  local copies, waits for them, and re-layouts: 20.8 us -> 6.29 us
  Pallas kernels: 51.4 us -> 60.8 us
  waiting for transfers between devices: 74.6 us -> 68.3 us
  other arithmetic: 9.37 us -> 13.4 us
    ppermute x10 -> x5, waiting for transfers between devices: 41.2 us -> 15.3 us  [halved(): return ([total(mine), lax.ppermute(leaves, 'mem', ways[step])], leaves)]
    ppermute x0 -> x5, waiting for transfers between devices: none -> 24.7 us  [shared(): return ([total, lax.ppermute(total, 'mem', ways[step])], total)]
    unnamed x58 -> x40, local copies, waits for them, and re-layouts: 19.8 us -> 5.22 us
    ppermute x8 -> x6, waiting for transfers between devices: 24.8 us -> 12.1 us  [doubled(): beside = lax.ppermute(part, 'mem', cores if step < 0 else ways[step])]
    ppermute x8 -> x6, starting transfers between devices: 5.16 us -> 14.6 us  [doubled(): beside = lax.ppermute(part, 'mem', cores if step < 0 else ways[step])]
    ppermute x5, waiting for transfers between devices: 0.01 us -> 7.71 us  [across(): return ([kept, kept_more, lax.ppermute(leaves, 'mem', ways[step])], leaves)]
    ppermute x10 -> x5, starting transfers between devices: 9.41 us -> 3.37 us  [halved(): return ([total(mine), lax.ppermute(leaves, 'mem', ways[step])], leaves)]
    ppermute x5, starting transfers between devices: 3.69 us -> 9.65 us  [by_levels(): second = lax.ppermute(quarters[2], 'mem', cores)]
  transfers between devices with their start and end apart: 40 -> 38, of which waited for: 13 -> 11; matrix products, arithmetic and copies ran while one was open for 4% -> 6% of each run, Pallas kernels for 26% -> 29%
where the time goes in v16:
time: 202 us
  waiting for transfers between devices  68.3 us (34%)
  Pallas kernels  60.8 us (30%)
  starting transfers between devices  52.5 us (26%)
  other arithmetic  13.4 us (7%)
  local copies, waits for them, and re-layouts  6.29 us (3%)
    pallas_call x5, Pallas kernels, window_tensor(): pl.pallas_call(functools.partial(window_kernel, window, len(waits)), out_...  50.6 us
    ppermute x5, waiting for transfers between devices, shared(): return ([total, lax.ppermute(total, 'mem', ways[step])], total)  24.7 us
    ppermute x5, waiting for transfers between devices, halved(): return ([total(mine), lax.ppermute(leaves, 'mem', ways[step])], leaves)  15.3 us
    ppermute x6, starting transfers between devices, doubled(): beside = lax.ppermute(part, 'mem', cores if step < 0 else ways[step])  14.6 us
    ppermute x6, waiting for transfers between devices, doubled(): beside = lax.ppermute(part, 'mem', cores if step < 0 else ways[step])  12.1 us
    pallas_call x3, Pallas kernels, pieces_of(): pl.pallas_call(functools.partial(pieces_kernel, windows, slots, count), i...  10.2 us
    ppermute x5, starting transfers between devices, by_levels(): second = lax.ppermute(quarters[2], 'mem', cores)  9.65 us
    ppermute x1, waiting for transfers between devices, by_levels(): remotes = [lax.ppermute(piece, 'band', swap)]  8.36 us
  transfers between devices with their start and end apart: 38, of which 11 were waited for; matrix products, arithmetic and copies ran while one was open for 6% of the time, Pallas kernels for 29%

profile of v16, /device:TPU:0, one launch (start us, length us, event | category | flops | bytes accessed | tf_op | source)
XLA Modules:
  0.0 201.9 jit_solution(2790982322808554517)
XLA Ops:
  0.0 2.6 %pieces_of.4 = f32[2,136,640]{2,1,0:T(8,128)} custom-call(s32[1]{0:T(128)} %bitcast.5.level_ref, f32[2,2,640,640]{3,2,1,0:T(8,128)} %bitcast.25), custom_call_target="tpu_custom_call" | custom-call | bytes 5242880 | tf_op jit(solution)/shard_map/pieces_of/pallas_call | solution.py:209
  2.6 3.0 %collective-permute-start = (f32[2,136,640]{2,1,0:T(8,128)}, f32[2,136,640]{2,1,0:T(8,128)S(1)}, u32[]{:S(2)}, u32[]{:S(2)}) collective-permute-start(f32[2,136,640]{2,1,0:T(8,128)} %pieces_of.4), channel_id=1, source_target_pairs={{0,1},{1,0},{2,3},{3,2},{4,5},{5,4},{6,7},{7,6},{8,9},{9,8},{10,11... | collective-permute-start | bytes 2088968 | tf_op jit(solution)/shard_map/ppermute | solution.py:443
  5.6 3.6 %pieces_of.5 = (f32[2,128,640]{2,1,0:T(8,128)}, f32[2,128,640]{2,1,0:T(8,128)}, f32[2,128,640]{2,1,0:T(8,128)}, f32[2,120,640]{2,1,0:T(8,128)}) custom-call(s32[1]{0:T(128)} %bitcast.5.level_ref, f32[2,2,640,640]{3,2,1,0:T(8,128)} %bitcast.26), custom_call_target="tpu_custom_call" | custom-call | bytes 10485760 | tf_op jit(solution)/shard_map/pieces_of/pallas_call | solution.py:209
  9.4 4.0 %pieces_of.3 = (f32[2,136,640]{2,1,0:T(8,128)}, f32[2,128,640]{2,1,0:T(8,128)}, f32[2,128,640]{2,1,0:T(8,128)}, f32[2,128,640]{2,1,0:T(8,128)}, f32[2,120,640]{2,1,0:T(8,128)}) custom-call(s32[1]{0:T(128)} %bitcast.level_ref, f32[2,2,640,640]{3,2,1,0:T(8,128)} %bitcast.27), custom_call_target="tpu_custom_call" | custom-call | bytes 13107200 | tf_op jit(solution)/shard_map/pieces_of/pallas_call | solution.py:209
  13.9 8.4 %collective-permute-done.refs_2_.refs_1_ = f32[2,136,640]{2,1,0:T(8,128)S(1)} collective-permute-done((f32[2,136,640]{2,1,0:T(8,128)}, f32[2,136,640]{2,1,0:T(8,128)S(1)}, u32[]{:S(2)}, u32[]{:S(2)}) %collective-permute-start) | collective-permute-done | bytes 696352 | tf_op jit(solution)/shard_map/ppermute | solution.py:443
  22.3 0.9 copy-done.2
  23.2 10.3 %window_tensor.5 = (f32[3,32,1280]{2,1,0:T(8,128)}, f32[3,32,1280]{2,1,0:T(8,128)}, f32[3,32,1280]{2,1,0:T(8,128)}, f32[3,32,1280]{2,1,0:T(8,128)}, f32[2,16,1280]{2,1,0:T(8,128)}) custom-call(s32[4]{0:T(128)} %pad_add_fusion.refs_0_, f32[2,136,640]{2,1,0:T(8,128)} %get-tuple-element.38.refs_1_, f32[2,136,640]{2,1,0:T(8,128)} %copy-done.2, ...), custom_call_target="tpu_custom_call" | custom-call | flops 10695475200 | bytes 6635520 | tf_op jit(solution)/shard_map/window_tensor/pallas_call | solution.py:395
  33.6 2.1 %collective-permute-start.13 = (f32[2,128,640]{2,1,0:T(8,128)}, f32[2,128,640]{2,1,0:T(8,128)S(1)}, u32[]{:S(2)}, u32[]{:S(2)}) collective-permute-start(f32[2,128,640]{2,1,0:T(8,128)} %gated.3), channel_id=1, source_target_pairs={{0,1},{1,0},{2,3},{3,2},{4,5},{5,4},{6,7},{7,6},{8,9},{9,8},{10,11... | collective-permute-start | bytes 1966088 | tf_op jit(solution)/shard_map/ppermute | solution.py:447
  36.5 9.9 %window_tensor.6 = (f32[3,32,1280]{2,1,0:T(8,128)}, f32[3,32,1280]{2,1,0:T(8,128)}, f32[3,32,1280]{2,1,0:T(8,128)}, f32[3,32,1280]{2,1,0:T(8,128)}, f32[2,16,1280]{2,1,0:T(8,128)}) custom-call(s32[4]{0:T(128)} %pad_add_fusion.refs_0_, f32[2,128,640]{2,1,0:T(8,128)} %get-tuple-element.43.refs_1_, f32[2,128,640]{2,1,0:T(8,128)} %copy-done.4, ...), custom_call_target="tpu_custom_call" | custom-call | flops 10066329600 | bytes 6553600 | tf_op jit(solution)/shard_map/window_tensor/pallas_call | solution.py:395
  46.7 1.5 collective-permute-start.23
  49.6 1.5 collective-permute-start.3
  51.2 1.9 add.266.refs_4_
  53.9 10.2 %window_tensor.7 = (f32[3,32,1280]{2,1,0:T(8,128)}, f32[3,32,1280]{2,1,0:T(8,128)}, f32[3,32,1280]{2,1,0:T(8,128)}, f32[3,32,1280]{2,1,0:T(8,128)}, f32[2,16,1280]{2,1,0:T(8,128)}) custom-call(s32[4]{0:T(128)} %pad_add_fusion.refs_0_, f32[2,128,640]{2,1,0:T(8,128)} %get-tuple-element.50.refs_1_, f32[2,128,640]{2,1,0:T(8,128)} %copy-done.3, ...), custom_call_target="tpu_custom_call" | custom-call | flops 10066329600 | bytes 6553600 | tf_op jit(solution)/shard_map/window_tensor/pallas_call | solution.py:395
  64.2 1.2 collective-permute-start.29
  66.1 1.6 collective-permute-start.4
  67.7 10.1 %window_tensor.8 = (f32[3,32,1280]{2,1,0:T(8,128)}, f32[3,32,1280]{2,1,0:T(8,128)}, f32[3,32,1280]{2,1,0:T(8,128)}, f32[3,32,1280]{2,1,0:T(8,128)}, f32[2,16,1280]{2,1,0:T(8,128)}) custom-call(s32[4]{0:T(128)} %pad_add_fusion.refs_0_, f32[2,128,640]{2,1,0:T(8,128)} %get-tuple-element.57.refs_1_, f32[2,128,640]{2,1,0:T(8,128)} %collective-permute-done.23.refs_2_, ...), custom_call_target="tpu_custom_call" | custom-call | flops 10066329600 | bytes 6553600 | tf_op jit(solution)/shard_map/window_tensor/pallas_call | solution.py:395
  77.9 0.9 collective-permute-start.14
  79.6 2.1 %add.277.refs_4_ = f32[3,32,1280]{2,1,0:T(8,128)} add(f32[3,32,1280]{2,1,0:T(8,128)} %get-tuple-element.55, f32[3,32,1280]{2,1,0:T(8,128)} %collective-permute-done.15) | non-fusion elementwise | flops 122880 | bytes 1474560 | tf_op jit(solution)/shard_map/add | solution.py:465
  81.7 1.6 collective-permute-start.10
  83.3 1.0 add_add_fusion.4.refs_6_
  84.3 6.2 %collective-permute-done.10 = f32[3,16,1280]{2,1,0:T(8,128)S(1)} collective-permute-done((f32[3,16,1280]{2,1,0:T(8,128)S(1)}, f32[3,16,1280]{2,1,0:T(8,128)S(1)}, u32[]{:S(2)}, u32[]{:S(2)}) %collective-permute-start.10) | collective-permute-done | bytes 245792 | tf_op jit(solution)/shard_map/ppermute | solution.py:461
  90.5 0.9 collective-permute-start.16
  91.6 1.9 collective-permute-start.5
  93.5 10.0 %window_tensor.9 = (f32[3,32,1280]{2,1,0:T(8,128)}, f32[3,32,1280]{2,1,0:T(8,128)}, f32[3,32,1280]{2,1,0:T(8,128)}, f32[3,32,1280]{2,1,0:T(8,128)}) custom-call(s32[4]{0:T(128)} %pad_add_fusion.refs_0_, f32[2,120,640]{2,1,0:T(8,128)} %get-tuple-element.64.refs_1_, f32[2,120,640]{2,1,0:T(8,128)} %collective-permute-done.29.refs_2_, ...), custom_call_target="tpu_custom_call" | custom-call | flops 9437184000 | bytes 6471680 | tf_op jit(solution)/shard_map/window_tensor/pallas_call | solution.py:395
  103.5 1.2 collective-permute-start.11
  104.7 1.0 add_multiply_fusion.4
  105.7 1.1 add.289
  106.8 7.0 %collective-permute-done.11 = f32[3,16,1280]{2,1,0:T(8,128)S(1)} collective-permute-done((f32[3,16,1280]{2,1,0:T(8,128)S(1)}, f32[3,16,1280]{2,1,0:T(8,128)S(1)}, u32[]{:S(2)}, u32[]{:S(2)}) %collective-permute-start.11) | collective-permute-done | bytes 245792 | tf_op jit(solution)/shard_map/ppermute | solution.py:470
  113.8 1.4 collective-permute-start.26
  116.2 6.7 %collective-permute-done.17 = f32[3,16,1280]{2,1,0:T(8,128)S(1)} collective-permute-done((f32[3,16,1280]{2,1,0:T(8,128)S(1)}, f32[3,16,1280]{2,1,0:T(8,128)S(1)}, u32[]{:S(2)}, u32[]{:S(2)}) %collective-permute-start.17) | collective-permute-done | bytes 245792 | tf_op jit(solution)/shard_map/ppermute | solution.py:461
  123.0 1.0 add_add_fusion.2
  124.4 2.0 collective-permute-start.12
  126.3 6.7 %collective-permute-done.18 = f32[3,16,1280]{2,1,0:T(8,128)S(1)} collective-permute-done((f32[3,16,1280]{2,1,0:T(8,128)S(1)}, f32[3,16,1280]{2,1,0:T(8,128)S(1)}, u32[]{:S(2)}, u32[]{:S(2)}) %collective-permute-start.18) | collective-permute-done | bytes 245792 | tf_op jit(solution)/shard_map/ppermute | solution.py:470
  133.1 0.9 collective-permute-start.19
  134.2 8.2 %collective-permute-start.30 = (f32[3,32,1280]{2,1,0:T(8,128)}, f32[3,32,1280]{2,1,0:T(8,128)S(1)}, u32[]{:S(2)}, u32[]{:S(2)}) collective-permute-start(f32[3,32,1280]{2,1,0:T(8,128)} %get-tuple-element.68), channel_id=1, source_target_pairs={{0,2},{2,0},{4,6},{6,4},{8,10},{10,8},{12,14},{14,12},{16,18},{18,... | collective-permute-start | bytes 1474568 | tf_op jit(solution)/shard_map/ppermute | solution.py:495
  142.4 1.1 add.300
  143.5 3.4 %collective-permute-start.32 = (f32[3,32,1280]{2,1,0:T(8,128)S(1)}, f32[3,32,1280]{2,1,0:T(8,128)S(1)}, u32[]{:S(2)}, u32[]{:S(2)}) collective-permute-start(f32[3,32,1280]{2,1,0:T(8,128)S(1)} %add.300), channel_id=1, source_target_pairs={{0,4},{2,10},{4,0},{6,14},{8,12},{10,2},{12,8},{14,6},{16,20},{18,... | collective-permute-start | bytes 1474568 | tf_op jit(solution)/shard_map/ppermute | solution.py:466
  147.7 7.7 %collective-permute-done.32 = f32[3,32,1280]{2,1,0:T(8,128)S(1)} collective-permute-done((f32[3,32,1280]{2,1,0:T(8,128)S(1)}, f32[3,32,1280]{2,1,0:T(8,128)S(1)}, u32[]{:S(2)}, u32[]{:S(2)}) %collective-permute-start.32) | collective-permute-done | bytes 491552 | tf_op jit(solution)/shard_map/ppermute | solution.py:466
  155.5 5.7 %collective-permute-done.20 = f32[3,16,1280]{2,1,0:T(8,128)S(1)} collective-permute-done((f32[3,16,1280]{2,1,0:T(8,128)S(1)}, f32[3,16,1280]{2,1,0:T(8,128)S(1)}, u32[]{:S(2)}, u32[]{:S(2)}) %collective-permute-start.20) | collective-permute-done | bytes 245792 | tf_op jit(solution)/shard_map/ppermute | solution.py:476
  161.6 2.3 %collective-permute-done.33 = f32[3,16,1280]{2,1,0:T(8,128)S(1)} collective-permute-done((f32[3,16,1280]{2,1,0:T(8,128)S(1)}, f32[3,16,1280]{2,1,0:T(8,128)S(1)}, u32[]{:S(2)}, u32[]{:S(2)}) %collective-permute-start.33) | collective-permute-done | bytes 245792 | tf_op jit(solution)/shard_map/ppermute | solution.py:461
  163.9 1.8 collective-permute-start.34
  165.8 11.1 %collective-permute-done.34 = f32[3,16,1280]{2,1,0:T(8,128)S(1)} collective-permute-done((f32[3,16,1280]{2,1,0:T(8,128)S(1)}, f32[3,16,1280]{2,1,0:T(8,128)S(1)}, u32[]{:S(2)}, u32[]{:S(2)}) %collective-permute-start.34) | collective-permute-done | bytes 245792 | tf_op jit(solution)/shard_map/ppermute | solution.py:470
  177.8 4.7 %collective-permute-done.35 = f32[2,16,1280]{2,1,0:T(8,128)S(1)} collective-permute-done((f32[2,16,1280]{2,1,0:T(8,128)S(1)}, f32[2,16,1280]{2,1,0:T(8,128)S(1)}, u32[]{:S(2)}, u32[]{:S(2)}) %collective-permute-start.35) | collective-permute-done | bytes 163872 | tf_op jit(solution)/shard_map/ppermute | solution.py:476
  182.4 2.8 %collective-permute-start.36 = (f32[2,32,1280]{2,1,0:T(8,128)S(1)}, f32[2,32,1280]{2,1,0:T(8,128)S(1)}, u32[]{:S(2)}, u32[]{:S(2)}) collective-permute-start(f32[2,32,1280]{2,1,0:T(8,128)S(1)} %maximum_select_fusion.6), channel_id=1, source_target_pairs={{0,4},{2,10},{4,0},{6,14},{8,12},{10,2},{12,8},{14,6},{16,20},{18,... | collective-permute-start | bytes 983048 | tf_op jit(solution)/shard_map/ppermute | solution.py:476
  185.3 5.0 %collective-permute-start.22 = (f32[3,64,1280]{2,1,0:T(8,128)S(1)}, f32[3,64,1280]{2,1,0:T(8,128)S(1)}, u32[]{:S(2)}, u32[]{:S(2)}) collective-permute-start(f32[3,64,1280]{2,1,0:T(8,128)S(1)} %maximum_select_fusion.3), channel_id=1, source_target_pairs={{0,2},{2,0},{4,6},{6,4},{8,10},{10,8},{12,14},{14,12},{16,18},{18,... | collective-permute-start | bytes 2949128 | tf_op jit(solution)/shard_map/ppermute | solution.py:476
  190.4 5.8 %collective-permute-start.37 = (f32[2,64,1280]{2,1,0:T(8,128)S(1)}, f32[2,64,1280]{2,1,0:T(8,128)S(1)}, u32[]{:S(2)}, u32[]{:S(2)}) collective-permute-start(f32[2,64,1280]{2,1,0:T(8,128)S(1)} %maximum_select_fusion.4), channel_id=1, source_target_pairs={{0,2},{2,0},{4,6},{6,4},{8,10},{10,8},{12,14},{14,12},{16,18},{18,... | collective-permute-start | bytes 1966088 | tf_op jit(solution)/shard_map/ppermute | solution.py:476
  196.2 1.7 collective-permute-done.37
  199.3 1.7 copy-done
  (120 shorter events, 11.9 us)
Async XLA Ops:
  2.6 19.6 %collective-permute-start = (f32[2,136,640]{2,1,0:T(8,128)}, f32[2,136,640]{2,1,0:T(8,128)S(1)}, u32[]{:S(2)}, u32[]{:S(2)}) collective-permute-start(f32[2,136,640]{2,1,0:T(8,128)} %pieces_of.4), channel_id=1, source_target_pairs={{0,1},{1,0},{2,3},{3,2},{4,5},{5,4},{6,7},{7,6},{8,9},{9,8},{10,11... | collective-permute-start | bytes 2088968 | tf_op jit(solution)/shard_map/ppermute | solution.py:443
  9.2 26.5 %collective-permute-start.6 = (f32[2,128,640]{2,1,0:T(8,128)}, f32[2,128,640]{2,1,0:T(8,128)S(1)}, u32[]{:S(2)}, u32[]{:S(2)}) collective-permute-start(f32[2,128,640]{2,1,0:T(8,128)} %get-tuple-element.44), channel_id=1, source_target_pairs={{0,1},{1,0},{2,3},{3,2},{4,5},{5,4},{6,7},{7,6},{8,9},{9,8},{10,11... | collective-permute-start | bytes 1966088 | tf_op jit(solution)/shard_map/ppermute | solution.py:447
  33.5 14.8 %collective-permute-start.2 = (f32[3,32,1280]{2,1,0:T(8,128)}, f32[3,32,1280]{2,1,0:T(8,128)S(1)}, u32[]{:S(2)}, u32[]{:S(2)}) collective-permute-start(f32[3,32,1280]{2,1,0:T(8,128)} %get-tuple-element.42), channel_id=1, source_target_pairs={{0,2},{2,0},{4,6},{6,4},{8,10},{10,8},{12,14},{14,12},{16,18},{18,... | collective-permute-start | bytes 1474568 | tf_op jit(solution)/shard_map/ppermute | solution.py:494
  33.6 19.5 %collective-permute-start.13 = (f32[2,128,640]{2,1,0:T(8,128)}, f32[2,128,640]{2,1,0:T(8,128)S(1)}, u32[]{:S(2)}, u32[]{:S(2)}) collective-permute-start(f32[2,128,640]{2,1,0:T(8,128)} %gated.3), channel_id=1, source_target_pairs={{0,1},{1,0},{2,3},{3,2},{4,5},{5,4},{6,7},{7,6},{8,9},{9,8},{10,11... | collective-permute-start | bytes 1966088 | tf_op jit(solution)/shard_map/ppermute | solution.py:447
  46.5 3.1 %collective-permute-start.8 = (f32[3,32,1280]{2,1,0:T(8,128)}, f32[3,32,1280]{2,1,0:T(8,128)}, u32[]{:S(2)}, u32[]{:S(2)}) collective-permute-start(f32[3,32,1280]{2,1,0:T(8,128)} %get-tuple-element.49), channel_id=1, source_target_pairs={{0,2},{2,0},{4,6},{6,4},{8,10},{10,8},{12,14},{14,12},{16,18},{18,... | collective-permute-start | bytes 1474568 | tf_op jit(solution)/shard_map/ppermute | solution.py:494
  46.7 19.4 %collective-permute-start.23 = (f32[2,128,640]{2,1,0:T(8,128)}, f32[2,128,640]{2,1,0:T(8,128)}, u32[]{:S(2)}, u32[]{:S(2)}) collective-permute-start(f32[2,128,640]{2,1,0:T(8,128)} %gated.4), channel_id=1, source_target_pairs={{0,1},{1,0},{2,3},{3,2},{4,5},{5,4},{6,7},{7,6},{8,9},{9,8},{10,11... | collective-permute-start | bytes 1966088 | tf_op jit(solution)/shard_map/ppermute | solution.py:447
  48.3 15.9 %collective-permute-start.1 = (f32[3,32,1280]{2,1,0:T(8,128)}, f32[3,32,1280]{2,1,0:T(8,128)S(1)}, u32[]{:S(2)}, u32[]{:S(2)}) collective-permute-start(f32[3,32,1280]{2,1,0:T(8,128)} %get-tuple-element.40), channel_id=1, source_target_pairs={{0,2},{2,0},{4,6},{6,4},{8,10},{10,8},{12,14},{14,12},{16,18},{18,... | collective-permute-start | bytes 1474568 | tf_op jit(solution)/shard_map/ppermute | solution.py:495
  48.3 29.5 %collective-permute-start.7 = (f32[3,32,1280]{2,1,0:T(8,128)}, f32[3,32,1280]{2,1,0:T(8,128)S(1)}, u32[]{:S(2)}, u32[]{:S(2)}) collective-permute-start(f32[3,32,1280]{2,1,0:T(8,128)} %get-tuple-element.47), channel_id=1, source_target_pairs={{0,2},{2,0},{4,6},{6,4},{8,10},{10,8},{12,14},{14,12},{16,18},{18,... | collective-permute-start | bytes 1474568 | tf_op jit(solution)/shard_map/ppermute | solution.py:495
  49.6 14.6 %collective-permute-start.3 = (f32[3,32,1280]{2,1,0:T(8,128)}, f32[3,32,1280]{2,1,0:T(8,128)S(1)}, u32[]{:S(2)}, u32[]{:S(2)}) collective-permute-start(f32[3,32,1280]{2,1,0:T(8,128)} %add.254.refs_4_), channel_id=1, source_target_pairs={{0,4},{2,10},{4,0},{6,14},{8,12},{10,2},{12,8},{14,6},{16,20},{18,... | collective-permute-start | bytes 1474568 | tf_op jit(solution)/shard_map/ppermute | solution.py:466
  53.0 25.8 %collective-permute-start.9 = (f32[3,32,1280]{2,1,0:T(8,128)}, f32[3,32,1280]{2,1,0:T(8,128)S(1)}, u32[]{:S(2)}, u32[]{:S(2)}) collective-permute-start(f32[3,32,1280]{2,1,0:T(8,128)} %add.266.refs_4_), channel_id=1, source_target_pairs={{0,4},{2,10},{4,0},{6,14},{8,12},{10,2},{12,8},{14,6},{16,20},{18,... | collective-permute-start | bytes 1474568 | tf_op jit(solution)/shard_map/ppermute | solution.py:466
  64.1 14.9 %collective-permute-start.15 = (f32[3,32,1280]{2,1,0:T(8,128)}, f32[3,32,1280]{2,1,0:T(8,128)}, u32[]{:S(2)}, u32[]{:S(2)}) collective-permute-start(f32[3,32,1280]{2,1,0:T(8,128)} %get-tuple-element.56), channel_id=1, source_target_pairs={{0,2},{2,0},{4,6},{6,4},{8,10},{10,8},{12,14},{14,12},{16,18},{18,... | collective-permute-start | bytes 1474568 | tf_op jit(solution)/shard_map/ppermute | solution.py:494
  64.2 13.7 %copy-start.16 = (f32[3,32,1280]{2,1,0:T(8,128)}, f32[3,32,1280]{2,1,0:T(8,128)S(1)}, u32[]{:S(2)}) copy-start(f32[3,32,1280]{2,1,0:T(8,128)S(1)} %collective-permute-done.3) | copy-start | bytes 1474564
  64.2 27.3 %collective-permute-start.29 = (f32[2,120,640]{2,1,0:T(8,128)}, f32[2,120,640]{2,1,0:T(8,128)}, u32[]{:S(2)}, u32[]{:S(2)}) collective-permute-start(f32[2,120,640]{2,1,0:T(8,128)} %gated.5), channel_id=1, source_target_pairs={{0,1},{1,0},{2,3},{3,2},{4,5},{5,4},{6,7},{7,6},{8,9},{9,8},{10,11... | collective-permute-start | bytes 1843208 | tf_op jit(solution)/shard_map/ppermute | solution.py:447
  66.1 15.6 %collective-permute-start.4 = (f32[3,16,1280]{2,1,0:T(8,128)}, f32[3,16,1280]{2,1,0:T(8,128)}, u32[]{:S(2)}, u32[]{:S(2)}) collective-permute-start(f32[3,16,1280]{2,1,0:T(8,128)} %dynamic-slice_add_fusion.4.refs_5_), channel_id=1, source_target_pairs={{0,8},{2,18},{4,12},{6,22},{8,0},{10,26},{12,4},{14,30},{16,24},{1... | collective-permute-start | bytes 737288 | tf_op jit(solution)/shard_map/ppermute | solution.py:461
  67.7 11.2 %copy-start.6 = (f32[3,32,1280]{2,1,0:T(8,128)S(1)}, f32[3,32,1280]{2,1,0:T(8,128)}, u32[]{:S(2)}) copy-start(f32[3,32,1280]{2,1,0:T(8,128)} %get-tuple-element.46) | copy-start | bytes 1474564
  77.9 37.3 %collective-permute-start.14 = (f32[3,32,1280]{2,1,0:T(8,128)}, f32[3,32,1280]{2,1,0:T(8,128)S(1)}, u32[]{:S(2)}, u32[]{:S(2)}) collective-permute-start(f32[3,32,1280]{2,1,0:T(8,128)} %get-tuple-element.54), channel_id=1, source_target_pairs={{0,2},{2,0},{4,6},{6,4},{8,10},{10,8},{12,14},{14,12},{16,18},{18,... | collective-permute-start | bytes 1474568 | tf_op jit(solution)/shard_map/ppermute | solution.py:495
  78.8 26.8 %collective-permute-start.25 = (f32[3,32,1280]{2,1,0:T(8,128)}, f32[3,32,1280]{2,1,0:T(8,128)}, u32[]{:S(2)}, u32[]{:S(2)}) collective-permute-start(f32[3,32,1280]{2,1,0:T(8,128)} %get-tuple-element.63), channel_id=1, source_target_pairs={{0,2},{2,0},{4,6},{6,4},{8,10},{10,8},{12,14},{14,12},{16,18},{18,... | collective-permute-start | bytes 1474568 | tf_op jit(solution)/shard_map/ppermute | solution.py:494
  79.0 12.6 %copy-start.19 = (f32[3,16,1280]{2,1,0:T(8,128)}, f32[3,16,1280]{2,1,0:T(8,128)S(1)}, u32[]{:S(2)}) copy-start(f32[3,16,1280]{2,1,0:T(8,128)S(1)} %dynamic-slice_add_fusion.3.refs_5_) | copy-start | bytes 737284
  79.6 11.9 %copy-start.14 = (f32[3,32,1280]{2,1,0:T(8,128)S(1)}, f32[3,32,1280]{2,1,0:T(8,128)}, u32[]{:S(2)}) copy-start(f32[3,32,1280]{2,1,0:T(8,128)} %copy-done.13) | copy-start | bytes 1474564
  79.6 54.4 %collective-permute-start.24 = (f32[3,32,1280]{2,1,0:T(8,128)}, f32[3,32,1280]{2,1,0:T(8,128)S(1)}, u32[]{:S(2)}, u32[]{:S(2)}) collective-permute-start(f32[3,32,1280]{2,1,0:T(8,128)} %get-tuple-element.61), channel_id=1, source_target_pairs={{0,2},{2,0},{4,6},{6,4},{8,10},{10,8},{12,14},{14,12},{16,18},{18,... | collective-permute-start | bytes 1474568 | tf_op jit(solution)/shard_map/ppermute | solution.py:495
  81.7 8.8 %collective-permute-start.10 = (f32[3,16,1280]{2,1,0:T(8,128)S(1)}, f32[3,16,1280]{2,1,0:T(8,128)S(1)}, u32[]{:S(2)}, u32[]{:S(2)}) collective-permute-start(f32[3,16,1280]{2,1,0:T(8,128)S(1)} %dynamic-slice_add_fusion.3.refs_5_), channel_id=1, source_target_pairs={{0,8},{2,18},{4,12},{6,22},{8,0},{10,26},{12,4},{14,30},{16,24},{1... | collective-permute-start | bytes 737288 | tf_op jit(solution)/shard_map/ppermute | solution.py:461
  84.3 9.2 %copy-start.1 = (f32[3,16,1280]{2,1,0:T(8,128)}, f32[3,16,1280]{2,1,0:T(8,128)S(1)}, u32[]{:S(2)}) copy-start(f32[3,16,1280]{2,1,0:T(8,128)S(1)} %add_add_fusion.4.refs_6_) | copy-start | bytes 737284
  90.5 24.7 %collective-permute-start.16 = (f32[3,32,1280]{2,1,0:T(8,128)}, f32[3,32,1280]{2,1,0:T(8,128)S(1)}, u32[]{:S(2)}, u32[]{:S(2)}) collective-permute-start(f32[3,32,1280]{2,1,0:T(8,128)} %add.277.refs_4_), channel_id=1, source_target_pairs={{0,4},{2,10},{4,0},{6,14},{8,12},{10,2},{12,8},{14,6},{16,20},{18,... | collective-permute-start | bytes 1474568 | tf_op jit(solution)/shard_map/ppermute | solution.py:466
  91.6 11.9 %collective-permute-start.5 = (f32[3,16,1280]{2,1,0:T(8,128)S(1)}, f32[3,16,1280]{2,1,0:T(8,128)S(1)}, u32[]{:S(2)}, u32[]{:S(2)}) collective-permute-start(f32[3,16,1280]{2,1,0:T(8,128)S(1)} %add_add_fusion.4.refs_6_), channel_id=1, source_target_pairs={{0,16},{2,6},{4,20},{6,2},{8,24},{10,14},{12,28},{14,10},{16,0},{1... | collective-permute-start | bytes 737288 | tf_op jit(solution)/shard_map/ppermute | solution.py:470
  93.5 12.3 %copy-start.15 = (f32[3,32,1280]{2,1,0:T(8,128)S(1)}, f32[3,32,1280]{2,1,0:T(8,128)}, u32[]{:S(2)}) copy-start(f32[3,32,1280]{2,1,0:T(8,128)} %get-tuple-element.62) | copy-start | bytes 1474564
  103.5 12.5 %copy-start.9 = (f32[3,32,1280]{2,1,0:T(8,128)S(1)}, f32[3,32,1280]{2,1,0:T(8,128)}, u32[]{:S(2)}) copy-start(f32[3,32,1280]{2,1,0:T(8,128)} %get-tuple-element.53) | copy-start | bytes 1474564
  103.5 10.3 %collective-permute-start.11 = (f32[3,16,1280]{2,1,0:T(8,128)S(1)}, f32[3,16,1280]{2,1,0:T(8,128)S(1)}, u32[]{:S(2)}, u32[]{:S(2)}) collective-permute-start(f32[3,16,1280]{2,1,0:T(8,128)S(1)} %add_add_fusion.3), channel_id=1, source_target_pairs={{0,16},{2,6},{4,20},{6,2},{8,24},{10,14},{12,28},{14,10},{16,0},{1... | collective-permute-start | bytes 737288 | tf_op jit(solution)/shard_map/ppermute | solution.py:470
  105.6 36.8 %collective-permute-start.31 = (f32[3,32,1280]{2,1,0:T(8,128)}, f32[3,32,1280]{2,1,0:T(8,128)}, u32[]{:S(2)}, u32[]{:S(2)}) collective-permute-start(f32[3,32,1280]{2,1,0:T(8,128)} %get-tuple-element.70), channel_id=1, source_target_pairs={{0,2},{2,0},{4,6},{6,4},{8,10},{10,8},{12,14},{14,12},{16,18},{18,... | collective-permute-start | bytes 1474568 | tf_op jit(solution)/shard_map/ppermute | solution.py:494
  113.8 20.3 %collective-permute-start.26 = (f32[3,32,1280]{2,1,0:T(8,128)S(1)}, f32[3,32,1280]{2,1,0:T(8,128)S(1)}, u32[]{:S(2)}, u32[]{:S(2)}) collective-permute-start(f32[3,32,1280]{2,1,0:T(8,128)S(1)} %add.289), channel_id=1, source_target_pairs={{0,4},{2,10},{4,0},{6,14},{8,12},{10,2},{12,8},{14,6},{16,20},{18,... | collective-permute-start | bytes 1474568 | tf_op jit(solution)/shard_map/ppermute | solution.py:466
  116.1 18.0 %copy-start.7 = (f32[3,32,1280]{2,1,0:T(8,128)S(1)}, f32[3,32,1280]{2,1,0:T(8,128)}, u32[]{:S(2)}) copy-start(f32[3,32,1280]{2,1,0:T(8,128)} %get-tuple-element.60) | copy-start | bytes 1474564
  116.1 6.9 %collective-permute-start.17 = (f32[3,16,1280]{2,1,0:T(8,128)S(1)}, f32[3,16,1280]{2,1,0:T(8,128)S(1)}, u32[]{:S(2)}, u32[]{:S(2)}) collective-permute-start(f32[3,16,1280]{2,1,0:T(8,128)S(1)} %dynamic-slice_add_fusion.2), channel_id=1, source_target_pairs={{0,8},{2,18},{4,12},{6,22},{8,0},{10,26},{12,4},{14,30},{16,24},{1... | collective-permute-start | bytes 737288 | tf_op jit(solution)/shard_map/ppermute | solution.py:461
  124.0 18.4 %copy-start.11 = (f32[3,32,1280]{2,1,0:T(8,128)S(1)}, f32[3,32,1280]{2,1,0:T(8,128)}, u32[]{:S(2)}) copy-start(f32[3,32,1280]{2,1,0:T(8,128)} %get-tuple-element.69) | copy-start | bytes 1474564
  124.0 9.0 %collective-permute-start.18 = (f32[3,16,1280]{2,1,0:T(8,128)S(1)}, f32[3,16,1280]{2,1,0:T(8,128)S(1)}, u32[]{:S(2)}, u32[]{:S(2)}) collective-permute-start(f32[3,16,1280]{2,1,0:T(8,128)S(1)} %add_add_fusion.2), channel_id=1, source_target_pairs={{0,16},{2,6},{4,20},{6,2},{8,24},{10,14},{12,28},{14,10},{16,0},{1... | collective-permute-start | bytes 737288 | tf_op jit(solution)/shard_map/ppermute | solution.py:470
  124.4 22.6 %collective-permute-start.12 = (f32[2,16,1280]{2,1,0:T(8,128)S(1)}, f32[2,16,1280]{2,1,0:T(8,128)S(1)}, u32[]{:S(2)}, u32[]{:S(2)}) collective-permute-start(f32[2,16,1280]{2,1,0:T(8,128)S(1)} %pad_maximum_fusion.1), channel_id=1, source_target_pairs={{0,1},{1,0},{2,3},{3,2},{4,5},{5,4},{6,7},{7,6},{8,9},{9,8},{10,11... | collective-permute-start | bytes 491528 | tf_op jit(solution)/shard_map/ppermute | solution.py:504
  133.1 13.8 %collective-permute-start.19 = (f32[16,1280]{1,0:T(8,128)S(1)}, f32[16,1280]{1,0:T(8,128)S(1)}, u32[]{:S(2)}, u32[]{:S(2)}) collective-permute-start(f32[16,1280]{1,0:T(8,128)S(1)} %fusion.18), channel_id=1, source_target_pairs={{0,0},{1,2},{2,1},{3,3},{4,4},{5,10},{6,17},{7,7},{8,8},{9,18},{10... | collective-permute-start | bytes 245768 | tf_op jit(solution)/shard_map/ppermute | solution.py:515
  134.1 21.2 %copy-start.8 = (f32[3,32,1280]{2,1,0:T(8,128)S(1)}, f32[3,32,1280]{2,1,0:T(8,128)}, u32[]{:S(2)}) copy-start(f32[3,32,1280]{2,1,0:T(8,128)} %get-tuple-element.67) | copy-start | bytes 1474564
  134.1 12.9 %collective-permute-start.27 = (f32[3,16,1280]{2,1,0:T(8,128)S(1)}, f32[3,16,1280]{2,1,0:T(8,128)S(1)}, u32[]{:S(2)}, u32[]{:S(2)}) collective-permute-start(f32[3,16,1280]{2,1,0:T(8,128)S(1)} %dynamic-slice_add_fusion.1), channel_id=1, source_target_pairs={{0,8},{2,18},{4,12},{6,22},{8,0},{10,26},{12,4},{14,30},{16,24},{1... | collective-permute-start | bytes 737288 | tf_op jit(solution)/shard_map/ppermute | solution.py:461
  134.2 13.4 %collective-permute-start.30 = (f32[3,32,1280]{2,1,0:T(8,128)}, f32[3,32,1280]{2,1,0:T(8,128)S(1)}, u32[]{:S(2)}, u32[]{:S(2)}) collective-permute-start(f32[3,32,1280]{2,1,0:T(8,128)} %get-tuple-element.68), channel_id=1, source_target_pairs={{0,2},{2,0},{4,6},{6,4},{8,10},{10,8},{12,14},{14,12},{16,18},{18,... | collective-permute-start | bytes 1474568 | tf_op jit(solution)/shard_map/ppermute | solution.py:495
  143.5 11.9 %collective-permute-start.32 = (f32[3,32,1280]{2,1,0:T(8,128)S(1)}, f32[3,32,1280]{2,1,0:T(8,128)S(1)}, u32[]{:S(2)}, u32[]{:S(2)}) collective-permute-start(f32[3,32,1280]{2,1,0:T(8,128)S(1)} %add.300), channel_id=1, source_target_pairs={{0,4},{2,10},{4,0},{6,14},{8,12},{10,2},{12,8},{14,6},{16,20},{18,... | collective-permute-start | bytes 1474568 | tf_op jit(solution)/shard_map/ppermute | solution.py:466
  147.0 14.3 %collective-permute-start.20 = (f32[3,16,1280]{2,1,0:T(8,128)S(1)}, f32[3,16,1280]{2,1,0:T(8,128)S(1)}, u32[]{:S(2)}, u32[]{:S(2)}) collective-permute-start(f32[3,16,1280]{2,1,0:T(8,128)S(1)} %pad_maximum_fusion), channel_id=1, source_target_pairs={{0,8},{2,18},{4,12},{6,22},{8,0},{10,26},{12,4},{14,30},{16,24},{1... | collective-permute-start | bytes 737288 | tf_op jit(solution)/shard_map/ppermute | solution.py:476
  147.1 14.4 %collective-permute-start.28 = (f32[3,16,1280]{2,1,0:T(8,128)S(1)}, f32[3,16,1280]{2,1,0:T(8,128)S(1)}, u32[]{:S(2)}, u32[]{:S(2)}) collective-permute-start(f32[3,16,1280]{2,1,0:T(8,128)S(1)} %add_add_fusion.1), channel_id=1, source_target_pairs={{0,16},{2,6},{4,20},{6,2},{8,24},{10,14},{12,28},{14,10},{16,0},{1... | collective-permute-start | bytes 737288 | tf_op jit(solution)/shard_map/ppermute | solution.py:470
  155.4 8.4 %collective-permute-start.33 = (f32[3,16,1280]{2,1,0:T(8,128)S(1)}, f32[3,16,1280]{2,1,0:T(8,128)S(1)}, u32[]{:S(2)}, u32[]{:S(2)}) collective-permute-start(f32[3,16,1280]{2,1,0:T(8,128)S(1)} %dynamic-slice_add_fusion), channel_id=1, source_target_pairs={{0,8},{2,18},{4,12},{6,22},{8,0},{10,26},{12,4},{14,30},{16,24},{1... | collective-permute-start | bytes 737288 | tf_op jit(solution)/shard_map/ppermute | solution.py:461
  161.3 24.0 %collective-permute-start.21 = (f32[3,32,1280]{2,1,0:T(8,128)S(1)}, f32[3,32,1280]{2,1,0:T(8,128)S(1)}, u32[]{:S(2)}, u32[]{:S(2)}) collective-permute-start(f32[3,32,1280]{2,1,0:T(8,128)S(1)} %maximum_select_fusion.5), channel_id=1, source_target_pairs={{0,4},{2,10},{4,0},{6,14},{8,12},{10,2},{12,8},{14,6},{16,20},{18,... | collective-permute-start | bytes 1474568 | tf_op jit(solution)/shard_map/ppermute | solution.py:476
  163.9 13.0 %collective-permute-start.34 = (f32[3,16,1280]{2,1,0:T(8,128)S(1)}, f32[3,16,1280]{2,1,0:T(8,128)S(1)}, u32[]{:S(2)}, u32[]{:S(2)}) collective-permute-start(f32[3,16,1280]{2,1,0:T(8,128)S(1)} %add_add_fusion), channel_id=1, source_target_pairs={{0,16},{2,6},{4,20},{6,2},{8,24},{10,14},{12,28},{14,10},{16,0},{1... | collective-permute-start | bytes 737288 | tf_op jit(solution)/shard_map/ppermute | solution.py:470
  177.0 5.4 %collective-permute-start.35 = (f32[2,16,1280]{2,1,0:T(8,128)S(1)}, f32[2,16,1280]{2,1,0:T(8,128)S(1)}, u32[]{:S(2)}, u32[]{:S(2)}) collective-permute-start(f32[2,16,1280]{2,1,0:T(8,128)S(1)} %pad_maximum_fusion.2), channel_id=1, source_target_pairs={{0,8},{2,18},{4,12},{6,22},{8,0},{10,26},{12,4},{14,30},{16,24},{1... | collective-permute-start | bytes 491528 | tf_op jit(solution)/shard_map/ppermute | solution.py:476
  182.4 7.9 %collective-permute-start.36 = (f32[2,32,1280]{2,1,0:T(8,128)S(1)}, f32[2,32,1280]{2,1,0:T(8,128)S(1)}, u32[]{:S(2)}, u32[]{:S(2)}) collective-permute-start(f32[2,32,1280]{2,1,0:T(8,128)S(1)} %maximum_select_fusion.6), channel_id=1, source_target_pairs={{0,4},{2,10},{4,0},{6,14},{8,12},{10,2},{12,8},{14,6},{16,20},{18,... | collective-permute-start | bytes 983048 | tf_op jit(solution)/shard_map/ppermute | solution.py:476
  185.3 12.7 %collective-permute-start.22 = (f32[3,64,1280]{2,1,0:T(8,128)S(1)}, f32[3,64,1280]{2,1,0:T(8,128)S(1)}, u32[]{:S(2)}, u32[]{:S(2)}) collective-permute-start(f32[3,64,1280]{2,1,0:T(8,128)S(1)} %maximum_select_fusion.3), channel_id=1, source_target_pairs={{0,2},{2,0},{4,6},{6,4},{8,10},{10,8},{12,14},{14,12},{16,18},{18,... | collective-permute-start | bytes 2949128 | tf_op jit(solution)/shard_map/ppermute | solution.py:476
  190.4 7.5 %collective-permute-start.37 = (f32[2,64,1280]{2,1,0:T(8,128)S(1)}, f32[2,64,1280]{2,1,0:T(8,128)S(1)}, u32[]{:S(2)}, u32[]{:S(2)}) collective-permute-start(f32[2,64,1280]{2,1,0:T(8,128)S(1)} %maximum_select_fusion.4), channel_id=1, source_target_pairs={{0,2},{2,0},{4,6},{6,4},{8,10},{10,8},{12,14},{14,12},{16,18},{18,... | collective-permute-start | bytes 1966088 | tf_op jit(solution)/shard_map/ppermute | solution.py:476
  (10 other events, 19.3 us)

commit v17 on v15

--- a/solution.py
+++ b/solution.py
@@ -14,10 +14,11 @@
 STEPS = 1
 SUB = 8
 LANE = 128
-VMEM_LIMIT = 28 * 1024 * 1024
+VMEM_LIMIT = 60 * 1024 * 1024
 KERNEL_WORK = 8
 ORDER = ((2, 4, 8), (4, 8, 2))
-AHEAD = ((), (), (0,), (1, 0), (2, 1, 0))
+BATCHES = ((0, 1, 2), (3, 4))
+AHEAD = ((), (), (), (), (0,))
 
 
 def padded(cells, sides, width):
@@ -252,10 +253,10 @@
     return above - below
 
 
-def window_kernel(window, depth, waits, *refs):
+def window_kernel(window, slot, waits, *refs):
     refs = list(refs)
     place_ref, local_ref, remote_ref, table_ref = refs[:4]
-    refs = refs[4 + waits :]
+    refs = refs[4 + waits + (len(QUARTERS) if slot else 0) :]
     carry_ref = None if window.first else refs.pop(0)
     out_refs = [refs.pop(0) for _ in range(4)]
     carried_ref = None if window.last else refs.pop(0)
@@ -365,7 +366,7 @@
     for n, (a, b) in reversed(list(enumerate(QUARTERS))):
         side = sides[a]
         entries(results.at[n], (2 * (core + a - 2 * core * a) + (side + b - 2 * side * b)) * quarter)
-        copies.append(pltpu.make_async_copy(results.at[n], out_refs[n], out_sems.at[n]))
+        copies.append(pltpu.make_async_copy(results.at[n], out_refs[n].at[slot], out_sems.at[n]))
         copies[-1].start()
     for copy in copies:
         copy.wait()
@@ -376,7 +377,7 @@
 QUARTERS = ((0, 0), (0, 1), (1, 0), (1, 1))
 
 
-def window_tensor(window, place, local, remote, table, waits, carry):
+def window_tensor(window, slot, slots, place, local, remote, table, made, waits, carry):
     depth = local.shape[2]
     vmem = pl.BlockSpec(memory_space=pltpu.VMEM)
     in_specs = [
@@ -387,16 +388,21 @@
     ]
     in_specs += [pl.BlockSpec(memory_space=pl.ANY)] * len(waits)
     operands = [place, local, remote, table, *waits]
+    aliases = {}
+    if slot:
+        aliases = {len(operands) + n: n for n in range(len(QUARTERS))}
+        in_specs += [pl.BlockSpec(memory_space=pl.ANY)] * len(QUARTERS)
+        operands += made
     if not window.first:
         in_specs.append(vmem)
         operands.append(carry)
-    out_shape = [jax.ShapeDtypeStruct((3, window.width // 4, NLON), jnp.float32)] * 4
+    out_shape = [jax.ShapeDtypeStruct((slots, 3, window.width // 4, NLON), jnp.float32)] * len(QUARTERS)
     if not window.last:
         out_shape.append(jax.ShapeDtypeStruct((2, 2 * SUB, NLON), jnp.float32))
     field = pltpu.VMEM((2, window.extended, NLON), jnp.float32)
     lhs_shape = (2, 2 * window.rows, depth)
     out = pl.pallas_call(
-        functools.partial(window_kernel, window, depth, len(waits)),
+        functools.partial(window_kernel, window, slot, len(waits)),
         out_shape=out_shape,
         in_specs=in_specs,
         out_specs=[pl.BlockSpec(memory_space=pl.ANY)] * len(out_shape),
@@ -413,6 +419,7 @@
             pltpu.SemaphoreType.DMA,
             pltpu.SemaphoreType.DMA((5,)),
         ],
+        input_output_aliases=aliases,
         compiler_params=pltpu.CompilerParams(vmem_limit_bytes=VMEM_LIMIT),
         cost_estimate=pl.CostEstimate(
             flops=KERNEL_WORK * 3 * 2 * 2 * window.rows * depth * NLON,
@@ -421,7 +428,7 @@
         ),
         name="window_tensor",
     )(*operands)
-    return out[:4], (None if window.last else out[4])
+    return list(out[:4]), (None if window.last else out[4])
 
 
 def by_levels(coeffs):
@@ -442,21 +449,19 @@
 
     (piece,) = pieces_of(spec, 1 - band, windows[:1], count)
     remotes = [lax.ppermute(piece, "band", swap)]
-    for k, piece in enumerate(pieces_of(spec, 1 - band, windows[1:], count), 1):
-        if k > 1:
-            piece = gated(piece, [remotes[k - 2]])
-        remotes.append(lax.ppermute(piece, "band", swap))
+    outgoing = [None, *pieces_of(spec, 1 - band, windows[1:], count)]
+    remotes.append(lax.ppermute(outgoing[1], "band", swap))
     local = pieces_of(spec, band, windows, count)
 
     cores = [(m, m ^ 1) for m in range(members)]
     ways = [[(m, m ^ ORDER[m % 2][step]) for m in range(members)] for step in range(len(ORDER[0]))]
 
     def halved(parts_of, step):
-        half = parts_of[0].shape[1] // 2
+        half = parts_of[0].shape[2] // 2
         mine = half_of[step]
 
         def total(which):
-            return sum(lax.dynamic_slice_in_dim(part, which * half, half, axis=1) for part in parts_of)
+            return sum(lax.dynamic_slice_in_dim(part, which * half, half, axis=2) for part in parts_of)
 
         leaves = total(1 - mine)
         return [total(mine), lax.ppermute(leaves, "mem", ways[step])], leaves
@@ -464,6 +469,8 @@
     def across(parts_of, step):
         kept, passed, kept_more, passed_more = parts_of
         leaves = passed + passed_more
+        if len(sums) == 1:
+            leaves = gated(leaves, [remotes[-1]])
         return [kept, kept_more, lax.ppermute(leaves, "mem", ways[step])], leaves
 
     def advanced(parts_of, step):
@@ -481,24 +488,31 @@
 
     carry = None
     sums, done = [], []
-    for k, window in enumerate(windows):
-        waits = []
-        for j in AHEAD[k]:
-            sums[j], left = advanced(sums[j], done[j])
-            done[j] += 1
-            waits.append(left)
-        quarters, carry = window_tensor(window, place, local[k], remotes[k], table, waits, carry)
-        first = lax.ppermute(quarters[3], "mem", cores)
-        second = lax.ppermute(quarters[2], "mem", cores)
-        sums.append([quarters[0], quarters[1], second, first])
+    for batch in BATCHES:
+        made = None
+        for slot, k in enumerate(batch):
+            if k + 2 < count:
+                piece = gated(outgoing[k + 2], [remotes[k]] if carry is None else [remotes[k], carry])
+                remotes.append(lax.ppermute(piece, "band", swap))
+            waits = []
+            for j in AHEAD[k]:
+                sums[j], left = advanced(sums[j], done[j])
+                done[j] += 1
+                waits.append(left)
+            made, carry = window_tensor(
+                windows[k], slot, len(batch), place, local[k], remotes[k], table, made, waits, carry
+            )
+        first = lax.ppermute(made[3], "mem", cores)
+        second = lax.ppermute(made[2], "mem", cores)
+        sums.append([made[0], made[1], second, first])
         done.append(0)
-    pieces = {"own": [], "both": [], "other": []}
-    for k, window in enumerate(windows):
-        for step in range(done[k], len(ways)):
-            sums[k], _ = advanced(sums[k], step)
-        pieces[window.side].append(exponent_of(sum(sums[k]), members))
-
-    other = lax.ppermute(jnp.stack(pieces["other"]), "band", swap)
+    results = []
+    for j in range(len(BATCHES)):
+        for step in range(done[j], len(ways)):
+            sums[j], _ = advanced(sums[j], step)
+        results.append(exponent_of(sum(sums[j]), members))
+
+    other = lax.ppermute(results[0][:2], "band", swap)
     place_of = {}
     for m in range(members):
         for b in range(2):
@@ -509,9 +523,9 @@
     for (piece, b), index in place_of.items():
         mate = (piece, b) if (piece < half) == (b == 0) else ((piece + half) % members, 1 - b)
         trades.append((index, place_of[mate]))
-    both = lax.ppermute(pieces["both"][0], ("mem", "band"), trades)
-
-    early = gathered(jnp.concatenate([other, both[None]]))
+    both = lax.ppermute(results[0][2:], ("mem", "band"), trades)
+
+    early = gathered(jnp.concatenate([other, both]))
     other, both = early[:-1], early[-1]
     middle = both.shape[0] // 2
     low, high = both[:middle], both[middle:]
@@ -520,7 +534,7 @@
     up = jnp.stack([jnp.concatenate([low, *other[::-1]]), jnp.concatenate([high, rest])])
     out = jnp.where(band == 0, down, up)
 
-    own = gathered(jnp.stack(pieces["own"]))
+    own = gathered(results[1])
     for k, block in enumerate(own):
         width = block.shape[0]
         row = choose(band, (nlat // 2 - middle - (k + 1) * width, middle + k * width))

time: 191 us -> 200 us (1.047)
  the two profiles are of different devices: /device:TPU:0 before, /device:TPU:7 now
where the time goes in v17:
time: 200 us
  waiting for transfers between devices  82.2 us (41%)
  Pallas kernels  61.3 us (31%)
  starting transfers between devices  36.4 us (18%)
  other arithmetic  13.4 us (7%)
  local copies, waits for them, and re-layouts  6.29 us (3%)
    pallas_call x5, Pallas kernels, window_tensor(): pl.pallas_call(functools.partial(window_kernel, window, slot, len(waits))...  51.2 us
    ppermute x4, waiting for transfers between devices, halved(): return ([total(mine), lax.ppermute(leaves, 'mem', ways[step])], leaves)  23.1 us
    ppermute x8, waiting for transfers between devices, doubled(): beside = lax.ppermute(part, 'mem', cores if step < 0 else ways[step])  22 us
    ppermute x8, starting transfers between devices, doubled(): beside = lax.ppermute(part, 'mem', cores if step < 0 else ways[step])  19.4 us
    ppermute x2, waiting for transfers between devices, across(): return ([kept, kept_more, lax.ppermute(leaves, 'mem', ways[step])], leaves)  19.2 us
    pallas_call x3, Pallas kernels, pieces_of(): pl.pallas_call(functools.partial(pieces_kernel, windows, slots, count), i...  10.1 us
    ppermute x4, starting transfers between devices, halved(): return ([total(mine), lax.ppermute(leaves, 'mem', ways[step])], leaves)  7.62 us
    ppermute x1, waiting for transfers between devices, by_levels(): remotes = [lax.ppermute(piece, 'band', swap)]  6.94 us
  transfers between devices with their start and end apart: 25, of which 14 were waited for; matrix products, arithmetic and copies ran while one was open for 6% of the time, Pallas kernels for 29%

profile of v17, /device:TPU:7, one launch (start us, length us, event | category | flops | bytes accessed | tf_op | source)
XLA Modules:
  0.0 199.8 jit_solution(5058116284552312769)
XLA Ops:
  0.0 2.6 %pieces_of.5 = f32[2,136,640]{2,1,0:T(8,128)} custom-call(s32[1]{0:T(128)} %bitcast.5.level_ref, f32[2,2,640,640]{3,2,1,0:T(8,128)} %bitcast.28), custom_call_target="tpu_custom_call" | custom-call | bytes 5242880 | tf_op jit(solution)/shard_map/pieces_of/pallas_call | solution.py:210
  2.9 3.6 %pieces_of.4 = (f32[2,128,640]{2,1,0:T(8,128)}, f32[2,128,640]{2,1,0:T(8,128)}, f32[2,128,640]{2,1,0:T(8,128)}, f32[2,120,640]{2,1,0:T(8,128)}) custom-call(s32[1]{0:T(128)} %bitcast.5.level_ref, f32[2,2,640,640]{3,2,1,0:T(8,128)} %bitcast.29), custom_call_target="tpu_custom_call" | custom-call | bytes 10485760 | tf_op jit(solution)/shard_map/pieces_of/pallas_call | solution.py:210
  6.5 1.3 collective-permute-start.2
  7.8 4.0 %pieces_of.3 = (f32[2,136,640]{2,1,0:T(8,128)}, f32[2,128,640]{2,1,0:T(8,128)}, f32[2,128,640]{2,1,0:T(8,128)}, f32[2,128,640]{2,1,0:T(8,128)}, f32[2,120,640]{2,1,0:T(8,128)}) custom-call(s32[1]{0:T(128)} %bitcast.level_ref, f32[2,2,640,640]{3,2,1,0:T(8,128)} %bitcast.30), custom_call_target="tpu_custom_call" | custom-call | bytes 13107200 | tf_op jit(solution)/shard_map/pieces_of/pallas_call | solution.py:210
  12.4 6.9 %collective-permute-done.refs_1_.refs_2_ = f32[2,136,640]{2,1,0:T(8,128)S(1)} collective-permute-done((f32[2,136,640]{2,1,0:T(8,128)}, f32[2,136,640]{2,1,0:T(8,128)S(1)}, u32[]{:S(2)}, u32[]{:S(2)}) %collective-permute-start) | collective-permute-done | bytes 696352 | tf_op jit(solution)/shard_map/ppermute | solution.py:451
  19.3 0.9 copy-done.4
  20.4 10.5 %window_tensor.5 = (f32[3,3,32,1280]{3,2,1,0:T(8,128)}, f32[3,3,32,1280]{3,2,1,0:T(8,128)}, f32[3,3,32,1280]{3,2,1,0:T(8,128)}, f32[3,3,32,1280]{3,2,1,0:T(8,128)}, f32[2,16,1280]{2,1,0:T(8,128)}) custom-call(s32[4]{0:T(128)} %pad_add_fusion.refs_0_, f32[2,136,640]{2,1,0:T(8,128)} %get-tuple-element.42.refs_1_, f32[2,136,640]{2,1,0:T(8,128)} %copy-done.4, ...), custom_call_target="tpu_custom_call" | custom-call | flops 10695475200 | bytes 6635520 | tf_op jit(solution)/shard_map/window_tensor/pallas_call | solution.py:404
  30.9 2.4 %collective-permute-done.2.refs_2_.refs_1_ = f32[2,128,640]{2,1,0:T(8,128)S(1)} collective-permute-done((f32[2,128,640]{2,1,0:T(8,128)}, f32[2,128,640]{2,1,0:T(8,128)S(1)}, u32[]{:S(2)}, u32[]{:S(2)}) %collective-permute-start.2) | collective-permute-done | bytes 655392 | tf_op jit(solution)/shard_map/ppermute | solution.py:453
  33.4 0.9 copy-done.5
  34.5 10.1 %window_tensor.6 = (f32[3,3,32,1280]{3,2,1,0:T(8,128)}, f32[3,3,32,1280]{3,2,1,0:T(8,128)}, f32[3,3,32,1280]{3,2,1,0:T(8,128)}, f32[3,3,32,1280]{3,2,1,0:T(8,128)}, f32[2,16,1280]{2,1,0:T(8,128)}) custom-call(s32[4]{0:T(128)} %pad_add_fusion.refs_0_, ...), custom_call_target="tpu_custom_call", output_to_operand_aliasing={{0}: (4, {}), {1}: (5, {}), {2}: (6, {}), {3}: (7, {})} | custom-call | flops 10066329600 | bytes 6553600 | tf_op jit(solution)/shard_map/window_tensor/pallas_call | solution.py:404
  44.6 2.8 %collective-permute-done.1.refs_2_.refs_1_ = f32[2,128,640]{2,1,0:T(8,128)S(1)} collective-permute-done((f32[2,128,640]{2,1,0:T(8,128)}, f32[2,128,640]{2,1,0:T(8,128)S(1)}, u32[]{:S(2)}, u32[]{:S(2)}) %collective-permute-start.1) | collective-permute-done | bytes 655392 | tf_op jit(solution)/shard_map/ppermute | solution.py:496
  47.4 0.9 copy-done.6
  48.3 10.1 %window_tensor.7 = (f32[3,3,32,1280]{3,2,1,0:T(8,128)}, f32[3,3,32,1280]{3,2,1,0:T(8,128)}, f32[3,3,32,1280]{3,2,1,0:T(8,128)}, f32[3,3,32,1280]{3,2,1,0:T(8,128)}, f32[2,16,1280]{2,1,0:T(8,128)}) custom-call(s32[4]{0:T(128)} %pad_add_fusion.refs_0_, ...), custom_call_target="tpu_custom_call", output_to_operand_aliasing={{0}: (4, {}), {1}: (5, {}), {2}: (6, {}), {3}: (7, {})} | custom-call | flops 10066329600 | bytes 6553600 | tf_op jit(solution)/shard_map/window_tensor/pallas_call | solution.py:404
  58.4 2.8 %collective-permute-start.4 = (f32[3,3,32,1280]{3,2,1,0:T(8,128)}, f32[3,3,32,1280]{3,2,1,0:T(8,128)}, u32[]{:S(2)}, u32[]{:S(2)}) collective-permute-start(f32[3,3,32,1280]{3,2,1,0:T(8,128)} %get-tuple-element.56), channel_id=1, source_target_pairs={{0,2},{2,0},{4,6},{6,4},{8,10},{10,8},{12,14},{14,12},{16,18},{18,... | collective-permute-start | bytes 4423688 | tf_op jit(solution)/shard_map/ppermute | solution.py:505
  61.8 0.8 copy-done.7
  62.6 10.5 %window_tensor.8 = (f32[2,3,32,1280]{3,2,1,0:T(8,128)}, f32[2,3,32,1280]{3,2,1,0:T(8,128)}, f32[2,3,32,1280]{3,2,1,0:T(8,128)}, f32[2,3,32,1280]{3,2,1,0:T(8,128)}, f32[2,16,1280]{2,1,0:T(8,128)}) custom-call(s32[4]{0:T(128)} %pad_add_fusion.refs_0_, f32[2,128,640]{2,1,0:T(8,128)} %get-tuple-element.59.refs_1_, f32[2,128,640]{2,1,0:T(8,128)} %copy-done.7, ...), custom_call_target="tpu_custom_call" | custom-call | flops 10066329600 | bytes 6553600 | tf_op jit(solution)/shard_map/window_tensor/pallas_call | solution.py:404
  73.1 2.6 %add.151.refs_0_ = f32[3,3,32,1280]{3,2,1,0:T(8,128)} add(f32[3,3,32,1280]{3,2,1,0:T(8,128)S(1)} %copy-done.1, f32[3,3,32,1280]{3,2,1,0:T(8,128)} %collective-permute-done.4) | non-fusion elementwise | flops 368640 | bytes 4423680 | tf_op jit(solution)/shard_map/add | solution.py:471
  75.8 1.1 collective-permute-done.5.refs_1_.refs_2_
  76.9 1.3 collective-permute-start.6
  78.2 10.1 %window_tensor.9 = (f32[2,3,32,1280]{3,2,1,0:T(8,128)}, f32[2,3,32,1280]{3,2,1,0:T(8,128)}, f32[2,3,32,1280]{3,2,1,0:T(8,128)}, f32[2,3,32,1280]{3,2,1,0:T(8,128)}) custom-call(s32[4]{0:T(128)} %pad_add_fusion.refs_0_, f32[2,120,640]{2,1,0:T(8,128)} %get-tuple-element.58.refs_1_, ...), custom_call_target="tpu_custom_call", output_to_operand_aliasing={{0}: (5, {}), {1}: (6, {}), {2}: (7, {}), {3}: (8, {})} | custom-call | flops 9437184000 | bytes 6471680 | tf_op jit(solution)/shard_map/window_tensor/pallas_call | solution.py:404
  88.8 2.3 %collective-permute-done.17 = f32[2,3,32,1280]{3,2,1,0:T(8,128)S(1)} collective-permute-done((f32[2,3,32,1280]{3,2,1,0:T(8,128)}, f32[2,3,32,1280]{3,2,1,0:T(8,128)S(1)}, u32[]{:S(2)}, u32[]{:S(2)}) %collective-permute-start.17) | collective-permute-done | bytes 983072 | tf_op jit(solution)/shard_map/ppermute | solution.py:505
  91.1 2.3 %add.168 = f32[2,3,32,1280]{3,2,1,0:T(8,128)} add(f32[2,3,32,1280]{3,2,1,0:T(8,128)} %get-tuple-element.69, f32[2,3,32,1280]{3,2,1,0:T(8,128)S(1)} %collective-permute-done.17) | non-fusion elementwise | flops 245760 | bytes 2949120 | tf_op jit(solution)/shard_map/add | solution.py:471
  93.4 1.0 collective-permute-start.18
  94.4 1.3 collective-permute-done.6
  95.7 3.0 %dynamic-slice_add_fusion.1 = (f32[3,3,16,1280]{3,2,1,0:T(8,128)S(1)}, f32[3,3,16,1280]{3,2,1,0:T(8,128)}) fusion(f32[3,3,32,1280]{3,2,1,0:T(8,128)} %collective-permute-done.6, s32[]{:T(128)S(6)} %select_n.185, f32[3,3,32,1280]{3,2,1,0:T(8,128)S(1)} %collective-permute-done.3, f32[3,3,32,1280]{3,2,1,0:T(8,128)} %get-tuple-element.53, s32[]{:T(128)S(6)} %select_n.187), kind=kLoop, calls=%fused_computation.9 | loop fusion | flops 737280 | bytes 5898248 | tf_op jit(solution)/shard_map/add | solution.py:464
  98.7 2.3 %collective-permute-start.7 = (f32[3,3,16,1280]{3,2,1,0:T(8,128)}, f32[3,3,16,1280]{3,2,1,0:T(8,128)S(1)}, u32[]{:S(2)}, u32[]{:S(2)}) collective-permute-start(f32[3,3,16,1280]{3,2,1,0:T(8,128)} %get-tuple-element.72), channel_id=1, source_target_pairs={{0,8},{2,18},{4,12},{6,22},{8,0},{10,26},{12,4},{14,30},{16,24},{1... | collective-permute-start | bytes 2211848 | tf_op jit(solution)/shard_map/ppermute | solution.py:467
  101.0 17.8 %collective-permute-done.18 = f32[2,3,32,1280]{3,2,1,0:T(8,128)} collective-permute-done((f32[2,3,32,1280]{3,2,1,0:T(8,128)}, f32[2,3,32,1280]{3,2,1,0:T(8,128)}, u32[]{:S(2)}, u32[]{:S(2)}) %collective-permute-start.18) | collective-permute-done | bytes 983072 | tf_op jit(solution)/shard_map/ppermute | solution.py:474
  118.9 2.1 %dynamic-slice_add_fusion.3 = (f32[2,3,16,1280]{3,2,1,0:T(8,128)S(1)}, f32[2,3,16,1280]{3,2,1,0:T(8,128)}) fusion(f32[2,3,32,1280]{3,2,1,0:T(8,128)} %collective-permute-done.18, s32[]{:T(128)S(6)} %select_n.185, f32[2,3,32,1280]{3,2,1,0:T(8,128)S(1)} %collective-permute-done.16, f32[2,3,32,1280]{3,2,1,0:T(8,128)S(1)} %copy-done.2, s32[]{:T(128)S(6)} %select_n.187), kind=kLoop, calls=%fused_computation.17 | loop fusion | flops 491520 | bytes 3932168 | tf_op jit(solution)/shard_map/add | solution.py:464
  121.0 0.9 collective-permute-start.19
  121.9 2.3 %collective-permute-done.7 = f32[3,3,16,1280]{3,2,1,0:T(8,128)S(1)} collective-permute-done((f32[3,3,16,1280]{3,2,1,0:T(8,128)}, f32[3,3,16,1280]{3,2,1,0:T(8,128)S(1)}, u32[]{:S(2)}, u32[]{:S(2)}) %collective-permute-start.7) | collective-permute-done | bytes 737312 | tf_op jit(solution)/shard_map/ppermute | solution.py:467
  124.2 2.3 %collective-permute-start.8 = (f32[3,3,8,1280]{3,2,1,0:T(8,128)S(1)}, f32[3,3,8,1280]{3,2,1,0:T(8,128)S(1)}, u32[]{:S(2)}, u32[]{:S(2)}) collective-permute-start(f32[3,3,8,1280]{3,2,1,0:T(8,128)S(1)} %dynamic-slice_add_fusion.4), channel_id=1, source_target_pairs={{0,16},{2,6},{4,20},{6,2},{8,24},{10,14},{12,28},{14,10},{16,0},{1... | collective-permute-start | bytes 1105928 | tf_op jit(solution)/shard_map/ppermute | solution.py:467
  126.6 20.8 %collective-permute-done.19 = f32[2,3,16,1280]{3,2,1,0:T(8,128)S(1)} collective-permute-done((f32[2,3,16,1280]{3,2,1,0:T(8,128)}, f32[2,3,16,1280]{3,2,1,0:T(8,128)S(1)}, u32[]{:S(2)}, u32[]{:S(2)}) %collective-permute-start.19) | collective-permute-done | bytes 491552 | tf_op jit(solution)/shard_map/ppermute | solution.py:467
  147.4 2.1 %collective-permute-start.20 = (f32[2,3,8,1280]{3,2,1,0:T(8,128)S(1)}, f32[2,3,8,1280]{3,2,1,0:T(8,128)S(1)}, u32[]{:S(2)}, u32[]{:S(2)}) collective-permute-start(f32[2,3,8,1280]{3,2,1,0:T(8,128)S(1)} %dynamic-slice_add_fusion.5), channel_id=1, source_target_pairs={{0,16},{2,6},{4,20},{6,2},{8,24},{10,14},{12,28},{14,10},{16,0},{1... | collective-permute-start | bytes 737288 | tf_op jit(solution)/shard_map/ppermute | solution.py:467
  149.5 1.1 add_multiply_fusion
  151.0 0.7 collective-permute-start.10
  151.7 2.3 %collective-permute-done.9 = f32[2,8,1280]{2,1,0:T(8,128)S(1)} collective-permute-done((f32[2,8,1280]{2,1,0:T(8,128)S(1)}, f32[2,8,1280]{2,1,0:T(8,128)S(1)}, u32[]{:S(2)}, u32[]{:S(2)}) %collective-permute-start.9) | collective-permute-done | bytes 81952 | tf_op jit(solution)/shard_map/ppermute | solution.py:515
  154.0 1.0 collective-permute-start.11
  155.1 2.8 %collective-permute-done.11 = f32[3,8,1280]{2,1,0:T(8,128)S(1)} collective-permute-done((f32[3,8,1280]{2,1,0:T(8,128)S(1)}, f32[3,8,1280]{2,1,0:T(8,128)S(1)}, u32[]{:S(2)}, u32[]{:S(2)}) %collective-permute-start.11) | collective-permute-done | bytes 122912 | tf_op jit(solution)/shard_map/ppermute | solution.py:480
  158.0 1.0 collective-permute-start.21
  159.0 9.2 %collective-permute-done.12 = f32[3,16,1280]{2,1,0:T(8,128)S(1)} collective-permute-done((f32[3,16,1280]{2,1,0:T(8,128)S(1)}, f32[3,16,1280]{2,1,0:T(8,128)S(1)}, u32[]{:S(2)}, u32[]{:S(2)}) %collective-permute-start.12) | collective-permute-done | bytes 245792 | tf_op jit(solution)/shard_map/ppermute | solution.py:480
  168.3 1.3 collective-permute-start.22
  169.6 8.3 %collective-permute-done.22 = f32[2,16,1280]{2,1,0:T(8,128)S(1)} collective-permute-done((f32[2,16,1280]{2,1,0:T(8,128)S(1)}, f32[2,16,1280]{2,1,0:T(8,128)S(1)}, u32[]{:S(2)}, u32[]{:S(2)}) %collective-permute-start.22) | collective-permute-done | bytes 163872 | tf_op jit(solution)/shard_map/ppermute | solution.py:480
  178.0 2.6 %collective-permute-start.23 = (f32[2,32,1280]{2,1,0:T(8,128)S(1)}, f32[2,32,1280]{2,1,0:T(8,128)S(1)}, u32[]{:S(2)}, u32[]{:S(2)}) collective-permute-start(f32[2,32,1280]{2,1,0:T(8,128)S(1)} %maximum_select_fusion.6), channel_id=1, source_target_pairs={{0,4},{2,10},{4,0},{6,14},{8,12},{10,2},{12,8},{14,6},{16,20},{18,... | collective-permute-start | bytes 983048 | tf_op jit(solution)/shard_map/ppermute | solution.py:480
  180.6 6.5 %collective-permute-start.14 = (f32[3,64,1280]{2,1,0:T(8,128)S(1)}, f32[3,64,1280]{2,1,0:T(8,128)S(1)}, u32[]{:S(2)}, u32[]{:S(2)}) collective-permute-start(f32[3,64,1280]{2,1,0:T(8,128)S(1)} %maximum_select_fusion.3), channel_id=1, source_target_pairs={{0,2},{2,0},{4,6},{6,4},{8,10},{10,8},{12,14},{14,12},{16,18},{18,... | collective-permute-start | bytes 2949128 | tf_op jit(solution)/shard_map/ppermute | solution.py:480
  187.2 7.0 %collective-permute-start.24 = (f32[2,64,1280]{2,1,0:T(8,128)S(1)}, f32[2,64,1280]{2,1,0:T(8,128)S(1)}, u32[]{:S(2)}, u32[]{:S(2)}) collective-permute-start(f32[2,64,1280]{2,1,0:T(8,128)S(1)} %maximum_select_fusion.4), channel_id=1, source_target_pairs={{0,2},{2,0},{4,6},{6,4},{8,10},{10,8},{12,14},{14,12},{16,18},{18,... | collective-permute-start | bytes 1966088 | tf_op jit(solution)/shard_map/ppermute | solution.py:480
  194.1 1.7 collective-permute-done.24
  197.3 1.7 copy-done
  199.0 0.9 slice_dynamic-update-slice_fusion
  (59 shorter events, 5.1 us)
Async XLA Ops:
  2.6 16.8 %collective-permute-start = (f32[2,136,640]{2,1,0:T(8,128)}, f32[2,136,640]{2,1,0:T(8,128)S(1)}, u32[]{:S(2)}, u32[]{:S(2)}) collective-permute-start(f32[2,136,640]{2,1,0:T(8,128)} %pieces_of.5), channel_id=1, source_target_pairs={{0,1},{1,0},{2,3},{3,2},{4,5},{5,4},{6,7},{7,6},{8,9},{9,8},{10,11... | collective-permute-start | bytes 2088968 | tf_op jit(solution)/shard_map/ppermute | solution.py:451
  6.5 26.9 %collective-permute-start.2 = (f32[2,128,640]{2,1,0:T(8,128)}, f32[2,128,640]{2,1,0:T(8,128)S(1)}, u32[]{:S(2)}, u32[]{:S(2)}) collective-permute-start(f32[2,128,640]{2,1,0:T(8,128)} %get-tuple-element.41), channel_id=1, source_target_pairs={{0,1},{1,0},{2,3},{3,2},{4,5},{5,4},{6,7},{7,6},{8,9},{9,8},{10,11... | collective-permute-start | bytes 1966088 | tf_op jit(solution)/shard_map/ppermute | solution.py:453
  19.3 0.9 copy-start.4
  20.2 27.2 %collective-permute-start.1 = (f32[2,128,640]{2,1,0:T(8,128)}, f32[2,128,640]{2,1,0:T(8,128)S(1)}, u32[]{:S(2)}, u32[]{:S(2)}) collective-permute-start(f32[2,128,640]{2,1,0:T(8,128)} %gated.4), channel_id=1, source_target_pairs={{0,1},{1,0},{2,3},{3,2},{4,5},{5,4},{6,7},{7,6},{8,9},{9,8},{10,11... | collective-permute-start | bytes 1966088 | tf_op jit(solution)/shard_map/ppermute | solution.py:496
  33.4 0.9 copy-start.5
  34.3 27.5 %collective-permute-start.15 = (f32[2,128,640]{2,1,0:T(8,128)}, f32[2,128,640]{2,1,0:T(8,128)S(1)}, u32[]{:S(2)}, u32[]{:S(2)}) collective-permute-start(f32[2,128,640]{2,1,0:T(8,128)} %gated.7), channel_id=1, source_target_pairs={{0,1},{1,0},{2,3},{3,2},{4,5},{5,4},{6,7},{7,6},{8,9},{9,8},{10,11... | collective-permute-start | bytes 1966088 | tf_op jit(solution)/shard_map/ppermute | solution.py:496
  47.4 0.9 copy-start.6
  58.4 14.7 %collective-permute-start.4 = (f32[3,3,32,1280]{3,2,1,0:T(8,128)}, f32[3,3,32,1280]{3,2,1,0:T(8,128)}, u32[]{:S(2)}, u32[]{:S(2)}) collective-permute-start(f32[3,3,32,1280]{3,2,1,0:T(8,128)} %get-tuple-element.56), channel_id=1, source_target_pairs={{0,2},{2,0},{4,6},{6,4},{8,10},{10,8},{12,14},{14,12},{16,18},{18,... | collective-permute-start | bytes 4423688 | tf_op jit(solution)/shard_map/ppermute | solution.py:505
  61.2 15.7 %collective-permute-start.5 = (f32[2,120,640]{2,1,0:T(8,128)}, f32[2,120,640]{2,1,0:T(8,128)}, u32[]{:S(2)}, u32[]{:S(2)}) collective-permute-start(f32[2,120,640]{2,1,0:T(8,128)} %gated.5), channel_id=1, source_target_pairs={{0,1},{1,0},{2,3},{3,2},{4,5},{5,4},{6,7},{7,6},{8,9},{9,8},{10,11... | collective-permute-start | bytes 1843208 | tf_op jit(solution)/shard_map/ppermute | solution.py:496
  61.4 33.0 %collective-permute-start.3 = (f32[3,3,32,1280]{3,2,1,0:T(8,128)}, f32[3,3,32,1280]{3,2,1,0:T(8,128)S(1)}, u32[]{:S(2)}, u32[]{:S(2)}) collective-permute-start(f32[3,3,32,1280]{3,2,1,0:T(8,128)} %get-tuple-element.54), channel_id=1, source_target_pairs={{0,2},{2,0},{4,6},{6,4},{8,10},{10,8},{12,14},{14,12},{16,18},{18,... | collective-permute-start | bytes 4423688 | tf_op jit(solution)/shard_map/ppermute | solution.py:506
  61.8 0.8 copy-start.7
  62.6 10.5 %copy-start.1 = (f32[3,3,32,1280]{3,2,1,0:T(8,128)S(1)}, f32[3,3,32,1280]{3,2,1,0:T(8,128)}, u32[]{:S(2)}) copy-start(f32[3,3,32,1280]{3,2,1,0:T(8,128)} %get-tuple-element.55) | copy-start | bytes 4423684
  76.9 18.8 %collective-permute-start.6 = (f32[3,3,32,1280]{3,2,1,0:T(8,128)}, f32[3,3,32,1280]{3,2,1,0:T(8,128)}, u32[]{:S(2)}, u32[]{:S(2)}) collective-permute-start(f32[3,3,32,1280]{3,2,1,0:T(8,128)} %gated.6.refs_4_), channel_id=1, source_target_pairs={{0,4},{2,10},{4,0},{6,14},{8,12},{10,2},{12,8},{14,6},{16,20},{18,... | collective-permute-start | bytes 4423688 | tf_op jit(solution)/shard_map/ppermute | solution.py:474
  88.3 2.8 %collective-permute-start.17 = (f32[2,3,32,1280]{3,2,1,0:T(8,128)}, f32[2,3,32,1280]{3,2,1,0:T(8,128)S(1)}, u32[]{:S(2)}, u32[]{:S(2)}) collective-permute-start(f32[2,3,32,1280]{3,2,1,0:T(8,128)} %get-tuple-element.70), channel_id=1, source_target_pairs={{0,2},{2,0},{4,6},{6,4},{8,10},{10,8},{12,14},{14,12},{16,18},{18,... | collective-permute-start | bytes 2949128 | tf_op jit(solution)/shard_map/ppermute | solution.py:505
  88.4 12.6 %collective-permute-start.16 = (f32[2,3,32,1280]{3,2,1,0:T(8,128)}, f32[2,3,32,1280]{3,2,1,0:T(8,128)S(1)}, u32[]{:S(2)}, u32[]{:S(2)}) collective-permute-start(f32[2,3,32,1280]{3,2,1,0:T(8,128)} %get-tuple-element.68), channel_id=1, source_target_pairs={{0,2},{2,0},{4,6},{6,4},{8,10},{10,8},{12,14},{14,12},{16,18},{18,... | collective-permute-start | bytes 2949128 | tf_op jit(solution)/shard_map/ppermute | solution.py:506
  93.4 25.5 %collective-permute-start.18 = (f32[2,3,32,1280]{3,2,1,0:T(8,128)}, f32[2,3,32,1280]{3,2,1,0:T(8,128)}, u32[]{:S(2)}, u32[]{:S(2)}) collective-permute-start(f32[2,3,32,1280]{3,2,1,0:T(8,128)} %add.168), channel_id=1, source_target_pairs={{0,4},{2,10},{4,0},{6,14},{8,12},{10,2},{12,8},{14,6},{16,20},{18,... | collective-permute-start | bytes 2949128 | tf_op jit(solution)/shard_map/ppermute | solution.py:474
  95.7 23.1 %copy-start.2 = (f32[2,3,32,1280]{3,2,1,0:T(8,128)S(1)}, f32[2,3,32,1280]{3,2,1,0:T(8,128)}, u32[]{:S(2)}) copy-start(f32[2,3,32,1280]{3,2,1,0:T(8,128)} %get-tuple-element.67) | copy-start | bytes 2949124
  98.7 25.5 %collective-permute-start.7 = (f32[3,3,16,1280]{3,2,1,0:T(8,128)}, f32[3,3,16,1280]{3,2,1,0:T(8,128)S(1)}, u32[]{:S(2)}, u32[]{:S(2)}) collective-permute-start(f32[3,3,16,1280]{3,2,1,0:T(8,128)} %get-tuple-element.72), channel_id=1, source_target_pairs={{0,8},{2,18},{4,12},{6,22},{8,0},{10,26},{12,4},{14,30},{16,24},{1... | collective-permute-start | bytes 2211848 | tf_op jit(solution)/shard_map/ppermute | solution.py:467
  121.0 26.3 %collective-permute-start.19 = (f32[2,3,16,1280]{3,2,1,0:T(8,128)}, f32[2,3,16,1280]{3,2,1,0:T(8,128)S(1)}, u32[]{:S(2)}, u32[]{:S(2)}) collective-permute-start(f32[2,3,16,1280]{3,2,1,0:T(8,128)} %get-tuple-element.74), channel_id=1, source_target_pairs={{0,8},{2,18},{4,12},{6,22},{8,0},{10,26},{12,4},{14,30},{16,24},{1... | collective-permute-start | bytes 1474568 | tf_op jit(solution)/shard_map/ppermute | solution.py:467
  124.2 25.3 %copy-start.3 = (f32[3,3,16,1280]{3,2,1,0:T(8,128)}, f32[3,3,16,1280]{3,2,1,0:T(8,128)S(1)}, u32[]{:S(2)}) copy-start(f32[3,3,16,1280]{3,2,1,0:T(8,128)S(1)} %collective-permute-done.7) | copy-start | bytes 2211844
  124.2 25.2 %collective-permute-start.8 = (f32[3,3,8,1280]{3,2,1,0:T(8,128)S(1)}, f32[3,3,8,1280]{3,2,1,0:T(8,128)S(1)}, u32[]{:S(2)}, u32[]{:S(2)}) collective-permute-start(f32[3,3,8,1280]{3,2,1,0:T(8,128)S(1)} %dynamic-slice_add_fusion.4), channel_id=1, source_target_pairs={{0,16},{2,6},{4,20},{6,2},{8,24},{10,14},{12,28},{14,10},{16,0},{1... | collective-permute-start | bytes 1105928 | tf_op jit(solution)/shard_map/ppermute | solution.py:467
  147.4 7.6 %collective-permute-start.20 = (f32[2,3,8,1280]{3,2,1,0:T(8,128)S(1)}, f32[2,3,8,1280]{3,2,1,0:T(8,128)S(1)}, u32[]{:S(2)}, u32[]{:S(2)}) collective-permute-start(f32[2,3,8,1280]{3,2,1,0:T(8,128)S(1)} %dynamic-slice_add_fusion.5), channel_id=1, source_target_pairs={{0,16},{2,6},{4,20},{6,2},{8,24},{10,14},{12,28},{14,10},{16,0},{1... | collective-permute-start | bytes 737288 | tf_op jit(solution)/shard_map/ppermute | solution.py:467
  150.7 3.4 %collective-permute-start.9 = (f32[2,8,1280]{2,1,0:T(8,128)S(1)}, f32[2,8,1280]{2,1,0:T(8,128)S(1)}, u32[]{:S(2)}, u32[]{:S(2)}) collective-permute-start(f32[2,8,1280]{2,1,0:T(8,128)S(1)} %slice_bitcast_fusion.4), channel_id=1, source_target_pairs={{0,1},{1,0},{2,3},{3,2},{4,5},{5,4},{6,7},{7,6},{8,9},{9,8},{10,11... | collective-permute-start | bytes 245768 | tf_op jit(solution)/shard_map/ppermute | solution.py:515
  151.0 3.0 %collective-permute-start.10 = (f32[1,8,1280]{2,1,0:T(8,128)S(1)}, f32[1,8,1280]{2,1,0:T(8,128)S(1)}, u32[]{:S(2)}, u32[]{:S(2)}) collective-permute-start(f32[1,8,1280]{2,1,0:T(8,128)S(1)} %slice_bitcast_fusion.5), channel_id=1, source_target_pairs={{0,0},{1,2},{2,1},{3,3},{4,4},{5,10},{6,17},{7,7},{8,8},{9,18},{10... | collective-permute-start | bytes 122888 | tf_op jit(solution)/shard_map/ppermute | solution.py:526
  154.0 3.8 %collective-permute-start.11 = (f32[3,8,1280]{2,1,0:T(8,128)S(1)}, f32[3,8,1280]{2,1,0:T(8,128)S(1)}, u32[]{:S(2)}, u32[]{:S(2)}) collective-permute-start(f32[3,8,1280]{2,1,0:T(8,128)S(1)} %constant_dynamic-update-slice_fusion), channel_id=1, source_target_pairs={{0,16},{2,6},{4,20},{6,2},{8,24},{10,14},{12,28},{14,10},{16,0},{1... | collective-permute-start | bytes 368648 | tf_op jit(solution)/shard_map/ppermute | solution.py:480
  157.9 10.3 %collective-permute-start.12 = (f32[3,16,1280]{2,1,0:T(8,128)S(1)}, f32[3,16,1280]{2,1,0:T(8,128)S(1)}, u32[]{:S(2)}, u32[]{:S(2)}) collective-permute-start(f32[3,16,1280]{2,1,0:T(8,128)S(1)} %maximum_select_fusion.7), channel_id=1, source_target_pairs={{0,8},{2,18},{4,12},{6,22},{8,0},{10,26},{12,4},{14,30},{16,24},{1... | collective-permute-start | bytes 737288 | tf_op jit(solution)/shard_map/ppermute | solution.py:480
  158.0 10.3 %collective-permute-start.21 = (f32[2,8,1280]{2,1,0:T(8,128)S(1)}, f32[2,8,1280]{2,1,0:T(8,128)S(1)}, u32[]{:S(2)}, u32[]{:S(2)}) collective-permute-start(f32[2,8,1280]{2,1,0:T(8,128)S(1)} %fusion.12), channel_id=1, source_target_pairs={{0,16},{2,6},{4,20},{6,2},{8,24},{10,14},{12,28},{14,10},{16,0},{1... | collective-permute-start | bytes 245768 | tf_op jit(solution)/shard_map/ppermute | solution.py:480
  168.2 12.3 %collective-permute-start.13 = (f32[3,32,1280]{2,1,0:T(8,128)S(1)}, f32[3,32,1280]{2,1,0:T(8,128)S(1)}, u32[]{:S(2)}, u32[]{:S(2)}) collective-permute-start(f32[3,32,1280]{2,1,0:T(8,128)S(1)} %maximum_select_fusion.5), channel_id=1, source_target_pairs={{0,4},{2,10},{4,0},{6,14},{8,12},{10,2},{12,8},{14,6},{16,20},{18,... | collective-permute-start | bytes 1474568 | tf_op jit(solution)/shard_map/ppermute | solution.py:480
  168.3 9.6 %collective-permute-start.22 = (f32[2,16,1280]{2,1,0:T(8,128)S(1)}, f32[2,16,1280]{2,1,0:T(8,128)S(1)}, u32[]{:S(2)}, u32[]{:S(2)}) collective-permute-start(f32[2,16,1280]{2,1,0:T(8,128)S(1)} %maximum_select_fusion.8), channel_id=1, source_target_pairs={{0,8},{2,18},{4,12},{6,22},{8,0},{10,26},{12,4},{14,30},{16,24},{1... | collective-permute-start | bytes 491528 | tf_op jit(solution)/shard_map/ppermute | solution.py:480
  178.0 9.1 %collective-permute-start.23 = (f32[2,32,1280]{2,1,0:T(8,128)S(1)}, f32[2,32,1280]{2,1,0:T(8,128)S(1)}, u32[]{:S(2)}, u32[]{:S(2)}) collective-permute-start(f32[2,32,1280]{2,1,0:T(8,128)S(1)} %maximum_select_fusion.6), channel_id=1, source_target_pairs={{0,4},{2,10},{4,0},{6,14},{8,12},{10,2},{12,8},{14,6},{16,20},{18,... | collective-permute-start | bytes 983048 | tf_op jit(solution)/shard_map/ppermute | solution.py:480
  180.6 15.3 %collective-permute-start.14 = (f32[3,64,1280]{2,1,0:T(8,128)S(1)}, f32[3,64,1280]{2,1,0:T(8,128)S(1)}, u32[]{:S(2)}, u32[]{:S(2)}) collective-permute-start(f32[3,64,1280]{2,1,0:T(8,128)S(1)} %maximum_select_fusion.3), channel_id=1, source_target_pairs={{0,2},{2,0},{4,6},{6,4},{8,10},{10,8},{12,14},{14,12},{16,18},{18,... | collective-permute-start | bytes 2949128 | tf_op jit(solution)/shard_map/ppermute | solution.py:480
  187.2 8.7 %collective-permute-start.24 = (f32[2,64,1280]{2,1,0:T(8,128)S(1)}, f32[2,64,1280]{2,1,0:T(8,128)S(1)}, u32[]{:S(2)}, u32[]{:S(2)}) collective-permute-start(f32[2,64,1280]{2,1,0:T(8,128)S(1)} %maximum_select_fusion.4), channel_id=1, source_target_pairs={{0,2},{2,0},{4,6},{6,4},{8,10},{10,8},{12,14},{14,12},{16,18},{18,... | collective-permute-start | bytes 1966088 | tf_op jit(solution)/shard_map/ppermute | solution.py:480
  197.3 1.7 copy-start

commit v18 on v15

--- a/solution.py
+++ b/solution.py
@@ -14,9 +14,9 @@
 STEPS = 1
 SUB = 8
 LANE = 128
-VMEM_LIMIT = 28 * 1024 * 1024
+VMEM_LIMIT = 60 * 1024 * 1024
 KERNEL_WORK = 8
-ORDER = ((2, 4, 8), (4, 8, 2))
+ORDER = ((2, 4, 8), (4, 2, 8))
 AHEAD = ((), (), (0,), (1, 0), (2, 1, 0))
 
 

time: 191 us -> 178 us (0.932)
  local copies, waits for them, and re-layouts: 20.8 us -> 4.56 us
  Pallas kernels: 51.4 us -> 61.5 us
  waiting for transfers between devices: 74.6 us -> 66.2 us
  starting transfers between devices: 33.3 us -> 36.4 us
    unnamed x58 -> x34, local copies, waits for them, and re-layouts: 19.8 us -> 3.5 us
    pallas_call x5, Pallas kernels: 44.8 us -> 51.3 us  [window_tensor(): pl.pallas_call(functools.partial(window_kernel, window, depth, len(waits)...]
    ppermute x10, waiting for transfers between devices: 41.2 us -> 35.6 us  [halved(): return ([total(mine), lax.ppermute(leaves, 'mem', ways[step])], leaves)]
    pallas_call x3, Pallas kernels: 6.65 us -> 10.2 us  [pieces_of(): pl.pallas_call(functools.partial(pieces_kernel, windows, slots, count), i...]
    ppermute x1, waiting for transfers between devices: 5.35 us -> 8.2 us  [by_levels(): remotes = [lax.ppermute(piece, 'band', swap)]]
    ppermute x8, waiting for transfers between devices: 24.8 us -> 22 us  [doubled(): beside = lax.ppermute(part, 'mem', cores if step < 0 else ways[step])]
    ppermute x4, waiting for transfers between devices: 3.18 us -> 0.35 us  [by_levels(): remotes.append(lax.ppermute(piece, 'band', swap))]
    ppermute x8, starting transfers between devices: 5.16 us -> 7.82 us  [doubled(): beside = lax.ppermute(part, 'mem', cores if step < 0 else ways[step])]
  transfers between devices with their start and end apart: 40 -> 40, of which waited for: 13 -> 13; matrix products, arithmetic and copies ran while one was open for 4% -> 4% of each run, Pallas kernels for 26% -> 33%
where the time goes in v18:
time: 178 us
  waiting for transfers between devices  66.2 us (37%)
  Pallas kernels  61.5 us (35%)
  starting transfers between devices  36.4 us (20%)
  other arithmetic  8.5 us (5%)
  local copies, waits for them, and re-layouts  4.56 us (3%)
    pallas_call x5, Pallas kernels, window_tensor(): pl.pallas_call(functools.partial(window_kernel, window, depth, len(waits)...  51.3 us
    ppermute x10, waiting for transfers between devices, halved(): return ([total(mine), lax.ppermute(leaves, 'mem', ways[step])], leaves)  35.6 us
    ppermute x8, waiting for transfers between devices, doubled(): beside = lax.ppermute(part, 'mem', cores if step < 0 else ways[step])  22 us
    pallas_call x3, Pallas kernels, pieces_of(): pl.pallas_call(functools.partial(pieces_kernel, windows, slots, count), i...  10.2 us
    ppermute x10, starting transfers between devices, halved(): return ([total(mine), lax.ppermute(leaves, 'mem', ways[step])], leaves)  9.6 us
    ppermute x1, waiting for transfers between devices, by_levels(): remotes = [lax.ppermute(piece, 'band', swap)]  8.2 us
    ppermute x8, starting transfers between devices, doubled(): beside = lax.ppermute(part, 'mem', cores if step < 0 else ways[step])  7.82 us
    ppermute x5, starting transfers between devices, across(): return ([kept, kept_more, lax.ppermute(leaves, 'mem', ways[step])], leaves)  5.28 us
  transfers between devices with their start and end apart: 40, of which 13 were waited for; matrix products, arithmetic and copies ran while one was open for 4% of the time, Pallas kernels for 33%

profile of v18, /device:TPU:0, one launch (start us, length us, event | category | flops | bytes accessed | tf_op | source)
XLA Modules:
  0.0 177.8 jit_solution(14257432594612784041)
XLA Ops:
  0.0 2.6 %pieces_of.4 = f32[2,136,640]{2,1,0:T(8,128)} custom-call(s32[1]{0:T(128)} %bitcast.5.level_ref, f32[2,2,640,640]{3,2,1,0:T(8,128)} %bitcast.25), custom_call_target="tpu_custom_call" | custom-call | bytes 5242880 | tf_op jit(solution)/shard_map/pieces_of/pallas_call | solution.py:209
  2.6 3.0 %collective-permute-start = (f32[2,136,640]{2,1,0:T(8,128)}, f32[2,136,640]{2,1,0:T(8,128)S(1)}, u32[]{:S(2)}, u32[]{:S(2)}) collective-permute-start(f32[2,136,640]{2,1,0:T(8,128)} %pieces_of.4), channel_id=1, source_target_pairs={{0,1},{1,0},{2,3},{3,2},{4,5},{5,4},{6,7},{7,6},{8,9},{9,8},{10,11... | collective-permute-start | bytes 2088968 | tf_op jit(solution)/shard_map/ppermute | solution.py:444
  5.6 3.6 %pieces_of.5 = (f32[2,128,640]{2,1,0:T(8,128)}, f32[2,128,640]{2,1,0:T(8,128)}, f32[2,128,640]{2,1,0:T(8,128)}, f32[2,120,640]{2,1,0:T(8,128)}) custom-call(s32[1]{0:T(128)} %bitcast.5.level_ref, f32[2,2,640,640]{3,2,1,0:T(8,128)} %bitcast.26), custom_call_target="tpu_custom_call" | custom-call | bytes 10485760 | tf_op jit(solution)/shard_map/pieces_of/pallas_call | solution.py:209
  9.4 4.0 %pieces_of.3 = (f32[2,136,640]{2,1,0:T(8,128)}, f32[2,128,640]{2,1,0:T(8,128)}, f32[2,128,640]{2,1,0:T(8,128)}, f32[2,128,640]{2,1,0:T(8,128)}, f32[2,120,640]{2,1,0:T(8,128)}) custom-call(s32[1]{0:T(128)} %bitcast.level_ref, f32[2,2,640,640]{3,2,1,0:T(8,128)} %bitcast.27), custom_call_target="tpu_custom_call" | custom-call | bytes 13107200 | tf_op jit(solution)/shard_map/pieces_of/pallas_call | solution.py:209
  14.0 8.2 %collective-permute-done.refs_2_.refs_1_ = f32[2,136,640]{2,1,0:T(8,128)S(1)} collective-permute-done((f32[2,136,640]{2,1,0:T(8,128)}, f32[2,136,640]{2,1,0:T(8,128)S(1)}, u32[]{:S(2)}, u32[]{:S(2)}) %collective-permute-start) | collective-permute-done | bytes 696352 | tf_op jit(solution)/shard_map/ppermute | solution.py:444
  22.2 0.9 copy-done.1
  23.1 10.5 %window_tensor.5 = (f32[3,32,1280]{2,1,0:T(8,128)}, f32[3,32,1280]{2,1,0:T(8,128)}, f32[3,32,1280]{2,1,0:T(8,128)}, f32[3,32,1280]{2,1,0:T(8,128)}, f32[2,16,1280]{2,1,0:T(8,128)}) custom-call(s32[4]{0:T(128)} %pad_add_fusion.refs_0_, f32[2,136,640]{2,1,0:T(8,128)} %get-tuple-element.38.refs_1_, f32[2,136,640]{2,1,0:T(8,128)} %copy-done.1, ...), custom_call_target="tpu_custom_call" | custom-call | flops 10695475200 | bytes 6635520 | tf_op jit(solution)/shard_map/window_tensor/pallas_call | solution.py:398
  33.8 2.1 %collective-permute-start.13 = (f32[2,128,640]{2,1,0:T(8,128)}, f32[2,128,640]{2,1,0:T(8,128)S(1)}, u32[]{:S(2)}, u32[]{:S(2)}) collective-permute-start(f32[2,128,640]{2,1,0:T(8,128)} %gated.3), channel_id=1, source_target_pairs={{0,1},{1,0},{2,3},{3,2},{4,5},{5,4},{6,7},{7,6},{8,9},{9,8},{10,11... | collective-permute-start | bytes 1966088 | tf_op jit(solution)/shard_map/ppermute | solution.py:448
  35.9 0.8 copy-done.3
  36.7 10.1 %window_tensor.6 = (f32[3,32,1280]{2,1,0:T(8,128)}, f32[3,32,1280]{2,1,0:T(8,128)}, f32[3,32,1280]{2,1,0:T(8,128)}, f32[3,32,1280]{2,1,0:T(8,128)}, f32[2,16,1280]{2,1,0:T(8,128)}) custom-call(s32[4]{0:T(128)} %pad_add_fusion.refs_0_, f32[2,128,640]{2,1,0:T(8,128)} %get-tuple-element.43.refs_1_, f32[2,128,640]{2,1,0:T(8,128)} %copy-done.3, ...), custom_call_target="tpu_custom_call" | custom-call | flops 10066329600 | bytes 6553600 | tf_op jit(solution)/shard_map/window_tensor/pallas_call | solution.py:398
  47.1 1.3 collective-permute-start.24
  48.9 0.8 add.295.refs_4_
  49.7 1.5 collective-permute-start.3
  51.7 2.0 %collective-permute-start.9 = (f32[3,32,1280]{2,1,0:T(8,128)S(1)}, f32[3,32,1280]{2,1,0:T(8,128)}, u32[]{:S(2)}, u32[]{:S(2)}) collective-permute-start(f32[3,32,1280]{2,1,0:T(8,128)S(1)} %add.310.refs_4_), channel_id=1, source_target_pairs={{0,4},{2,10},{4,0},{6,14},{8,12},{10,2},{12,8},{14,6},{16,20},{18,... | collective-permute-start | bytes 1474568 | tf_op jit(solution)/shard_map/ppermute | solution.py:467
  53.7 10.4 %window_tensor.7 = (f32[3,32,1280]{2,1,0:T(8,128)}, f32[3,32,1280]{2,1,0:T(8,128)}, f32[3,32,1280]{2,1,0:T(8,128)}, f32[3,32,1280]{2,1,0:T(8,128)}, f32[2,16,1280]{2,1,0:T(8,128)}) custom-call(s32[4]{0:T(128)} %pad_add_fusion.refs_0_, f32[2,128,640]{2,1,0:T(8,128)} %get-tuple-element.50.refs_1_, f32[2,128,640]{2,1,0:T(8,128)} %copy-done.2, ...), custom_call_target="tpu_custom_call" | custom-call | flops 10066329600 | bytes 6553600 | tf_op jit(solution)/shard_map/window_tensor/pallas_call | solution.py:398
  64.2 1.6 collective-permute-start.30
  65.7 1.8 %dynamic-slice_add_fusion.9 = (f32[3,16,1280]{2,1,0:T(8,128)S(1)}, f32[3,16,1280]{2,1,0:T(8,128)}) fusion(f32[3,32,1280]{2,1,0:T(8,128)} %collective-permute-done.3, s32[]{:T(128)S(6)} %select_n.212, f32[3,32,1280]{2,1,0:T(8,128)S(1)} %collective-permute-done.1, f32[3,32,1280]{2,1,0:T(8,128)S(1)} %copy-done.4, s32[]{:T(128)S(6)} %select_n.214), kind=kLoop, calls=%fused_computation.27 | loop fusion | flops 245760 | bytes 1966088 | tf_op jit(solution)/shard_map/add | solution.py:459
  67.7 1.6 collective-permute-start.4
  69.3 1.4 dynamic-slice_add_fusion.7
  71.2 10.2 %window_tensor.8 = (f32[3,32,1280]{2,1,0:T(8,128)}, f32[3,32,1280]{2,1,0:T(8,128)}, f32[3,32,1280]{2,1,0:T(8,128)}, f32[3,32,1280]{2,1,0:T(8,128)}, f32[2,16,1280]{2,1,0:T(8,128)}) custom-call(s32[4]{0:T(128)} %pad_add_fusion.refs_0_, f32[2,128,640]{2,1,0:T(8,128)} %get-tuple-element.57.refs_1_, f32[2,128,640]{2,1,0:T(8,128)} %collective-permute-done.24.refs_2_, ...), custom_call_target="tpu_custom_call" | custom-call | flops 10066329600 | bytes 6553600 | tf_op jit(solution)/shard_map/window_tensor/pallas_call | solution.py:398
  82.1 0.7 dynamic-slice_add_fusion.14.refs_6_
  82.8 0.8 collective-permute-start.16
  83.7 2.7 %collective-permute-start.5 = (f32[3,8,1280]{2,1,0:T(8,128)}, f32[3,8,1280]{2,1,0:T(8,128)}, u32[]{:S(2)}, u32[]{:S(2)}) collective-permute-start(f32[3,8,1280]{2,1,0:T(8,128)} %dynamic-slice_add_fusion.14.refs_6_), channel_id=1, source_target_pairs={{0,16},{2,18},{4,20},{6,22},{8,24},{10,26},{12,28},{14,30},{16,0},... | collective-permute-start | bytes 368648 | tf_op jit(solution)/shard_map/ppermute | solution.py:462
  86.3 10.1 %window_tensor.9 = (f32[3,32,1280]{2,1,0:T(8,128)}, f32[3,32,1280]{2,1,0:T(8,128)}, f32[3,32,1280]{2,1,0:T(8,128)}, f32[3,32,1280]{2,1,0:T(8,128)}) custom-call(s32[4]{0:T(128)} %pad_add_fusion.refs_0_, f32[2,120,640]{2,1,0:T(8,128)} %get-tuple-element.64.refs_1_, f32[2,120,640]{2,1,0:T(8,128)} %collective-permute-done.30.refs_2_, ...), custom_call_target="tpu_custom_call" | custom-call | flops 9437184000 | bytes 6471680 | tf_op jit(solution)/shard_map/window_tensor/pallas_call | solution.py:398
  96.9 0.9 add_multiply_fusion.4
  97.9 7.6 %collective-permute-done.11 = f32[3,8,1280]{2,1,0:T(8,128)S(1)} collective-permute-done((f32[3,8,1280]{2,1,0:T(8,128)S(1)}, f32[3,8,1280]{2,1,0:T(8,128)S(1)}, u32[]{:S(2)}, u32[]{:S(2)}) %collective-permute-start.11) | collective-permute-done | bytes 122912 | tf_op jit(solution)/shard_map/ppermute | solution.py:462
  105.8 6.1 %collective-permute-done.17 = f32[3,16,1280]{2,1,0:T(8,128)S(1)} collective-permute-done((f32[3,16,1280]{2,1,0:T(8,128)S(1)}, f32[3,16,1280]{2,1,0:T(8,128)S(1)}, u32[]{:S(2)}, u32[]{:S(2)}) %collective-permute-start.17) | collective-permute-done | bytes 245792 | tf_op jit(solution)/shard_map/ppermute | solution.py:462
  112.0 0.8 collective-permute-start.12
  112.9 0.9 collective-permute-start.27
  113.8 5.4 %collective-permute-done.18 = f32[3,8,1280]{2,1,0:T(8,128)S(1)} collective-permute-done((f32[3,8,1280]{2,1,0:T(8,128)S(1)}, f32[3,8,1280]{2,1,0:T(8,128)S(1)}, u32[]{:S(2)}, u32[]{:S(2)}) %collective-permute-start.18) | collective-permute-done | bytes 122912 | tf_op jit(solution)/shard_map/ppermute | solution.py:462
  119.2 0.9 collective-permute-start.19
  120.1 2.2 %collective-permute-start.31 = (f32[3,32,1280]{2,1,0:T(8,128)}, f32[3,32,1280]{2,1,0:T(8,128)S(1)}, u32[]{:S(2)}, u32[]{:S(2)}) collective-permute-start(f32[3,32,1280]{2,1,0:T(8,128)} %get-tuple-element.68), channel_id=1, source_target_pairs={{0,2},{2,0},{4,6},{6,4},{8,10},{10,8},{12,14},{14,12},{16,18},{18,... | collective-permute-start | bytes 1474568 | tf_op jit(solution)/shard_map/ppermute | solution.py:492
  122.5 3.2 %collective-permute-start.20 = (f32[3,8,1280]{2,1,0:T(8,128)S(1)}, f32[3,8,1280]{2,1,0:T(8,128)S(1)}, u32[]{:S(2)}, u32[]{:S(2)}) collective-permute-start(f32[3,8,1280]{2,1,0:T(8,128)S(1)} %pad_maximum_fusion), channel_id=1, source_target_pairs={{0,16},{2,18},{4,20},{6,22},{8,24},{10,26},{12,28},{14,30},{16,0},... | collective-permute-start | bytes 368648 | tf_op jit(solution)/shard_map/ppermute | solution.py:473
  125.9 5.0 %collective-permute-done.20 = f32[3,8,1280]{2,1,0:T(8,128)S(1)} collective-permute-done((f32[3,8,1280]{2,1,0:T(8,128)S(1)}, f32[3,8,1280]{2,1,0:T(8,128)S(1)}, u32[]{:S(2)}, u32[]{:S(2)}) %collective-permute-start.20) | collective-permute-done | bytes 122912 | tf_op jit(solution)/shard_map/ppermute | solution.py:473
  130.9 0.7 collective-permute-start.21
  131.6 4.1 %collective-permute-done.28 = f32[3,16,1280]{2,1,0:T(8,128)S(1)} collective-permute-done((f32[3,16,1280]{2,1,0:T(8,128)S(1)}, f32[3,16,1280]{2,1,0:T(8,128)S(1)}, u32[]{:S(2)}, u32[]{:S(2)}) %collective-permute-start.28) | collective-permute-done | bytes 245792 | tf_op jit(solution)/shard_map/ppermute | solution.py:462
  135.8 1.7 collective-permute-start.34
  137.5 7.1 %collective-permute-done.29 = f32[3,8,1280]{2,1,0:T(8,128)S(1)} collective-permute-done((f32[3,8,1280]{2,1,0:T(8,128)S(1)}, f32[3,8,1280]{2,1,0:T(8,128)S(1)}, u32[]{:S(2)}, u32[]{:S(2)}) %collective-permute-start.29) | collective-permute-done | bytes 122912 | tf_op jit(solution)/shard_map/ppermute | solution.py:462
  144.6 2.5 %collective-permute-start.35 = (f32[3,8,1280]{2,1,0:T(8,128)S(1)}, f32[3,8,1280]{2,1,0:T(8,128)S(1)}, u32[]{:S(2)}, u32[]{:S(2)}) collective-permute-start(f32[3,8,1280]{2,1,0:T(8,128)S(1)} %dynamic-slice_add_fusion.10), channel_id=1, source_target_pairs={{0,16},{2,18},{4,20},{6,22},{8,24},{10,26},{12,28},{14,30},{16,0},... | collective-permute-start | bytes 368648 | tf_op jit(solution)/shard_map/ppermute | solution.py:462
  147.2 5.3 %collective-permute-done.35 = f32[3,8,1280]{2,1,0:T(8,128)S(1)} collective-permute-done((f32[3,8,1280]{2,1,0:T(8,128)S(1)}, f32[3,8,1280]{2,1,0:T(8,128)S(1)}, u32[]{:S(2)}, u32[]{:S(2)}) %collective-permute-start.35) | collective-permute-done | bytes 122912 | tf_op jit(solution)/shard_map/ppermute | solution.py:462
  153.1 1.6 collective-permute-start.22
  154.7 4.1 %collective-permute-done.36 = f32[2,8,1280]{2,1,0:T(8,128)S(1)} collective-permute-done((f32[2,8,1280]{2,1,0:T(8,128)S(1)}, f32[2,8,1280]{2,1,0:T(8,128)S(1)}, u32[]{:S(2)}, u32[]{:S(2)}) %collective-permute-start.36) | collective-permute-done | bytes 81952 | tf_op jit(solution)/shard_map/ppermute | solution.py:473
  159.4 5.0 %collective-permute-done.37 = f32[2,16,1280]{2,1,0:T(8,128)S(1)} collective-permute-done((f32[2,16,1280]{2,1,0:T(8,128)S(1)}, f32[2,16,1280]{2,1,0:T(8,128)S(1)}, u32[]{:S(2)}, u32[]{:S(2)}) %collective-permute-start.37) | collective-permute-done | bytes 163872 | tf_op jit(solution)/shard_map/ppermute | solution.py:473
  164.5 1.2 collective-permute-start.38
  165.8 5.8 %collective-permute-done.38 = f32[2,32,1280]{2,1,0:T(8,128)S(1)} collective-permute-done((f32[2,32,1280]{2,1,0:T(8,128)S(1)}, f32[2,32,1280]{2,1,0:T(8,128)S(1)}, u32[]{:S(2)}, u32[]{:S(2)}) %collective-permute-start.38) | collective-permute-done | bytes 327712 | tf_op jit(solution)/shard_map/ppermute | solution.py:473
  171.8 2.1 %collective-permute-done.39 = f32[2,64,1280]{2,1,0:T(8,128)S(1)} collective-permute-done((f32[2,64,1280]{2,1,0:T(8,128)S(1)}, f32[2,64,1280]{2,1,0:T(8,128)S(1)}, u32[]{:S(2)}, u32[]{:S(2)}) %collective-permute-start.39) | collective-permute-done | bytes 655392 | tf_op jit(solution)/shard_map/ppermute | solution.py:473
  175.3 1.7 copy-done
  177.0 0.9 slice_dynamic-update-slice_fusion
  (120 shorter events, 7.8 us)
Async XLA Ops:
  2.6 19.6 %collective-permute-start = (f32[2,136,640]{2,1,0:T(8,128)}, f32[2,136,640]{2,1,0:T(8,128)S(1)}, u32[]{:S(2)}, u32[]{:S(2)}) collective-permute-start(f32[2,136,640]{2,1,0:T(8,128)} %pieces_of.4), channel_id=1, source_target_pairs={{0,1},{1,0},{2,3},{3,2},{4,5},{5,4},{6,7},{7,6},{8,9},{9,8},{10,11... | collective-permute-start | bytes 2088968 | tf_op jit(solution)/shard_map/ppermute | solution.py:444
  9.2 26.7 %collective-permute-start.6 = (f32[2,128,640]{2,1,0:T(8,128)}, f32[2,128,640]{2,1,0:T(8,128)S(1)}, u32[]{:S(2)}, u32[]{:S(2)}) collective-permute-start(f32[2,128,640]{2,1,0:T(8,128)} %get-tuple-element.44), channel_id=1, source_target_pairs={{0,1},{1,0},{2,3},{3,2},{4,5},{5,4},{6,7},{7,6},{8,9},{9,8},{10,11... | collective-permute-start | bytes 1966088 | tf_op jit(solution)/shard_map/ppermute | solution.py:448
  33.7 14.8 %collective-permute-start.2 = (f32[3,32,1280]{2,1,0:T(8,128)}, f32[3,32,1280]{2,1,0:T(8,128)S(1)}, u32[]{:S(2)}, u32[]{:S(2)}) collective-permute-start(f32[3,32,1280]{2,1,0:T(8,128)} %get-tuple-element.42), channel_id=1, source_target_pairs={{0,2},{2,0},{4,6},{6,4},{8,10},{10,8},{12,14},{14,12},{16,18},{18,... | collective-permute-start | bytes 1474568 | tf_op jit(solution)/shard_map/ppermute | solution.py:491
  33.8 17.9 %collective-permute-start.13 = (f32[2,128,640]{2,1,0:T(8,128)}, f32[2,128,640]{2,1,0:T(8,128)S(1)}, u32[]{:S(2)}, u32[]{:S(2)}) collective-permute-start(f32[2,128,640]{2,1,0:T(8,128)} %gated.3), channel_id=1, source_target_pairs={{0,1},{1,0},{2,3},{3,2},{4,5},{5,4},{6,7},{7,6},{8,9},{9,8},{10,11... | collective-permute-start | bytes 1966088 | tf_op jit(solution)/shard_map/ppermute | solution.py:448
  46.8 2.9 %collective-permute-start.8 = (f32[3,32,1280]{2,1,0:T(8,128)}, f32[3,32,1280]{2,1,0:T(8,128)S(1)}, u32[]{:S(2)}, u32[]{:S(2)}) collective-permute-start(f32[3,32,1280]{2,1,0:T(8,128)} %get-tuple-element.49), channel_id=1, source_target_pairs={{0,2},{2,0},{4,6},{6,4},{8,10},{10,8},{12,14},{14,12},{16,18},{18,... | collective-permute-start | bytes 1474568 | tf_op jit(solution)/shard_map/ppermute | solution.py:491
  47.1 23.6 %collective-permute-start.24 = (f32[2,128,640]{2,1,0:T(8,128)}, f32[2,128,640]{2,1,0:T(8,128)}, u32[]{:S(2)}, u32[]{:S(2)}) collective-permute-start(f32[2,128,640]{2,1,0:T(8,128)} %gated.4), channel_id=1, source_target_pairs={{0,1},{1,0},{2,3},{3,2},{4,5},{5,4},{6,7},{7,6},{8,9},{9,8},{10,11... | collective-permute-start | bytes 1966088 | tf_op jit(solution)/shard_map/ppermute | solution.py:448
  48.4 15.7 %collective-permute-start.1 = (f32[3,32,1280]{2,1,0:T(8,128)}, f32[3,32,1280]{2,1,0:T(8,128)S(1)}, u32[]{:S(2)}, u32[]{:S(2)}) collective-permute-start(f32[3,32,1280]{2,1,0:T(8,128)} %get-tuple-element.40), channel_id=1, source_target_pairs={{0,2},{2,0},{4,6},{6,4},{8,10},{10,8},{12,14},{14,12},{16,18},{18,... | collective-permute-start | bytes 1474568 | tf_op jit(solution)/shard_map/ppermute | solution.py:492
  48.5 19.1 %collective-permute-start.7 = (f32[3,32,1280]{2,1,0:T(8,128)}, f32[3,32,1280]{2,1,0:T(8,128)}, u32[]{:S(2)}, u32[]{:S(2)}) collective-permute-start(f32[3,32,1280]{2,1,0:T(8,128)} %get-tuple-element.47), channel_id=1, source_target_pairs={{0,2},{2,0},{4,6},{6,4},{8,10},{10,8},{12,14},{14,12},{16,18},{18,... | collective-permute-start | bytes 1474568 | tf_op jit(solution)/shard_map/ppermute | solution.py:492
  49.7 14.4 %collective-permute-start.3 = (f32[3,32,1280]{2,1,0:T(8,128)}, f32[3,32,1280]{2,1,0:T(8,128)}, u32[]{:S(2)}, u32[]{:S(2)}) collective-permute-start(f32[3,32,1280]{2,1,0:T(8,128)} %add.295.refs_4_), channel_id=1, source_target_pairs={{0,4},{2,10},{4,0},{6,14},{8,12},{10,2},{12,8},{14,6},{16,20},{18,... | collective-permute-start | bytes 1474568 | tf_op jit(solution)/shard_map/ppermute | solution.py:467
  51.3 12.7 %copy-start.13 = (f32[3,32,1280]{2,1,0:T(8,128)}, f32[3,32,1280]{2,1,0:T(8,128)S(1)}, u32[]{:S(2)}) copy-start(f32[3,32,1280]{2,1,0:T(8,128)S(1)} %add.310.refs_4_) | copy-start | bytes 1474564
  51.7 16.0 %collective-permute-start.9 = (f32[3,32,1280]{2,1,0:T(8,128)S(1)}, f32[3,32,1280]{2,1,0:T(8,128)}, u32[]{:S(2)}, u32[]{:S(2)}) collective-permute-start(f32[3,32,1280]{2,1,0:T(8,128)S(1)} %add.310.refs_4_), channel_id=1, source_target_pairs={{0,4},{2,10},{4,0},{6,14},{8,12},{10,2},{12,8},{14,6},{16,20},{18,... | collective-permute-start | bytes 1474568 | tf_op jit(solution)/shard_map/ppermute | solution.py:467
  64.1 17.3 %collective-permute-start.15 = (f32[3,32,1280]{2,1,0:T(8,128)}, f32[3,32,1280]{2,1,0:T(8,128)S(1)}, u32[]{:S(2)}, u32[]{:S(2)}) collective-permute-start(f32[3,32,1280]{2,1,0:T(8,128)} %get-tuple-element.56), channel_id=1, source_target_pairs={{0,2},{2,0},{4,6},{6,4},{8,10},{10,8},{12,14},{14,12},{16,18},{18,... | collective-permute-start | bytes 1474568 | tf_op jit(solution)/shard_map/ppermute | solution.py:491
  64.2 19.5 %collective-permute-start.30 = (f32[2,120,640]{2,1,0:T(8,128)}, f32[2,120,640]{2,1,0:T(8,128)}, u32[]{:S(2)}, u32[]{:S(2)}) collective-permute-start(f32[2,120,640]{2,1,0:T(8,128)} %gated.5), channel_id=1, source_target_pairs={{0,1},{1,0},{2,3},{3,2},{4,5},{5,4},{6,7},{7,6},{8,9},{9,8},{10,11... | collective-permute-start | bytes 1843208 | tf_op jit(solution)/shard_map/ppermute | solution.py:448
  67.6 37.9 %collective-permute-start.14 = (f32[3,32,1280]{2,1,0:T(8,128)}, f32[3,32,1280]{2,1,0:T(8,128)S(1)}, u32[]{:S(2)}, u32[]{:S(2)}) collective-permute-start(f32[3,32,1280]{2,1,0:T(8,128)} %get-tuple-element.54), channel_id=1, source_target_pairs={{0,2},{2,0},{4,6},{6,4},{8,10},{10,8},{12,14},{14,12},{16,18},{18,... | collective-permute-start | bytes 1474568 | tf_op jit(solution)/shard_map/ppermute | solution.py:492
  67.7 13.9 %collective-permute-start.4 = (f32[3,16,1280]{2,1,0:T(8,128)}, f32[3,16,1280]{2,1,0:T(8,128)S(1)}, u32[]{:S(2)}, u32[]{:S(2)}) collective-permute-start(f32[3,16,1280]{2,1,0:T(8,128)} %get-tuple-element.80.refs_5_), channel_id=1, source_target_pairs={{0,8},{2,6},{4,12},{6,2},{8,0},{10,14},{12,4},{14,10},{16,24},{18,... | collective-permute-start | bytes 737288 | tf_op jit(solution)/shard_map/ppermute | solution.py:462
  70.7 10.7 %copy-start.16 = (f32[3,16,1280]{2,1,0:T(8,128)}, f32[3,16,1280]{2,1,0:T(8,128)S(1)}, u32[]{:S(2)}) copy-start(f32[3,16,1280]{2,1,0:T(8,128)S(1)} %get-tuple-element.82.refs_5_) | copy-start | bytes 737284
  70.7 12.1 %collective-permute-start.10 = (f32[3,16,1280]{2,1,0:T(8,128)S(1)}, f32[3,16,1280]{2,1,0:T(8,128)S(1)}, u32[]{:S(2)}, u32[]{:S(2)}) collective-permute-start(f32[3,16,1280]{2,1,0:T(8,128)S(1)} %get-tuple-element.82.refs_5_), channel_id=1, source_target_pairs={{0,8},{2,6},{4,12},{6,2},{8,0},{10,14},{12,4},{14,10},{16,24},{18,... | collective-permute-start | bytes 737288 | tf_op jit(solution)/shard_map/ppermute | solution.py:462
  71.2 10.3 %copy-start.14 = (f32[3,32,1280]{2,1,0:T(8,128)S(1)}, f32[3,32,1280]{2,1,0:T(8,128)}, u32[]{:S(2)}) copy-start(f32[3,32,1280]{2,1,0:T(8,128)} %get-tuple-element.55) | copy-start | bytes 1474564
  81.4 31.4 %collective-permute-start.26 = (f32[3,32,1280]{2,1,0:T(8,128)}, f32[3,32,1280]{2,1,0:T(8,128)S(1)}, u32[]{:S(2)}, u32[]{:S(2)}) collective-permute-start(f32[3,32,1280]{2,1,0:T(8,128)} %get-tuple-element.63), channel_id=1, source_target_pairs={{0,2},{2,0},{4,6},{6,4},{8,10},{10,8},{12,14},{14,12},{16,18},{18,... | collective-permute-start | bytes 1474568 | tf_op jit(solution)/shard_map/ppermute | solution.py:491
  81.6 44.1 %collective-permute-start.25 = (f32[3,32,1280]{2,1,0:T(8,128)}, f32[3,32,1280]{2,1,0:T(8,128)S(1)}, u32[]{:S(2)}, u32[]{:S(2)}) collective-permute-start(f32[3,32,1280]{2,1,0:T(8,128)} %get-tuple-element.61), channel_id=1, source_target_pairs={{0,2},{2,0},{4,6},{6,4},{8,10},{10,8},{12,14},{14,12},{16,18},{18,... | collective-permute-start | bytes 1474568 | tf_op jit(solution)/shard_map/ppermute | solution.py:492
  82.8 22.7 %collective-permute-start.16 = (f32[3,32,1280]{2,1,0:T(8,128)S(1)}, f32[3,32,1280]{2,1,0:T(8,128)S(1)}, u32[]{:S(2)}, u32[]{:S(2)}) collective-permute-start(f32[3,32,1280]{2,1,0:T(8,128)S(1)} %add.322.refs_4_), channel_id=1, source_target_pairs={{0,4},{2,10},{4,0},{6,14},{8,12},{10,2},{12,8},{14,6},{16,20},{18,... | collective-permute-start | bytes 1474568 | tf_op jit(solution)/shard_map/ppermute | solution.py:467
  83.7 12.8 %collective-permute-start.5 = (f32[3,8,1280]{2,1,0:T(8,128)}, f32[3,8,1280]{2,1,0:T(8,128)}, u32[]{:S(2)}, u32[]{:S(2)}) collective-permute-start(f32[3,8,1280]{2,1,0:T(8,128)} %dynamic-slice_add_fusion.14.refs_6_), channel_id=1, source_target_pairs={{0,16},{2,18},{4,20},{6,22},{8,24},{10,26},{12,28},{14,30},{16,0},... | collective-permute-start | bytes 368648 | tf_op jit(solution)/shard_map/ppermute | solution.py:462
  86.3 19.2 %copy-start.8 = (f32[3,32,1280]{2,1,0:T(8,128)S(1)}, f32[3,32,1280]{2,1,0:T(8,128)}, u32[]{:S(2)}) copy-start(f32[3,32,1280]{2,1,0:T(8,128)} %get-tuple-element.53) | copy-start | bytes 1474564
  96.5 9.0 %collective-permute-start.11 = (f32[3,8,1280]{2,1,0:T(8,128)S(1)}, f32[3,8,1280]{2,1,0:T(8,128)S(1)}, u32[]{:S(2)}, u32[]{:S(2)}) collective-permute-start(f32[3,8,1280]{2,1,0:T(8,128)S(1)} %dynamic-slice_add_fusion.13), channel_id=1, source_target_pairs={{0,16},{2,18},{4,20},{6,22},{8,24},{10,26},{12,28},{14,30},{16,0},... | collective-permute-start | bytes 368648 | tf_op jit(solution)/shard_map/ppermute | solution.py:462
  97.8 15.0 %copy-start.11 = (f32[3,32,1280]{2,1,0:T(8,128)S(1)}, f32[3,32,1280]{2,1,0:T(8,128)}, u32[]{:S(2)}) copy-start(f32[3,32,1280]{2,1,0:T(8,128)} %get-tuple-element.62) | copy-start | bytes 1474564
  105.4 14.7 %collective-permute-start.32 = (f32[3,32,1280]{2,1,0:T(8,128)}, f32[3,32,1280]{2,1,0:T(8,128)S(1)}, u32[]{:S(2)}, u32[]{:S(2)}) collective-permute-start(f32[3,32,1280]{2,1,0:T(8,128)} %get-tuple-element.70), channel_id=1, source_target_pairs={{0,2},{2,0},{4,6},{6,4},{8,10},{10,8},{12,14},{14,12},{16,18},{18,... | collective-permute-start | bytes 1474568 | tf_op jit(solution)/shard_map/ppermute | solution.py:491
  105.6 16.7 %copy-start.12 = (f32[3,32,1280]{2,1,0:T(8,128)S(1)}, f32[3,32,1280]{2,1,0:T(8,128)}, u32[]{:S(2)}) copy-start(f32[3,32,1280]{2,1,0:T(8,128)} %get-tuple-element.69) | copy-start | bytes 1474564
  105.6 6.3 %collective-permute-start.17 = (f32[3,16,1280]{2,1,0:T(8,128)S(1)}, f32[3,16,1280]{2,1,0:T(8,128)S(1)}, u32[]{:S(2)}, u32[]{:S(2)}) collective-permute-start(f32[3,16,1280]{2,1,0:T(8,128)S(1)} %get-tuple-element.84), channel_id=1, source_target_pairs={{0,8},{2,6},{4,12},{6,2},{8,0},{10,14},{12,4},{14,10},{16,24},{18,... | collective-permute-start | bytes 737288 | tf_op jit(solution)/shard_map/ppermute | solution.py:462
  111.9 7.2 %collective-permute-start.18 = (f32[3,8,1280]{2,1,0:T(8,128)S(1)}, f32[3,8,1280]{2,1,0:T(8,128)S(1)}, u32[]{:S(2)}, u32[]{:S(2)}) collective-permute-start(f32[3,8,1280]{2,1,0:T(8,128)S(1)} %dynamic-slice_add_fusion.12), channel_id=1, source_target_pairs={{0,16},{2,18},{4,20},{6,22},{8,24},{10,26},{12,28},{14,30},{16,0},... | collective-permute-start | bytes 368648 | tf_op jit(solution)/shard_map/ppermute | solution.py:462
  112.0 10.4 %collective-permute-start.12 = (f32[2,8,1280]{2,1,0:T(8,128)S(1)}, f32[2,8,1280]{2,1,0:T(8,128)S(1)}, u32[]{:S(2)}, u32[]{:S(2)}) collective-permute-start(f32[2,8,1280]{2,1,0:T(8,128)S(1)} %pad_maximum_fusion.1), channel_id=1, source_target_pairs={{0,1},{1,0},{2,3},{3,2},{4,5},{5,4},{6,7},{7,6},{8,9},{9,8},{10,11... | collective-permute-start | bytes 245768 | tf_op jit(solution)/shard_map/ppermute | solution.py:501
  112.8 12.8 %copy-start.6 = (f32[3,32,1280]{2,1,0:T(8,128)S(1)}, f32[3,32,1280]{2,1,0:T(8,128)}, u32[]{:S(2)}) copy-start(f32[3,32,1280]{2,1,0:T(8,128)} %get-tuple-element.60) | copy-start | bytes 1474564
  112.9 12.8 %collective-permute-start.27 = (f32[3,32,1280]{2,1,0:T(8,128)S(1)}, f32[3,32,1280]{2,1,0:T(8,128)S(1)}, u32[]{:S(2)}, u32[]{:S(2)}) collective-permute-start(f32[3,32,1280]{2,1,0:T(8,128)S(1)} %add.335), channel_id=1, source_target_pairs={{0,4},{2,10},{4,0},{6,14},{8,12},{10,2},{12,8},{14,6},{16,20},{18,... | collective-permute-start | bytes 1474568 | tf_op jit(solution)/shard_map/ppermute | solution.py:467
  119.2 3.3 %collective-permute-start.19 = (f32[8,1280]{1,0:T(8,128)S(1)}, f32[8,1280]{1,0:T(8,128)S(1)}, u32[]{:S(2)}, u32[]{:S(2)}) collective-permute-start(f32[8,1280]{1,0:T(8,128)S(1)} %fusion.18), channel_id=1, source_target_pairs={{0,0},{1,2},{2,1},{3,3},{4,4},{5,10},{6,9},{7,7},{8,8},{9,6},{10,5... | collective-permute-start | bytes 122888 | tf_op jit(solution)/shard_map/ppermute | solution.py:512
  120.1 15.6 %collective-permute-start.31 = (f32[3,32,1280]{2,1,0:T(8,128)}, f32[3,32,1280]{2,1,0:T(8,128)S(1)}, u32[]{:S(2)}, u32[]{:S(2)}) collective-permute-start(f32[3,32,1280]{2,1,0:T(8,128)} %get-tuple-element.68), channel_id=1, source_target_pairs={{0,2},{2,0},{4,6},{6,4},{8,10},{10,8},{12,14},{14,12},{16,18},{18,... | collective-permute-start | bytes 1474568 | tf_op jit(solution)/shard_map/ppermute | solution.py:492
  122.4 13.4 %copy-start.7 = (f32[3,32,1280]{2,1,0:T(8,128)S(1)}, f32[3,32,1280]{2,1,0:T(8,128)}, u32[]{:S(2)}) copy-start(f32[3,32,1280]{2,1,0:T(8,128)} %get-tuple-element.67) | copy-start | bytes 1474564
  122.4 13.3 %collective-permute-start.33 = (f32[3,32,1280]{2,1,0:T(8,128)S(1)}, f32[3,32,1280]{2,1,0:T(8,128)S(1)}, u32[]{:S(2)}, u32[]{:S(2)}) collective-permute-start(f32[3,32,1280]{2,1,0:T(8,128)S(1)} %add.347), channel_id=1, source_target_pairs={{0,4},{2,10},{4,0},{6,14},{8,12},{10,2},{12,8},{14,6},{16,20},{18,... | collective-permute-start | bytes 1474568 | tf_op jit(solution)/shard_map/ppermute | solution.py:467
  122.5 8.4 %collective-permute-start.20 = (f32[3,8,1280]{2,1,0:T(8,128)S(1)}, f32[3,8,1280]{2,1,0:T(8,128)S(1)}, u32[]{:S(2)}, u32[]{:S(2)}) collective-permute-start(f32[3,8,1280]{2,1,0:T(8,128)S(1)} %pad_maximum_fusion), channel_id=1, source_target_pairs={{0,16},{2,18},{4,20},{6,22},{8,24},{10,26},{12,28},{14,30},{16,0},... | collective-permute-start | bytes 368648 | tf_op jit(solution)/shard_map/ppermute | solution.py:473
  125.8 9.9 %collective-permute-start.28 = (f32[3,16,1280]{2,1,0:T(8,128)S(1)}, f32[3,16,1280]{2,1,0:T(8,128)S(1)}, u32[]{:S(2)}, u32[]{:S(2)}) collective-permute-start(f32[3,16,1280]{2,1,0:T(8,128)S(1)} %get-tuple-element.76), channel_id=1, source_target_pairs={{0,8},{2,6},{4,12},{6,2},{8,0},{10,14},{12,4},{14,10},{16,24},{18,... | collective-permute-start | bytes 737288 | tf_op jit(solution)/shard_map/ppermute | solution.py:462
  130.9 22.2 %collective-permute-start.21 = (f32[3,16,1280]{2,1,0:T(8,128)S(1)}, f32[3,16,1280]{2,1,0:T(8,128)S(1)}, u32[]{:S(2)}, u32[]{:S(2)}) collective-permute-start(f32[3,16,1280]{2,1,0:T(8,128)S(1)} %maximum_select_fusion.7), channel_id=1, source_target_pairs={{0,8},{2,6},{4,12},{6,2},{8,0},{10,14},{12,4},{14,10},{16,24},{18,... | collective-permute-start | bytes 737288 | tf_op jit(solution)/shard_map/ppermute | solution.py:473
  135.6 8.9 %collective-permute-start.29 = (f32[3,8,1280]{2,1,0:T(8,128)S(1)}, f32[3,8,1280]{2,1,0:T(8,128)S(1)}, u32[]{:S(2)}, u32[]{:S(2)}) collective-permute-start(f32[3,8,1280]{2,1,0:T(8,128)S(1)} %dynamic-slice_add_fusion.11), channel_id=1, source_target_pairs={{0,16},{2,18},{4,20},{6,22},{8,24},{10,26},{12,28},{14,30},{16,0},... | collective-permute-start | bytes 368648 | tf_op jit(solution)/shard_map/ppermute | solution.py:462
  135.8 8.8 %collective-permute-start.34 = (f32[3,16,1280]{2,1,0:T(8,128)S(1)}, f32[3,16,1280]{2,1,0:T(8,128)S(1)}, u32[]{:S(2)}, u32[]{:S(2)}) collective-permute-start(f32[3,16,1280]{2,1,0:T(8,128)S(1)} %get-tuple-element.78), channel_id=1, source_target_pairs={{0,8},{2,6},{4,12},{6,2},{8,0},{10,14},{12,4},{14,10},{16,24},{18,... | collective-permute-start | bytes 737288 | tf_op jit(solution)/shard_map/ppermute | solution.py:462
  144.6 7.9 %collective-permute-start.35 = (f32[3,8,1280]{2,1,0:T(8,128)S(1)}, f32[3,8,1280]{2,1,0:T(8,128)S(1)}, u32[]{:S(2)}, u32[]{:S(2)}) collective-permute-start(f32[3,8,1280]{2,1,0:T(8,128)S(1)} %dynamic-slice_add_fusion.10), channel_id=1, source_target_pairs={{0,16},{2,18},{4,20},{6,22},{8,24},{10,26},{12,28},{14,30},{16,0},... | collective-permute-start | bytes 368648 | tf_op jit(solution)/shard_map/ppermute | solution.py:462
  152.6 6.2 %collective-permute-start.36 = (f32[2,8,1280]{2,1,0:T(8,128)S(1)}, f32[2,8,1280]{2,1,0:T(8,128)S(1)}, u32[]{:S(2)}, u32[]{:S(2)}) collective-permute-start(f32[2,8,1280]{2,1,0:T(8,128)S(1)} %pad_maximum_fusion.2), channel_id=1, source_target_pairs={{0,16},{2,18},{4,20},{6,22},{8,24},{10,26},{12,28},{14,30},{16,0},... | collective-permute-start | bytes 245768 | tf_op jit(solution)/shard_map/ppermute | solution.py:473
  153.1 12.5 %collective-permute-start.22 = (f32[3,32,1280]{2,1,0:T(8,128)S(1)}, f32[3,32,1280]{2,1,0:T(8,128)S(1)}, u32[]{:S(2)}, u32[]{:S(2)}) collective-permute-start(f32[3,32,1280]{2,1,0:T(8,128)S(1)} %maximum_select_fusion.5), channel_id=1, source_target_pairs={{0,4},{2,10},{4,0},{6,14},{8,12},{10,2},{12,8},{14,6},{16,20},{18,... | collective-permute-start | bytes 1474568 | tf_op jit(solution)/shard_map/ppermute | solution.py:473
  158.9 5.6 %collective-permute-start.37 = (f32[2,16,1280]{2,1,0:T(8,128)S(1)}, f32[2,16,1280]{2,1,0:T(8,128)S(1)}, u32[]{:S(2)}, u32[]{:S(2)}) collective-permute-start(f32[2,16,1280]{2,1,0:T(8,128)S(1)} %maximum_select_fusion.8), channel_id=1, source_target_pairs={{0,8},{2,6},{4,12},{6,2},{8,0},{10,14},{12,4},{14,10},{16,24},{18,... | collective-permute-start | bytes 491528 | tf_op jit(solution)/shard_map/ppermute | solution.py:473
  164.5 7.1 %collective-permute-start.38 = (f32[2,32,1280]{2,1,0:T(8,128)S(1)}, f32[2,32,1280]{2,1,0:T(8,128)S(1)}, u32[]{:S(2)}, u32[]{:S(2)}) collective-permute-start(f32[2,32,1280]{2,1,0:T(8,128)S(1)} %maximum_select_fusion.6), channel_id=1, source_target_pairs={{0,4},{2,10},{4,0},{6,14},{8,12},{10,2},{12,8},{14,6},{16,20},{18,... | collective-permute-start | bytes 983048 | tf_op jit(solution)/shard_map/ppermute | solution.py:473
  165.7 8.2 %collective-permute-start.23 = (f32[3,64,1280]{2,1,0:T(8,128)S(1)}, f32[3,64,1280]{2,1,0:T(8,128)S(1)}, u32[]{:S(2)}, u32[]{:S(2)}) collective-permute-start(f32[3,64,1280]{2,1,0:T(8,128)S(1)} %maximum_select_fusion.3), channel_id=1, source_target_pairs={{0,2},{2,0},{4,6},{6,4},{8,10},{10,8},{12,14},{14,12},{16,18},{18,... | collective-permute-start | bytes 2949128 | tf_op jit(solution)/shard_map/ppermute | solution.py:473
  171.7 2.2 %collective-permute-start.39 = (f32[2,64,1280]{2,1,0:T(8,128)S(1)}, f32[2,64,1280]{2,1,0:T(8,128)S(1)}, u32[]{:S(2)}, u32[]{:S(2)}) collective-permute-start(f32[2,64,1280]{2,1,0:T(8,128)S(1)} %maximum_select_fusion.4), channel_id=1, source_target_pairs={{0,2},{2,0},{4,6},{6,4},{8,10},{10,8},{12,14},{14,12},{16,18},{18,... | collective-permute-start | bytes 1966088 | tf_op jit(solution)/shard_map/ppermute | solution.py:473
  (9 other events, 23.4 us)

commit v19 on v17

--- a/solution.py
+++ b/solution.py
@@ -16,7 +16,7 @@
 LANE = 128
 VMEM_LIMIT = 60 * 1024 * 1024
 KERNEL_WORK = 8
-ORDER = ((2, 4, 8), (4, 8, 2))
+ORDER = ((2, 4, 8), (4, 2, 8))
 BATCHES = ((0, 1, 2), (3, 4))
 AHEAD = ((), (), (), (), (0,))
 

time: 200 us -> 188 us (0.940)
  the two profiles are of different devices: /device:TPU:7 before, /device:TPU:0 now
where the time goes in v19:
time: 188 us
  waiting for transfers between devices  80.4 us (43%)
  Pallas kernels  61.3 us (33%)
  starting transfers between devices  26.7 us (14%)
  other arithmetic  11.7 us (6%)
  local copies, waits for them, and re-layouts  7.13 us (4%)
    pallas_call x5, Pallas kernels, window_tensor(): pl.pallas_call(functools.partial(window_kernel, window, slot, len(waits))...  51.2 us
    ppermute x8, waiting for transfers between devices, doubled(): beside = lax.ppermute(part, 'mem', cores if step < 0 else ways[step])  29.8 us
    ppermute x2, waiting for transfers between devices, across(): return ([kept, kept_more, lax.ppermute(leaves, 'mem', ways[step])], leaves)  17.7 us
    ppermute x4, waiting for transfers between devices, halved(): return ([total(mine), lax.ppermute(leaves, 'mem', ways[step])], leaves)  17.2 us
    pallas_call x3, Pallas kernels, pieces_of(): pl.pallas_call(functools.partial(pieces_kernel, windows, slots, count), i...  10.2 us
    ppermute x1, waiting for transfers between devices, by_levels(): remotes = [lax.ppermute(piece, 'band', swap)]  8.3 us
    ppermute x4, starting transfers between devices, halved(): return ([total(mine), lax.ppermute(leaves, 'mem', ways[step])], leaves)  7.96 us
    ppermute x3, starting transfers between devices, by_levels(): remotes.append(lax.ppermute(piece, 'band', swap))  6.25 us
  transfers between devices with their start and end apart: 25, of which 15 were waited for; matrix products, arithmetic and copies ran while one was open for 6% of the time, Pallas kernels for 31%

profile of v19, /device:TPU:0, one launch (start us, length us, event | category | flops | bytes accessed | tf_op | source)
XLA Modules:
  0.0 187.7 jit_solution(5642272870250165341)
XLA Ops:
  0.0 2.6 %pieces_of.5 = f32[2,136,640]{2,1,0:T(8,128)} custom-call(s32[1]{0:T(128)} %bitcast.5.level_ref, f32[2,2,640,640]{3,2,1,0:T(8,128)} %bitcast.28), custom_call_target="tpu_custom_call" | custom-call | bytes 5242880 | tf_op jit(solution)/shard_map/pieces_of/pallas_call | solution.py:210
  2.6 3.0 %collective-permute-start = (f32[2,136,640]{2,1,0:T(8,128)}, f32[2,136,640]{2,1,0:T(8,128)S(1)}, u32[]{:S(2)}, u32[]{:S(2)}) collective-permute-start(f32[2,136,640]{2,1,0:T(8,128)} %pieces_of.5), channel_id=1, source_target_pairs={{0,1},{1,0},{2,3},{3,2},{4,5},{5,4},{6,7},{7,6},{8,9},{9,8},{10,11... | collective-permute-start | bytes 2088968 | tf_op jit(solution)/shard_map/ppermute | solution.py:451
  5.6 3.6 %pieces_of.4 = (f32[2,128,640]{2,1,0:T(8,128)}, f32[2,128,640]{2,1,0:T(8,128)}, f32[2,128,640]{2,1,0:T(8,128)}, f32[2,120,640]{2,1,0:T(8,128)}) custom-call(s32[1]{0:T(128)} %bitcast.5.level_ref, f32[2,2,640,640]{3,2,1,0:T(8,128)} %bitcast.29), custom_call_target="tpu_custom_call" | custom-call | bytes 10485760 | tf_op jit(solution)/shard_map/pieces_of/pallas_call | solution.py:210
  9.3 4.0 %pieces_of.3 = (f32[2,136,640]{2,1,0:T(8,128)}, f32[2,128,640]{2,1,0:T(8,128)}, f32[2,128,640]{2,1,0:T(8,128)}, f32[2,128,640]{2,1,0:T(8,128)}, f32[2,120,640]{2,1,0:T(8,128)}) custom-call(s32[1]{0:T(128)} %bitcast.level_ref, f32[2,2,640,640]{3,2,1,0:T(8,128)} %bitcast.30), custom_call_target="tpu_custom_call" | custom-call | bytes 13107200 | tf_op jit(solution)/shard_map/pieces_of/pallas_call | solution.py:210
  13.3 0.6 pad_add_fusion.refs_0_
  13.9 8.3 %collective-permute-done.refs_1_.refs_2_ = f32[2,136,640]{2,1,0:T(8,128)S(1)} collective-permute-done((f32[2,136,640]{2,1,0:T(8,128)}, f32[2,136,640]{2,1,0:T(8,128)S(1)}, u32[]{:S(2)}, u32[]{:S(2)}) %collective-permute-start) | collective-permute-done | bytes 696352 | tf_op jit(solution)/shard_map/ppermute | solution.py:451
  22.2 0.9 copy-done.3
  23.1 2.1 %collective-permute-start.1 = (f32[2,128,640]{2,1,0:T(8,128)}, f32[2,128,640]{2,1,0:T(8,128)S(1)}, u32[]{:S(2)}, u32[]{:S(2)}) collective-permute-start(f32[2,128,640]{2,1,0:T(8,128)} %gated.4), channel_id=1, source_target_pairs={{0,1},{1,0},{2,3},{3,2},{4,5},{5,4},{6,7},{7,6},{8,9},{9,8},{10,11... | collective-permute-start | bytes 1966088 | tf_op jit(solution)/shard_map/ppermute | solution.py:496
  25.2 10.5 %window_tensor.5 = (f32[3,3,32,1280]{3,2,1,0:T(8,128)}, f32[3,3,32,1280]{3,2,1,0:T(8,128)}, f32[3,3,32,1280]{3,2,1,0:T(8,128)}, f32[3,3,32,1280]{3,2,1,0:T(8,128)}, f32[2,16,1280]{2,1,0:T(8,128)}) custom-call(s32[4]{0:T(128)} %pad_add_fusion.refs_0_, f32[2,136,640]{2,1,0:T(8,128)} %get-tuple-element.42.refs_1_, f32[2,136,640]{2,1,0:T(8,128)} %copy-done.3, ...), custom_call_target="tpu_custom_call" | custom-call | flops 10695475200 | bytes 6635520 | tf_op jit(solution)/shard_map/window_tensor/pallas_call | solution.py:404
  35.6 0.6 collective-permute-done.2.refs_2_.refs_1_
  36.3 0.9 copy-done.4
  37.2 2.1 %collective-permute-start.15 = (f32[2,128,640]{2,1,0:T(8,128)}, f32[2,128,640]{2,1,0:T(8,128)S(1)}, u32[]{:S(2)}, u32[]{:S(2)}) collective-permute-start(f32[2,128,640]{2,1,0:T(8,128)} %gated.7), channel_id=1, source_target_pairs={{0,1},{1,0},{2,3},{3,2},{4,5},{5,4},{6,7},{7,6},{8,9},{9,8},{10,11... | collective-permute-start | bytes 1966088 | tf_op jit(solution)/shard_map/ppermute | solution.py:496
  39.2 10.1 %window_tensor.6 = (f32[3,3,32,1280]{3,2,1,0:T(8,128)}, f32[3,3,32,1280]{3,2,1,0:T(8,128)}, f32[3,3,32,1280]{3,2,1,0:T(8,128)}, f32[3,3,32,1280]{3,2,1,0:T(8,128)}, f32[2,16,1280]{2,1,0:T(8,128)}) custom-call(s32[4]{0:T(128)} %pad_add_fusion.refs_0_, ...), custom_call_target="tpu_custom_call", output_to_operand_aliasing={{0}: (4, {}), {1}: (5, {}), {2}: (6, {}), {3}: (7, {})} | custom-call | flops 10066329600 | bytes 6553600 | tf_op jit(solution)/shard_map/window_tensor/pallas_call | solution.py:404
  49.3 1.0 collective-permute-done.1.refs_2_.refs_1_
  50.3 0.9 copy-done.5
  51.2 10.1 %window_tensor.7 = (f32[3,3,32,1280]{3,2,1,0:T(8,128)}, f32[3,3,32,1280]{3,2,1,0:T(8,128)}, f32[3,3,32,1280]{3,2,1,0:T(8,128)}, f32[3,3,32,1280]{3,2,1,0:T(8,128)}, f32[2,16,1280]{2,1,0:T(8,128)}) custom-call(s32[4]{0:T(128)} %pad_add_fusion.refs_0_, ...), custom_call_target="tpu_custom_call", output_to_operand_aliasing={{0}: (4, {}), {1}: (5, {}), {2}: (6, {}), {3}: (7, {})} | custom-call | flops 10066329600 | bytes 6553600 | tf_op jit(solution)/shard_map/window_tensor/pallas_call | solution.py:404
  61.4 2.1 %collective-permute-start.5 = (f32[2,120,640]{2,1,0:T(8,128)}, f32[2,120,640]{2,1,0:T(8,128)S(1)}, u32[]{:S(2)}, u32[]{:S(2)}) collective-permute-start(f32[2,120,640]{2,1,0:T(8,128)} %gated.5), channel_id=1, source_target_pairs={{0,1},{1,0},{2,3},{3,2},{4,5},{5,4},{6,7},{7,6},{8,9},{9,8},{10,11... | collective-permute-start | bytes 1843208 | tf_op jit(solution)/shard_map/ppermute | solution.py:496
  63.7 0.8 copy-done.7
  64.5 10.4 %window_tensor.8 = (f32[2,3,32,1280]{3,2,1,0:T(8,128)}, f32[2,3,32,1280]{3,2,1,0:T(8,128)}, f32[2,3,32,1280]{3,2,1,0:T(8,128)}, f32[2,3,32,1280]{3,2,1,0:T(8,128)}, f32[2,16,1280]{2,1,0:T(8,128)}) custom-call(s32[4]{0:T(128)} %pad_add_fusion.refs_0_, f32[2,128,640]{2,1,0:T(8,128)} %get-tuple-element.59.refs_1_, f32[2,128,640]{2,1,0:T(8,128)} %copy-done.7, ...), custom_call_target="tpu_custom_call" | custom-call | flops 10066329600 | bytes 6553600 | tf_op jit(solution)/shard_map/window_tensor/pallas_call | solution.py:404
  75.0 2.6 %add.151.refs_0_ = f32[3,3,32,1280]{3,2,1,0:T(8,128)} add(f32[3,3,32,1280]{3,2,1,0:T(8,128)S(1)} %copy-done.1, f32[3,3,32,1280]{3,2,1,0:T(8,128)} %collective-permute-done.4) | non-fusion elementwise | flops 368640 | bytes 4423680 | tf_op jit(solution)/shard_map/add | solution.py:471
  78.2 0.8 copy-done.6
  79.0 1.8 collective-permute-start.6
  80.8 10.1 %window_tensor.9 = (f32[2,3,32,1280]{3,2,1,0:T(8,128)}, f32[2,3,32,1280]{3,2,1,0:T(8,128)}, f32[2,3,32,1280]{3,2,1,0:T(8,128)}, f32[2,3,32,1280]{3,2,1,0:T(8,128)}) custom-call(s32[4]{0:T(128)} %pad_add_fusion.refs_0_, f32[2,120,640]{2,1,0:T(8,128)} %get-tuple-element.58.refs_1_, ...), custom_call_target="tpu_custom_call", output_to_operand_aliasing={{0}: (5, {}), {1}: (6, {}), {2}: (7, {}), {3}: (8, {})} | custom-call | flops 9437184000 | bytes 6471680 | tf_op jit(solution)/shard_map/window_tensor/pallas_call | solution.py:404
  91.4 2.9 %collective-permute-done.17 = f32[2,3,32,1280]{3,2,1,0:T(8,128)S(1)} collective-permute-done((f32[2,3,32,1280]{3,2,1,0:T(8,128)}, f32[2,3,32,1280]{3,2,1,0:T(8,128)S(1)}, u32[]{:S(2)}, u32[]{:S(2)}) %collective-permute-start.17) | collective-permute-done | bytes 983072 | tf_op jit(solution)/shard_map/ppermute | solution.py:505
  94.3 2.2 %add.168 = f32[2,3,32,1280]{3,2,1,0:T(8,128)} add(f32[2,3,32,1280]{3,2,1,0:T(8,128)} %get-tuple-element.69, f32[2,3,32,1280]{3,2,1,0:T(8,128)S(1)} %collective-permute-done.17) | non-fusion elementwise | flops 245760 | bytes 2949120 | tf_op jit(solution)/shard_map/add | solution.py:471
  96.6 0.6 collective-permute-start.18
  97.1 1.6 collective-permute-done.6
  98.7 2.1 %dynamic-slice_add_fusion.1 = (f32[3,3,16,1280]{3,2,1,0:T(8,128)S(1)}, f32[3,3,16,1280]{3,2,1,0:T(8,128)S(1)}) fusion(f32[3,3,32,1280]{3,2,1,0:T(8,128)} %collective-permute-done.6, s32[]{:T(128)S(6)} %select_n.182, f32[3,3,32,1280]{3,2,1,0:T(8,128)S(1)} %collective-permute-done.3, f32[3,3,32,1280]{3,2,1,0:T(8,128)} %get-tuple-element.53, s32[]{:T(128)S(6)} %select_n.184), kind=kLoop, calls=%fused_computation.9 | loop fusion | flops 737280 | bytes 5898248 | tf_op jit(solution)/shard_map/add | solution.py:464
  100.8 1.9 %collective-permute-start.7 = (f32[3,3,16,1280]{3,2,1,0:T(8,128)S(1)}, f32[3,3,16,1280]{3,2,1,0:T(8,128)S(1)}, u32[]{:S(2)}, u32[]{:S(2)}) collective-permute-start(f32[3,3,16,1280]{3,2,1,0:T(8,128)S(1)} %get-tuple-element.72), channel_id=1, source_target_pairs={{0,8},{2,6},{4,12},{6,2},{8,0},{10,14},{12,4},{14,10},{16,24},{18,... | collective-permute-start | bytes 2211848 | tf_op jit(solution)/shard_map/ppermute | solution.py:467
  102.7 16.2 %collective-permute-done.18 = f32[2,3,32,1280]{3,2,1,0:T(8,128)} collective-permute-done((f32[2,3,32,1280]{3,2,1,0:T(8,128)}, f32[2,3,32,1280]{3,2,1,0:T(8,128)}, u32[]{:S(2)}, u32[]{:S(2)}) %collective-permute-start.18) | collective-permute-done | bytes 983072 | tf_op jit(solution)/shard_map/ppermute | solution.py:474
  118.9 2.4 %dynamic-slice_add_fusion.3 = (f32[2,3,16,1280]{3,2,1,0:T(8,128)S(1)}, f32[2,3,16,1280]{3,2,1,0:T(8,128)}) fusion(f32[2,3,32,1280]{3,2,1,0:T(8,128)} %collective-permute-done.18, s32[]{:T(128)S(6)} %select_n.182, f32[2,3,32,1280]{3,2,1,0:T(8,128)} %collective-permute-done.16, f32[2,3,32,1280]{3,2,1,0:T(8,128)S(1)} %copy-done.2, s32[]{:T(128)S(6)} %select_n.184), kind=kLoop, calls=%fused_computation.17 | loop fusion | flops 491520 | bytes 3932168 | tf_op jit(solution)/shard_map/add | solution.py:464
  121.3 1.6 collective-permute-start.19
  122.9 2.7 %collective-permute-start.8 = (f32[3,3,8,1280]{3,2,1,0:T(8,128)S(1)}, f32[3,3,8,1280]{3,2,1,0:T(8,128)S(1)}, u32[]{:S(2)}, u32[]{:S(2)}) collective-permute-start(f32[3,3,8,1280]{3,2,1,0:T(8,128)S(1)} %dynamic-slice_add_fusion.4), channel_id=1, source_target_pairs={{0,16},{2,18},{4,20},{6,22},{8,24},{10,26},{12,28},{14,30},{16,0},... | collective-permute-start | bytes 1105928 | tf_op jit(solution)/shard_map/ppermute | solution.py:467
  125.6 10.0 %collective-permute-done.19 = f32[2,3,16,1280]{3,2,1,0:T(8,128)S(1)} collective-permute-done((f32[2,3,16,1280]{3,2,1,0:T(8,128)}, f32[2,3,16,1280]{3,2,1,0:T(8,128)S(1)}, u32[]{:S(2)}, u32[]{:S(2)}) %collective-permute-start.19) | collective-permute-done | bytes 491552 | tf_op jit(solution)/shard_map/ppermute | solution.py:467
  135.7 1.8 collective-permute-start.20
  137.5 7.2 %collective-permute-done.8 = f32[3,3,8,1280]{3,2,1,0:T(8,128)S(1)} collective-permute-done((f32[3,3,8,1280]{3,2,1,0:T(8,128)S(1)}, f32[3,3,8,1280]{3,2,1,0:T(8,128)S(1)}, u32[]{:S(2)}, u32[]{:S(2)}) %collective-permute-start.8) | collective-permute-done | bytes 368672 | tf_op jit(solution)/shard_map/ppermute | solution.py:467
  144.9 1.6 collective-permute-start.9
  146.4 0.7 collective-permute-start.10
  147.1 2.3 %collective-permute-done.9 = f32[2,8,1280]{2,1,0:T(8,128)S(1)} collective-permute-done((f32[2,8,1280]{2,1,0:T(8,128)S(1)}, f32[2,8,1280]{2,1,0:T(8,128)S(1)}, u32[]{:S(2)}, u32[]{:S(2)}) %collective-permute-start.9) | collective-permute-done | bytes 81952 | tf_op jit(solution)/shard_map/ppermute | solution.py:515
  149.6 9.4 %collective-permute-done.11 = f32[3,8,1280]{2,1,0:T(8,128)S(1)} collective-permute-done((f32[3,8,1280]{2,1,0:T(8,128)S(1)}, f32[3,8,1280]{2,1,0:T(8,128)S(1)}, u32[]{:S(2)}, u32[]{:S(2)}) %collective-permute-start.11) | collective-permute-done | bytes 122912 | tf_op jit(solution)/shard_map/ppermute | solution.py:480
  159.6 7.4 %collective-permute-done.12 = f32[3,16,1280]{2,1,0:T(8,128)S(1)} collective-permute-done((f32[3,16,1280]{2,1,0:T(8,128)S(1)}, f32[3,16,1280]{2,1,0:T(8,128)S(1)}, u32[]{:S(2)}, u32[]{:S(2)}) %collective-permute-start.12) | collective-permute-done | bytes 245792 | tf_op jit(solution)/shard_map/ppermute | solution.py:480
  167.0 1.0 collective-permute-start.13
  168.1 6.1 %collective-permute-done.22 = f32[2,16,1280]{2,1,0:T(8,128)S(1)} collective-permute-done((f32[2,16,1280]{2,1,0:T(8,128)S(1)}, f32[2,16,1280]{2,1,0:T(8,128)S(1)}, u32[]{:S(2)}, u32[]{:S(2)}) %collective-permute-start.22) | collective-permute-done | bytes 163872 | tf_op jit(solution)/shard_map/ppermute | solution.py:480
  174.3 2.2 %collective-permute-start.23 = (f32[2,32,1280]{2,1,0:T(8,128)S(1)}, f32[2,32,1280]{2,1,0:T(8,128)S(1)}, u32[]{:S(2)}, u32[]{:S(2)}) collective-permute-start(f32[2,32,1280]{2,1,0:T(8,128)S(1)} %maximum_select_fusion.6), channel_id=1, source_target_pairs={{0,4},{2,10},{4,0},{6,14},{8,12},{10,2},{12,8},{14,6},{16,20},{18,... | collective-permute-start | bytes 983048 | tf_op jit(solution)/shard_map/ppermute | solution.py:480
  176.6 4.9 %collective-permute-done.23 = f32[2,32,1280]{2,1,0:T(8,128)S(1)} collective-permute-done((f32[2,32,1280]{2,1,0:T(8,128)S(1)}, f32[2,32,1280]{2,1,0:T(8,128)S(1)}, u32[]{:S(2)}, u32[]{:S(2)}) %collective-permute-start.23) | collective-permute-done | bytes 327712 | tf_op jit(solution)/shard_map/ppermute | solution.py:480
  181.6 2.1 %collective-permute-done.24 = f32[2,64,1280]{2,1,0:T(8,128)S(1)} collective-permute-done((f32[2,64,1280]{2,1,0:T(8,128)S(1)}, f32[2,64,1280]{2,1,0:T(8,128)S(1)}, u32[]{:S(2)}, u32[]{:S(2)}) %collective-permute-start.24) | collective-permute-done | bytes 655392 | tf_op jit(solution)/shard_map/ppermute | solution.py:480
  185.1 1.7 copy-done
  186.8 0.9 slice_dynamic-update-slice_fusion
  (59 shorter events, 4.2 us)
Async XLA Ops:
  2.6 19.7 %collective-permute-start = (f32[2,136,640]{2,1,0:T(8,128)}, f32[2,136,640]{2,1,0:T(8,128)S(1)}, u32[]{:S(2)}, u32[]{:S(2)}) collective-permute-start(f32[2,136,640]{2,1,0:T(8,128)} %pieces_of.5), channel_id=1, source_target_pairs={{0,1},{1,0},{2,3},{3,2},{4,5},{5,4},{6,7},{7,6},{8,9},{9,8},{10,11... | collective-permute-start | bytes 2088968 | tf_op jit(solution)/shard_map/ppermute | solution.py:451
  9.2 27.1 %collective-permute-start.2 = (f32[2,128,640]{2,1,0:T(8,128)}, f32[2,128,640]{2,1,0:T(8,128)S(1)}, u32[]{:S(2)}, u32[]{:S(2)}) collective-permute-start(f32[2,128,640]{2,1,0:T(8,128)} %get-tuple-element.41), channel_id=1, source_target_pairs={{0,1},{1,0},{2,3},{3,2},{4,5},{5,4},{6,7},{7,6},{8,9},{9,8},{10,11... | collective-permute-start | bytes 1966088 | tf_op jit(solution)/shard_map/ppermute | solution.py:453
  22.2 0.9 copy-start.3
  23.1 27.2 %collective-permute-start.1 = (f32[2,128,640]{2,1,0:T(8,128)}, f32[2,128,640]{2,1,0:T(8,128)S(1)}, u32[]{:S(2)}, u32[]{:S(2)}) collective-permute-start(f32[2,128,640]{2,1,0:T(8,128)} %gated.4), channel_id=1, source_target_pairs={{0,1},{1,0},{2,3},{3,2},{4,5},{5,4},{6,7},{7,6},{8,9},{9,8},{10,11... | collective-permute-start | bytes 1966088 | tf_op jit(solution)/shard_map/ppermute | solution.py:496
  36.3 0.9 copy-start.4
  37.2 26.5 %collective-permute-start.15 = (f32[2,128,640]{2,1,0:T(8,128)}, f32[2,128,640]{2,1,0:T(8,128)S(1)}, u32[]{:S(2)}, u32[]{:S(2)}) collective-permute-start(f32[2,128,640]{2,1,0:T(8,128)} %gated.7), channel_id=1, source_target_pairs={{0,1},{1,0},{2,3},{3,2},{4,5},{5,4},{6,7},{7,6},{8,9},{9,8},{10,11... | collective-permute-start | bytes 1966088 | tf_op jit(solution)/shard_map/ppermute | solution.py:496
  50.3 0.9 copy-start.5
  61.3 13.7 %collective-permute-start.4 = (f32[3,3,32,1280]{3,2,1,0:T(8,128)}, f32[3,3,32,1280]{3,2,1,0:T(8,128)}, u32[]{:S(2)}, u32[]{:S(2)}) collective-permute-start(f32[3,3,32,1280]{3,2,1,0:T(8,128)} %get-tuple-element.56), channel_id=1, source_target_pairs={{0,2},{2,0},{4,6},{6,4},{8,10},{10,8},{12,14},{14,12},{16,18},{18,... | collective-permute-start | bytes 4423688 | tf_op jit(solution)/shard_map/ppermute | solution.py:505
  61.4 16.8 %collective-permute-start.5 = (f32[2,120,640]{2,1,0:T(8,128)}, f32[2,120,640]{2,1,0:T(8,128)S(1)}, u32[]{:S(2)}, u32[]{:S(2)}) collective-permute-start(f32[2,120,640]{2,1,0:T(8,128)} %gated.5), channel_id=1, source_target_pairs={{0,1},{1,0},{2,3},{3,2},{4,5},{5,4},{6,7},{7,6},{8,9},{9,8},{10,11... | collective-permute-start | bytes 1843208 | tf_op jit(solution)/shard_map/ppermute | solution.py:496
  63.5 33.6 %collective-permute-start.3 = (f32[3,3,32,1280]{3,2,1,0:T(8,128)}, f32[3,3,32,1280]{3,2,1,0:T(8,128)S(1)}, u32[]{:S(2)}, u32[]{:S(2)}) collective-permute-start(f32[3,3,32,1280]{3,2,1,0:T(8,128)} %get-tuple-element.54), channel_id=1, source_target_pairs={{0,2},{2,0},{4,6},{6,4},{8,10},{10,8},{12,14},{14,12},{16,18},{18,... | collective-permute-start | bytes 4423688 | tf_op jit(solution)/shard_map/ppermute | solution.py:506
  63.7 0.8 copy-start.7
  64.5 10.5 %copy-start.1 = (f32[3,3,32,1280]{3,2,1,0:T(8,128)S(1)}, f32[3,3,32,1280]{3,2,1,0:T(8,128)}, u32[]{:S(2)}) copy-start(f32[3,3,32,1280]{3,2,1,0:T(8,128)} %get-tuple-element.55) | copy-start | bytes 4423684
  78.2 0.8 copy-start.6
  79.0 19.7 %collective-permute-start.6 = (f32[3,3,32,1280]{3,2,1,0:T(8,128)}, f32[3,3,32,1280]{3,2,1,0:T(8,128)}, u32[]{:S(2)}, u32[]{:S(2)}) collective-permute-start(f32[3,3,32,1280]{3,2,1,0:T(8,128)} %gated.6.refs_4_), channel_id=1, source_target_pairs={{0,4},{2,10},{4,0},{6,14},{8,12},{10,2},{12,8},{14,6},{16,20},{18,... | collective-permute-start | bytes 4423688 | tf_op jit(solution)/shard_map/ppermute | solution.py:474
  90.9 3.5 %collective-permute-start.17 = (f32[2,3,32,1280]{3,2,1,0:T(8,128)}, f32[2,3,32,1280]{3,2,1,0:T(8,128)S(1)}, u32[]{:S(2)}, u32[]{:S(2)}) collective-permute-start(f32[2,3,32,1280]{3,2,1,0:T(8,128)} %get-tuple-element.70), channel_id=1, source_target_pairs={{0,2},{2,0},{4,6},{6,4},{8,10},{10,8},{12,14},{14,12},{16,18},{18,... | collective-permute-start | bytes 2949128 | tf_op jit(solution)/shard_map/ppermute | solution.py:505
  90.9 11.8 %collective-permute-start.16 = (f32[2,3,32,1280]{3,2,1,0:T(8,128)}, f32[2,3,32,1280]{3,2,1,0:T(8,128)}, u32[]{:S(2)}, u32[]{:S(2)}) collective-permute-start(f32[2,3,32,1280]{3,2,1,0:T(8,128)} %get-tuple-element.68), channel_id=1, source_target_pairs={{0,2},{2,0},{4,6},{6,4},{8,10},{10,8},{12,14},{14,12},{16,18},{18,... | collective-permute-start | bytes 2949128 | tf_op jit(solution)/shard_map/ppermute | solution.py:506
  96.6 22.3 %collective-permute-start.18 = (f32[2,3,32,1280]{3,2,1,0:T(8,128)}, f32[2,3,32,1280]{3,2,1,0:T(8,128)}, u32[]{:S(2)}, u32[]{:S(2)}) collective-permute-start(f32[2,3,32,1280]{3,2,1,0:T(8,128)} %add.168), channel_id=1, source_target_pairs={{0,4},{2,10},{4,0},{6,14},{8,12},{10,2},{12,8},{14,6},{16,20},{18,... | collective-permute-start | bytes 2949128 | tf_op jit(solution)/shard_map/ppermute | solution.py:474
  98.7 20.2 %copy-start.2 = (f32[2,3,32,1280]{3,2,1,0:T(8,128)S(1)}, f32[2,3,32,1280]{3,2,1,0:T(8,128)}, u32[]{:S(2)}) copy-start(f32[2,3,32,1280]{3,2,1,0:T(8,128)} %get-tuple-element.67) | copy-start | bytes 2949124
  100.8 22.1 %collective-permute-start.7 = (f32[3,3,16,1280]{3,2,1,0:T(8,128)S(1)}, f32[3,3,16,1280]{3,2,1,0:T(8,128)S(1)}, u32[]{:S(2)}, u32[]{:S(2)}) collective-permute-start(f32[3,3,16,1280]{3,2,1,0:T(8,128)S(1)} %get-tuple-element.72), channel_id=1, source_target_pairs={{0,8},{2,6},{4,12},{6,2},{8,0},{10,14},{12,4},{14,10},{16,24},{18,... | collective-permute-start | bytes 2211848 | tf_op jit(solution)/shard_map/ppermute | solution.py:467
  121.3 14.3 %collective-permute-start.19 = (f32[2,3,16,1280]{3,2,1,0:T(8,128)}, f32[2,3,16,1280]{3,2,1,0:T(8,128)S(1)}, u32[]{:S(2)}, u32[]{:S(2)}) collective-permute-start(f32[2,3,16,1280]{3,2,1,0:T(8,128)} %get-tuple-element.74), channel_id=1, source_target_pairs={{0,8},{2,6},{4,12},{6,2},{8,0},{10,14},{12,4},{14,10},{16,24},{18,... | collective-permute-start | bytes 1474568 | tf_op jit(solution)/shard_map/ppermute | solution.py:467
  122.9 21.8 %collective-permute-start.8 = (f32[3,3,8,1280]{3,2,1,0:T(8,128)S(1)}, f32[3,3,8,1280]{3,2,1,0:T(8,128)S(1)}, u32[]{:S(2)}, u32[]{:S(2)}) collective-permute-start(f32[3,3,8,1280]{3,2,1,0:T(8,128)S(1)} %dynamic-slice_add_fusion.4), channel_id=1, source_target_pairs={{0,16},{2,18},{4,20},{6,22},{8,24},{10,26},{12,28},{14,30},{16,0},... | collective-permute-start | bytes 1105928 | tf_op jit(solution)/shard_map/ppermute | solution.py:467
  135.7 13.8 %collective-permute-start.20 = (f32[2,3,8,1280]{3,2,1,0:T(8,128)S(1)}, f32[2,3,8,1280]{3,2,1,0:T(8,128)S(1)}, u32[]{:S(2)}, u32[]{:S(2)}) collective-permute-start(f32[2,3,8,1280]{3,2,1,0:T(8,128)S(1)} %dynamic-slice_add_fusion.5), channel_id=1, source_target_pairs={{0,16},{2,18},{4,20},{6,22},{8,24},{10,26},{12,28},{14,30},{16,0},... | collective-permute-start | bytes 737288 | tf_op jit(solution)/shard_map/ppermute | solution.py:467
  144.9 4.5 %collective-permute-start.9 = (f32[2,8,1280]{2,1,0:T(8,128)S(1)}, f32[2,8,1280]{2,1,0:T(8,128)S(1)}, u32[]{:S(2)}, u32[]{:S(2)}) collective-permute-start(f32[2,8,1280]{2,1,0:T(8,128)S(1)} %slice_bitcast_fusion.4), channel_id=1, source_target_pairs={{0,1},{1,0},{2,3},{3,2},{4,5},{5,4},{6,7},{7,6},{8,9},{9,8},{10,11... | collective-permute-start | bytes 245768 | tf_op jit(solution)/shard_map/ppermute | solution.py:515
  146.4 2.9 %collective-permute-start.10 = (f32[1,8,1280]{2,1,0:T(8,128)S(1)}, f32[1,8,1280]{2,1,0:T(8,128)S(1)}, u32[]{:S(2)}, u32[]{:S(2)}) collective-permute-start(f32[1,8,1280]{2,1,0:T(8,128)S(1)} %slice_bitcast_fusion.5), channel_id=1, source_target_pairs={{0,0},{1,2},{2,1},{3,3},{4,4},{5,10},{6,9},{7,7},{8,8},{9,6},{10,5... | collective-permute-start | bytes 122888 | tf_op jit(solution)/shard_map/ppermute | solution.py:526
  149.4 9.5 %collective-permute-start.11 = (f32[3,8,1280]{2,1,0:T(8,128)S(1)}, f32[3,8,1280]{2,1,0:T(8,128)S(1)}, u32[]{:S(2)}, u32[]{:S(2)}) collective-permute-start(f32[3,8,1280]{2,1,0:T(8,128)S(1)} %constant_dynamic-update-slice_fusion), channel_id=1, source_target_pairs={{0,16},{2,18},{4,20},{6,22},{8,24},{10,26},{12,28},{14,30},{16,0},... | collective-permute-start | bytes 368648 | tf_op jit(solution)/shard_map/ppermute | solution.py:480
  159.0 8.0 %collective-permute-start.12 = (f32[3,16,1280]{2,1,0:T(8,128)S(1)}, f32[3,16,1280]{2,1,0:T(8,128)S(1)}, u32[]{:S(2)}, u32[]{:S(2)}) collective-permute-start(f32[3,16,1280]{2,1,0:T(8,128)S(1)} %maximum_select_fusion.7), channel_id=1, source_target_pairs={{0,8},{2,6},{4,12},{6,2},{8,0},{10,14},{12,4},{14,10},{16,24},{18,... | collective-permute-start | bytes 737288 | tf_op jit(solution)/shard_map/ppermute | solution.py:480
  159.1 8.9 %collective-permute-start.21 = (f32[2,8,1280]{2,1,0:T(8,128)S(1)}, f32[2,8,1280]{2,1,0:T(8,128)S(1)}, u32[]{:S(2)}, u32[]{:S(2)}) collective-permute-start(f32[2,8,1280]{2,1,0:T(8,128)S(1)} %fusion.12), channel_id=1, source_target_pairs={{0,16},{2,18},{4,20},{6,22},{8,24},{10,26},{12,28},{14,30},{16,0},... | collective-permute-start | bytes 245768 | tf_op jit(solution)/shard_map/ppermute | solution.py:480
  167.0 9.4 %collective-permute-start.13 = (f32[3,32,1280]{2,1,0:T(8,128)S(1)}, f32[3,32,1280]{2,1,0:T(8,128)S(1)}, u32[]{:S(2)}, u32[]{:S(2)}) collective-permute-start(f32[3,32,1280]{2,1,0:T(8,128)S(1)} %maximum_select_fusion.5), channel_id=1, source_target_pairs={{0,4},{2,10},{4,0},{6,14},{8,12},{10,2},{12,8},{14,6},{16,20},{18,... | collective-permute-start | bytes 1474568 | tf_op jit(solution)/shard_map/ppermute | solution.py:480
  168.0 6.2 %collective-permute-start.22 = (f32[2,16,1280]{2,1,0:T(8,128)S(1)}, f32[2,16,1280]{2,1,0:T(8,128)S(1)}, u32[]{:S(2)}, u32[]{:S(2)}) collective-permute-start(f32[2,16,1280]{2,1,0:T(8,128)S(1)} %maximum_select_fusion.8), channel_id=1, source_target_pairs={{0,8},{2,6},{4,12},{6,2},{8,0},{10,14},{12,4},{14,10},{16,24},{18,... | collective-permute-start | bytes 491528 | tf_op jit(solution)/shard_map/ppermute | solution.py:480
  174.3 7.2 %collective-permute-start.23 = (f32[2,32,1280]{2,1,0:T(8,128)S(1)}, f32[2,32,1280]{2,1,0:T(8,128)S(1)}, u32[]{:S(2)}, u32[]{:S(2)}) collective-permute-start(f32[2,32,1280]{2,1,0:T(8,128)S(1)} %maximum_select_fusion.6), channel_id=1, source_target_pairs={{0,4},{2,10},{4,0},{6,14},{8,12},{10,2},{12,8},{14,6},{16,20},{18,... | collective-permute-start | bytes 983048 | tf_op jit(solution)/shard_map/ppermute | solution.py:480
  176.5 7.3 %collective-permute-start.14 = (f32[3,64,1280]{2,1,0:T(8,128)S(1)}, f32[3,64,1280]{2,1,0:T(8,128)S(1)}, u32[]{:S(2)}, u32[]{:S(2)}) collective-permute-start(f32[3,64,1280]{2,1,0:T(8,128)S(1)} %maximum_select_fusion.3), channel_id=1, source_target_pairs={{0,2},{2,0},{4,6},{6,4},{8,10},{10,8},{12,14},{14,12},{16,18},{18,... | collective-permute-start | bytes 2949128 | tf_op jit(solution)/shard_map/ppermute | solution.py:480
  181.5 2.2 %collective-permute-start.24 = (f32[2,64,1280]{2,1,0:T(8,128)S(1)}, f32[2,64,1280]{2,1,0:T(8,128)S(1)}, u32[]{:S(2)}, u32[]{:S(2)}) collective-permute-start(f32[2,64,1280]{2,1,0:T(8,128)S(1)} %maximum_select_fusion.4), channel_id=1, source_target_pairs={{0,2},{2,0},{4,6},{6,4},{8,10},{10,8},{12,14},{14,12},{16,18},{18,... | collective-permute-start | bytes 1966088 | tf_op jit(solution)/shard_map/ppermute | solution.py:480
  185.1 1.7 copy-start

commit v20 on v18

--- a/solution.py
+++ b/solution.py
@@ -17,7 +17,7 @@
 VMEM_LIMIT = 60 * 1024 * 1024
 KERNEL_WORK = 8
 ORDER = ((2, 4, 8), (4, 2, 8))
-AHEAD = ((), (), (0,), (1, 0), (2, 1, 0))
+AHEAD = ((), (), (0,), (1, 0), (3, 2, 1))
 
 
 def padded(cells, sides, width):
@@ -451,7 +451,7 @@
     cores = [(m, m ^ 1) for m in range(members)]
     ways = [[(m, m ^ ORDER[m % 2][step]) for m in range(members)] for step in range(len(ORDER[0]))]
 
-    def halved(parts_of, step):
+    def halved(parts_of, step, waits=()):
         half = parts_of[0].shape[1] // 2
         mine = half_of[step]
 
@@ -459,6 +459,8 @@
             return sum(lax.dynamic_slice_in_dim(part, which * half, half, axis=1) for part in parts_of)
 
         leaves = total(1 - mine)
+        if waits:
+            leaves = gated(leaves, waits)
         return [total(mine), lax.ppermute(leaves, "mem", ways[step])], leaves
 
     def across(parts_of, step):
@@ -492,13 +494,20 @@
         second = lax.ppermute(quarters[2], "mem", cores)
         sums.append([quarters[0], quarters[1], second, first])
         done.append(0)
+    last = count - 1
+    sums[last], _ = across(sums[last], 0)
+    done[last] = 1
+    over = sums[last][2]
     pieces = {"own": [], "both": [], "other": []}
     for k, window in enumerate(windows):
         for step in range(done[k], len(ways)):
-            sums[k], _ = advanced(sums[k], step)
+            if window.side == "other":
+                sums[k], _ = halved(sums[k], step, [first])
+            else:
+                sums[k], _ = advanced(sums[k], step)
         pieces[window.side].append(exponent_of(sum(sums[k]), members))
 
-    other = lax.ppermute(jnp.stack(pieces["other"]), "band", swap)
+    other = lax.ppermute(gated(jnp.stack(pieces["other"]), [over]), "band", swap)
     place_of = {}
     for m in range(members):
         for b in range(2):
@@ -511,20 +520,22 @@
         trades.append((index, place_of[mate]))
     both = lax.ppermute(pieces["both"][0], ("mem", "band"), trades)
 
-    early = gathered(jnp.concatenate([other, both[None]]))
-    other, both = early[:-1], early[-1]
-    middle = both.shape[0] // 2
-    low, high = both[:middle], both[middle:]
-    rest = jnp.zeros((nlat // 2 - middle, NLON), jnp.float32)
-    down = jnp.stack([jnp.concatenate([rest, low]), jnp.concatenate([*other, high])])
-    up = jnp.stack([jnp.concatenate([low, *other[::-1]]), jnp.concatenate([high, rest])])
+    far = gathered(other)
+    near = gathered(jnp.concatenate([both[None], jnp.stack(pieces["own"])]))
+    middle = near.shape[1] // 2
+    rest = jnp.zeros((nlat // 2, NLON), jnp.float32)
+    down = jnp.stack([rest, jnp.concatenate([*far, rest[:middle]])])
+    up = jnp.stack([jnp.concatenate([rest[:middle], *far[::-1]]), rest])
     out = jnp.where(band == 0, down, up)
 
-    own = gathered(jnp.stack(pieces["own"]))
-    for k, block in enumerate(own):
-        width = block.shape[0]
-        row = choose(band, (nlat // 2 - middle - (k + 1) * width, middle + k * width))
-        out = lax.dynamic_update_slice(out, block[None], (band, row.astype(jnp.int32), jnp.int32(0)))
+    def put(block, level, pair):
+        return lax.dynamic_update_slice(out, block[None], (level, choose(band, pair).astype(jnp.int32), jnp.int32(0)))
+
+    edge = nlat // 2 - middle
+    out = put(near[0, :middle], 0, (edge, 0))
+    out = put(near[0, middle:], 1, (edge, 0))
+    for k, block in enumerate(near[1:]):
+        out = put(block, band, (edge - (k + 1) * LANE, middle + k * LANE))
     return out
 
 

time: 178 us -> 184 us (1.034)
  other arithmetic: 8.5 us -> 19.8 us
  waiting for transfers between devices: 66.2 us -> 59.1 us
  local copies, waits for them, and re-layouts: 4.56 us -> 6.55 us
    ppermute x10, waiting for transfers between devices: 35.6 us -> 22.4 us  [halved(): return ([total(mine), lax.ppermute(leaves, 'mem', ways[step])], leaves)]
    ppermute x8, starting transfers between devices: 7.82 us -> 2.52 us  [doubled(): beside = lax.ppermute(part, 'mem', cores if step < 0 else ways[step])]
    add x10, other arithmetic: 4.18 us -> 9.43 us  [total(): sum((lax.dynamic_slice_in_dim(part, which * half, half, axis=1) for part...]
    add x5, other arithmetic: 1.04 us -> 4.96 us  [across(): leaves = passed + passed_more]
    ppermute x1, starting transfers between devices: 0.82 us -> 3.4 us  [by_levels(): lax.ppermute(gated(jnp.stack(pieces['other']), [over]), 'band', swap)]
    ppermute x10, starting transfers between devices: 9.6 us -> 12.1 us  [halved(): return ([total(mine), lax.ppermute(leaves, 'mem', ways[step])], leaves)]
    ppermute x1, waiting for transfers between devices: 0.01 us -> 2.48 us  [by_levels(): lax.ppermute(gated(jnp.stack(pieces['other']), [over]), 'band', swap)]
    ppermute x8, waiting for transfers between devices: 22 us -> 24.4 us  [doubled(): beside = lax.ppermute(part, 'mem', cores if step < 0 else ways[step])]
  transfers between devices with their start and end apart: 40 -> 40, of which waited for: 13 -> 14; matrix products, arithmetic and copies ran while one was open for 4% -> 11% of each run, Pallas kernels for 33% -> 32%
where the time goes in v20:
time: 184 us; the launch traced here: 183 us
  Pallas kernels  61.5 us (33%)
  waiting for transfers between devices  59.1 us (32%)
  starting transfers between devices  35.2 us (19%)
  other arithmetic  19.8 us (11%)
  local copies, waits for them, and re-layouts  6.55 us (4%)
    pallas_call x5, Pallas kernels, window_tensor(): pl.pallas_call(functools.partial(window_kernel, window, depth, len(waits)...  51.4 us
    ppermute x8, waiting for transfers between devices, doubled(): beside = lax.ppermute(part, 'mem', cores if step < 0 else ways[step])  24.4 us
    ppermute x10, waiting for transfers between devices, halved(): return ([total(mine), lax.ppermute(leaves, 'mem', ways[step])], leaves)  22.4 us
    ppermute x10, starting transfers between devices, halved(): return ([total(mine), lax.ppermute(leaves, 'mem', ways[step])], leaves)  12.1 us
    pallas_call x3, Pallas kernels, pieces_of(): pl.pallas_call(functools.partial(pieces_kernel, windows, slots, count), i...  10.2 us
    add x10, other arithmetic, total(): sum((lax.dynamic_slice_in_dim(part, which * half, half, axis=1) for part...  9.43 us
    ppermute x1, waiting for transfers between devices, by_levels(): remotes = [lax.ppermute(piece, 'band', swap)]  8.25 us
    ppermute x4, starting transfers between devices, by_levels(): remotes.append(lax.ppermute(piece, 'band', swap))  5.74 us
  transfers between devices with their start and end apart: 40, of which 14 were waited for; matrix products, arithmetic and copies ran while one was open for 11% of the time, Pallas kernels for 32%

profile of v20, /device:TPU:0, one launch (start us, length us, event | category | flops | bytes accessed | tf_op | source)
XLA Modules:
  0.0 182.8 jit_solution(2840747740561624703)
XLA Ops:
  0.0 2.6 %pieces_of.4 = f32[2,136,640]{2,1,0:T(8,128)} custom-call(s32[1]{0:T(128)} %bitcast.5.level_ref, f32[2,2,640,640]{3,2,1,0:T(8,128)} %bitcast.17), custom_call_target="tpu_custom_call" | custom-call | bytes 5242880 | tf_op jit(solution)/shard_map/pieces_of/pallas_call | solution.py:209
  2.6 3.0 %collective-permute-start = (f32[2,136,640]{2,1,0:T(8,128)}, f32[2,136,640]{2,1,0:T(8,128)S(1)}, u32[]{:S(2)}, u32[]{:S(2)}) collective-permute-start(f32[2,136,640]{2,1,0:T(8,128)} %pieces_of.4), channel_id=1, source_target_pairs={{0,1},{1,0},{2,3},{3,2},{4,5},{5,4},{6,7},{7,6},{8,9},{9,8},{10,11... | collective-permute-start | bytes 2088968 | tf_op jit(solution)/shard_map/ppermute | solution.py:444
  5.6 3.6 %pieces_of.5 = (f32[2,128,640]{2,1,0:T(8,128)}, f32[2,128,640]{2,1,0:T(8,128)}, f32[2,128,640]{2,1,0:T(8,128)}, f32[2,120,640]{2,1,0:T(8,128)}) custom-call(s32[1]{0:T(128)} %bitcast.5.level_ref, f32[2,2,640,640]{3,2,1,0:T(8,128)} %bitcast.18), custom_call_target="tpu_custom_call" | custom-call | bytes 10485760 | tf_op jit(solution)/shard_map/pieces_of/pallas_call | solution.py:209
  9.4 4.0 %pieces_of.3 = (f32[2,136,640]{2,1,0:T(8,128)}, f32[2,128,640]{2,1,0:T(8,128)}, f32[2,128,640]{2,1,0:T(8,128)}, f32[2,128,640]{2,1,0:T(8,128)}, f32[2,120,640]{2,1,0:T(8,128)}) custom-call(s32[1]{0:T(128)} %bitcast.level_ref, f32[2,2,640,640]{3,2,1,0:T(8,128)} %bitcast.19), custom_call_target="tpu_custom_call" | custom-call | bytes 13107200 | tf_op jit(solution)/shard_map/pieces_of/pallas_call | solution.py:209
  14.0 8.3 %collective-permute-done.refs_2_.refs_1_ = f32[2,136,640]{2,1,0:T(8,128)S(1)} collective-permute-done((f32[2,136,640]{2,1,0:T(8,128)}, f32[2,136,640]{2,1,0:T(8,128)S(1)}, u32[]{:S(2)}, u32[]{:S(2)}) %collective-permute-start) | collective-permute-done | bytes 696352 | tf_op jit(solution)/shard_map/ppermute | solution.py:444
  22.3 0.9 copy-done.3
  23.2 2.1 %collective-permute-start.5 = (f32[2,128,640]{2,1,0:T(8,128)}, f32[2,128,640]{2,1,0:T(8,128)S(1)}, u32[]{:S(2)}, u32[]{:S(2)}) collective-permute-start(f32[2,128,640]{2,1,0:T(8,128)} %gated.6), channel_id=1, source_target_pairs={{0,1},{1,0},{2,3},{3,2},{4,5},{5,4},{6,7},{7,6},{8,9},{9,8},{10,11... | collective-permute-start | bytes 1966088 | tf_op jit(solution)/shard_map/ppermute | solution.py:448
  25.3 10.5 %window_tensor.5 = (f32[3,32,1280]{2,1,0:T(8,128)}, f32[3,32,1280]{2,1,0:T(8,128)}, f32[3,32,1280]{2,1,0:T(8,128)}, f32[3,32,1280]{2,1,0:T(8,128)}, f32[2,16,1280]{2,1,0:T(8,128)}) custom-call(s32[4]{0:T(128)} %pad_add_fusion.refs_0_, f32[2,136,640]{2,1,0:T(8,128)} %get-tuple-element.38.refs_1_, f32[2,136,640]{2,1,0:T(8,128)} %copy-done.3, ...), custom_call_target="tpu_custom_call" | custom-call | flops 10695475200 | bytes 6635520 | tf_op jit(solution)/shard_map/window_tensor/pallas_call | solution.py:398
  37.1 10.1 %window_tensor.6 = (f32[3,32,1280]{2,1,0:T(8,128)}, f32[3,32,1280]{2,1,0:T(8,128)}, f32[3,32,1280]{2,1,0:T(8,128)}, f32[3,32,1280]{2,1,0:T(8,128)}, f32[2,16,1280]{2,1,0:T(8,128)}) custom-call(s32[4]{0:T(128)} %pad_add_fusion.refs_0_, f32[2,128,640]{2,1,0:T(8,128)} %get-tuple-element.49.refs_1_, f32[2,128,640]{2,1,0:T(8,128)} %copy-done.5, ...), custom_call_target="tpu_custom_call" | custom-call | flops 10066329600 | bytes 6553600 | tf_op jit(solution)/shard_map/window_tensor/pallas_call | solution.py:398
  47.4 2.1 %collective-permute-start.8 = (f32[2,128,640]{2,1,0:T(8,128)}, f32[2,128,640]{2,1,0:T(8,128)}, u32[]{:S(2)}, u32[]{:S(2)}) collective-permute-start(f32[2,128,640]{2,1,0:T(8,128)} %gated.8), channel_id=1, source_target_pairs={{0,1},{1,0},{2,3},{3,2},{4,5},{5,4},{6,7},{7,6},{8,9},{9,8},{10,11... | collective-permute-start | bytes 1966088 | tf_op jit(solution)/shard_map/ppermute | solution.py:448
  50.9 1.5 collective-permute-start.3
  53.4 10.4 %window_tensor.7 = (f32[3,32,1280]{2,1,0:T(8,128)}, f32[3,32,1280]{2,1,0:T(8,128)}, f32[3,32,1280]{2,1,0:T(8,128)}, f32[3,32,1280]{2,1,0:T(8,128)}, f32[2,16,1280]{2,1,0:T(8,128)}) custom-call(s32[4]{0:T(128)} %pad_add_fusion.refs_0_, f32[2,128,640]{2,1,0:T(8,128)} %get-tuple-element.53.refs_1_, f32[2,128,640]{2,1,0:T(8,128)} %copy-done.4, ...), custom_call_target="tpu_custom_call" | custom-call | flops 10066329600 | bytes 6553600 | tf_op jit(solution)/shard_map/window_tensor/pallas_call | solution.py:398
  63.9 1.9 %dynamic-slice_add_fusion.9 = (f32[3,16,1280]{2,1,0:T(8,128)S(1)}, f32[3,16,1280]{2,1,0:T(8,128)}) fusion(f32[3,32,1280]{2,1,0:T(8,128)} %collective-permute-done.3, s32[]{:T(128)S(6)} %select_n.218, f32[3,32,1280]{2,1,0:T(8,128)S(1)} %collective-permute-done.1, f32[3,32,1280]{2,1,0:T(8,128)S(1)} %copy-done.13, s32[]{:T(128)S(6)} %select_n.220), kind=kLoop, calls=%fused_computation.25 | loop fusion | flops 245760 | bytes 1966088 | tf_op jit(solution)/shard_map/add | solution.py:459
  65.8 10.2 %window_tensor.8 = (f32[3,32,1280]{2,1,0:T(8,128)}, f32[3,32,1280]{2,1,0:T(8,128)}, f32[3,32,1280]{2,1,0:T(8,128)}, f32[3,32,1280]{2,1,0:T(8,128)}, f32[2,16,1280]{2,1,0:T(8,128)}) custom-call(s32[4]{0:T(128)} %pad_add_fusion.refs_0_, f32[2,128,640]{2,1,0:T(8,128)} %get-tuple-element.46.refs_1_, f32[2,128,640]{2,1,0:T(8,128)} %collective-permute-done.8.refs_2_, ...), custom_call_target="tpu_custom_call" | custom-call | flops 10066329600 | bytes 6553600 | tf_op jit(solution)/shard_map/window_tensor/pallas_call | solution.py:398
  76.6 1.1 add.308.refs_5_
  77.7 1.4 collective-permute-start.25
  79.2 1.4 collective-permute-start.4
  80.6 1.5 collective-permute-start.6
  82.8 5.4 %collective-permute-done.4 = f32[3,16,1280]{2,1,0:T(8,128)S(1)} collective-permute-done((f32[3,16,1280]{2,1,0:T(8,128)}, f32[3,16,1280]{2,1,0:T(8,128)S(1)}, u32[]{:S(2)}, u32[]{:S(2)}) %collective-permute-start.4) | collective-permute-done | bytes 245792 | tf_op jit(solution)/shard_map/ppermute | solution.py:464
  88.9 1.4 collective-permute-start.16
  90.4 1.9 %add.307.refs_4_ = f32[3,32,1280]{2,1,0:T(8,128)} add(f32[3,32,1280]{2,1,0:T(8,128)S(1)} %copy-done.11, f32[3,32,1280]{2,1,0:T(8,128)} %collective-permute-done.10) | non-fusion elementwise | flops 122880 | bytes 1474560 | tf_op jit(solution)/shard_map/add | solution.py:468
  93.0 1.9 %dynamic-slice_add_fusion.5 = (f32[3,16,1280]{2,1,0:T(8,128)S(1)}, f32[3,16,1280]{2,1,0:T(8,128)}) fusion(f32[3,32,1280]{2,1,0:T(8,128)} %collective-permute-done.25, s32[]{:T(128)S(6)} %select_n.218, f32[3,32,1280]{2,1,0:T(8,128)S(1)} %collective-permute-done.24, f32[3,32,1280]{2,1,0:T(8,128)S(1)} %copy-done.8, s32[]{:T(128)S(6)} %select_n.220), kind=kLoop, calls=%fused_computation.21 | loop fusion | flops 245760 | bytes 1966088 | tf_op jit(solution)/shard_map/add | solution.py:459
  95.4 1.1 collective-permute-done.6.refs_2_
  97.3 10.1 %window_tensor.9 = (f32[3,32,1280]{2,1,0:T(8,128)}, f32[3,32,1280]{2,1,0:T(8,128)}, f32[3,32,1280]{2,1,0:T(8,128)}, f32[3,32,1280]{2,1,0:T(8,128)}) custom-call(s32[4]{0:T(128)} %pad_add_fusion.refs_0_, f32[2,120,640]{2,1,0:T(8,128)} %get-tuple-element.43.refs_1_, f32[2,120,640]{2,1,0:T(8,128)} %copy-done.19, bf16[4,640,640]{2,1,0:T(8,128)(2,1)} %constant.125.clone.refs_3_, ...), custom_call_target="tpu_custom_call" | custom-call | flops 9437184000 | bytes 6471680 | tf_op jit(solution)/shard_map/window_tensor/pallas_call | solution.py:398
  109.4 2.6 %collective-permute-start.27 = (f32[3,8,1280]{2,1,0:T(8,128)}, f32[3,8,1280]{2,1,0:T(8,128)}, u32[]{:S(2)}, u32[]{:S(2)}) collective-permute-start(f32[3,8,1280]{2,1,0:T(8,128)} %dynamic-slice_add_fusion.12), channel_id=1, source_target_pairs={{0,16},{2,18},{4,20},{6,22},{8,24},{10,26},{12,28},{14,30},{16,0},... | collective-permute-start | bytes 368648 | tf_op jit(solution)/shard_map/ppermute | solution.py:464
  112.0 1.8 %dynamic-slice_add_fusion.3 = (f32[3,16,1280]{2,1,0:T(8,128)S(1)}, f32[3,16,1280]{2,1,0:T(8,128)}) fusion(f32[3,32,1280]{2,1,0:T(8,128)} %collective-permute-done.30, s32[]{:T(128)S(6)} %select_n.218, f32[3,32,1280]{2,1,0:T(8,128)S(1)} %collective-permute-done.29, f32[3,32,1280]{2,1,0:T(8,128)S(1)} %copy-done.7, s32[]{:T(128)S(6)} %select_n.220), kind=kLoop, calls=%fused_computation.19 | loop fusion | flops 245760 | bytes 1966088 | tf_op jit(solution)/shard_map/add | solution.py:459
  115.5 2.6 %collective-permute-start.17 = (f32[3,8,1280]{2,1,0:T(8,128)}, f32[3,8,1280]{2,1,0:T(8,128)S(1)}, u32[]{:S(2)}, u32[]{:S(2)}) collective-permute-start(f32[3,8,1280]{2,1,0:T(8,128)} %gated.10), channel_id=1, source_target_pairs={{0,16},{2,18},{4,20},{6,22},{8,24},{10,26},{12,28},{14,30},{16,0},... | collective-permute-start | bytes 368648 | tf_op jit(solution)/shard_map/ppermute | solution.py:464
  118.1 1.1 add.325
  119.2 1.3 collective-permute-start.18
  120.5 1.0 add_multiply_fusion.2
  121.5 6.0 %collective-permute-done.15 = f32[3,8,1280]{2,1,0:T(8,128)} collective-permute-done((f32[3,8,1280]{2,1,0:T(8,128)}, f32[3,8,1280]{2,1,0:T(8,128)}, u32[]{:S(2)}, u32[]{:S(2)}) %collective-permute-start.15) | collective-permute-done | bytes 122912 | tf_op jit(solution)/shard_map/ppermute | solution.py:464
  127.5 0.9 collective-permute-start.28
  128.4 0.9 add_multiply_fusion.4
  130.1 0.9 dynamic-slice_add_fusion.11
  131.3 2.5 %collective-permute-start.34 = (f32[3,16,1280]{2,1,0:T(8,128)S(1)}, f32[3,16,1280]{2,1,0:T(8,128)S(1)}, u32[]{:S(2)}, u32[]{:S(2)}) collective-permute-start(f32[3,16,1280]{2,1,0:T(8,128)S(1)} %get-tuple-element.78), channel_id=1, source_target_pairs={{0,8},{2,6},{4,12},{6,2},{8,0},{10,14},{12,4},{14,10},{16,24},{18,... | collective-permute-start | bytes 737288 | tf_op jit(solution)/shard_map/ppermute | solution.py:464
  133.9 3.6 %collective-permute-done.32 = f32[3,8,1280]{2,1,0:T(8,128)S(1)} collective-permute-done((f32[3,8,1280]{2,1,0:T(8,128)S(1)}, f32[3,8,1280]{2,1,0:T(8,128)S(1)}, u32[]{:S(2)}, u32[]{:S(2)}) %collective-permute-start.32) | collective-permute-done | bytes 122912 | tf_op jit(solution)/shard_map/ppermute | solution.py:464
  137.5 0.9 add_multiply_fusion.1
  138.5 3.4 %collective-permute-start.19 = (f32[2,8,1280]{2,1,0:T(8,128)}, f32[2,8,1280]{2,1,0:T(8,128)S(1)}, u32[]{:S(2)}, u32[]{:S(2)}) collective-permute-start(f32[2,8,1280]{2,1,0:T(8,128)} %gated.11), channel_id=1, source_target_pairs={{0,1},{1,0},{2,3},{3,2},{4,5},{5,4},{6,7},{7,6},{8,9},{9,8},{10,11... | collective-permute-start | bytes 245768 | tf_op jit(solution)/shard_map/ppermute | solution.py:510
  142.0 2.5 %collective-permute-done.19 = f32[2,8,1280]{2,1,0:T(8,128)S(1)} collective-permute-done((f32[2,8,1280]{2,1,0:T(8,128)}, f32[2,8,1280]{2,1,0:T(8,128)S(1)}, u32[]{:S(2)}, u32[]{:S(2)}) %collective-permute-start.19) | collective-permute-done | bytes 81952 | tf_op jit(solution)/shard_map/ppermute | solution.py:510
  145.0 7.4 %collective-permute-done.35 = f32[3,8,1280]{2,1,0:T(8,128)S(1)} collective-permute-done((f32[3,8,1280]{2,1,0:T(8,128)S(1)}, f32[3,8,1280]{2,1,0:T(8,128)S(1)}, u32[]{:S(2)}, u32[]{:S(2)}) %collective-permute-start.35) | collective-permute-done | bytes 122912 | tf_op jit(solution)/shard_map/ppermute | solution.py:464
  152.5 1.6 collective-permute-done.20
  154.1 1.3 collective-permute-start.21
  155.4 4.2 %collective-permute-done.36 = f32[3,8,1280]{2,1,0:T(8,128)S(1)} collective-permute-done((f32[3,8,1280]{2,1,0:T(8,128)S(1)}, f32[3,8,1280]{2,1,0:T(8,128)S(1)}, u32[]{:S(2)}, u32[]{:S(2)}) %collective-permute-start.36) | collective-permute-done | bytes 122912 | tf_op jit(solution)/shard_map/ppermute | solution.py:475
  159.8 1.1 collective-permute-done.21
  161.2 7.1 %collective-permute-done.37 = f32[3,16,1280]{2,1,0:T(8,128)S(1)} collective-permute-done((f32[3,16,1280]{2,1,0:T(8,128)S(1)}, f32[3,16,1280]{2,1,0:T(8,128)S(1)}, u32[]{:S(2)}, u32[]{:S(2)}) %collective-permute-start.37) | collective-permute-done | bytes 245792 | tf_op jit(solution)/shard_map/ppermute | solution.py:475
  168.6 8.6 %collective-permute-done.38 = f32[3,32,1280]{2,1,0:T(8,128)S(1)} collective-permute-done((f32[3,32,1280]{2,1,0:T(8,128)S(1)}, f32[3,32,1280]{2,1,0:T(8,128)S(1)}, u32[]{:S(2)}, u32[]{:S(2)}) %collective-permute-start.38) | collective-permute-done | bytes 491552 | tf_op jit(solution)/shard_map/ppermute | solution.py:475
  178.1 1.8 collective-permute-done.39
  180.3 1.7 copy-done.1
  (130 shorter events, 17.0 us)
Async XLA Ops:
  2.6 19.7 %collective-permute-start = (f32[2,136,640]{2,1,0:T(8,128)}, f32[2,136,640]{2,1,0:T(8,128)S(1)}, u32[]{:S(2)}, u32[]{:S(2)}) collective-permute-start(f32[2,136,640]{2,1,0:T(8,128)} %pieces_of.4), channel_id=1, source_target_pairs={{0,1},{1,0},{2,3},{3,2},{4,5},{5,4},{6,7},{7,6},{8,9},{9,8},{10,11... | collective-permute-start | bytes 2088968 | tf_op jit(solution)/shard_map/ppermute | solution.py:444
  9.2 27.1 %collective-permute-start.7 = (f32[2,128,640]{2,1,0:T(8,128)}, f32[2,128,640]{2,1,0:T(8,128)S(1)}, u32[]{:S(2)}, u32[]{:S(2)}) collective-permute-start(f32[2,128,640]{2,1,0:T(8,128)} %get-tuple-element.48), channel_id=1, source_target_pairs={{0,1},{1,0},{2,3},{3,2},{4,5},{5,4},{6,7},{7,6},{8,9},{9,8},{10,11... | collective-permute-start | bytes 1966088 | tf_op jit(solution)/shard_map/ppermute | solution.py:448
  23.2 29.3 %collective-permute-start.5 = (f32[2,128,640]{2,1,0:T(8,128)}, f32[2,128,640]{2,1,0:T(8,128)S(1)}, u32[]{:S(2)}, u32[]{:S(2)}) collective-permute-start(f32[2,128,640]{2,1,0:T(8,128)} %gated.6), channel_id=1, source_target_pairs={{0,1},{1,0},{2,3},{3,2},{4,5},{5,4},{6,7},{7,6},{8,9},{9,8},{10,11... | collective-permute-start | bytes 1966088 | tf_op jit(solution)/shard_map/ppermute | solution.py:448
  35.8 13.9 %collective-permute-start.2 = (f32[3,32,1280]{2,1,0:T(8,128)}, f32[3,32,1280]{2,1,0:T(8,128)S(1)}, u32[]{:S(2)}, u32[]{:S(2)}) collective-permute-start(f32[3,32,1280]{2,1,0:T(8,128)} %get-tuple-element.42), channel_id=1, source_target_pairs={{0,2},{2,0},{4,6},{6,4},{8,10},{10,8},{12,14},{14,12},{16,18},{18,... | collective-permute-start | bytes 1474568 | tf_op jit(solution)/shard_map/ppermute | solution.py:493
  47.3 3.6 %collective-permute-start.9 = (f32[3,32,1280]{2,1,0:T(8,128)}, f32[3,32,1280]{2,1,0:T(8,128)S(1)}, u32[]{:S(2)}, u32[]{:S(2)}) collective-permute-start(f32[3,32,1280]{2,1,0:T(8,128)} %get-tuple-element.52), channel_id=1, source_target_pairs={{0,2},{2,0},{4,6},{6,4},{8,10},{10,8},{12,14},{14,12},{16,18},{18,... | collective-permute-start | bytes 1474568 | tf_op jit(solution)/shard_map/ppermute | solution.py:493
  47.4 18.4 %collective-permute-start.8 = (f32[2,128,640]{2,1,0:T(8,128)}, f32[2,128,640]{2,1,0:T(8,128)}, u32[]{:S(2)}, u32[]{:S(2)}) collective-permute-start(f32[2,128,640]{2,1,0:T(8,128)} %gated.8), channel_id=1, source_target_pairs={{0,1},{1,0},{2,3},{3,2},{4,5},{5,4},{6,7},{7,6},{8,9},{9,8},{10,11... | collective-permute-start | bytes 1966088 | tf_op jit(solution)/shard_map/ppermute | solution.py:448
  49.5 14.3 %collective-permute-start.1 = (f32[3,32,1280]{2,1,0:T(8,128)}, f32[3,32,1280]{2,1,0:T(8,128)S(1)}, u32[]{:S(2)}, u32[]{:S(2)}) collective-permute-start(f32[3,32,1280]{2,1,0:T(8,128)} %get-tuple-element.40), channel_id=1, source_target_pairs={{0,2},{2,0},{4,6},{6,4},{8,10},{10,8},{12,14},{14,12},{16,18},{18,... | collective-permute-start | bytes 1474568 | tf_op jit(solution)/shard_map/ppermute | solution.py:494
  49.7 29.5 %collective-permute-start.12 = (f32[3,32,1280]{2,1,0:T(8,128)}, f32[3,32,1280]{2,1,0:T(8,128)S(1)}, u32[]{:S(2)}, u32[]{:S(2)}) collective-permute-start(f32[3,32,1280]{2,1,0:T(8,128)} %get-tuple-element.61), channel_id=1, source_target_pairs={{0,2},{2,0},{4,6},{6,4},{8,10},{10,8},{12,14},{14,12},{16,18},{18,... | collective-permute-start | bytes 1474568 | tf_op jit(solution)/shard_map/ppermute | solution.py:494
  50.9 13.0 %collective-permute-start.3 = (f32[3,32,1280]{2,1,0:T(8,128)}, f32[3,32,1280]{2,1,0:T(8,128)}, u32[]{:S(2)}, u32[]{:S(2)}) collective-permute-start(f32[3,32,1280]{2,1,0:T(8,128)} %add.297.refs_4_), channel_id=1, source_target_pairs={{0,4},{2,10},{4,0},{6,14},{8,12},{10,2},{12,8},{14,6},{16,20},{18,... | collective-permute-start | bytes 1474568 | tf_op jit(solution)/shard_map/ppermute | solution.py:469
  52.4 11.3 %copy-start.10 = (f32[3,32,1280]{2,1,0:T(8,128)}, f32[3,32,1280]{2,1,0:T(8,128)S(1)}, u32[]{:S(2)}) copy-start(f32[3,32,1280]{2,1,0:T(8,128)S(1)} %add.306.refs_4_) | copy-start | bytes 1474564
  52.5 28.1 %collective-permute-start.13 = (f32[3,32,1280]{2,1,0:T(8,128)S(1)}, f32[3,32,1280]{2,1,0:T(8,128)S(1)}, u32[]{:S(2)}, u32[]{:S(2)}) collective-permute-start(f32[3,32,1280]{2,1,0:T(8,128)S(1)} %add.306.refs_4_), channel_id=1, source_target_pairs={{0,4},{2,10},{4,0},{6,14},{8,12},{10,2},{12,8},{14,6},{16,20},{18,... | collective-permute-start | bytes 1474568 | tf_op jit(solution)/shard_map/ppermute | solution.py:469
  53.4 10.5 %copy-start.13 = (f32[3,32,1280]{2,1,0:T(8,128)S(1)}, f32[3,32,1280]{2,1,0:T(8,128)}, u32[]{:S(2)}) copy-start(f32[3,32,1280]{2,1,0:T(8,128)} %get-tuple-element.39) | copy-start | bytes 1474564
  63.8 12.8 %collective-permute-start.11 = (f32[3,32,1280]{2,1,0:T(8,128)}, f32[3,32,1280]{2,1,0:T(8,128)}, u32[]{:S(2)}, u32[]{:S(2)}) collective-permute-start(f32[3,32,1280]{2,1,0:T(8,128)} %get-tuple-element.59), channel_id=1, source_target_pairs={{0,2},{2,0},{4,6},{6,4},{8,10},{10,8},{12,14},{14,12},{16,18},{18,... | collective-permute-start | bytes 1474568 | tf_op jit(solution)/shard_map/ppermute | solution.py:493
  65.8 10.9 %copy-start.17 = (f32[3,32,1280]{2,1,0:T(8,128)S(1)}, f32[3,32,1280]{2,1,0:T(8,128)}, u32[]{:S(2)}) copy-start(f32[3,32,1280]{2,1,0:T(8,128)} %get-tuple-element.58) | copy-start | bytes 1474564
  76.0 12.9 %collective-permute-start.10 = (f32[3,32,1280]{2,1,0:T(8,128)}, f32[3,32,1280]{2,1,0:T(8,128)}, u32[]{:S(2)}, u32[]{:S(2)}) collective-permute-start(f32[3,32,1280]{2,1,0:T(8,128)} %get-tuple-element.57), channel_id=1, source_target_pairs={{0,2},{2,0},{4,6},{6,4},{8,10},{10,8},{12,14},{14,12},{16,18},{18,... | collective-permute-start | bytes 1474568 | tf_op jit(solution)/shard_map/ppermute | solution.py:493
  76.5 15.7 %collective-permute-start.24 = (f32[3,32,1280]{2,1,0:T(8,128)}, f32[3,32,1280]{2,1,0:T(8,128)S(1)}, u32[]{:S(2)}, u32[]{:S(2)}) collective-permute-start(f32[3,32,1280]{2,1,0:T(8,128)} %get-tuple-element.66), channel_id=1, source_target_pairs={{0,2},{2,0},{4,6},{6,4},{8,10},{10,8},{12,14},{14,12},{16,18},{18,... | collective-permute-start | bytes 1474568 | tf_op jit(solution)/shard_map/ppermute | solution.py:494
  77.7 11.2 %copy-start.9 = (f32[3,32,1280]{2,1,0:T(8,128)}, f32[3,32,1280]{2,1,0:T(8,128)S(1)}, u32[]{:S(2)}) copy-start(f32[3,32,1280]{2,1,0:T(8,128)S(1)} %add.308.refs_5_) | copy-start | bytes 1474564
  77.7 15.3 %collective-permute-start.25 = (f32[3,32,1280]{2,1,0:T(8,128)S(1)}, f32[3,32,1280]{2,1,0:T(8,128)}, u32[]{:S(2)}, u32[]{:S(2)}) collective-permute-start(f32[3,32,1280]{2,1,0:T(8,128)S(1)} %add.308.refs_5_), channel_id=1, source_target_pairs={{0,4},{2,10},{4,0},{6,14},{8,12},{10,2},{12,8},{14,6},{16,20},{18,... | collective-permute-start | bytes 1474568 | tf_op jit(solution)/shard_map/ppermute | solution.py:469
  79.2 9.1 %collective-permute-start.4 = (f32[3,16,1280]{2,1,0:T(8,128)}, f32[3,16,1280]{2,1,0:T(8,128)S(1)}, u32[]{:S(2)}, u32[]{:S(2)}) collective-permute-start(f32[3,16,1280]{2,1,0:T(8,128)} %get-tuple-element.80.refs_5_), channel_id=1, source_target_pairs={{0,8},{2,6},{4,12},{6,2},{8,0},{10,14},{12,4},{14,10},{16,24},{18,... | collective-permute-start | bytes 737288 | tf_op jit(solution)/shard_map/ppermute | solution.py:464
  80.6 12.5 %copy-start.8 = (f32[3,32,1280]{2,1,0:T(8,128)S(1)}, f32[3,32,1280]{2,1,0:T(8,128)}, u32[]{:S(2)}) copy-start(f32[3,32,1280]{2,1,0:T(8,128)} %get-tuple-element.65) | copy-start | bytes 1474564
  80.6 15.9 %collective-permute-start.6 = (f32[2,120,640]{2,1,0:T(8,128)}, f32[2,120,640]{2,1,0:T(8,128)S(1)}, u32[]{:S(2)}, u32[]{:S(2)}) collective-permute-start(f32[2,120,640]{2,1,0:T(8,128)} %gated.7), channel_id=1, source_target_pairs={{0,1},{1,0},{2,3},{3,2},{4,5},{5,4},{6,7},{7,6},{8,9},{9,8},{10,11... | collective-permute-start | bytes 1843208 | tf_op jit(solution)/shard_map/ppermute | solution.py:448
  88.3 23.8 %collective-permute-start.29 = (f32[3,32,1280]{2,1,0:T(8,128)}, f32[3,32,1280]{2,1,0:T(8,128)S(1)}, u32[]{:S(2)}, u32[]{:S(2)}) collective-permute-start(f32[3,32,1280]{2,1,0:T(8,128)} %get-tuple-element.68), channel_id=1, source_target_pairs={{0,2},{2,0},{4,6},{6,4},{8,10},{10,8},{12,14},{14,12},{16,18},{18,... | collective-permute-start | bytes 1474568 | tf_op jit(solution)/shard_map/ppermute | solution.py:494
  88.9 18.6 %collective-permute-start.16 = (f32[3,16,1280]{2,1,0:T(8,128)}, f32[3,16,1280]{2,1,0:T(8,128)S(1)}, u32[]{:S(2)}, u32[]{:S(2)}) collective-permute-start(f32[3,16,1280]{2,1,0:T(8,128)} %get-tuple-element.82.refs_6_), channel_id=1, source_target_pairs={{0,8},{2,6},{4,12},{6,2},{8,0},{10,14},{12,4},{14,10},{16,24},{18,... | collective-permute-start | bytes 737288 | tf_op jit(solution)/shard_map/ppermute | solution.py:464
  92.2 19.8 %collective-permute-start.30 = (f32[3,32,1280]{2,1,0:T(8,128)}, f32[3,32,1280]{2,1,0:T(8,128)}, u32[]{:S(2)}, u32[]{:S(2)}) collective-permute-start(f32[3,32,1280]{2,1,0:T(8,128)} %add.307.refs_4_), channel_id=1, source_target_pairs={{0,4},{2,10},{4,0},{6,14},{8,12},{10,2},{12,8},{14,6},{16,20},{18,... | collective-permute-start | bytes 1474568 | tf_op jit(solution)/shard_map/ppermute | solution.py:469
  94.9 13.8 %collective-permute-start.26 = (f32[3,16,1280]{2,1,0:T(8,128)}, f32[3,16,1280]{2,1,0:T(8,128)S(1)}, u32[]{:S(2)}, u32[]{:S(2)}) collective-permute-start(f32[3,16,1280]{2,1,0:T(8,128)} %get-tuple-element.74), channel_id=1, source_target_pairs={{0,8},{2,6},{4,12},{6,2},{8,0},{10,14},{12,4},{14,10},{16,24},{18,... | collective-permute-start | bytes 737288 | tf_op jit(solution)/shard_map/ppermute | solution.py:464
  97.3 14.7 %copy-start.7 = (f32[3,32,1280]{2,1,0:T(8,128)S(1)}, f32[3,32,1280]{2,1,0:T(8,128)}, u32[]{:S(2)}) copy-start(f32[3,32,1280]{2,1,0:T(8,128)} %get-tuple-element.67) | copy-start | bytes 1474564
  107.4 6.9 %collective-permute-start.14 = (f32[3,32,1280]{2,1,0:T(8,128)}, f32[3,32,1280]{2,1,0:T(8,128)S(1)}, u32[]{:S(2)}, u32[]{:S(2)}) collective-permute-start(f32[3,32,1280]{2,1,0:T(8,128)} %get-tuple-element.63), channel_id=1, source_target_pairs={{0,2},{2,0},{4,6},{6,4},{8,10},{10,8},{12,14},{14,12},{16,18},{18,... | collective-permute-start | bytes 1474568 | tf_op jit(solution)/shard_map/ppermute | solution.py:493
  108.2 9.8 %copy-start.14 = (f32[3,32,1280]{2,1,0:T(8,128)S(1)}, f32[3,32,1280]{2,1,0:T(8,128)}, u32[]{:S(2)}) copy-start(f32[3,32,1280]{2,1,0:T(8,128)} %get-tuple-element.64) | copy-start | bytes 1474564
  108.2 23.0 %collective-permute-start.33 = (f32[3,32,1280]{2,1,0:T(8,128)}, f32[3,32,1280]{2,1,0:T(8,128)S(1)}, u32[]{:S(2)}, u32[]{:S(2)}) collective-permute-start(f32[3,32,1280]{2,1,0:T(8,128)} %get-tuple-element.70), channel_id=1, source_target_pairs={{0,2},{2,0},{4,6},{6,4},{8,10},{10,8},{12,14},{14,12},{16,18},{18,... | collective-permute-start | bytes 1474568 | tf_op jit(solution)/shard_map/ppermute | solution.py:494
  109.4 9.8 %collective-permute-start.27 = (f32[3,8,1280]{2,1,0:T(8,128)}, f32[3,8,1280]{2,1,0:T(8,128)}, u32[]{:S(2)}, u32[]{:S(2)}) collective-permute-start(f32[3,8,1280]{2,1,0:T(8,128)} %dynamic-slice_add_fusion.12), channel_id=1, source_target_pairs={{0,16},{2,18},{4,20},{6,22},{8,24},{10,26},{12,28},{14,30},{16,0},... | collective-permute-start | bytes 368648 | tf_op jit(solution)/shard_map/ppermute | solution.py:464
  113.9 16.2 %collective-permute-start.31 = (f32[3,16,1280]{2,1,0:T(8,128)}, f32[3,16,1280]{2,1,0:T(8,128)}, u32[]{:S(2)}, u32[]{:S(2)}) collective-permute-start(f32[3,16,1280]{2,1,0:T(8,128)} %get-tuple-element.76), channel_id=1, source_target_pairs={{0,8},{2,6},{4,12},{6,2},{8,0},{10,14},{12,4},{14,10},{16,24},{18,... | collective-permute-start | bytes 737288 | tf_op jit(solution)/shard_map/ppermute | solution.py:464
  115.1 12.4 %collective-permute-start.15 = (f32[3,8,1280]{2,1,0:T(8,128)}, f32[3,8,1280]{2,1,0:T(8,128)}, u32[]{:S(2)}, u32[]{:S(2)}) collective-permute-start(f32[3,8,1280]{2,1,0:T(8,128)} %gated.9), channel_id=1, source_target_pairs={{0,16},{2,18},{4,20},{6,22},{8,24},{10,26},{12,28},{14,30},{16,0},... | collective-permute-start | bytes 368648 | tf_op jit(solution)/shard_map/ppermute | solution.py:464
  115.5 13.9 %collective-permute-start.17 = (f32[3,8,1280]{2,1,0:T(8,128)}, f32[3,8,1280]{2,1,0:T(8,128)S(1)}, u32[]{:S(2)}, u32[]{:S(2)}) collective-permute-start(f32[3,8,1280]{2,1,0:T(8,128)} %gated.10), channel_id=1, source_target_pairs={{0,16},{2,18},{4,20},{6,22},{8,24},{10,26},{12,28},{14,30},{16,0},... | collective-permute-start | bytes 368648 | tf_op jit(solution)/shard_map/ppermute | solution.py:464
  118.1 13.2 %copy-start.12 = (f32[3,32,1280]{2,1,0:T(8,128)S(1)}, f32[3,32,1280]{2,1,0:T(8,128)}, u32[]{:S(2)}) copy-start(f32[3,32,1280]{2,1,0:T(8,128)} %get-tuple-element.69) | copy-start | bytes 1474564
  119.2 12.0 %collective-permute-start.18 = (f32[3,32,1280]{2,1,0:T(8,128)S(1)}, f32[3,32,1280]{2,1,0:T(8,128)S(1)}, u32[]{:S(2)}, u32[]{:S(2)}) collective-permute-start(f32[3,32,1280]{2,1,0:T(8,128)S(1)} %add.325), channel_id=1, source_target_pairs={{0,4},{2,10},{4,0},{6,14},{8,12},{10,2},{12,8},{14,6},{16,20},{18,... | collective-permute-start | bytes 1474568 | tf_op jit(solution)/shard_map/ppermute | solution.py:469
  127.5 24.9 %collective-permute-start.28 = (f32[8,1280]{1,0:T(8,128)S(1)}, f32[8,1280]{1,0:T(8,128)S(1)}, u32[]{:S(2)}, u32[]{:S(2)}) collective-permute-start(f32[8,1280]{1,0:T(8,128)S(1)} %fusion.18), channel_id=1, source_target_pairs={{0,0},{1,2},{2,1},{3,3},{4,4},{5,10},{6,9},{7,7},{8,8},{9,6},{10,5... | collective-permute-start | bytes 122888 | tf_op jit(solution)/shard_map/ppermute | solution.py:521
  131.0 6.5 %collective-permute-start.32 = (f32[3,8,1280]{2,1,0:T(8,128)S(1)}, f32[3,8,1280]{2,1,0:T(8,128)S(1)}, u32[]{:S(2)}, u32[]{:S(2)}) collective-permute-start(f32[3,8,1280]{2,1,0:T(8,128)S(1)} %dynamic-slice_add_fusion.11), channel_id=1, source_target_pairs={{0,16},{2,18},{4,20},{6,22},{8,24},{10,26},{12,28},{14,30},{16,0},... | collective-permute-start | bytes 368648 | tf_op jit(solution)/shard_map/ppermute | solution.py:464
  131.3 10.5 %collective-permute-start.34 = (f32[3,16,1280]{2,1,0:T(8,128)S(1)}, f32[3,16,1280]{2,1,0:T(8,128)S(1)}, u32[]{:S(2)}, u32[]{:S(2)}) collective-permute-start(f32[3,16,1280]{2,1,0:T(8,128)S(1)} %get-tuple-element.78), channel_id=1, source_target_pairs={{0,8},{2,6},{4,12},{6,2},{8,0},{10,14},{12,4},{14,10},{16,24},{18,... | collective-permute-start | bytes 737288 | tf_op jit(solution)/shard_map/ppermute | solution.py:464
  138.5 6.0 %collective-permute-start.19 = (f32[2,8,1280]{2,1,0:T(8,128)}, f32[2,8,1280]{2,1,0:T(8,128)S(1)}, u32[]{:S(2)}, u32[]{:S(2)}) collective-permute-start(f32[2,8,1280]{2,1,0:T(8,128)} %gated.11), channel_id=1, source_target_pairs={{0,1},{1,0},{2,3},{3,2},{4,5},{5,4},{6,7},{7,6},{8,9},{9,8},{10,11... | collective-permute-start | bytes 245768 | tf_op jit(solution)/shard_map/ppermute | solution.py:510
  141.9 10.5 %collective-permute-start.35 = (f32[3,8,1280]{2,1,0:T(8,128)S(1)}, f32[3,8,1280]{2,1,0:T(8,128)S(1)}, u32[]{:S(2)}, u32[]{:S(2)}) collective-permute-start(f32[3,8,1280]{2,1,0:T(8,128)S(1)} %dynamic-slice_add_fusion.10), channel_id=1, source_target_pairs={{0,16},{2,18},{4,20},{6,22},{8,24},{10,26},{12,28},{14,30},{16,0},... | collective-permute-start | bytes 368648 | tf_op jit(solution)/shard_map/ppermute | solution.py:464
  144.5 9.6 %collective-permute-start.20 = (f32[2,8,1280]{2,1,0:T(8,128)S(1)}, f32[2,8,1280]{2,1,0:T(8,128)S(1)}, u32[]{:S(2)}, u32[]{:S(2)}) collective-permute-start(f32[2,8,1280]{2,1,0:T(8,128)S(1)} %collective-permute-done.19), channel_id=1, source_target_pairs={{0,16},{2,18},{4,20},{6,22},{8,24},{10,26},{12,28},{14,30},{16,0},... | collective-permute-start | bytes 245768 | tf_op jit(solution)/shard_map/ppermute | solution.py:475
  152.5 7.2 %collective-permute-start.36 = (f32[3,8,1280]{2,1,0:T(8,128)S(1)}, f32[3,8,1280]{2,1,0:T(8,128)S(1)}, u32[]{:S(2)}, u32[]{:S(2)}) collective-permute-start(f32[3,8,1280]{2,1,0:T(8,128)S(1)} %pad_maximum_fusion), channel_id=1, source_target_pairs={{0,16},{2,18},{4,20},{6,22},{8,24},{10,26},{12,28},{14,30},{16,0},... | collective-permute-start | bytes 368648 | tf_op jit(solution)/shard_map/ppermute | solution.py:475
  154.1 6.8 %collective-permute-start.21 = (f32[2,16,1280]{2,1,0:T(8,128)S(1)}, f32[2,16,1280]{2,1,0:T(8,128)S(1)}, u32[]{:S(2)}, u32[]{:S(2)}) collective-permute-start(f32[2,16,1280]{2,1,0:T(8,128)S(1)} %maximum_select_fusion.7), channel_id=1, source_target_pairs={{0,8},{2,6},{4,12},{6,2},{8,0},{10,14},{12,4},{14,10},{16,24},{18,... | collective-permute-start | bytes 491528 | tf_op jit(solution)/shard_map/ppermute | solution.py:475
  159.7 8.6 %collective-permute-start.37 = (f32[3,16,1280]{2,1,0:T(8,128)S(1)}, f32[3,16,1280]{2,1,0:T(8,128)S(1)}, u32[]{:S(2)}, u32[]{:S(2)}) collective-permute-start(f32[3,16,1280]{2,1,0:T(8,128)S(1)} %maximum_select_fusion.6), channel_id=1, source_target_pairs={{0,8},{2,6},{4,12},{6,2},{8,0},{10,14},{12,4},{14,10},{16,24},{18,... | collective-permute-start | bytes 737288 | tf_op jit(solution)/shard_map/ppermute | solution.py:475
  160.9 7.6 %collective-permute-start.22 = (f32[2,32,1280]{2,1,0:T(8,128)S(1)}, f32[2,32,1280]{2,1,0:T(8,128)S(1)}, u32[]{:S(2)}, u32[]{:S(2)}) collective-permute-start(f32[2,32,1280]{2,1,0:T(8,128)S(1)} %maximum_select_fusion.5), channel_id=1, source_target_pairs={{0,4},{2,10},{4,0},{6,14},{8,12},{10,2},{12,8},{14,6},{16,20},{18,... | collective-permute-start | bytes 983048 | tf_op jit(solution)/shard_map/ppermute | solution.py:475
  168.3 8.9 %collective-permute-start.38 = (f32[3,32,1280]{2,1,0:T(8,128)S(1)}, f32[3,32,1280]{2,1,0:T(8,128)S(1)}, u32[]{:S(2)}, u32[]{:S(2)}) collective-permute-start(f32[3,32,1280]{2,1,0:T(8,128)S(1)} %maximum_select_fusion.4), channel_id=1, source_target_pairs={{0,4},{2,10},{4,0},{6,14},{8,12},{10,2},{12,8},{14,6},{16,20},{18,... | collective-permute-start | bytes 1474568 | tf_op jit(solution)/shard_map/ppermute | solution.py:475
  168.5 8.8 %collective-permute-start.23 = (f32[2,64,1280]{2,1,0:T(8,128)S(1)}, f32[2,64,1280]{2,1,0:T(8,128)S(1)}, u32[]{:S(2)}, u32[]{:S(2)}) collective-permute-start(f32[2,64,1280]{2,1,0:T(8,128)S(1)} %maximum_select_fusion.3), channel_id=1, source_target_pairs={{0,2},{2,0},{4,6},{6,4},{8,10},{10,8},{12,14},{14,12},{16,18},{18,... | collective-permute-start | bytes 1966088 | tf_op jit(solution)/shard_map/ppermute | solution.py:475
  177.3 2.6 %collective-permute-start.39 = (f32[3,64,1280]{2,1,0:T(8,128)S(1)}, f32[3,64,1280]{2,1,0:T(8,128)S(1)}, u32[]{:S(2)}, u32[]{:S(2)}) collective-permute-start(f32[3,64,1280]{2,1,0:T(8,128)S(1)} %maximum_select_fusion.2), channel_id=1, source_target_pairs={{0,2},{2,0},{4,6},{6,4},{8,10},{10,8},{12,14},{14,12},{16,18},{18,... | collective-permute-start | bytes 2949128 | tf_op jit(solution)/shard_map/ppermute | solution.py:475
  (12 other events, 40.3 us)

commit v21 on v16

--- a/solution.py
+++ b/solution.py
@@ -16,7 +16,7 @@
 LANE = 128
 VMEM_LIMIT = 60 * 1024 * 1024
 KERNEL_WORK = 8
-ORDER = ((2, 4, 8), (4, 8, 2))
+ORDER = ((2, 4, 8), (4, 2, 8))
 AHEAD = ((), (), (0,), (1, 0), (2, 1, 0))
 
 
@@ -335,19 +335,19 @@
             result.append((east_of(here), north_of(field[c, rows_of(before), :], here, field[c, rows_of(after), :])))
         return result
 
-    @pl.loop(0, blocks, unroll=6)
+    @pl.loop(0, blocks, unroll=9)
     def _(block):
         flow = [wind[c, rows_of(block), :] for c in range(2)]
         for c, (east, north) in enumerate(derivatives(wind, block)):
             second[c, rows_of(block), :] = 0.25 * (flow[0] * east + flow[1] * north) - flow[c]
 
-    @pl.loop(0, blocks, unroll=6)
+    @pl.loop(0, blocks, unroll=9)
     def _(block):
         flow = [wind[c, rows_of(block), :] for c in range(2)]
         for c, (east, north) in enumerate(derivatives(second, block)):
             third[c, rows_of(block), :] = -flow[c] - 0.25 * (flow[0] * east + flow[1] * north)
 
-    @pl.loop(0, blocks, unroll=6)
+    @pl.loop(0, blocks, unroll=9)
     def _(block):
         flow = [wind[c, rows_of(block), :] for c in range(2)]
         for c, (east, north) in enumerate(derivatives(third, block)):
@@ -465,12 +465,8 @@
         leaves = passed + passed_more
         return [kept, kept_more, lax.ppermute(leaves, "mem", ways[step])], leaves
 
-    def shared(parts_of, step):
-        total = sum(parts_of)
-        return [total, lax.ppermute(total, "mem", ways[step])], total
-
     def advanced(parts_of, step):
-        return (across if step == 0 else halved if step + 1 < len(ways) else shared)(parts_of, step)
+        return (across if step == 0 else halved)(parts_of, step)
 
     def doubled(part, step):
         beside = lax.ppermute(part, "mem", cores if step < 0 else ways[step])
@@ -478,7 +474,7 @@
         return jnp.where(mine == 0, jnp.concatenate([part, beside], axis=1), jnp.concatenate([beside, part], axis=1))
 
     def gathered(part):
-        for step in range(len(ways) - 2, -2, -1):
+        for step in range(len(ways) - 1, -2, -1):
             part = doubled(part, step)
         return part
 
@@ -505,13 +501,13 @@
     place_of = {}
     for m in range(members):
         for b in range(2):
-            *bits, last = ORDER[m % 2]
+            bits = ORDER[m % 2]
             piece = functools.reduce(lambda value, bit: 2 * value + m // bit % 2, bits, m % 2)
-            place_of[piece, m // last % 2, b] = m * 2 + b
-    trades, half = [], members // 4
-    for (piece, twin, b), index in place_of.items():
-        mate = (piece, b) if (piece < half) == (b == 0) else ((piece + half) % (2 * half), 1 - b)
-        trades.append((index, place_of[mate[0], twin, mate[1]]))
+            place_of[piece, b] = m * 2 + b
+    trades, half = [], members // 2
+    for (piece, b), index in place_of.items():
+        mate = (piece, b) if (piece < half) == (b == 0) else ((piece + half) % members, 1 - b)
+        trades.append((index, place_of[mate]))
     both = lax.ppermute(pieces["both"][0], ("mem", "band"), trades)
 
     early = gathered(jnp.concatenate([other, both[None]]))

time: 202 us -> 177 us (0.88)
  starting transfers between devices: 52.5 us -> 36.8 us
  other arithmetic: 13.4 us -> 8.5 us
  waiting for transfers between devices: 68.3 us -> 66.1 us
    ppermute x5 -> x0, waiting for transfers between devices: 24.7 us -> none  [shared(): return ([total, lax.ppermute(total, 'mem', ways[step])], total)]
    ppermute x5 -> x10, waiting for transfers between devices: 15.3 us -> 35.5 us  [halved(): return ([total(mine), lax.ppermute(leaves, 'mem', ways[step])], leaves)]
    ppermute x6 -> x8, waiting for transfers between devices: 12.1 us -> 22 us  [doubled(): beside = lax.ppermute(part, 'mem', cores if step < 0 else ways[step])]
    ppermute x5, waiting for transfers between devices: 7.71 us -> 0.01 us  [across(): return ([kept, kept_more, lax.ppermute(leaves, 'mem', ways[step])], leaves)]
    ppermute x6 -> x8, starting transfers between devices: 14.6 us -> 7.82 us  [doubled(): beside = lax.ppermute(part, 'mem', cores if step < 0 else ways[step])]
    ppermute x5, starting transfers between devices: 9.65 us -> 3.39 us  [by_levels(): second = lax.ppermute(quarters[2], 'mem', cores)]
    ppermute x5 -> x10, starting transfers between devices: 3.37 us -> 9.61 us  [halved(): return ([total(mine), lax.ppermute(leaves, 'mem', ways[step])], leaves)]
    add x5, other arithmetic: 6.95 us -> 1.04 us  [across(): leaves = passed + passed_more]
  transfers between devices with their start and end apart: 38 -> 40, of which waited for: 11 -> 13; matrix products, arithmetic and copies ran while one was open for 6% -> 4% of each run, Pallas kernels for 29% -> 33%
where the time goes in v21:
time: 177 us
  waiting for transfers between devices  66.1 us (37%)
  Pallas kernels  60.1 us (34%)
  starting transfers between devices  36.8 us (21%)
  other arithmetic  8.5 us (5%)
  local copies, waits for them, and re-layouts  4.56 us (3%)
    pallas_call x5, Pallas kernels, window_tensor(): pl.pallas_call(functools.partial(window_kernel, window, len(waits)), out_...  49.9 us
    ppermute x10, waiting for transfers between devices, halved(): return ([total(mine), lax.ppermute(leaves, 'mem', ways[step])], leaves)  35.5 us
    ppermute x8, waiting for transfers between devices, doubled(): beside = lax.ppermute(part, 'mem', cores if step < 0 else ways[step])  22 us
    pallas_call x3, Pallas kernels, pieces_of(): pl.pallas_call(functools.partial(pieces_kernel, windows, slots, count), i...  10.2 us
    ppermute x10, starting transfers between devices, halved(): return ([total(mine), lax.ppermute(leaves, 'mem', ways[step])], leaves)  9.61 us
    ppermute x1, waiting for transfers between devices, by_levels(): remotes = [lax.ppermute(piece, 'band', swap)]  8.2 us
    ppermute x8, starting transfers between devices, doubled(): beside = lax.ppermute(part, 'mem', cores if step < 0 else ways[step])  7.82 us
    ppermute x4, starting transfers between devices, by_levels(): remotes.append(lax.ppermute(piece, 'band', swap))  5.44 us
  transfers between devices with their start and end apart: 40, of which 13 were waited for; matrix products, arithmetic and copies ran while one was open for 4% of the time, Pallas kernels for 33%

profile of v21, /device:TPU:0, one launch (start us, length us, event | category | flops | bytes accessed | tf_op | source)
XLA Modules:
  0.0 176.7 jit_solution(2237249896451602772)
XLA Ops:
  0.0 2.6 %pieces_of.4 = f32[2,136,640]{2,1,0:T(8,128)} custom-call(s32[1]{0:T(128)} %bitcast.5.level_ref, f32[2,2,640,640]{3,2,1,0:T(8,128)} %bitcast.25), custom_call_target="tpu_custom_call" | custom-call | bytes 5242880 | tf_op jit(solution)/shard_map/pieces_of/pallas_call | solution.py:209
  2.6 3.0 %collective-permute-start = (f32[2,136,640]{2,1,0:T(8,128)}, f32[2,136,640]{2,1,0:T(8,128)S(1)}, u32[]{:S(2)}, u32[]{:S(2)}) collective-permute-start(f32[2,136,640]{2,1,0:T(8,128)} %pieces_of.4), channel_id=1, source_target_pairs={{0,1},{1,0},{2,3},{3,2},{4,5},{5,4},{6,7},{7,6},{8,9},{9,8},{10,11... | collective-permute-start | bytes 2088968 | tf_op jit(solution)/shard_map/ppermute | solution.py:443
  5.6 3.6 %pieces_of.5 = (f32[2,128,640]{2,1,0:T(8,128)}, f32[2,128,640]{2,1,0:T(8,128)}, f32[2,128,640]{2,1,0:T(8,128)}, f32[2,120,640]{2,1,0:T(8,128)}) custom-call(s32[1]{0:T(128)} %bitcast.5.level_ref, f32[2,2,640,640]{3,2,1,0:T(8,128)} %bitcast.26), custom_call_target="tpu_custom_call" | custom-call | bytes 10485760 | tf_op jit(solution)/shard_map/pieces_of/pallas_call | solution.py:209
  9.4 4.0 %pieces_of.3 = (f32[2,136,640]{2,1,0:T(8,128)}, f32[2,128,640]{2,1,0:T(8,128)}, f32[2,128,640]{2,1,0:T(8,128)}, f32[2,128,640]{2,1,0:T(8,128)}, f32[2,120,640]{2,1,0:T(8,128)}) custom-call(s32[1]{0:T(128)} %bitcast.level_ref, f32[2,2,640,640]{3,2,1,0:T(8,128)} %bitcast.27), custom_call_target="tpu_custom_call" | custom-call | bytes 13107200 | tf_op jit(solution)/shard_map/pieces_of/pallas_call | solution.py:209
  13.4 0.7 pad_add_fusion.refs_0_
  14.0 8.2 %collective-permute-done.refs_2_.refs_1_ = f32[2,136,640]{2,1,0:T(8,128)S(1)} collective-permute-done((f32[2,136,640]{2,1,0:T(8,128)}, f32[2,136,640]{2,1,0:T(8,128)S(1)}, u32[]{:S(2)}, u32[]{:S(2)}) %collective-permute-start) | collective-permute-done | bytes 696352 | tf_op jit(solution)/shard_map/ppermute | solution.py:443
  22.2 0.9 copy-done.1
  23.1 10.2 %window_tensor.5 = (f32[3,32,1280]{2,1,0:T(8,128)}, f32[3,32,1280]{2,1,0:T(8,128)}, f32[3,32,1280]{2,1,0:T(8,128)}, f32[3,32,1280]{2,1,0:T(8,128)}, f32[2,16,1280]{2,1,0:T(8,128)}) custom-call(s32[4]{0:T(128)} %pad_add_fusion.refs_0_, f32[2,136,640]{2,1,0:T(8,128)} %get-tuple-element.38.refs_1_, f32[2,136,640]{2,1,0:T(8,128)} %copy-done.1, ...), custom_call_target="tpu_custom_call" | custom-call | flops 10695475200 | bytes 6635520 | tf_op jit(solution)/shard_map/window_tensor/pallas_call | solution.py:395
  33.4 2.1 %collective-permute-start.13 = (f32[2,128,640]{2,1,0:T(8,128)}, f32[2,128,640]{2,1,0:T(8,128)S(1)}, u32[]{:S(2)}, u32[]{:S(2)}) collective-permute-start(f32[2,128,640]{2,1,0:T(8,128)} %gated.3), channel_id=1, source_target_pairs={{0,1},{1,0},{2,3},{3,2},{4,5},{5,4},{6,7},{7,6},{8,9},{9,8},{10,11... | collective-permute-start | bytes 1966088 | tf_op jit(solution)/shard_map/ppermute | solution.py:447
  35.5 0.8 copy-done.3
  36.4 9.8 %window_tensor.6 = (f32[3,32,1280]{2,1,0:T(8,128)}, f32[3,32,1280]{2,1,0:T(8,128)}, f32[3,32,1280]{2,1,0:T(8,128)}, f32[3,32,1280]{2,1,0:T(8,128)}, f32[2,16,1280]{2,1,0:T(8,128)}) custom-call(s32[4]{0:T(128)} %pad_add_fusion.refs_0_, f32[2,128,640]{2,1,0:T(8,128)} %get-tuple-element.43.refs_1_, f32[2,128,640]{2,1,0:T(8,128)} %copy-done.3, ...), custom_call_target="tpu_custom_call" | custom-call | flops 10066329600 | bytes 6553600 | tf_op jit(solution)/shard_map/window_tensor/pallas_call | solution.py:395
  46.4 1.7 collective-permute-start.24
  48.6 0.8 add.295.refs_4_
  49.4 1.5 collective-permute-start.3
  51.3 2.0 %collective-permute-start.9 = (f32[3,32,1280]{2,1,0:T(8,128)S(1)}, f32[3,32,1280]{2,1,0:T(8,128)}, u32[]{:S(2)}, u32[]{:S(2)}) collective-permute-start(f32[3,32,1280]{2,1,0:T(8,128)S(1)} %add.310.refs_4_), channel_id=1, source_target_pairs={{0,4},{2,10},{4,0},{6,14},{8,12},{10,2},{12,8},{14,6},{16,20},{18,... | collective-permute-start | bytes 1474568 | tf_op jit(solution)/shard_map/ppermute | solution.py:466
  53.3 10.1 %window_tensor.7 = (f32[3,32,1280]{2,1,0:T(8,128)}, f32[3,32,1280]{2,1,0:T(8,128)}, f32[3,32,1280]{2,1,0:T(8,128)}, f32[3,32,1280]{2,1,0:T(8,128)}, f32[2,16,1280]{2,1,0:T(8,128)}) custom-call(s32[4]{0:T(128)} %pad_add_fusion.refs_0_, f32[2,128,640]{2,1,0:T(8,128)} %get-tuple-element.50.refs_1_, f32[2,128,640]{2,1,0:T(8,128)} %copy-done.2, ...), custom_call_target="tpu_custom_call" | custom-call | flops 10066329600 | bytes 6553600 | tf_op jit(solution)/shard_map/window_tensor/pallas_call | solution.py:395
  63.5 1.6 collective-permute-start.30
  65.1 1.8 %dynamic-slice_add_fusion.9 = (f32[3,16,1280]{2,1,0:T(8,128)S(1)}, f32[3,16,1280]{2,1,0:T(8,128)}) fusion(f32[3,32,1280]{2,1,0:T(8,128)} %collective-permute-done.3, s32[]{:T(128)S(6)} %select_n.212, f32[3,32,1280]{2,1,0:T(8,128)S(1)} %collective-permute-done.1, f32[3,32,1280]{2,1,0:T(8,128)S(1)} %copy-done.4, s32[]{:T(128)S(6)} %select_n.214), kind=kLoop, calls=%fused_computation.27 | loop fusion | flops 245760 | bytes 1966088 | tf_op jit(solution)/shard_map/add | solution.py:458
  67.1 1.6 collective-permute-start.4
  68.7 1.4 dynamic-slice_add_fusion.7
  70.6 9.9 %window_tensor.8 = (f32[3,32,1280]{2,1,0:T(8,128)}, f32[3,32,1280]{2,1,0:T(8,128)}, f32[3,32,1280]{2,1,0:T(8,128)}, f32[3,32,1280]{2,1,0:T(8,128)}, f32[2,16,1280]{2,1,0:T(8,128)}) custom-call(s32[4]{0:T(128)} %pad_add_fusion.refs_0_, f32[2,128,640]{2,1,0:T(8,128)} %get-tuple-element.57.refs_1_, f32[2,128,640]{2,1,0:T(8,128)} %collective-permute-done.24.refs_2_, ...), custom_call_target="tpu_custom_call" | custom-call | flops 10066329600 | bytes 6553600 | tf_op jit(solution)/shard_map/window_tensor/pallas_call | solution.py:395
  81.3 0.7 dynamic-slice_add_fusion.14.refs_6_
  81.9 0.8 collective-permute-start.16
  82.8 2.7 %collective-permute-start.5 = (f32[3,8,1280]{2,1,0:T(8,128)}, f32[3,8,1280]{2,1,0:T(8,128)}, u32[]{:S(2)}, u32[]{:S(2)}) collective-permute-start(f32[3,8,1280]{2,1,0:T(8,128)} %dynamic-slice_add_fusion.14.refs_6_), channel_id=1, source_target_pairs={{0,16},{2,18},{4,20},{6,22},{8,24},{10,26},{12,28},{14,30},{16,0},... | collective-permute-start | bytes 368648 | tf_op jit(solution)/shard_map/ppermute | solution.py:461
  85.5 9.9 %window_tensor.9 = (f32[3,32,1280]{2,1,0:T(8,128)}, f32[3,32,1280]{2,1,0:T(8,128)}, f32[3,32,1280]{2,1,0:T(8,128)}, f32[3,32,1280]{2,1,0:T(8,128)}) custom-call(s32[4]{0:T(128)} %pad_add_fusion.refs_0_, f32[2,120,640]{2,1,0:T(8,128)} %get-tuple-element.64.refs_1_, f32[2,120,640]{2,1,0:T(8,128)} %collective-permute-done.30.refs_2_, ...), custom_call_target="tpu_custom_call" | custom-call | flops 9437184000 | bytes 6471680 | tf_op jit(solution)/shard_map/window_tensor/pallas_call | solution.py:395
  95.8 0.9 add_multiply_fusion.4
  96.7 7.6 %collective-permute-done.11 = f32[3,8,1280]{2,1,0:T(8,128)S(1)} collective-permute-done((f32[3,8,1280]{2,1,0:T(8,128)S(1)}, f32[3,8,1280]{2,1,0:T(8,128)S(1)}, u32[]{:S(2)}, u32[]{:S(2)}) %collective-permute-start.11) | collective-permute-done | bytes 122912 | tf_op jit(solution)/shard_map/ppermute | solution.py:461
  104.6 6.1 %collective-permute-done.17 = f32[3,16,1280]{2,1,0:T(8,128)S(1)} collective-permute-done((f32[3,16,1280]{2,1,0:T(8,128)S(1)}, f32[3,16,1280]{2,1,0:T(8,128)S(1)}, u32[]{:S(2)}, u32[]{:S(2)}) %collective-permute-start.17) | collective-permute-done | bytes 245792 | tf_op jit(solution)/shard_map/ppermute | solution.py:461
  110.9 0.8 collective-permute-start.12
  111.8 0.9 collective-permute-start.27
  112.6 5.4 %collective-permute-done.18 = f32[3,8,1280]{2,1,0:T(8,128)S(1)} collective-permute-done((f32[3,8,1280]{2,1,0:T(8,128)S(1)}, f32[3,8,1280]{2,1,0:T(8,128)S(1)}, u32[]{:S(2)}, u32[]{:S(2)}) %collective-permute-start.18) | collective-permute-done | bytes 122912 | tf_op jit(solution)/shard_map/ppermute | solution.py:461
  118.1 0.9 collective-permute-start.19
  119.0 2.2 %collective-permute-start.31 = (f32[3,32,1280]{2,1,0:T(8,128)}, f32[3,32,1280]{2,1,0:T(8,128)S(1)}, u32[]{:S(2)}, u32[]{:S(2)}) collective-permute-start(f32[3,32,1280]{2,1,0:T(8,128)} %get-tuple-element.68), channel_id=1, source_target_pairs={{0,2},{2,0},{4,6},{6,4},{8,10},{10,8},{12,14},{14,12},{16,18},{18,... | collective-permute-start | bytes 1474568 | tf_op jit(solution)/shard_map/ppermute | solution.py:491
  121.4 3.2 %collective-permute-start.20 = (f32[3,8,1280]{2,1,0:T(8,128)S(1)}, f32[3,8,1280]{2,1,0:T(8,128)S(1)}, u32[]{:S(2)}, u32[]{:S(2)}) collective-permute-start(f32[3,8,1280]{2,1,0:T(8,128)S(1)} %pad_maximum_fusion), channel_id=1, source_target_pairs={{0,16},{2,18},{4,20},{6,22},{8,24},{10,26},{12,28},{14,30},{16,0},... | collective-permute-start | bytes 368648 | tf_op jit(solution)/shard_map/ppermute | solution.py:472
  124.7 5.0 %collective-permute-done.20 = f32[3,8,1280]{2,1,0:T(8,128)S(1)} collective-permute-done((f32[3,8,1280]{2,1,0:T(8,128)S(1)}, f32[3,8,1280]{2,1,0:T(8,128)S(1)}, u32[]{:S(2)}, u32[]{:S(2)}) %collective-permute-start.20) | collective-permute-done | bytes 122912 | tf_op jit(solution)/shard_map/ppermute | solution.py:472
  130.4 4.1 %collective-permute-done.28 = f32[3,16,1280]{2,1,0:T(8,128)S(1)} collective-permute-done((f32[3,16,1280]{2,1,0:T(8,128)S(1)}, f32[3,16,1280]{2,1,0:T(8,128)S(1)}, u32[]{:S(2)}, u32[]{:S(2)}) %collective-permute-start.28) | collective-permute-done | bytes 245792 | tf_op jit(solution)/shard_map/ppermute | solution.py:461
  134.7 1.7 collective-permute-start.34
  136.4 7.1 %collective-permute-done.29 = f32[3,8,1280]{2,1,0:T(8,128)S(1)} collective-permute-done((f32[3,8,1280]{2,1,0:T(8,128)S(1)}, f32[3,8,1280]{2,1,0:T(8,128)S(1)}, u32[]{:S(2)}, u32[]{:S(2)}) %collective-permute-start.29) | collective-permute-done | bytes 122912 | tf_op jit(solution)/shard_map/ppermute | solution.py:461
  143.5 2.5 %collective-permute-start.35 = (f32[3,8,1280]{2,1,0:T(8,128)S(1)}, f32[3,8,1280]{2,1,0:T(8,128)S(1)}, u32[]{:S(2)}, u32[]{:S(2)}) collective-permute-start(f32[3,8,1280]{2,1,0:T(8,128)S(1)} %dynamic-slice_add_fusion.10), channel_id=1, source_target_pairs={{0,16},{2,18},{4,20},{6,22},{8,24},{10,26},{12,28},{14,30},{16,0},... | collective-permute-start | bytes 368648 | tf_op jit(solution)/shard_map/ppermute | solution.py:461
  146.1 5.3 %collective-permute-done.35 = f32[3,8,1280]{2,1,0:T(8,128)S(1)} collective-permute-done((f32[3,8,1280]{2,1,0:T(8,128)S(1)}, f32[3,8,1280]{2,1,0:T(8,128)S(1)}, u32[]{:S(2)}, u32[]{:S(2)}) %collective-permute-start.35) | collective-permute-done | bytes 122912 | tf_op jit(solution)/shard_map/ppermute | solution.py:461
  152.0 1.6 collective-permute-start.22
  153.6 4.1 %collective-permute-done.36 = f32[2,8,1280]{2,1,0:T(8,128)S(1)} collective-permute-done((f32[2,8,1280]{2,1,0:T(8,128)S(1)}, f32[2,8,1280]{2,1,0:T(8,128)S(1)}, u32[]{:S(2)}, u32[]{:S(2)}) %collective-permute-start.36) | collective-permute-done | bytes 81952 | tf_op jit(solution)/shard_map/ppermute | solution.py:472
  158.3 5.0 %collective-permute-done.37 = f32[2,16,1280]{2,1,0:T(8,128)S(1)} collective-permute-done((f32[2,16,1280]{2,1,0:T(8,128)S(1)}, f32[2,16,1280]{2,1,0:T(8,128)S(1)}, u32[]{:S(2)}, u32[]{:S(2)}) %collective-permute-start.37) | collective-permute-done | bytes 163872 | tf_op jit(solution)/shard_map/ppermute | solution.py:472
  163.3 1.2 collective-permute-start.38
  164.7 5.8 %collective-permute-done.38 = f32[2,32,1280]{2,1,0:T(8,128)S(1)} collective-permute-done((f32[2,32,1280]{2,1,0:T(8,128)S(1)}, f32[2,32,1280]{2,1,0:T(8,128)S(1)}, u32[]{:S(2)}, u32[]{:S(2)}) %collective-permute-start.38) | collective-permute-done | bytes 327712 | tf_op jit(solution)/shard_map/ppermute | solution.py:472
  170.6 2.1 %collective-permute-done.39 = f32[2,64,1280]{2,1,0:T(8,128)S(1)} collective-permute-done((f32[2,64,1280]{2,1,0:T(8,128)S(1)}, f32[2,64,1280]{2,1,0:T(8,128)S(1)}, u32[]{:S(2)}, u32[]{:S(2)}) %collective-permute-start.39) | collective-permute-done | bytes 655392 | tf_op jit(solution)/shard_map/ppermute | solution.py:472
  174.1 1.7 copy-done
  175.8 0.9 slice_dynamic-update-slice_fusion
  (120 shorter events, 7.8 us)
Async XLA Ops:
  2.6 19.6 %collective-permute-start = (f32[2,136,640]{2,1,0:T(8,128)}, f32[2,136,640]{2,1,0:T(8,128)S(1)}, u32[]{:S(2)}, u32[]{:S(2)}) collective-permute-start(f32[2,136,640]{2,1,0:T(8,128)} %pieces_of.4), channel_id=1, source_target_pairs={{0,1},{1,0},{2,3},{3,2},{4,5},{5,4},{6,7},{7,6},{8,9},{9,8},{10,11... | collective-permute-start | bytes 2088968 | tf_op jit(solution)/shard_map/ppermute | solution.py:443
  9.2 26.3 %collective-permute-start.6 = (f32[2,128,640]{2,1,0:T(8,128)}, f32[2,128,640]{2,1,0:T(8,128)S(1)}, u32[]{:S(2)}, u32[]{:S(2)}) collective-permute-start(f32[2,128,640]{2,1,0:T(8,128)} %get-tuple-element.44), channel_id=1, source_target_pairs={{0,1},{1,0},{2,3},{3,2},{4,5},{5,4},{6,7},{7,6},{8,9},{9,8},{10,11... | collective-permute-start | bytes 1966088 | tf_op jit(solution)/shard_map/ppermute | solution.py:447
  33.3 14.8 %collective-permute-start.2 = (f32[3,32,1280]{2,1,0:T(8,128)}, f32[3,32,1280]{2,1,0:T(8,128)S(1)}, u32[]{:S(2)}, u32[]{:S(2)}) collective-permute-start(f32[3,32,1280]{2,1,0:T(8,128)} %get-tuple-element.42), channel_id=1, source_target_pairs={{0,2},{2,0},{4,6},{6,4},{8,10},{10,8},{12,14},{14,12},{16,18},{18,... | collective-permute-start | bytes 1474568 | tf_op jit(solution)/shard_map/ppermute | solution.py:490
  33.4 17.9 %collective-permute-start.13 = (f32[2,128,640]{2,1,0:T(8,128)}, f32[2,128,640]{2,1,0:T(8,128)S(1)}, u32[]{:S(2)}, u32[]{:S(2)}) collective-permute-start(f32[2,128,640]{2,1,0:T(8,128)} %gated.3), channel_id=1, source_target_pairs={{0,1},{1,0},{2,3},{3,2},{4,5},{5,4},{6,7},{7,6},{8,9},{9,8},{10,11... | collective-permute-start | bytes 1966088 | tf_op jit(solution)/shard_map/ppermute | solution.py:447
  46.2 3.2 %collective-permute-start.8 = (f32[3,32,1280]{2,1,0:T(8,128)}, f32[3,32,1280]{2,1,0:T(8,128)S(1)}, u32[]{:S(2)}, u32[]{:S(2)}) collective-permute-start(f32[3,32,1280]{2,1,0:T(8,128)} %get-tuple-element.49), channel_id=1, source_target_pairs={{0,2},{2,0},{4,6},{6,4},{8,10},{10,8},{12,14},{14,12},{16,18},{18,... | collective-permute-start | bytes 1474568 | tf_op jit(solution)/shard_map/ppermute | solution.py:490
  46.4 23.6 %collective-permute-start.24 = (f32[2,128,640]{2,1,0:T(8,128)}, f32[2,128,640]{2,1,0:T(8,128)}, u32[]{:S(2)}, u32[]{:S(2)}) collective-permute-start(f32[2,128,640]{2,1,0:T(8,128)} %gated.4), channel_id=1, source_target_pairs={{0,1},{1,0},{2,3},{3,2},{4,5},{5,4},{6,7},{7,6},{8,9},{9,8},{10,11... | collective-permute-start | bytes 1966088 | tf_op jit(solution)/shard_map/ppermute | solution.py:447
  48.1 15.3 %collective-permute-start.1 = (f32[3,32,1280]{2,1,0:T(8,128)}, f32[3,32,1280]{2,1,0:T(8,128)S(1)}, u32[]{:S(2)}, u32[]{:S(2)}) collective-permute-start(f32[3,32,1280]{2,1,0:T(8,128)} %get-tuple-element.40), channel_id=1, source_target_pairs={{0,2},{2,0},{4,6},{6,4},{8,10},{10,8},{12,14},{14,12},{16,18},{18,... | collective-permute-start | bytes 1474568 | tf_op jit(solution)/shard_map/ppermute | solution.py:491
  48.2 18.8 %collective-permute-start.7 = (f32[3,32,1280]{2,1,0:T(8,128)}, f32[3,32,1280]{2,1,0:T(8,128)}, u32[]{:S(2)}, u32[]{:S(2)}) collective-permute-start(f32[3,32,1280]{2,1,0:T(8,128)} %get-tuple-element.47), channel_id=1, source_target_pairs={{0,2},{2,0},{4,6},{6,4},{8,10},{10,8},{12,14},{14,12},{16,18},{18,... | collective-permute-start | bytes 1474568 | tf_op jit(solution)/shard_map/ppermute | solution.py:491
  49.4 14.1 %collective-permute-start.3 = (f32[3,32,1280]{2,1,0:T(8,128)}, f32[3,32,1280]{2,1,0:T(8,128)}, u32[]{:S(2)}, u32[]{:S(2)}) collective-permute-start(f32[3,32,1280]{2,1,0:T(8,128)} %add.295.refs_4_), channel_id=1, source_target_pairs={{0,4},{2,10},{4,0},{6,14},{8,12},{10,2},{12,8},{14,6},{16,20},{18,... | collective-permute-start | bytes 1474568 | tf_op jit(solution)/shard_map/ppermute | solution.py:466
  51.0 12.4 %copy-start.13 = (f32[3,32,1280]{2,1,0:T(8,128)}, f32[3,32,1280]{2,1,0:T(8,128)S(1)}, u32[]{:S(2)}) copy-start(f32[3,32,1280]{2,1,0:T(8,128)S(1)} %add.310.refs_4_) | copy-start | bytes 1474564
  51.3 15.7 %collective-permute-start.9 = (f32[3,32,1280]{2,1,0:T(8,128)S(1)}, f32[3,32,1280]{2,1,0:T(8,128)}, u32[]{:S(2)}, u32[]{:S(2)}) collective-permute-start(f32[3,32,1280]{2,1,0:T(8,128)S(1)} %add.310.refs_4_), channel_id=1, source_target_pairs={{0,4},{2,10},{4,0},{6,14},{8,12},{10,2},{12,8},{14,6},{16,20},{18,... | collective-permute-start | bytes 1474568 | tf_op jit(solution)/shard_map/ppermute | solution.py:466
  63.4 17.1 %collective-permute-start.15 = (f32[3,32,1280]{2,1,0:T(8,128)}, f32[3,32,1280]{2,1,0:T(8,128)S(1)}, u32[]{:S(2)}, u32[]{:S(2)}) collective-permute-start(f32[3,32,1280]{2,1,0:T(8,128)} %get-tuple-element.56), channel_id=1, source_target_pairs={{0,2},{2,0},{4,6},{6,4},{8,10},{10,8},{12,14},{14,12},{16,18},{18,... | collective-permute-start | bytes 1474568 | tf_op jit(solution)/shard_map/ppermute | solution.py:490
  63.5 19.3 %collective-permute-start.30 = (f32[2,120,640]{2,1,0:T(8,128)}, f32[2,120,640]{2,1,0:T(8,128)}, u32[]{:S(2)}, u32[]{:S(2)}) collective-permute-start(f32[2,120,640]{2,1,0:T(8,128)} %gated.5), channel_id=1, source_target_pairs={{0,1},{1,0},{2,3},{3,2},{4,5},{5,4},{6,7},{7,6},{8,9},{9,8},{10,11... | collective-permute-start | bytes 1843208 | tf_op jit(solution)/shard_map/ppermute | solution.py:447
  66.9 37.5 %collective-permute-start.14 = (f32[3,32,1280]{2,1,0:T(8,128)}, f32[3,32,1280]{2,1,0:T(8,128)S(1)}, u32[]{:S(2)}, u32[]{:S(2)}) collective-permute-start(f32[3,32,1280]{2,1,0:T(8,128)} %get-tuple-element.54), channel_id=1, source_target_pairs={{0,2},{2,0},{4,6},{6,4},{8,10},{10,8},{12,14},{14,12},{16,18},{18,... | collective-permute-start | bytes 1474568 | tf_op jit(solution)/shard_map/ppermute | solution.py:491
  67.1 13.6 %collective-permute-start.4 = (f32[3,16,1280]{2,1,0:T(8,128)}, f32[3,16,1280]{2,1,0:T(8,128)S(1)}, u32[]{:S(2)}, u32[]{:S(2)}) collective-permute-start(f32[3,16,1280]{2,1,0:T(8,128)} %get-tuple-element.80.refs_5_), channel_id=1, source_target_pairs={{0,8},{2,6},{4,12},{6,2},{8,0},{10,14},{12,4},{14,10},{16,24},{18,... | collective-permute-start | bytes 737288 | tf_op jit(solution)/shard_map/ppermute | solution.py:461
  70.0 10.5 %copy-start.16 = (f32[3,16,1280]{2,1,0:T(8,128)}, f32[3,16,1280]{2,1,0:T(8,128)S(1)}, u32[]{:S(2)}) copy-start(f32[3,16,1280]{2,1,0:T(8,128)S(1)} %get-tuple-element.82.refs_5_) | copy-start | bytes 737284
  70.1 11.9 %collective-permute-start.10 = (f32[3,16,1280]{2,1,0:T(8,128)S(1)}, f32[3,16,1280]{2,1,0:T(8,128)S(1)}, u32[]{:S(2)}, u32[]{:S(2)}) collective-permute-start(f32[3,16,1280]{2,1,0:T(8,128)S(1)} %get-tuple-element.82.refs_5_), channel_id=1, source_target_pairs={{0,8},{2,6},{4,12},{6,2},{8,0},{10,14},{12,4},{14,10},{16,24},{18,... | collective-permute-start | bytes 737288 | tf_op jit(solution)/shard_map/ppermute | solution.py:461
  70.6 10.0 %copy-start.14 = (f32[3,32,1280]{2,1,0:T(8,128)S(1)}, f32[3,32,1280]{2,1,0:T(8,128)}, u32[]{:S(2)}) copy-start(f32[3,32,1280]{2,1,0:T(8,128)} %get-tuple-element.55) | copy-start | bytes 1474564
  80.5 31.2 %collective-permute-start.26 = (f32[3,32,1280]{2,1,0:T(8,128)}, f32[3,32,1280]{2,1,0:T(8,128)S(1)}, u32[]{:S(2)}, u32[]{:S(2)}) collective-permute-start(f32[3,32,1280]{2,1,0:T(8,128)} %get-tuple-element.63), channel_id=1, source_target_pairs={{0,2},{2,0},{4,6},{6,4},{8,10},{10,8},{12,14},{14,12},{16,18},{18,... | collective-permute-start | bytes 1474568 | tf_op jit(solution)/shard_map/ppermute | solution.py:490
  80.7 43.8 %collective-permute-start.25 = (f32[3,32,1280]{2,1,0:T(8,128)}, f32[3,32,1280]{2,1,0:T(8,128)S(1)}, u32[]{:S(2)}, u32[]{:S(2)}) collective-permute-start(f32[3,32,1280]{2,1,0:T(8,128)} %get-tuple-element.61), channel_id=1, source_target_pairs={{0,2},{2,0},{4,6},{6,4},{8,10},{10,8},{12,14},{14,12},{16,18},{18,... | collective-permute-start | bytes 1474568 | tf_op jit(solution)/shard_map/ppermute | solution.py:491
  81.9 22.5 %collective-permute-start.16 = (f32[3,32,1280]{2,1,0:T(8,128)S(1)}, f32[3,32,1280]{2,1,0:T(8,128)S(1)}, u32[]{:S(2)}, u32[]{:S(2)}) collective-permute-start(f32[3,32,1280]{2,1,0:T(8,128)S(1)} %add.322.refs_4_), channel_id=1, source_target_pairs={{0,4},{2,10},{4,0},{6,14},{8,12},{10,2},{12,8},{14,6},{16,20},{18,... | collective-permute-start | bytes 1474568 | tf_op jit(solution)/shard_map/ppermute | solution.py:466
  82.8 12.6 %collective-permute-start.5 = (f32[3,8,1280]{2,1,0:T(8,128)}, f32[3,8,1280]{2,1,0:T(8,128)}, u32[]{:S(2)}, u32[]{:S(2)}) collective-permute-start(f32[3,8,1280]{2,1,0:T(8,128)} %dynamic-slice_add_fusion.14.refs_6_), channel_id=1, source_target_pairs={{0,16},{2,18},{4,20},{6,22},{8,24},{10,26},{12,28},{14,30},{16,0},... | collective-permute-start | bytes 368648 | tf_op jit(solution)/shard_map/ppermute | solution.py:461
  85.5 19.0 %copy-start.8 = (f32[3,32,1280]{2,1,0:T(8,128)S(1)}, f32[3,32,1280]{2,1,0:T(8,128)}, u32[]{:S(2)}) copy-start(f32[3,32,1280]{2,1,0:T(8,128)} %get-tuple-element.53) | copy-start | bytes 1474564
  95.4 9.0 %collective-permute-start.11 = (f32[3,8,1280]{2,1,0:T(8,128)S(1)}, f32[3,8,1280]{2,1,0:T(8,128)S(1)}, u32[]{:S(2)}, u32[]{:S(2)}) collective-permute-start(f32[3,8,1280]{2,1,0:T(8,128)S(1)} %dynamic-slice_add_fusion.13), channel_id=1, source_target_pairs={{0,16},{2,18},{4,20},{6,22},{8,24},{10,26},{12,28},{14,30},{16,0},... | collective-permute-start | bytes 368648 | tf_op jit(solution)/shard_map/ppermute | solution.py:461
  96.7 15.0 %copy-start.11 = (f32[3,32,1280]{2,1,0:T(8,128)S(1)}, f32[3,32,1280]{2,1,0:T(8,128)}, u32[]{:S(2)}) copy-start(f32[3,32,1280]{2,1,0:T(8,128)} %get-tuple-element.62) | copy-start | bytes 1474564
  104.3 14.7 %collective-permute-start.32 = (f32[3,32,1280]{2,1,0:T(8,128)}, f32[3,32,1280]{2,1,0:T(8,128)S(1)}, u32[]{:S(2)}, u32[]{:S(2)}) collective-permute-start(f32[3,32,1280]{2,1,0:T(8,128)} %get-tuple-element.70), channel_id=1, source_target_pairs={{0,2},{2,0},{4,6},{6,4},{8,10},{10,8},{12,14},{14,12},{16,18},{18,... | collective-permute-start | bytes 1474568 | tf_op jit(solution)/shard_map/ppermute | solution.py:490
  104.5 16.7 %copy-start.12 = (f32[3,32,1280]{2,1,0:T(8,128)S(1)}, f32[3,32,1280]{2,1,0:T(8,128)}, u32[]{:S(2)}) copy-start(f32[3,32,1280]{2,1,0:T(8,128)} %get-tuple-element.69) | copy-start | bytes 1474564
  104.5 6.3 %collective-permute-start.17 = (f32[3,16,1280]{2,1,0:T(8,128)S(1)}, f32[3,16,1280]{2,1,0:T(8,128)S(1)}, u32[]{:S(2)}, u32[]{:S(2)}) collective-permute-start(f32[3,16,1280]{2,1,0:T(8,128)S(1)} %get-tuple-element.84), channel_id=1, source_target_pairs={{0,8},{2,6},{4,12},{6,2},{8,0},{10,14},{12,4},{14,10},{16,24},{18,... | collective-permute-start | bytes 737288 | tf_op jit(solution)/shard_map/ppermute | solution.py:461
  110.8 7.2 %collective-permute-start.18 = (f32[3,8,1280]{2,1,0:T(8,128)S(1)}, f32[3,8,1280]{2,1,0:T(8,128)S(1)}, u32[]{:S(2)}, u32[]{:S(2)}) collective-permute-start(f32[3,8,1280]{2,1,0:T(8,128)S(1)} %dynamic-slice_add_fusion.12), channel_id=1, source_target_pairs={{0,16},{2,18},{4,20},{6,22},{8,24},{10,26},{12,28},{14,30},{16,0},... | collective-permute-start | bytes 368648 | tf_op jit(solution)/shard_map/ppermute | solution.py:461
  110.9 10.4 %collective-permute-start.12 = (f32[2,8,1280]{2,1,0:T(8,128)S(1)}, f32[2,8,1280]{2,1,0:T(8,128)S(1)}, u32[]{:S(2)}, u32[]{:S(2)}) collective-permute-start(f32[2,8,1280]{2,1,0:T(8,128)S(1)} %pad_maximum_fusion.1), channel_id=1, source_target_pairs={{0,1},{1,0},{2,3},{3,2},{4,5},{5,4},{6,7},{7,6},{8,9},{9,8},{10,11... | collective-permute-start | bytes 245768 | tf_op jit(solution)/shard_map/ppermute | solution.py:500
  111.7 12.8 %copy-start.6 = (f32[3,32,1280]{2,1,0:T(8,128)S(1)}, f32[3,32,1280]{2,1,0:T(8,128)}, u32[]{:S(2)}) copy-start(f32[3,32,1280]{2,1,0:T(8,128)} %get-tuple-element.60) | copy-start | bytes 1474564
  111.8 12.8 %collective-permute-start.27 = (f32[3,32,1280]{2,1,0:T(8,128)S(1)}, f32[3,32,1280]{2,1,0:T(8,128)S(1)}, u32[]{:S(2)}, u32[]{:S(2)}) collective-permute-start(f32[3,32,1280]{2,1,0:T(8,128)S(1)} %add.335), channel_id=1, source_target_pairs={{0,4},{2,10},{4,0},{6,14},{8,12},{10,2},{12,8},{14,6},{16,20},{18,... | collective-permute-start | bytes 1474568 | tf_op jit(solution)/shard_map/ppermute | solution.py:466
  118.1 3.3 %collective-permute-start.19 = (f32[8,1280]{1,0:T(8,128)S(1)}, f32[8,1280]{1,0:T(8,128)S(1)}, u32[]{:S(2)}, u32[]{:S(2)}) collective-permute-start(f32[8,1280]{1,0:T(8,128)S(1)} %fusion.18), channel_id=1, source_target_pairs={{0,0},{1,2},{2,1},{3,3},{4,4},{5,10},{6,9},{7,7},{8,8},{9,6},{10,5... | collective-permute-start | bytes 122888 | tf_op jit(solution)/shard_map/ppermute | solution.py:511
  119.0 15.6 %collective-permute-start.31 = (f32[3,32,1280]{2,1,0:T(8,128)}, f32[3,32,1280]{2,1,0:T(8,128)S(1)}, u32[]{:S(2)}, u32[]{:S(2)}) collective-permute-start(f32[3,32,1280]{2,1,0:T(8,128)} %get-tuple-element.68), channel_id=1, source_target_pairs={{0,2},{2,0},{4,6},{6,4},{8,10},{10,8},{12,14},{14,12},{16,18},{18,... | collective-permute-start | bytes 1474568 | tf_op jit(solution)/shard_map/ppermute | solution.py:491
  121.3 13.4 %copy-start.7 = (f32[3,32,1280]{2,1,0:T(8,128)S(1)}, f32[3,32,1280]{2,1,0:T(8,128)}, u32[]{:S(2)}) copy-start(f32[3,32,1280]{2,1,0:T(8,128)} %get-tuple-element.67) | copy-start | bytes 1474564
  121.3 13.3 %collective-permute-start.33 = (f32[3,32,1280]{2,1,0:T(8,128)S(1)}, f32[3,32,1280]{2,1,0:T(8,128)S(1)}, u32[]{:S(2)}, u32[]{:S(2)}) collective-permute-start(f32[3,32,1280]{2,1,0:T(8,128)S(1)} %add.347), channel_id=1, source_target_pairs={{0,4},{2,10},{4,0},{6,14},{8,12},{10,2},{12,8},{14,6},{16,20},{18,... | collective-permute-start | bytes 1474568 | tf_op jit(solution)/shard_map/ppermute | solution.py:466
  121.4 8.4 %collective-permute-start.20 = (f32[3,8,1280]{2,1,0:T(8,128)S(1)}, f32[3,8,1280]{2,1,0:T(8,128)S(1)}, u32[]{:S(2)}, u32[]{:S(2)}) collective-permute-start(f32[3,8,1280]{2,1,0:T(8,128)S(1)} %pad_maximum_fusion), channel_id=1, source_target_pairs={{0,16},{2,18},{4,20},{6,22},{8,24},{10,26},{12,28},{14,30},{16,0},... | collective-permute-start | bytes 368648 | tf_op jit(solution)/shard_map/ppermute | solution.py:472
  124.7 9.9 %collective-permute-start.28 = (f32[3,16,1280]{2,1,0:T(8,128)S(1)}, f32[3,16,1280]{2,1,0:T(8,128)S(1)}, u32[]{:S(2)}, u32[]{:S(2)}) collective-permute-start(f32[3,16,1280]{2,1,0:T(8,128)S(1)} %get-tuple-element.76), channel_id=1, source_target_pairs={{0,8},{2,6},{4,12},{6,2},{8,0},{10,14},{12,4},{14,10},{16,24},{18,... | collective-permute-start | bytes 737288 | tf_op jit(solution)/shard_map/ppermute | solution.py:461
  129.8 22.2 %collective-permute-start.21 = (f32[3,16,1280]{2,1,0:T(8,128)S(1)}, f32[3,16,1280]{2,1,0:T(8,128)S(1)}, u32[]{:S(2)}, u32[]{:S(2)}) collective-permute-start(f32[3,16,1280]{2,1,0:T(8,128)S(1)} %maximum_select_fusion.7), channel_id=1, source_target_pairs={{0,8},{2,6},{4,12},{6,2},{8,0},{10,14},{12,4},{14,10},{16,24},{18,... | collective-permute-start | bytes 737288 | tf_op jit(solution)/shard_map/ppermute | solution.py:472
  134.5 8.9 %collective-permute-start.29 = (f32[3,8,1280]{2,1,0:T(8,128)S(1)}, f32[3,8,1280]{2,1,0:T(8,128)S(1)}, u32[]{:S(2)}, u32[]{:S(2)}) collective-permute-start(f32[3,8,1280]{2,1,0:T(8,128)S(1)} %dynamic-slice_add_fusion.11), channel_id=1, source_target_pairs={{0,16},{2,18},{4,20},{6,22},{8,24},{10,26},{12,28},{14,30},{16,0},... | collective-permute-start | bytes 368648 | tf_op jit(solution)/shard_map/ppermute | solution.py:461
  134.7 8.8 %collective-permute-start.34 = (f32[3,16,1280]{2,1,0:T(8,128)S(1)}, f32[3,16,1280]{2,1,0:T(8,128)S(1)}, u32[]{:S(2)}, u32[]{:S(2)}) collective-permute-start(f32[3,16,1280]{2,1,0:T(8,128)S(1)} %get-tuple-element.78), channel_id=1, source_target_pairs={{0,8},{2,6},{4,12},{6,2},{8,0},{10,14},{12,4},{14,10},{16,24},{18,... | collective-permute-start | bytes 737288 | tf_op jit(solution)/shard_map/ppermute | solution.py:461
  143.5 7.9 %collective-permute-start.35 = (f32[3,8,1280]{2,1,0:T(8,128)S(1)}, f32[3,8,1280]{2,1,0:T(8,128)S(1)}, u32[]{:S(2)}, u32[]{:S(2)}) collective-permute-start(f32[3,8,1280]{2,1,0:T(8,128)S(1)} %dynamic-slice_add_fusion.10), channel_id=1, source_target_pairs={{0,16},{2,18},{4,20},{6,22},{8,24},{10,26},{12,28},{14,30},{16,0},... | collective-permute-start | bytes 368648 | tf_op jit(solution)/shard_map/ppermute | solution.py:461
  151.5 6.2 %collective-permute-start.36 = (f32[2,8,1280]{2,1,0:T(8,128)S(1)}, f32[2,8,1280]{2,1,0:T(8,128)S(1)}, u32[]{:S(2)}, u32[]{:S(2)}) collective-permute-start(f32[2,8,1280]{2,1,0:T(8,128)S(1)} %pad_maximum_fusion.2), channel_id=1, source_target_pairs={{0,16},{2,18},{4,20},{6,22},{8,24},{10,26},{12,28},{14,30},{16,0},... | collective-permute-start | bytes 245768 | tf_op jit(solution)/shard_map/ppermute | solution.py:472
  152.0 12.5 %collective-permute-start.22 = (f32[3,32,1280]{2,1,0:T(8,128)S(1)}, f32[3,32,1280]{2,1,0:T(8,128)S(1)}, u32[]{:S(2)}, u32[]{:S(2)}) collective-permute-start(f32[3,32,1280]{2,1,0:T(8,128)S(1)} %maximum_select_fusion.5), channel_id=1, source_target_pairs={{0,4},{2,10},{4,0},{6,14},{8,12},{10,2},{12,8},{14,6},{16,20},{18,... | collective-permute-start | bytes 1474568 | tf_op jit(solution)/shard_map/ppermute | solution.py:472
  157.7 5.6 %collective-permute-start.37 = (f32[2,16,1280]{2,1,0:T(8,128)S(1)}, f32[2,16,1280]{2,1,0:T(8,128)S(1)}, u32[]{:S(2)}, u32[]{:S(2)}) collective-permute-start(f32[2,16,1280]{2,1,0:T(8,128)S(1)} %maximum_select_fusion.8), channel_id=1, source_target_pairs={{0,8},{2,6},{4,12},{6,2},{8,0},{10,14},{12,4},{14,10},{16,24},{18,... | collective-permute-start | bytes 491528 | tf_op jit(solution)/shard_map/ppermute | solution.py:472
  163.3 7.1 %collective-permute-start.38 = (f32[2,32,1280]{2,1,0:T(8,128)S(1)}, f32[2,32,1280]{2,1,0:T(8,128)S(1)}, u32[]{:S(2)}, u32[]{:S(2)}) collective-permute-start(f32[2,32,1280]{2,1,0:T(8,128)S(1)} %maximum_select_fusion.6), channel_id=1, source_target_pairs={{0,4},{2,10},{4,0},{6,14},{8,12},{10,2},{12,8},{14,6},{16,20},{18,... | collective-permute-start | bytes 983048 | tf_op jit(solution)/shard_map/ppermute | solution.py:472
  164.6 8.2 %collective-permute-start.23 = (f32[3,64,1280]{2,1,0:T(8,128)S(1)}, f32[3,64,1280]{2,1,0:T(8,128)S(1)}, u32[]{:S(2)}, u32[]{:S(2)}) collective-permute-start(f32[3,64,1280]{2,1,0:T(8,128)S(1)} %maximum_select_fusion.3), channel_id=1, source_target_pairs={{0,2},{2,0},{4,6},{6,4},{8,10},{10,8},{12,14},{14,12},{16,18},{18,... | collective-permute-start | bytes 2949128 | tf_op jit(solution)/shard_map/ppermute | solution.py:472
  170.5 2.2 %collective-permute-start.39 = (f32[2,64,1280]{2,1,0:T(8,128)S(1)}, f32[2,64,1280]{2,1,0:T(8,128)S(1)}, u32[]{:S(2)}, u32[]{:S(2)}) collective-permute-start(f32[2,64,1280]{2,1,0:T(8,128)S(1)} %maximum_select_fusion.4), channel_id=1, source_target_pairs={{0,2},{2,0},{4,6},{6,4},{8,10},{10,8},{12,14},{14,12},{16,18},{18,... | collective-permute-start | bytes 1966088 | tf_op jit(solution)/shard_map/ppermute | solution.py:472
  (9 other events, 24.1 us)

commit v22 on v21

--- a/solution.py
+++ b/solution.py
@@ -17,7 +17,7 @@
 VMEM_LIMIT = 60 * 1024 * 1024
 KERNEL_WORK = 8
 ORDER = ((2, 4, 8), (4, 2, 8))
-AHEAD = ((), (), (0,), (1, 0), (2, 1, 0))
+AHEAD = ((), (), (0,), (1,), (2, 1, 0))
 
 
 def padded(cells, sides, width):

time: 177 us -> 181 us (1.023)
  other arithmetic: 8.5 us -> 15.7 us
  starting transfers between devices: 36.8 us -> 31.6 us
    add x10, other arithmetic: 4.18 us -> 8.56 us  [total(): sum((lax.dynamic_slice_in_dim(part, which * half, half, axis=1) for part...]
    ppermute x8, starting transfers between devices: 7.82 us -> 4.91 us  [doubled(): beside = lax.ppermute(part, 'mem', cores if step < 0 else ways[step])]
    ppermute x10, starting transfers between devices: 9.61 us -> 7.43 us  [halved(): return ([total(mine), lax.ppermute(leaves, 'mem', ways[step])], leaves)]
    ppermute x8, waiting for transfers between devices: 22 us -> 20 us  [doubled(): beside = lax.ppermute(part, 'mem', cores if step < 0 else ways[step])]
    add x5, other arithmetic: 1.04 us -> 2.93 us  [across(): leaves = passed + passed_more]
    unnamed x34 -> x36, local copies, waits for them, and re-layouts: 3.5 us -> 4.57 us
  transfers between devices with their start and end apart: 40 -> 40, of which waited for: 13 -> 17; matrix products, arithmetic and copies ran while one was open for 4% -> 8% of each run, Pallas kernels for 33% -> 32%
where the time goes in v22:
time: 181 us; the launch traced here: 180 us
  waiting for transfers between devices  66.3 us (37%)
  Pallas kernels  59.9 us (33%)
  starting transfers between devices  31.6 us (17%)
  other arithmetic  15.7 us (9%)
  local copies, waits for them, and re-layouts  5.64 us (3%)
    pallas_call x5, Pallas kernels, window_tensor(): pl.pallas_call(functools.partial(window_kernel, window, len(waits)), out_...  49.7 us
    ppermute x10, waiting for transfers between devices, halved(): return ([total(mine), lax.ppermute(leaves, 'mem', ways[step])], leaves)  36.6 us
    ppermute x8, waiting for transfers between devices, doubled(): beside = lax.ppermute(part, 'mem', cores if step < 0 else ways[step])  20 us
    pallas_call x3, Pallas kernels, pieces_of(): pl.pallas_call(functools.partial(pieces_kernel, windows, slots, count), i...  10.2 us
    add x10, other arithmetic, total(): sum((lax.dynamic_slice_in_dim(part, which * half, half, axis=1) for part...  8.56 us
    ppermute x1, waiting for transfers between devices, by_levels(): remotes = [lax.ppermute(piece, 'band', swap)]  8.27 us
    ppermute x10, starting transfers between devices, halved(): return ([total(mine), lax.ppermute(leaves, 'mem', ways[step])], leaves)  7.43 us
    ppermute x5, starting transfers between devices, across(): return ([kept, kept_more, lax.ppermute(leaves, 'mem', ways[step])], leaves)  6.28 us
  transfers between devices with their start and end apart: 40, of which 17 were waited for; matrix products, arithmetic and copies ran while one was open for 8% of the time, Pallas kernels for 32%

profile of v22, /device:TPU:0, one launch (start us, length us, event | category | flops | bytes accessed | tf_op | source)
XLA Modules:
  0.0 179.7 jit_solution(739088270231615922)
XLA Ops:
  0.0 2.6 %pieces_of.4 = f32[2,136,640]{2,1,0:T(8,128)} custom-call(s32[1]{0:T(128)} %bitcast.5.level_ref, f32[2,2,640,640]{3,2,1,0:T(8,128)} %bitcast.25), custom_call_target="tpu_custom_call" | custom-call | bytes 5242880 | tf_op jit(solution)/shard_map/pieces_of/pallas_call | solution.py:209
  2.6 3.0 %collective-permute-start = (f32[2,136,640]{2,1,0:T(8,128)}, f32[2,136,640]{2,1,0:T(8,128)S(1)}, u32[]{:S(2)}, u32[]{:S(2)}) collective-permute-start(f32[2,136,640]{2,1,0:T(8,128)} %pieces_of.4), channel_id=1, source_target_pairs={{0,1},{1,0},{2,3},{3,2},{4,5},{5,4},{6,7},{7,6},{8,9},{9,8},{10,11... | collective-permute-start | bytes 2088968 | tf_op jit(solution)/shard_map/ppermute | solution.py:443
  5.6 3.6 %pieces_of.5 = (f32[2,128,640]{2,1,0:T(8,128)}, f32[2,128,640]{2,1,0:T(8,128)}, f32[2,128,640]{2,1,0:T(8,128)}, f32[2,120,640]{2,1,0:T(8,128)}) custom-call(s32[1]{0:T(128)} %bitcast.5.level_ref, f32[2,2,640,640]{3,2,1,0:T(8,128)} %bitcast.26), custom_call_target="tpu_custom_call" | custom-call | bytes 10485760 | tf_op jit(solution)/shard_map/pieces_of/pallas_call | solution.py:209
  9.4 4.0 %pieces_of.3 = (f32[2,136,640]{2,1,0:T(8,128)}, f32[2,128,640]{2,1,0:T(8,128)}, f32[2,128,640]{2,1,0:T(8,128)}, f32[2,128,640]{2,1,0:T(8,128)}, f32[2,120,640]{2,1,0:T(8,128)}) custom-call(s32[1]{0:T(128)} %bitcast.level_ref, f32[2,2,640,640]{3,2,1,0:T(8,128)} %bitcast.27), custom_call_target="tpu_custom_call" | custom-call | bytes 13107200 | tf_op jit(solution)/shard_map/pieces_of/pallas_call | solution.py:209
  14.0 8.3 %collective-permute-done.refs_2_.refs_1_ = f32[2,136,640]{2,1,0:T(8,128)S(1)} collective-permute-done((f32[2,136,640]{2,1,0:T(8,128)}, f32[2,136,640]{2,1,0:T(8,128)S(1)}, u32[]{:S(2)}, u32[]{:S(2)}) %collective-permute-start) | collective-permute-done | bytes 696352 | tf_op jit(solution)/shard_map/ppermute | solution.py:443
  23.1 10.2 %window_tensor.5 = (f32[3,32,1280]{2,1,0:T(8,128)}, f32[3,32,1280]{2,1,0:T(8,128)}, f32[3,32,1280]{2,1,0:T(8,128)}, f32[3,32,1280]{2,1,0:T(8,128)}, f32[2,16,1280]{2,1,0:T(8,128)}) custom-call(s32[4]{0:T(128)} %pad_add_fusion.refs_0_, f32[2,136,640]{2,1,0:T(8,128)} %get-tuple-element.38.refs_1_, f32[2,136,640]{2,1,0:T(8,128)} %copy-done.1, ...), custom_call_target="tpu_custom_call" | custom-call | flops 10695475200 | bytes 6635520 | tf_op jit(solution)/shard_map/window_tensor/pallas_call | solution.py:395
  33.4 2.1 %collective-permute-start.13 = (f32[2,128,640]{2,1,0:T(8,128)}, f32[2,128,640]{2,1,0:T(8,128)S(1)}, u32[]{:S(2)}, u32[]{:S(2)}) collective-permute-start(f32[2,128,640]{2,1,0:T(8,128)} %gated.3), channel_id=1, source_target_pairs={{0,1},{1,0},{2,3},{3,2},{4,5},{5,4},{6,7},{7,6},{8,9},{9,8},{10,11... | collective-permute-start | bytes 1966088 | tf_op jit(solution)/shard_map/ppermute | solution.py:447
  36.4 9.8 %window_tensor.6 = (f32[3,32,1280]{2,1,0:T(8,128)}, f32[3,32,1280]{2,1,0:T(8,128)}, f32[3,32,1280]{2,1,0:T(8,128)}, f32[3,32,1280]{2,1,0:T(8,128)}, f32[2,16,1280]{2,1,0:T(8,128)}) custom-call(s32[4]{0:T(128)} %pad_add_fusion.refs_0_, f32[2,128,640]{2,1,0:T(8,128)} %get-tuple-element.43.refs_1_, f32[2,128,640]{2,1,0:T(8,128)} %copy-done.3, ...), custom_call_target="tpu_custom_call" | custom-call | flops 10066329600 | bytes 6553600 | tf_op jit(solution)/shard_map/window_tensor/pallas_call | solution.py:395
  46.4 1.6 collective-permute-start.24
  49.4 1.5 collective-permute-start.3
  51.0 1.9 %add.310.refs_4_ = f32[3,32,1280]{2,1,0:T(8,128)} add(f32[3,32,1280]{2,1,0:T(8,128)S(1)} %copy-done.17, f32[3,32,1280]{2,1,0:T(8,128)} %collective-permute-done.8) | non-fusion elementwise | flops 122880 | bytes 1474560 | tf_op jit(solution)/shard_map/add | solution.py:465
  53.7 10.1 %window_tensor.7 = (f32[3,32,1280]{2,1,0:T(8,128)}, f32[3,32,1280]{2,1,0:T(8,128)}, f32[3,32,1280]{2,1,0:T(8,128)}, f32[3,32,1280]{2,1,0:T(8,128)}, f32[2,16,1280]{2,1,0:T(8,128)}) custom-call(s32[4]{0:T(128)} %pad_add_fusion.refs_0_, f32[2,128,640]{2,1,0:T(8,128)} %get-tuple-element.50.refs_1_, f32[2,128,640]{2,1,0:T(8,128)} %copy-done.2, ...), custom_call_target="tpu_custom_call" | custom-call | flops 10066329600 | bytes 6553600 | tf_op jit(solution)/shard_map/window_tensor/pallas_call | solution.py:395
  63.9 1.3 collective-permute-done.24.refs_2_
  65.2 9.8 %window_tensor.8 = (f32[3,32,1280]{2,1,0:T(8,128)}, f32[3,32,1280]{2,1,0:T(8,128)}, f32[3,32,1280]{2,1,0:T(8,128)}, f32[3,32,1280]{2,1,0:T(8,128)}, f32[2,16,1280]{2,1,0:T(8,128)}) custom-call(s32[4]{0:T(128)} %pad_add_fusion.refs_0_, f32[2,128,640]{2,1,0:T(8,128)} %get-tuple-element.57.refs_1_, f32[2,128,640]{2,1,0:T(8,128)} %collective-permute-done.24.refs_2_, ...), custom_call_target="tpu_custom_call" | custom-call | flops 10066329600 | bytes 6553600 | tf_op jit(solution)/shard_map/window_tensor/pallas_call | solution.py:395
  75.7 1.8 collective-permute-start.30
  77.5 2.1 %dynamic-slice_add_fusion.9 = (f32[3,16,1280]{2,1,0:T(8,128)S(1)}, f32[3,16,1280]{2,1,0:T(8,128)}) fusion(f32[3,32,1280]{2,1,0:T(8,128)} %copy-done.16, s32[]{:T(128)S(6)} %select_n.212, f32[3,32,1280]{2,1,0:T(8,128)} %copy-done.12, f32[3,32,1280]{2,1,0:T(8,128)S(1)} %copy-done.9, s32[]{:T(128)S(6)} %select_n.214), kind=kLoop, calls=%fused_computation.27 | loop fusion | flops 245760 | bytes 1966088 | tf_op jit(solution)/shard_map/add | solution.py:458
  79.6 1.6 collective-permute-start.4
  81.2 1.9 %dynamic-slice_add_fusion.7 = (f32[3,16,1280]{2,1,0:T(8,128)S(1)}, f32[3,16,1280]{2,1,0:T(8,128)}) fusion(f32[3,32,1280]{2,1,0:T(8,128)} %collective-permute-done.9, s32[]{:T(128)S(6)} %select_n.212, f32[3,32,1280]{2,1,0:T(8,128)S(1)} %collective-permute-done.7, f32[3,32,1280]{2,1,0:T(8,128)S(1)} %copy-done.10, s32[]{:T(128)S(6)} %select_n.214), kind=kLoop, calls=%fused_computation.25 | loop fusion | flops 245760 | bytes 1966088 | tf_op jit(solution)/shard_map/add | solution.py:458
  84.3 1.9 %collective-permute-done.4 = f32[3,16,1280]{2,1,0:T(8,128)} collective-permute-done((f32[3,16,1280]{2,1,0:T(8,128)}, f32[3,16,1280]{2,1,0:T(8,128)}, u32[]{:S(2)}, u32[]{:S(2)}) %collective-permute-start.4) | collective-permute-done | bytes 245792 | tf_op jit(solution)/shard_map/ppermute | solution.py:461
  86.1 1.5 collective-permute-start.27
  87.7 1.6 dynamic-slice_add_fusion.14
  89.2 2.2 %collective-permute-done.10 = f32[3,16,1280]{2,1,0:T(8,128)} collective-permute-done((f32[3,16,1280]{2,1,0:T(8,128)}, f32[3,16,1280]{2,1,0:T(8,128)}, u32[]{:S(2)}, u32[]{:S(2)}) %collective-permute-start.10) | collective-permute-done | bytes 245792 | tf_op jit(solution)/shard_map/ppermute | solution.py:461
  91.5 1.5 collective-permute-start.16
  93.0 1.6 dynamic-slice_add_fusion.13
  94.5 2.6 %collective-permute-start.5 = (f32[3,8,1280]{2,1,0:T(8,128)}, f32[3,8,1280]{2,1,0:T(8,128)}, u32[]{:S(2)}, u32[]{:S(2)}) collective-permute-start(f32[3,8,1280]{2,1,0:T(8,128)} %dynamic-slice_add_fusion.14), channel_id=1, source_target_pairs={{0,16},{2,18},{4,20},{6,22},{8,24},{10,26},{12,28},{14,30},{16,0},... | collective-permute-start | bytes 368648 | tf_op jit(solution)/shard_map/ppermute | solution.py:461
  97.1 9.8 %window_tensor.9 = (f32[3,32,1280]{2,1,0:T(8,128)}, f32[3,32,1280]{2,1,0:T(8,128)}, f32[3,32,1280]{2,1,0:T(8,128)}, f32[3,32,1280]{2,1,0:T(8,128)}) custom-call(s32[4]{0:T(128)} %pad_add_fusion.refs_0_, f32[2,120,640]{2,1,0:T(8,128)} %get-tuple-element.64.refs_1_, f32[2,120,640]{2,1,0:T(8,128)} %collective-permute-done.30.refs_2_, ...), custom_call_target="tpu_custom_call" | custom-call | flops 9437184000 | bytes 6471680 | tf_op jit(solution)/shard_map/window_tensor/pallas_call | solution.py:395
  107.3 1.0 add_multiply_fusion.4
  108.3 5.2 %collective-permute-done.11 = f32[3,8,1280]{2,1,0:T(8,128)S(1)} collective-permute-done((f32[3,8,1280]{2,1,0:T(8,128)}, f32[3,8,1280]{2,1,0:T(8,128)S(1)}, u32[]{:S(2)}, u32[]{:S(2)}) %collective-permute-start.11) | collective-permute-done | bytes 122912 | tf_op jit(solution)/shard_map/ppermute | solution.py:461
  113.5 0.9 add_multiply_fusion.3
  115.9 1.2 dynamic-slice_add_fusion.5
  117.3 2.1 %collective-permute-start.28 = (f32[3,16,1280]{2,1,0:T(8,128)S(1)}, f32[3,16,1280]{2,1,0:T(8,128)S(1)}, u32[]{:S(2)}, u32[]{:S(2)}) collective-permute-start(f32[3,16,1280]{2,1,0:T(8,128)S(1)} %get-tuple-element.76), channel_id=1, source_target_pairs={{0,8},{2,6},{4,12},{6,2},{8,0},{10,14},{12,4},{14,10},{16,24},{18,... | collective-permute-start | bytes 737288 | tf_op jit(solution)/shard_map/ppermute | solution.py:461
  120.3 1.2 collective-permute-start.33
  121.5 3.0 %collective-permute-done.17 = f32[3,16,1280]{2,1,0:T(8,128)S(1)} collective-permute-done((f32[3,16,1280]{2,1,0:T(8,128)S(1)}, f32[3,16,1280]{2,1,0:T(8,128)S(1)}, u32[]{:S(2)}, u32[]{:S(2)}) %collective-permute-start.17) | collective-permute-done | bytes 245792 | tf_op jit(solution)/shard_map/ppermute | solution.py:461
  124.6 8.0 %collective-permute-done.28 = f32[3,16,1280]{2,1,0:T(8,128)S(1)} collective-permute-done((f32[3,16,1280]{2,1,0:T(8,128)S(1)}, f32[3,16,1280]{2,1,0:T(8,128)S(1)}, u32[]{:S(2)}, u32[]{:S(2)}) %collective-permute-start.28) | collective-permute-done | bytes 245792 | tf_op jit(solution)/shard_map/ppermute | solution.py:461
  132.7 2.6 %collective-permute-done.18 = f32[3,8,1280]{2,1,0:T(8,128)S(1)} collective-permute-done((f32[3,8,1280]{2,1,0:T(8,128)S(1)}, f32[3,8,1280]{2,1,0:T(8,128)S(1)}, u32[]{:S(2)}, u32[]{:S(2)}) %collective-permute-start.18) | collective-permute-done | bytes 122912 | tf_op jit(solution)/shard_map/ppermute | solution.py:461
  136.3 2.3 %collective-permute-done.29 = f32[3,8,1280]{2,1,0:T(8,128)S(1)} collective-permute-done((f32[3,8,1280]{2,1,0:T(8,128)S(1)}, f32[3,8,1280]{2,1,0:T(8,128)S(1)}, u32[]{:S(2)}, u32[]{:S(2)}) %collective-permute-start.29) | collective-permute-done | bytes 122912 | tf_op jit(solution)/shard_map/ppermute | solution.py:461
  139.0 1.6 collective-permute-start.20
  140.6 6.0 %collective-permute-done.34 = f32[3,16,1280]{2,1,0:T(8,128)S(1)} collective-permute-done((f32[3,16,1280]{2,1,0:T(8,128)S(1)}, f32[3,16,1280]{2,1,0:T(8,128)S(1)}, u32[]{:S(2)}, u32[]{:S(2)}) %collective-permute-start.34) | collective-permute-done | bytes 245792 | tf_op jit(solution)/shard_map/ppermute | solution.py:461
  146.7 2.1 %collective-permute-done.20 = f32[3,8,1280]{2,1,0:T(8,128)S(1)} collective-permute-done((f32[3,8,1280]{2,1,0:T(8,128)S(1)}, f32[3,8,1280]{2,1,0:T(8,128)S(1)}, u32[]{:S(2)}, u32[]{:S(2)}) %collective-permute-start.20) | collective-permute-done | bytes 122912 | tf_op jit(solution)/shard_map/ppermute | solution.py:472
  148.9 5.3 %collective-permute-done.35 = f32[3,8,1280]{2,1,0:T(8,128)S(1)} collective-permute-done((f32[3,8,1280]{2,1,0:T(8,128)S(1)}, f32[3,8,1280]{2,1,0:T(8,128)S(1)}, u32[]{:S(2)}, u32[]{:S(2)}) %collective-permute-start.35) | collective-permute-done | bytes 122912 | tf_op jit(solution)/shard_map/ppermute | solution.py:461
  154.4 2.4 %collective-permute-done.21 = f32[3,16,1280]{2,1,0:T(8,128)S(1)} collective-permute-done((f32[3,16,1280]{2,1,0:T(8,128)S(1)}, f32[3,16,1280]{2,1,0:T(8,128)S(1)}, u32[]{:S(2)}, u32[]{:S(2)}) %collective-permute-start.21) | collective-permute-done | bytes 245792 | tf_op jit(solution)/shard_map/ppermute | solution.py:472
  156.8 1.2 collective-permute-start.22
  158.0 1.9 %collective-permute-done.36 = f32[2,8,1280]{2,1,0:T(8,128)S(1)} collective-permute-done((f32[2,8,1280]{2,1,0:T(8,128)S(1)}, f32[2,8,1280]{2,1,0:T(8,128)S(1)}, u32[]{:S(2)}, u32[]{:S(2)}) %collective-permute-start.36) | collective-permute-done | bytes 81952 | tf_op jit(solution)/shard_map/ppermute | solution.py:472
  160.0 6.3 %collective-permute-done.37 = f32[2,16,1280]{2,1,0:T(8,128)S(1)} collective-permute-done((f32[2,16,1280]{2,1,0:T(8,128)S(1)}, f32[2,16,1280]{2,1,0:T(8,128)S(1)}, u32[]{:S(2)}, u32[]{:S(2)}) %collective-permute-start.37) | collective-permute-done | bytes 163872 | tf_op jit(solution)/shard_map/ppermute | solution.py:472
  166.4 1.7 collective-permute-start.38
  168.2 5.3 %collective-permute-done.38 = f32[2,32,1280]{2,1,0:T(8,128)S(1)} collective-permute-done((f32[2,32,1280]{2,1,0:T(8,128)S(1)}, f32[2,32,1280]{2,1,0:T(8,128)S(1)}, u32[]{:S(2)}, u32[]{:S(2)}) %collective-permute-start.38) | collective-permute-done | bytes 327712 | tf_op jit(solution)/shard_map/ppermute | solution.py:472
  173.6 2.1 %collective-permute-done.39 = f32[2,64,1280]{2,1,0:T(8,128)S(1)} collective-permute-done((f32[2,64,1280]{2,1,0:T(8,128)S(1)}, f32[2,64,1280]{2,1,0:T(8,128)S(1)}, u32[]{:S(2)}, u32[]{:S(2)}) %collective-permute-start.39) | collective-permute-done | bytes 655392 | tf_op jit(solution)/shard_map/ppermute | solution.py:472
  177.1 1.7 copy-done
  (122 shorter events, 14.0 us)
Async XLA Ops:
  2.6 19.7 %collective-permute-start = (f32[2,136,640]{2,1,0:T(8,128)}, f32[2,136,640]{2,1,0:T(8,128)S(1)}, u32[]{:S(2)}, u32[]{:S(2)}) collective-permute-start(f32[2,136,640]{2,1,0:T(8,128)} %pieces_of.4), channel_id=1, source_target_pairs={{0,1},{1,0},{2,3},{3,2},{4,5},{5,4},{6,7},{7,6},{8,9},{9,8},{10,11... | collective-permute-start | bytes 2088968 | tf_op jit(solution)/shard_map/ppermute | solution.py:443
  9.2 26.3 %collective-permute-start.6 = (f32[2,128,640]{2,1,0:T(8,128)}, f32[2,128,640]{2,1,0:T(8,128)S(1)}, u32[]{:S(2)}, u32[]{:S(2)}) collective-permute-start(f32[2,128,640]{2,1,0:T(8,128)} %get-tuple-element.44), channel_id=1, source_target_pairs={{0,1},{1,0},{2,3},{3,2},{4,5},{5,4},{6,7},{7,6},{8,9},{9,8},{10,11... | collective-permute-start | bytes 1966088 | tf_op jit(solution)/shard_map/ppermute | solution.py:447
  33.3 14.9 %collective-permute-start.2 = (f32[3,32,1280]{2,1,0:T(8,128)}, f32[3,32,1280]{2,1,0:T(8,128)S(1)}, u32[]{:S(2)}, u32[]{:S(2)}) collective-permute-start(f32[3,32,1280]{2,1,0:T(8,128)} %get-tuple-element.42), channel_id=1, source_target_pairs={{0,2},{2,0},{4,6},{6,4},{8,10},{10,8},{12,14},{14,12},{16,18},{18,... | collective-permute-start | bytes 1474568 | tf_op jit(solution)/shard_map/ppermute | solution.py:490
  33.4 19.5 %collective-permute-start.13 = (f32[2,128,640]{2,1,0:T(8,128)}, f32[2,128,640]{2,1,0:T(8,128)S(1)}, u32[]{:S(2)}, u32[]{:S(2)}) collective-permute-start(f32[2,128,640]{2,1,0:T(8,128)} %gated.3), channel_id=1, source_target_pairs={{0,1},{1,0},{2,3},{3,2},{4,5},{5,4},{6,7},{7,6},{8,9},{9,8},{10,11... | collective-permute-start | bytes 1966088 | tf_op jit(solution)/shard_map/ppermute | solution.py:447
  46.2 3.2 %collective-permute-start.8 = (f32[3,32,1280]{2,1,0:T(8,128)}, f32[3,32,1280]{2,1,0:T(8,128)}, u32[]{:S(2)}, u32[]{:S(2)}) collective-permute-start(f32[3,32,1280]{2,1,0:T(8,128)} %get-tuple-element.49), channel_id=1, source_target_pairs={{0,2},{2,0},{4,6},{6,4},{8,10},{10,8},{12,14},{14,12},{16,18},{18,... | collective-permute-start | bytes 1474568 | tf_op jit(solution)/shard_map/ppermute | solution.py:490
  46.4 4.5 %copy-start.17 = (f32[3,32,1280]{2,1,0:T(8,128)S(1)}, f32[3,32,1280]{2,1,0:T(8,128)}, u32[]{:S(2)}) copy-start(f32[3,32,1280]{2,1,0:T(8,128)} %get-tuple-element.48) | copy-start | bytes 1474564
  46.4 18.8 %collective-permute-start.24 = (f32[2,128,640]{2,1,0:T(8,128)}, f32[2,128,640]{2,1,0:T(8,128)}, u32[]{:S(2)}, u32[]{:S(2)}) collective-permute-start(f32[2,128,640]{2,1,0:T(8,128)} %gated.4), channel_id=1, source_target_pairs={{0,1},{1,0},{2,3},{3,2},{4,5},{5,4},{6,7},{7,6},{8,9},{9,8},{10,11... | collective-permute-start | bytes 1966088 | tf_op jit(solution)/shard_map/ppermute | solution.py:447
  48.1 27.1 %collective-permute-start.1 = (f32[3,32,1280]{2,1,0:T(8,128)}, f32[3,32,1280]{2,1,0:T(8,128)S(1)}, u32[]{:S(2)}, u32[]{:S(2)}) collective-permute-start(f32[3,32,1280]{2,1,0:T(8,128)} %get-tuple-element.40), channel_id=1, source_target_pairs={{0,2},{2,0},{4,6},{6,4},{8,10},{10,8},{12,14},{14,12},{16,18},{18,... | collective-permute-start | bytes 1474568 | tf_op jit(solution)/shard_map/ppermute | solution.py:491
  48.2 31.4 %collective-permute-start.7 = (f32[3,32,1280]{2,1,0:T(8,128)}, f32[3,32,1280]{2,1,0:T(8,128)S(1)}, u32[]{:S(2)}, u32[]{:S(2)}) collective-permute-start(f32[3,32,1280]{2,1,0:T(8,128)} %get-tuple-element.47), channel_id=1, source_target_pairs={{0,2},{2,0},{4,6},{6,4},{8,10},{10,8},{12,14},{14,12},{16,18},{18,... | collective-permute-start | bytes 1474568 | tf_op jit(solution)/shard_map/ppermute | solution.py:491
  49.4 26.3 %collective-permute-start.3 = (f32[3,32,1280]{2,1,0:T(8,128)}, f32[3,32,1280]{2,1,0:T(8,128)S(1)}, u32[]{:S(2)}, u32[]{:S(2)}) collective-permute-start(f32[3,32,1280]{2,1,0:T(8,128)} %add.295.refs_4_), channel_id=1, source_target_pairs={{0,4},{2,10},{4,0},{6,14},{8,12},{10,2},{12,8},{14,6},{16,20},{18,... | collective-permute-start | bytes 1474568 | tf_op jit(solution)/shard_map/ppermute | solution.py:466
  52.9 28.3 %collective-permute-start.9 = (f32[3,32,1280]{2,1,0:T(8,128)}, f32[3,32,1280]{2,1,0:T(8,128)}, u32[]{:S(2)}, u32[]{:S(2)}) collective-permute-start(f32[3,32,1280]{2,1,0:T(8,128)} %add.310.refs_4_), channel_id=1, source_target_pairs={{0,4},{2,10},{4,0},{6,14},{8,12},{10,2},{12,8},{14,6},{16,20},{18,... | collective-permute-start | bytes 1474568 | tf_op jit(solution)/shard_map/ppermute | solution.py:466
  75.0 8.5 %collective-permute-start.26 = (f32[3,32,1280]{2,1,0:T(8,128)}, f32[3,32,1280]{2,1,0:T(8,128)S(1)}, u32[]{:S(2)}, u32[]{:S(2)}) collective-permute-start(f32[3,32,1280]{2,1,0:T(8,128)} %get-tuple-element.63), channel_id=1, source_target_pairs={{0,2},{2,0},{4,6},{6,4},{8,10},{10,8},{12,14},{14,12},{16,18},{18,... | collective-permute-start | bytes 1474568 | tf_op jit(solution)/shard_map/ppermute | solution.py:490
  75.1 6.1 %copy-start.10 = (f32[3,32,1280]{2,1,0:T(8,128)S(1)}, f32[3,32,1280]{2,1,0:T(8,128)}, u32[]{:S(2)}) copy-start(f32[3,32,1280]{2,1,0:T(8,128)} %get-tuple-element.46) | copy-start | bytes 1474564
  75.2 8.5 %collective-permute-start.15 = (f32[3,32,1280]{2,1,0:T(8,128)}, f32[3,32,1280]{2,1,0:T(8,128)S(1)}, u32[]{:S(2)}, u32[]{:S(2)}) collective-permute-start(f32[3,32,1280]{2,1,0:T(8,128)} %get-tuple-element.56), channel_id=1, source_target_pairs={{0,2},{2,0},{4,6},{6,4},{8,10},{10,8},{12,14},{14,12},{16,18},{18,... | collective-permute-start | bytes 1474568 | tf_op jit(solution)/shard_map/ppermute | solution.py:490
  75.7 18.8 %collective-permute-start.30 = (f32[2,120,640]{2,1,0:T(8,128)}, f32[2,120,640]{2,1,0:T(8,128)}, u32[]{:S(2)}, u32[]{:S(2)}) collective-permute-start(f32[2,120,640]{2,1,0:T(8,128)} %gated.5), channel_id=1, source_target_pairs={{0,1},{1,0},{2,3},{3,2},{4,5},{5,4},{6,7},{7,6},{8,9},{9,8},{10,11... | collective-permute-start | bytes 1843208 | tf_op jit(solution)/shard_map/ppermute | solution.py:447
  77.5 6.1 %copy-start.8 = (f32[3,32,1280]{2,1,0:T(8,128)S(1)}, f32[3,32,1280]{2,1,0:T(8,128)}, u32[]{:S(2)}) copy-start(f32[3,32,1280]{2,1,0:T(8,128)} %get-tuple-element.62) | copy-start | bytes 1474564
  79.6 6.5 %collective-permute-start.4 = (f32[3,16,1280]{2,1,0:T(8,128)}, f32[3,16,1280]{2,1,0:T(8,128)}, u32[]{:S(2)}, u32[]{:S(2)}) collective-permute-start(f32[3,16,1280]{2,1,0:T(8,128)} %get-tuple-element.80.refs_6_), channel_id=1, source_target_pairs={{0,8},{2,6},{4,12},{6,2},{8,0},{10,14},{12,4},{14,10},{16,24},{18,... | collective-permute-start | bytes 737288 | tf_op jit(solution)/shard_map/ppermute | solution.py:461
  83.1 8.4 %collective-permute-start.10 = (f32[3,16,1280]{2,1,0:T(8,128)}, f32[3,16,1280]{2,1,0:T(8,128)}, u32[]{:S(2)}, u32[]{:S(2)}) collective-permute-start(f32[3,16,1280]{2,1,0:T(8,128)} %get-tuple-element.82.refs_5_), channel_id=1, source_target_pairs={{0,8},{2,6},{4,12},{6,2},{8,0},{10,14},{12,4},{14,10},{16,24},{18,... | collective-permute-start | bytes 737288 | tf_op jit(solution)/shard_map/ppermute | solution.py:461
  83.6 33.6 %collective-permute-start.25 = (f32[3,32,1280]{2,1,0:T(8,128)}, f32[3,32,1280]{2,1,0:T(8,128)S(1)}, u32[]{:S(2)}, u32[]{:S(2)}) collective-permute-start(f32[3,32,1280]{2,1,0:T(8,128)} %get-tuple-element.61), channel_id=1, source_target_pairs={{0,2},{2,0},{4,6},{6,4},{8,10},{10,8},{12,14},{14,12},{16,18},{18,... | collective-permute-start | bytes 1474568 | tf_op jit(solution)/shard_map/ppermute | solution.py:491
  83.6 30.9 %collective-permute-start.14 = (f32[3,32,1280]{2,1,0:T(8,128)}, f32[3,32,1280]{2,1,0:T(8,128)S(1)}, u32[]{:S(2)}, u32[]{:S(2)}) collective-permute-start(f32[3,32,1280]{2,1,0:T(8,128)} %get-tuple-element.54), channel_id=1, source_target_pairs={{0,2},{2,0},{4,6},{6,4},{8,10},{10,8},{12,14},{14,12},{16,18},{18,... | collective-permute-start | bytes 1474568 | tf_op jit(solution)/shard_map/ppermute | solution.py:491
  84.3 12.9 %copy-start.13 = (f32[3,32,1280]{2,1,0:T(8,128)}, f32[3,32,1280]{2,1,0:T(8,128)S(1)}, u32[]{:S(2)}) copy-start(f32[3,32,1280]{2,1,0:T(8,128)S(1)} %add.322.refs_4_) | copy-start | bytes 1474564
  86.1 31.1 %collective-permute-start.27 = (f32[3,32,1280]{2,1,0:T(8,128)S(1)}, f32[3,32,1280]{2,1,0:T(8,128)S(1)}, u32[]{:S(2)}, u32[]{:S(2)}) collective-permute-start(f32[3,32,1280]{2,1,0:T(8,128)S(1)} %add.335), channel_id=1, source_target_pairs={{0,4},{2,10},{4,0},{6,14},{8,12},{10,2},{12,8},{14,6},{16,20},{18,... | collective-permute-start | bytes 1474568 | tf_op jit(solution)/shard_map/ppermute | solution.py:466
  91.5 23.7 %collective-permute-start.16 = (f32[3,32,1280]{2,1,0:T(8,128)S(1)}, f32[3,32,1280]{2,1,0:T(8,128)S(1)}, u32[]{:S(2)}, u32[]{:S(2)}) collective-permute-start(f32[3,32,1280]{2,1,0:T(8,128)S(1)} %add.322.refs_4_), channel_id=1, source_target_pairs={{0,4},{2,10},{4,0},{6,14},{8,12},{10,2},{12,8},{14,6},{16,20},{18,... | collective-permute-start | bytes 1474568 | tf_op jit(solution)/shard_map/ppermute | solution.py:466
  94.5 12.4 %collective-permute-start.5 = (f32[3,8,1280]{2,1,0:T(8,128)}, f32[3,8,1280]{2,1,0:T(8,128)}, u32[]{:S(2)}, u32[]{:S(2)}) collective-permute-start(f32[3,8,1280]{2,1,0:T(8,128)} %dynamic-slice_add_fusion.14), channel_id=1, source_target_pairs={{0,16},{2,18},{4,20},{6,22},{8,24},{10,26},{12,28},{14,30},{16,0},... | collective-permute-start | bytes 368648 | tf_op jit(solution)/shard_map/ppermute | solution.py:461
  106.9 9.0 %copy-start.5 = (f32[3,32,1280]{2,1,0:T(8,128)S(1)}, f32[3,32,1280]{2,1,0:T(8,128)}, u32[]{:S(2)}) copy-start(f32[3,32,1280]{2,1,0:T(8,128)} %get-tuple-element.53) | copy-start | bytes 1474564
  106.9 10.3 %copy-start.4 = (f32[3,32,1280]{2,1,0:T(8,128)S(1)}, f32[3,32,1280]{2,1,0:T(8,128)}, u32[]{:S(2)}) copy-start(f32[3,32,1280]{2,1,0:T(8,128)} %get-tuple-element.60) | copy-start | bytes 1474564
  106.9 6.6 %collective-permute-start.11 = (f32[3,8,1280]{2,1,0:T(8,128)}, f32[3,8,1280]{2,1,0:T(8,128)S(1)}, u32[]{:S(2)}, u32[]{:S(2)}) collective-permute-start(f32[3,8,1280]{2,1,0:T(8,128)} %dynamic-slice_add_fusion.13), channel_id=1, source_target_pairs={{0,16},{2,18},{4,20},{6,22},{8,24},{10,26},{12,28},{14,30},{16,0},... | collective-permute-start | bytes 368648 | tf_op jit(solution)/shard_map/ppermute | solution.py:461
  113.5 6.7 %collective-permute-start.32 = (f32[3,32,1280]{2,1,0:T(8,128)}, f32[3,32,1280]{2,1,0:T(8,128)S(1)}, u32[]{:S(2)}, u32[]{:S(2)}) collective-permute-start(f32[3,32,1280]{2,1,0:T(8,128)} %get-tuple-element.70), channel_id=1, source_target_pairs={{0,2},{2,0},{4,6},{6,4},{8,10},{10,8},{12,14},{14,12},{16,18},{18,... | collective-permute-start | bytes 1474568 | tf_op jit(solution)/shard_map/ppermute | solution.py:490
  114.6 24.1 %collective-permute-start.31 = (f32[3,32,1280]{2,1,0:T(8,128)}, f32[3,32,1280]{2,1,0:T(8,128)S(1)}, u32[]{:S(2)}, u32[]{:S(2)}) collective-permute-start(f32[3,32,1280]{2,1,0:T(8,128)} %get-tuple-element.68), channel_id=1, source_target_pairs={{0,2},{2,0},{4,6},{6,4},{8,10},{10,8},{12,14},{14,12},{16,18},{18,... | collective-permute-start | bytes 1474568 | tf_op jit(solution)/shard_map/ppermute | solution.py:491
  115.9 4.3 %copy-start.11 = (f32[3,32,1280]{2,1,0:T(8,128)S(1)}, f32[3,32,1280]{2,1,0:T(8,128)}, u32[]{:S(2)}) copy-start(f32[3,32,1280]{2,1,0:T(8,128)} %get-tuple-element.69) | copy-start | bytes 1474564
  117.1 7.4 %collective-permute-start.17 = (f32[3,16,1280]{2,1,0:T(8,128)S(1)}, f32[3,16,1280]{2,1,0:T(8,128)S(1)}, u32[]{:S(2)}, u32[]{:S(2)}) collective-permute-start(f32[3,16,1280]{2,1,0:T(8,128)S(1)} %get-tuple-element.84), channel_id=1, source_target_pairs={{0,8},{2,6},{4,12},{6,2},{8,0},{10,14},{12,4},{14,10},{16,24},{18,... | collective-permute-start | bytes 737288 | tf_op jit(solution)/shard_map/ppermute | solution.py:461
  117.3 15.3 %collective-permute-start.28 = (f32[3,16,1280]{2,1,0:T(8,128)S(1)}, f32[3,16,1280]{2,1,0:T(8,128)S(1)}, u32[]{:S(2)}, u32[]{:S(2)}) collective-permute-start(f32[3,16,1280]{2,1,0:T(8,128)S(1)} %get-tuple-element.76), channel_id=1, source_target_pairs={{0,8},{2,6},{4,12},{6,2},{8,0},{10,14},{12,4},{14,10},{16,24},{18,... | collective-permute-start | bytes 737288 | tf_op jit(solution)/shard_map/ppermute | solution.py:461
  119.4 19.6 %collective-permute-start.12 = (f32[2,8,1280]{2,1,0:T(8,128)S(1)}, f32[2,8,1280]{2,1,0:T(8,128)S(1)}, u32[]{:S(2)}, u32[]{:S(2)}) collective-permute-start(f32[2,8,1280]{2,1,0:T(8,128)S(1)} %pad_maximum_fusion.1), channel_id=1, source_target_pairs={{0,1},{1,0},{2,3},{3,2},{4,5},{5,4},{6,7},{7,6},{8,9},{9,8},{10,11... | collective-permute-start | bytes 245768 | tf_op jit(solution)/shard_map/ppermute | solution.py:500
  120.3 18.5 %copy-start.7 = (f32[3,32,1280]{2,1,0:T(8,128)S(1)}, f32[3,32,1280]{2,1,0:T(8,128)}, u32[]{:S(2)}) copy-start(f32[3,32,1280]{2,1,0:T(8,128)} %get-tuple-element.67) | copy-start | bytes 1474564
  120.3 18.4 %collective-permute-start.33 = (f32[3,32,1280]{2,1,0:T(8,128)S(1)}, f32[3,32,1280]{2,1,0:T(8,128)S(1)}, u32[]{:S(2)}, u32[]{:S(2)}) collective-permute-start(f32[3,32,1280]{2,1,0:T(8,128)S(1)} %add.347), channel_id=1, source_target_pairs={{0,4},{2,10},{4,0},{6,14},{8,12},{10,2},{12,8},{14,6},{16,20},{18,... | collective-permute-start | bytes 1474568 | tf_op jit(solution)/shard_map/ppermute | solution.py:466
  124.6 10.8 %collective-permute-start.18 = (f32[3,8,1280]{2,1,0:T(8,128)S(1)}, f32[3,8,1280]{2,1,0:T(8,128)S(1)}, u32[]{:S(2)}, u32[]{:S(2)}) collective-permute-start(f32[3,8,1280]{2,1,0:T(8,128)S(1)} %dynamic-slice_add_fusion.12), channel_id=1, source_target_pairs={{0,16},{2,18},{4,20},{6,22},{8,24},{10,26},{12,28},{14,30},{16,0},... | collective-permute-start | bytes 368648 | tf_op jit(solution)/shard_map/ppermute | solution.py:461
  132.7 6.0 %collective-permute-start.29 = (f32[3,8,1280]{2,1,0:T(8,128)S(1)}, f32[3,8,1280]{2,1,0:T(8,128)S(1)}, u32[]{:S(2)}, u32[]{:S(2)}) collective-permute-start(f32[3,8,1280]{2,1,0:T(8,128)S(1)} %dynamic-slice_add_fusion.11), channel_id=1, source_target_pairs={{0,16},{2,18},{4,20},{6,22},{8,24},{10,26},{12,28},{14,30},{16,0},... | collective-permute-start | bytes 368648 | tf_op jit(solution)/shard_map/ppermute | solution.py:461
  135.4 3.5 %collective-permute-start.19 = (f32[8,1280]{1,0:T(8,128)S(1)}, f32[8,1280]{1,0:T(8,128)S(1)}, u32[]{:S(2)}, u32[]{:S(2)}) collective-permute-start(f32[8,1280]{1,0:T(8,128)S(1)} %fusion.18), channel_id=1, source_target_pairs={{0,0},{1,2},{2,1},{3,3},{4,4},{5,10},{6,9},{7,7},{8,8},{9,6},{10,5... | collective-permute-start | bytes 122888 | tf_op jit(solution)/shard_map/ppermute | solution.py:511
  138.8 7.8 %collective-permute-start.34 = (f32[3,16,1280]{2,1,0:T(8,128)S(1)}, f32[3,16,1280]{2,1,0:T(8,128)S(1)}, u32[]{:S(2)}, u32[]{:S(2)}) collective-permute-start(f32[3,16,1280]{2,1,0:T(8,128)S(1)} %get-tuple-element.78), channel_id=1, source_target_pairs={{0,8},{2,6},{4,12},{6,2},{8,0},{10,14},{12,4},{14,10},{16,24},{18,... | collective-permute-start | bytes 737288 | tf_op jit(solution)/shard_map/ppermute | solution.py:461
  139.0 9.8 %collective-permute-start.20 = (f32[3,8,1280]{2,1,0:T(8,128)S(1)}, f32[3,8,1280]{2,1,0:T(8,128)S(1)}, u32[]{:S(2)}, u32[]{:S(2)}) collective-permute-start(f32[3,8,1280]{2,1,0:T(8,128)S(1)} %pad_maximum_fusion), channel_id=1, source_target_pairs={{0,16},{2,18},{4,20},{6,22},{8,24},{10,26},{12,28},{14,30},{16,0},... | collective-permute-start | bytes 368648 | tf_op jit(solution)/shard_map/ppermute | solution.py:472
  146.6 7.6 %collective-permute-start.35 = (f32[3,8,1280]{2,1,0:T(8,128)S(1)}, f32[3,8,1280]{2,1,0:T(8,128)S(1)}, u32[]{:S(2)}, u32[]{:S(2)}) collective-permute-start(f32[3,8,1280]{2,1,0:T(8,128)S(1)} %dynamic-slice_add_fusion.10), channel_id=1, source_target_pairs={{0,16},{2,18},{4,20},{6,22},{8,24},{10,26},{12,28},{14,30},{16,0},... | collective-permute-start | bytes 368648 | tf_op jit(solution)/shard_map/ppermute | solution.py:461
  148.8 7.9 %collective-permute-start.21 = (f32[3,16,1280]{2,1,0:T(8,128)S(1)}, f32[3,16,1280]{2,1,0:T(8,128)S(1)}, u32[]{:S(2)}, u32[]{:S(2)}) collective-permute-start(f32[3,16,1280]{2,1,0:T(8,128)S(1)} %maximum_select_fusion.7), channel_id=1, source_target_pairs={{0,8},{2,6},{4,12},{6,2},{8,0},{10,14},{12,4},{14,10},{16,24},{18,... | collective-permute-start | bytes 737288 | tf_op jit(solution)/shard_map/ppermute | solution.py:472
  154.3 5.6 %collective-permute-start.36 = (f32[2,8,1280]{2,1,0:T(8,128)S(1)}, f32[2,8,1280]{2,1,0:T(8,128)S(1)}, u32[]{:S(2)}, u32[]{:S(2)}) collective-permute-start(f32[2,8,1280]{2,1,0:T(8,128)S(1)} %pad_maximum_fusion.2), channel_id=1, source_target_pairs={{0,16},{2,18},{4,20},{6,22},{8,24},{10,26},{12,28},{14,30},{16,0},... | collective-permute-start | bytes 245768 | tf_op jit(solution)/shard_map/ppermute | solution.py:472
  156.8 11.3 %collective-permute-start.22 = (f32[3,32,1280]{2,1,0:T(8,128)S(1)}, f32[3,32,1280]{2,1,0:T(8,128)S(1)}, u32[]{:S(2)}, u32[]{:S(2)}) collective-permute-start(f32[3,32,1280]{2,1,0:T(8,128)S(1)} %maximum_select_fusion.5), channel_id=1, source_target_pairs={{0,4},{2,10},{4,0},{6,14},{8,12},{10,2},{12,8},{14,6},{16,20},{18,... | collective-permute-start | bytes 1474568 | tf_op jit(solution)/shard_map/ppermute | solution.py:472
  159.9 6.4 %collective-permute-start.37 = (f32[2,16,1280]{2,1,0:T(8,128)S(1)}, f32[2,16,1280]{2,1,0:T(8,128)S(1)}, u32[]{:S(2)}, u32[]{:S(2)}) collective-permute-start(f32[2,16,1280]{2,1,0:T(8,128)S(1)} %maximum_select_fusion.8), channel_id=1, source_target_pairs={{0,8},{2,6},{4,12},{6,2},{8,0},{10,14},{12,4},{14,10},{16,24},{18,... | collective-permute-start | bytes 491528 | tf_op jit(solution)/shard_map/ppermute | solution.py:472
  166.4 7.1 %collective-permute-start.38 = (f32[2,32,1280]{2,1,0:T(8,128)S(1)}, f32[2,32,1280]{2,1,0:T(8,128)S(1)}, u32[]{:S(2)}, u32[]{:S(2)}) collective-permute-start(f32[2,32,1280]{2,1,0:T(8,128)S(1)} %maximum_select_fusion.6), channel_id=1, source_target_pairs={{0,4},{2,10},{4,0},{6,14},{8,12},{10,2},{12,8},{14,6},{16,20},{18,... | collective-permute-start | bytes 983048 | tf_op jit(solution)/shard_map/ppermute | solution.py:472
  168.1 7.7 %collective-permute-start.23 = (f32[3,64,1280]{2,1,0:T(8,128)S(1)}, f32[3,64,1280]{2,1,0:T(8,128)S(1)}, u32[]{:S(2)}, u32[]{:S(2)}) collective-permute-start(f32[3,64,1280]{2,1,0:T(8,128)S(1)} %maximum_select_fusion.3), channel_id=1, source_target_pairs={{0,2},{2,0},{4,6},{6,4},{8,10},{10,8},{12,14},{14,12},{16,18},{18,... | collective-permute-start | bytes 2949128 | tf_op jit(solution)/shard_map/ppermute | solution.py:472
  173.6 2.2 %collective-permute-start.39 = (f32[2,64,1280]{2,1,0:T(8,128)S(1)}, f32[2,64,1280]{2,1,0:T(8,128)S(1)}, u32[]{:S(2)}, u32[]{:S(2)}) collective-permute-start(f32[2,64,1280]{2,1,0:T(8,128)S(1)} %maximum_select_fusion.4), channel_id=1, source_target_pairs={{0,2},{2,0},{4,6},{6,4},{8,10},{10,8},{12,14},{14,12},{16,18},{18,... | collective-permute-start | bytes 1966088 | tf_op jit(solution)/shard_map/ppermute | solution.py:472
  (10 other events, 17.0 us)

commit v23 on v22

--- a/solution.py
+++ b/solution.py
@@ -494,6 +494,8 @@
     pieces = {"own": [], "both": [], "other": []}
     for k, window in enumerate(windows):
         for step in range(done[k], len(ways)):
+            if window.side == "other" and step + 1 == len(ways):
+                sums[k] = [sums[k][0], gated(sums[k][1], [quarters[0]])]
             sums[k], _ = advanced(sums[k], step)
         pieces[window.side].append(exponent_of(sum(sums[k]), members))
 

time: 181 us -> 182 us (level)
  starting transfers between devices: 31.6 us -> 41.9 us
  waiting for transfers between devices: 66.3 us -> 57.1 us
    ppermute x10, waiting for transfers between devices: 36.6 us -> 25.5 us  [halved(): return ([total(mine), lax.ppermute(leaves, 'mem', ways[step])], leaves)]
    ppermute x10, starting transfers between devices: 7.43 us -> 18.1 us  [halved(): return ([total(mine), lax.ppermute(leaves, 'mem', ways[step])], leaves)]
    add x5, other arithmetic: 2.93 us -> 5.96 us  [across(): leaves = passed + passed_more]
    ppermute x8, waiting for transfers between devices: 20 us -> 22.7 us  [doubled(): beside = lax.ppermute(part, 'mem', cores if step < 0 else ways[step])]
    unnamed x36 -> x44, local copies, waits for them, and re-layouts: 4.57 us -> 4.36 us
  transfers between devices with their start and end apart: 40 -> 40, of which waited for: 17 -> 15; matrix products, arithmetic and copies ran while one was open for 8% -> 9% of each run, Pallas kernels for 32% -> 32%
where the time goes in v23:
time: 182 us
  Pallas kernels  60 us (33%)
  waiting for transfers between devices  57.1 us (31%)
  starting transfers between devices  41.9 us (23%)
  other arithmetic  16.9 us (9%)
  local copies, waits for them, and re-layouts  5.42 us (3%)
    pallas_call x5, Pallas kernels, window_tensor(): pl.pallas_call(functools.partial(window_kernel, window, len(waits)), out_...  49.8 us
    ppermute x10, waiting for transfers between devices, halved(): return ([total(mine), lax.ppermute(leaves, 'mem', ways[step])], leaves)  25.5 us
    ppermute x8, waiting for transfers between devices, doubled(): beside = lax.ppermute(part, 'mem', cores if step < 0 else ways[step])  22.7 us
    ppermute x10, starting transfers between devices, halved(): return ([total(mine), lax.ppermute(leaves, 'mem', ways[step])], leaves)  18.1 us
    pallas_call x3, Pallas kernels, pieces_of(): pl.pallas_call(functools.partial(pieces_kernel, windows, slots, count), i...  10.2 us
    ppermute x1, waiting for transfers between devices, by_levels(): remotes = [lax.ppermute(piece, 'band', swap)]  8.27 us
    add x10, other arithmetic, total(): sum((lax.dynamic_slice_in_dim(part, which * half, half, axis=1) for part...  7.63 us
    ppermute x5, starting transfers between devices, across(): return ([kept, kept_more, lax.ppermute(leaves, 'mem', ways[step])], leaves)  6.04 us
  transfers between devices with their start and end apart: 40, of which 15 were waited for; matrix products, arithmetic and copies ran while one was open for 9% of the time, Pallas kernels for 32%

profile of v23, /device:TPU:0, one launch (start us, length us, event | category | flops | bytes accessed | tf_op | source)
XLA Modules:
  0.0 181.9 jit_solution(8780588829324288680)
XLA Ops:
  0.0 2.6 %pieces_of.4 = f32[2,136,640]{2,1,0:T(8,128)} custom-call(s32[1]{0:T(128)} %bitcast.5.level_ref, f32[2,2,640,640]{3,2,1,0:T(8,128)} %bitcast.25), custom_call_target="tpu_custom_call" | custom-call | bytes 5242880 | tf_op jit(solution)/shard_map/pieces_of/pallas_call | solution.py:209
  2.6 3.0 %collective-permute-start = (f32[2,136,640]{2,1,0:T(8,128)}, f32[2,136,640]{2,1,0:T(8,128)S(1)}, u32[]{:S(2)}, u32[]{:S(2)}) collective-permute-start(f32[2,136,640]{2,1,0:T(8,128)} %pieces_of.4), channel_id=1, source_target_pairs={{0,1},{1,0},{2,3},{3,2},{4,5},{5,4},{6,7},{7,6},{8,9},{9,8},{10,11... | collective-permute-start | bytes 2088968 | tf_op jit(solution)/shard_map/ppermute | solution.py:443
  5.6 3.6 %pieces_of.5 = (f32[2,128,640]{2,1,0:T(8,128)}, f32[2,128,640]{2,1,0:T(8,128)}, f32[2,128,640]{2,1,0:T(8,128)}, f32[2,120,640]{2,1,0:T(8,128)}) custom-call(s32[1]{0:T(128)} %bitcast.5.level_ref, f32[2,2,640,640]{3,2,1,0:T(8,128)} %bitcast.26), custom_call_target="tpu_custom_call" | custom-call | bytes 10485760 | tf_op jit(solution)/shard_map/pieces_of/pallas_call | solution.py:209
  9.3 4.0 %pieces_of.3 = (f32[2,136,640]{2,1,0:T(8,128)}, f32[2,128,640]{2,1,0:T(8,128)}, f32[2,128,640]{2,1,0:T(8,128)}, f32[2,128,640]{2,1,0:T(8,128)}, f32[2,120,640]{2,1,0:T(8,128)}) custom-call(s32[1]{0:T(128)} %bitcast.level_ref, f32[2,2,640,640]{3,2,1,0:T(8,128)} %bitcast.27), custom_call_target="tpu_custom_call" | custom-call | bytes 13107200 | tf_op jit(solution)/shard_map/pieces_of/pallas_call | solution.py:209
  14.0 8.3 %collective-permute-done.refs_2_.refs_1_ = f32[2,136,640]{2,1,0:T(8,128)S(1)} collective-permute-done((f32[2,136,640]{2,1,0:T(8,128)}, f32[2,136,640]{2,1,0:T(8,128)S(1)}, u32[]{:S(2)}, u32[]{:S(2)}) %collective-permute-start) | collective-permute-done | bytes 696352 | tf_op jit(solution)/shard_map/ppermute | solution.py:443
  23.1 10.1 %window_tensor.5 = (f32[3,32,1280]{2,1,0:T(8,128)}, f32[3,32,1280]{2,1,0:T(8,128)}, f32[3,32,1280]{2,1,0:T(8,128)}, f32[3,32,1280]{2,1,0:T(8,128)}, f32[2,16,1280]{2,1,0:T(8,128)}) custom-call(s32[4]{0:T(128)} %pad_add_fusion.refs_0_, f32[2,136,640]{2,1,0:T(8,128)} %get-tuple-element.38.refs_1_, f32[2,136,640]{2,1,0:T(8,128)} %copy-done.5, ...), custom_call_target="tpu_custom_call" | custom-call | flops 10695475200 | bytes 6635520 | tf_op jit(solution)/shard_map/window_tensor/pallas_call | solution.py:395
  33.4 2.1 %collective-permute-start.5 = (f32[2,128,640]{2,1,0:T(8,128)}, f32[2,128,640]{2,1,0:T(8,128)S(1)}, u32[]{:S(2)}, u32[]{:S(2)}) collective-permute-start(f32[2,128,640]{2,1,0:T(8,128)} %gated.5), channel_id=1, source_target_pairs={{0,1},{1,0},{2,3},{3,2},{4,5},{5,4},{6,7},{7,6},{8,9},{9,8},{10,11... | collective-permute-start | bytes 1966088 | tf_op jit(solution)/shard_map/ppermute | solution.py:447
  36.3 9.9 %window_tensor.6 = (f32[3,32,1280]{2,1,0:T(8,128)}, f32[3,32,1280]{2,1,0:T(8,128)}, f32[3,32,1280]{2,1,0:T(8,128)}, f32[3,32,1280]{2,1,0:T(8,128)}, f32[2,16,1280]{2,1,0:T(8,128)}) custom-call(s32[4]{0:T(128)} %pad_add_fusion.refs_0_, f32[2,128,640]{2,1,0:T(8,128)} %get-tuple-element.47.refs_1_, f32[2,128,640]{2,1,0:T(8,128)} %copy-done.7, ...), custom_call_target="tpu_custom_call" | custom-call | flops 10066329600 | bytes 6553600 | tf_op jit(solution)/shard_map/window_tensor/pallas_call | solution.py:395
  46.4 1.7 collective-permute-start.12
  49.0 1.1 add.295.refs_4_
  50.1 1.6 collective-permute-start.3
  51.7 1.9 %add.303.refs_4_ = f32[3,32,1280]{2,1,0:T(8,128)} add(f32[3,32,1280]{2,1,0:T(8,128)S(1)} %copy-done.19, f32[3,32,1280]{2,1,0:T(8,128)} %collective-permute-done.10) | non-fusion elementwise | flops 122880 | bytes 1474560 | tf_op jit(solution)/shard_map/add | solution.py:465
  54.5 10.2 %window_tensor.7 = (f32[3,32,1280]{2,1,0:T(8,128)}, f32[3,32,1280]{2,1,0:T(8,128)}, f32[3,32,1280]{2,1,0:T(8,128)}, f32[3,32,1280]{2,1,0:T(8,128)}, f32[2,16,1280]{2,1,0:T(8,128)}) custom-call(s32[4]{0:T(128)} %pad_add_fusion.refs_0_, f32[2,128,640]{2,1,0:T(8,128)} %get-tuple-element.46.refs_1_, f32[2,128,640]{2,1,0:T(8,128)} %copy-done.6, ...), custom_call_target="tpu_custom_call" | custom-call | flops 10066329600 | bytes 6553600 | tf_op jit(solution)/shard_map/window_tensor/pallas_call | solution.py:395
  65.2 1.8 collective-permute-start.6
  66.9 10.0 %window_tensor.8 = (f32[3,32,1280]{2,1,0:T(8,128)}, f32[3,32,1280]{2,1,0:T(8,128)}, f32[3,32,1280]{2,1,0:T(8,128)}, f32[3,32,1280]{2,1,0:T(8,128)}, f32[2,16,1280]{2,1,0:T(8,128)}) custom-call(s32[4]{0:T(128)} %pad_add_fusion.refs_0_, f32[2,128,640]{2,1,0:T(8,128)} %get-tuple-element.57.refs_1_, f32[2,128,640]{2,1,0:T(8,128)} %collective-permute-done.12.refs_2_, ...), custom_call_target="tpu_custom_call" | custom-call | flops 10066329600 | bytes 6553600 | tf_op jit(solution)/shard_map/window_tensor/pallas_call | solution.py:395
  77.5 1.2 dynamic-slice_add_fusion.9
  79.3 1.9 %dynamic-slice_add_fusion.6 = (f32[3,16,1280]{2,1,0:T(8,128)S(1)}, f32[3,16,1280]{2,1,0:T(8,128)}) fusion(f32[3,32,1280]{2,1,0:T(8,128)} %collective-permute-done.11, s32[]{:T(128)S(6)} %select_n.212, f32[3,32,1280]{2,1,0:T(8,128)S(1)} %collective-permute-done.9, f32[3,32,1280]{2,1,0:T(8,128)S(1)} %copy-done.11, s32[]{:T(128)S(6)} %select_n.214), kind=kLoop, calls=%fused_computation.24 | loop fusion | flops 245760 | bytes 1966088 | tf_op jit(solution)/shard_map/add | solution.py:458
  81.2 1.6 collective-permute-start.4
  82.8 1.1 add.335
  84.4 1.9 %add.301.refs_4_ = f32[3,32,1280]{2,1,0:T(8,128)} add(f32[3,32,1280]{2,1,0:T(8,128)S(1)} %copy-done.13, f32[3,32,1280]{2,1,0:T(8,128)} %collective-permute-done.8) | non-fusion elementwise | flops 122880 | bytes 1474560 | tf_op jit(solution)/shard_map/add | solution.py:465
  86.3 1.5 collective-permute-start.18
  87.8 9.8 %window_tensor.9 = (f32[3,32,1280]{2,1,0:T(8,128)}, f32[3,32,1280]{2,1,0:T(8,128)}, f32[3,32,1280]{2,1,0:T(8,128)}, f32[3,32,1280]{2,1,0:T(8,128)}) custom-call(s32[4]{0:T(128)} %pad_add_fusion.refs_0_, f32[2,120,640]{2,1,0:T(8,128)} %get-tuple-element.43.refs_1_, f32[2,120,640]{2,1,0:T(8,128)} %collective-permute-done.6.refs_2_, ...), custom_call_target="tpu_custom_call" | custom-call | flops 9437184000 | bytes 6471680 | tf_op jit(solution)/shard_map/window_tensor/pallas_call | solution.py:395
  98.3 1.0 dynamic-slice_add_fusion.14
  99.3 2.7 %collective-permute-start.13 = (f32[3,8,1280]{2,1,0:T(8,128)S(1)}, f32[3,8,1280]{2,1,0:T(8,128)S(1)}, u32[]{:S(2)}, u32[]{:S(2)}) collective-permute-start(f32[3,8,1280]{2,1,0:T(8,128)S(1)} %dynamic-slice_add_fusion.14), channel_id=1, source_target_pairs={{0,16},{2,18},{4,20},{6,22},{8,24},{10,26},{12,28},{14,30},{16,0},... | collective-permute-start | bytes 368648 | tf_op jit(solution)/shard_map/ppermute | solution.py:461
  102.0 1.0 dynamic-slice_add_fusion.13
  103.0 2.5 %collective-permute-done.13 = f32[3,8,1280]{2,1,0:T(8,128)S(1)} collective-permute-done((f32[3,8,1280]{2,1,0:T(8,128)S(1)}, f32[3,8,1280]{2,1,0:T(8,128)S(1)}, u32[]{:S(2)}, u32[]{:S(2)}) %collective-permute-start.13) | collective-permute-done | bytes 122912 | tf_op jit(solution)/shard_map/ppermute | solution.py:461
  105.5 3.4 %collective-permute-start.15 = (f32[3,8,1280]{2,1,0:T(8,128)S(1)}, f32[3,8,1280]{2,1,0:T(8,128)S(1)}, u32[]{:S(2)}, u32[]{:S(2)}) collective-permute-start(f32[3,8,1280]{2,1,0:T(8,128)S(1)} %dynamic-slice_add_fusion.13), channel_id=1, source_target_pairs={{0,16},{2,18},{4,20},{6,22},{8,24},{10,26},{12,28},{14,30},{16,0},... | collective-permute-start | bytes 368648 | tf_op jit(solution)/shard_map/ppermute | solution.py:461
  108.9 3.2 %collective-permute-done.15 = f32[3,8,1280]{2,1,0:T(8,128)S(1)} collective-permute-done((f32[3,8,1280]{2,1,0:T(8,128)S(1)}, f32[3,8,1280]{2,1,0:T(8,128)S(1)}, u32[]{:S(2)}, u32[]{:S(2)}) %collective-permute-start.15) | collective-permute-done | bytes 122912 | tf_op jit(solution)/shard_map/ppermute | solution.py:461
  112.1 0.9 add_multiply_fusion.3
  113.8 1.2 dynamic-slice_add_fusion.5
  115.0 3.5 %collective-permute-start.19 = (f32[3,16,1280]{2,1,0:T(8,128)S(1)}, f32[3,16,1280]{2,1,0:T(8,128)S(1)}, u32[]{:S(2)}, u32[]{:S(2)}) collective-permute-start(f32[3,16,1280]{2,1,0:T(8,128)S(1)} %get-tuple-element.84), channel_id=1, source_target_pairs={{0,8},{2,6},{4,12},{6,2},{8,0},{10,14},{12,4},{14,10},{16,24},{18,... | collective-permute-start | bytes 737288 | tf_op jit(solution)/shard_map/ppermute | solution.py:461
  118.5 1.2 dynamic-slice_add_fusion.3
  120.1 1.9 %collective-permute-start.33 = (f32[3,32,1280]{2,1,0:T(8,128)S(1)}, f32[3,32,1280]{2,1,0:T(8,128)S(1)}, u32[]{:S(2)}, u32[]{:S(2)}) collective-permute-start(f32[3,32,1280]{2,1,0:T(8,128)S(1)} %add.347), channel_id=1, source_target_pairs={{0,4},{2,10},{4,0},{6,14},{8,12},{10,2},{12,8},{14,6},{16,20},{18,... | collective-permute-start | bytes 1474568 | tf_op jit(solution)/shard_map/ppermute | solution.py:466
  122.8 3.4 %collective-permute-start.20 = (f32[3,8,1280]{2,1,0:T(8,128)S(1)}, f32[3,8,1280]{2,1,0:T(8,128)S(1)}, u32[]{:S(2)}, u32[]{:S(2)}) collective-permute-start(f32[3,8,1280]{2,1,0:T(8,128)S(1)} %dynamic-slice_add_fusion.12), channel_id=1, source_target_pairs={{0,16},{2,18},{4,20},{6,22},{8,24},{10,26},{12,28},{14,30},{16,0},... | collective-permute-start | bytes 368648 | tf_op jit(solution)/shard_map/ppermute | solution.py:461
  126.2 6.2 %collective-permute-done.29 = f32[3,16,1280]{2,1,0:T(8,128)S(1)} collective-permute-done((f32[3,16,1280]{2,1,0:T(8,128)S(1)}, f32[3,16,1280]{2,1,0:T(8,128)S(1)}, u32[]{:S(2)}, u32[]{:S(2)}) %collective-permute-start.29) | collective-permute-done | bytes 245792 | tf_op jit(solution)/shard_map/ppermute | solution.py:461
  132.5 2.2 %collective-permute-start.30 = (f32[3,8,1280]{2,1,0:T(8,128)S(1)}, f32[3,8,1280]{2,1,0:T(8,128)S(1)}, u32[]{:S(2)}, u32[]{:S(2)}) collective-permute-start(f32[3,8,1280]{2,1,0:T(8,128)S(1)} %dynamic-slice_add_fusion.11), channel_id=1, source_target_pairs={{0,16},{2,18},{4,20},{6,22},{8,24},{10,26},{12,28},{14,30},{16,0},... | collective-permute-start | bytes 368648 | tf_op jit(solution)/shard_map/ppermute | solution.py:461
  135.7 4.2 %collective-permute-done.30 = f32[3,8,1280]{2,1,0:T(8,128)S(1)} collective-permute-done((f32[3,8,1280]{2,1,0:T(8,128)S(1)}, f32[3,8,1280]{2,1,0:T(8,128)S(1)}, u32[]{:S(2)}, u32[]{:S(2)}) %collective-permute-start.30) | collective-permute-done | bytes 122912 | tf_op jit(solution)/shard_map/ppermute | solution.py:461
  140.5 3.0 %collective-permute-start.22 = (f32[3,8,1280]{2,1,0:T(8,128)S(1)}, f32[3,8,1280]{2,1,0:T(8,128)S(1)}, u32[]{:S(2)}, u32[]{:S(2)}) collective-permute-start(f32[3,8,1280]{2,1,0:T(8,128)S(1)} %pad_maximum_fusion), channel_id=1, source_target_pairs={{0,16},{2,18},{4,20},{6,22},{8,24},{10,26},{12,28},{14,30},{16,0},... | collective-permute-start | bytes 368648 | tf_op jit(solution)/shard_map/ppermute | solution.py:472
  143.6 4.8 %collective-permute-done.34 = f32[3,16,1280]{2,1,0:T(8,128)S(1)} collective-permute-done((f32[3,16,1280]{2,1,0:T(8,128)S(1)}, f32[3,16,1280]{2,1,0:T(8,128)S(1)}, u32[]{:S(2)}, u32[]{:S(2)}) %collective-permute-start.34) | collective-permute-done | bytes 245792 | tf_op jit(solution)/shard_map/ppermute | solution.py:461
  148.7 3.0 %collective-permute-done.22 = f32[3,8,1280]{2,1,0:T(8,128)S(1)} collective-permute-done((f32[3,8,1280]{2,1,0:T(8,128)S(1)}, f32[3,8,1280]{2,1,0:T(8,128)S(1)}, u32[]{:S(2)}, u32[]{:S(2)}) %collective-permute-start.22) | collective-permute-done | bytes 122912 | tf_op jit(solution)/shard_map/ppermute | solution.py:472
  151.8 3.8 %collective-permute-done.35 = f32[3,8,1280]{2,1,0:T(8,128)S(1)} collective-permute-done((f32[3,8,1280]{2,1,0:T(8,128)S(1)}, f32[3,8,1280]{2,1,0:T(8,128)S(1)}, u32[]{:S(2)}, u32[]{:S(2)}) %collective-permute-start.35) | collective-permute-done | bytes 122912 | tf_op jit(solution)/shard_map/ppermute | solution.py:461
  155.8 2.4 %collective-permute-done.23 = f32[3,16,1280]{2,1,0:T(8,128)S(1)} collective-permute-done((f32[3,16,1280]{2,1,0:T(8,128)S(1)}, f32[3,16,1280]{2,1,0:T(8,128)S(1)}, u32[]{:S(2)}, u32[]{:S(2)}) %collective-permute-start.23) | collective-permute-done | bytes 245792 | tf_op jit(solution)/shard_map/ppermute | solution.py:472
  158.3 1.5 collective-permute-start.24
  159.8 2.2 %collective-permute-done.36 = f32[2,8,1280]{2,1,0:T(8,128)S(1)} collective-permute-done((f32[2,8,1280]{2,1,0:T(8,128)S(1)}, f32[2,8,1280]{2,1,0:T(8,128)S(1)}, u32[]{:S(2)}, u32[]{:S(2)}) %collective-permute-start.36) | collective-permute-done | bytes 81952 | tf_op jit(solution)/shard_map/ppermute | solution.py:472
  162.1 6.4 %collective-permute-done.37 = f32[2,16,1280]{2,1,0:T(8,128)S(1)} collective-permute-done((f32[2,16,1280]{2,1,0:T(8,128)S(1)}, f32[2,16,1280]{2,1,0:T(8,128)S(1)}, u32[]{:S(2)}, u32[]{:S(2)}) %collective-permute-start.37) | collective-permute-done | bytes 163872 | tf_op jit(solution)/shard_map/ppermute | solution.py:472
  169.1 6.5 %collective-permute-done.38 = f32[2,32,1280]{2,1,0:T(8,128)S(1)} collective-permute-done((f32[2,32,1280]{2,1,0:T(8,128)S(1)}, f32[2,32,1280]{2,1,0:T(8,128)S(1)}, u32[]{:S(2)}, u32[]{:S(2)}) %collective-permute-start.38) | collective-permute-done | bytes 327712 | tf_op jit(solution)/shard_map/ppermute | solution.py:472
  175.8 2.1 %collective-permute-done.39 = f32[2,64,1280]{2,1,0:T(8,128)S(1)} collective-permute-done((f32[2,64,1280]{2,1,0:T(8,128)S(1)}, f32[2,64,1280]{2,1,0:T(8,128)S(1)}, u32[]{:S(2)}, u32[]{:S(2)}) %collective-permute-start.39) | collective-permute-done | bytes 655392 | tf_op jit(solution)/shard_map/ppermute | solution.py:472
  179.3 1.7 copy-done.1
  (132 shorter events, 14.8 us)
Async XLA Ops:
  2.6 19.6 %collective-permute-start = (f32[2,136,640]{2,1,0:T(8,128)}, f32[2,136,640]{2,1,0:T(8,128)S(1)}, u32[]{:S(2)}, u32[]{:S(2)}) collective-permute-start(f32[2,136,640]{2,1,0:T(8,128)} %pieces_of.4), channel_id=1, source_target_pairs={{0,1},{1,0},{2,3},{3,2},{4,5},{5,4},{6,7},{7,6},{8,9},{9,8},{10,11... | collective-permute-start | bytes 2088968 | tf_op jit(solution)/shard_map/ppermute | solution.py:443
  9.2 26.3 %collective-permute-start.7 = (f32[2,128,640]{2,1,0:T(8,128)}, f32[2,128,640]{2,1,0:T(8,128)S(1)}, u32[]{:S(2)}, u32[]{:S(2)}) collective-permute-start(f32[2,128,640]{2,1,0:T(8,128)} %get-tuple-element.48), channel_id=1, source_target_pairs={{0,1},{1,0},{2,3},{3,2},{4,5},{5,4},{6,7},{7,6},{8,9},{9,8},{10,11... | collective-permute-start | bytes 1966088 | tf_op jit(solution)/shard_map/ppermute | solution.py:447
  33.3 15.0 %collective-permute-start.2 = (f32[3,32,1280]{2,1,0:T(8,128)}, f32[3,32,1280]{2,1,0:T(8,128)S(1)}, u32[]{:S(2)}, u32[]{:S(2)}) collective-permute-start(f32[3,32,1280]{2,1,0:T(8,128)} %get-tuple-element.42), channel_id=1, source_target_pairs={{0,2},{2,0},{4,6},{6,4},{8,10},{10,8},{12,14},{14,12},{16,18},{18,... | collective-permute-start | bytes 1474568 | tf_op jit(solution)/shard_map/ppermute | solution.py:490
  33.4 20.3 %collective-permute-start.5 = (f32[2,128,640]{2,1,0:T(8,128)}, f32[2,128,640]{2,1,0:T(8,128)S(1)}, u32[]{:S(2)}, u32[]{:S(2)}) collective-permute-start(f32[2,128,640]{2,1,0:T(8,128)} %gated.5), channel_id=1, source_target_pairs={{0,1},{1,0},{2,3},{3,2},{4,5},{5,4},{6,7},{7,6},{8,9},{9,8},{10,11... | collective-permute-start | bytes 1966088 | tf_op jit(solution)/shard_map/ppermute | solution.py:447
  46.2 3.9 %collective-permute-start.10 = (f32[3,32,1280]{2,1,0:T(8,128)}, f32[3,32,1280]{2,1,0:T(8,128)}, u32[]{:S(2)}, u32[]{:S(2)}) collective-permute-start(f32[3,32,1280]{2,1,0:T(8,128)} %get-tuple-element.56), channel_id=1, source_target_pairs={{0,2},{2,0},{4,6},{6,4},{8,10},{10,8},{12,14},{14,12},{16,18},{18,... | collective-permute-start | bytes 1474568 | tf_op jit(solution)/shard_map/ppermute | solution.py:490
  46.4 18.7 %collective-permute-start.12 = (f32[2,128,640]{2,1,0:T(8,128)}, f32[2,128,640]{2,1,0:T(8,128)}, u32[]{:S(2)}, u32[]{:S(2)}) collective-permute-start(f32[2,128,640]{2,1,0:T(8,128)} %gated.7), channel_id=1, source_target_pairs={{0,1},{1,0},{2,3},{3,2},{4,5},{5,4},{6,7},{7,6},{8,9},{9,8},{10,11... | collective-permute-start | bytes 1966088 | tf_op jit(solution)/shard_map/ppermute | solution.py:447
  48.1 28.8 %collective-permute-start.1 = (f32[3,32,1280]{2,1,0:T(8,128)}, f32[3,32,1280]{2,1,0:T(8,128)S(1)}, u32[]{:S(2)}, u32[]{:S(2)}) collective-permute-start(f32[3,32,1280]{2,1,0:T(8,128)} %get-tuple-element.40), channel_id=1, source_target_pairs={{0,2},{2,0},{4,6},{6,4},{8,10},{10,8},{12,14},{14,12},{16,18},{18,... | collective-permute-start | bytes 1474568 | tf_op jit(solution)/shard_map/ppermute | solution.py:491
  48.3 30.5 %collective-permute-start.9 = (f32[3,32,1280]{2,1,0:T(8,128)}, f32[3,32,1280]{2,1,0:T(8,128)S(1)}, u32[]{:S(2)}, u32[]{:S(2)}) collective-permute-start(f32[3,32,1280]{2,1,0:T(8,128)} %get-tuple-element.54), channel_id=1, source_target_pairs={{0,2},{2,0},{4,6},{6,4},{8,10},{10,8},{12,14},{14,12},{16,18},{18,... | collective-permute-start | bytes 1474568 | tf_op jit(solution)/shard_map/ppermute | solution.py:491
  50.1 26.8 %collective-permute-start.3 = (f32[3,32,1280]{2,1,0:T(8,128)S(1)}, f32[3,32,1280]{2,1,0:T(8,128)}, u32[]{:S(2)}, u32[]{:S(2)}) collective-permute-start(f32[3,32,1280]{2,1,0:T(8,128)S(1)} %add.295.refs_4_), channel_id=1, source_target_pairs={{0,4},{2,10},{4,0},{6,14},{8,12},{10,2},{12,8},{14,6},{16,20},{18,... | collective-permute-start | bytes 1474568 | tf_op jit(solution)/shard_map/ppermute | solution.py:466
  53.6 25.3 %collective-permute-start.11 = (f32[3,32,1280]{2,1,0:T(8,128)}, f32[3,32,1280]{2,1,0:T(8,128)}, u32[]{:S(2)}, u32[]{:S(2)}) collective-permute-start(f32[3,32,1280]{2,1,0:T(8,128)} %add.303.refs_4_), channel_id=1, source_target_pairs={{0,4},{2,10},{4,0},{6,14},{8,12},{10,2},{12,8},{14,6},{16,20},{18,... | collective-permute-start | bytes 1474568 | tf_op jit(solution)/shard_map/ppermute | solution.py:466
  54.5 10.7 %copy-start.8 = (f32[2,120,640]{2,1,0:T(8,128)S(1)}, f32[2,120,640]{2,1,0:T(8,128)}, u32[]{:S(2)}) copy-start(f32[2,120,640]{2,1,0:T(8,128)} %gated.6) | copy-start | bytes 1843204
  65.2 21.1 %collective-permute-start.6 = (f32[2,120,640]{2,1,0:T(8,128)S(1)}, f32[2,120,640]{2,1,0:T(8,128)}, u32[]{:S(2)}, u32[]{:S(2)}) collective-permute-start(f32[2,120,640]{2,1,0:T(8,128)S(1)} %copy-done.8), channel_id=1, source_target_pairs={{0,1},{1,0},{2,3},{3,2},{4,5},{5,4},{6,7},{7,6},{8,9},{9,8},{10,11... | collective-permute-start | bytes 1843208 | tf_op jit(solution)/shard_map/ppermute | solution.py:447
  66.9 10.6 %copy-start.12 = (f32[3,32,1280]{2,1,0:T(8,128)S(1)}, f32[3,32,1280]{2,1,0:T(8,128)}, u32[]{:S(2)}) copy-start(f32[3,32,1280]{2,1,0:T(8,128)} %get-tuple-element.39) | copy-start | bytes 1474564
  76.9 4.3 %collective-permute-start.27 = (f32[3,32,1280]{2,1,0:T(8,128)}, f32[3,32,1280]{2,1,0:T(8,128)}, u32[]{:S(2)}, u32[]{:S(2)}) collective-permute-start(f32[3,32,1280]{2,1,0:T(8,128)} %get-tuple-element.67), channel_id=1, source_target_pairs={{0,2},{2,0},{4,6},{6,4},{8,10},{10,8},{12,14},{14,12},{16,18},{18,... | collective-permute-start | bytes 1474568 | tf_op jit(solution)/shard_map/ppermute | solution.py:490
  77.0 6.9 %collective-permute-start.8 = (f32[3,32,1280]{2,1,0:T(8,128)}, f32[3,32,1280]{2,1,0:T(8,128)}, u32[]{:S(2)}, u32[]{:S(2)}) collective-permute-start(f32[3,32,1280]{2,1,0:T(8,128)} %get-tuple-element.52), channel_id=1, source_target_pairs={{0,2},{2,0},{4,6},{6,4},{8,10},{10,8},{12,14},{14,12},{16,18},{18,... | collective-permute-start | bytes 1474568 | tf_op jit(solution)/shard_map/ppermute | solution.py:490
  78.7 39.7 %collective-permute-start.26 = (f32[3,32,1280]{2,1,0:T(8,128)}, f32[3,32,1280]{2,1,0:T(8,128)S(1)}, u32[]{:S(2)}, u32[]{:S(2)}) collective-permute-start(f32[3,32,1280]{2,1,0:T(8,128)} %get-tuple-element.65), channel_id=1, source_target_pairs={{0,2},{2,0},{4,6},{6,4},{8,10},{10,8},{12,14},{14,12},{16,18},{18,... | collective-permute-start | bytes 1474568 | tf_op jit(solution)/shard_map/ppermute | solution.py:491
  78.9 34.3 %collective-permute-start.17 = (f32[3,32,1280]{2,1,0:T(8,128)}, f32[3,32,1280]{2,1,0:T(8,128)}, u32[]{:S(2)}, u32[]{:S(2)}) collective-permute-start(f32[3,32,1280]{2,1,0:T(8,128)} %get-tuple-element.63), channel_id=1, source_target_pairs={{0,2},{2,0},{4,6},{6,4},{8,10},{10,8},{12,14},{14,12},{16,18},{18,... | collective-permute-start | bytes 1474568 | tf_op jit(solution)/shard_map/ppermute | solution.py:491
  81.2 16.4 %collective-permute-start.4 = (f32[3,16,1280]{2,1,0:T(8,128)S(1)}, f32[3,16,1280]{2,1,0:T(8,128)S(1)}, u32[]{:S(2)}, u32[]{:S(2)}) collective-permute-start(f32[3,16,1280]{2,1,0:T(8,128)S(1)} %get-tuple-element.80.refs_6_), channel_id=1, source_target_pairs={{0,8},{2,6},{4,12},{6,2},{8,0},{10,14},{12,4},{14,10},{16,24},{18,... | collective-permute-start | bytes 737288 | tf_op jit(solution)/shard_map/ppermute | solution.py:461
  83.9 15.4 %collective-permute-start.14 = (f32[3,16,1280]{2,1,0:T(8,128)}, f32[3,16,1280]{2,1,0:T(8,128)S(1)}, u32[]{:S(2)}, u32[]{:S(2)}) collective-permute-start(f32[3,16,1280]{2,1,0:T(8,128)} %get-tuple-element.82.refs_5_), channel_id=1, source_target_pairs={{0,8},{2,6},{4,12},{6,2},{8,0},{10,14},{12,4},{14,10},{16,24},{18,... | collective-permute-start | bytes 737288 | tf_op jit(solution)/shard_map/ppermute | solution.py:461
  86.3 27.4 %collective-permute-start.18 = (f32[3,32,1280]{2,1,0:T(8,128)}, f32[3,32,1280]{2,1,0:T(8,128)S(1)}, u32[]{:S(2)}, u32[]{:S(2)}) collective-permute-start(f32[3,32,1280]{2,1,0:T(8,128)} %add.301.refs_4_), channel_id=1, source_target_pairs={{0,4},{2,10},{4,0},{6,14},{8,12},{10,2},{12,8},{14,6},{16,20},{18,... | collective-permute-start | bytes 1474568 | tf_op jit(solution)/shard_map/ppermute | solution.py:466
  97.6 20.8 %collective-permute-start.28 = (f32[3,32,1280]{2,1,0:T(8,128)S(1)}, f32[3,32,1280]{2,1,0:T(8,128)}, u32[]{:S(2)}, u32[]{:S(2)}) collective-permute-start(f32[3,32,1280]{2,1,0:T(8,128)S(1)} %add.335), channel_id=1, source_target_pairs={{0,4},{2,10},{4,0},{6,14},{8,12},{10,2},{12,8},{14,6},{16,20},{18,... | collective-permute-start | bytes 1474568 | tf_op jit(solution)/shard_map/ppermute | solution.py:466
  98.3 10.6 %copy-start.4 = (f32[3,16,1280]{2,1,0:T(8,128)S(1)}, f32[3,16,1280]{2,1,0:T(8,128)}, u32[]{:S(2)}) copy-start(f32[3,16,1280]{2,1,0:T(8,128)} %gated.8) | copy-start | bytes 737284
  98.3 15.4 %copy-start.10 = (f32[3,32,1280]{2,1,0:T(8,128)S(1)}, f32[3,32,1280]{2,1,0:T(8,128)}, u32[]{:S(2)}) copy-start(f32[3,32,1280]{2,1,0:T(8,128)} %get-tuple-element.62) | copy-start | bytes 1474564
  99.3 6.2 %collective-permute-start.13 = (f32[3,8,1280]{2,1,0:T(8,128)S(1)}, f32[3,8,1280]{2,1,0:T(8,128)S(1)}, u32[]{:S(2)}, u32[]{:S(2)}) collective-permute-start(f32[3,8,1280]{2,1,0:T(8,128)S(1)} %dynamic-slice_add_fusion.14), channel_id=1, source_target_pairs={{0,16},{2,18},{4,20},{6,22},{8,24},{10,26},{12,28},{14,30},{16,0},... | collective-permute-start | bytes 368648 | tf_op jit(solution)/shard_map/ppermute | solution.py:461
  102.0 11.2 %copy-start.21 = (f32[3,32,1280]{2,1,0:T(8,128)S(1)}, f32[3,32,1280]{2,1,0:T(8,128)}, u32[]{:S(2)}) copy-start(f32[3,32,1280]{2,1,0:T(8,128)} %get-tuple-element.68) | copy-start | bytes 1474564
  103.0 15.5 %copy-start.9 = (f32[3,32,1280]{2,1,0:T(8,128)S(1)}, f32[3,32,1280]{2,1,0:T(8,128)}, u32[]{:S(2)}) copy-start(f32[3,32,1280]{2,1,0:T(8,128)} %get-tuple-element.64) | copy-start | bytes 1474564
  105.5 6.7 %collective-permute-start.15 = (f32[3,8,1280]{2,1,0:T(8,128)S(1)}, f32[3,8,1280]{2,1,0:T(8,128)S(1)}, u32[]{:S(2)}, u32[]{:S(2)}) collective-permute-start(f32[3,8,1280]{2,1,0:T(8,128)S(1)} %dynamic-slice_add_fusion.13), channel_id=1, source_target_pairs={{0,16},{2,18},{4,20},{6,22},{8,24},{10,26},{12,28},{14,30},{16,0},... | collective-permute-start | bytes 368648 | tf_op jit(solution)/shard_map/ppermute | solution.py:461
  112.1 7.9 %collective-permute-start.32 = (f32[3,32,1280]{2,1,0:T(8,128)}, f32[3,32,1280]{2,1,0:T(8,128)S(1)}, u32[]{:S(2)}, u32[]{:S(2)}) collective-permute-start(f32[3,32,1280]{2,1,0:T(8,128)} %get-tuple-element.70), channel_id=1, source_target_pairs={{0,2},{2,0},{4,6},{6,4},{8,10},{10,8},{12,14},{14,12},{16,18},{18,... | collective-permute-start | bytes 1474568 | tf_op jit(solution)/shard_map/ppermute | solution.py:490
  113.2 26.7 %collective-permute-start.31 = (f32[3,32,1280]{2,1,0:T(8,128)S(1)}, f32[3,32,1280]{2,1,0:T(8,128)S(1)}, u32[]{:S(2)}, u32[]{:S(2)}) collective-permute-start(f32[3,32,1280]{2,1,0:T(8,128)S(1)} %copy-done.21), channel_id=1, source_target_pairs={{0,2},{2,0},{4,6},{6,4},{8,10},{10,8},{12,14},{14,12},{16,18},{18,... | collective-permute-start | bytes 1474568 | tf_op jit(solution)/shard_map/ppermute | solution.py:491
  113.8 6.3 %copy-start.15 = (f32[3,32,1280]{2,1,0:T(8,128)S(1)}, f32[3,32,1280]{2,1,0:T(8,128)}, u32[]{:S(2)}) copy-start(f32[3,32,1280]{2,1,0:T(8,128)} %get-tuple-element.69) | copy-start | bytes 1474564
  115.0 7.8 %collective-permute-start.19 = (f32[3,16,1280]{2,1,0:T(8,128)S(1)}, f32[3,16,1280]{2,1,0:T(8,128)S(1)}, u32[]{:S(2)}, u32[]{:S(2)}) collective-permute-start(f32[3,16,1280]{2,1,0:T(8,128)S(1)} %get-tuple-element.84), channel_id=1, source_target_pairs={{0,8},{2,6},{4,12},{6,2},{8,0},{10,14},{12,4},{14,10},{16,24},{18,... | collective-permute-start | bytes 737288 | tf_op jit(solution)/shard_map/ppermute | solution.py:461
  119.6 12.8 %collective-permute-start.29 = (f32[3,16,1280]{2,1,0:T(8,128)S(1)}, f32[3,16,1280]{2,1,0:T(8,128)S(1)}, u32[]{:S(2)}, u32[]{:S(2)}) collective-permute-start(f32[3,16,1280]{2,1,0:T(8,128)S(1)} %get-tuple-element.76), channel_id=1, source_target_pairs={{0,8},{2,6},{4,12},{6,2},{8,0},{10,14},{12,4},{14,10},{16,24},{18,... | collective-permute-start | bytes 737288 | tf_op jit(solution)/shard_map/ppermute | solution.py:461
  119.7 20.8 %collective-permute-start.16 = (f32[2,8,1280]{2,1,0:T(8,128)S(1)}, f32[2,8,1280]{2,1,0:T(8,128)S(1)}, u32[]{:S(2)}, u32[]{:S(2)}) collective-permute-start(f32[2,8,1280]{2,1,0:T(8,128)S(1)} %pad_maximum_fusion.1), channel_id=1, source_target_pairs={{0,1},{1,0},{2,3},{3,2},{4,5},{5,4},{6,7},{7,6},{8,9},{9,8},{10,11... | collective-permute-start | bytes 245768 | tf_op jit(solution)/shard_map/ppermute | solution.py:502
  120.1 19.9 %copy-start = (f32[3,32,1280]{2,1,0:T(8,128)S(1)}, f32[3,32,1280]{2,1,0:T(8,128)}, u32[]{:S(2)}) copy-start(f32[3,32,1280]{2,1,0:T(8,128)} %get-tuple-element.61.refs_1_) | copy-start | bytes 1474564
  120.1 19.8 %collective-permute-start.33 = (f32[3,32,1280]{2,1,0:T(8,128)S(1)}, f32[3,32,1280]{2,1,0:T(8,128)S(1)}, u32[]{:S(2)}, u32[]{:S(2)}) collective-permute-start(f32[3,32,1280]{2,1,0:T(8,128)S(1)} %add.347), channel_id=1, source_target_pairs={{0,4},{2,10},{4,0},{6,14},{8,12},{10,2},{12,8},{14,6},{16,20},{18,... | collective-permute-start | bytes 1474568 | tf_op jit(solution)/shard_map/ppermute | solution.py:466
  122.8 11.9 %collective-permute-start.20 = (f32[3,8,1280]{2,1,0:T(8,128)S(1)}, f32[3,8,1280]{2,1,0:T(8,128)S(1)}, u32[]{:S(2)}, u32[]{:S(2)}) collective-permute-start(f32[3,8,1280]{2,1,0:T(8,128)S(1)} %dynamic-slice_add_fusion.12), channel_id=1, source_target_pairs={{0,16},{2,18},{4,20},{6,22},{8,24},{10,26},{12,28},{14,30},{16,0},... | collective-permute-start | bytes 368648 | tf_op jit(solution)/shard_map/ppermute | solution.py:461
  132.5 7.4 %collective-permute-start.30 = (f32[3,8,1280]{2,1,0:T(8,128)S(1)}, f32[3,8,1280]{2,1,0:T(8,128)S(1)}, u32[]{:S(2)}, u32[]{:S(2)}) collective-permute-start(f32[3,8,1280]{2,1,0:T(8,128)S(1)} %dynamic-slice_add_fusion.11), channel_id=1, source_target_pairs={{0,16},{2,18},{4,20},{6,22},{8,24},{10,26},{12,28},{14,30},{16,0},... | collective-permute-start | bytes 368648 | tf_op jit(solution)/shard_map/ppermute | solution.py:461
  134.7 5.8 %collective-permute-start.21 = (f32[8,1280]{1,0:T(8,128)S(1)}, f32[8,1280]{1,0:T(8,128)S(1)}, u32[]{:S(2)}, u32[]{:S(2)}) collective-permute-start(f32[8,1280]{1,0:T(8,128)S(1)} %fusion.18), channel_id=1, source_target_pairs={{0,0},{1,2},{2,1},{3,3},{4,4},{5,10},{6,9},{7,7},{8,8},{9,6},{10,5... | collective-permute-start | bytes 122888 | tf_op jit(solution)/shard_map/ppermute | solution.py:513
  140.0 8.3 %collective-permute-start.34 = (f32[3,16,1280]{2,1,0:T(8,128)S(1)}, f32[3,16,1280]{2,1,0:T(8,128)S(1)}, u32[]{:S(2)}, u32[]{:S(2)}) collective-permute-start(f32[3,16,1280]{2,1,0:T(8,128)S(1)} %get-tuple-element.78), channel_id=1, source_target_pairs={{0,8},{2,6},{4,12},{6,2},{8,0},{10,14},{12,4},{14,10},{16,24},{18,... | collective-permute-start | bytes 737288 | tf_op jit(solution)/shard_map/ppermute | solution.py:461
  140.5 11.2 %collective-permute-start.22 = (f32[3,8,1280]{2,1,0:T(8,128)S(1)}, f32[3,8,1280]{2,1,0:T(8,128)S(1)}, u32[]{:S(2)}, u32[]{:S(2)}) collective-permute-start(f32[3,8,1280]{2,1,0:T(8,128)S(1)} %pad_maximum_fusion), channel_id=1, source_target_pairs={{0,16},{2,18},{4,20},{6,22},{8,24},{10,26},{12,28},{14,30},{16,0},... | collective-permute-start | bytes 368648 | tf_op jit(solution)/shard_map/ppermute | solution.py:472
  148.4 7.2 %collective-permute-start.35 = (f32[3,8,1280]{2,1,0:T(8,128)S(1)}, f32[3,8,1280]{2,1,0:T(8,128)S(1)}, u32[]{:S(2)}, u32[]{:S(2)}) collective-permute-start(f32[3,8,1280]{2,1,0:T(8,128)S(1)} %dynamic-slice_add_fusion.10), channel_id=1, source_target_pairs={{0,16},{2,18},{4,20},{6,22},{8,24},{10,26},{12,28},{14,30},{16,0},... | collective-permute-start | bytes 368648 | tf_op jit(solution)/shard_map/ppermute | solution.py:461
  151.8 6.5 %collective-permute-start.23 = (f32[3,16,1280]{2,1,0:T(8,128)S(1)}, f32[3,16,1280]{2,1,0:T(8,128)S(1)}, u32[]{:S(2)}, u32[]{:S(2)}) collective-permute-start(f32[3,16,1280]{2,1,0:T(8,128)S(1)} %maximum_select_fusion.7), channel_id=1, source_target_pairs={{0,8},{2,6},{4,12},{6,2},{8,0},{10,14},{12,4},{14,10},{16,24},{18,... | collective-permute-start | bytes 737288 | tf_op jit(solution)/shard_map/ppermute | solution.py:472
  155.7 6.3 %collective-permute-start.36 = (f32[2,8,1280]{2,1,0:T(8,128)S(1)}, f32[2,8,1280]{2,1,0:T(8,128)S(1)}, u32[]{:S(2)}, u32[]{:S(2)}) collective-permute-start(f32[2,8,1280]{2,1,0:T(8,128)S(1)} %pad_maximum_fusion.2), channel_id=1, source_target_pairs={{0,16},{2,18},{4,20},{6,22},{8,24},{10,26},{12,28},{14,30},{16,0},... | collective-permute-start | bytes 245768 | tf_op jit(solution)/shard_map/ppermute | solution.py:472
  158.3 10.7 %collective-permute-start.24 = (f32[3,32,1280]{2,1,0:T(8,128)S(1)}, f32[3,32,1280]{2,1,0:T(8,128)S(1)}, u32[]{:S(2)}, u32[]{:S(2)}) collective-permute-start(f32[3,32,1280]{2,1,0:T(8,128)S(1)} %maximum_select_fusion.5), channel_id=1, source_target_pairs={{0,4},{2,10},{4,0},{6,14},{8,12},{10,2},{12,8},{14,6},{16,20},{18,... | collective-permute-start | bytes 1474568 | tf_op jit(solution)/shard_map/ppermute | solution.py:472
  162.0 6.5 %collective-permute-start.37 = (f32[2,16,1280]{2,1,0:T(8,128)S(1)}, f32[2,16,1280]{2,1,0:T(8,128)S(1)}, u32[]{:S(2)}, u32[]{:S(2)}) collective-permute-start(f32[2,16,1280]{2,1,0:T(8,128)S(1)} %maximum_select_fusion.8), channel_id=1, source_target_pairs={{0,8},{2,6},{4,12},{6,2},{8,0},{10,14},{12,4},{14,10},{16,24},{18,... | collective-permute-start | bytes 491528 | tf_op jit(solution)/shard_map/ppermute | solution.py:472
  168.5 7.1 %collective-permute-start.38 = (f32[2,32,1280]{2,1,0:T(8,128)S(1)}, f32[2,32,1280]{2,1,0:T(8,128)S(1)}, u32[]{:S(2)}, u32[]{:S(2)}) collective-permute-start(f32[2,32,1280]{2,1,0:T(8,128)S(1)} %maximum_select_fusion.6), channel_id=1, source_target_pairs={{0,4},{2,10},{4,0},{6,14},{8,12},{10,2},{12,8},{14,6},{16,20},{18,... | collective-permute-start | bytes 983048 | tf_op jit(solution)/shard_map/ppermute | solution.py:472
  169.1 8.9 %collective-permute-start.25 = (f32[3,64,1280]{2,1,0:T(8,128)S(1)}, f32[3,64,1280]{2,1,0:T(8,128)S(1)}, u32[]{:S(2)}, u32[]{:S(2)}) collective-permute-start(f32[3,64,1280]{2,1,0:T(8,128)S(1)} %maximum_select_fusion.3), channel_id=1, source_target_pairs={{0,2},{2,0},{4,6},{6,4},{8,10},{10,8},{12,14},{14,12},{16,18},{18,... | collective-permute-start | bytes 2949128 | tf_op jit(solution)/shard_map/ppermute | solution.py:472
  175.7 2.2 %collective-permute-start.39 = (f32[2,64,1280]{2,1,0:T(8,128)S(1)}, f32[2,64,1280]{2,1,0:T(8,128)S(1)}, u32[]{:S(2)}, u32[]{:S(2)}) collective-permute-start(f32[2,64,1280]{2,1,0:T(8,128)S(1)} %maximum_select_fusion.4), channel_id=1, source_target_pairs={{0,2},{2,0},{4,6},{6,4},{8,10},{10,8},{12,14},{14,12},{16,18},{18,... | collective-permute-start | bytes 1966088 | tf_op jit(solution)/shard_map/ppermute | solution.py:472
  (14 other events, 38.9 us)

commit v24 on v21

--- a/solution.py
+++ b/solution.py
@@ -519,7 +519,9 @@
     up = jnp.stack([jnp.concatenate([low, *other[::-1]]), jnp.concatenate([high, rest])])
     out = jnp.where(band == 0, down, up)
 
-    own = gathered(jnp.stack(pieces["own"]))
+    own = jnp.stack(pieces["own"])
+    for step in range(len(ways) - 1, -2, -1):
+        own = doubled(gated(own, [out]) if step < 0 else own, step)
     for k, block in enumerate(own):
         width = block.shape[0]
         row = choose(band, (nlat // 2 - middle - (k + 1) * width, middle + k * width))

time: 177 us -> 185 us (1.045)
  other arithmetic: 8.5 us -> 14.7 us
    select_n x8, other arithmetic: 0.48 us -> 2.71 us  [doubled(): jnp.where(mine == 0, jnp.concatenate([part, beside], axis=1), jnp.concate...]
  transfers between devices with their start and end apart: 40 -> 40, of which waited for: 13 -> 14; matrix products, arithmetic and copies ran while one was open for 4% -> 6% of each run, Pallas kernels for 33% -> 31%
where the time goes in v24:
time: 185 us; the launch traced here: 184 us
  waiting for transfers between devices  65.9 us (36%)
  Pallas kernels  60.1 us (32%)
  starting transfers between devices  38.3 us (21%)
  other arithmetic  14.7 us (8%)
  local copies, waits for them, and re-layouts  4.46 us (2%)
    pallas_call x5, Pallas kernels, window_tensor(): pl.pallas_call(functools.partial(window_kernel, window, len(waits)), out_...  49.9 us
    ppermute x10, waiting for transfers between devices, halved(): return ([total(mine), lax.ppermute(leaves, 'mem', ways[step])], leaves)  35.5 us
    ppermute x8, waiting for transfers between devices, doubled(): beside = lax.ppermute(part, 'mem', cores if step < 0 else ways[step])  21.9 us
    pallas_call x3, Pallas kernels, pieces_of(): pl.pallas_call(functools.partial(pieces_kernel, windows, slots, count), i...  10.2 us
    ppermute x10, starting transfers between devices, halved(): return ([total(mine), lax.ppermute(leaves, 'mem', ways[step])], leaves)  9.5 us
    ppermute x8, starting transfers between devices, doubled(): beside = lax.ppermute(part, 'mem', cores if step < 0 else ways[step])  9.5 us
    ppermute x1, waiting for transfers between devices, by_levels(): remotes = [lax.ppermute(piece, 'band', swap)]  8.25 us
    ppermute x4, starting transfers between devices, by_levels(): remotes.append(lax.ppermute(piece, 'band', swap))  5.46 us
  transfers between devices with their start and end apart: 40, of which 14 were waited for; matrix products, arithmetic and copies ran while one was open for 6% of the time, Pallas kernels for 31%

profile of v24, /device:TPU:0, one launch (start us, length us, event | category | flops | bytes accessed | tf_op | source)
XLA Modules:
  0.0 184.2 jit_solution(1588315661729566297)
XLA Ops:
  0.0 2.6 %pieces_of.4 = f32[2,136,640]{2,1,0:T(8,128)} custom-call(s32[1]{0:T(128)} %bitcast.5.level_ref, f32[2,2,640,640]{3,2,1,0:T(8,128)} %bitcast.25), custom_call_target="tpu_custom_call" | custom-call | bytes 5242880 | tf_op jit(solution)/shard_map/pieces_of/pallas_call | solution.py:209
  2.6 3.0 %collective-permute-start = (f32[2,136,640]{2,1,0:T(8,128)}, f32[2,136,640]{2,1,0:T(8,128)S(1)}, u32[]{:S(2)}, u32[]{:S(2)}) collective-permute-start(f32[2,136,640]{2,1,0:T(8,128)} %pieces_of.4), channel_id=1, source_target_pairs={{0,1},{1,0},{2,3},{3,2},{4,5},{5,4},{6,7},{7,6},{8,9},{9,8},{10,11... | collective-permute-start | bytes 2088968 | tf_op jit(solution)/shard_map/ppermute | solution.py:443
  5.6 3.6 %pieces_of.5 = (f32[2,128,640]{2,1,0:T(8,128)}, f32[2,128,640]{2,1,0:T(8,128)}, f32[2,128,640]{2,1,0:T(8,128)}, f32[2,120,640]{2,1,0:T(8,128)}) custom-call(s32[1]{0:T(128)} %bitcast.5.level_ref, f32[2,2,640,640]{3,2,1,0:T(8,128)} %bitcast.26), custom_call_target="tpu_custom_call" | custom-call | bytes 10485760 | tf_op jit(solution)/shard_map/pieces_of/pallas_call | solution.py:209
  9.4 4.0 %pieces_of.3 = (f32[2,136,640]{2,1,0:T(8,128)}, f32[2,128,640]{2,1,0:T(8,128)}, f32[2,128,640]{2,1,0:T(8,128)}, f32[2,128,640]{2,1,0:T(8,128)}, f32[2,120,640]{2,1,0:T(8,128)}) custom-call(s32[1]{0:T(128)} %bitcast.level_ref, f32[2,2,640,640]{3,2,1,0:T(8,128)} %bitcast.27), custom_call_target="tpu_custom_call" | custom-call | bytes 13107200 | tf_op jit(solution)/shard_map/pieces_of/pallas_call | solution.py:209
  14.0 8.2 %collective-permute-done.refs_2_.refs_1_ = f32[2,136,640]{2,1,0:T(8,128)S(1)} collective-permute-done((f32[2,136,640]{2,1,0:T(8,128)}, f32[2,136,640]{2,1,0:T(8,128)S(1)}, u32[]{:S(2)}, u32[]{:S(2)}) %collective-permute-start) | collective-permute-done | bytes 696352 | tf_op jit(solution)/shard_map/ppermute | solution.py:443
  22.2 0.9 copy-done
  23.1 10.2 %window_tensor.5 = (f32[3,32,1280]{2,1,0:T(8,128)}, f32[3,32,1280]{2,1,0:T(8,128)}, f32[3,32,1280]{2,1,0:T(8,128)}, f32[3,32,1280]{2,1,0:T(8,128)}, f32[2,16,1280]{2,1,0:T(8,128)}) custom-call(s32[4]{0:T(128)} %pad_add_fusion.refs_0_, f32[2,136,640]{2,1,0:T(8,128)} %get-tuple-element.38.refs_1_, f32[2,136,640]{2,1,0:T(8,128)} %copy-done, ...), custom_call_target="tpu_custom_call" | custom-call | flops 10695475200 | bytes 6635520 | tf_op jit(solution)/shard_map/window_tensor/pallas_call | solution.py:395
  33.4 2.1 %collective-permute-start.13 = (f32[2,128,640]{2,1,0:T(8,128)}, f32[2,128,640]{2,1,0:T(8,128)S(1)}, u32[]{:S(2)}, u32[]{:S(2)}) collective-permute-start(f32[2,128,640]{2,1,0:T(8,128)} %gated.4), channel_id=1, source_target_pairs={{0,1},{1,0},{2,3},{3,2},{4,5},{5,4},{6,7},{7,6},{8,9},{9,8},{10,11... | collective-permute-start | bytes 1966088 | tf_op jit(solution)/shard_map/ppermute | solution.py:447
  36.4 9.8 %window_tensor.6 = (f32[3,32,1280]{2,1,0:T(8,128)}, f32[3,32,1280]{2,1,0:T(8,128)}, f32[3,32,1280]{2,1,0:T(8,128)}, f32[3,32,1280]{2,1,0:T(8,128)}, f32[2,16,1280]{2,1,0:T(8,128)}) custom-call(s32[4]{0:T(128)} %pad_add_fusion.refs_0_, f32[2,128,640]{2,1,0:T(8,128)} %get-tuple-element.43.refs_1_, f32[2,128,640]{2,1,0:T(8,128)} %copy-done.2, ...), custom_call_target="tpu_custom_call" | custom-call | flops 10066329600 | bytes 6553600 | tf_op jit(solution)/shard_map/window_tensor/pallas_call | solution.py:395
  46.4 1.7 collective-permute-start.24
  49.5 1.5 collective-permute-start.3
  51.3 2.0 %collective-permute-start.9 = (f32[3,32,1280]{2,1,0:T(8,128)S(1)}, f32[3,32,1280]{2,1,0:T(8,128)S(1)}, u32[]{:S(2)}, u32[]{:S(2)}) collective-permute-start(f32[3,32,1280]{2,1,0:T(8,128)S(1)} %add.310.refs_4_), channel_id=1, source_target_pairs={{0,4},{2,10},{4,0},{6,14},{8,12},{10,2},{12,8},{14,6},{16,20},{18,... | collective-permute-start | bytes 1474568 | tf_op jit(solution)/shard_map/ppermute | solution.py:466
  53.3 10.1 %window_tensor.7 = (f32[3,32,1280]{2,1,0:T(8,128)}, f32[3,32,1280]{2,1,0:T(8,128)}, f32[3,32,1280]{2,1,0:T(8,128)}, f32[3,32,1280]{2,1,0:T(8,128)}, f32[2,16,1280]{2,1,0:T(8,128)}) custom-call(s32[4]{0:T(128)} %pad_add_fusion.refs_0_, f32[2,128,640]{2,1,0:T(8,128)} %get-tuple-element.50.refs_1_, f32[2,128,640]{2,1,0:T(8,128)} %copy-done.1, ...), custom_call_target="tpu_custom_call" | custom-call | flops 10066329600 | bytes 6553600 | tf_op jit(solution)/shard_map/window_tensor/pallas_call | solution.py:395
  63.5 1.6 collective-permute-start.30
  65.1 1.8 dynamic-slice_add_fusion.9
  67.1 1.6 collective-permute-start.4
  68.7 1.1 dynamic-slice_add_fusion.7
  70.4 9.9 %window_tensor.8 = (f32[3,32,1280]{2,1,0:T(8,128)}, f32[3,32,1280]{2,1,0:T(8,128)}, f32[3,32,1280]{2,1,0:T(8,128)}, f32[3,32,1280]{2,1,0:T(8,128)}, f32[2,16,1280]{2,1,0:T(8,128)}) custom-call(s32[4]{0:T(128)} %pad_add_fusion.refs_0_, f32[2,128,640]{2,1,0:T(8,128)} %get-tuple-element.57.refs_1_, f32[2,128,640]{2,1,0:T(8,128)} %collective-permute-done.24.refs_2_, ...), custom_call_target="tpu_custom_call" | custom-call | flops 10066329600 | bytes 6553600 | tf_op jit(solution)/shard_map/window_tensor/pallas_call | solution.py:395
  81.1 1.1 add.322.refs_4_
  85.0 2.6 %collective-permute-start.5 = (f32[3,8,1280]{2,1,0:T(8,128)}, f32[3,8,1280]{2,1,0:T(8,128)}, u32[]{:S(2)}, u32[]{:S(2)}) collective-permute-start(f32[3,8,1280]{2,1,0:T(8,128)} %dynamic-slice_add_fusion.14.refs_6_), channel_id=1, source_target_pairs={{0,16},{2,18},{4,20},{6,22},{8,24},{10,26},{12,28},{14,30},{16,0},... | collective-permute-start | bytes 368648 | tf_op jit(solution)/shard_map/ppermute | solution.py:461
  87.5 9.9 %window_tensor.9 = (f32[3,32,1280]{2,1,0:T(8,128)}, f32[3,32,1280]{2,1,0:T(8,128)}, f32[3,32,1280]{2,1,0:T(8,128)}, f32[3,32,1280]{2,1,0:T(8,128)}) custom-call(s32[4]{0:T(128)} %pad_add_fusion.refs_0_, f32[2,120,640]{2,1,0:T(8,128)} %get-tuple-element.64.refs_1_, f32[2,120,640]{2,1,0:T(8,128)} %collective-permute-done.30.refs_2_, ...), custom_call_target="tpu_custom_call" | custom-call | flops 9437184000 | bytes 6471680 | tf_op jit(solution)/shard_map/window_tensor/pallas_call | solution.py:395
  97.9 0.9 add_multiply_fusion.4
  98.8 7.8 %collective-permute-done.11 = f32[3,8,1280]{2,1,0:T(8,128)S(1)} collective-permute-done((f32[3,8,1280]{2,1,0:T(8,128)}, f32[3,8,1280]{2,1,0:T(8,128)S(1)}, u32[]{:S(2)}, u32[]{:S(2)}) %collective-permute-start.11) | collective-permute-done | bytes 122912 | tf_op jit(solution)/shard_map/ppermute | solution.py:461
  106.7 0.9 add_multiply_fusion.3
  107.8 6.1 %collective-permute-done.17 = f32[3,16,1280]{2,1,0:T(8,128)S(1)} collective-permute-done((f32[3,16,1280]{2,1,0:T(8,128)S(1)}, f32[3,16,1280]{2,1,0:T(8,128)S(1)}, u32[]{:S(2)}, u32[]{:S(2)}) %collective-permute-start.17) | collective-permute-done | bytes 245792 | tf_op jit(solution)/shard_map/ppermute | solution.py:461
  115.0 0.9 collective-permute-start.27
  115.8 5.4 %collective-permute-done.18 = f32[3,8,1280]{2,1,0:T(8,128)S(1)} collective-permute-done((f32[3,8,1280]{2,1,0:T(8,128)S(1)}, f32[3,8,1280]{2,1,0:T(8,128)S(1)}, u32[]{:S(2)}, u32[]{:S(2)}) %collective-permute-start.18) | collective-permute-done | bytes 122912 | tf_op jit(solution)/shard_map/ppermute | solution.py:461
  121.3 0.9 collective-permute-start.19
  122.2 2.2 %collective-permute-start.31 = (f32[3,32,1280]{2,1,0:T(8,128)}, f32[3,32,1280]{2,1,0:T(8,128)S(1)}, u32[]{:S(2)}, u32[]{:S(2)}) collective-permute-start(f32[3,32,1280]{2,1,0:T(8,128)} %get-tuple-element.68), channel_id=1, source_target_pairs={{0,2},{2,0},{4,6},{6,4},{8,10},{10,8},{12,14},{14,12},{16,18},{18,... | collective-permute-start | bytes 1474568 | tf_op jit(solution)/shard_map/ppermute | solution.py:491
  124.6 3.2 %collective-permute-start.20 = (f32[3,8,1280]{2,1,0:T(8,128)S(1)}, f32[3,8,1280]{2,1,0:T(8,128)S(1)}, u32[]{:S(2)}, u32[]{:S(2)}) collective-permute-start(f32[3,8,1280]{2,1,0:T(8,128)S(1)} %pad_maximum_fusion), channel_id=1, source_target_pairs={{0,16},{2,18},{4,20},{6,22},{8,24},{10,26},{12,28},{14,30},{16,0},... | collective-permute-start | bytes 368648 | tf_op jit(solution)/shard_map/ppermute | solution.py:472
  128.0 5.0 %collective-permute-done.20 = f32[3,8,1280]{2,1,0:T(8,128)S(1)} collective-permute-done((f32[3,8,1280]{2,1,0:T(8,128)S(1)}, f32[3,8,1280]{2,1,0:T(8,128)S(1)}, u32[]{:S(2)}, u32[]{:S(2)}) %collective-permute-start.20) | collective-permute-done | bytes 122912 | tf_op jit(solution)/shard_map/ppermute | solution.py:472
  133.6 4.1 %collective-permute-done.28 = f32[3,16,1280]{2,1,0:T(8,128)S(1)} collective-permute-done((f32[3,16,1280]{2,1,0:T(8,128)S(1)}, f32[3,16,1280]{2,1,0:T(8,128)S(1)}, u32[]{:S(2)}, u32[]{:S(2)}) %collective-permute-start.28) | collective-permute-done | bytes 245792 | tf_op jit(solution)/shard_map/ppermute | solution.py:461
  137.9 1.7 collective-permute-start.34
  139.6 7.1 %collective-permute-done.29 = f32[3,8,1280]{2,1,0:T(8,128)S(1)} collective-permute-done((f32[3,8,1280]{2,1,0:T(8,128)S(1)}, f32[3,8,1280]{2,1,0:T(8,128)S(1)}, u32[]{:S(2)}, u32[]{:S(2)}) %collective-permute-start.29) | collective-permute-done | bytes 122912 | tf_op jit(solution)/shard_map/ppermute | solution.py:461
  146.8 2.5 %collective-permute-start.35 = (f32[3,8,1280]{2,1,0:T(8,128)S(1)}, f32[3,8,1280]{2,1,0:T(8,128)S(1)}, u32[]{:S(2)}, u32[]{:S(2)}) collective-permute-start(f32[3,8,1280]{2,1,0:T(8,128)S(1)} %dynamic-slice_add_fusion.10), channel_id=1, source_target_pairs={{0,16},{2,18},{4,20},{6,22},{8,24},{10,26},{12,28},{14,30},{16,0},... | collective-permute-start | bytes 368648 | tf_op jit(solution)/shard_map/ppermute | solution.py:461
  149.6 5.0 %collective-permute-done.35 = f32[3,8,1280]{2,1,0:T(8,128)S(1)} collective-permute-done((f32[3,8,1280]{2,1,0:T(8,128)S(1)}, f32[3,8,1280]{2,1,0:T(8,128)S(1)}, u32[]{:S(2)}, u32[]{:S(2)}) %collective-permute-start.35) | collective-permute-done | bytes 122912 | tf_op jit(solution)/shard_map/ppermute | solution.py:461
  154.7 1.8 collective-permute-start.36
  156.5 1.6 collective-permute-done.22
  158.9 2.1 %collective-permute-done.36 = f32[2,8,1280]{2,1,0:T(8,128)S(1)} collective-permute-done((f32[2,8,1280]{2,1,0:T(8,128)S(1)}, f32[2,8,1280]{2,1,0:T(8,128)S(1)}, u32[]{:S(2)}, u32[]{:S(2)}) %collective-permute-start.36) | collective-permute-done | bytes 81952 | tf_op jit(solution)/shard_map/ppermute | solution.py:472
  161.0 5.8 %collective-permute-done.37 = f32[2,16,1280]{2,1,0:T(8,128)S(1)} collective-permute-done((f32[2,16,1280]{2,1,0:T(8,128)S(1)}, f32[2,16,1280]{2,1,0:T(8,128)S(1)}, u32[]{:S(2)}, u32[]{:S(2)}) %collective-permute-start.37) | collective-permute-done | bytes 163872 | tf_op jit(solution)/shard_map/ppermute | solution.py:472
  166.8 2.9 %collective-permute-start.38 = (f32[2,32,1280]{2,1,0:T(8,128)S(1)}, f32[2,32,1280]{2,1,0:T(8,128)S(1)}, u32[]{:S(2)}, u32[]{:S(2)}) collective-permute-start(f32[2,32,1280]{2,1,0:T(8,128)S(1)} %maximum_select_fusion.6), channel_id=1, source_target_pairs={{0,4},{2,10},{4,0},{6,14},{8,12},{10,2},{12,8},{14,6},{16,20},{18,... | collective-permute-start | bytes 983048 | tf_op jit(solution)/shard_map/ppermute | solution.py:472
  169.7 5.1 %collective-permute-done.38 = f32[2,32,1280]{2,1,0:T(8,128)S(1)} collective-permute-done((f32[2,32,1280]{2,1,0:T(8,128)S(1)}, f32[2,32,1280]{2,1,0:T(8,128)S(1)}, u32[]{:S(2)}, u32[]{:S(2)}) %collective-permute-start.38) | collective-permute-done | bytes 327712 | tf_op jit(solution)/shard_map/ppermute | solution.py:472
  174.8 0.9 maximum_select_fusion.4.refs_0_
  176.6 2.1 %maximum_select_fusion.refs_1_ = f32[2,320,1280]{2,1,0:T(8,128)} fusion(f32[1,320,1280]{2,1,0:T(8,128)S(1)} %get-tuple-element.86, f32[1,320,1280]{2,1,0:T(8,128)S(1)} %get-tuple-element.88, f32[1,320,1280]{2,1,0:T(8,128)S(1)} %get-tuple-element.87, f32[1,320,1280]{2,1,0:T(8,128)S(1)} %get-tuple-element.85, pred[]{:T(512)S(6)} %eq.37), kind=kLoop, calls=%fused_computation | loop fusion | flops 2457600 | bytes 9830401 | tf_op jit(solution)/shard_map/jit(_where)/select_n | solution.py:520
  178.7 2.3 %collective-permute-done.39 = f32[2,64,1280]{2,1,0:T(8,128)S(1)} collective-permute-done((f32[2,64,1280]{2,1,0:T(8,128)}, f32[2,64,1280]{2,1,0:T(8,128)S(1)}, u32[]{:S(2)}, u32[]{:S(2)}) %collective-permute-start.39) | collective-permute-done | bytes 655392 | tf_op jit(solution)/shard_map/ppermute | solution.py:472
  181.0 1.4 maximum_select_fusion.2
  182.4 0.9 slice_dynamic-update-slice_fusion.1
  183.3 0.9 slice_dynamic-update-slice_fusion
  (123 shorter events, 12.8 us)
Async XLA Ops:
  2.6 19.6 %collective-permute-start = (f32[2,136,640]{2,1,0:T(8,128)}, f32[2,136,640]{2,1,0:T(8,128)S(1)}, u32[]{:S(2)}, u32[]{:S(2)}) collective-permute-start(f32[2,136,640]{2,1,0:T(8,128)} %pieces_of.4), channel_id=1, source_target_pairs={{0,1},{1,0},{2,3},{3,2},{4,5},{5,4},{6,7},{7,6},{8,9},{9,8},{10,11... | collective-permute-start | bytes 2088968 | tf_op jit(solution)/shard_map/ppermute | solution.py:443
  9.2 26.3 %collective-permute-start.6 = (f32[2,128,640]{2,1,0:T(8,128)}, f32[2,128,640]{2,1,0:T(8,128)S(1)}, u32[]{:S(2)}, u32[]{:S(2)}) collective-permute-start(f32[2,128,640]{2,1,0:T(8,128)} %get-tuple-element.44), channel_id=1, source_target_pairs={{0,1},{1,0},{2,3},{3,2},{4,5},{5,4},{6,7},{7,6},{8,9},{9,8},{10,11... | collective-permute-start | bytes 1966088 | tf_op jit(solution)/shard_map/ppermute | solution.py:447
  33.3 14.9 %collective-permute-start.2 = (f32[3,32,1280]{2,1,0:T(8,128)}, f32[3,32,1280]{2,1,0:T(8,128)S(1)}, u32[]{:S(2)}, u32[]{:S(2)}) collective-permute-start(f32[3,32,1280]{2,1,0:T(8,128)} %get-tuple-element.42), channel_id=1, source_target_pairs={{0,2},{2,0},{4,6},{6,4},{8,10},{10,8},{12,14},{14,12},{16,18},{18,... | collective-permute-start | bytes 1474568 | tf_op jit(solution)/shard_map/ppermute | solution.py:490
  33.4 17.9 %collective-permute-start.13 = (f32[2,128,640]{2,1,0:T(8,128)}, f32[2,128,640]{2,1,0:T(8,128)S(1)}, u32[]{:S(2)}, u32[]{:S(2)}) collective-permute-start(f32[2,128,640]{2,1,0:T(8,128)} %gated.4), channel_id=1, source_target_pairs={{0,1},{1,0},{2,3},{3,2},{4,5},{5,4},{6,7},{7,6},{8,9},{9,8},{10,11... | collective-permute-start | bytes 1966088 | tf_op jit(solution)/shard_map/ppermute | solution.py:447
  46.2 3.3 %collective-permute-start.8 = (f32[3,32,1280]{2,1,0:T(8,128)}, f32[3,32,1280]{2,1,0:T(8,128)S(1)}, u32[]{:S(2)}, u32[]{:S(2)}) collective-permute-start(f32[3,32,1280]{2,1,0:T(8,128)} %get-tuple-element.49), channel_id=1, source_target_pairs={{0,2},{2,0},{4,6},{6,4},{8,10},{10,8},{12,14},{14,12},{16,18},{18,... | collective-permute-start | bytes 1474568 | tf_op jit(solution)/shard_map/ppermute | solution.py:490
  46.4 23.4 %collective-permute-start.24 = (f32[2,128,640]{2,1,0:T(8,128)}, f32[2,128,640]{2,1,0:T(8,128)}, u32[]{:S(2)}, u32[]{:S(2)}) collective-permute-start(f32[2,128,640]{2,1,0:T(8,128)} %gated.5), channel_id=1, source_target_pairs={{0,1},{1,0},{2,3},{3,2},{4,5},{5,4},{6,7},{7,6},{8,9},{9,8},{10,11... | collective-permute-start | bytes 1966088 | tf_op jit(solution)/shard_map/ppermute | solution.py:447
  48.1 15.3 %collective-permute-start.1 = (f32[3,32,1280]{2,1,0:T(8,128)}, f32[3,32,1280]{2,1,0:T(8,128)}, u32[]{:S(2)}, u32[]{:S(2)}) collective-permute-start(f32[3,32,1280]{2,1,0:T(8,128)} %get-tuple-element.40), channel_id=1, source_target_pairs={{0,2},{2,0},{4,6},{6,4},{8,10},{10,8},{12,14},{14,12},{16,18},{18,... | collective-permute-start | bytes 1474568 | tf_op jit(solution)/shard_map/ppermute | solution.py:491
  48.2 18.8 %collective-permute-start.7 = (f32[3,32,1280]{2,1,0:T(8,128)}, f32[3,32,1280]{2,1,0:T(8,128)}, u32[]{:S(2)}, u32[]{:S(2)}) collective-permute-start(f32[3,32,1280]{2,1,0:T(8,128)} %get-tuple-element.47), channel_id=1, source_target_pairs={{0,2},{2,0},{4,6},{6,4},{8,10},{10,8},{12,14},{14,12},{16,18},{18,... | collective-permute-start | bytes 1474568 | tf_op jit(solution)/shard_map/ppermute | solution.py:491
  49.5 14.1 %collective-permute-start.3 = (f32[3,32,1280]{2,1,0:T(8,128)}, f32[3,32,1280]{2,1,0:T(8,128)S(1)}, u32[]{:S(2)}, u32[]{:S(2)}) collective-permute-start(f32[3,32,1280]{2,1,0:T(8,128)} %add.295.refs_4_), channel_id=1, source_target_pairs={{0,4},{2,10},{4,0},{6,14},{8,12},{10,2},{12,8},{14,6},{16,20},{18,... | collective-permute-start | bytes 1474568 | tf_op jit(solution)/shard_map/ppermute | solution.py:466
  51.1 12.3 %copy-start.12 = (f32[3,32,1280]{2,1,0:T(8,128)}, f32[3,32,1280]{2,1,0:T(8,128)S(1)}, u32[]{:S(2)}) copy-start(f32[3,32,1280]{2,1,0:T(8,128)S(1)} %add.310.refs_4_) | copy-start | bytes 1474564
  51.3 15.8 %collective-permute-start.9 = (f32[3,32,1280]{2,1,0:T(8,128)S(1)}, f32[3,32,1280]{2,1,0:T(8,128)S(1)}, u32[]{:S(2)}, u32[]{:S(2)}) collective-permute-start(f32[3,32,1280]{2,1,0:T(8,128)S(1)} %add.310.refs_4_), channel_id=1, source_target_pairs={{0,4},{2,10},{4,0},{6,14},{8,12},{10,2},{12,8},{14,6},{16,20},{18,... | collective-permute-start | bytes 1474568 | tf_op jit(solution)/shard_map/ppermute | solution.py:466
  63.4 16.9 %collective-permute-start.15 = (f32[3,32,1280]{2,1,0:T(8,128)}, f32[3,32,1280]{2,1,0:T(8,128)S(1)}, u32[]{:S(2)}, u32[]{:S(2)}) collective-permute-start(f32[3,32,1280]{2,1,0:T(8,128)} %get-tuple-element.56), channel_id=1, source_target_pairs={{0,2},{2,0},{4,6},{6,4},{8,10},{10,8},{12,14},{14,12},{16,18},{18,... | collective-permute-start | bytes 1474568 | tf_op jit(solution)/shard_map/ppermute | solution.py:490
  63.5 21.4 %collective-permute-start.30 = (f32[2,120,640]{2,1,0:T(8,128)}, f32[2,120,640]{2,1,0:T(8,128)}, u32[]{:S(2)}, u32[]{:S(2)}) collective-permute-start(f32[2,120,640]{2,1,0:T(8,128)} %gated.6), channel_id=1, source_target_pairs={{0,1},{1,0},{2,3},{3,2},{4,5},{5,4},{6,7},{7,6},{8,9},{9,8},{10,11... | collective-permute-start | bytes 1843208 | tf_op jit(solution)/shard_map/ppermute | solution.py:447
  66.9 40.7 %collective-permute-start.14 = (f32[3,32,1280]{2,1,0:T(8,128)}, f32[3,32,1280]{2,1,0:T(8,128)S(1)}, u32[]{:S(2)}, u32[]{:S(2)}) collective-permute-start(f32[3,32,1280]{2,1,0:T(8,128)} %get-tuple-element.54), channel_id=1, source_target_pairs={{0,2},{2,0},{4,6},{6,4},{8,10},{10,8},{12,14},{14,12},{16,18},{18,... | collective-permute-start | bytes 1474568 | tf_op jit(solution)/shard_map/ppermute | solution.py:491
  67.1 15.1 %collective-permute-start.4 = (f32[3,16,1280]{2,1,0:T(8,128)}, f32[3,16,1280]{2,1,0:T(8,128)S(1)}, u32[]{:S(2)}, u32[]{:S(2)}) collective-permute-start(f32[3,16,1280]{2,1,0:T(8,128)} %get-tuple-element.80.refs_5_), channel_id=1, source_target_pairs={{0,8},{2,6},{4,12},{6,2},{8,0},{10,14},{12,4},{14,10},{16,24},{18,... | collective-permute-start | bytes 737288 | tf_op jit(solution)/shard_map/ppermute | solution.py:461
  69.8 13.6 %collective-permute-start.10 = (f32[3,16,1280]{2,1,0:T(8,128)S(1)}, f32[3,16,1280]{2,1,0:T(8,128)S(1)}, u32[]{:S(2)}, u32[]{:S(2)}) collective-permute-start(f32[3,16,1280]{2,1,0:T(8,128)S(1)} %get-tuple-element.82.refs_5_), channel_id=1, source_target_pairs={{0,8},{2,6},{4,12},{6,2},{8,0},{10,14},{12,4},{14,10},{16,24},{18,... | collective-permute-start | bytes 737288 | tf_op jit(solution)/shard_map/ppermute | solution.py:461
  70.4 10.8 %copy-start.13 = (f32[3,32,1280]{2,1,0:T(8,128)S(1)}, f32[3,32,1280]{2,1,0:T(8,128)}, u32[]{:S(2)}) copy-start(f32[3,32,1280]{2,1,0:T(8,128)} %get-tuple-element.55) | copy-start | bytes 1474564
  81.1 33.8 %collective-permute-start.26 = (f32[3,32,1280]{2,1,0:T(8,128)}, f32[3,32,1280]{2,1,0:T(8,128)S(1)}, u32[]{:S(2)}, u32[]{:S(2)}) collective-permute-start(f32[3,32,1280]{2,1,0:T(8,128)} %get-tuple-element.63), channel_id=1, source_target_pairs={{0,2},{2,0},{4,6},{6,4},{8,10},{10,8},{12,14},{14,12},{16,18},{18,... | collective-permute-start | bytes 1474568 | tf_op jit(solution)/shard_map/ppermute | solution.py:490
  82.2 45.5 %collective-permute-start.25 = (f32[3,32,1280]{2,1,0:T(8,128)}, f32[3,32,1280]{2,1,0:T(8,128)S(1)}, u32[]{:S(2)}, u32[]{:S(2)}) collective-permute-start(f32[3,32,1280]{2,1,0:T(8,128)} %get-tuple-element.61), channel_id=1, source_target_pairs={{0,2},{2,0},{4,6},{6,4},{8,10},{10,8},{12,14},{14,12},{16,18},{18,... | collective-permute-start | bytes 1474568 | tf_op jit(solution)/shard_map/ppermute | solution.py:491
  83.5 14.0 %copy-start.16 = (f32[3,16,1280]{2,1,0:T(8,128)}, f32[3,16,1280]{2,1,0:T(8,128)S(1)}, u32[]{:S(2)}) copy-start(f32[3,16,1280]{2,1,0:T(8,128)S(1)} %collective-permute-done.10) | copy-start | bytes 737284
  83.5 24.1 %collective-permute-start.16 = (f32[3,32,1280]{2,1,0:T(8,128)S(1)}, f32[3,32,1280]{2,1,0:T(8,128)S(1)}, u32[]{:S(2)}, u32[]{:S(2)}) collective-permute-start(f32[3,32,1280]{2,1,0:T(8,128)S(1)} %add.322.refs_4_), channel_id=1, source_target_pairs={{0,4},{2,10},{4,0},{6,14},{8,12},{10,2},{12,8},{14,6},{16,20},{18,... | collective-permute-start | bytes 1474568 | tf_op jit(solution)/shard_map/ppermute | solution.py:466
  85.0 12.5 %collective-permute-start.5 = (f32[3,8,1280]{2,1,0:T(8,128)}, f32[3,8,1280]{2,1,0:T(8,128)}, u32[]{:S(2)}, u32[]{:S(2)}) collective-permute-start(f32[3,8,1280]{2,1,0:T(8,128)} %dynamic-slice_add_fusion.14.refs_6_), channel_id=1, source_target_pairs={{0,16},{2,18},{4,20},{6,22},{8,24},{10,26},{12,28},{14,30},{16,0},... | collective-permute-start | bytes 368648 | tf_op jit(solution)/shard_map/ppermute | solution.py:461
  87.5 20.1 %copy-start.7 = (f32[3,32,1280]{2,1,0:T(8,128)S(1)}, f32[3,32,1280]{2,1,0:T(8,128)}, u32[]{:S(2)}) copy-start(f32[3,32,1280]{2,1,0:T(8,128)} %get-tuple-element.53) | copy-start | bytes 1474564
  97.5 9.2 %collective-permute-start.11 = (f32[3,8,1280]{2,1,0:T(8,128)}, f32[3,8,1280]{2,1,0:T(8,128)S(1)}, u32[]{:S(2)}, u32[]{:S(2)}) collective-permute-start(f32[3,8,1280]{2,1,0:T(8,128)} %dynamic-slice_add_fusion.13), channel_id=1, source_target_pairs={{0,16},{2,18},{4,20},{6,22},{8,24},{10,26},{12,28},{14,30},{16,0},... | collective-permute-start | bytes 368648 | tf_op jit(solution)/shard_map/ppermute | solution.py:461
  98.8 16.1 %copy-start.10 = (f32[3,32,1280]{2,1,0:T(8,128)S(1)}, f32[3,32,1280]{2,1,0:T(8,128)}, u32[]{:S(2)}) copy-start(f32[3,32,1280]{2,1,0:T(8,128)} %get-tuple-element.62) | copy-start | bytes 1474564
  106.6 15.6 %collective-permute-start.32 = (f32[3,32,1280]{2,1,0:T(8,128)}, f32[3,32,1280]{2,1,0:T(8,128)S(1)}, u32[]{:S(2)}, u32[]{:S(2)}) collective-permute-start(f32[3,32,1280]{2,1,0:T(8,128)} %get-tuple-element.70), channel_id=1, source_target_pairs={{0,2},{2,0},{4,6},{6,4},{8,10},{10,8},{12,14},{14,12},{16,18},{18,... | collective-permute-start | bytes 1474568 | tf_op jit(solution)/shard_map/ppermute | solution.py:490
  107.7 16.7 %copy-start.11 = (f32[3,32,1280]{2,1,0:T(8,128)S(1)}, f32[3,32,1280]{2,1,0:T(8,128)}, u32[]{:S(2)}) copy-start(f32[3,32,1280]{2,1,0:T(8,128)} %get-tuple-element.69) | copy-start | bytes 1474564
  107.7 6.3 %collective-permute-start.17 = (f32[3,16,1280]{2,1,0:T(8,128)S(1)}, f32[3,16,1280]{2,1,0:T(8,128)S(1)}, u32[]{:S(2)}, u32[]{:S(2)}) collective-permute-start(f32[3,16,1280]{2,1,0:T(8,128)S(1)} %get-tuple-element.84), channel_id=1, source_target_pairs={{0,8},{2,6},{4,12},{6,2},{8,0},{10,14},{12,4},{14,10},{16,24},{18,... | collective-permute-start | bytes 737288 | tf_op jit(solution)/shard_map/ppermute | solution.py:461
  114.0 7.2 %collective-permute-start.18 = (f32[3,8,1280]{2,1,0:T(8,128)S(1)}, f32[3,8,1280]{2,1,0:T(8,128)S(1)}, u32[]{:S(2)}, u32[]{:S(2)}) collective-permute-start(f32[3,8,1280]{2,1,0:T(8,128)S(1)} %dynamic-slice_add_fusion.12), channel_id=1, source_target_pairs={{0,16},{2,18},{4,20},{6,22},{8,24},{10,26},{12,28},{14,30},{16,0},... | collective-permute-start | bytes 368648 | tf_op jit(solution)/shard_map/ppermute | solution.py:461
  114.1 10.4 %collective-permute-start.12 = (f32[2,8,1280]{2,1,0:T(8,128)S(1)}, f32[2,8,1280]{2,1,0:T(8,128)S(1)}, u32[]{:S(2)}, u32[]{:S(2)}) collective-permute-start(f32[2,8,1280]{2,1,0:T(8,128)S(1)} %pad_maximum_fusion.1), channel_id=1, source_target_pairs={{0,1},{1,0},{2,3},{3,2},{4,5},{5,4},{6,7},{7,6},{8,9},{9,8},{10,11... | collective-permute-start | bytes 245768 | tf_op jit(solution)/shard_map/ppermute | solution.py:500
  114.9 12.9 %copy-start.6 = (f32[3,32,1280]{2,1,0:T(8,128)S(1)}, f32[3,32,1280]{2,1,0:T(8,128)}, u32[]{:S(2)}) copy-start(f32[3,32,1280]{2,1,0:T(8,128)} %get-tuple-element.60) | copy-start | bytes 1474564
  115.0 12.8 %collective-permute-start.27 = (f32[3,32,1280]{2,1,0:T(8,128)S(1)}, f32[3,32,1280]{2,1,0:T(8,128)S(1)}, u32[]{:S(2)}, u32[]{:S(2)}) collective-permute-start(f32[3,32,1280]{2,1,0:T(8,128)S(1)} %add.335), channel_id=1, source_target_pairs={{0,4},{2,10},{4,0},{6,14},{8,12},{10,2},{12,8},{14,6},{16,20},{18,... | collective-permute-start | bytes 1474568 | tf_op jit(solution)/shard_map/ppermute | solution.py:466
  121.3 3.3 %collective-permute-start.19 = (f32[8,1280]{1,0:T(8,128)S(1)}, f32[8,1280]{1,0:T(8,128)S(1)}, u32[]{:S(2)}, u32[]{:S(2)}) collective-permute-start(f32[8,1280]{1,0:T(8,128)S(1)} %fusion.18), channel_id=1, source_target_pairs={{0,0},{1,2},{2,1},{3,3},{4,4},{5,10},{6,9},{7,7},{8,8},{9,6},{10,5... | collective-permute-start | bytes 122888 | tf_op jit(solution)/shard_map/ppermute | solution.py:511
  122.2 15.6 %collective-permute-start.31 = (f32[3,32,1280]{2,1,0:T(8,128)}, f32[3,32,1280]{2,1,0:T(8,128)S(1)}, u32[]{:S(2)}, u32[]{:S(2)}) collective-permute-start(f32[3,32,1280]{2,1,0:T(8,128)} %get-tuple-element.68), channel_id=1, source_target_pairs={{0,2},{2,0},{4,6},{6,4},{8,10},{10,8},{12,14},{14,12},{16,18},{18,... | collective-permute-start | bytes 1474568 | tf_op jit(solution)/shard_map/ppermute | solution.py:491
  124.5 13.4 %copy-start.5 = (f32[3,32,1280]{2,1,0:T(8,128)S(1)}, f32[3,32,1280]{2,1,0:T(8,128)}, u32[]{:S(2)}) copy-start(f32[3,32,1280]{2,1,0:T(8,128)} %get-tuple-element.67) | copy-start | bytes 1474564
  124.5 13.3 %collective-permute-start.33 = (f32[3,32,1280]{2,1,0:T(8,128)S(1)}, f32[3,32,1280]{2,1,0:T(8,128)S(1)}, u32[]{:S(2)}, u32[]{:S(2)}) collective-permute-start(f32[3,32,1280]{2,1,0:T(8,128)S(1)} %add.347), channel_id=1, source_target_pairs={{0,4},{2,10},{4,0},{6,14},{8,12},{10,2},{12,8},{14,6},{16,20},{18,... | collective-permute-start | bytes 1474568 | tf_op jit(solution)/shard_map/ppermute | solution.py:466
  124.6 8.4 %collective-permute-start.20 = (f32[3,8,1280]{2,1,0:T(8,128)S(1)}, f32[3,8,1280]{2,1,0:T(8,128)S(1)}, u32[]{:S(2)}, u32[]{:S(2)}) collective-permute-start(f32[3,8,1280]{2,1,0:T(8,128)S(1)} %pad_maximum_fusion), channel_id=1, source_target_pairs={{0,16},{2,18},{4,20},{6,22},{8,24},{10,26},{12,28},{14,30},{16,0},... | collective-permute-start | bytes 368648 | tf_op jit(solution)/shard_map/ppermute | solution.py:472
  127.9 9.8 %collective-permute-start.28 = (f32[3,16,1280]{2,1,0:T(8,128)S(1)}, f32[3,16,1280]{2,1,0:T(8,128)S(1)}, u32[]{:S(2)}, u32[]{:S(2)}) collective-permute-start(f32[3,16,1280]{2,1,0:T(8,128)S(1)} %get-tuple-element.76), channel_id=1, source_target_pairs={{0,8},{2,6},{4,12},{6,2},{8,0},{10,14},{12,4},{14,10},{16,24},{18,... | collective-permute-start | bytes 737288 | tf_op jit(solution)/shard_map/ppermute | solution.py:461
  133.0 16.2 %collective-permute-start.21 = (f32[3,16,1280]{2,1,0:T(8,128)S(1)}, f32[3,16,1280]{2,1,0:T(8,128)S(1)}, u32[]{:S(2)}, u32[]{:S(2)}) collective-permute-start(f32[3,16,1280]{2,1,0:T(8,128)S(1)} %maximum_select_fusion.7), channel_id=1, source_target_pairs={{0,8},{2,6},{4,12},{6,2},{8,0},{10,14},{12,4},{14,10},{16,24},{18,... | collective-permute-start | bytes 737288 | tf_op jit(solution)/shard_map/ppermute | solution.py:472
  137.7 8.9 %collective-permute-start.29 = (f32[3,8,1280]{2,1,0:T(8,128)S(1)}, f32[3,8,1280]{2,1,0:T(8,128)S(1)}, u32[]{:S(2)}, u32[]{:S(2)}) collective-permute-start(f32[3,8,1280]{2,1,0:T(8,128)S(1)} %dynamic-slice_add_fusion.11), channel_id=1, source_target_pairs={{0,16},{2,18},{4,20},{6,22},{8,24},{10,26},{12,28},{14,30},{16,0},... | collective-permute-start | bytes 368648 | tf_op jit(solution)/shard_map/ppermute | solution.py:461
  137.9 8.8 %collective-permute-start.34 = (f32[3,16,1280]{2,1,0:T(8,128)S(1)}, f32[3,16,1280]{2,1,0:T(8,128)S(1)}, u32[]{:S(2)}, u32[]{:S(2)}) collective-permute-start(f32[3,16,1280]{2,1,0:T(8,128)S(1)} %get-tuple-element.78), channel_id=1, source_target_pairs={{0,8},{2,6},{4,12},{6,2},{8,0},{10,14},{12,4},{14,10},{16,24},{18,... | collective-permute-start | bytes 737288 | tf_op jit(solution)/shard_map/ppermute | solution.py:461
  146.8 7.8 %collective-permute-start.35 = (f32[3,8,1280]{2,1,0:T(8,128)S(1)}, f32[3,8,1280]{2,1,0:T(8,128)S(1)}, u32[]{:S(2)}, u32[]{:S(2)}) collective-permute-start(f32[3,8,1280]{2,1,0:T(8,128)S(1)} %dynamic-slice_add_fusion.10), channel_id=1, source_target_pairs={{0,16},{2,18},{4,20},{6,22},{8,24},{10,26},{12,28},{14,30},{16,0},... | collective-permute-start | bytes 368648 | tf_op jit(solution)/shard_map/ppermute | solution.py:461
  149.3 8.9 %collective-permute-start.22 = (f32[3,32,1280]{2,1,0:T(8,128)S(1)}, f32[3,32,1280]{2,1,0:T(8,128)S(1)}, u32[]{:S(2)}, u32[]{:S(2)}) collective-permute-start(f32[3,32,1280]{2,1,0:T(8,128)S(1)} %maximum_select_fusion.5), channel_id=1, source_target_pairs={{0,4},{2,10},{4,0},{6,14},{8,12},{10,2},{12,8},{14,6},{16,20},{18,... | collective-permute-start | bytes 1474568 | tf_op jit(solution)/shard_map/ppermute | solution.py:472
  154.7 6.3 %collective-permute-start.36 = (f32[2,8,1280]{2,1,0:T(8,128)S(1)}, f32[2,8,1280]{2,1,0:T(8,128)S(1)}, u32[]{:S(2)}, u32[]{:S(2)}) collective-permute-start(f32[2,8,1280]{2,1,0:T(8,128)S(1)} %pad_maximum_fusion.2), channel_id=1, source_target_pairs={{0,16},{2,18},{4,20},{6,22},{8,24},{10,26},{12,28},{14,30},{16,0},... | collective-permute-start | bytes 245768 | tf_op jit(solution)/shard_map/ppermute | solution.py:472
  158.3 17.5 %collective-permute-start.23 = (f32[3,64,1280]{2,1,0:T(8,128)S(1)}, f32[3,64,1280]{2,1,0:T(8,128)S(1)}, u32[]{:S(2)}, u32[]{:S(2)}) collective-permute-start(f32[3,64,1280]{2,1,0:T(8,128)S(1)} %maximum_select_fusion.3), channel_id=1, source_target_pairs={{0,2},{2,0},{4,6},{6,4},{8,10},{10,8},{12,14},{14,12},{16,18},{18,... | collective-permute-start | bytes 2949128 | tf_op jit(solution)/shard_map/ppermute | solution.py:472
  161.0 5.9 %collective-permute-start.37 = (f32[2,16,1280]{2,1,0:T(8,128)S(1)}, f32[2,16,1280]{2,1,0:T(8,128)S(1)}, u32[]{:S(2)}, u32[]{:S(2)}) collective-permute-start(f32[2,16,1280]{2,1,0:T(8,128)S(1)} %maximum_select_fusion.8), channel_id=1, source_target_pairs={{0,8},{2,6},{4,12},{6,2},{8,0},{10,14},{12,4},{14,10},{16,24},{18,... | collective-permute-start | bytes 491528 | tf_op jit(solution)/shard_map/ppermute | solution.py:472
  166.8 8.0 %collective-permute-start.38 = (f32[2,32,1280]{2,1,0:T(8,128)S(1)}, f32[2,32,1280]{2,1,0:T(8,128)S(1)}, u32[]{:S(2)}, u32[]{:S(2)}) collective-permute-start(f32[2,32,1280]{2,1,0:T(8,128)S(1)} %maximum_select_fusion.6), channel_id=1, source_target_pairs={{0,4},{2,10},{4,0},{6,14},{8,12},{10,2},{12,8},{14,6},{16,20},{18,... | collective-permute-start | bytes 983048 | tf_op jit(solution)/shard_map/ppermute | solution.py:472
  178.7 2.3 %collective-permute-start.39 = (f32[2,64,1280]{2,1,0:T(8,128)}, f32[2,64,1280]{2,1,0:T(8,128)S(1)}, u32[]{:S(2)}, u32[]{:S(2)}) collective-permute-start(f32[2,64,1280]{2,1,0:T(8,128)} %gated.7), channel_id=1, source_target_pairs={{0,2},{2,0},{4,6},{6,4},{8,10},{10,8},{12,14},{14,12},{16,18},{18,... | collective-permute-start | bytes 1966088 | tf_op jit(solution)/shard_map/ppermute | solution.py:472
  (10 other events, 34.3 us)

commit v25 on v21

--- a/solution.py
+++ b/solution.py
@@ -510,20 +510,22 @@
         trades.append((index, place_of[mate]))
     both = lax.ppermute(pieces["both"][0], ("mem", "band"), trades)
 
-    early = gathered(jnp.concatenate([other, both[None]]))
-    other, both = early[:-1], early[-1]
-    middle = both.shape[0] // 2
-    low, high = both[:middle], both[middle:]
-    rest = jnp.zeros((nlat // 2 - middle, NLON), jnp.float32)
-    down = jnp.stack([jnp.concatenate([rest, low]), jnp.concatenate([*other, high])])
-    up = jnp.stack([jnp.concatenate([low, *other[::-1]]), jnp.concatenate([high, rest])])
+    far = gathered(other)
+    near = gathered(jnp.concatenate([both[None], jnp.stack(pieces["own"])]))
+    middle = near.shape[1] // 2
+    rest = jnp.zeros((nlat // 2, NLON), jnp.float32)
+    down = jnp.stack([rest, jnp.concatenate([*far, rest[:middle]])])
+    up = jnp.stack([jnp.concatenate([rest[:middle], *far[::-1]]), rest])
     out = jnp.where(band == 0, down, up)
 
-    own = gathered(jnp.stack(pieces["own"]))
-    for k, block in enumerate(own):
-        width = block.shape[0]
-        row = choose(band, (nlat // 2 - middle - (k + 1) * width, middle + k * width))
-        out = lax.dynamic_update_slice(out, block[None], (band, row.astype(jnp.int32), jnp.int32(0)))
+    def put(block, level, pair):
+        return lax.dynamic_update_slice(out, block[None], (level, choose(band, pair).astype(jnp.int32), jnp.int32(0)))
+
+    edge = nlat // 2 - middle
+    out = put(near[0, :middle], 0, (edge, 0))
+    out = put(near[0, middle:], 1, (edge, 0))
+    for k, block in enumerate(near[1:]):
+        out = put(block, band, (edge - (k + 1) * LANE, middle + k * LANE))
     return out
 
 

time: 177 us -> 185 us (1.045)
  waiting for transfers between devices: 66.1 us -> 72.5 us
    ppermute x10, starting transfers between devices: 9.61 us -> 15.5 us  [halved(): return ([total(mine), lax.ppermute(leaves, 'mem', ways[step])], leaves)]
    ppermute x8, starting transfers between devices: 7.82 us -> 2.38 us  [doubled(): beside = lax.ppermute(part, 'mem', cores if step < 0 else ways[step])]
    ppermute x10, waiting for transfers between devices: 35.5 us -> 40.3 us  [halved(): return ([total(mine), lax.ppermute(leaves, 'mem', ways[step])], leaves)]
    add x5, other arithmetic: 1.04 us -> 3.9 us  [across(): leaves = passed + passed_more]
    ppermute x5, starting transfers between devices: 3.39 us -> 1 us  [by_levels(): second = lax.ppermute(quarters[2], 'mem', cores)]
    unnamed x34 -> x42, local copies, waits for them, and re-layouts: 3.5 us -> 4.81 us
  transfers between devices with their start and end apart: 40 -> 40, of which waited for: 13 -> 16; matrix products, arithmetic and copies ran while one was open for 4% -> 4% of each run, Pallas kernels for 33% -> 31%
where the time goes in v25:
time: 185 us; the launch traced here: 183 us
  waiting for transfers between devices  72.5 us (39%)
  Pallas kernels  60 us (32%)
  starting transfers between devices  35.5 us (19%)
  other arithmetic  8.34 us (5%)
  local copies, waits for them, and re-layouts  5.91 us (3%)
    pallas_call x5, Pallas kernels, window_tensor(): pl.pallas_call(functools.partial(window_kernel, window, len(waits)), out_...  49.9 us
    ppermute x10, waiting for transfers between devices, halved(): return ([total(mine), lax.ppermute(leaves, 'mem', ways[step])], leaves)  40.3 us
    ppermute x8, waiting for transfers between devices, doubled(): beside = lax.ppermute(part, 'mem', cores if step < 0 else ways[step])  23 us
    ppermute x10, starting transfers between devices, halved(): return ([total(mine), lax.ppermute(leaves, 'mem', ways[step])], leaves)  15.5 us
    pallas_call x3, Pallas kernels, pieces_of(): pl.pallas_call(functools.partial(pieces_kernel, windows, slots, count), i...  10.2 us
    ppermute x1, waiting for transfers between devices, by_levels(): remotes = [lax.ppermute(piece, 'band', swap)]  8.25 us
    ppermute x5, starting transfers between devices, across(): return ([kept, kept_more, lax.ppermute(leaves, 'mem', ways[step])], leaves)  5.95 us
    ppermute x4, starting transfers between devices, by_levels(): remotes.append(lax.ppermute(piece, 'band', swap))  4.91 us
  transfers between devices with their start and end apart: 40, of which 16 were waited for; matrix products, arithmetic and copies ran while one was open for 4% of the time, Pallas kernels for 31%

profile of v25, /device:TPU:0, one launch (start us, length us, event | category | flops | bytes accessed | tf_op | source)
XLA Modules:
  0.0 183.0 jit_solution(11119466324794173923)
XLA Ops:
  0.0 2.6 %pieces_of.4 = f32[2,136,640]{2,1,0:T(8,128)} custom-call(s32[1]{0:T(128)} %bitcast.5.level_ref, f32[2,2,640,640]{3,2,1,0:T(8,128)} %bitcast.17), custom_call_target="tpu_custom_call" | custom-call | bytes 5242880 | tf_op jit(solution)/shard_map/pieces_of/pallas_call | solution.py:209
  2.6 3.0 %collective-permute-start = (f32[2,136,640]{2,1,0:T(8,128)}, f32[2,136,640]{2,1,0:T(8,128)S(1)}, u32[]{:S(2)}, u32[]{:S(2)}) collective-permute-start(f32[2,136,640]{2,1,0:T(8,128)} %pieces_of.4), channel_id=1, source_target_pairs={{0,1},{1,0},{2,3},{3,2},{4,5},{5,4},{6,7},{7,6},{8,9},{9,8},{10,11... | collective-permute-start | bytes 2088968 | tf_op jit(solution)/shard_map/ppermute | solution.py:443
  5.6 3.6 %pieces_of.5 = (f32[2,128,640]{2,1,0:T(8,128)}, f32[2,128,640]{2,1,0:T(8,128)}, f32[2,128,640]{2,1,0:T(8,128)}, f32[2,120,640]{2,1,0:T(8,128)}) custom-call(s32[1]{0:T(128)} %bitcast.5.level_ref, f32[2,2,640,640]{3,2,1,0:T(8,128)} %bitcast.18), custom_call_target="tpu_custom_call" | custom-call | bytes 10485760 | tf_op jit(solution)/shard_map/pieces_of/pallas_call | solution.py:209
  9.4 4.0 %pieces_of.3 = (f32[2,136,640]{2,1,0:T(8,128)}, f32[2,128,640]{2,1,0:T(8,128)}, f32[2,128,640]{2,1,0:T(8,128)}, f32[2,128,640]{2,1,0:T(8,128)}, f32[2,120,640]{2,1,0:T(8,128)}) custom-call(s32[1]{0:T(128)} %bitcast.level_ref, f32[2,2,640,640]{3,2,1,0:T(8,128)} %bitcast.19), custom_call_target="tpu_custom_call" | custom-call | bytes 13107200 | tf_op jit(solution)/shard_map/pieces_of/pallas_call | solution.py:209
  14.0 8.3 %collective-permute-done.refs_2_.refs_1_ = f32[2,136,640]{2,1,0:T(8,128)S(1)} collective-permute-done((f32[2,136,640]{2,1,0:T(8,128)}, f32[2,136,640]{2,1,0:T(8,128)S(1)}, u32[]{:S(2)}, u32[]{:S(2)}) %collective-permute-start) | collective-permute-done | bytes 696352 | tf_op jit(solution)/shard_map/ppermute | solution.py:443
  22.3 0.9 copy-done.1
  23.2 2.1 %collective-permute-start.17 = (f32[2,128,640]{2,1,0:T(8,128)}, f32[2,128,640]{2,1,0:T(8,128)S(1)}, u32[]{:S(2)}, u32[]{:S(2)}) collective-permute-start(f32[2,128,640]{2,1,0:T(8,128)} %gated.3), channel_id=1, source_target_pairs={{0,1},{1,0},{2,3},{3,2},{4,5},{5,4},{6,7},{7,6},{8,9},{9,8},{10,11... | collective-permute-start | bytes 1966088 | tf_op jit(solution)/shard_map/ppermute | solution.py:447
  25.2 10.1 %window_tensor.5 = (f32[3,32,1280]{2,1,0:T(8,128)}, f32[3,32,1280]{2,1,0:T(8,128)}, f32[3,32,1280]{2,1,0:T(8,128)}, f32[3,32,1280]{2,1,0:T(8,128)}, f32[2,16,1280]{2,1,0:T(8,128)}) custom-call(s32[4]{0:T(128)} %pad_add_fusion.refs_0_, f32[2,136,640]{2,1,0:T(8,128)} %get-tuple-element.38.refs_1_, f32[2,136,640]{2,1,0:T(8,128)} %copy-done.1, ...), custom_call_target="tpu_custom_call" | custom-call | flops 10695475200 | bytes 6635520 | tf_op jit(solution)/shard_map/window_tensor/pallas_call | solution.py:395
  35.4 0.9 collective-permute-done.6.refs_2_.refs_1_
  36.3 0.8 copy-done.3
  37.1 9.9 %window_tensor.6 = (f32[3,32,1280]{2,1,0:T(8,128)}, f32[3,32,1280]{2,1,0:T(8,128)}, f32[3,32,1280]{2,1,0:T(8,128)}, f32[3,32,1280]{2,1,0:T(8,128)}, f32[2,16,1280]{2,1,0:T(8,128)}) custom-call(s32[4]{0:T(128)} %pad_add_fusion.refs_0_, f32[2,128,640]{2,1,0:T(8,128)} %get-tuple-element.43.refs_1_, f32[2,128,640]{2,1,0:T(8,128)} %copy-done.3, ...), custom_call_target="tpu_custom_call" | custom-call | flops 10066329600 | bytes 6553600 | tf_op jit(solution)/shard_map/window_tensor/pallas_call | solution.py:395
  47.2 2.1 %collective-permute-start.24 = (f32[2,128,640]{2,1,0:T(8,128)}, f32[2,128,640]{2,1,0:T(8,128)}, u32[]{:S(2)}, u32[]{:S(2)}) collective-permute-start(f32[2,128,640]{2,1,0:T(8,128)} %gated.4), channel_id=1, source_target_pairs={{0,1},{1,0},{2,3},{3,2},{4,5},{5,4},{6,7},{7,6},{8,9},{9,8},{10,11... | collective-permute-start | bytes 1966088 | tf_op jit(solution)/shard_map/ppermute | solution.py:447
  49.9 0.8 add.297.refs_4_
  50.7 1.5 collective-permute-start.3
  53.2 10.0 %window_tensor.7 = (f32[3,32,1280]{2,1,0:T(8,128)}, f32[3,32,1280]{2,1,0:T(8,128)}, f32[3,32,1280]{2,1,0:T(8,128)}, f32[3,32,1280]{2,1,0:T(8,128)}, f32[2,16,1280]{2,1,0:T(8,128)}) custom-call(s32[4]{0:T(128)} %pad_add_fusion.refs_0_, f32[2,128,640]{2,1,0:T(8,128)} %get-tuple-element.50.refs_1_, f32[2,128,640]{2,1,0:T(8,128)} %copy-done.2, ...), custom_call_target="tpu_custom_call" | custom-call | flops 10066329600 | bytes 6553600 | tf_op jit(solution)/shard_map/window_tensor/pallas_call | solution.py:395
  64.3 1.4 dynamic-slice_add_fusion.9
  65.9 1.6 collective-permute-start.4
  68.1 9.9 %window_tensor.8 = (f32[3,32,1280]{2,1,0:T(8,128)}, f32[3,32,1280]{2,1,0:T(8,128)}, f32[3,32,1280]{2,1,0:T(8,128)}, f32[3,32,1280]{2,1,0:T(8,128)}, f32[2,16,1280]{2,1,0:T(8,128)}) custom-call(s32[4]{0:T(128)} %pad_add_fusion.refs_0_, f32[2,128,640]{2,1,0:T(8,128)} %get-tuple-element.57.refs_1_, f32[2,128,640]{2,1,0:T(8,128)} %collective-permute-done.24.refs_2_, ...), custom_call_target="tpu_custom_call" | custom-call | flops 10066329600 | bytes 6553600 | tf_op jit(solution)/shard_map/window_tensor/pallas_call | solution.py:395
  78.2 1.1 add.324.refs_4_
  79.3 1.3 collective-permute-start.20
  80.6 2.7 %collective-permute-start.5 = (f32[3,8,1280]{2,1,0:T(8,128)S(1)}, f32[3,8,1280]{2,1,0:T(8,128)S(1)}, u32[]{:S(2)}, u32[]{:S(2)}) collective-permute-start(f32[3,8,1280]{2,1,0:T(8,128)S(1)} %dynamic-slice_add_fusion.14.refs_6_), channel_id=1, source_target_pairs={{0,16},{2,18},{4,20},{6,22},{8,24},{10,26},{12,28},{14,30},{16,0},... | collective-permute-start | bytes 368648 | tf_op jit(solution)/shard_map/ppermute | solution.py:461
  83.3 5.3 %collective-permute-done.5 = f32[3,8,1280]{2,1,0:T(8,128)S(1)} collective-permute-done((f32[3,8,1280]{2,1,0:T(8,128)S(1)}, f32[3,8,1280]{2,1,0:T(8,128)S(1)}, u32[]{:S(2)}, u32[]{:S(2)}) %collective-permute-start.5) | collective-permute-done | bytes 122912 | tf_op jit(solution)/shard_map/ppermute | solution.py:461
  88.6 1.8 collective-permute-start.11
  90.5 7.5 %collective-permute-done.11 = f32[3,8,1280]{2,1,0:T(8,128)S(1)} collective-permute-done((f32[3,8,1280]{2,1,0:T(8,128)S(1)}, f32[3,8,1280]{2,1,0:T(8,128)S(1)}, u32[]{:S(2)}, u32[]{:S(2)}) %collective-permute-start.11) | collective-permute-done | bytes 122912 | tf_op jit(solution)/shard_map/ppermute | solution.py:461
  98.1 1.6 collective-permute-start.12
  99.6 9.9 %window_tensor.9 = (f32[3,32,1280]{2,1,0:T(8,128)}, f32[3,32,1280]{2,1,0:T(8,128)}, f32[3,32,1280]{2,1,0:T(8,128)}, f32[3,32,1280]{2,1,0:T(8,128)}) custom-call(s32[4]{0:T(128)} %pad_add_fusion.refs_0_, f32[2,120,640]{2,1,0:T(8,128)} %get-tuple-element.64.refs_1_, f32[2,120,640]{2,1,0:T(8,128)} %collective-permute-done.30.refs_2_, ...), custom_call_target="tpu_custom_call" | custom-call | flops 9437184000 | bytes 6471680 | tf_op jit(solution)/shard_map/window_tensor/pallas_call | solution.py:395
  110.8 0.8 add.337
  111.6 1.3 collective-permute-start.27
  113.7 3.1 %collective-permute-start.21 = (f32[3,16,1280]{2,1,0:T(8,128)}, f32[3,16,1280]{2,1,0:T(8,128)S(1)}, u32[]{:S(2)}, u32[]{:S(2)}) collective-permute-start(f32[3,16,1280]{2,1,0:T(8,128)} %get-tuple-element.74), channel_id=1, source_target_pairs={{0,8},{2,6},{4,12},{6,2},{8,0},{10,14},{12,4},{14,10},{16,24},{18,... | collective-permute-start | bytes 737288 | tf_op jit(solution)/shard_map/ppermute | solution.py:461
  116.8 1.4 collective-permute-done.13
  118.3 1.1 add.349
  119.4 4.5 %collective-permute-done.21 = f32[3,16,1280]{2,1,0:T(8,128)S(1)} collective-permute-done((f32[3,16,1280]{2,1,0:T(8,128)}, f32[3,16,1280]{2,1,0:T(8,128)S(1)}, u32[]{:S(2)}, u32[]{:S(2)}) %collective-permute-start.21) | collective-permute-done | bytes 245792 | tf_op jit(solution)/shard_map/ppermute | solution.py:461
  123.9 1.2 collective-permute-start.33
  125.1 1.3 collective-permute-start.22
  126.5 1.9 %collective-permute-start.28 = (f32[3,16,1280]{2,1,0:T(8,128)S(1)}, f32[3,16,1280]{2,1,0:T(8,128)S(1)}, u32[]{:S(2)}, u32[]{:S(2)}) collective-permute-start(f32[3,16,1280]{2,1,0:T(8,128)S(1)} %get-tuple-element.76), channel_id=1, source_target_pairs={{0,8},{2,6},{4,12},{6,2},{8,0},{10,14},{12,4},{14,10},{16,24},{18,... | collective-permute-start | bytes 737288 | tf_op jit(solution)/shard_map/ppermute | solution.py:461
  128.4 3.0 %collective-permute-done.22 = f32[3,8,1280]{2,1,0:T(8,128)S(1)} collective-permute-done((f32[3,8,1280]{2,1,0:T(8,128)S(1)}, f32[3,8,1280]{2,1,0:T(8,128)S(1)}, u32[]{:S(2)}, u32[]{:S(2)}) %collective-permute-start.22) | collective-permute-done | bytes 122912 | tf_op jit(solution)/shard_map/ppermute | solution.py:461
  132.1 4.3 %collective-permute-done.28 = f32[3,16,1280]{2,1,0:T(8,128)S(1)} collective-permute-done((f32[3,16,1280]{2,1,0:T(8,128)S(1)}, f32[3,16,1280]{2,1,0:T(8,128)S(1)}, u32[]{:S(2)}, u32[]{:S(2)}) %collective-permute-start.28) | collective-permute-done | bytes 245792 | tf_op jit(solution)/shard_map/ppermute | solution.py:461
  136.4 1.2 collective-permute-start.29
  137.7 1.3 collective-permute-start.34
  139.0 7.2 %collective-permute-done.29 = f32[3,8,1280]{2,1,0:T(8,128)S(1)} collective-permute-done((f32[3,8,1280]{2,1,0:T(8,128)S(1)}, f32[3,8,1280]{2,1,0:T(8,128)S(1)}, u32[]{:S(2)}, u32[]{:S(2)}) %collective-permute-start.29) | collective-permute-done | bytes 122912 | tf_op jit(solution)/shard_map/ppermute | solution.py:461
  146.8 8.3 %collective-permute-done.35 = f32[3,8,1280]{2,1,0:T(8,128)S(1)} collective-permute-done((f32[3,8,1280]{2,1,0:T(8,128)S(1)}, f32[3,8,1280]{2,1,0:T(8,128)S(1)}, u32[]{:S(2)}, u32[]{:S(2)}) %collective-permute-start.35) | collective-permute-done | bytes 122912 | tf_op jit(solution)/shard_map/ppermute | solution.py:461
  156.1 6.0 %collective-permute-done.36 = f32[3,8,1280]{2,1,0:T(8,128)S(1)} collective-permute-done((f32[3,8,1280]{2,1,0:T(8,128)S(1)}, f32[3,8,1280]{2,1,0:T(8,128)S(1)}, u32[]{:S(2)}, u32[]{:S(2)}) %collective-permute-start.36) | collective-permute-done | bytes 122912 | tf_op jit(solution)/shard_map/ppermute | solution.py:472
  162.5 0.9 collective-permute-start.16
  163.4 5.0 %collective-permute-done.37 = f32[3,16,1280]{2,1,0:T(8,128)S(1)} collective-permute-done((f32[3,16,1280]{2,1,0:T(8,128)S(1)}, f32[3,16,1280]{2,1,0:T(8,128)S(1)}, u32[]{:S(2)}, u32[]{:S(2)}) %collective-permute-start.37) | collective-permute-done | bytes 245792 | tf_op jit(solution)/shard_map/ppermute | solution.py:472
  169.0 8.4 %collective-permute-done.38 = f32[3,32,1280]{2,1,0:T(8,128)S(1)} collective-permute-done((f32[3,32,1280]{2,1,0:T(8,128)S(1)}, f32[3,32,1280]{2,1,0:T(8,128)S(1)}, u32[]{:S(2)}, u32[]{:S(2)}) %collective-permute-start.38) | collective-permute-done | bytes 491552 | tf_op jit(solution)/shard_map/ppermute | solution.py:472
  178.1 1.9 %collective-permute-done.39 = f32[3,64,1280]{2,1,0:T(8,128)S(1)} collective-permute-done((f32[3,64,1280]{2,1,0:T(8,128)S(1)}, f32[3,64,1280]{2,1,0:T(8,128)S(1)}, u32[]{:S(2)}, u32[]{:S(2)}) %collective-permute-start.39) | collective-permute-done | bytes 983072 | tf_op jit(solution)/shard_map/ppermute | solution.py:472
  180.4 1.7 copy-done
  182.1 0.9 slice_dynamic-update-slice_fusion
  (129 shorter events, 11.1 us)
Async XLA Ops:
  2.6 19.6 %collective-permute-start = (f32[2,136,640]{2,1,0:T(8,128)}, f32[2,136,640]{2,1,0:T(8,128)S(1)}, u32[]{:S(2)}, u32[]{:S(2)}) collective-permute-start(f32[2,136,640]{2,1,0:T(8,128)} %pieces_of.4), channel_id=1, source_target_pairs={{0,1},{1,0},{2,3},{3,2},{4,5},{5,4},{6,7},{7,6},{8,9},{9,8},{10,11... | collective-permute-start | bytes 2088968 | tf_op jit(solution)/shard_map/ppermute | solution.py:443
  9.2 27.1 %collective-permute-start.6 = (f32[2,128,640]{2,1,0:T(8,128)}, f32[2,128,640]{2,1,0:T(8,128)S(1)}, u32[]{:S(2)}, u32[]{:S(2)}) collective-permute-start(f32[2,128,640]{2,1,0:T(8,128)} %get-tuple-element.44), channel_id=1, source_target_pairs={{0,1},{1,0},{2,3},{3,2},{4,5},{5,4},{6,7},{7,6},{8,9},{9,8},{10,11... | collective-permute-start | bytes 1966088 | tf_op jit(solution)/shard_map/ppermute | solution.py:447
  23.2 29.2 %collective-permute-start.17 = (f32[2,128,640]{2,1,0:T(8,128)}, f32[2,128,640]{2,1,0:T(8,128)S(1)}, u32[]{:S(2)}, u32[]{:S(2)}) collective-permute-start(f32[2,128,640]{2,1,0:T(8,128)} %gated.3), channel_id=1, source_target_pairs={{0,1},{1,0},{2,3},{3,2},{4,5},{5,4},{6,7},{7,6},{8,9},{9,8},{10,11... | collective-permute-start | bytes 1966088 | tf_op jit(solution)/shard_map/ppermute | solution.py:447
  35.4 14.1 %collective-permute-start.2 = (f32[3,32,1280]{2,1,0:T(8,128)}, f32[3,32,1280]{2,1,0:T(8,128)S(1)}, u32[]{:S(2)}, u32[]{:S(2)}) collective-permute-start(f32[3,32,1280]{2,1,0:T(8,128)} %get-tuple-element.42), channel_id=1, source_target_pairs={{0,2},{2,0},{4,6},{6,4},{8,10},{10,8},{12,14},{14,12},{16,18},{18,... | collective-permute-start | bytes 1474568 | tf_op jit(solution)/shard_map/ppermute | solution.py:490
  47.1 3.7 %collective-permute-start.8 = (f32[3,32,1280]{2,1,0:T(8,128)}, f32[3,32,1280]{2,1,0:T(8,128)S(1)}, u32[]{:S(2)}, u32[]{:S(2)}) collective-permute-start(f32[3,32,1280]{2,1,0:T(8,128)} %get-tuple-element.49), channel_id=1, source_target_pairs={{0,2},{2,0},{4,6},{6,4},{8,10},{10,8},{12,14},{14,12},{16,18},{18,... | collective-permute-start | bytes 1474568 | tf_op jit(solution)/shard_map/ppermute | solution.py:490
  47.2 20.4 %collective-permute-start.24 = (f32[2,128,640]{2,1,0:T(8,128)}, f32[2,128,640]{2,1,0:T(8,128)}, u32[]{:S(2)}, u32[]{:S(2)}) collective-permute-start(f32[2,128,640]{2,1,0:T(8,128)} %gated.4), channel_id=1, source_target_pairs={{0,1},{1,0},{2,3},{3,2},{4,5},{5,4},{6,7},{7,6},{8,9},{9,8},{10,11... | collective-permute-start | bytes 1966088 | tf_op jit(solution)/shard_map/ppermute | solution.py:447
  49.4 14.0 %collective-permute-start.1 = (f32[3,32,1280]{2,1,0:T(8,128)}, f32[3,32,1280]{2,1,0:T(8,128)}, u32[]{:S(2)}, u32[]{:S(2)}) collective-permute-start(f32[3,32,1280]{2,1,0:T(8,128)} %get-tuple-element.40), channel_id=1, source_target_pairs={{0,2},{2,0},{4,6},{6,4},{8,10},{10,8},{12,14},{14,12},{16,18},{18,... | collective-permute-start | bytes 1474568 | tf_op jit(solution)/shard_map/ppermute | solution.py:491
  49.4 16.3 %collective-permute-start.7 = (f32[3,32,1280]{2,1,0:T(8,128)}, f32[3,32,1280]{2,1,0:T(8,128)S(1)}, u32[]{:S(2)}, u32[]{:S(2)}) collective-permute-start(f32[3,32,1280]{2,1,0:T(8,128)} %get-tuple-element.47), channel_id=1, source_target_pairs={{0,2},{2,0},{4,6},{6,4},{8,10},{10,8},{12,14},{14,12},{16,18},{18,... | collective-permute-start | bytes 1474568 | tf_op jit(solution)/shard_map/ppermute | solution.py:491
  50.7 13.2 %collective-permute-start.3 = (f32[3,32,1280]{2,1,0:T(8,128)}, f32[3,32,1280]{2,1,0:T(8,128)}, u32[]{:S(2)}, u32[]{:S(2)}) collective-permute-start(f32[3,32,1280]{2,1,0:T(8,128)} %add.297.refs_4_), channel_id=1, source_target_pairs={{0,4},{2,10},{4,0},{6,14},{8,12},{10,2},{12,8},{14,6},{16,20},{18,... | collective-permute-start | bytes 1474568 | tf_op jit(solution)/shard_map/ppermute | solution.py:466
  52.3 11.0 %copy-start.13 = (f32[3,32,1280]{2,1,0:T(8,128)}, f32[3,32,1280]{2,1,0:T(8,128)S(1)}, u32[]{:S(2)}) copy-start(f32[3,32,1280]{2,1,0:T(8,128)S(1)} %add.312.refs_4_) | copy-start | bytes 1474564
  52.3 13.6 %collective-permute-start.9 = (f32[3,32,1280]{2,1,0:T(8,128)S(1)}, f32[3,32,1280]{2,1,0:T(8,128)S(1)}, u32[]{:S(2)}, u32[]{:S(2)}) collective-permute-start(f32[3,32,1280]{2,1,0:T(8,128)S(1)} %add.312.refs_4_), channel_id=1, source_target_pairs={{0,4},{2,10},{4,0},{6,14},{8,12},{10,2},{12,8},{14,6},{16,20},{18,... | collective-permute-start | bytes 1474568 | tf_op jit(solution)/shard_map/ppermute | solution.py:466
  63.3 36.3 %collective-permute-start.30 = (f32[2,120,640]{2,1,0:T(8,128)}, f32[2,120,640]{2,1,0:T(8,128)}, u32[]{:S(2)}, u32[]{:S(2)}) collective-permute-start(f32[2,120,640]{2,1,0:T(8,128)} %gated.5), channel_id=1, source_target_pairs={{0,1},{1,0},{2,3},{3,2},{4,5},{5,4},{6,7},{7,6},{8,9},{9,8},{10,11... | collective-permute-start | bytes 1843208 | tf_op jit(solution)/shard_map/ppermute | solution.py:447
  63.9 47.7 %collective-permute-start.18 = (f32[3,32,1280]{2,1,0:T(8,128)}, f32[3,32,1280]{2,1,0:T(8,128)S(1)}, u32[]{:S(2)}, u32[]{:S(2)}) collective-permute-start(f32[3,32,1280]{2,1,0:T(8,128)} %get-tuple-element.54), channel_id=1, source_target_pairs={{0,2},{2,0},{4,6},{6,4},{8,10},{10,8},{12,14},{14,12},{16,18},{18,... | collective-permute-start | bytes 1474568 | tf_op jit(solution)/shard_map/ppermute | solution.py:491
  65.7 12.3 %collective-permute-start.19 = (f32[3,32,1280]{2,1,0:T(8,128)}, f32[3,32,1280]{2,1,0:T(8,128)}, u32[]{:S(2)}, u32[]{:S(2)}) collective-permute-start(f32[3,32,1280]{2,1,0:T(8,128)} %get-tuple-element.56), channel_id=1, source_target_pairs={{0,2},{2,0},{4,6},{6,4},{8,10},{10,8},{12,14},{14,12},{16,18},{18,... | collective-permute-start | bytes 1474568 | tf_op jit(solution)/shard_map/ppermute | solution.py:490
  65.9 13.3 %collective-permute-start.4 = (f32[3,16,1280]{2,1,0:T(8,128)S(1)}, f32[3,16,1280]{2,1,0:T(8,128)S(1)}, u32[]{:S(2)}, u32[]{:S(2)}) collective-permute-start(f32[3,16,1280]{2,1,0:T(8,128)S(1)} %get-tuple-element.80.refs_5_), channel_id=1, source_target_pairs={{0,8},{2,6},{4,12},{6,2},{8,0},{10,14},{12,4},{14,10},{16,24},{18,... | collective-permute-start | bytes 737288 | tf_op jit(solution)/shard_map/ppermute | solution.py:461
  67.6 10.5 %copy-start.16 = (f32[3,16,1280]{2,1,0:T(8,128)}, f32[3,16,1280]{2,1,0:T(8,128)S(1)}, u32[]{:S(2)}) copy-start(f32[3,16,1280]{2,1,0:T(8,128)S(1)} %get-tuple-element.82.refs_5_) | copy-start | bytes 737284
  67.6 13.0 %collective-permute-start.10 = (f32[3,16,1280]{2,1,0:T(8,128)S(1)}, f32[3,16,1280]{2,1,0:T(8,128)S(1)}, u32[]{:S(2)}, u32[]{:S(2)}) collective-permute-start(f32[3,16,1280]{2,1,0:T(8,128)S(1)} %get-tuple-element.82.refs_5_), channel_id=1, source_target_pairs={{0,8},{2,6},{4,12},{6,2},{8,0},{10,14},{12,4},{14,10},{16,24},{18,... | collective-permute-start | bytes 737288 | tf_op jit(solution)/shard_map/ppermute | solution.py:461
  78.1 32.7 %collective-permute-start.26 = (f32[3,32,1280]{2,1,0:T(8,128)}, f32[3,32,1280]{2,1,0:T(8,128)S(1)}, u32[]{:S(2)}, u32[]{:S(2)}) collective-permute-start(f32[3,32,1280]{2,1,0:T(8,128)} %get-tuple-element.63), channel_id=1, source_target_pairs={{0,2},{2,0},{4,6},{6,4},{8,10},{10,8},{12,14},{14,12},{16,18},{18,... | collective-permute-start | bytes 1474568 | tf_op jit(solution)/shard_map/ppermute | solution.py:490
  79.2 20.4 %copy-start.12 = (f32[3,32,1280]{2,1,0:T(8,128)}, f32[3,32,1280]{2,1,0:T(8,128)S(1)}, u32[]{:S(2)}) copy-start(f32[3,32,1280]{2,1,0:T(8,128)S(1)} %add.324.refs_4_) | copy-start | bytes 1474564
  79.3 33.7 %collective-permute-start.20 = (f32[3,32,1280]{2,1,0:T(8,128)S(1)}, f32[3,32,1280]{2,1,0:T(8,128)S(1)}, u32[]{:S(2)}, u32[]{:S(2)}) collective-permute-start(f32[3,32,1280]{2,1,0:T(8,128)S(1)} %add.324.refs_4_), channel_id=1, source_target_pairs={{0,4},{2,10},{4,0},{6,14},{8,12},{10,2},{12,8},{14,6},{16,20},{18,... | collective-permute-start | bytes 1474568 | tf_op jit(solution)/shard_map/ppermute | solution.py:466
  80.6 19.0 %copy-start.18 = (f32[3,8,1280]{2,1,0:T(8,128)}, f32[3,8,1280]{2,1,0:T(8,128)S(1)}, u32[]{:S(2)}) copy-start(f32[3,8,1280]{2,1,0:T(8,128)S(1)} %dynamic-slice_add_fusion.14.refs_6_) | copy-start | bytes 368644
  80.6 8.0 %collective-permute-start.5 = (f32[3,8,1280]{2,1,0:T(8,128)S(1)}, f32[3,8,1280]{2,1,0:T(8,128)S(1)}, u32[]{:S(2)}, u32[]{:S(2)}) collective-permute-start(f32[3,8,1280]{2,1,0:T(8,128)S(1)} %dynamic-slice_add_fusion.14.refs_6_), channel_id=1, source_target_pairs={{0,16},{2,18},{4,20},{6,22},{8,24},{10,26},{12,28},{14,30},{16,0},... | collective-permute-start | bytes 368648 | tf_op jit(solution)/shard_map/ppermute | solution.py:461
  88.6 9.4 %collective-permute-start.11 = (f32[3,8,1280]{2,1,0:T(8,128)S(1)}, f32[3,8,1280]{2,1,0:T(8,128)S(1)}, u32[]{:S(2)}, u32[]{:S(2)}) collective-permute-start(f32[3,8,1280]{2,1,0:T(8,128)S(1)} %dynamic-slice_add_fusion.13), channel_id=1, source_target_pairs={{0,16},{2,18},{4,20},{6,22},{8,24},{10,26},{12,28},{14,30},{16,0},... | collective-permute-start | bytes 368648 | tf_op jit(solution)/shard_map/ppermute | solution.py:461
  98.1 11.6 %collective-permute-start.12 = (f32[2,8,1280]{2,1,0:T(8,128)S(1)}, f32[2,8,1280]{2,1,0:T(8,128)S(1)}, u32[]{:S(2)}, u32[]{:S(2)}) collective-permute-start(f32[2,8,1280]{2,1,0:T(8,128)S(1)} %pad_maximum_fusion.1), channel_id=1, source_target_pairs={{0,1},{1,0},{2,3},{3,2},{4,5},{5,4},{6,7},{7,6},{8,9},{9,8},{10,11... | collective-permute-start | bytes 245768 | tf_op jit(solution)/shard_map/ppermute | solution.py:500
  99.6 11.1 %copy-start.11 = (f32[3,32,1280]{2,1,0:T(8,128)S(1)}, f32[3,32,1280]{2,1,0:T(8,128)}, u32[]{:S(2)}) copy-start(f32[3,32,1280]{2,1,0:T(8,128)} %get-tuple-element.62) | copy-start | bytes 1474564
  99.6 13.3 %copy-start.5 = (f32[3,32,1280]{2,1,0:T(8,128)S(1)}, f32[3,32,1280]{2,1,0:T(8,128)}, u32[]{:S(2)}) copy-start(f32[3,32,1280]{2,1,0:T(8,128)} %get-tuple-element.53) | copy-start | bytes 1474564
  109.5 8.6 %collective-permute-start.32 = (f32[3,32,1280]{2,1,0:T(8,128)}, f32[3,32,1280]{2,1,0:T(8,128)}, u32[]{:S(2)}, u32[]{:S(2)}) collective-permute-start(f32[3,32,1280]{2,1,0:T(8,128)} %get-tuple-element.70), channel_id=1, source_target_pairs={{0,2},{2,0},{4,6},{6,4},{8,10},{10,8},{12,14},{14,12},{16,18},{18,... | collective-permute-start | bytes 1474568 | tf_op jit(solution)/shard_map/ppermute | solution.py:490
  110.3 14.8 %collective-permute-start.25 = (f32[3,32,1280]{2,1,0:T(8,128)}, f32[3,32,1280]{2,1,0:T(8,128)S(1)}, u32[]{:S(2)}, u32[]{:S(2)}) collective-permute-start(f32[3,32,1280]{2,1,0:T(8,128)} %get-tuple-element.61), channel_id=1, source_target_pairs={{0,2},{2,0},{4,6},{6,4},{8,10},{10,8},{12,14},{14,12},{16,18},{18,... | collective-permute-start | bytes 1474568 | tf_op jit(solution)/shard_map/ppermute | solution.py:491
  110.8 7.4 %collective-permute-start.13 = (f32[2,8,1280]{2,1,0:T(8,128)}, f32[2,8,1280]{2,1,0:T(8,128)S(1)}, u32[]{:S(2)}, u32[]{:S(2)}) collective-permute-start(f32[2,8,1280]{2,1,0:T(8,128)} %copy-done.19), channel_id=1, source_target_pairs={{0,16},{2,18},{4,20},{6,22},{8,24},{10,26},{12,28},{14,30},{16,0},... | collective-permute-start | bytes 245768 | tf_op jit(solution)/shard_map/ppermute | solution.py:472
  111.6 14.9 %collective-permute-start.27 = (f32[3,32,1280]{2,1,0:T(8,128)}, f32[3,32,1280]{2,1,0:T(8,128)S(1)}, u32[]{:S(2)}, u32[]{:S(2)}) collective-permute-start(f32[3,32,1280]{2,1,0:T(8,128)} %add.337), channel_id=1, source_target_pairs={{0,4},{2,10},{4,0},{6,14},{8,12},{10,2},{12,8},{14,6},{16,20},{18,... | collective-permute-start | bytes 1474568 | tf_op jit(solution)/shard_map/ppermute | solution.py:466
  113.0 13.5 %copy-start.7 = (f32[3,32,1280]{2,1,0:T(8,128)S(1)}, f32[3,32,1280]{2,1,0:T(8,128)}, u32[]{:S(2)}) copy-start(f32[3,32,1280]{2,1,0:T(8,128)} %get-tuple-element.60) | copy-start | bytes 1474564
  113.7 10.1 %collective-permute-start.21 = (f32[3,16,1280]{2,1,0:T(8,128)}, f32[3,16,1280]{2,1,0:T(8,128)S(1)}, u32[]{:S(2)}, u32[]{:S(2)}) collective-permute-start(f32[3,16,1280]{2,1,0:T(8,128)} %get-tuple-element.74), channel_id=1, source_target_pairs={{0,8},{2,6},{4,12},{6,2},{8,0},{10,14},{12,4},{14,10},{16,24},{18,... | collective-permute-start | bytes 737288 | tf_op jit(solution)/shard_map/ppermute | solution.py:461
  118.2 19.4 %collective-permute-start.31 = (f32[3,32,1280]{2,1,0:T(8,128)}, f32[3,32,1280]{2,1,0:T(8,128)S(1)}, u32[]{:S(2)}, u32[]{:S(2)}) collective-permute-start(f32[3,32,1280]{2,1,0:T(8,128)} %get-tuple-element.68), channel_id=1, source_target_pairs={{0,2},{2,0},{4,6},{6,4},{8,10},{10,8},{12,14},{14,12},{16,18},{18,... | collective-permute-start | bytes 1474568 | tf_op jit(solution)/shard_map/ppermute | solution.py:491
  118.2 37.1 %collective-permute-start.14 = (f32[2,16,1280]{2,1,0:T(8,128)S(1)}, f32[2,16,1280]{2,1,0:T(8,128)S(1)}, u32[]{:S(2)}, u32[]{:S(2)}) collective-permute-start(f32[2,16,1280]{2,1,0:T(8,128)S(1)} %maximum_select_fusion.7), channel_id=1, source_target_pairs={{0,8},{2,6},{4,12},{6,2},{8,0},{10,14},{12,4},{14,10},{16,24},{18,... | collective-permute-start | bytes 491528 | tf_op jit(solution)/shard_map/ppermute | solution.py:472
  119.4 18.2 %copy-start.8 = (f32[3,32,1280]{2,1,0:T(8,128)S(1)}, f32[3,32,1280]{2,1,0:T(8,128)}, u32[]{:S(2)}) copy-start(f32[3,32,1280]{2,1,0:T(8,128)} %get-tuple-element.67) | copy-start | bytes 1474564
  123.9 13.7 %collective-permute-start.33 = (f32[3,32,1280]{2,1,0:T(8,128)S(1)}, f32[3,32,1280]{2,1,0:T(8,128)S(1)}, u32[]{:S(2)}, u32[]{:S(2)}) collective-permute-start(f32[3,32,1280]{2,1,0:T(8,128)S(1)} %add.349), channel_id=1, source_target_pairs={{0,4},{2,10},{4,0},{6,14},{8,12},{10,2},{12,8},{14,6},{16,20},{18,... | collective-permute-start | bytes 1474568 | tf_op jit(solution)/shard_map/ppermute | solution.py:466
  125.1 6.2 %collective-permute-start.22 = (f32[3,8,1280]{2,1,0:T(8,128)S(1)}, f32[3,8,1280]{2,1,0:T(8,128)S(1)}, u32[]{:S(2)}, u32[]{:S(2)}) collective-permute-start(f32[3,8,1280]{2,1,0:T(8,128)S(1)} %dynamic-slice_add_fusion.12), channel_id=1, source_target_pairs={{0,16},{2,18},{4,20},{6,22},{8,24},{10,26},{12,28},{14,30},{16,0},... | collective-permute-start | bytes 368648 | tf_op jit(solution)/shard_map/ppermute | solution.py:461
  126.5 9.8 %collective-permute-start.28 = (f32[3,16,1280]{2,1,0:T(8,128)S(1)}, f32[3,16,1280]{2,1,0:T(8,128)S(1)}, u32[]{:S(2)}, u32[]{:S(2)}) collective-permute-start(f32[3,16,1280]{2,1,0:T(8,128)S(1)} %get-tuple-element.76), channel_id=1, source_target_pairs={{0,8},{2,6},{4,12},{6,2},{8,0},{10,14},{12,4},{14,10},{16,24},{18,... | collective-permute-start | bytes 737288 | tf_op jit(solution)/shard_map/ppermute | solution.py:461
  131.4 23.7 %collective-permute-start.23 = (f32[8,1280]{1,0:T(8,128)S(1)}, f32[8,1280]{1,0:T(8,128)S(1)}, u32[]{:S(2)}, u32[]{:S(2)}) collective-permute-start(f32[8,1280]{1,0:T(8,128)S(1)} %fusion.18), channel_id=1, source_target_pairs={{0,0},{1,2},{2,1},{3,3},{4,4},{5,10},{6,9},{7,7},{8,8},{9,6},{10,5... | collective-permute-start | bytes 122888 | tf_op jit(solution)/shard_map/ppermute | solution.py:511
  136.4 9.7 %collective-permute-start.29 = (f32[3,8,1280]{2,1,0:T(8,128)S(1)}, f32[3,8,1280]{2,1,0:T(8,128)S(1)}, u32[]{:S(2)}, u32[]{:S(2)}) collective-permute-start(f32[3,8,1280]{2,1,0:T(8,128)S(1)} %dynamic-slice_add_fusion.11), channel_id=1, source_target_pairs={{0,16},{2,18},{4,20},{6,22},{8,24},{10,26},{12,28},{14,30},{16,0},... | collective-permute-start | bytes 368648 | tf_op jit(solution)/shard_map/ppermute | solution.py:461
  137.7 8.9 %collective-permute-start.34 = (f32[3,16,1280]{2,1,0:T(8,128)S(1)}, f32[3,16,1280]{2,1,0:T(8,128)S(1)}, u32[]{:S(2)}, u32[]{:S(2)}) collective-permute-start(f32[3,16,1280]{2,1,0:T(8,128)S(1)} %get-tuple-element.78), channel_id=1, source_target_pairs={{0,8},{2,6},{4,12},{6,2},{8,0},{10,14},{12,4},{14,10},{16,24},{18,... | collective-permute-start | bytes 737288 | tf_op jit(solution)/shard_map/ppermute | solution.py:461
  146.6 8.5 %collective-permute-start.35 = (f32[3,8,1280]{2,1,0:T(8,128)S(1)}, f32[3,8,1280]{2,1,0:T(8,128)S(1)}, u32[]{:S(2)}, u32[]{:S(2)}) collective-permute-start(f32[3,8,1280]{2,1,0:T(8,128)S(1)} %dynamic-slice_add_fusion.10), channel_id=1, source_target_pairs={{0,16},{2,18},{4,20},{6,22},{8,24},{10,26},{12,28},{14,30},{16,0},... | collective-permute-start | bytes 368648 | tf_op jit(solution)/shard_map/ppermute | solution.py:461
  155.2 6.9 %collective-permute-start.36 = (f32[3,8,1280]{2,1,0:T(8,128)S(1)}, f32[3,8,1280]{2,1,0:T(8,128)S(1)}, u32[]{:S(2)}, u32[]{:S(2)}) collective-permute-start(f32[3,8,1280]{2,1,0:T(8,128)S(1)} %pad_maximum_fusion), channel_id=1, source_target_pairs={{0,16},{2,18},{4,20},{6,22},{8,24},{10,26},{12,28},{14,30},{16,0},... | collective-permute-start | bytes 368648 | tf_op jit(solution)/shard_map/ppermute | solution.py:472
  155.3 7.1 %collective-permute-start.15 = (f32[2,32,1280]{2,1,0:T(8,128)S(1)}, f32[2,32,1280]{2,1,0:T(8,128)S(1)}, u32[]{:S(2)}, u32[]{:S(2)}) collective-permute-start(f32[2,32,1280]{2,1,0:T(8,128)S(1)} %maximum_select_fusion.5), channel_id=1, source_target_pairs={{0,4},{2,10},{4,0},{6,14},{8,12},{10,2},{12,8},{14,6},{16,20},{18,... | collective-permute-start | bytes 983048 | tf_op jit(solution)/shard_map/ppermute | solution.py:472
  162.1 6.3 %collective-permute-start.37 = (f32[3,16,1280]{2,1,0:T(8,128)S(1)}, f32[3,16,1280]{2,1,0:T(8,128)S(1)}, u32[]{:S(2)}, u32[]{:S(2)}) collective-permute-start(f32[3,16,1280]{2,1,0:T(8,128)S(1)} %maximum_select_fusion.6), channel_id=1, source_target_pairs={{0,8},{2,6},{4,12},{6,2},{8,0},{10,14},{12,4},{14,10},{16,24},{18,... | collective-permute-start | bytes 737288 | tf_op jit(solution)/shard_map/ppermute | solution.py:472
  162.5 6.4 %collective-permute-start.16 = (f32[2,64,1280]{2,1,0:T(8,128)S(1)}, f32[2,64,1280]{2,1,0:T(8,128)S(1)}, u32[]{:S(2)}, u32[]{:S(2)}) collective-permute-start(f32[2,64,1280]{2,1,0:T(8,128)S(1)} %maximum_select_fusion.3), channel_id=1, source_target_pairs={{0,2},{2,0},{4,6},{6,4},{8,10},{10,8},{12,14},{14,12},{16,18},{18,... | collective-permute-start | bytes 1966088 | tf_op jit(solution)/shard_map/ppermute | solution.py:472
  168.4 8.9 %collective-permute-start.38 = (f32[3,32,1280]{2,1,0:T(8,128)S(1)}, f32[3,32,1280]{2,1,0:T(8,128)S(1)}, u32[]{:S(2)}, u32[]{:S(2)}) collective-permute-start(f32[3,32,1280]{2,1,0:T(8,128)S(1)} %maximum_select_fusion.4), channel_id=1, source_target_pairs={{0,4},{2,10},{4,0},{6,14},{8,12},{10,2},{12,8},{14,6},{16,20},{18,... | collective-permute-start | bytes 1474568 | tf_op jit(solution)/shard_map/ppermute | solution.py:472
  177.4 2.6 %collective-permute-start.39 = (f32[3,64,1280]{2,1,0:T(8,128)S(1)}, f32[3,64,1280]{2,1,0:T(8,128)S(1)}, u32[]{:S(2)}, u32[]{:S(2)}) collective-permute-start(f32[3,64,1280]{2,1,0:T(8,128)S(1)} %maximum_select_fusion.2), channel_id=1, source_target_pairs={{0,2},{2,0},{4,6},{6,4},{8,10},{10,8},{12,14},{14,12},{16,18},{18,... | collective-permute-start | bytes 2949128 | tf_op jit(solution)/shard_map/ppermute | solution.py:472
  (13 other events, 47.3 us)

commit v26 on v21

--- a/solution.py
+++ b/solution.py
@@ -307,8 +307,9 @@
         columns = slice(start, stop)
         sums = []
         for parity in range(2):
-            total = dot(lhs_high[parity], table[2 * parity, :, columns])
-            total += dot(lhs_low[parity], table[2 * parity, :, columns])
+            terms = jnp.concatenate([lhs_high[parity], lhs_low[parity]])
+            both = dot(terms, table[2 * parity, :, columns])
+            total = both[: 2 * rows] + both[2 * rows :]
             total += dot(lhs_high[parity], table[2 * parity + 1, :, columns])
             sums.append(total)
         for c in range(2):

time: 177 us -> 177 us (level)
  transfers between devices with their start and end apart: 40 -> 40, of which waited for: 13 -> 13; matrix products, arithmetic and copies ran while one was open for 4% -> 4% of each run, Pallas kernels for 33% -> 32%
where the time goes in v26:
time: 177 us
  waiting for transfers between devices  66.1 us (37%)
  Pallas kernels  59.9 us (34%)
  starting transfers between devices  36.8 us (21%)
  other arithmetic  8.5 us (5%)
  local copies, waits for them, and re-layouts  4.56 us (3%)
    pallas_call x5, Pallas kernels, window_tensor(): pl.pallas_call(functools.partial(window_kernel, window, len(waits)), out_...  49.7 us
    ppermute x10, waiting for transfers between devices, halved(): return ([total(mine), lax.ppermute(leaves, 'mem', ways[step])], leaves)  35.6 us
    ppermute x8, waiting for transfers between devices, doubled(): beside = lax.ppermute(part, 'mem', cores if step < 0 else ways[step])  22 us
    pallas_call x3, Pallas kernels, pieces_of(): pl.pallas_call(functools.partial(pieces_kernel, windows, slots, count), i...  10.2 us
    ppermute x10, starting transfers between devices, halved(): return ([total(mine), lax.ppermute(leaves, 'mem', ways[step])], leaves)  9.6 us
    ppermute x1, waiting for transfers between devices, by_levels(): remotes = [lax.ppermute(piece, 'band', swap)]  8.2 us
    ppermute x8, starting transfers between devices, doubled(): beside = lax.ppermute(part, 'mem', cores if step < 0 else ways[step])  7.82 us
    ppermute x4, starting transfers between devices, by_levels(): remotes.append(lax.ppermute(piece, 'band', swap))  5.5 us
  transfers between devices with their start and end apart: 40, of which 13 were waited for; matrix products, arithmetic and copies ran while one was open for 4% of the time, Pallas kernels for 32%

profile of v26, /device:TPU:0, one launch (start us, length us, event | category | flops | bytes accessed | tf_op | source)
XLA Modules:
  0.0 176.6 jit_solution(9048175316825145616)
XLA Ops:
  0.0 2.6 %pieces_of.4 = f32[2,136,640]{2,1,0:T(8,128)} custom-call(s32[1]{0:T(128)} %bitcast.5.level_ref, f32[2,2,640,640]{3,2,1,0:T(8,128)} %bitcast.25), custom_call_target="tpu_custom_call" | custom-call | bytes 5242880 | tf_op jit(solution)/shard_map/pieces_of/pallas_call | solution.py:209
  2.6 3.0 %collective-permute-start = (f32[2,136,640]{2,1,0:T(8,128)}, f32[2,136,640]{2,1,0:T(8,128)S(1)}, u32[]{:S(2)}, u32[]{:S(2)}) collective-permute-start(f32[2,136,640]{2,1,0:T(8,128)} %pieces_of.4), channel_id=1, source_target_pairs={{0,1},{1,0},{2,3},{3,2},{4,5},{5,4},{6,7},{7,6},{8,9},{9,8},{10,11... | collective-permute-start | bytes 2088968 | tf_op jit(solution)/shard_map/ppermute | solution.py:444
  5.6 3.6 %pieces_of.5 = (f32[2,128,640]{2,1,0:T(8,128)}, f32[2,128,640]{2,1,0:T(8,128)}, f32[2,128,640]{2,1,0:T(8,128)}, f32[2,120,640]{2,1,0:T(8,128)}) custom-call(s32[1]{0:T(128)} %bitcast.5.level_ref, f32[2,2,640,640]{3,2,1,0:T(8,128)} %bitcast.26), custom_call_target="tpu_custom_call" | custom-call | bytes 10485760 | tf_op jit(solution)/shard_map/pieces_of/pallas_call | solution.py:209
  9.4 4.0 %pieces_of.3 = (f32[2,136,640]{2,1,0:T(8,128)}, f32[2,128,640]{2,1,0:T(8,128)}, f32[2,128,640]{2,1,0:T(8,128)}, f32[2,128,640]{2,1,0:T(8,128)}, f32[2,120,640]{2,1,0:T(8,128)}) custom-call(s32[1]{0:T(128)} %bitcast.level_ref, f32[2,2,640,640]{3,2,1,0:T(8,128)} %bitcast.27), custom_call_target="tpu_custom_call" | custom-call | bytes 13107200 | tf_op jit(solution)/shard_map/pieces_of/pallas_call | solution.py:209
  14.0 8.2 %collective-permute-done.refs_2_.refs_1_ = f32[2,136,640]{2,1,0:T(8,128)S(1)} collective-permute-done((f32[2,136,640]{2,1,0:T(8,128)}, f32[2,136,640]{2,1,0:T(8,128)S(1)}, u32[]{:S(2)}, u32[]{:S(2)}) %collective-permute-start) | collective-permute-done | bytes 696352 | tf_op jit(solution)/shard_map/ppermute | solution.py:444
  22.2 0.9 copy-done.1
  23.1 10.1 %window_tensor.5 = (f32[3,32,1280]{2,1,0:T(8,128)}, f32[3,32,1280]{2,1,0:T(8,128)}, f32[3,32,1280]{2,1,0:T(8,128)}, f32[3,32,1280]{2,1,0:T(8,128)}, f32[2,16,1280]{2,1,0:T(8,128)}) custom-call(s32[4]{0:T(128)} %pad_add_fusion.refs_0_, f32[2,136,640]{2,1,0:T(8,128)} %get-tuple-element.38.refs_1_, f32[2,136,640]{2,1,0:T(8,128)} %copy-done.1, ...), custom_call_target="tpu_custom_call" | custom-call | flops 10695475200 | bytes 6635520 | tf_op jit(solution)/shard_map/window_tensor/pallas_call | solution.py:396
  33.3 2.1 %collective-permute-start.13 = (f32[2,128,640]{2,1,0:T(8,128)}, f32[2,128,640]{2,1,0:T(8,128)S(1)}, u32[]{:S(2)}, u32[]{:S(2)}) collective-permute-start(f32[2,128,640]{2,1,0:T(8,128)} %gated.3), channel_id=1, source_target_pairs={{0,1},{1,0},{2,3},{3,2},{4,5},{5,4},{6,7},{7,6},{8,9},{9,8},{10,11... | collective-permute-start | bytes 1966088 | tf_op jit(solution)/shard_map/ppermute | solution.py:448
  35.5 0.8 copy-done.3
  36.3 9.8 %window_tensor.6 = (f32[3,32,1280]{2,1,0:T(8,128)}, f32[3,32,1280]{2,1,0:T(8,128)}, f32[3,32,1280]{2,1,0:T(8,128)}, f32[3,32,1280]{2,1,0:T(8,128)}, f32[2,16,1280]{2,1,0:T(8,128)}) custom-call(s32[4]{0:T(128)} %pad_add_fusion.refs_0_, f32[2,128,640]{2,1,0:T(8,128)} %get-tuple-element.43.refs_1_, f32[2,128,640]{2,1,0:T(8,128)} %copy-done.3, ...), custom_call_target="tpu_custom_call" | custom-call | flops 10066329600 | bytes 6553600 | tf_op jit(solution)/shard_map/window_tensor/pallas_call | solution.py:396
  46.3 1.7 collective-permute-start.24
  48.6 0.8 add.295.refs_4_
  49.4 1.5 collective-permute-start.3
  51.3 2.0 %collective-permute-start.9 = (f32[3,32,1280]{2,1,0:T(8,128)S(1)}, f32[3,32,1280]{2,1,0:T(8,128)}, u32[]{:S(2)}, u32[]{:S(2)}) collective-permute-start(f32[3,32,1280]{2,1,0:T(8,128)S(1)} %add.310.refs_4_), channel_id=1, source_target_pairs={{0,4},{2,10},{4,0},{6,14},{8,12},{10,2},{12,8},{14,6},{16,20},{18,... | collective-permute-start | bytes 1474568 | tf_op jit(solution)/shard_map/ppermute | solution.py:467
  53.3 10.0 %window_tensor.7 = (f32[3,32,1280]{2,1,0:T(8,128)}, f32[3,32,1280]{2,1,0:T(8,128)}, f32[3,32,1280]{2,1,0:T(8,128)}, f32[3,32,1280]{2,1,0:T(8,128)}, f32[2,16,1280]{2,1,0:T(8,128)}) custom-call(s32[4]{0:T(128)} %pad_add_fusion.refs_0_, f32[2,128,640]{2,1,0:T(8,128)} %get-tuple-element.50.refs_1_, f32[2,128,640]{2,1,0:T(8,128)} %copy-done.2, ...), custom_call_target="tpu_custom_call" | custom-call | flops 10066329600 | bytes 6553600 | tf_op jit(solution)/shard_map/window_tensor/pallas_call | solution.py:396
  63.5 1.6 collective-permute-start.30
  65.0 1.8 %dynamic-slice_add_fusion.9 = (f32[3,16,1280]{2,1,0:T(8,128)S(1)}, f32[3,16,1280]{2,1,0:T(8,128)}) fusion(f32[3,32,1280]{2,1,0:T(8,128)} %collective-permute-done.3, s32[]{:T(128)S(6)} %select_n.212, f32[3,32,1280]{2,1,0:T(8,128)S(1)} %collective-permute-done.1, f32[3,32,1280]{2,1,0:T(8,128)S(1)} %copy-done.4, s32[]{:T(128)S(6)} %select_n.214), kind=kLoop, calls=%fused_computation.27 | loop fusion | flops 245760 | bytes 1966088 | tf_op jit(solution)/shard_map/add | solution.py:459
  67.0 1.6 collective-permute-start.4
  68.6 1.4 dynamic-slice_add_fusion.7
  70.5 9.9 %window_tensor.8 = (f32[3,32,1280]{2,1,0:T(8,128)}, f32[3,32,1280]{2,1,0:T(8,128)}, f32[3,32,1280]{2,1,0:T(8,128)}, f32[3,32,1280]{2,1,0:T(8,128)}, f32[2,16,1280]{2,1,0:T(8,128)}) custom-call(s32[4]{0:T(128)} %pad_add_fusion.refs_0_, f32[2,128,640]{2,1,0:T(8,128)} %get-tuple-element.57.refs_1_, f32[2,128,640]{2,1,0:T(8,128)} %collective-permute-done.24.refs_2_, ...), custom_call_target="tpu_custom_call" | custom-call | flops 10066329600 | bytes 6553600 | tf_op jit(solution)/shard_map/window_tensor/pallas_call | solution.py:396
  81.2 0.7 dynamic-slice_add_fusion.14.refs_6_
  81.8 0.8 collective-permute-start.16
  82.7 2.7 %collective-permute-start.5 = (f32[3,8,1280]{2,1,0:T(8,128)}, f32[3,8,1280]{2,1,0:T(8,128)}, u32[]{:S(2)}, u32[]{:S(2)}) collective-permute-start(f32[3,8,1280]{2,1,0:T(8,128)} %dynamic-slice_add_fusion.14.refs_6_), channel_id=1, source_target_pairs={{0,16},{2,18},{4,20},{6,22},{8,24},{10,26},{12,28},{14,30},{16,0},... | collective-permute-start | bytes 368648 | tf_op jit(solution)/shard_map/ppermute | solution.py:462
  85.4 9.8 %window_tensor.9 = (f32[3,32,1280]{2,1,0:T(8,128)}, f32[3,32,1280]{2,1,0:T(8,128)}, f32[3,32,1280]{2,1,0:T(8,128)}, f32[3,32,1280]{2,1,0:T(8,128)}) custom-call(s32[4]{0:T(128)} %pad_add_fusion.refs_0_, f32[2,120,640]{2,1,0:T(8,128)} %get-tuple-element.64.refs_1_, f32[2,120,640]{2,1,0:T(8,128)} %collective-permute-done.30.refs_2_, ...), custom_call_target="tpu_custom_call" | custom-call | flops 9437184000 | bytes 6471680 | tf_op jit(solution)/shard_map/window_tensor/pallas_call | solution.py:396
  95.6 0.9 add_multiply_fusion.4
  96.6 7.6 %collective-permute-done.11 = f32[3,8,1280]{2,1,0:T(8,128)S(1)} collective-permute-done((f32[3,8,1280]{2,1,0:T(8,128)S(1)}, f32[3,8,1280]{2,1,0:T(8,128)S(1)}, u32[]{:S(2)}, u32[]{:S(2)}) %collective-permute-start.11) | collective-permute-done | bytes 122912 | tf_op jit(solution)/shard_map/ppermute | solution.py:462
  104.5 6.1 %collective-permute-done.17 = f32[3,16,1280]{2,1,0:T(8,128)S(1)} collective-permute-done((f32[3,16,1280]{2,1,0:T(8,128)S(1)}, f32[3,16,1280]{2,1,0:T(8,128)S(1)}, u32[]{:S(2)}, u32[]{:S(2)}) %collective-permute-start.17) | collective-permute-done | bytes 245792 | tf_op jit(solution)/shard_map/ppermute | solution.py:462
  110.7 0.8 collective-permute-start.12
  111.6 0.9 collective-permute-start.27
  112.5 5.4 %collective-permute-done.18 = f32[3,8,1280]{2,1,0:T(8,128)S(1)} collective-permute-done((f32[3,8,1280]{2,1,0:T(8,128)S(1)}, f32[3,8,1280]{2,1,0:T(8,128)S(1)}, u32[]{:S(2)}, u32[]{:S(2)}) %collective-permute-start.18) | collective-permute-done | bytes 122912 | tf_op jit(solution)/shard_map/ppermute | solution.py:462
  117.9 0.9 collective-permute-start.19
  118.9 2.2 %collective-permute-start.31 = (f32[3,32,1280]{2,1,0:T(8,128)}, f32[3,32,1280]{2,1,0:T(8,128)S(1)}, u32[]{:S(2)}, u32[]{:S(2)}) collective-permute-start(f32[3,32,1280]{2,1,0:T(8,128)} %get-tuple-element.68), channel_id=1, source_target_pairs={{0,2},{2,0},{4,6},{6,4},{8,10},{10,8},{12,14},{14,12},{16,18},{18,... | collective-permute-start | bytes 1474568 | tf_op jit(solution)/shard_map/ppermute | solution.py:492
  121.2 3.2 %collective-permute-start.20 = (f32[3,8,1280]{2,1,0:T(8,128)S(1)}, f32[3,8,1280]{2,1,0:T(8,128)S(1)}, u32[]{:S(2)}, u32[]{:S(2)}) collective-permute-start(f32[3,8,1280]{2,1,0:T(8,128)S(1)} %pad_maximum_fusion), channel_id=1, source_target_pairs={{0,16},{2,18},{4,20},{6,22},{8,24},{10,26},{12,28},{14,30},{16,0},... | collective-permute-start | bytes 368648 | tf_op jit(solution)/shard_map/ppermute | solution.py:473
  124.6 5.0 %collective-permute-done.20 = f32[3,8,1280]{2,1,0:T(8,128)S(1)} collective-permute-done((f32[3,8,1280]{2,1,0:T(8,128)S(1)}, f32[3,8,1280]{2,1,0:T(8,128)S(1)}, u32[]{:S(2)}, u32[]{:S(2)}) %collective-permute-start.20) | collective-permute-done | bytes 122912 | tf_op jit(solution)/shard_map/ppermute | solution.py:473
  129.6 0.7 collective-permute-start.21
  130.3 4.1 %collective-permute-done.28 = f32[3,16,1280]{2,1,0:T(8,128)S(1)} collective-permute-done((f32[3,16,1280]{2,1,0:T(8,128)S(1)}, f32[3,16,1280]{2,1,0:T(8,128)S(1)}, u32[]{:S(2)}, u32[]{:S(2)}) %collective-permute-start.28) | collective-permute-done | bytes 245792 | tf_op jit(solution)/shard_map/ppermute | solution.py:462
  134.6 1.7 collective-permute-start.34
  136.2 7.1 %collective-permute-done.29 = f32[3,8,1280]{2,1,0:T(8,128)S(1)} collective-permute-done((f32[3,8,1280]{2,1,0:T(8,128)S(1)}, f32[3,8,1280]{2,1,0:T(8,128)S(1)}, u32[]{:S(2)}, u32[]{:S(2)}) %collective-permute-start.29) | collective-permute-done | bytes 122912 | tf_op jit(solution)/shard_map/ppermute | solution.py:462
  143.4 2.5 %collective-permute-start.35 = (f32[3,8,1280]{2,1,0:T(8,128)S(1)}, f32[3,8,1280]{2,1,0:T(8,128)S(1)}, u32[]{:S(2)}, u32[]{:S(2)}) collective-permute-start(f32[3,8,1280]{2,1,0:T(8,128)S(1)} %dynamic-slice_add_fusion.10), channel_id=1, source_target_pairs={{0,16},{2,18},{4,20},{6,22},{8,24},{10,26},{12,28},{14,30},{16,0},... | collective-permute-start | bytes 368648 | tf_op jit(solution)/shard_map/ppermute | solution.py:462
  145.9 5.3 %collective-permute-done.35 = f32[3,8,1280]{2,1,0:T(8,128)S(1)} collective-permute-done((f32[3,8,1280]{2,1,0:T(8,128)S(1)}, f32[3,8,1280]{2,1,0:T(8,128)S(1)}, u32[]{:S(2)}, u32[]{:S(2)}) %collective-permute-start.35) | collective-permute-done | bytes 122912 | tf_op jit(solution)/shard_map/ppermute | solution.py:462
  151.8 1.6 collective-permute-start.22
  153.5 4.1 %collective-permute-done.36 = f32[2,8,1280]{2,1,0:T(8,128)S(1)} collective-permute-done((f32[2,8,1280]{2,1,0:T(8,128)S(1)}, f32[2,8,1280]{2,1,0:T(8,128)S(1)}, u32[]{:S(2)}, u32[]{:S(2)}) %collective-permute-start.36) | collective-permute-done | bytes 81952 | tf_op jit(solution)/shard_map/ppermute | solution.py:473
  158.2 5.0 %collective-permute-done.37 = f32[2,16,1280]{2,1,0:T(8,128)S(1)} collective-permute-done((f32[2,16,1280]{2,1,0:T(8,128)S(1)}, f32[2,16,1280]{2,1,0:T(8,128)S(1)}, u32[]{:S(2)}, u32[]{:S(2)}) %collective-permute-start.37) | collective-permute-done | bytes 163872 | tf_op jit(solution)/shard_map/ppermute | solution.py:473
  163.2 1.2 collective-permute-start.38
  164.6 5.8 %collective-permute-done.38 = f32[2,32,1280]{2,1,0:T(8,128)S(1)} collective-permute-done((f32[2,32,1280]{2,1,0:T(8,128)S(1)}, f32[2,32,1280]{2,1,0:T(8,128)S(1)}, u32[]{:S(2)}, u32[]{:S(2)}) %collective-permute-start.38) | collective-permute-done | bytes 327712 | tf_op jit(solution)/shard_map/ppermute | solution.py:473
  170.5 2.1 %collective-permute-done.39 = f32[2,64,1280]{2,1,0:T(8,128)S(1)} collective-permute-done((f32[2,64,1280]{2,1,0:T(8,128)S(1)}, f32[2,64,1280]{2,1,0:T(8,128)S(1)}, u32[]{:S(2)}, u32[]{:S(2)}) %collective-permute-start.39) | collective-permute-done | bytes 655392 | tf_op jit(solution)/shard_map/ppermute | solution.py:473
  174.0 1.7 copy-done
  175.7 0.9 slice_dynamic-update-slice_fusion
  (120 shorter events, 7.7 us)
Async XLA Ops:
  2.6 19.6 %collective-permute-start = (f32[2,136,640]{2,1,0:T(8,128)}, f32[2,136,640]{2,1,0:T(8,128)S(1)}, u32[]{:S(2)}, u32[]{:S(2)}) collective-permute-start(f32[2,136,640]{2,1,0:T(8,128)} %pieces_of.4), channel_id=1, source_target_pairs={{0,1},{1,0},{2,3},{3,2},{4,5},{5,4},{6,7},{7,6},{8,9},{9,8},{10,11... | collective-permute-start | bytes 2088968 | tf_op jit(solution)/shard_map/ppermute | solution.py:444
  9.2 26.3 %collective-permute-start.6 = (f32[2,128,640]{2,1,0:T(8,128)}, f32[2,128,640]{2,1,0:T(8,128)S(1)}, u32[]{:S(2)}, u32[]{:S(2)}) collective-permute-start(f32[2,128,640]{2,1,0:T(8,128)} %get-tuple-element.44), channel_id=1, source_target_pairs={{0,1},{1,0},{2,3},{3,2},{4,5},{5,4},{6,7},{7,6},{8,9},{9,8},{10,11... | collective-permute-start | bytes 1966088 | tf_op jit(solution)/shard_map/ppermute | solution.py:448
  33.3 14.9 %collective-permute-start.2 = (f32[3,32,1280]{2,1,0:T(8,128)}, f32[3,32,1280]{2,1,0:T(8,128)S(1)}, u32[]{:S(2)}, u32[]{:S(2)}) collective-permute-start(f32[3,32,1280]{2,1,0:T(8,128)} %get-tuple-element.42), channel_id=1, source_target_pairs={{0,2},{2,0},{4,6},{6,4},{8,10},{10,8},{12,14},{14,12},{16,18},{18,... | collective-permute-start | bytes 1474568 | tf_op jit(solution)/shard_map/ppermute | solution.py:491
  33.3 17.9 %collective-permute-start.13 = (f32[2,128,640]{2,1,0:T(8,128)}, f32[2,128,640]{2,1,0:T(8,128)S(1)}, u32[]{:S(2)}, u32[]{:S(2)}) collective-permute-start(f32[2,128,640]{2,1,0:T(8,128)} %gated.3), channel_id=1, source_target_pairs={{0,1},{1,0},{2,3},{3,2},{4,5},{5,4},{6,7},{7,6},{8,9},{9,8},{10,11... | collective-permute-start | bytes 1966088 | tf_op jit(solution)/shard_map/ppermute | solution.py:448
  46.1 3.3 %collective-permute-start.8 = (f32[3,32,1280]{2,1,0:T(8,128)}, f32[3,32,1280]{2,1,0:T(8,128)S(1)}, u32[]{:S(2)}, u32[]{:S(2)}) collective-permute-start(f32[3,32,1280]{2,1,0:T(8,128)} %get-tuple-element.49), channel_id=1, source_target_pairs={{0,2},{2,0},{4,6},{6,4},{8,10},{10,8},{12,14},{14,12},{16,18},{18,... | collective-permute-start | bytes 1474568 | tf_op jit(solution)/shard_map/ppermute | solution.py:491
  46.3 23.6 %collective-permute-start.24 = (f32[2,128,640]{2,1,0:T(8,128)}, f32[2,128,640]{2,1,0:T(8,128)}, u32[]{:S(2)}, u32[]{:S(2)}) collective-permute-start(f32[2,128,640]{2,1,0:T(8,128)} %gated.4), channel_id=1, source_target_pairs={{0,1},{1,0},{2,3},{3,2},{4,5},{5,4},{6,7},{7,6},{8,9},{9,8},{10,11... | collective-permute-start | bytes 1966088 | tf_op jit(solution)/shard_map/ppermute | solution.py:448
  48.1 15.3 %collective-permute-start.1 = (f32[3,32,1280]{2,1,0:T(8,128)}, f32[3,32,1280]{2,1,0:T(8,128)S(1)}, u32[]{:S(2)}, u32[]{:S(2)}) collective-permute-start(f32[3,32,1280]{2,1,0:T(8,128)} %get-tuple-element.40), channel_id=1, source_target_pairs={{0,2},{2,0},{4,6},{6,4},{8,10},{10,8},{12,14},{14,12},{16,18},{18,... | collective-permute-start | bytes 1474568 | tf_op jit(solution)/shard_map/ppermute | solution.py:492
  48.1 18.7 %collective-permute-start.7 = (f32[3,32,1280]{2,1,0:T(8,128)}, f32[3,32,1280]{2,1,0:T(8,128)}, u32[]{:S(2)}, u32[]{:S(2)}) collective-permute-start(f32[3,32,1280]{2,1,0:T(8,128)} %get-tuple-element.47), channel_id=1, source_target_pairs={{0,2},{2,0},{4,6},{6,4},{8,10},{10,8},{12,14},{14,12},{16,18},{18,... | collective-permute-start | bytes 1474568 | tf_op jit(solution)/shard_map/ppermute | solution.py:492
  49.4 14.0 %collective-permute-start.3 = (f32[3,32,1280]{2,1,0:T(8,128)}, f32[3,32,1280]{2,1,0:T(8,128)}, u32[]{:S(2)}, u32[]{:S(2)}) collective-permute-start(f32[3,32,1280]{2,1,0:T(8,128)} %add.295.refs_4_), channel_id=1, source_target_pairs={{0,4},{2,10},{4,0},{6,14},{8,12},{10,2},{12,8},{14,6},{16,20},{18,... | collective-permute-start | bytes 1474568 | tf_op jit(solution)/shard_map/ppermute | solution.py:467
  51.0 12.3 %copy-start.13 = (f32[3,32,1280]{2,1,0:T(8,128)}, f32[3,32,1280]{2,1,0:T(8,128)S(1)}, u32[]{:S(2)}) copy-start(f32[3,32,1280]{2,1,0:T(8,128)S(1)} %add.310.refs_4_) | copy-start | bytes 1474564
  51.3 15.7 %collective-permute-start.9 = (f32[3,32,1280]{2,1,0:T(8,128)S(1)}, f32[3,32,1280]{2,1,0:T(8,128)}, u32[]{:S(2)}, u32[]{:S(2)}) collective-permute-start(f32[3,32,1280]{2,1,0:T(8,128)S(1)} %add.310.refs_4_), channel_id=1, source_target_pairs={{0,4},{2,10},{4,0},{6,14},{8,12},{10,2},{12,8},{14,6},{16,20},{18,... | collective-permute-start | bytes 1474568 | tf_op jit(solution)/shard_map/ppermute | solution.py:467
  63.4 17.1 %collective-permute-start.15 = (f32[3,32,1280]{2,1,0:T(8,128)}, f32[3,32,1280]{2,1,0:T(8,128)S(1)}, u32[]{:S(2)}, u32[]{:S(2)}) collective-permute-start(f32[3,32,1280]{2,1,0:T(8,128)} %get-tuple-element.56), channel_id=1, source_target_pairs={{0,2},{2,0},{4,6},{6,4},{8,10},{10,8},{12,14},{14,12},{16,18},{18,... | collective-permute-start | bytes 1474568 | tf_op jit(solution)/shard_map/ppermute | solution.py:491
  63.5 19.2 %collective-permute-start.30 = (f32[2,120,640]{2,1,0:T(8,128)}, f32[2,120,640]{2,1,0:T(8,128)}, u32[]{:S(2)}, u32[]{:S(2)}) collective-permute-start(f32[2,120,640]{2,1,0:T(8,128)} %gated.5), channel_id=1, source_target_pairs={{0,1},{1,0},{2,3},{3,2},{4,5},{5,4},{6,7},{7,6},{8,9},{9,8},{10,11... | collective-permute-start | bytes 1843208 | tf_op jit(solution)/shard_map/ppermute | solution.py:448
  66.8 37.4 %collective-permute-start.14 = (f32[3,32,1280]{2,1,0:T(8,128)}, f32[3,32,1280]{2,1,0:T(8,128)S(1)}, u32[]{:S(2)}, u32[]{:S(2)}) collective-permute-start(f32[3,32,1280]{2,1,0:T(8,128)} %get-tuple-element.54), channel_id=1, source_target_pairs={{0,2},{2,0},{4,6},{6,4},{8,10},{10,8},{12,14},{14,12},{16,18},{18,... | collective-permute-start | bytes 1474568 | tf_op jit(solution)/shard_map/ppermute | solution.py:492
  67.0 13.6 %collective-permute-start.4 = (f32[3,16,1280]{2,1,0:T(8,128)}, f32[3,16,1280]{2,1,0:T(8,128)S(1)}, u32[]{:S(2)}, u32[]{:S(2)}) collective-permute-start(f32[3,16,1280]{2,1,0:T(8,128)} %get-tuple-element.80.refs_5_), channel_id=1, source_target_pairs={{0,8},{2,6},{4,12},{6,2},{8,0},{10,14},{12,4},{14,10},{16,24},{18,... | collective-permute-start | bytes 737288 | tf_op jit(solution)/shard_map/ppermute | solution.py:462
  70.0 10.5 %copy-start.16 = (f32[3,16,1280]{2,1,0:T(8,128)}, f32[3,16,1280]{2,1,0:T(8,128)S(1)}, u32[]{:S(2)}) copy-start(f32[3,16,1280]{2,1,0:T(8,128)S(1)} %get-tuple-element.82.refs_5_) | copy-start | bytes 737284
  70.0 11.9 %collective-permute-start.10 = (f32[3,16,1280]{2,1,0:T(8,128)S(1)}, f32[3,16,1280]{2,1,0:T(8,128)S(1)}, u32[]{:S(2)}, u32[]{:S(2)}) collective-permute-start(f32[3,16,1280]{2,1,0:T(8,128)S(1)} %get-tuple-element.82.refs_5_), channel_id=1, source_target_pairs={{0,8},{2,6},{4,12},{6,2},{8,0},{10,14},{12,4},{14,10},{16,24},{18,... | collective-permute-start | bytes 737288 | tf_op jit(solution)/shard_map/ppermute | solution.py:462
  70.5 10.0 %copy-start.14 = (f32[3,32,1280]{2,1,0:T(8,128)S(1)}, f32[3,32,1280]{2,1,0:T(8,128)}, u32[]{:S(2)}) copy-start(f32[3,32,1280]{2,1,0:T(8,128)} %get-tuple-element.55) | copy-start | bytes 1474564
  80.5 31.1 %collective-permute-start.26 = (f32[3,32,1280]{2,1,0:T(8,128)}, f32[3,32,1280]{2,1,0:T(8,128)S(1)}, u32[]{:S(2)}, u32[]{:S(2)}) collective-permute-start(f32[3,32,1280]{2,1,0:T(8,128)} %get-tuple-element.63), channel_id=1, source_target_pairs={{0,2},{2,0},{4,6},{6,4},{8,10},{10,8},{12,14},{14,12},{16,18},{18,... | collective-permute-start | bytes 1474568 | tf_op jit(solution)/shard_map/ppermute | solution.py:491
  80.6 43.8 %collective-permute-start.25 = (f32[3,32,1280]{2,1,0:T(8,128)}, f32[3,32,1280]{2,1,0:T(8,128)S(1)}, u32[]{:S(2)}, u32[]{:S(2)}) collective-permute-start(f32[3,32,1280]{2,1,0:T(8,128)} %get-tuple-element.61), channel_id=1, source_target_pairs={{0,2},{2,0},{4,6},{6,4},{8,10},{10,8},{12,14},{14,12},{16,18},{18,... | collective-permute-start | bytes 1474568 | tf_op jit(solution)/shard_map/ppermute | solution.py:492
  81.8 22.4 %collective-permute-start.16 = (f32[3,32,1280]{2,1,0:T(8,128)S(1)}, f32[3,32,1280]{2,1,0:T(8,128)S(1)}, u32[]{:S(2)}, u32[]{:S(2)}) collective-permute-start(f32[3,32,1280]{2,1,0:T(8,128)S(1)} %add.322.refs_4_), channel_id=1, source_target_pairs={{0,4},{2,10},{4,0},{6,14},{8,12},{10,2},{12,8},{14,6},{16,20},{18,... | collective-permute-start | bytes 1474568 | tf_op jit(solution)/shard_map/ppermute | solution.py:467
  82.7 12.5 %collective-permute-start.5 = (f32[3,8,1280]{2,1,0:T(8,128)}, f32[3,8,1280]{2,1,0:T(8,128)}, u32[]{:S(2)}, u32[]{:S(2)}) collective-permute-start(f32[3,8,1280]{2,1,0:T(8,128)} %dynamic-slice_add_fusion.14.refs_6_), channel_id=1, source_target_pairs={{0,16},{2,18},{4,20},{6,22},{8,24},{10,26},{12,28},{14,30},{16,0},... | collective-permute-start | bytes 368648 | tf_op jit(solution)/shard_map/ppermute | solution.py:462
  85.4 18.9 %copy-start.8 = (f32[3,32,1280]{2,1,0:T(8,128)S(1)}, f32[3,32,1280]{2,1,0:T(8,128)}, u32[]{:S(2)}) copy-start(f32[3,32,1280]{2,1,0:T(8,128)} %get-tuple-element.53) | copy-start | bytes 1474564
  95.2 9.0 %collective-permute-start.11 = (f32[3,8,1280]{2,1,0:T(8,128)S(1)}, f32[3,8,1280]{2,1,0:T(8,128)S(1)}, u32[]{:S(2)}, u32[]{:S(2)}) collective-permute-start(f32[3,8,1280]{2,1,0:T(8,128)S(1)} %dynamic-slice_add_fusion.13), channel_id=1, source_target_pairs={{0,16},{2,18},{4,20},{6,22},{8,24},{10,26},{12,28},{14,30},{16,0},... | collective-permute-start | bytes 368648 | tf_op jit(solution)/shard_map/ppermute | solution.py:462
  96.5 15.0 %copy-start.11 = (f32[3,32,1280]{2,1,0:T(8,128)S(1)}, f32[3,32,1280]{2,1,0:T(8,128)}, u32[]{:S(2)}) copy-start(f32[3,32,1280]{2,1,0:T(8,128)} %get-tuple-element.62) | copy-start | bytes 1474564
  104.2 14.7 %collective-permute-start.32 = (f32[3,32,1280]{2,1,0:T(8,128)}, f32[3,32,1280]{2,1,0:T(8,128)S(1)}, u32[]{:S(2)}, u32[]{:S(2)}) collective-permute-start(f32[3,32,1280]{2,1,0:T(8,128)} %get-tuple-element.70), channel_id=1, source_target_pairs={{0,2},{2,0},{4,6},{6,4},{8,10},{10,8},{12,14},{14,12},{16,18},{18,... | collective-permute-start | bytes 1474568 | tf_op jit(solution)/shard_map/ppermute | solution.py:491
  104.3 16.7 %copy-start.12 = (f32[3,32,1280]{2,1,0:T(8,128)S(1)}, f32[3,32,1280]{2,1,0:T(8,128)}, u32[]{:S(2)}) copy-start(f32[3,32,1280]{2,1,0:T(8,128)} %get-tuple-element.69) | copy-start | bytes 1474564
  104.4 6.3 %collective-permute-start.17 = (f32[3,16,1280]{2,1,0:T(8,128)S(1)}, f32[3,16,1280]{2,1,0:T(8,128)S(1)}, u32[]{:S(2)}, u32[]{:S(2)}) collective-permute-start(f32[3,16,1280]{2,1,0:T(8,128)S(1)} %get-tuple-element.84), channel_id=1, source_target_pairs={{0,8},{2,6},{4,12},{6,2},{8,0},{10,14},{12,4},{14,10},{16,24},{18,... | collective-permute-start | bytes 737288 | tf_op jit(solution)/shard_map/ppermute | solution.py:462
  110.6 7.2 %collective-permute-start.18 = (f32[3,8,1280]{2,1,0:T(8,128)S(1)}, f32[3,8,1280]{2,1,0:T(8,128)S(1)}, u32[]{:S(2)}, u32[]{:S(2)}) collective-permute-start(f32[3,8,1280]{2,1,0:T(8,128)S(1)} %dynamic-slice_add_fusion.12), channel_id=1, source_target_pairs={{0,16},{2,18},{4,20},{6,22},{8,24},{10,26},{12,28},{14,30},{16,0},... | collective-permute-start | bytes 368648 | tf_op jit(solution)/shard_map/ppermute | solution.py:462
  110.7 10.4 %collective-permute-start.12 = (f32[2,8,1280]{2,1,0:T(8,128)S(1)}, f32[2,8,1280]{2,1,0:T(8,128)S(1)}, u32[]{:S(2)}, u32[]{:S(2)}) collective-permute-start(f32[2,8,1280]{2,1,0:T(8,128)S(1)} %pad_maximum_fusion.1), channel_id=1, source_target_pairs={{0,1},{1,0},{2,3},{3,2},{4,5},{5,4},{6,7},{7,6},{8,9},{9,8},{10,11... | collective-permute-start | bytes 245768 | tf_op jit(solution)/shard_map/ppermute | solution.py:501
  111.6 12.8 %copy-start.6 = (f32[3,32,1280]{2,1,0:T(8,128)S(1)}, f32[3,32,1280]{2,1,0:T(8,128)}, u32[]{:S(2)}) copy-start(f32[3,32,1280]{2,1,0:T(8,128)} %get-tuple-element.60) | copy-start | bytes 1474564
  111.6 12.8 %collective-permute-start.27 = (f32[3,32,1280]{2,1,0:T(8,128)S(1)}, f32[3,32,1280]{2,1,0:T(8,128)S(1)}, u32[]{:S(2)}, u32[]{:S(2)}) collective-permute-start(f32[3,32,1280]{2,1,0:T(8,128)S(1)} %add.335), channel_id=1, source_target_pairs={{0,4},{2,10},{4,0},{6,14},{8,12},{10,2},{12,8},{14,6},{16,20},{18,... | collective-permute-start | bytes 1474568 | tf_op jit(solution)/shard_map/ppermute | solution.py:467
  117.9 3.3 %collective-permute-start.19 = (f32[8,1280]{1,0:T(8,128)S(1)}, f32[8,1280]{1,0:T(8,128)S(1)}, u32[]{:S(2)}, u32[]{:S(2)}) collective-permute-start(f32[8,1280]{1,0:T(8,128)S(1)} %fusion.18), channel_id=1, source_target_pairs={{0,0},{1,2},{2,1},{3,3},{4,4},{5,10},{6,9},{7,7},{8,8},{9,6},{10,5... | collective-permute-start | bytes 122888 | tf_op jit(solution)/shard_map/ppermute | solution.py:512
  118.9 15.6 %collective-permute-start.31 = (f32[3,32,1280]{2,1,0:T(8,128)}, f32[3,32,1280]{2,1,0:T(8,128)S(1)}, u32[]{:S(2)}, u32[]{:S(2)}) collective-permute-start(f32[3,32,1280]{2,1,0:T(8,128)} %get-tuple-element.68), channel_id=1, source_target_pairs={{0,2},{2,0},{4,6},{6,4},{8,10},{10,8},{12,14},{14,12},{16,18},{18,... | collective-permute-start | bytes 1474568 | tf_op jit(solution)/shard_map/ppermute | solution.py:492
  121.1 13.4 %copy-start.7 = (f32[3,32,1280]{2,1,0:T(8,128)S(1)}, f32[3,32,1280]{2,1,0:T(8,128)}, u32[]{:S(2)}) copy-start(f32[3,32,1280]{2,1,0:T(8,128)} %get-tuple-element.67) | copy-start | bytes 1474564
  121.1 13.3 %collective-permute-start.33 = (f32[3,32,1280]{2,1,0:T(8,128)S(1)}, f32[3,32,1280]{2,1,0:T(8,128)S(1)}, u32[]{:S(2)}, u32[]{:S(2)}) collective-permute-start(f32[3,32,1280]{2,1,0:T(8,128)S(1)} %add.347), channel_id=1, source_target_pairs={{0,4},{2,10},{4,0},{6,14},{8,12},{10,2},{12,8},{14,6},{16,20},{18,... | collective-permute-start | bytes 1474568 | tf_op jit(solution)/shard_map/ppermute | solution.py:467
  121.2 8.4 %collective-permute-start.20 = (f32[3,8,1280]{2,1,0:T(8,128)S(1)}, f32[3,8,1280]{2,1,0:T(8,128)S(1)}, u32[]{:S(2)}, u32[]{:S(2)}) collective-permute-start(f32[3,8,1280]{2,1,0:T(8,128)S(1)} %pad_maximum_fusion), channel_id=1, source_target_pairs={{0,16},{2,18},{4,20},{6,22},{8,24},{10,26},{12,28},{14,30},{16,0},... | collective-permute-start | bytes 368648 | tf_op jit(solution)/shard_map/ppermute | solution.py:473
  124.5 9.9 %collective-permute-start.28 = (f32[3,16,1280]{2,1,0:T(8,128)S(1)}, f32[3,16,1280]{2,1,0:T(8,128)S(1)}, u32[]{:S(2)}, u32[]{:S(2)}) collective-permute-start(f32[3,16,1280]{2,1,0:T(8,128)S(1)} %get-tuple-element.76), channel_id=1, source_target_pairs={{0,8},{2,6},{4,12},{6,2},{8,0},{10,14},{12,4},{14,10},{16,24},{18,... | collective-permute-start | bytes 737288 | tf_op jit(solution)/shard_map/ppermute | solution.py:462
  129.6 22.2 %collective-permute-start.21 = (f32[3,16,1280]{2,1,0:T(8,128)S(1)}, f32[3,16,1280]{2,1,0:T(8,128)S(1)}, u32[]{:S(2)}, u32[]{:S(2)}) collective-permute-start(f32[3,16,1280]{2,1,0:T(8,128)S(1)} %maximum_select_fusion.7), channel_id=1, source_target_pairs={{0,8},{2,6},{4,12},{6,2},{8,0},{10,14},{12,4},{14,10},{16,24},{18,... | collective-permute-start | bytes 737288 | tf_op jit(solution)/shard_map/ppermute | solution.py:473
  134.4 8.9 %collective-permute-start.29 = (f32[3,8,1280]{2,1,0:T(8,128)S(1)}, f32[3,8,1280]{2,1,0:T(8,128)S(1)}, u32[]{:S(2)}, u32[]{:S(2)}) collective-permute-start(f32[3,8,1280]{2,1,0:T(8,128)S(1)} %dynamic-slice_add_fusion.11), channel_id=1, source_target_pairs={{0,16},{2,18},{4,20},{6,22},{8,24},{10,26},{12,28},{14,30},{16,0},... | collective-permute-start | bytes 368648 | tf_op jit(solution)/shard_map/ppermute | solution.py:462
  134.6 8.8 %collective-permute-start.34 = (f32[3,16,1280]{2,1,0:T(8,128)S(1)}, f32[3,16,1280]{2,1,0:T(8,128)S(1)}, u32[]{:S(2)}, u32[]{:S(2)}) collective-permute-start(f32[3,16,1280]{2,1,0:T(8,128)S(1)} %get-tuple-element.78), channel_id=1, source_target_pairs={{0,8},{2,6},{4,12},{6,2},{8,0},{10,14},{12,4},{14,10},{16,24},{18,... | collective-permute-start | bytes 737288 | tf_op jit(solution)/shard_map/ppermute | solution.py:462
  143.4 7.9 %collective-permute-start.35 = (f32[3,8,1280]{2,1,0:T(8,128)S(1)}, f32[3,8,1280]{2,1,0:T(8,128)S(1)}, u32[]{:S(2)}, u32[]{:S(2)}) collective-permute-start(f32[3,8,1280]{2,1,0:T(8,128)S(1)} %dynamic-slice_add_fusion.10), channel_id=1, source_target_pairs={{0,16},{2,18},{4,20},{6,22},{8,24},{10,26},{12,28},{14,30},{16,0},... | collective-permute-start | bytes 368648 | tf_op jit(solution)/shard_map/ppermute | solution.py:462
  151.3 6.2 %collective-permute-start.36 = (f32[2,8,1280]{2,1,0:T(8,128)S(1)}, f32[2,8,1280]{2,1,0:T(8,128)S(1)}, u32[]{:S(2)}, u32[]{:S(2)}) collective-permute-start(f32[2,8,1280]{2,1,0:T(8,128)S(1)} %pad_maximum_fusion.2), channel_id=1, source_target_pairs={{0,16},{2,18},{4,20},{6,22},{8,24},{10,26},{12,28},{14,30},{16,0},... | collective-permute-start | bytes 245768 | tf_op jit(solution)/shard_map/ppermute | solution.py:473
  151.8 12.5 %collective-permute-start.22 = (f32[3,32,1280]{2,1,0:T(8,128)S(1)}, f32[3,32,1280]{2,1,0:T(8,128)S(1)}, u32[]{:S(2)}, u32[]{:S(2)}) collective-permute-start(f32[3,32,1280]{2,1,0:T(8,128)S(1)} %maximum_select_fusion.5), channel_id=1, source_target_pairs={{0,4},{2,10},{4,0},{6,14},{8,12},{10,2},{12,8},{14,6},{16,20},{18,... | collective-permute-start | bytes 1474568 | tf_op jit(solution)/shard_map/ppermute | solution.py:473
  157.6 5.6 %collective-permute-start.37 = (f32[2,16,1280]{2,1,0:T(8,128)S(1)}, f32[2,16,1280]{2,1,0:T(8,128)S(1)}, u32[]{:S(2)}, u32[]{:S(2)}) collective-permute-start(f32[2,16,1280]{2,1,0:T(8,128)S(1)} %maximum_select_fusion.8), channel_id=1, source_target_pairs={{0,8},{2,6},{4,12},{6,2},{8,0},{10,14},{12,4},{14,10},{16,24},{18,... | collective-permute-start | bytes 491528 | tf_op jit(solution)/shard_map/ppermute | solution.py:473
  163.2 7.1 %collective-permute-start.38 = (f32[2,32,1280]{2,1,0:T(8,128)S(1)}, f32[2,32,1280]{2,1,0:T(8,128)S(1)}, u32[]{:S(2)}, u32[]{:S(2)}) collective-permute-start(f32[2,32,1280]{2,1,0:T(8,128)S(1)} %maximum_select_fusion.6), channel_id=1, source_target_pairs={{0,4},{2,10},{4,0},{6,14},{8,12},{10,2},{12,8},{14,6},{16,20},{18,... | collective-permute-start | bytes 983048 | tf_op jit(solution)/shard_map/ppermute | solution.py:473
  164.5 8.2 %collective-permute-start.23 = (f32[3,64,1280]{2,1,0:T(8,128)S(1)}, f32[3,64,1280]{2,1,0:T(8,128)S(1)}, u32[]{:S(2)}, u32[]{:S(2)}) collective-permute-start(f32[3,64,1280]{2,1,0:T(8,128)S(1)} %maximum_select_fusion.3), channel_id=1, source_target_pairs={{0,2},{2,0},{4,6},{6,4},{8,10},{10,8},{12,14},{14,12},{16,18},{18,... | collective-permute-start | bytes 2949128 | tf_op jit(solution)/shard_map/ppermute | solution.py:473
  170.4 2.2 %collective-permute-start.39 = (f32[2,64,1280]{2,1,0:T(8,128)S(1)}, f32[2,64,1280]{2,1,0:T(8,128)S(1)}, u32[]{:S(2)}, u32[]{:S(2)}) collective-permute-start(f32[2,64,1280]{2,1,0:T(8,128)S(1)} %maximum_select_fusion.4), channel_id=1, source_target_pairs={{0,2},{2,0},{4,6},{6,4},{8,10},{10,8},{12,14},{14,12},{16,18},{18,... | collective-permute-start | bytes 1966088 | tf_op jit(solution)/shard_map/ppermute | solution.py:473
  (9 other events, 24.2 us)
